TPU v7x, 32 devices: a whole 2x2x4 slice. The times are simulated.
32 devices in a mesh: dp: 4 (over x, core), ctx: 8 (over z, y).
Axes of the slice: x: 2, y: 2, z: 4, core: 2. Of those that a mesh axis runs over, the one named last changes fastest.
Arguments:
- saved_input: bfloat16 [4, 4096, 1024], P('dp', None, 'ctx'), may hold values from -6 to 6
- out_gate: bfloat16 [4, 4096, 1024], P('dp', None, 'ctx'), may hold values from -6 to 6
- grad_out: bfloat16 [4, 4096, 1024], P('dp', None, 'ctx'), may hold values from -6 to 6
- long_filter: float32 [4096, 1024], P('ctx'), may hold values from -0.1875 to 0.1875
Outputs:
- grad_input: bfloat16 [4, 4096, 1024], P('dp', None, 'ctx')
- grad_filter: float32 [4096, 1024], P('ctx', 'dp')
All inputs are finite; a program needn't handle non-finite values.
Results may differ from a plain program's by a relative error of at most 0.0085.
Values may be sent and summed in bfloat16 or wider, within the bound.
No kernel may reach another device: no remote copies, remote signals or barrier semaphores. Data moves between devices by JAX's collectives and lax.ppermute only.
A program may use at most 128 MiB of HBM per device.

v0:
```python
import math

import jax
import jax.numpy as jnp
from jax import lax
from jax.sharding import PartitionSpec as P

RADIX = 128


def exact_product(form, left, right):
    return jnp.einsum(form, left, right, precision=lax.Precision.HIGH)


def phase_table(rows_count, cols_count, period, row_offset, col_offset):
    row_index = lax.broadcasted_iota(jnp.int32, (rows_count, cols_count), 0) + row_offset
    col_index = lax.broadcasted_iota(jnp.int32, (rows_count, cols_count), 1) + col_offset
    product_mod = row_index * col_index % period
    angles = product_mod.astype(jnp.float32) * (2.0 * math.pi / period)
    return (jnp.cos(angles), jnp.sin(angles))


def swap_halves(stacked):
    return jnp.concatenate([stacked[..., RADIX:], stacked[..., :RADIX]], axis=-1)


def apply_twist(stacked, rows_here, points, row_offset, sign):
    twist_cos, twist_sin = phase_table(rows_here, RADIX, points, row_offset, 0)
    gain = jnp.concatenate([twist_cos, twist_cos], axis=-1)
    cross = jnp.concatenate([sign * twist_sin, -sign * twist_sin], axis=-1)
    return stacked * gain + swap_halves(stacked) * cross


def mixing_matrix(sign):
    last_cos, last_sin = phase_table(RADIX, RADIX, RADIX, 0, 0)
    upper = jnp.concatenate([last_cos, -sign * last_sin], axis=1)
    lower = jnp.concatenate([sign * last_sin, last_cos], axis=1)
    return jnp.concatenate([upper, lower], axis=0)


def forward_spectrum(signal):
    channels, length = signal.shape
    half_rows = length // RADIX
    rows_all = 2 * half_rows
    points = 2 * length
    blocked = signal.reshape(channels, half_rows, RADIX)
    first_cos, first_sin = phase_table(rows_all, half_rows, rows_all, 0, 0)
    first_table = jnp.stack([first_cos, -first_sin])
    section = exact_product("pkn,cnm->ckpm", first_table, blocked).reshape(
        channels, rows_all, 2 * RADIX
    )
    twisted = apply_twist(section, rows_all, points, 0, 1.0)
    return exact_product("ckn,nm->ckm", twisted, mixing_matrix(1.0))


def inverse_first(spec, row_offset, points):
    rows_here = spec.shape[1]
    inner = exact_product("ckn,nm->ckm", spec, mixing_matrix(-1.0))
    return apply_twist(inner, rows_here, points, row_offset, -1.0)


def back_table(span_rows, rows_here, rows_all, row_begin, col_offset):
    back_cos, back_sin = phase_table(span_rows, rows_here, rows_all, row_begin, col_offset)
    return jnp.stack([back_cos, -back_sin], axis=-1)


def inverse_second(outer, row_begin, span_rows, col_offset, rows_all, points):
    channels, rows_here = (outer.shape[0], outer.shape[1])
    table = back_table(span_rows, rows_here, rows_all, row_begin, col_offset)
    split = outer.reshape(channels, rows_here, 2, RADIX)
    return exact_product("nkp,ckpm->cnm", table, split) * (1.0 / points)


def on_device(saved_input, out_gate, grad_out, long_filter):
    conv_grad = (out_gate.astype(jnp.float32) * grad_out.astype(jnp.float32)).astype(jnp.bfloat16)
    moved_input, moved_grad = (
        lax.all_to_all(saved_input, "ctx", split_axis=1, concat_axis=2, tiled=True),
        lax.all_to_all(conv_grad, "ctx", split_axis=1, concat_axis=2, tiled=True),
    )
    signal_input = moved_input[0].astype(jnp.float32)
    signal_grad = moved_grad[0].astype(jnp.float32)
    channels, length = signal_input.shape
    half_rows = length // RADIX
    rows_all = 2 * half_rows
    points = 2 * length
    grad_scale = 1.0 / math.sqrt(lax.axis_size("dp") * length)
    input_spec = forward_spectrum(signal_input)
    grad_spec = forward_spectrum(signal_grad)
    taps_spec = forward_spectrum(long_filter)
    input_real, input_imag = (input_spec[..., :RADIX], input_spec[..., RADIX:])
    grad_real, grad_imag = (grad_spec[..., :RADIX], grad_spec[..., RADIX:])
    taps_real, taps_imag = (taps_spec[..., :RADIX], taps_spec[..., RADIX:])
    back_spec = jnp.concatenate(
        [
            taps_real * grad_real + taps_imag * grad_imag,
            taps_real * grad_imag - taps_imag * grad_real,
        ],
        axis=-1,
    )
    outer = inverse_first(back_spec, 0, points)
    signal_back = inverse_second(outer, 0, half_rows, 0, rows_all, points)
    grad_channels = signal_back.reshape(1, channels, length).astype(jnp.bfloat16)
    grad_input = lax.all_to_all(grad_channels, "ctx", split_axis=2, concat_axis=1, tiled=True)
    cross_spec = jnp.concatenate(
        [
            grad_real * input_real + grad_imag * input_imag,
            grad_imag * input_real - grad_real * input_imag,
        ],
        axis=-1,
    )
    cross_outer = inverse_first(cross_spec, 0, points)
    own_filter = inverse_second(cross_outer, 0, half_rows, 0, rows_all, points)
    own_filter = own_filter.reshape(channels, length)
    grad_filter = lax.psum_scatter(own_filter, "dp", scatter_dimension=1, tiled=True) * grad_scale
    return (grad_input, grad_filter)


def solution(mesh):
    in_specs = (P("dp", None, "ctx"), P("dp", None, "ctx"), P("dp", None, "ctx"), P("ctx", None))
    out_specs = (P("dp", None, "ctx"), P("ctx", "dp"))
    return jax.shard_map(
        on_device, mesh=mesh, in_specs=in_specs, out_specs=out_specs, check_vma=False
    )
```

profile of v0, /device:TPU:0, one launch (start us, length us, event | category | flops | bytes accessed | tf_op | source)
XLA Modules:
  0.0 342.6 jit_solution(8020254298373914990)
XLA Ops:
  7.2 1.8 multiply_convert_fusion
  9.0 16.7 %copy.121 = bf16[1,4096,128]{2,0,1:T(2,128)(2,1)S(1)} copy(bf16[1,4096,128]{2,1,0:T(8,128)(2,1)S(1)} %multiply_convert_fusion) | data formatting | bytes 2097152 | tf_op jit(solution)/shard_map/convert_element_type | solution.py:75
  25.7 0.6 broadcast.253
  26.3 22.4 %reduce.1 = bf16[4096,128]{1,0:T(8,128)(2,1)S(1)} reduce(bf16[4096,1,128]{2,1,0:T(2,128)(2,1)S(1)} %bitcast.105, bf16[]{:T(256)} %broadcast.253), dimensions={1}, to_apply=%bitcast.88.reduce_sub_computation | reduce | bytes 2097154
  48.8 1.1 reshape.193
  49.9 7.8 %all-to-all-start = ((bf16[8,2,32768]{2,1,0:T(2,128)(2,1)}), bf16[8,2,32768]{2,1,0:T(2,128)(2,1)S(1)}, u32[]{:S(2)}, u32[]{:S(2)}) async-start(bf16[8,2,32768]{2,1,0:T(2,128)(2,1)} %reshape.193), calls=%async_computation | async-start | bytes 2097152 | tf_op jit(solution)/shard_map/all_to_all | solution.py:78
  57.7 3.2 copy.120
  60.9 23.4 %reduce = bf16[4096,128]{1,0:T(8,128)(2,1)} reduce(bf16[4096,1,128]{2,1,0:T(2,128)(2,1)S(1)} %bitcast.107, bf16[]{:T(256)} %broadcast.253), dimensions={1}, to_apply=%bitcast.87.reduce_sub_computation | reduce | bytes 2097154
  84.3 2.2 reshape.197
  86.5 2.1 copy.106
  88.6 0.1 sine_negate_fusion.1
  88.6 5.9 %convolution_bitcast_fusion.2 = f32[512,16,2,128]{3,1,0,2:T(8,128)} fusion(f32[512,8,128,1]{2,1,0,3:T(8,128)S(1)} %bitcast.108, f32[1,16,8]{1,2,0:T(8,128)S(1)} %get-tuple-element.22, f32[1,16,8]{1,2,0:T(8,128)S(1)} %get-tuple-element.23), kind=kOutput, calls=%fused_computation.42 | convolution fusion | flops 100663552 | bytes 10486784 | tf_op jit(solution)/shard_map/pkn,cnm->ckpm/dot_general | solution.py:12
  94.6 9.9 %copy.78 = f32[512,16,2,128]{0,3,2,1:T(8,128)} copy(f32[512,16,2,128]{3,1,0,2:T(8,128)} %convolution_bitcast_fusion.2) | data formatting | bytes 16777216 | tf_op jit(solution)/shard_map/pkn,cnm->ckpm/transpose | solution.py:12
  104.5 0.1 fusion.75
  104.6 0.1 broadcast_multiply_fusion.2
  104.6 0.6 pad_maximum_fusion.6
  105.2 0.3 fusion.56
  105.5 0.0 copy-start.3
  105.5 8.5 %fusion.96 = (f32[512,16,128]{0,2,1:T(8,128)}, f32[512,16,128]{0,2,1:T(8,128)}) fusion(f32[512,16,256]{0,2,1:T(8,128)} %bitcast.89), kind=kLoop, calls=%fused_computation.130 | loop fusion | bytes 16777216 | tf_op jit(solution)/shard_map/slice | solution.py:24
  114.0 6.0 %all-to-all-start.2 = ((bf16[8,2,32768]{2,1,0:T(2,128)(2,1)}), bf16[8,2,32768]{2,1,0:T(2,128)(2,1)}, u32[]{:S(2)}, u32[]{:S(2)}) async-start(bf16[8,2,32768]{2,1,0:T(2,128)(2,1)} %reshape.197), calls=%async_computation.2 | async-start | bytes 2097152 | tf_op jit(solution)/shard_map/all_to_all | solution.py:77
  120.0 0.2 reduce-scatter.2.cloned.1.call-start
  120.2 0.1 sine_negate_fusion
  120.3 0.3 broadcast_multiply_fusion.1
  120.5 0.0 copy-start.9
  120.6 0.6 copy-done.6
  121.1 0.0 copy-done.9
  121.2 11.9 %fusion.1 = f32[512,16,256]{0,2,1:T(8,128)} fusion(f32[512,16,128]{0,2,1:T(8,128)} %get-tuple-element.17, f32[512,16,128]{0,2,1:T(8,128)} %get-tuple-element.16, f32[512,16,256]{0,2,1:T(8,128)} %bitcast.90, f32[16,256]{1,0:T(8,128)S(1)} %get-tuple-element.21, f32[16,256]{1,0:T(8,128)S(1)} %pad_maximum_fusion.4, f32[128,128]{0,1:T(8,128)S(1)} %fusion.56, ...), kind=kOutput, calls=%fused_computation.2 | convolution fusion | flops 3229810688 | bytes 25395200 | tf_op jit(solution)/shard_map/ckn,nm->ckm/dot_general | solution.py:12
  133.1 1.0 reshape.194
  134.1 0.1 copy.103
  134.2 5.8 %convolution_bitcast_fusion.1 = f32[512,16,2,128]{3,1,2,0:T(8,128)} fusion(bf16[1,8,512,128]{3,2,1,0:T(8,128)(2,1)S(1)} %bitcast.112, f32[1,16,8]{1,2,0:T(8,128)S(1)} %get-tuple-element.22, f32[1,16,8]{1,2,0:T(8,128)S(1)} %get-tuple-element.23), kind=kOutput, calls=%fused_computation.41 | convolution fusion | flops 100663552 | bytes 9438208 | tf_op jit(solution)/shard_map/pkn,cnm->ckpm/dot_general | solution.py:12
  140.0 10.0 %copy.82 = f32[512,16,2,128]{0,3,2,1:T(8,128)} copy(f32[512,16,2,128]{3,1,2,0:T(8,128)} %convolution_bitcast_fusion.1) | data formatting | bytes 16777216 | tf_op jit(solution)/shard_map/pkn,cnm->ckpm/transpose | solution.py:12
  150.0 8.4 %fusion.95 = (f32[512,16,128]{0,2,1:T(8,128)}, f32[512,16,128]{0,2,1:T(8,128)}) fusion(f32[512,16,256]{0,2,1:T(8,128)} %bitcast.91), kind=kLoop, calls=%fused_computation.129 | loop fusion | bytes 16777216 | tf_op jit(solution)/shard_map/slice | solution.py:24
  158.4 4.3 %reshape.198 = bf16[4096,1,128]{2,1,0:T(2,128)(2,1)S(1)} reshape(bf16[8,2,32768]{2,1,0:T(2,128)(2,1)} %all-to-all-done.2) | data formatting | bytes 2097152
  162.7 0.1 copy.105
  162.9 6.4 %convolution_bitcast_fusion = f32[512,16,2,128]{3,1,0,2:T(8,128)} fusion(bf16[1,8,512,128]{3,2,1,0:T(8,128)(2,1)S(1)} %bitcast.111, f32[1,16,8]{1,2,0:T(8,128)S(1)} %get-tuple-element.22, f32[1,16,8]{1,2,0:T(8,128)S(1)} %get-tuple-element.23), kind=kOutput, calls=%fused_computation.40 | convolution fusion | flops 100663552 | bytes 9438208 | tf_op jit(solution)/shard_map/pkn,cnm->ckpm/dot_general | solution.py:12
  169.3 10.0 %copy.90 = f32[512,16,2,128]{0,3,2,1:T(8,128)} copy(f32[512,16,2,128]{3,1,0,2:T(8,128)} %convolution_bitcast_fusion) | data formatting | bytes 16777216 | tf_op jit(solution)/shard_map/pkn,cnm->ckpm/transpose | solution.py:12
  179.3 8.9 %fusion.93 = (f32[512,16,128]{0,2,1:T(8,128)}, f32[512,16,128]{0,2,1:T(8,128)}) fusion(f32[512,16,256]{0,2,1:T(8,128)} %bitcast.93), kind=kLoop, calls=%fused_computation.127 | loop fusion | bytes 16777216 | tf_op jit(solution)/shard_map/slice | solution.py:24
  188.3 12.2 %fusion.6 = f32[512,16,256]{0,2,1:T(8,128)} fusion(f32[512,16,128]{0,2,1:T(8,128)S(1)} %copy-done.1, f32[512,16,128]{0,2,1:T(8,128)S(1)} %copy-done, f32[512,16,256]{0,2,1:T(8,128)} %bitcast.92, f32[16,256]{1,0:T(8,128)S(1)} %get-tuple-element.21, f32[16,256]{1,0:T(8,128)S(1)} %pad_maximum_fusion.4, f32[128,128]{0,1:T(8,128)} %copy-done.3, ...), kind=kOutput, calls=%fused_computation.7 | convolution fusion | flops 3229810688 | bytes 25395200 | tf_op jit(solution)/shard_map/ckn,nm->ckm/dot_general | solution.py:12
  200.5 11.8 %fusion.16 = f32[512,16,256]{0,2,1:T(8,128)} fusion(f32[512,16,128]{0,2,1:T(8,128)} %get-tuple-element.11, f32[512,16,128]{0,2,1:T(8,128)} %get-tuple-element.10, f32[512,16,256]{0,2,1:T(8,128)S(1)} %bitcast.96, f32[16,256]{1,0:T(8,128)S(1)} %get-tuple-element.21, f32[16,256]{1,0:T(8,128)S(1)} %pad_maximum_fusion.4, f32[128,128]{0,1:T(8,128)} %copy-done.3, ...), kind=kOutput, calls=%fused_computation.18 | convolution fusion | flops 3229810688 | bytes 25395200 | tf_op jit(solution)/shard_map/ckn,nm->ckm/dot_general | solution.py:12
  212.3 0.0 copy-start.4
  212.3 0.0 copy-start.10
  212.3 11.2 %multiply_add_fusion = (f32[512,16,128]{0,2,1:T(8,128)S(1)}, f32[512,16,128]{0,2,1:T(8,128)}, f32[512,16,128]{0,2,1:T(8,128)}, f32[512,16,128]{0,2,1:T(8,128)}) fusion(f32[512,16,256]{0,2,1:T(8,128)} %fusion.16, f32[512,16,256]{0,2,1:T(8,128)} %fusion.6, f32[512,16,256]{0,2,1:T(8,128)S(1)} %bitcast.98), kind=kLoop, calls=%fused_computation.31 | loop fusion | flops 12582912 | bytes 41943040 | tf_op jit(solution)/shard_map/add | solution.py:106
  223.6 7.0 %fusion.10 = f32[512,16,256]{0,2,1:T(8,128)S(1)} fusion(f32[512,16,128]{0,2,1:T(8,128)} %get-tuple-element.8, f32[512,16,128]{0,2,1:T(8,128)} %get-tuple-element.9, f32[128,128]{0,1:T(8,128)S(1)} %copy-done.4, f32[128,128]{0,1:T(8,128)S(1)} %copy-done.7, f32[128,128]{0,1:T(8,128)S(1)} %copy-done.10), kind=kOutput, calls=%fused_computation.10 | convolution fusion | flops 3223519232 | bytes 16973824 | tf_op jit(solution)/shard_map/ckn,nm->ckm/dot_general | solution.py:12
  230.6 0.0 copy-start.5
  230.6 0.0 copy-start.11
  230.6 4.3 %fusion.94 = (f32[512,16,128]{0,2,1:T(8,128)}, f32[512,16,128]{0,2,1:T(8,128)}) fusion(f32[512,16,256]{0,2,1:T(8,128)S(1)} %fusion.10), kind=kLoop, calls=%fused_computation.128 | loop fusion | bytes 16777216 | tf_op jit(solution)/shard_map/slice | solution.py:24
  234.9 6.8 %fusion.20 = f32[512,16,256]{0,2,1:T(8,128)S(1)} fusion(f32[512,16,128]{0,2,1:T(8,128)} %get-tuple-element.3, f32[512,16,128]{0,2,1:T(8,128)S(1)} %get-tuple-element.2, f32[128,128]{0,1:T(8,128)S(1)} %copy-done.5, f32[128,128]{0,1:T(8,128)S(1)} %copy-done.8, f32[128,128]{0,1:T(8,128)S(1)} %copy-done.11), kind=kOutput, calls=%fused_computation.21 | convolution fusion | flops 3223519232 | bytes 16973824 | tf_op jit(solution)/shard_map/ckn,nm->ckm/dot_general | solution.py:12
  241.8 4.3 %fusion.92 = (f32[512,16,128]{0,2,1:T(8,128)}, f32[512,16,128]{0,2,1:T(8,128)}) fusion(f32[512,16,256]{0,2,1:T(8,128)S(1)} %fusion.20), kind=kLoop, calls=%fused_computation.126 | loop fusion | bytes 16777216 | tf_op jit(solution)/shard_map/slice | solution.py:24
  246.0 10.9 %fusion.24 = (f32[512,16,256]{0,2,1:T(8,128)}, f32[512,16,256]{0,2,1:T(8,128)}) fusion(f32[512,16,128]{0,2,1:T(8,128)} %get-tuple-element.7, f32[512,16,128]{0,2,1:T(8,128)} %get-tuple-element.6, f32[512,16,256]{0,2,1:T(8,128)S(1)} %fusion.20, f32[16,256]{1,0:T(8,128)S(1)} %copy-done.12, f32[16,256]{1,0:T(8,128)S(1)} %pad_maximum_fusion.4, ...), kind=kLoop, calls=%fused_computation.26 | loop fusion | flops 16777216 | bytes 50364416 | tf_op jit(solution)/shard_map/add | solution.py:31
  256.9 10.4 %copy.93 = f32[512,16,2,128]{3,1,2,0:T(8,128)} copy(f32[512,16,2,128]{0,3,2,1:T(8,128)} %bitcast.100) | data formatting | bytes 16777216 | tf_op jit(solution)/shard_map/reshape | solution.py:70
  267.3 4.6 %bitcast_multiply_fusion = f32[512,128,8]{1,2,0:T(8,128)S(1)} fusion(f32[512,16,2,128]{3,1,2,0:T(8,128)} %copy.93, f32[8,16,1]{1,0,2:T(8,128)S(1)} %get-tuple-element.28, f32[8,16,1]{1,0,2:T(8,128)S(1)} %get-tuple-element.29), kind=kOutput, calls=%fused_computation.44 | convolution fusion | flops 101187840 | bytes 10486784 | tf_op jit(solution)/shard_map/nkp,ckpm->cnm/dot_general | solution.py:12
  272.0 1.8 copy.119
  273.8 0.0 reduce-scatter.2.cloned.1.call-update
  273.8 10.5 %copy.85 = f32[512,16,2,128]{3,1,2,0:T(8,128)} copy(f32[512,16,2,128]{0,3,2,1:T(8,128)} %bitcast.99) | data formatting | bytes 16777216 | tf_op jit(solution)/shard_map/reshape | solution.py:70
  284.3 5.6 %fusion.35 = bf16[512,8,128]{2,1,0:T(8,128)(2,1)S(1)} fusion(f32[512,16,2,128]{3,1,2,0:T(8,128)} %copy.85, f32[8,16,1]{1,0,2:T(8,128)S(1)} %get-tuple-element.28, f32[8,16,1]{1,0,2:T(8,128)S(1)} %get-tuple-element.29), kind=kOutput, calls=%fused_computation.48 | convolution fusion | flops 101712128 | bytes 9438208 | tf_op jit(solution)/shard_map/nkp,ckpm->cnm/dot_general | solution.py:12
  289.9 0.5 convert_element_type.110
  290.4 2.0 copy.86
  292.4 7.1 %reduce.2 = bf16[1024,512]{1,0:T(8,128)(2,1)S(1)} reduce(bf16[1024,1,512]{2,1,0:T(2,128)(2,1)S(1)} %bitcast.106, bf16[]{:T(256)} %broadcast.253), dimensions={1}, to_apply=%bitcast.77.reduce_sub_computation | reduce | bytes 2097154
  299.5 0.8 reshape.195
  300.3 30.8 %all_to_all.48 = bf16[8,2,32768]{2,1,0:T(2,128)(2,1)S(1)} all-to-all(bf16[8,2,32768]{2,1,0:T(2,128)(2,1)S(1)} %reshape.195), channel_id=1, replica_groups=mesh['dp'=4,'ctx'=8] {'ctx'}, dimensions={0} | all-to-all | bytes 2097152 | tf_op jit(solution)/shard_map/all_to_all | solution.py:103
  331.1 1.0 reshape.196
  332.1 0.3 copy.104
  332.4 1.3 copy.87
  333.7 1.9 broadcast_multiply_fusion
  (32 shorter events, 0.1 us)
Async XLA Ops:
  49.9 64.1 %all-to-all-start = ((bf16[8,2,32768]{2,1,0:T(2,128)(2,1)}), bf16[8,2,32768]{2,1,0:T(2,128)(2,1)S(1)}, u32[]{:S(2)}, u32[]{:S(2)}) async-start(bf16[8,2,32768]{2,1,0:T(2,128)(2,1)} %reshape.193), calls=%async_computation | async-start | bytes 2097152 | tf_op jit(solution)/shard_map/all_to_all | solution.py:78
  105.5 15.0 %copy-start.3 = (f32[128,128]{0,1:T(8,128)}, f32[128,128]{0,1:T(8,128)S(1)}, u32[]{:S(2)}) copy-start(f32[128,128]{0,1:T(8,128)S(1)} %fusion.56) | copy-start | bytes 196612
  114.0 44.4 %all-to-all-start.2 = ((bf16[8,2,32768]{2,1,0:T(2,128)(2,1)}), bf16[8,2,32768]{2,1,0:T(2,128)(2,1)}, u32[]{:S(2)}, u32[]{:S(2)}) async-start(bf16[8,2,32768]{2,1,0:T(2,128)(2,1)} %reshape.197), calls=%async_computation.2 | async-start | bytes 2097152 | tf_op jit(solution)/shard_map/all_to_all | solution.py:77
  120.0 213.7 %reduce-scatter.2.cloned.1.call-start = ((), (), s32[]{:S(2)}) async-start(), calls=%async_computation.4 | async-start | bytes 2621440 | tf_op jit(solution)/shard_map/reduce_scatter | solution.py:114
  120.5 0.6 copy-start.6
  120.5 0.6 copy-start.9
  179.3 8.9 %copy-start = (f32[512,16,128]{0,2,1:T(8,128)S(1)}, f32[512,16,128]{0,2,1:T(8,128)}, u32[]{:S(2)}) copy-start(f32[512,16,128]{0,2,1:T(8,128)} %get-tuple-element.14) | copy-start | bytes 12582916
  179.3 9.0 %copy-start.1 = (f32[512,16,128]{0,2,1:T(8,128)S(1)}, f32[512,16,128]{0,2,1:T(8,128)}, u32[]{:S(2)}) copy-start(f32[512,16,128]{0,2,1:T(8,128)} %get-tuple-element.15) | copy-start | bytes 12582916
  179.3 21.2 %slice-start = ((s8[8388608]{0:T(1024)(128)(4,1)}), s8[4194304]{0:T(1024)(128)(4,1)S(1)}, s32[]{:S(2)}) async-start(s8[8388608]{0:T(1024)(128)(4,1)} %bitcast.94), calls=%async_computation.5 | async-start | bytes 8388608
  188.2 12.3 %slice-start.1 = ((s8[8388608]{0:T(1024)(128)(4,1)}), s8[4194304]{0:T(1024)(128)(4,1)S(1)}, s32[]{:S(2)}) async-start(s8[8388608]{0:T(1024)(128)(4,1)} %bitcast.94), calls=%async_computation.6 | async-start | bytes 8388608
  188.3 24.0 %slice-start.2 = ((s8[8388608]{0:T(1024)(128)(4,1)}), s8[4194304]{0:T(1024)(128)(4,1)S(1)}, s32[]{:S(2)}) async-start(s8[8388608]{0:T(1024)(128)(4,1)} %bitcast.97), calls=%async_computation.7 | async-start | bytes 8388608
  200.5 11.8 %slice-start.3 = ((s8[8388608]{0:T(1024)(128)(4,1)}), s8[4194304]{0:T(1024)(128)(4,1)S(1)}, s32[]{:S(2)}) async-start(s8[8388608]{0:T(1024)(128)(4,1)} %bitcast.97), calls=%async_computation.8 | async-start | bytes 8388608
  212.3 11.3 %copy-start.4 = (f32[128,128]{0,1:T(8,128)S(1)}, f32[128,128]{0,1:T(8,128)}, u32[]{:S(2)}) copy-start(f32[128,128]{0,1:T(8,128)} %copy-done.3) | copy-start | bytes 196612
  212.3 11.2 %copy-start.7 = (f32[128,128]{0,1:T(8,128)S(1)}, f32[128,128]{0,1:T(8,128)}, u32[]{:S(2)}) copy-start(f32[128,128]{0,1:T(8,128)} %copy-done.6) | copy-start | bytes 196612
  212.3 11.2 %copy-start.10 = (f32[128,128]{0,1:T(8,128)S(1)}, f32[128,128]{0,1:T(8,128)}, u32[]{:S(2)}) copy-start(f32[128,128]{0,1:T(8,128)} %copy-done.9) | copy-start | bytes 196612
  230.6 4.3 %copy-start.5 = (f32[128,128]{0,1:T(8,128)S(1)}, f32[128,128]{0,1:T(8,128)}, u32[]{:S(2)}) copy-start(f32[128,128]{0,1:T(8,128)} %copy-done.3) | copy-start | bytes 196612
  230.6 4.3 %copy-start.8 = (f32[128,128]{0,1:T(8,128)S(1)}, f32[128,128]{0,1:T(8,128)}, u32[]{:S(2)}) copy-start(f32[128,128]{0,1:T(8,128)} %copy-done.6) | copy-start | bytes 196612
  230.6 4.3 %copy-start.11 = (f32[128,128]{0,1:T(8,128)S(1)}, f32[128,128]{0,1:T(8,128)}, u32[]{:S(2)}) copy-start(f32[128,128]{0,1:T(8,128)} %copy-done.9) | copy-start | bytes 196612
  241.7 4.3 %copy-start.2 = (f32[512,16,128]{0,2,1:T(8,128)S(1)}, f32[512,16,128]{0,2,1:T(8,128)}, u32[]{:S(2)}) copy-start(f32[512,16,128]{0,2,1:T(8,128)} %get-tuple-element.12) | copy-start | bytes 12582916
  241.7 4.3 %copy-start.12 = (f32[16,256]{1,0:T(8,128)S(1)}, f32[16,256]{1,0:T(8,128)}, u32[]{:S(2)}) copy-start(f32[16,256]{1,0:T(8,128)} %get-tuple-element.20) | copy-start | bytes 49156
Sparse Core Ops, SparseCore 0:
  273.9 32.8 reduce-scatter.1
where the time goes:
time: 349 us; the launch traced here: 343 us
  local copies, waits for them, and re-layouts  125 us (36%)
  other arithmetic  80.1 us (23%)
  matrix products  78 us (22%)
  blocking collectives  30.8 us (9%)
  between operations  14.5 us (4%)
  starting transfers between devices  14 us (4%)
    dot_general x10, matrix products, exact_product(): return jnp.einsum(form, left, right, precision=lax.Precision.HIGH)  78 us
    unnamed x5, other arithmetic  52.9 us
    slice x5, local copies, waits for them, and re-layouts, swap_halves(): stacked[..., RADIX:]  34.4 us
    all_to_all x1, blocking collectives, on_device(): lax.all_to_all(grad_channels, 'ctx', split_axis=2, concat_axis=1, tiled=T...  30.8 us
    transpose x3, local copies, waits for them, and re-layouts, exact_product(): return jnp.einsum(form, left, right, precision=lax.Precision.HIGH)  29.9 us
    reshape x2, local copies, waits for them, and re-layouts, inverse_second(): split = outer.reshape(channels, rows_here, 2, RADIX)  20.9 us
    unnamed x47, local copies, waits for them, and re-layouts  19.4 us
    convert_element_type x1, local copies, waits for them, and re-layouts, on_device(): (out_gate.astype(jnp.float32) * grad_out.astype(jnp.float32)).astype(jnp....  16.7 us
  transfers between devices with their start and end apart: 3, of which 0 were waited for; matrix products, arithmetic and copies ran while one was open for 36% of the time, Pallas kernels for 0%

commit v1 on v0

v1 whole, which is shorter than its diff:
```python
import functools
import math

import jax
import jax.numpy as jnp
import ml_dtypes
import numpy as np
from jax import lax
from jax.experimental import pallas as pl
from jax.experimental.pallas import tpu as pltpu
from jax.sharding import PartitionSpec as P

BLOCKS = 8
GROUPS = 9
TILE = 16
C1 = math.cos(math.pi / 8)
C2 = math.cos(math.pi / 4)
C3 = math.cos(3 * math.pi / 8)
LIMIT = 56 * 1024 * 1024


def transform_tables(width):
    points = 2 * BLOCKS * width
    row = np.arange(width)
    forward = np.zeros((GROUPS, 2 * width, 2 * width), np.float64)
    for r in range(GROUPS):
        angle = 2.0 * np.pi * (np.outer(row, 16 * row + r) % points) / points
        cos, sin = np.cos(angle), np.sin(angle)
        forward[r] = np.block([[cos, -sin], [sin, cos]])
    scale = np.full((GROUPS, 1, 1), 2.0 / points)
    scale[0] = scale[-1] = 1.0 / points
    backward = np.swapaxes(forward, 1, 2) * scale
    return forward.astype(ml_dtypes.bfloat16), backward.astype(ml_dtypes.bfloat16)


def first_stage(b):
    e = [b[p] + b[p + 4] for p in range(4)]
    f = [b[p] - b[p + 4] for p in range(4)]
    e02, e13 = e[0] + e[2], e[1] + e[3]
    fd, fs = C2 * (f[1] - f[3]), C2 * (f[1] + f[3])
    d = [None] + [b[p] - b[8 - p] for p in (1, 2, 3)]
    g = [None] + [b[p] + b[8 - p] for p in (1, 2, 3)]
    d2, g2 = C2 * d[2], C2 * g[2]
    re1, re3 = C1 * d[1] + C3 * d[3], C3 * d[1] - C1 * d[3]
    im1, im3 = C3 * g[1] + C1 * g[3], C1 * g[1] - C3 * g[3]
    up, down = b[0] + d2, b[0] - d2
    bp, bm = b[4] + g2, b[4] - g2
    return [
        (e02 + e13, None),
        (up + re1, -(bp + im1)),
        (f[0] + fd, -(f[2] + fs)),
        (down + re3, bm - im3),
        (e[0] - e[2], e[3] - e[1]),
        (down - re3, -(bm + im3)),
        (f[0] - fd, f[2] - fs),
        (up - re1, bp - im1),
        (e02 - e13, None),
    ]


def last_stage(u):
    re = [pair[0] for pair in u]
    im = [pair[1] for pair in u]
    sum08, dif08 = re[0] + re[8], re[0] - re[8]
    r26, i26 = re[2] + re[6], im[2] - im[6]
    rd, sd = C2 * (re[2] - re[6]), C2 * (im[2] + im[6])
    top, low = sum08 + re[4], sum08 - re[4]
    dp, dm = dif08 + rd, dif08 - rd
    ip, im4 = sd + im[4], sd - im[4]
    even = [
        top + r26,
        dp - ip,
        low - i26,
        dm - im4,
        top - r26,
        dm + im4,
        low + i26,
        dp + ip,
    ]
    a1p, a1m = re[1] + re[7], re[1] - re[7]
    a3p, a3m = re[3] + re[5], re[3] - re[5]
    j1p, j1m = im[1] + im[7], im[1] - im[7]
    j3p, j3m = im[3] + im[5], im[3] - im[5]
    c1, c3 = C1 * a1m + C3 * a3m, C3 * a1m - C1 * a3m
    c2 = C2 * (a1p - a3p)
    s1, s3 = C3 * j1p + C1 * j3p, C1 * j1p - C3 * j3p
    s2 = C2 * (j1m + j3m)
    odd = [
        a1p + a3p,
        c1 - s1,
        c2 - s2,
        c3 - s3,
        j3m - j1m,
        -(c3 + s3),
        -(c2 + s2),
        -(c1 + s1),
    ]
    return [x + y for x, y in zip(even, odd)]


def rows_loop(rows, body):
    @pl.loop(0, rows // TILE)
    def _(step):
        body(pl.ds(pl.multiple_of(step * TILE, TILE), TILE))


def split_rows(load, mid, rows, width):
    def body(at):
        for r, pair in enumerate(first_stage([load(p, at) for p in range(BLOCKS)])):
            mid[r, at, :width] = pair[0].astype(jnp.bfloat16)
            if pair[1] is not None:
                mid[r, at, width:] = pair[1].astype(jnp.bfloat16)

    rows_loop(rows, body)


def spectrum(mid, table, r, width):
    if r in (0, GROUPS - 1):
        return jnp.dot(mid[r, :, :width], table[r, :width, :], preferred_element_type=jnp.float32)
    return jnp.dot(mid[r], table[r], preferred_element_type=jnp.float32)


def invert_group(product, table, r, width, wide):
    if r in (0, GROUPS - 1):
        wide[r, :, :width] = jnp.dot(product, table[r, :, :width], preferred_element_type=jnp.float32)
    else:
        wide[r] = jnp.dot(product, table[r], preferred_element_type=jnp.float32)


def merge_rows(wide, store, rows, width):
    def body(at):
        parts = []
        for r in range(GROUPS):
            im = None if r in (0, GROUPS - 1) else wide[r, at, width:]
            parts.append((wide[r, at, :width], im))
        for p, value in enumerate(last_stage(parts)):
            store(p, at, value)

    rows_loop(rows, body)


def gate_kernel(where, gate, upper, *outs):
    rows = outs[0].shape[0]
    for k, out in enumerate(outs):
        start = pl.multiple_of(lax.rem(where[0] + k, len(outs)) * rows, rows)
        product = gate[pl.ds(start, rows), :].astype(jnp.float32) * upper[pl.ds(start, rows), :].astype(jnp.float32)
        out[...] = product.astype(jnp.bfloat16)


def pick_kernel(where, whole, *outs):
    rows = outs[0].shape[0]
    for k, out in enumerate(outs):
        start = pl.multiple_of(lax.rem(where[0] + k, len(outs)) * rows, rows)
        out[...] = whole[pl.ds(start, rows), :]


def place_kernel(where, *refs):
    out = refs[-1]
    rows, count = refs[0].shape[0], len(refs) - 1
    for k, ref in enumerate(refs[:-1]):
        start = pl.multiple_of(lax.rem(where[0] + count - k, count) * rows, rows)
        out[pl.ds(start, rows), :] = ref[...]


def taps_kernel(taps, forward, out, mid):
    rows, width = (taps.shape[0], taps.shape[1] // BLOCKS)
    split_rows(lambda p, at: taps[at, p * width : (p + 1) * width], mid, rows, width)
    for r in range(GROUPS):
        out[r] = spectrum(mid, forward, r, width).astype(out.dtype)


def ordered(where, refs, held):
    span = refs[0].shape[1]
    for k, ref in enumerate(refs):
        start = pl.multiple_of(lax.rem(where[0] + len(refs) - k, len(refs)) * span, span)
        held[:, pl.ds(start, span)] = ref[...]


def block_of(held, width):
    return lambda p, at: held[at, p * width : (p + 1) * width].astype(jnp.float32)


def block_into(held, width):
    def store(p, at, value):
        held[at, p * width : (p + 1) * width] = value.astype(jnp.bfloat16)

    return store


def back_kernel(count, where, *refs):
    blocks, (taps_spec, forward, backward) = refs[:count], refs[count : count + 3]
    outs, grad_spec = refs[count + 3 : 2 * count + 3], refs[2 * count + 3]
    held, mid, wide = refs[2 * count + 4 :]
    rows, width = held.shape[0], held.shape[1] // BLOCKS
    ordered(where, blocks, held)
    split_rows(block_of(held, width), mid, rows, width)
    for r in range(GROUPS):
        grad = spectrum(mid, forward, r, width)
        grad_spec[r] = grad.astype(grad_spec.dtype)
        taps = taps_spec[r].astype(jnp.float32)
        gr, gi, hr, hi = grad[:, :width], grad[:, width:], taps[:, :width], taps[:, width:]
        product = jnp.concatenate([hr * gr + hi * gi, hr * gi - hi * gr], axis=1)
        invert_group(product.astype(jnp.bfloat16), backward, r, width, wide)
    merge_rows(wide, block_into(held, width), rows, width)
    span = outs[0].shape[1]
    for k, out in enumerate(outs):
        start = pl.multiple_of(lax.rem(where[0] + k, count) * span, span)
        out[...] = held[:, pl.ds(start, span)]


def cross_kernel(count, shares, where, *refs):
    blocks, (grad_spec, forward, backward) = refs[:count], refs[count : count + 3]
    outs = refs[count + 3 : count + 3 + shares]
    held, mid, wide = refs[count + 3 + shares :]
    rows, width = held.shape[0], held.shape[1] // BLOCKS
    ordered(where, blocks, held)
    split_rows(block_of(held, width), mid, rows, width)
    for r in range(GROUPS):
        signal = spectrum(mid, forward, r, width)
        grad = grad_spec[r].astype(jnp.float32)
        gr, gi, xr, xi = grad[:, :width], grad[:, width:], signal[:, :width], signal[:, width:]
        product = jnp.concatenate([gr * xr + gi * xi, gi * xr - gr * xi], axis=1)
        invert_group(product.astype(jnp.bfloat16), backward, r, width, wide)
    merge_rows(wide, block_into(held, width), rows, width)
    part = held.shape[1] // shares
    for k, out in enumerate(outs):
        start = pl.multiple_of(lax.rem(where[1] + k, shares) * part, part)
        out[...] = held[:, pl.ds(start, part)]


def sum_kernel(scale, *refs):
    total = refs[0][...].astype(jnp.float32)
    for ref in refs[1:-1]:
        total = total + ref[...].astype(jnp.float32)
    refs[-1][...] = total * scale


def call(kernel, operands, outs, scratch=(), scalar=True, flops=0):
    specs = [pl.BlockSpec(memory_space=pltpu.VMEM)] * len(operands)
    if scalar:
        specs[0] = pl.BlockSpec(memory_space=pltpu.SMEM)
    size = sum(math.prod(o.shape) * o.dtype.itemsize for o in list(operands) + list(outs))
    return pl.pallas_call(
        kernel,
        out_shape=list(outs),
        in_specs=specs,
        out_specs=[pl.BlockSpec(memory_space=pltpu.VMEM)] * len(outs),
        scratch_shapes=list(scratch),
        compiler_params=pltpu.CompilerParams(vmem_limit_bytes=LIMIT),
        cost_estimate=pl.CostEstimate(flops=flops, bytes_accessed=size, transcendentals=0),
    )(*operands)


def exchange(pieces, axis, size):
    moved = [pieces[0]]
    for k in range(1, size):
        pairs = [(i, (i + k) % size) for i in range(size)]
        moved.append(lax.ppermute(pieces[k], axis, pairs))
    return moved


def on_device(saved_input, out_gate, grad_out, long_filter):
    count, shares = lax.axis_size("ctx"), lax.axis_size("dp")
    channels, span = saved_input.shape[1:]
    rows, length = long_filter.shape
    width = length // BLOCKS
    where = jnp.stack([lax.axis_index("ctx"), lax.axis_index("dp")]).astype(jnp.int32)
    forward, backward = (jnp.asarray(t) for t in transform_tables(width))
    half, full = jnp.bfloat16, jnp.float32
    piece = jax.ShapeDtypeStruct((rows, span), half)
    spec = jax.ShapeDtypeStruct((GROUPS, rows, 2 * width), half)
    held = pltpu.VMEM((rows, length), half)
    mid = pltpu.VMEM((GROUPS, rows, 2 * width), half)
    wide = pltpu.VMEM((GROUPS, rows, 2 * width), full)
    work = 2 * GROUPS * rows * 4 * width * width

    grad_pieces = call(gate_kernel, [where, out_gate[0], grad_out[0]], [piece] * count)
    grad_blocks = exchange(grad_pieces, "ctx", count)
    input_pieces = call(pick_kernel, [where, saved_input[0]], [piece] * count)
    input_blocks = exchange(input_pieces, "ctx", count)
    (taps_spec,) = call(taps_kernel, [long_filter, forward], [spec], [mid], scalar=False, flops=work)
    *back, grad_spec = call(
        functools.partial(back_kernel, count),
        [where, *grad_blocks, taps_spec, forward, backward],
        [piece] * count + [spec],
        [held, mid, wide],
        flops=2 * work,
    )
    back_blocks = exchange(back, "ctx", count)
    share = jax.ShapeDtypeStruct((rows, length // shares), half)
    cross = call(
        functools.partial(cross_kernel, count, shares),
        [where, *input_blocks, grad_spec, forward, backward],
        [share] * shares,
        [held, mid, wide],
        flops=2 * work,
    )
    cross_blocks = exchange(cross, "dp", shares)
    scale = 1.0 / math.sqrt(shares * length)
    (grad_filter,) = call(
        functools.partial(sum_kernel, scale),
        cross_blocks,
        [jax.ShapeDtypeStruct((rows, length // shares), full)],
        scalar=False,
    )
    (grad_input,) = call(place_kernel, [where, *back_blocks], [jax.ShapeDtypeStruct((channels, span), half)])
    return (grad_input[None], grad_filter)


def solution(mesh):
    in_specs = (P("dp", None, "ctx"), P("dp", None, "ctx"), P("dp", None, "ctx"), P("ctx", None))
    out_specs = (P("dp", None, "ctx"), P("ctx", "dp"))
    return jax.shard_map(
        on_device, mesh=mesh, in_specs=in_specs, out_specs=out_specs, check_vma=False
    )
```

time: 349 us -> 99.5 us (0.29); the launches traced: 343 us -> 99.3 us
  local copies, waits for them, and re-layouts: 125 us -> 2.14 us
  other arithmetic: 80.1 us -> 0.64 us
  matrix products: 78 us -> 0 us
  starting transfers between devices: 14 us -> 49.4 us
  blocking collectives: 30.8 us -> 0 us
  Pallas kernels: 0 us -> 29.8 us
  waiting for transfers between devices: 0.02 us -> 16.4 us
  between operations: 14.5 us -> 0.89 us
    dot_general x10 -> x0, matrix products: 78 us -> none  [exact_product(): return jnp.einsum(form, left, right, precision=lax.Precision.HIGH)]
    unnamed x5 -> x0, other arithmetic: 52.9 us -> none
    ppermute x0 -> x24, starting transfers between devices: none -> 49.4 us  [exchange(): moved.append(lax.ppermute(pieces[k], axis, pairs))]
    slice x5 -> x0, local copies, waits for them, and re-layouts: 34.4 us -> none  [swap_halves(): stacked[..., RADIX:]]
    all_to_all x1 -> x0, blocking collectives: 30.8 us -> none  [on_device(): lax.all_to_all(grad_channels, 'ctx', split_axis=2, concat_axis=1, tiled=T...]
    transpose x3 -> x0, local copies, waits for them, and re-layouts: 29.9 us -> none  [exact_product(): return jnp.einsum(form, left, right, precision=lax.Precision.HIGH)]
    pallas_call x0 -> x7, Pallas kernels: none -> 29.8 us  [call(): pl.pallas_call(kernel, out_shape=list(outs), in_specs=specs, out_specs=[p...]
    add x2 -> x0, other arithmetic: 22.1 us -> none  [the longest x1 11.2 us: on_device(): grad_real * input_real + grad_imag * input_imag]
  transfers between devices with their start and end apart: 3 -> 24, of which waited for: 0 -> 4; matrix products, arithmetic and copies ran while one was open for 36% -> 0% of each run, Pallas kernels for 0% -> 25%
where the time goes in v1:
time: 99.5 us; the launch traced here: 99.3 us
  starting transfers between devices  49.4 us (50%)
  Pallas kernels  29.8 us (30%)
  waiting for transfers between devices  16.4 us (16%)
  local copies, waits for them, and re-layouts  2.14 us (2%)
    ppermute x24, starting transfers between devices, exchange(): moved.append(lax.ppermute(pieces[k], axis, pairs))  49.4 us
    pallas_call x7, Pallas kernels, call(): pl.pallas_call(kernel, out_shape=list(outs), in_specs=specs, out_specs=[p...  29.8 us
    ppermute x24, waiting for transfers between devices, exchange(): moved.append(lax.ppermute(pieces[k], axis, pairs))  16.4 us
    unnamed x52, local copies, waits for them, and re-layouts  2.14 us
  transfers between devices with their start and end apart: 24, of which 4 were waited for; matrix products, arithmetic and copies ran while one was open for 0% of the time, Pallas kernels for 25%

profile of v1, /device:TPU:0, one launch (start us, length us, event | category | flops | bytes accessed | tf_op | source)
XLA Modules:
  0.0 99.3 jit_solution(15240145110701307659)
XLA Ops:
  0.6 0.6 pad_add_fusion.where
  1.3 2.7 %shard_map.77 = (bf16[512,128]{1,0:T(8,128)(2,1)}, bf16[512,128]{1,0:T(8,128)(2,1)}, bf16[512,128]{1,0:T(8,128)(2,1)}, bf16[512,128]{1,0:T(8,128)(2,1)}, bf16[51...) custom-call(s32[2]{0:T(128)} %pad_add_fusion.where, ...), custom_call_target="tpu_custom_call" | custom-call | bytes 3145736 | tf_op jit(solution)/shard_map/pallas_call | solution.py:243
  4.0 3.0 %collective-permute-start = (bf16[512,128]{1,0:T(8,128)(2,1)}, bf16[512,128]{1,0:T(8,128)(2,1)S(1)}, u32[]{:S(2)}, u32[]{:S(2)}) collective-permute-start(bf16[512,128]{1,0:T(8,128)(2,1)} %get-tuple-element.32), channel_id=1, source_target_pairs={{0,1},{1,2},{2,3},{3,4},{4,5},{5,6},{6,7},{7,0},{8,9},{9,10},{10,1... | collective-permute-start | bytes 393224 | tf_op jit(solution)/shard_map/ppermute | solution.py:258
  6.9 1.6 %collective-permute-start.1 = (bf16[512,128]{1,0:T(8,128)(2,1)}, bf16[512,128]{1,0:T(8,128)(2,1)S(1)}, u32[]{:S(2)}, u32[]{:S(2)}) collective-permute-start(bf16[512,128]{1,0:T(8,128)(2,1)} %get-tuple-element.33), channel_id=1, source_target_pairs={{0,2},{1,3},{2,4},{3,5},{4,6},{5,7},{6,0},{7,1},{8,10},{9,11},{10,... | collective-permute-start | bytes 393224 | tf_op jit(solution)/shard_map/ppermute | solution.py:258
  8.5 2.5 %collective-permute-start.2 = (bf16[512,128]{1,0:T(8,128)(2,1)}, bf16[512,128]{1,0:T(8,128)(2,1)S(1)}, u32[]{:S(2)}, u32[]{:S(2)}) collective-permute-start(bf16[512,128]{1,0:T(8,128)(2,1)} %get-tuple-element.34), channel_id=1, source_target_pairs={{0,3},{1,4},{2,5},{3,6},{4,7},{5,0},{6,1},{7,2},{8,11},{9,12},{10,... | collective-permute-start | bytes 393224 | tf_op jit(solution)/shard_map/ppermute | solution.py:258
  11.0 1.2 %collective-permute-start.3 = (bf16[512,128]{1,0:T(8,128)(2,1)}, bf16[512,128]{1,0:T(8,128)(2,1)S(1)}, u32[]{:S(2)}, u32[]{:S(2)}) collective-permute-start(bf16[512,128]{1,0:T(8,128)(2,1)} %get-tuple-element.35), channel_id=1, source_target_pairs={{0,4},{1,5},{2,6},{3,7},{4,0},{5,1},{6,2},{7,3},{8,12},{9,13},{10,... | collective-permute-start | bytes 393224 | tf_op jit(solution)/shard_map/ppermute | solution.py:258
  12.3 2.6 %collective-permute-start.4 = (bf16[512,128]{1,0:T(8,128)(2,1)}, bf16[512,128]{1,0:T(8,128)(2,1)S(1)}, u32[]{:S(2)}, u32[]{:S(2)}) collective-permute-start(bf16[512,128]{1,0:T(8,128)(2,1)} %get-tuple-element.36), channel_id=1, source_target_pairs={{0,5},{1,6},{2,7},{3,0},{4,1},{5,2},{6,3},{7,4},{8,13},{9,14},{10,... | collective-permute-start | bytes 393224 | tf_op jit(solution)/shard_map/ppermute | solution.py:258
  14.9 2.3 %shard_map.81 = (bf16[512,128]{1,0:T(8,128)(2,1)}, bf16[512,128]{1,0:T(8,128)(2,1)}, bf16[512,128]{1,0:T(8,128)(2,1)}, bf16[512,128]{1,0:T(8,128)(2,1)}, bf16[51...) custom-call(s32[2]{0:T(128)} %pad_add_fusion.where, ...), custom_call_target="tpu_custom_call" | custom-call | bytes 2097160 | tf_op jit(solution)/shard_map/pallas_call | solution.py:243
  17.2 0.0 collective-permute-done.refs_1_
  17.2 1.4 %collective-permute-start.5 = (bf16[512,128]{1,0:T(8,128)(2,1)}, bf16[512,128]{1,0:T(8,128)(2,1)S(1)}, u32[]{:S(2)}, u32[]{:S(2)}) collective-permute-start(bf16[512,128]{1,0:T(8,128)(2,1)} %get-tuple-element.37), channel_id=1, source_target_pairs={{0,6},{1,7},{2,0},{3,1},{4,2},{5,3},{6,4},{7,5},{8,14},{9,15},{10,... | collective-permute-start | bytes 393224 | tf_op jit(solution)/shard_map/ppermute | solution.py:258
  18.6 0.0 collective-permute-done.1.refs_2_
  18.6 1.4 %collective-permute-start.6 = (bf16[512,128]{1,0:T(8,128)(2,1)}, bf16[512,128]{1,0:T(8,128)(2,1)S(1)}, u32[]{:S(2)}, u32[]{:S(2)}) collective-permute-start(bf16[512,128]{1,0:T(8,128)(2,1)} %get-tuple-element.38), channel_id=1, source_target_pairs={{0,7},{1,0},{2,1},{3,2},{4,3},{5,4},{6,5},{7,6},{8,15},{9,8},{10,9... | collective-permute-start | bytes 393224 | tf_op jit(solution)/shard_map/ppermute | solution.py:258
  20.0 5.0 %collective-permute-done.2.refs_3_ = bf16[512,128]{1,0:T(8,128)(2,1)S(1)} collective-permute-done((bf16[512,128]{1,0:T(8,128)(2,1)}, bf16[512,128]{1,0:T(8,128)(2,1)S(1)}, u32[]{:S(2)}, u32[]{:S(2)}) %collective-permute-start.2) | collective-permute-done | bytes 131104 | tf_op jit(solution)/shard_map/ppermute | solution.py:258
  25.0 0.0 collective-permute-start.14
  25.0 0.3 collective-permute-done.3.refs_4_
  25.4 5.8 %collective-permute-start.15 = (bf16[512,128]{1,0:T(8,128)(2,1)}, bf16[512,128]{1,0:T(8,128)(2,1)S(1)}, u32[]{:S(2)}, u32[]{:S(2)}) collective-permute-start(bf16[512,128]{1,0:T(8,128)(2,1)} %get-tuple-element.49), channel_id=1, source_target_pairs={{0,2},{1,3},{2,4},{3,5},{4,6},{5,7},{6,0},{7,1},{8,10},{9,11},{10,... | collective-permute-start | bytes 393224 | tf_op jit(solution)/shard_map/ppermute | solution.py:258
  31.2 0.0 collective-permute-done.4.refs_5_
  31.2 4.1 %collective-permute-start.16 = (bf16[512,128]{1,0:T(8,128)(2,1)}, bf16[512,128]{1,0:T(8,128)(2,1)S(1)}, u32[]{:S(2)}, u32[]{:S(2)}) collective-permute-start(bf16[512,128]{1,0:T(8,128)(2,1)} %get-tuple-element.50), channel_id=1, source_target_pairs={{0,3},{1,4},{2,5},{3,6},{4,7},{5,0},{6,1},{7,2},{8,11},{9,12},{10,... | collective-permute-start | bytes 393224 | tf_op jit(solution)/shard_map/ppermute | solution.py:258
  35.3 0.0 collective-permute-done.5.refs_6_
  35.3 2.9 %collective-permute-start.17 = (bf16[512,128]{1,0:T(8,128)(2,1)}, bf16[512,128]{1,0:T(8,128)(2,1)S(1)}, u32[]{:S(2)}, u32[]{:S(2)}) collective-permute-start(bf16[512,128]{1,0:T(8,128)(2,1)} %get-tuple-element.51), channel_id=1, source_target_pairs={{0,4},{1,5},{2,6},{3,7},{4,0},{5,1},{6,2},{7,3},{8,12},{9,13},{10,... | collective-permute-start | bytes 393224 | tf_op jit(solution)/shard_map/ppermute | solution.py:258
  38.2 0.0 collective-permute-done.6.refs_7_
  38.2 0.1 collective-permute-start.18
  38.3 0.0 collective-permute-done.14.refs_1_
  38.3 8.3 %collective-permute-start.19 = (bf16[512,128]{1,0:T(8,128)(2,1)}, bf16[512,128]{1,0:T(8,128)(2,1)S(1)}, u32[]{:S(2)}, u32[]{:S(2)}) collective-permute-start(bf16[512,128]{1,0:T(8,128)(2,1)} %get-tuple-element.53), channel_id=1, source_target_pairs={{0,6},{1,7},{2,0},{3,1},{4,2},{5,3},{6,4},{7,5},{8,14},{9,15},{10,... | collective-permute-start | bytes 393224 | tf_op jit(solution)/shard_map/ppermute | solution.py:258
  46.6 0.0 collective-permute-done.15.refs_2_
  46.6 0.1 collective-permute-start.20
  46.7 4.8 %shard_map.78.refs_8_ = bf16[9,512,256]{2,1,0:T(8,128)(2,1)} custom-call(f32[512,1024]{1,0:T(8,128)} %taps.1, bf16[9,256,256]{2,1,0:T(8,128)(2,1)} %constant.12.clone.forward.refs_9_), custom_call_target="tpu_custom_call" | custom-call | flops 603979776 | bytes 5636096 | tf_op jit(solution)/shard_map/pallas_call | solution.py:243
  51.5 0.0 copy-done.5
  51.5 0.0 copy-done.7
  51.6 8.2 %shard_map.79 = (bf16[512,128]{1,0:T(8,128)(2,1)}, bf16[512,128]{1,0:T(8,128)(2,1)}, bf16[512,128]{1,0:T(8,128)(2,1)}, bf16[512,128]{1,0:T(8,128)(2,1)}, bf16[51...) custom-call(s32[2]{0:T(128)} %pad_add_fusion.where, ...), custom_call_target="tpu_custom_call" | custom-call | flops 1207959552 | bytes 9175048 | tf_op jit(solution)/shard_map/pallas_call | solution.py:243
  59.8 0.0 collective-permute-done.16.refs_3_
  59.8 0.0 copy-start.8
  59.9 3.6 %collective-permute-start.10 = (bf16[512,128]{1,0:T(8,128)(2,1)}, bf16[512,128]{1,0:T(8,128)(2,1)S(1)}, u32[]{:S(2)}, u32[]{:S(2)}) collective-permute-start(bf16[512,128]{1,0:T(8,128)(2,1)} %get-tuple-element.43), channel_id=1, source_target_pairs={{0,4},{1,5},{2,6},{3,7},{4,0},{5,1},{6,2},{7,3},{8,12},{9,13},{10,... | collective-permute-start | bytes 393224 | tf_op jit(solution)/shard_map/ppermute | solution.py:258
  63.5 0.0 collective-permute-done.17.refs_4_
  63.5 0.7 collective-permute-start.11
  64.2 0.0 collective-permute-done.18.refs_5_
  64.2 1.2 %collective-permute-start.12 = (bf16[512,128]{1,0:T(8,128)(2,1)}, bf16[512,128]{1,0:T(8,128)(2,1)S(1)}, u32[]{:S(2)}, u32[]{:S(2)}) collective-permute-start(bf16[512,128]{1,0:T(8,128)(2,1)} %get-tuple-element.45), channel_id=1, source_target_pairs={{0,6},{1,7},{2,0},{3,1},{4,2},{5,3},{6,4},{7,5},{8,14},{9,15},{10,... | collective-permute-start | bytes 393224 | tf_op jit(solution)/shard_map/ppermute | solution.py:258
  65.5 0.0 collective-permute-done.19.refs_6_
  65.5 4.2 %collective-permute-start.13 = (bf16[512,128]{1,0:T(8,128)(2,1)}, bf16[512,128]{1,0:T(8,128)(2,1)S(1)}, u32[]{:S(2)}, u32[]{:S(2)}) collective-permute-start(bf16[512,128]{1,0:T(8,128)(2,1)} %get-tuple-element.46), channel_id=1, source_target_pairs={{0,7},{1,0},{2,1},{3,2},{4,3},{5,4},{6,5},{7,6},{8,15},{9,8},{10,9... | collective-permute-start | bytes 393224 | tf_op jit(solution)/shard_map/ppermute | solution.py:258
  69.7 0.0 collective-permute-done.20.refs_7_
  69.7 0.0 collective-permute-start.7
  69.7 0.6 copy-done.19
  70.4 7.3 %shard_map.82 = (bf16[512,256]{1,0:T(8,128)(2,1)}, bf16[512,256]{1,0:T(8,128)(2,1)}, bf16[512,256]{1,0:T(8,128)(2,1)}, bf16[512,256]{1,0:T(8,128)(2,1)}) custom-call(s32[2]{0:T(128)} %pad_add_fusion.where, bf16[512,128]{1,0:T(8,128)(2,1)} %get-tuple-element.47.refs_0_, bf16[512,128]{1,0:T(8,128)(2,1)} %copy-done.3, bf16[512,128]{1,0:T(8,128)(2,1)} %copy-done.4, ...), custom_call_target="tpu_custom_call" | custom-call | flops 1207959552 | bytes 6815752 | tf_op jit(solution)/shard_map/pallas_call | solution.py:243
  77.7 0.0 collective-permute-done.10.refs_4_
  77.7 0.1 collective-permute-start.21
  77.7 0.0 collective-permute-done.11.refs_5_
  77.8 1.6 %collective-permute-start.22 = (bf16[512,256]{1,0:T(8,128)(2,1)}, bf16[512,256]{1,0:T(8,128)(2,1)S(1)}, u32[]{:S(2)}, u32[]{:S(2)}) collective-permute-start(bf16[512,256]{1,0:T(8,128)(2,1)} %get-tuple-element.58), channel_id=1, source_target_pairs={{0,16},{8,24},{16,0},{24,8},{1,17},{9,25},{17,1},{25,9},{2,18},{10... | collective-permute-start | bytes 786440 | tf_op jit(solution)/shard_map/ppermute | solution.py:258
  79.3 0.0 collective-permute-done.12.refs_6_
  79.3 1.4 %collective-permute-start.23 = (bf16[512,256]{1,0:T(8,128)(2,1)}, bf16[512,256]{1,0:T(8,128)(2,1)S(1)}, u32[]{:S(2)}, u32[]{:S(2)}) collective-permute-start(bf16[512,256]{1,0:T(8,128)(2,1)} %get-tuple-element.59), channel_id=1, source_target_pairs={{0,24},{8,0},{16,8},{24,16},{1,25},{9,1},{17,9},{25,17},{2,26},{10... | collective-permute-start | bytes 786440 | tf_op jit(solution)/shard_map/ppermute | solution.py:258
  80.7 0.0 collective-permute-done.13.refs_7_
  80.7 0.1 collective-permute-start.8
  80.8 0.0 collective-permute-done.7.refs_1_
  80.8 1.5 %collective-permute-start.9 = (bf16[512,128]{1,0:T(8,128)(2,1)S(1)}, bf16[512,128]{1,0:T(8,128)(2,1)S(1)}, u32[]{:S(2)}, u32[]{:S(2)}) collective-permute-start(bf16[512,128]{1,0:T(8,128)(2,1)S(1)} %copy-done.24), channel_id=1, source_target_pairs={{0,3},{1,4},{2,5},{3,6},{4,7},{5,0},{6,1},{7,2},{8,11},{9,12},{10,... | collective-permute-start | bytes 393224 | tf_op jit(solution)/shard_map/ppermute | solution.py:258
  82.3 6.2 %collective-permute-done.8.refs_2_ = bf16[512,128]{1,0:T(8,128)(2,1)S(1)} collective-permute-done((bf16[512,128]{1,0:T(8,128)(2,1)S(1)}, bf16[512,128]{1,0:T(8,128)(2,1)S(1)}, u32[]{:S(2)}, u32[]{:S(2)}) %collective-permute-start.8) | collective-permute-done | bytes 131104 | tf_op jit(solution)/shard_map/ppermute | solution.py:258
  88.5 4.8 %collective-permute-done.9.refs_3_ = bf16[512,128]{1,0:T(8,128)(2,1)S(1)} collective-permute-done((bf16[512,128]{1,0:T(8,128)(2,1)S(1)}, bf16[512,128]{1,0:T(8,128)(2,1)S(1)}, u32[]{:S(2)}, u32[]{:S(2)}) %collective-permute-start.9) | collective-permute-done | bytes 131104 | tf_op jit(solution)/shard_map/ppermute | solution.py:258
  93.3 0.6 copy-done.23
  93.9 2.3 %shard_map.80 = bf16[4096,128]{1,0:T(8,128)(2,1)} custom-call(s32[2]{0:T(128)} %pad_add_fusion.where, bf16[512,128]{1,0:T(8,128)(2,1)} %get-tuple-element.39.refs_0_, bf16[512,128]{1,0:T(8,128)(2,1)} %copy-done.21, bf16[512,128]{1,0:T(8,128)(2,1)} %copy-done.22, bf16[512,128]{1,0:T(8,128)(2,1)} %copy-done.23, bf16[512,128]{1,0:T(8,128)(2,1)} %copy-done.10, ...), custom_call_target="tpu_custom_call" | custom-call | bytes 2097160 | tf_op jit(solution)/shard_map/pallas_call | solution.py:243
  96.3 0.0 collective-permute-done.21.refs_1_
  96.3 0.0 collective-permute-done.22.refs_2_
  96.3 0.0 collective-permute-done.23.refs_3_
  96.3 0.7 copy-done
  97.0 0.1 copy-done.1
  97.1 0.1 copy-done.2
  97.2 2.1 %shard_map.83 = f32[512,256]{1,0:T(8,128)} custom-call(bf16[512,256]{1,0:T(8,128)(2,1)} %get-tuple-element.56.refs_0_, bf16[512,256]{1,0:T(8,128)(2,1)} %copy-done, bf16[512,256]{1,0:T(8,128)(2,1)} %copy-done.1, bf16[512,256]{1,0:T(8,128)(2,1)} %copy-done.2), custom_call_target="tpu_custom_call" | custom-call | bytes 1572864 | tf_op jit(solution)/shard_map/pallas_call | solution.py:243
  (44 shorter events, 0.1 us)
Async XLA Ops:
  4.0 13.3 %collective-permute-start = (bf16[512,128]{1,0:T(8,128)(2,1)}, bf16[512,128]{1,0:T(8,128)(2,1)S(1)}, u32[]{:S(2)}, u32[]{:S(2)}) collective-permute-start(bf16[512,128]{1,0:T(8,128)(2,1)} %get-tuple-element.32), channel_id=1, source_target_pairs={{0,1},{1,2},{2,3},{3,4},{4,5},{5,6},{6,7},{7,0},{8,9},{9,10},{10,1... | collective-permute-start | bytes 393224 | tf_op jit(solution)/shard_map/ppermute | solution.py:258
  6.9 11.7 %collective-permute-start.1 = (bf16[512,128]{1,0:T(8,128)(2,1)}, bf16[512,128]{1,0:T(8,128)(2,1)S(1)}, u32[]{:S(2)}, u32[]{:S(2)}) collective-permute-start(bf16[512,128]{1,0:T(8,128)(2,1)} %get-tuple-element.33), channel_id=1, source_target_pairs={{0,2},{1,3},{2,4},{3,5},{4,6},{5,7},{6,0},{7,1},{8,10},{9,11},{10,... | collective-permute-start | bytes 393224 | tf_op jit(solution)/shard_map/ppermute | solution.py:258
  8.5 16.5 %collective-permute-start.2 = (bf16[512,128]{1,0:T(8,128)(2,1)}, bf16[512,128]{1,0:T(8,128)(2,1)S(1)}, u32[]{:S(2)}, u32[]{:S(2)}) collective-permute-start(bf16[512,128]{1,0:T(8,128)(2,1)} %get-tuple-element.34), channel_id=1, source_target_pairs={{0,3},{1,4},{2,5},{3,6},{4,7},{5,0},{6,1},{7,2},{8,11},{9,12},{10,... | collective-permute-start | bytes 393224 | tf_op jit(solution)/shard_map/ppermute | solution.py:258
  11.0 14.3 %collective-permute-start.3 = (bf16[512,128]{1,0:T(8,128)(2,1)}, bf16[512,128]{1,0:T(8,128)(2,1)S(1)}, u32[]{:S(2)}, u32[]{:S(2)}) collective-permute-start(bf16[512,128]{1,0:T(8,128)(2,1)} %get-tuple-element.35), channel_id=1, source_target_pairs={{0,4},{1,5},{2,6},{3,7},{4,0},{5,1},{6,2},{7,3},{8,12},{9,13},{10,... | collective-permute-start | bytes 393224 | tf_op jit(solution)/shard_map/ppermute | solution.py:258
  12.3 18.9 %collective-permute-start.4 = (bf16[512,128]{1,0:T(8,128)(2,1)}, bf16[512,128]{1,0:T(8,128)(2,1)S(1)}, u32[]{:S(2)}, u32[]{:S(2)}) collective-permute-start(bf16[512,128]{1,0:T(8,128)(2,1)} %get-tuple-element.36), channel_id=1, source_target_pairs={{0,5},{1,6},{2,7},{3,0},{4,1},{5,2},{6,3},{7,4},{8,13},{9,14},{10,... | collective-permute-start | bytes 393224 | tf_op jit(solution)/shard_map/ppermute | solution.py:258
  17.2 34.3 %copy-start.5 = (bf16[512,128]{1,0:T(8,128)(2,1)}, bf16[512,128]{1,0:T(8,128)(2,1)S(1)}, u32[]{:S(2)}) copy-start(bf16[512,128]{1,0:T(8,128)(2,1)S(1)} %collective-permute-done.refs_1_) | copy-start | bytes 393220
  17.2 18.0 %collective-permute-start.5 = (bf16[512,128]{1,0:T(8,128)(2,1)}, bf16[512,128]{1,0:T(8,128)(2,1)S(1)}, u32[]{:S(2)}, u32[]{:S(2)}) collective-permute-start(bf16[512,128]{1,0:T(8,128)(2,1)} %get-tuple-element.37), channel_id=1, source_target_pairs={{0,6},{1,7},{2,0},{3,1},{4,2},{5,3},{6,4},{7,5},{8,14},{9,15},{10,... | collective-permute-start | bytes 393224 | tf_op jit(solution)/shard_map/ppermute | solution.py:258
  18.6 32.9 %copy-start.6 = (bf16[512,128]{1,0:T(8,128)(2,1)}, bf16[512,128]{1,0:T(8,128)(2,1)S(1)}, u32[]{:S(2)}) copy-start(bf16[512,128]{1,0:T(8,128)(2,1)S(1)} %collective-permute-done.1.refs_2_) | copy-start | bytes 393220
  18.6 19.6 %collective-permute-start.6 = (bf16[512,128]{1,0:T(8,128)(2,1)}, bf16[512,128]{1,0:T(8,128)(2,1)S(1)}, u32[]{:S(2)}, u32[]{:S(2)}) collective-permute-start(bf16[512,128]{1,0:T(8,128)(2,1)} %get-tuple-element.38), channel_id=1, source_target_pairs={{0,7},{1,0},{2,1},{3,2},{4,3},{5,4},{6,5},{7,6},{8,15},{9,8},{10,9... | collective-permute-start | bytes 393224 | tf_op jit(solution)/shard_map/ppermute | solution.py:258
  25.0 26.5 %copy-start.7 = (bf16[512,128]{1,0:T(8,128)(2,1)}, bf16[512,128]{1,0:T(8,128)(2,1)S(1)}, u32[]{:S(2)}) copy-start(bf16[512,128]{1,0:T(8,128)(2,1)S(1)} %collective-permute-done.2.refs_3_) | copy-start | bytes 393220
  25.0 13.3 %collective-permute-start.14 = (bf16[512,128]{1,0:T(8,128)(2,1)}, bf16[512,128]{1,0:T(8,128)(2,1)S(1)}, u32[]{:S(2)}, u32[]{:S(2)}) collective-permute-start(bf16[512,128]{1,0:T(8,128)(2,1)} %get-tuple-element.48), channel_id=1, source_target_pairs={{0,1},{1,2},{2,3},{3,4},{4,5},{5,6},{6,7},{7,0},{8,9},{9,10},{10,1... | collective-permute-start | bytes 393224 | tf_op jit(solution)/shard_map/ppermute | solution.py:258
  25.4 26.2 %copy-start.9 = (bf16[512,128]{1,0:T(8,128)(2,1)}, bf16[512,128]{1,0:T(8,128)(2,1)S(1)}, u32[]{:S(2)}) copy-start(bf16[512,128]{1,0:T(8,128)(2,1)S(1)} %collective-permute-done.3.refs_4_) | copy-start | bytes 393220
  25.4 21.2 %collective-permute-start.15 = (bf16[512,128]{1,0:T(8,128)(2,1)}, bf16[512,128]{1,0:T(8,128)(2,1)S(1)}, u32[]{:S(2)}, u32[]{:S(2)}) collective-permute-start(bf16[512,128]{1,0:T(8,128)(2,1)} %get-tuple-element.49), channel_id=1, source_target_pairs={{0,2},{1,3},{2,4},{3,5},{4,6},{5,7},{6,0},{7,1},{8,10},{9,11},{10,... | collective-permute-start | bytes 393224 | tf_op jit(solution)/shard_map/ppermute | solution.py:258
  31.2 20.4 %copy-start.11 = (bf16[512,128]{1,0:T(8,128)(2,1)}, bf16[512,128]{1,0:T(8,128)(2,1)S(1)}, u32[]{:S(2)}) copy-start(bf16[512,128]{1,0:T(8,128)(2,1)S(1)} %collective-permute-done.4.refs_5_) | copy-start | bytes 393220
  31.2 28.7 %collective-permute-start.16 = (bf16[512,128]{1,0:T(8,128)(2,1)}, bf16[512,128]{1,0:T(8,128)(2,1)S(1)}, u32[]{:S(2)}, u32[]{:S(2)}) collective-permute-start(bf16[512,128]{1,0:T(8,128)(2,1)} %get-tuple-element.50), channel_id=1, source_target_pairs={{0,3},{1,4},{2,5},{3,6},{4,7},{5,0},{6,1},{7,2},{8,11},{9,12},{10,... | collective-permute-start | bytes 393224 | tf_op jit(solution)/shard_map/ppermute | solution.py:258
  35.3 16.3 %copy-start.17 = (bf16[512,128]{1,0:T(8,128)(2,1)}, bf16[512,128]{1,0:T(8,128)(2,1)S(1)}, u32[]{:S(2)}) copy-start(bf16[512,128]{1,0:T(8,128)(2,1)S(1)} %collective-permute-done.5.refs_6_) | copy-start | bytes 393220
  35.3 28.2 %collective-permute-start.17 = (bf16[512,128]{1,0:T(8,128)(2,1)}, bf16[512,128]{1,0:T(8,128)(2,1)S(1)}, u32[]{:S(2)}, u32[]{:S(2)}) collective-permute-start(bf16[512,128]{1,0:T(8,128)(2,1)} %get-tuple-element.51), channel_id=1, source_target_pairs={{0,4},{1,5},{2,6},{3,7},{4,0},{5,1},{6,2},{7,3},{8,12},{9,13},{10,... | collective-permute-start | bytes 393224 | tf_op jit(solution)/shard_map/ppermute | solution.py:258
  38.2 13.3 %copy-start.20 = (bf16[512,128]{1,0:T(8,128)(2,1)}, bf16[512,128]{1,0:T(8,128)(2,1)S(1)}, u32[]{:S(2)}) copy-start(bf16[512,128]{1,0:T(8,128)(2,1)S(1)} %collective-permute-done.6.refs_7_) | copy-start | bytes 393220
  38.2 26.0 %collective-permute-start.18 = (bf16[512,128]{1,0:T(8,128)(2,1)}, bf16[512,128]{1,0:T(8,128)(2,1)S(1)}, u32[]{:S(2)}, u32[]{:S(2)}) collective-permute-start(bf16[512,128]{1,0:T(8,128)(2,1)} %get-tuple-element.52), channel_id=1, source_target_pairs={{0,5},{1,6},{2,7},{3,0},{4,1},{5,2},{6,3},{7,4},{8,13},{9,14},{10,... | collective-permute-start | bytes 393224 | tf_op jit(solution)/shard_map/ppermute | solution.py:258
  38.3 13.3 %copy-start.3 = (bf16[512,128]{1,0:T(8,128)(2,1)}, bf16[512,128]{1,0:T(8,128)(2,1)S(1)}, u32[]{:S(2)}) copy-start(bf16[512,128]{1,0:T(8,128)(2,1)S(1)} %collective-permute-done.14.refs_1_) | copy-start | bytes 393220
  38.3 27.2 %collective-permute-start.19 = (bf16[512,128]{1,0:T(8,128)(2,1)}, bf16[512,128]{1,0:T(8,128)(2,1)S(1)}, u32[]{:S(2)}, u32[]{:S(2)}) collective-permute-start(bf16[512,128]{1,0:T(8,128)(2,1)} %get-tuple-element.53), channel_id=1, source_target_pairs={{0,6},{1,7},{2,0},{3,1},{4,2},{5,3},{6,4},{7,5},{8,14},{9,15},{10,... | collective-permute-start | bytes 393224 | tf_op jit(solution)/shard_map/ppermute | solution.py:258
  46.6 5.0 %copy-start.4 = (bf16[512,128]{1,0:T(8,128)(2,1)}, bf16[512,128]{1,0:T(8,128)(2,1)S(1)}, u32[]{:S(2)}) copy-start(bf16[512,128]{1,0:T(8,128)(2,1)S(1)} %collective-permute-done.15.refs_2_) | copy-start | bytes 393220
  46.6 23.1 %collective-permute-start.20 = (bf16[512,128]{1,0:T(8,128)(2,1)}, bf16[512,128]{1,0:T(8,128)(2,1)S(1)}, u32[]{:S(2)}, u32[]{:S(2)}) collective-permute-start(bf16[512,128]{1,0:T(8,128)(2,1)} %get-tuple-element.54), channel_id=1, source_target_pairs={{0,7},{1,0},{2,1},{3,2},{4,3},{5,4},{6,5},{7,6},{8,15},{9,8},{10,9... | collective-permute-start | bytes 393224 | tf_op jit(solution)/shard_map/ppermute | solution.py:258
  59.8 9.9 %copy-start.8 = (bf16[512,128]{1,0:T(8,128)(2,1)}, bf16[512,128]{1,0:T(8,128)(2,1)S(1)}, u32[]{:S(2)}) copy-start(bf16[512,128]{1,0:T(8,128)(2,1)S(1)} %collective-permute-done.16.refs_3_) | copy-start | bytes 393220
  59.9 17.8 %collective-permute-start.10 = (bf16[512,128]{1,0:T(8,128)(2,1)}, bf16[512,128]{1,0:T(8,128)(2,1)S(1)}, u32[]{:S(2)}, u32[]{:S(2)}) collective-permute-start(bf16[512,128]{1,0:T(8,128)(2,1)} %get-tuple-element.43), channel_id=1, source_target_pairs={{0,4},{1,5},{2,6},{3,7},{4,0},{5,1},{6,2},{7,3},{8,12},{9,13},{10,... | collective-permute-start | bytes 393224 | tf_op jit(solution)/shard_map/ppermute | solution.py:258
  63.5 6.2 %copy-start.12 = (bf16[512,128]{1,0:T(8,128)(2,1)}, bf16[512,128]{1,0:T(8,128)(2,1)S(1)}, u32[]{:S(2)}) copy-start(bf16[512,128]{1,0:T(8,128)(2,1)S(1)} %collective-permute-done.17.refs_4_) | copy-start | bytes 393220
  63.5 14.3 %collective-permute-start.11 = (bf16[512,128]{1,0:T(8,128)(2,1)}, bf16[512,128]{1,0:T(8,128)(2,1)S(1)}, u32[]{:S(2)}, u32[]{:S(2)}) collective-permute-start(bf16[512,128]{1,0:T(8,128)(2,1)} %get-tuple-element.44), channel_id=1, source_target_pairs={{0,5},{1,6},{2,7},{3,0},{4,1},{5,2},{6,3},{7,4},{8,13},{9,14},{10,... | collective-permute-start | bytes 393224 | tf_op jit(solution)/shard_map/ppermute | solution.py:258
  64.2 5.5 %copy-start.14 = (bf16[512,128]{1,0:T(8,128)(2,1)}, bf16[512,128]{1,0:T(8,128)(2,1)S(1)}, u32[]{:S(2)}) copy-start(bf16[512,128]{1,0:T(8,128)(2,1)S(1)} %collective-permute-done.18.refs_5_) | copy-start | bytes 393220
  64.2 15.1 %collective-permute-start.12 = (bf16[512,128]{1,0:T(8,128)(2,1)}, bf16[512,128]{1,0:T(8,128)(2,1)S(1)}, u32[]{:S(2)}, u32[]{:S(2)}) collective-permute-start(bf16[512,128]{1,0:T(8,128)(2,1)} %get-tuple-element.45), channel_id=1, source_target_pairs={{0,6},{1,7},{2,0},{3,1},{4,2},{5,3},{6,4},{7,5},{8,14},{9,15},{10,... | collective-permute-start | bytes 393224 | tf_op jit(solution)/shard_map/ppermute | solution.py:258
  65.5 4.3 %copy-start.16 = (bf16[512,128]{1,0:T(8,128)(2,1)}, bf16[512,128]{1,0:T(8,128)(2,1)S(1)}, u32[]{:S(2)}) copy-start(bf16[512,128]{1,0:T(8,128)(2,1)S(1)} %collective-permute-done.19.refs_6_) | copy-start | bytes 393220
  65.5 15.2 %collective-permute-start.13 = (bf16[512,128]{1,0:T(8,128)(2,1)}, bf16[512,128]{1,0:T(8,128)(2,1)S(1)}, u32[]{:S(2)}, u32[]{:S(2)}) collective-permute-start(bf16[512,128]{1,0:T(8,128)(2,1)} %get-tuple-element.46), channel_id=1, source_target_pairs={{0,7},{1,0},{2,1},{3,2},{4,3},{5,4},{6,5},{7,6},{8,15},{9,8},{10,9... | collective-permute-start | bytes 393224 | tf_op jit(solution)/shard_map/ppermute | solution.py:258
  69.7 0.7 copy-start.19
  69.7 11.1 %collective-permute-start.7 = (bf16[512,128]{1,0:T(8,128)(2,1)}, bf16[512,128]{1,0:T(8,128)(2,1)S(1)}, u32[]{:S(2)}, u32[]{:S(2)}) collective-permute-start(bf16[512,128]{1,0:T(8,128)(2,1)} %get-tuple-element.40), channel_id=1, source_target_pairs={{0,1},{1,2},{2,3},{3,4},{4,5},{5,6},{6,7},{7,0},{8,9},{9,10},{10,1... | collective-permute-start | bytes 393224 | tf_op jit(solution)/shard_map/ppermute | solution.py:258
  70.4 10.3 %copy-start.25 = (bf16[512,128]{1,0:T(8,128)(2,1)S(1)}, bf16[512,128]{1,0:T(8,128)(2,1)}, u32[]{:S(2)}) copy-start(bf16[512,128]{1,0:T(8,128)(2,1)} %get-tuple-element.41) | copy-start | bytes 393220
  70.4 10.4 %copy-start.24 = (bf16[512,128]{1,0:T(8,128)(2,1)S(1)}, bf16[512,128]{1,0:T(8,128)(2,1)}, u32[]{:S(2)}) copy-start(bf16[512,128]{1,0:T(8,128)(2,1)} %get-tuple-element.42) | copy-start | bytes 393220
  77.7 15.6 %copy-start.10 = (bf16[512,128]{1,0:T(8,128)(2,1)}, bf16[512,128]{1,0:T(8,128)(2,1)S(1)}, u32[]{:S(2)}) copy-start(bf16[512,128]{1,0:T(8,128)(2,1)S(1)} %collective-permute-done.10.refs_4_) | copy-start | bytes 393220
  77.7 18.6 %collective-permute-start.21 = (bf16[512,256]{1,0:T(8,128)(2,1)}, bf16[512,256]{1,0:T(8,128)(2,1)S(1)}, u32[]{:S(2)}, u32[]{:S(2)}) collective-permute-start(bf16[512,256]{1,0:T(8,128)(2,1)} %get-tuple-element.57), channel_id=1, source_target_pairs={{0,8},{8,16},{16,24},{24,0},{1,9},{9,17},{17,25},{25,1},{2,10},{10... | collective-permute-start | bytes 786440 | tf_op jit(solution)/shard_map/ppermute | solution.py:258
  77.8 15.5 %copy-start.13 = (bf16[512,128]{1,0:T(8,128)(2,1)}, bf16[512,128]{1,0:T(8,128)(2,1)S(1)}, u32[]{:S(2)}) copy-start(bf16[512,128]{1,0:T(8,128)(2,1)S(1)} %collective-permute-done.11.refs_5_) | copy-start | bytes 393220
  77.8 18.5 %collective-permute-start.22 = (bf16[512,256]{1,0:T(8,128)(2,1)}, bf16[512,256]{1,0:T(8,128)(2,1)S(1)}, u32[]{:S(2)}, u32[]{:S(2)}) collective-permute-start(bf16[512,256]{1,0:T(8,128)(2,1)} %get-tuple-element.58), channel_id=1, source_target_pairs={{0,16},{8,24},{16,0},{24,8},{1,17},{9,25},{17,1},{25,9},{2,18},{10... | collective-permute-start | bytes 786440 | tf_op jit(solution)/shard_map/ppermute | solution.py:258
  79.3 14.0 %copy-start.15 = (bf16[512,128]{1,0:T(8,128)(2,1)}, bf16[512,128]{1,0:T(8,128)(2,1)S(1)}, u32[]{:S(2)}) copy-start(bf16[512,128]{1,0:T(8,128)(2,1)S(1)} %collective-permute-done.12.refs_6_) | copy-start | bytes 393220
  79.3 17.0 %collective-permute-start.23 = (bf16[512,256]{1,0:T(8,128)(2,1)}, bf16[512,256]{1,0:T(8,128)(2,1)S(1)}, u32[]{:S(2)}, u32[]{:S(2)}) collective-permute-start(bf16[512,256]{1,0:T(8,128)(2,1)} %get-tuple-element.59), channel_id=1, source_target_pairs={{0,24},{8,0},{16,8},{24,16},{1,25},{9,1},{17,9},{25,17},{2,26},{10... | collective-permute-start | bytes 786440 | tf_op jit(solution)/shard_map/ppermute | solution.py:258
  80.7 12.6 %copy-start.18 = (bf16[512,128]{1,0:T(8,128)(2,1)}, bf16[512,128]{1,0:T(8,128)(2,1)S(1)}, u32[]{:S(2)}) copy-start(bf16[512,128]{1,0:T(8,128)(2,1)S(1)} %collective-permute-done.13.refs_7_) | copy-start | bytes 393220
  80.7 7.8 %collective-permute-start.8 = (bf16[512,128]{1,0:T(8,128)(2,1)S(1)}, bf16[512,128]{1,0:T(8,128)(2,1)S(1)}, u32[]{:S(2)}, u32[]{:S(2)}) collective-permute-start(bf16[512,128]{1,0:T(8,128)(2,1)S(1)} %copy-done.25), channel_id=1, source_target_pairs={{0,2},{1,3},{2,4},{3,5},{4,6},{5,7},{6,0},{7,1},{8,10},{9,11},{10,... | collective-permute-start | bytes 393224 | tf_op jit(solution)/shard_map/ppermute | solution.py:258
  80.8 12.5 %copy-start.21 = (bf16[512,128]{1,0:T(8,128)(2,1)}, bf16[512,128]{1,0:T(8,128)(2,1)S(1)}, u32[]{:S(2)}) copy-start(bf16[512,128]{1,0:T(8,128)(2,1)S(1)} %collective-permute-done.7.refs_1_) | copy-start | bytes 393220
  80.8 12.5 %collective-permute-start.9 = (bf16[512,128]{1,0:T(8,128)(2,1)S(1)}, bf16[512,128]{1,0:T(8,128)(2,1)S(1)}, u32[]{:S(2)}, u32[]{:S(2)}) collective-permute-start(bf16[512,128]{1,0:T(8,128)(2,1)S(1)} %copy-done.24), channel_id=1, source_target_pairs={{0,3},{1,4},{2,5},{3,6},{4,7},{5,0},{6,1},{7,2},{8,11},{9,12},{10,... | collective-permute-start | bytes 393224 | tf_op jit(solution)/shard_map/ppermute | solution.py:258
  88.5 4.8 %copy-start.22 = (bf16[512,128]{1,0:T(8,128)(2,1)}, bf16[512,128]{1,0:T(8,128)(2,1)S(1)}, u32[]{:S(2)}) copy-start(bf16[512,128]{1,0:T(8,128)(2,1)S(1)} %collective-permute-done.8.refs_2_) | copy-start | bytes 393220
  93.3 0.6 copy-start.23
  96.3 0.7 copy-start
  96.3 0.8 copy-start.1
  96.3 0.9 copy-start.2

commit v2 on v1

--- a/solution.py
+++ b/solution.py
@@ -139,27 +139,8 @@
     rows_loop(rows, body)
 
 
-def gate_kernel(where, gate, upper, *outs):
-    rows = outs[0].shape[0]
-    for k, out in enumerate(outs):
-        start = pl.multiple_of(lax.rem(where[0] + k, len(outs)) * rows, rows)
-        product = gate[pl.ds(start, rows), :].astype(jnp.float32) * upper[pl.ds(start, rows), :].astype(jnp.float32)
-        out[...] = product.astype(jnp.bfloat16)
-
-
-def pick_kernel(where, whole, *outs):
-    rows = outs[0].shape[0]
-    for k, out in enumerate(outs):
-        start = pl.multiple_of(lax.rem(where[0] + k, len(outs)) * rows, rows)
-        out[...] = whole[pl.ds(start, rows), :]
-
-
-def place_kernel(where, *refs):
-    out = refs[-1]
-    rows, count = refs[0].shape[0], len(refs) - 1
-    for k, ref in enumerate(refs[:-1]):
-        start = pl.multiple_of(lax.rem(where[0] + count - k, count) * rows, rows)
-        out[pl.ds(start, rows), :] = ref[...]
+def gate_kernel(gate, upper, out):
+    out[...] = (gate[...].astype(jnp.float32) * upper[...].astype(jnp.float32)).astype(jnp.bfloat16)
 
 
 def taps_kernel(taps, forward, out, mid):
@@ -169,11 +150,10 @@
         out[r] = spectrum(mid, forward, r, width).astype(out.dtype)
 
 
-def ordered(where, refs, held):
-    span = refs[0].shape[1]
-    for k, ref in enumerate(refs):
-        start = pl.multiple_of(lax.rem(where[0] + len(refs) - k, len(refs)) * span, span)
-        held[:, pl.ds(start, span)] = ref[...]
+def ordered(blocks, held):
+    span = blocks.shape[2]
+    for p in range(blocks.shape[0]):
+        held[:, p * span : (p + 1) * span] = blocks[p]
 
 
 def block_of(held, width):
@@ -187,12 +167,9 @@
     return store
 
 
-def back_kernel(count, where, *refs):
-    blocks, (taps_spec, forward, backward) = refs[:count], refs[count : count + 3]
-    outs, grad_spec = refs[count + 3 : 2 * count + 3], refs[2 * count + 3]
-    held, mid, wide = refs[2 * count + 4 :]
+def back_kernel(blocks, taps_spec, forward, backward, out, grad_spec, held, mid, wide):
     rows, width = held.shape[0], held.shape[1] // BLOCKS
-    ordered(where, blocks, held)
+    ordered(blocks, held)
     split_rows(block_of(held, width), mid, rows, width)
     for r in range(GROUPS):
         grad = spectrum(mid, forward, r, width)
@@ -202,18 +179,15 @@
         product = jnp.concatenate([hr * gr + hi * gi, hr * gi - hi * gr], axis=1)
         invert_group(product.astype(jnp.bfloat16), backward, r, width, wide)
     merge_rows(wide, block_into(held, width), rows, width)
-    span = outs[0].shape[1]
-    for k, out in enumerate(outs):
-        start = pl.multiple_of(lax.rem(where[0] + k, count) * span, span)
-        out[...] = held[:, pl.ds(start, span)]
-
-
-def cross_kernel(count, shares, where, *refs):
-    blocks, (grad_spec, forward, backward) = refs[:count], refs[count : count + 3]
-    outs = refs[count + 3 : count + 3 + shares]
-    held, mid, wide = refs[count + 3 + shares :]
+    span = out.shape[2]
+    for p in range(out.shape[0]):
+        out[p] = held[:, p * span : (p + 1) * span]
+
+
+def cross_kernel(where, blocks, grad_spec, forward, backward, *refs):
+    outs, (held, mid, wide) = refs[:-3], refs[-3:]
     rows, width = held.shape[0], held.shape[1] // BLOCKS
-    ordered(where, blocks, held)
+    ordered(blocks, held)
     split_rows(block_of(held, width), mid, rows, width)
     for r in range(GROUPS):
         signal = spectrum(mid, forward, r, width)
@@ -222,9 +196,9 @@
         product = jnp.concatenate([gr * xr + gi * xi, gi * xr - gr * xi], axis=1)
         invert_group(product.astype(jnp.bfloat16), backward, r, width, wide)
     merge_rows(wide, block_into(held, width), rows, width)
-    part = held.shape[1] // shares
+    part = held.shape[1] // len(outs)
     for k, out in enumerate(outs):
-        start = pl.multiple_of(lax.rem(where[1] + k, shares) * part, part)
+        start = pl.multiple_of(lax.rem(where[0] + k, len(outs)) * part, part)
         out[...] = held[:, pl.ds(start, part)]
 
 
@@ -259,38 +233,43 @@
     return moved
 
 
+def swap(blocks):
+    return lax.all_to_all(blocks, "ctx", split_axis=0, concat_axis=0, tiled=True)
+
+
 def on_device(saved_input, out_gate, grad_out, long_filter):
     count, shares = lax.axis_size("ctx"), lax.axis_size("dp")
     channels, span = saved_input.shape[1:]
     rows, length = long_filter.shape
     width = length // BLOCKS
-    where = jnp.stack([lax.axis_index("ctx"), lax.axis_index("dp")]).astype(jnp.int32)
+    where = lax.axis_index("dp").astype(jnp.int32)[None]
     forward, backward = (jnp.asarray(t) for t in transform_tables(width))
     half, full = jnp.bfloat16, jnp.float32
-    piece = jax.ShapeDtypeStruct((rows, span), half)
+    blocks = jax.ShapeDtypeStruct((count, rows, span), half)
     spec = jax.ShapeDtypeStruct((GROUPS, rows, 2 * width), half)
     held = pltpu.VMEM((rows, length), half)
     mid = pltpu.VMEM((GROUPS, rows, 2 * width), half)
     wide = pltpu.VMEM((GROUPS, rows, 2 * width), full)
     work = 2 * GROUPS * rows * 4 * width * width
 
-    grad_pieces = call(gate_kernel, [where, out_gate[0], grad_out[0]], [piece] * count)
-    grad_blocks = exchange(grad_pieces, "ctx", count)
-    input_pieces = call(pick_kernel, [where, saved_input[0]], [piece] * count)
-    input_blocks = exchange(input_pieces, "ctx", count)
+    saved_input, out_gate, grad_out = (x.reshape(blocks.shape) for x in (saved_input, out_gate, grad_out))
+    (conv_grad,) = call(gate_kernel, [out_gate, grad_out], [blocks], scalar=False)
+    grad_blocks = swap(conv_grad)
+    input_blocks = swap(saved_input)
     (taps_spec,) = call(taps_kernel, [long_filter, forward], [spec], [mid], scalar=False, flops=work)
-    *back, grad_spec = call(
-        functools.partial(back_kernel, count),
-        [where, *grad_blocks, taps_spec, forward, backward],
-        [piece] * count + [spec],
+    back, grad_spec = call(
+        back_kernel,
+        [grad_blocks, taps_spec, forward, backward],
+        [blocks, spec],
         [held, mid, wide],
+        scalar=False,
         flops=2 * work,
     )
-    back_blocks = exchange(back, "ctx", count)
+    grad_input = swap(back)
     share = jax.ShapeDtypeStruct((rows, length // shares), half)
     cross = call(
-        functools.partial(cross_kernel, count, shares),
-        [where, *input_blocks, grad_spec, forward, backward],
+        cross_kernel,
+        [where, input_blocks, grad_spec, forward, backward],
         [share] * shares,
         [held, mid, wide],
         flops=2 * work,
@@ -303,8 +282,7 @@
         [jax.ShapeDtypeStruct((rows, length // shares), full)],
         scalar=False,
     )
-    (grad_input,) = call(place_kernel, [where, *back_blocks], [jax.ShapeDtypeStruct((channels, span), half)])
-    return (grad_input[None], grad_filter)
+    return (grad_input.reshape(1, channels, span), grad_filter)
 
 
 def solution(mesh):

time: 99.5 us -> 96.4 us (0.969)
  starting transfers between devices: 49.4 us -> 10.1 us
  blocking collectives: 0 us -> 33.2 us
  waiting for transfers between devices: 16.4 us -> 25.9 us
  Pallas kernels: 29.8 us -> 24.6 us
    ppermute x24 -> x3, starting transfers between devices: 49.4 us -> 2.96 us  [exchange(): moved.append(lax.ppermute(pieces[k], axis, pairs))]
    all_to_all x0 -> x1, blocking collectives: none -> 33.2 us  [swap(): lax.all_to_all(blocks, 'ctx', split_axis=0, concat_axis=0, tiled=True)]
    all_to_all x0 -> x2, waiting for transfers between devices: none -> 15.3 us  [swap(): lax.all_to_all(blocks, 'ctx', split_axis=0, concat_axis=0, tiled=True)]
    all_to_all x0 -> x2, starting transfers between devices: none -> 7.15 us  [swap(): lax.all_to_all(blocks, 'ctx', split_axis=0, concat_axis=0, tiled=True)]
    ppermute x24 -> x3, waiting for transfers between devices: 16.4 us -> 10.6 us  [exchange(): moved.append(lax.ppermute(pieces[k], axis, pairs))]
    pallas_call x7 -> x5, Pallas kernels: 29.8 us -> 24.6 us  [call(): pl.pallas_call(kernel, out_shape=list(outs), in_specs=specs, out_specs=[p...]
    unnamed x52 -> x9, local copies, waits for them, and re-layouts: 2.14 us -> 1.67 us
  transfers between devices with their start and end apart: 24 -> 5, of which waited for: 4 -> 5; matrix products, arithmetic and copies ran while one was open for 0% -> 0% of each run, Pallas kernels for 25% -> 23%
where the time goes in v2:
time: 96.4 us; the launch traced here: 96.1 us
  blocking collectives  33.2 us (34%)
  waiting for transfers between devices  25.9 us (27%)
  Pallas kernels  24.6 us (26%)
  starting transfers between devices  10.1 us (10%)
  local copies, waits for them, and re-layouts  1.67 us (2%)
    all_to_all x1, blocking collectives, swap(): lax.all_to_all(blocks, 'ctx', split_axis=0, concat_axis=0, tiled=True)  33.2 us
    pallas_call x5, Pallas kernels, call(): pl.pallas_call(kernel, out_shape=list(outs), in_specs=specs, out_specs=[p...  24.6 us
    all_to_all x2, waiting for transfers between devices, swap(): lax.all_to_all(blocks, 'ctx', split_axis=0, concat_axis=0, tiled=True)  15.3 us
    ppermute x3, waiting for transfers between devices, exchange(): moved.append(lax.ppermute(pieces[k], axis, pairs))  10.6 us
    all_to_all x2, starting transfers between devices, swap(): lax.all_to_all(blocks, 'ctx', split_axis=0, concat_axis=0, tiled=True)  7.15 us
    ppermute x3, starting transfers between devices, exchange(): moved.append(lax.ppermute(pieces[k], axis, pairs))  2.96 us
  transfers between devices with their start and end apart: 5, of which 5 were waited for; matrix products, arithmetic and copies ran while one was open for 0% of the time, Pallas kernels for 23%

profile of v2, /device:TPU:0, one launch (start us, length us, event | category | flops | bytes accessed | tf_op | source)
XLA Modules:
  0.0 96.1 jit_solution(4287579863440890656)
XLA Ops:
  0.6 2.7 %shard_map.77 = bf16[8,512,128]{2,1,0:T(8,128)(2,1)} custom-call(bf16[8,512,128]{2,1,0:T(8,128)(2,1)} %bitcast.6, bf16[8,512,128]{2,1,0:T(8,128)(2,1)} %bitcast.7), custom_call_target="tpu_custom_call" | custom-call | bytes 3145728 | tf_op jit(solution)/shard_map/pallas_call | solution.py:217
  3.4 33.2 %all_to_all.15.blocks = bf16[8,512,128]{2,1,0:T(8,128)(2,1)} all-to-all(bf16[8,512,128]{2,1,0:T(8,128)(2,1)} %shard_map.77), channel_id=1, replica_groups=mesh['dp'=4,'ctx'=8] {'ctx'}, dimensions={0} | all-to-all | bytes 2097152 | tf_op jit(solution)/shard_map/all_to_all | solution.py:237
  36.5 3.6 %all-to-all-start.2 = ((bf16[8,512,128]{2,1,0:T(8,128)(2,1)}), bf16[8,512,128]{2,1,0:T(8,128)(2,1)S(1)}, u32[]{:S(2)}, u32[]{:S(2)}) async-start(bf16[8,512,128]{2,1,0:T(8,128)(2,1)} %bitcast.4), calls=%async_computation.2 | async-start | bytes 2097152 | tf_op jit(solution)/shard_map/all_to_all | solution.py:237
  40.1 4.8 %shard_map.78.taps_spec = bf16[9,512,256]{2,1,0:T(8,128)(2,1)} custom-call(f32[512,1024]{1,0:T(8,128)} %taps.1, bf16[9,256,256]{2,1,0:T(8,128)(2,1)} %constant.9.clone.forward), custom_call_target="tpu_custom_call" | custom-call | flops 603979776 | bytes 5636096 | tf_op jit(solution)/shard_map/pallas_call | solution.py:217
  44.9 7.8 %shard_map.79 = (bf16[8,512,128]{2,1,0:T(8,128)(2,1)}, bf16[9,512,256]{2,1,0:T(8,128)(2,1)}) custom-call(bf16[8,512,128]{2,1,0:T(8,128)(2,1)} %all_to_all.15.blocks, bf16[9,512,256]{2,1,0:T(8,128)(2,1)} %shard_map.78.taps_spec, bf16[9,256,256]{2,1,0:T(8,128)(2,1)} %constant.9.clone.forward, bf16[9,256,256]{2,1,0:T(8,128)(2,1)} %constant.10.clone.backward), custom_call_target="tpu_custom_call" | custom-call | flops 1207959552 | bytes 9175040 | tf_op jit(solution)/shard_map/pallas_call | solution.py:217
  52.7 13.0 %all-to-all-done.2.blocks = bf16[8,512,128]{2,1,0:T(8,128)(2,1)S(1)} async-done(((bf16[8,512,128]{2,1,0:T(8,128)(2,1)}), bf16[8,512,128]{2,1,0:T(8,128)(2,1)S(1)}, u32[]{:S(2)}, u32[]{:S(2)}) %all-to-all-start.2) | async-done | bytes 1048608 | tf_op jit(solution)/shard_map/all_to_all | solution.py:237
  65.7 0.0 copy-start
  65.7 3.6 %all-to-all-start.1 = ((bf16[8,512,128]{2,1,0:T(8,128)(2,1)}), bf16[8,512,128]{2,1,0:T(8,128)(2,1)S(1)}, u32[]{:S(2)}, u32[]{:S(2)}) async-start(bf16[8,512,128]{2,1,0:T(8,128)(2,1)} %get-tuple-element.8), calls=%async_computation.1 | async-start | bytes 2097152 | tf_op jit(solution)/shard_map/all_to_all | solution.py:237
  69.3 0.0 copy-done
  69.3 7.2 %shard_map.80 = (bf16[512,256]{1,0:T(8,128)(2,1)}, bf16[512,256]{1,0:T(8,128)(2,1)}, bf16[512,256]{1,0:T(8,128)(2,1)}, bf16[512,256]{1,0:T(8,128)(2,1)}) custom-call(s32[1]{0:T(128)} %bitcast.3.where, bf16[8,512,128]{2,1,0:T(8,128)(2,1)} %copy-done, bf16[9,512,256]{2,1,0:T(8,128)(2,1)} %get-tuple-element.9.grad_spec, ...), custom_call_target="tpu_custom_call" | custom-call | flops 1207959552 | bytes 6815748 | tf_op jit(solution)/shard_map/pallas_call | solution.py:217
  76.5 0.0 collective-permute-start
  76.5 1.5 %collective-permute-start.1 = (bf16[512,256]{1,0:T(8,128)(2,1)}, bf16[512,256]{1,0:T(8,128)(2,1)S(1)}, u32[]{:S(2)}, u32[]{:S(2)}) collective-permute-start(bf16[512,256]{1,0:T(8,128)(2,1)} %get-tuple-element.12), channel_id=1, source_target_pairs={{0,16},{8,24},{16,0},{24,8},{1,17},{9,25},{17,1},{25,9},{2,18},{10... | collective-permute-start | bytes 786440 | tf_op jit(solution)/shard_map/ppermute | solution.py:232
  78.0 1.4 %collective-permute-start.2 = (bf16[512,256]{1,0:T(8,128)(2,1)}, bf16[512,256]{1,0:T(8,128)(2,1)S(1)}, u32[]{:S(2)}, u32[]{:S(2)}) collective-permute-start(bf16[512,256]{1,0:T(8,128)(2,1)} %get-tuple-element.13), channel_id=1, source_target_pairs={{0,24},{8,0},{16,8},{24,16},{1,25},{9,1},{17,9},{25,17},{2,26},{10... | collective-permute-start | bytes 786440 | tf_op jit(solution)/shard_map/ppermute | solution.py:232
  79.4 5.3 %collective-permute-done.refs_1_ = bf16[512,256]{1,0:T(8,128)(2,1)S(1)} collective-permute-done((bf16[512,256]{1,0:T(8,128)(2,1)}, bf16[512,256]{1,0:T(8,128)(2,1)S(1)}, u32[]{:S(2)}, u32[]{:S(2)}) %collective-permute-start) | collective-permute-done | bytes 262176 | tf_op jit(solution)/shard_map/ppermute | solution.py:232
  84.7 0.0 copy-start.1
  84.7 1.1 %collective-permute-done.1.refs_2_ = bf16[512,256]{1,0:T(8,128)(2,1)S(1)} collective-permute-done((bf16[512,256]{1,0:T(8,128)(2,1)}, bf16[512,256]{1,0:T(8,128)(2,1)S(1)}, u32[]{:S(2)}, u32[]{:S(2)}) %collective-permute-start.1) | collective-permute-done | bytes 262176 | tf_op jit(solution)/shard_map/ppermute | solution.py:232
  85.8 0.0 copy-start.2
  85.8 4.2 %collective-permute-done.2.refs_3_ = bf16[512,256]{1,0:T(8,128)(2,1)S(1)} collective-permute-done((bf16[512,256]{1,0:T(8,128)(2,1)}, bf16[512,256]{1,0:T(8,128)(2,1)S(1)}, u32[]{:S(2)}, u32[]{:S(2)}) %collective-permute-start.2) | collective-permute-done | bytes 262176 | tf_op jit(solution)/shard_map/ppermute | solution.py:232
  90.0 0.0 copy-start.3
  90.0 0.0 copy-done.1
  90.0 0.0 copy-done.2
  90.0 0.7 copy-done.3
  90.7 2.1 %shard_map.81 = f32[512,256]{1,0:T(8,128)} custom-call(bf16[512,256]{1,0:T(8,128)(2,1)} %get-tuple-element.10.refs_0_, bf16[512,256]{1,0:T(8,128)(2,1)} %copy-done.1, bf16[512,256]{1,0:T(8,128)(2,1)} %copy-done.2, bf16[512,256]{1,0:T(8,128)(2,1)} %copy-done.3), custom_call_target="tpu_custom_call" | custom-call | bytes 1572864 | tf_op jit(solution)/shard_map/pallas_call | solution.py:217
  92.8 2.2 %all-to-all-done.1 = bf16[8,512,128]{2,1,0:T(8,128)(2,1)S(1)} async-done(((bf16[8,512,128]{2,1,0:T(8,128)(2,1)}), bf16[8,512,128]{2,1,0:T(8,128)(2,1)S(1)}, u32[]{:S(2)}, u32[]{:S(2)}) %all-to-all-start.1) | async-done | bytes 1048608 | tf_op jit(solution)/shard_map/all_to_all | solution.py:237
  95.1 1.0 %copy.9 = bf16[1,4096,128]{2,1,0:T(8,128)(2,1)} copy(bf16[1,4096,128]{2,1,0:T(8,128)(2,1)S(1)} %bitcast.5) | data formatting | bytes 2097152
Async XLA Ops:
  36.5 29.2 %all-to-all-start.2 = ((bf16[8,512,128]{2,1,0:T(8,128)(2,1)}), bf16[8,512,128]{2,1,0:T(8,128)(2,1)S(1)}, u32[]{:S(2)}, u32[]{:S(2)}) async-start(bf16[8,512,128]{2,1,0:T(8,128)(2,1)} %bitcast.4), calls=%async_computation.2 | async-start | bytes 2097152 | tf_op jit(solution)/shard_map/all_to_all | solution.py:237
  65.7 3.6 %copy-start = (bf16[8,512,128]{2,1,0:T(8,128)(2,1)}, bf16[8,512,128]{2,1,0:T(8,128)(2,1)S(1)}, u32[]{:S(2)}) copy-start(bf16[8,512,128]{2,1,0:T(8,128)(2,1)S(1)} %all-to-all-done.2.blocks) | copy-start | bytes 3145732
  65.7 29.4 %all-to-all-start.1 = ((bf16[8,512,128]{2,1,0:T(8,128)(2,1)}), bf16[8,512,128]{2,1,0:T(8,128)(2,1)S(1)}, u32[]{:S(2)}, u32[]{:S(2)}) async-start(bf16[8,512,128]{2,1,0:T(8,128)(2,1)} %get-tuple-element.8), calls=%async_computation.1 | async-start | bytes 2097152 | tf_op jit(solution)/shard_map/all_to_all | solution.py:237
  76.5 8.3 %collective-permute-start = (bf16[512,256]{1,0:T(8,128)(2,1)}, bf16[512,256]{1,0:T(8,128)(2,1)S(1)}, u32[]{:S(2)}, u32[]{:S(2)}) collective-permute-start(bf16[512,256]{1,0:T(8,128)(2,1)} %get-tuple-element.11), channel_id=1, source_target_pairs={{0,8},{8,16},{16,24},{24,0},{1,9},{9,17},{17,25},{25,1},{2,10},{10... | collective-permute-start | bytes 786440 | tf_op jit(solution)/shard_map/ppermute | solution.py:232
  76.5 9.4 %collective-permute-start.1 = (bf16[512,256]{1,0:T(8,128)(2,1)}, bf16[512,256]{1,0:T(8,128)(2,1)S(1)}, u32[]{:S(2)}, u32[]{:S(2)}) collective-permute-start(bf16[512,256]{1,0:T(8,128)(2,1)} %get-tuple-element.12), channel_id=1, source_target_pairs={{0,16},{8,24},{16,0},{24,8},{1,17},{9,25},{17,1},{25,9},{2,18},{10... | collective-permute-start | bytes 786440 | tf_op jit(solution)/shard_map/ppermute | solution.py:232
  78.0 12.0 %collective-permute-start.2 = (bf16[512,256]{1,0:T(8,128)(2,1)}, bf16[512,256]{1,0:T(8,128)(2,1)S(1)}, u32[]{:S(2)}, u32[]{:S(2)}) collective-permute-start(bf16[512,256]{1,0:T(8,128)(2,1)} %get-tuple-element.13), channel_id=1, source_target_pairs={{0,24},{8,0},{16,8},{24,16},{1,25},{9,1},{17,9},{25,17},{2,26},{10... | collective-permute-start | bytes 786440 | tf_op jit(solution)/shard_map/ppermute | solution.py:232
  84.7 5.3 %copy-start.1 = (bf16[512,256]{1,0:T(8,128)(2,1)}, bf16[512,256]{1,0:T(8,128)(2,1)S(1)}, u32[]{:S(2)}) copy-start(bf16[512,256]{1,0:T(8,128)(2,1)S(1)} %collective-permute-done.refs_1_) | copy-start | bytes 786436
  85.8 4.2 %copy-start.2 = (bf16[512,256]{1,0:T(8,128)(2,1)}, bf16[512,256]{1,0:T(8,128)(2,1)S(1)}, u32[]{:S(2)}) copy-start(bf16[512,256]{1,0:T(8,128)(2,1)S(1)} %collective-permute-done.1.refs_2_) | copy-start | bytes 786436
  90.0 0.7 copy-start.3

commit v3 on v1

--- a/solution.py
+++ b/solution.py
@@ -139,27 +139,52 @@
     rows_loop(rows, body)
 
 
-def gate_kernel(where, gate, upper, *outs):
+def piece_at(ref, where, k, rows):
+    start = pl.multiple_of(lax.bitwise_xor(where[0], k) * rows, rows)
+    return ref.at[pl.ds(start, rows), :]
+
+
+def gate_kernel(order, where, gate, upper, *refs):
+    outs, (left, right, product, sems, out_sems) = refs[: len(order)], refs[len(order) :]
     rows = outs[0].shape[0]
-    for k, out in enumerate(outs):
-        start = pl.multiple_of(lax.rem(where[0] + k, len(outs)) * rows, rows)
-        product = gate[pl.ds(start, rows), :].astype(jnp.float32) * upper[pl.ds(start, rows), :].astype(jnp.float32)
-        out[...] = product.astype(jnp.bfloat16)
-
-
-def pick_kernel(where, whole, *outs):
-    rows = outs[0].shape[0]
-    for k, out in enumerate(outs):
-        start = pl.multiple_of(lax.rem(where[0] + k, len(outs)) * rows, rows)
-        out[...] = whole[pl.ds(start, rows), :]
-
-
-def place_kernel(where, *refs):
-    out = refs[-1]
-    rows, count = refs[0].shape[0], len(refs) - 1
-    for k, ref in enumerate(refs[:-1]):
-        start = pl.multiple_of(lax.rem(where[0] + count - k, count) * rows, rows)
-        out[pl.ds(start, rows), :] = ref[...]
+    loads = []
+    for i, k in enumerate(order):
+        pair = (
+            pltpu.make_async_copy(piece_at(gate, where, k, rows), left.at[i], sems.at[0, i]),
+            pltpu.make_async_copy(piece_at(upper, where, k, rows), right.at[i], sems.at[1, i]),
+        )
+        for copy in pair:
+            copy.start()
+        loads.append(pair)
+    stores = []
+    for i, out in enumerate(outs):
+        for copy in loads[i]:
+            copy.wait()
+        product[i] = (left[i].astype(jnp.float32) * right[i].astype(jnp.float32)).astype(jnp.bfloat16)
+        stores.append(pltpu.make_async_copy(product.at[i], out, out_sems.at[i]))
+        stores[-1].start()
+    for copy in stores:
+        copy.wait()
+
+
+def pick_kernel(order, where, whole, *refs):
+    outs, sems = refs[:-1], refs[-1]
+    copies = []
+    for i, k in enumerate(order):
+        copies.append(pltpu.make_async_copy(piece_at(whole, where, k, outs[0].shape[0]), outs[i], sems.at[i]))
+        copies[-1].start()
+    for copy in copies:
+        copy.wait()
+
+
+def place_kernel(order, where, *refs):
+    pieces, whole, sems = refs[: len(order)], refs[-2], refs[-1]
+    copies = []
+    for i, k in enumerate(order):
+        copies.append(pltpu.make_async_copy(pieces[i], piece_at(whole, where, k, pieces[i].shape[0]), sems.at[i]))
+        copies[-1].start()
+    for copy in copies:
+        copy.wait()
 
 
 def taps_kernel(taps, forward, out, mid):
@@ -169,10 +194,10 @@
         out[r] = spectrum(mid, forward, r, width).astype(out.dtype)
 
 
-def ordered(where, refs, held):
+def ordered(order, where, refs, held):
     span = refs[0].shape[1]
-    for k, ref in enumerate(refs):
-        start = pl.multiple_of(lax.rem(where[0] + len(refs) - k, len(refs)) * span, span)
+    for k, ref in zip(order, refs):
+        start = pl.multiple_of(lax.bitwise_xor(where[0], k) * span, span)
         held[:, pl.ds(start, span)] = ref[...]
 
 
@@ -187,12 +212,11 @@
     return store
 
 
-def back_kernel(count, where, *refs):
-    blocks, (taps_spec, forward, backward) = refs[:count], refs[count : count + 3]
-    outs, grad_spec = refs[count + 3 : 2 * count + 3], refs[2 * count + 3]
-    held, mid, wide = refs[2 * count + 4 :]
+def back_kernel(order, where, *refs):
+    blocks, refs = refs[: len(order)], refs[len(order) :]
+    taps_spec, forward, backward, *outs, grad_spec, held, mid, wide = refs
     rows, width = held.shape[0], held.shape[1] // BLOCKS
-    ordered(where, blocks, held)
+    ordered(order, where, blocks, held)
     split_rows(block_of(held, width), mid, rows, width)
     for r in range(GROUPS):
         grad = spectrum(mid, forward, r, width)
@@ -203,17 +227,16 @@
         invert_group(product.astype(jnp.bfloat16), backward, r, width, wide)
     merge_rows(wide, block_into(held, width), rows, width)
     span = outs[0].shape[1]
-    for k, out in enumerate(outs):
-        start = pl.multiple_of(lax.rem(where[0] + k, count) * span, span)
+    for k, out in zip(order, outs):
+        start = pl.multiple_of(lax.bitwise_xor(where[0], k) * span, span)
         out[...] = held[:, pl.ds(start, span)]
 
 
-def cross_kernel(count, shares, where, *refs):
-    blocks, (grad_spec, forward, backward) = refs[:count], refs[count : count + 3]
-    outs = refs[count + 3 : count + 3 + shares]
-    held, mid, wide = refs[count + 3 + shares :]
+def cross_kernel(order, where, *refs):
+    blocks, refs = refs[: len(order)], refs[len(order) :]
+    grad_spec, forward, backward, *outs, held, mid, wide = refs
     rows, width = held.shape[0], held.shape[1] // BLOCKS
-    ordered(where, blocks, held)
+    ordered(order, where, blocks, held)
     split_rows(block_of(held, width), mid, rows, width)
     for r in range(GROUPS):
         signal = spectrum(mid, forward, r, width)
@@ -222,9 +245,9 @@
         product = jnp.concatenate([gr * xr + gi * xi, gi * xr - gr * xi], axis=1)
         invert_group(product.astype(jnp.bfloat16), backward, r, width, wide)
     merge_rows(wide, block_into(held, width), rows, width)
-    part = held.shape[1] // shares
+    part = held.shape[1] // len(outs)
     for k, out in enumerate(outs):
-        start = pl.multiple_of(lax.rem(where[1] + k, shares) * part, part)
+        start = pl.multiple_of(lax.bitwise_xor(where[1], k) * part, part)
         out[...] = held[:, pl.ds(start, part)]
 
 
@@ -235,8 +258,9 @@
     refs[-1][...] = total * scale
 
 
-def call(kernel, operands, outs, scratch=(), scalar=True, flops=0):
-    specs = [pl.BlockSpec(memory_space=pltpu.VMEM)] * len(operands)
+def call(kernel, operands, outs, scratch=(), scalar=True, flops=0, stream=False):
+    space = pl.ANY if stream else pltpu.VMEM
+    specs = [pl.BlockSpec(memory_space=space)] * len(operands)
     if scalar:
         specs[0] = pl.BlockSpec(memory_space=pltpu.SMEM)
     size = sum(math.prod(o.shape) * o.dtype.itemsize for o in list(operands) + list(outs))
@@ -244,18 +268,22 @@
         kernel,
         out_shape=list(outs),
         in_specs=specs,
-        out_specs=[pl.BlockSpec(memory_space=pltpu.VMEM)] * len(outs),
+        out_specs=[pl.BlockSpec(memory_space=space)] * len(outs),
         scratch_shapes=list(scratch),
         compiler_params=pltpu.CompilerParams(vmem_limit_bytes=LIMIT),
         cost_estimate=pl.CostEstimate(flops=flops, bytes_accessed=size, transcendentals=0),
     )(*operands)
 
 
-def exchange(pieces, axis, size):
-    moved = [pieces[0]]
-    for k in range(1, size):
-        pairs = [(i, (i + k) % size) for i in range(size)]
-        moved.append(lax.ppermute(pieces[k], axis, pairs))
+def far_first(size):
+    half = size // 2
+    return [k for pair in zip(range(half, size), [*range(1, half), 0]) for k in pair]
+
+
+def exchange(pieces, order, axis, size):
+    moved = []
+    for k, piece in zip(order, pieces):
+        moved.append(lax.ppermute(piece, axis, [(i, i ^ k) for i in range(size)]) if k else piece)
     return moved
 
 
@@ -264,38 +292,54 @@
     channels, span = saved_input.shape[1:]
     rows, length = long_filter.shape
     width = length // BLOCKS
+    order = far_first(count)
     where = jnp.stack([lax.axis_index("ctx"), lax.axis_index("dp")]).astype(jnp.int32)
     forward, backward = (jnp.asarray(t) for t in transform_tables(width))
     half, full = jnp.bfloat16, jnp.float32
     piece = jax.ShapeDtypeStruct((rows, span), half)
+    blocks = jax.ShapeDtypeStruct((count, rows, span), half)
     spec = jax.ShapeDtypeStruct((GROUPS, rows, 2 * width), half)
     held = pltpu.VMEM((rows, length), half)
     mid = pltpu.VMEM((GROUPS, rows, 2 * width), half)
     wide = pltpu.VMEM((GROUPS, rows, 2 * width), full)
+    slots = pltpu.VMEM(blocks.shape, half)
+    sems = pltpu.SemaphoreType.DMA
     work = 2 * GROUPS * rows * 4 * width * width
 
-    grad_pieces = call(gate_kernel, [where, out_gate[0], grad_out[0]], [piece] * count)
-    grad_blocks = exchange(grad_pieces, "ctx", count)
-    input_pieces = call(pick_kernel, [where, saved_input[0]], [piece] * count)
-    input_blocks = exchange(input_pieces, "ctx", count)
+    grad_pieces = call(
+        functools.partial(gate_kernel, order),
+        [where, out_gate[0], grad_out[0]],
+        [piece] * count,
+        [slots, slots, slots, sems((2, count)), sems((count,))],
+        stream=True,
+    )
+    grad_blocks = exchange(grad_pieces, order, "ctx", count)
+    input_pieces = call(
+        functools.partial(pick_kernel, order),
+        [where, saved_input[0]],
+        [piece] * count,
+        [sems((count,))],
+        stream=True,
+    )
+    input_blocks = exchange(input_pieces, order, "ctx", count)
     (taps_spec,) = call(taps_kernel, [long_filter, forward], [spec], [mid], scalar=False, flops=work)
     *back, grad_spec = call(
-        functools.partial(back_kernel, count),
+        functools.partial(back_kernel, order),
         [where, *grad_blocks, taps_spec, forward, backward],
         [piece] * count + [spec],
         [held, mid, wide],
         flops=2 * work,
     )
-    back_blocks = exchange(back, "ctx", count)
+    back_blocks = exchange(back, order, "ctx", count)
     share = jax.ShapeDtypeStruct((rows, length // shares), half)
     cross = call(
-        functools.partial(cross_kernel, count, shares),
+        functools.partial(cross_kernel, order),
         [where, *input_blocks, grad_spec, forward, backward],
         [share] * shares,
         [held, mid, wide],
         flops=2 * work,
     )
-    cross_blocks = exchange(cross, "dp", shares)
+    cross_blocks = exchange(cross, range(shares), "dp", shares)
     scale = 1.0 / math.sqrt(shares * length)
     (grad_filter,) = call(
         functools.partial(sum_kernel, scale),
@@ -303,7 +347,13 @@
         [jax.ShapeDtypeStruct((rows, length // shares), full)],
         scalar=False,
     )
-    (grad_input,) = call(place_kernel, [where, *back_blocks], [jax.ShapeDtypeStruct((channels, span), half)])
+    (grad_input,) = call(
+        functools.partial(place_kernel, order),
+        [where, *back_blocks],
+        [jax.ShapeDtypeStruct((channels, span), half)],
+        [sems((count,))],
+        stream=True,
+    )
     return (grad_input[None], grad_filter)
 
 

time: 99.5 us -> 153 us (1.54)
  Pallas kernels: 29.8 us -> 92.8 us
  starting transfers between devices: 49.4 us -> 36.2 us
  waiting for transfers between devices: 16.4 us -> 20.5 us
    pallas_call x7, Pallas kernels: 29.8 us -> 92.8 us  [call(): pl.pallas_call(kernel, out_shape=list(outs), in_specs=specs, out_specs=[p...]
    ppermute x24, starting transfers between devices: 49.4 us -> 36.2 us  [exchange(): lax.ppermute(piece, axis, [(i, i ^ k) for i in range(size)])]
    ppermute x24, waiting for transfers between devices: 16.4 us -> 20.5 us  [exchange(): lax.ppermute(piece, axis, [(i, i ^ k) for i in range(size)])]
  transfers between devices with their start and end apart: 24 -> 24, of which waited for: 4 -> 5; matrix products, arithmetic and copies ran while one was open for 0% -> 0% of each run, Pallas kernels for 25% -> 57%
where the time goes in v3:
time: 153 us
  Pallas kernels  92.8 us (61%)
  starting transfers between devices  36.2 us (24%)
  waiting for transfers between devices  20.5 us (13%)
  local copies, waits for them, and re-layouts  1.54 us (1%)
    pallas_call x7, Pallas kernels, call(): pl.pallas_call(kernel, out_shape=list(outs), in_specs=specs, out_specs=[p...  92.8 us
    ppermute x24, starting transfers between devices, exchange(): lax.ppermute(piece, axis, [(i, i ^ k) for i in range(size)])  36.2 us
    ppermute x24, waiting for transfers between devices, exchange(): lax.ppermute(piece, axis, [(i, i ^ k) for i in range(size)])  20.5 us
  transfers between devices with their start and end apart: 24, of which 5 were waited for; matrix products, arithmetic and copies ran while one was open for 0% of the time, Pallas kernels for 57%

profile of v3, /device:TPU:0, one launch (start us, length us, event | category | flops | bytes accessed | tf_op | source)
XLA Modules:
  0.0 152.6 jit_solution(12959235647275784985)
XLA Ops:
  0.6 0.6 pad_add_fusion.where
  1.3 3.1 %shard_map.77 = (bf16[512,128]{1,0:T(8,128)(2,1)}, bf16[512,128]{1,0:T(8,128)(2,1)}, bf16[512,128]{1,0:T(8,128)(2,1)}, bf16[512,128]{1,0:T(8,128)(2,1)}, bf16[51...) custom-call(s32[2]{0:T(128)} %pad_add_fusion.where, ...), custom_call_target="tpu_custom_call" | custom-call | bytes 3145736 | tf_op jit(solution)/shard_map/pallas_call | solution.py:267
  4.4 4.1 %collective-permute-start = (bf16[512,128]{1,0:T(8,128)(2,1)}, bf16[512,128]{1,0:T(8,128)(2,1)S(1)}, u32[]{:S(2)}, u32[]{:S(2)}) collective-permute-start(bf16[512,128]{1,0:T(8,128)(2,1)} %get-tuple-element.31), channel_id=1, source_target_pairs={{0,4},{1,5},{2,6},{3,7},{4,0},{5,1},{6,2},{7,3},{8,12},{9,13},{10,... | collective-permute-start | bytes 393224 | tf_op jit(solution)/shard_map/ppermute | solution.py:286
  8.5 1.5 collective-permute-start.1
  10.1 0.0 collective-permute-start.2
  10.1 1.8 %collective-permute-start.3 = (bf16[512,128]{1,0:T(8,128)(2,1)}, bf16[512,128]{1,0:T(8,128)(2,1)S(1)}, u32[]{:S(2)}, u32[]{:S(2)}) collective-permute-start(bf16[512,128]{1,0:T(8,128)(2,1)} %get-tuple-element.34), channel_id=1, source_target_pairs={{0,2},{1,3},{2,0},{3,1},{4,6},{5,7},{6,4},{7,5},{8,10},{9,11},{10,... | collective-permute-start | bytes 393224 | tf_op jit(solution)/shard_map/ppermute | solution.py:286
  11.9 2.5 %collective-permute-start.4 = (bf16[512,128]{1,0:T(8,128)(2,1)}, bf16[512,128]{1,0:T(8,128)(2,1)S(1)}, u32[]{:S(2)}, u32[]{:S(2)}) collective-permute-start(bf16[512,128]{1,0:T(8,128)(2,1)} %get-tuple-element.35), channel_id=1, source_target_pairs={{0,6},{1,7},{2,4},{3,5},{4,2},{5,3},{6,0},{7,1},{8,14},{9,15},{10,... | collective-permute-start | bytes 393224 | tf_op jit(solution)/shard_map/ppermute | solution.py:286
  14.4 33.6 %shard_map.81 = (bf16[512,128]{1,0:T(8,128)(2,1)}, bf16[512,128]{1,0:T(8,128)(2,1)}, bf16[512,128]{1,0:T(8,128)(2,1)}, bf16[512,128]{1,0:T(8,128)(2,1)}, bf16[51...) custom-call(s32[2]{0:T(128)} %pad_add_fusion.where, ...), custom_call_target="tpu_custom_call" | custom-call | bytes 2097160 | tf_op jit(solution)/shard_map/pallas_call | solution.py:267
  48.0 0.0 collective-permute-done.refs_0_
  48.0 0.0 copy-start.5
  48.0 1.7 %collective-permute-start.5 = (bf16[512,128]{1,0:T(8,128)(2,1)}, bf16[512,128]{1,0:T(8,128)(2,1)S(1)}, u32[]{:S(2)}, u32[]{:S(2)}) collective-permute-start(bf16[512,128]{1,0:T(8,128)(2,1)} %get-tuple-element.36), channel_id=1, source_target_pairs={{0,3},{1,2},{2,1},{3,0},{4,7},{5,6},{6,5},{7,4},{8,11},{9,10},{10,... | collective-permute-start | bytes 393224 | tf_op jit(solution)/shard_map/ppermute | solution.py:286
  49.7 0.0 collective-permute-done.1.refs_1_
  49.7 0.8 collective-permute-start.6
  50.6 0.0 collective-permute-done.2.refs_2_
  50.6 1.9 %collective-permute-start.14 = (bf16[512,128]{1,0:T(8,128)(2,1)}, bf16[512,128]{1,0:T(8,128)(2,1)S(1)}, u32[]{:S(2)}, u32[]{:S(2)}) collective-permute-start(bf16[512,128]{1,0:T(8,128)(2,1)} %get-tuple-element.47), channel_id=1, source_target_pairs={{0,4},{1,5},{2,6},{3,7},{4,0},{5,1},{6,2},{7,3},{8,12},{9,13},{10,... | collective-permute-start | bytes 393224 | tf_op jit(solution)/shard_map/ppermute | solution.py:286
  52.5 0.0 collective-permute-done.3.refs_3_
  52.5 1.5 collective-permute-start.15
  54.0 0.0 collective-permute-done.4.refs_4_
  54.0 1.0 collective-permute-start.16
  55.0 0.7 collective-permute-done.5.refs_5_
  55.7 2.3 %collective-permute-start.17 = (bf16[512,128]{1,0:T(8,128)(2,1)}, bf16[512,128]{1,0:T(8,128)(2,1)S(1)}, u32[]{:S(2)}, u32[]{:S(2)}) collective-permute-start(bf16[512,128]{1,0:T(8,128)(2,1)} %get-tuple-element.50), channel_id=1, source_target_pairs={{0,2},{1,3},{2,0},{3,1},{4,6},{5,7},{6,4},{7,5},{8,10},{9,11},{10,... | collective-permute-start | bytes 393224 | tf_op jit(solution)/shard_map/ppermute | solution.py:286
  58.0 1.1 collective-permute-done.6.refs_6_
  59.1 1.7 %collective-permute-start.18 = (bf16[512,128]{1,0:T(8,128)(2,1)}, bf16[512,128]{1,0:T(8,128)(2,1)S(1)}, u32[]{:S(2)}, u32[]{:S(2)}) collective-permute-start(bf16[512,128]{1,0:T(8,128)(2,1)} %get-tuple-element.51), channel_id=1, source_target_pairs={{0,6},{1,7},{2,4},{3,5},{4,2},{5,3},{6,0},{7,1},{8,14},{9,15},{10,... | collective-permute-start | bytes 393224 | tf_op jit(solution)/shard_map/ppermute | solution.py:286
  60.8 9.5 %collective-permute-done.14.refs_0_ = bf16[512,128]{1,0:T(8,128)(2,1)S(1)} collective-permute-done((bf16[512,128]{1,0:T(8,128)(2,1)}, bf16[512,128]{1,0:T(8,128)(2,1)S(1)}, u32[]{:S(2)}, u32[]{:S(2)}) %collective-permute-start.14) | collective-permute-done | bytes 131104 | tf_op jit(solution)/shard_map/ppermute | solution.py:286
  70.3 0.0 collective-permute-start.19
  70.3 0.0 collective-permute-done.15.refs_1_
  70.3 0.0 copy-start.4
  70.3 2.1 %collective-permute-start.20 = (bf16[512,128]{1,0:T(8,128)(2,1)}, bf16[512,128]{1,0:T(8,128)(2,1)S(1)}, u32[]{:S(2)}, u32[]{:S(2)}) collective-permute-start(bf16[512,128]{1,0:T(8,128)(2,1)} %get-tuple-element.53), channel_id=1, source_target_pairs={{0,7},{1,6},{2,5},{3,4},{4,3},{5,2},{6,1},{7,0},{8,15},{9,14},{10,... | collective-permute-start | bytes 393224 | tf_op jit(solution)/shard_map/ppermute | solution.py:286
  72.4 4.8 %shard_map.78.refs_8_ = bf16[9,512,256]{2,1,0:T(8,128)(2,1)} custom-call(f32[512,1024]{1,0:T(8,128)} %taps.1, bf16[9,256,256]{2,1,0:T(8,128)(2,1)} %constant.12.clone.forward.refs_9_), custom_call_target="tpu_custom_call" | custom-call | flops 603979776 | bytes 5636096 | tf_op jit(solution)/shard_map/pallas_call | solution.py:267
  77.2 0.0 copy-done.7
  77.3 8.2 %shard_map.79 = (bf16[512,128]{1,0:T(8,128)(2,1)}, bf16[512,128]{1,0:T(8,128)(2,1)}, bf16[512,128]{1,0:T(8,128)(2,1)}, bf16[512,128]{1,0:T(8,128)(2,1)}, bf16[51...) custom-call(s32[2]{0:T(128)} %pad_add_fusion.where, ...), custom_call_target="tpu_custom_call" | custom-call | flops 1207959552 | bytes 9175048 | tf_op jit(solution)/shard_map/pallas_call | solution.py:267
  85.5 0.0 collective-permute-done.16.refs_2_
  85.5 0.0 copy-start.8
  85.5 2.0 %collective-permute-start.10 = (bf16[512,128]{1,0:T(8,128)(2,1)}, bf16[512,128]{1,0:T(8,128)(2,1)S(1)}, u32[]{:S(2)}, u32[]{:S(2)}) collective-permute-start(bf16[512,128]{1,0:T(8,128)(2,1)} %get-tuple-element.42), channel_id=1, source_target_pairs={{0,2},{1,3},{2,0},{3,1},{4,6},{5,7},{6,4},{7,5},{8,10},{9,11},{10,... | collective-permute-start | bytes 393224 | tf_op jit(solution)/shard_map/ppermute | solution.py:286
  87.5 0.0 collective-permute-done.17.refs_3_
  87.5 1.9 %collective-permute-start.11 = (bf16[512,128]{1,0:T(8,128)(2,1)}, bf16[512,128]{1,0:T(8,128)(2,1)S(1)}, u32[]{:S(2)}, u32[]{:S(2)}) collective-permute-start(bf16[512,128]{1,0:T(8,128)(2,1)} %get-tuple-element.43), channel_id=1, source_target_pairs={{0,6},{1,7},{2,4},{3,5},{4,2},{5,3},{6,0},{7,1},{8,14},{9,15},{10,... | collective-permute-start | bytes 393224 | tf_op jit(solution)/shard_map/ppermute | solution.py:286
  89.4 0.0 collective-permute-done.18.refs_4_
  89.4 1.1 collective-permute-start.12
  90.5 0.0 collective-permute-done.19.refs_5_
  90.5 1.9 %collective-permute-start.13 = (bf16[512,128]{1,0:T(8,128)(2,1)}, bf16[512,128]{1,0:T(8,128)(2,1)S(1)}, u32[]{:S(2)}, u32[]{:S(2)}) collective-permute-start(bf16[512,128]{1,0:T(8,128)(2,1)} %get-tuple-element.45), channel_id=1, source_target_pairs={{0,7},{1,6},{2,5},{3,4},{4,3},{5,2},{6,1},{7,0},{8,15},{9,14},{10,... | collective-permute-start | bytes 393224 | tf_op jit(solution)/shard_map/ppermute | solution.py:286
  92.3 0.0 collective-permute-done.20.refs_6_
  92.3 1.5 collective-permute-start.7
  93.9 7.3 %shard_map.82 = (bf16[512,256]{1,0:T(8,128)(2,1)}, bf16[512,256]{1,0:T(8,128)(2,1)}, bf16[512,256]{1,0:T(8,128)(2,1)}, bf16[512,256]{1,0:T(8,128)(2,1)}) custom-call(s32[2]{0:T(128)} %pad_add_fusion.where, bf16[512,128]{1,0:T(8,128)(2,1)} %copy-done.3, bf16[512,128]{1,0:T(8,128)(2,1)} %copy-done.4, bf16[512,128]{1,0:T(8,128)(2,1)} %copy-done.8, ...), custom_call_target="tpu_custom_call" | custom-call | flops 1207959552 | bytes 6815752 | tf_op jit(solution)/shard_map/pallas_call | solution.py:267
  101.2 0.0 collective-permute-done.10.refs_3_
  101.2 0.1 collective-permute-start.21
  101.3 0.0 collective-permute-done.11.refs_4_
  101.3 1.6 %collective-permute-start.22 = (bf16[512,256]{1,0:T(8,128)(2,1)}, bf16[512,256]{1,0:T(8,128)(2,1)S(1)}, u32[]{:S(2)}, u32[]{:S(2)}) collective-permute-start(bf16[512,256]{1,0:T(8,128)(2,1)} %get-tuple-element.58), channel_id=1, source_target_pairs={{0,16},{8,24},{16,0},{24,8},{1,17},{9,25},{17,1},{25,9},{2,18},{10... | collective-permute-start | bytes 786440 | tf_op jit(solution)/shard_map/ppermute | solution.py:286
  102.9 0.0 collective-permute-done.12.refs_5_
  102.9 0.3 collective-permute-start.23
  103.1 0.0 collective-permute-done.13.refs_6_
  103.2 2.5 %collective-permute-start.8 = (bf16[512,128]{1,0:T(8,128)(2,1)S(1)}, bf16[512,128]{1,0:T(8,128)(2,1)S(1)}, u32[]{:S(2)}, u32[]{:S(2)}) collective-permute-start(bf16[512,128]{1,0:T(8,128)(2,1)S(1)} %copy-done.25), channel_id=1, source_target_pairs={{0,1},{1,0},{2,3},{3,2},{4,5},{5,4},{6,7},{7,6},{8,9},{9,8},{10,11... | collective-permute-start | bytes 393224 | tf_op jit(solution)/shard_map/ppermute | solution.py:286
  105.7 0.0 collective-permute-done.7.refs_0_
  105.7 0.6 collective-permute-start.9
  106.2 3.5 %collective-permute-done.8.refs_1_ = bf16[512,128]{1,0:T(8,128)(2,1)S(1)} collective-permute-done((bf16[512,128]{1,0:T(8,128)(2,1)S(1)}, bf16[512,128]{1,0:T(8,128)(2,1)S(1)}, u32[]{:S(2)}, u32[]{:S(2)}) %collective-permute-start.8) | collective-permute-done | bytes 131104 | tf_op jit(solution)/shard_map/ppermute | solution.py:286
  109.7 5.6 %collective-permute-done.9.refs_2_ = bf16[512,128]{1,0:T(8,128)(2,1)S(1)} collective-permute-done((bf16[512,128]{1,0:T(8,128)(2,1)S(1)}, bf16[512,128]{1,0:T(8,128)(2,1)S(1)}, u32[]{:S(2)}, u32[]{:S(2)}) %collective-permute-start.9) | collective-permute-done | bytes 131104 | tf_op jit(solution)/shard_map/ppermute | solution.py:286
  115.4 0.6 copy-done.23
  116.0 33.6 %shard_map.80 = bf16[4096,128]{1,0:T(8,128)(2,1)} custom-call(s32[2]{0:T(128)} %pad_add_fusion.where, bf16[512,128]{1,0:T(8,128)(2,1)} %copy-done.21, bf16[512,128]{1,0:T(8,128)(2,1)} %copy-done.22, bf16[512,128]{1,0:T(8,128)(2,1)} %copy-done.23, bf16[512,128]{1,0:T(8,128)(2,1)} %copy-done.10, bf16[512,128]{1,0:T(8,128)(2,1)} %copy-done.13, ...), custom_call_target="tpu_custom_call" | custom-call | bytes 2097160 | tf_op jit(solution)/shard_map/pallas_call | solution.py:267
  149.6 0.0 collective-permute-done.21.refs_1_
  149.6 0.0 collective-permute-done.22.refs_2_
  149.6 0.0 collective-permute-done.23.refs_3_
  149.6 0.7 copy-done
  150.3 0.1 copy-done.1
  150.4 0.1 copy-done.2
  150.5 2.1 %shard_map.83 = f32[512,256]{1,0:T(8,128)} custom-call(bf16[512,256]{1,0:T(8,128)(2,1)} %get-tuple-element.56.refs_0_, bf16[512,256]{1,0:T(8,128)(2,1)} %copy-done, bf16[512,256]{1,0:T(8,128)(2,1)} %copy-done.1, bf16[512,256]{1,0:T(8,128)(2,1)} %copy-done.2), custom_call_target="tpu_custom_call" | custom-call | bytes 1572864 | tf_op jit(solution)/shard_map/pallas_call | solution.py:267
  (44 shorter events, 0.1 us)
Async XLA Ops:
  4.4 43.6 %collective-permute-start = (bf16[512,128]{1,0:T(8,128)(2,1)}, bf16[512,128]{1,0:T(8,128)(2,1)S(1)}, u32[]{:S(2)}, u32[]{:S(2)}) collective-permute-start(bf16[512,128]{1,0:T(8,128)(2,1)} %get-tuple-element.31), channel_id=1, source_target_pairs={{0,4},{1,5},{2,6},{3,7},{4,0},{5,1},{6,2},{7,3},{8,12},{9,13},{10,... | collective-permute-start | bytes 393224 | tf_op jit(solution)/shard_map/ppermute | solution.py:286
  8.5 41.2 %collective-permute-start.1 = (bf16[512,128]{1,0:T(8,128)(2,1)}, bf16[512,128]{1,0:T(8,128)(2,1)S(1)}, u32[]{:S(2)}, u32[]{:S(2)}) collective-permute-start(bf16[512,128]{1,0:T(8,128)(2,1)} %get-tuple-element.32), channel_id=1, source_target_pairs={{0,1},{1,0},{2,3},{3,2},{4,5},{5,4},{6,7},{7,6},{8,9},{9,8},{10,11... | collective-permute-start | bytes 393224 | tf_op jit(solution)/shard_map/ppermute | solution.py:286
  10.1 40.5 %collective-permute-start.2 = (bf16[512,128]{1,0:T(8,128)(2,1)}, bf16[512,128]{1,0:T(8,128)(2,1)S(1)}, u32[]{:S(2)}, u32[]{:S(2)}) collective-permute-start(bf16[512,128]{1,0:T(8,128)(2,1)} %get-tuple-element.33), channel_id=1, source_target_pairs={{0,5},{1,4},{2,7},{3,6},{4,1},{5,0},{6,3},{7,2},{8,13},{9,12},{10,... | collective-permute-start | bytes 393224 | tf_op jit(solution)/shard_map/ppermute | solution.py:286
  10.1 42.4 %collective-permute-start.3 = (bf16[512,128]{1,0:T(8,128)(2,1)}, bf16[512,128]{1,0:T(8,128)(2,1)S(1)}, u32[]{:S(2)}, u32[]{:S(2)}) collective-permute-start(bf16[512,128]{1,0:T(8,128)(2,1)} %get-tuple-element.34), channel_id=1, source_target_pairs={{0,2},{1,3},{2,0},{3,1},{4,6},{5,7},{6,4},{7,5},{8,10},{9,11},{10,... | collective-permute-start | bytes 393224 | tf_op jit(solution)/shard_map/ppermute | solution.py:286
  11.9 42.1 %collective-permute-start.4 = (bf16[512,128]{1,0:T(8,128)(2,1)}, bf16[512,128]{1,0:T(8,128)(2,1)S(1)}, u32[]{:S(2)}, u32[]{:S(2)}) collective-permute-start(bf16[512,128]{1,0:T(8,128)(2,1)} %get-tuple-element.35), channel_id=1, source_target_pairs={{0,6},{1,7},{2,4},{3,5},{4,2},{5,3},{6,0},{7,1},{8,14},{9,15},{10,... | collective-permute-start | bytes 393224 | tf_op jit(solution)/shard_map/ppermute | solution.py:286
  48.0 29.2 %copy-start.5 = (bf16[512,128]{1,0:T(8,128)(2,1)}, bf16[512,128]{1,0:T(8,128)(2,1)S(1)}, u32[]{:S(2)}) copy-start(bf16[512,128]{1,0:T(8,128)(2,1)S(1)} %collective-permute-done.refs_0_) | copy-start | bytes 393220
  48.0 7.7 %collective-permute-start.5 = (bf16[512,128]{1,0:T(8,128)(2,1)}, bf16[512,128]{1,0:T(8,128)(2,1)S(1)}, u32[]{:S(2)}, u32[]{:S(2)}) collective-permute-start(bf16[512,128]{1,0:T(8,128)(2,1)} %get-tuple-element.36), channel_id=1, source_target_pairs={{0,3},{1,2},{2,1},{3,0},{4,7},{5,6},{6,5},{7,4},{8,11},{9,10},{10,... | collective-permute-start | bytes 393224 | tf_op jit(solution)/shard_map/ppermute | solution.py:286
  49.7 27.5 %copy-start.6 = (bf16[512,128]{1,0:T(8,128)(2,1)}, bf16[512,128]{1,0:T(8,128)(2,1)S(1)}, u32[]{:S(2)}) copy-start(bf16[512,128]{1,0:T(8,128)(2,1)S(1)} %collective-permute-done.1.refs_1_) | copy-start | bytes 393220
  49.7 9.4 %collective-permute-start.6 = (bf16[512,128]{1,0:T(8,128)(2,1)}, bf16[512,128]{1,0:T(8,128)(2,1)S(1)}, u32[]{:S(2)}, u32[]{:S(2)}) collective-permute-start(bf16[512,128]{1,0:T(8,128)(2,1)} %get-tuple-element.37), channel_id=1, source_target_pairs={{0,7},{1,6},{2,5},{3,4},{4,3},{5,2},{6,1},{7,0},{8,15},{9,14},{10,... | collective-permute-start | bytes 393224 | tf_op jit(solution)/shard_map/ppermute | solution.py:286
  50.6 26.7 %copy-start.7 = (bf16[512,128]{1,0:T(8,128)(2,1)}, bf16[512,128]{1,0:T(8,128)(2,1)S(1)}, u32[]{:S(2)}) copy-start(bf16[512,128]{1,0:T(8,128)(2,1)S(1)} %collective-permute-done.2.refs_2_) | copy-start | bytes 393220
  50.6 19.7 %collective-permute-start.14 = (bf16[512,128]{1,0:T(8,128)(2,1)}, bf16[512,128]{1,0:T(8,128)(2,1)S(1)}, u32[]{:S(2)}, u32[]{:S(2)}) collective-permute-start(bf16[512,128]{1,0:T(8,128)(2,1)} %get-tuple-element.47), channel_id=1, source_target_pairs={{0,4},{1,5},{2,6},{3,7},{4,0},{5,1},{6,2},{7,3},{8,12},{9,13},{10,... | collective-permute-start | bytes 393224 | tf_op jit(solution)/shard_map/ppermute | solution.py:286
  52.5 24.7 %copy-start.9 = (bf16[512,128]{1,0:T(8,128)(2,1)}, bf16[512,128]{1,0:T(8,128)(2,1)S(1)}, u32[]{:S(2)}) copy-start(bf16[512,128]{1,0:T(8,128)(2,1)S(1)} %collective-permute-done.3.refs_3_) | copy-start | bytes 393220
  52.5 17.8 %collective-permute-start.15 = (bf16[512,128]{1,0:T(8,128)(2,1)}, bf16[512,128]{1,0:T(8,128)(2,1)S(1)}, u32[]{:S(2)}, u32[]{:S(2)}) collective-permute-start(bf16[512,128]{1,0:T(8,128)(2,1)} %get-tuple-element.48), channel_id=1, source_target_pairs={{0,1},{1,0},{2,3},{3,2},{4,5},{5,4},{6,7},{7,6},{8,9},{9,8},{10,11... | collective-permute-start | bytes 393224 | tf_op jit(solution)/shard_map/ppermute | solution.py:286
  54.0 23.2 %copy-start.11 = (bf16[512,128]{1,0:T(8,128)(2,1)}, bf16[512,128]{1,0:T(8,128)(2,1)S(1)}, u32[]{:S(2)}) copy-start(bf16[512,128]{1,0:T(8,128)(2,1)S(1)} %collective-permute-done.4.refs_4_) | copy-start | bytes 393220
  54.0 31.5 %collective-permute-start.16 = (bf16[512,128]{1,0:T(8,128)(2,1)}, bf16[512,128]{1,0:T(8,128)(2,1)S(1)}, u32[]{:S(2)}, u32[]{:S(2)}) collective-permute-start(bf16[512,128]{1,0:T(8,128)(2,1)} %get-tuple-element.49), channel_id=1, source_target_pairs={{0,5},{1,4},{2,7},{3,6},{4,1},{5,0},{6,3},{7,2},{8,13},{9,12},{10,... | collective-permute-start | bytes 393224 | tf_op jit(solution)/shard_map/ppermute | solution.py:286
  55.7 21.5 %copy-start.17 = (bf16[512,128]{1,0:T(8,128)(2,1)}, bf16[512,128]{1,0:T(8,128)(2,1)S(1)}, u32[]{:S(2)}) copy-start(bf16[512,128]{1,0:T(8,128)(2,1)S(1)} %collective-permute-done.5.refs_5_) | copy-start | bytes 393220
  55.7 31.8 %collective-permute-start.17 = (bf16[512,128]{1,0:T(8,128)(2,1)}, bf16[512,128]{1,0:T(8,128)(2,1)S(1)}, u32[]{:S(2)}, u32[]{:S(2)}) collective-permute-start(bf16[512,128]{1,0:T(8,128)(2,1)} %get-tuple-element.50), channel_id=1, source_target_pairs={{0,2},{1,3},{2,0},{3,1},{4,6},{5,7},{6,4},{7,5},{8,10},{9,11},{10,... | collective-permute-start | bytes 393224 | tf_op jit(solution)/shard_map/ppermute | solution.py:286
  59.1 18.1 %copy-start.20 = (bf16[512,128]{1,0:T(8,128)(2,1)}, bf16[512,128]{1,0:T(8,128)(2,1)S(1)}, u32[]{:S(2)}) copy-start(bf16[512,128]{1,0:T(8,128)(2,1)S(1)} %collective-permute-done.6.refs_6_) | copy-start | bytes 393220
  59.1 30.3 %collective-permute-start.18 = (bf16[512,128]{1,0:T(8,128)(2,1)}, bf16[512,128]{1,0:T(8,128)(2,1)S(1)}, u32[]{:S(2)}, u32[]{:S(2)}) collective-permute-start(bf16[512,128]{1,0:T(8,128)(2,1)} %get-tuple-element.51), channel_id=1, source_target_pairs={{0,6},{1,7},{2,4},{3,5},{4,2},{5,3},{6,0},{7,1},{8,14},{9,15},{10,... | collective-permute-start | bytes 393224 | tf_op jit(solution)/shard_map/ppermute | solution.py:286
  70.3 7.0 %copy-start.3 = (bf16[512,128]{1,0:T(8,128)(2,1)}, bf16[512,128]{1,0:T(8,128)(2,1)S(1)}, u32[]{:S(2)}) copy-start(bf16[512,128]{1,0:T(8,128)(2,1)S(1)} %collective-permute-done.14.refs_0_) | copy-start | bytes 393220
  70.3 20.2 %collective-permute-start.19 = (bf16[512,128]{1,0:T(8,128)(2,1)}, bf16[512,128]{1,0:T(8,128)(2,1)S(1)}, u32[]{:S(2)}, u32[]{:S(2)}) collective-permute-start(bf16[512,128]{1,0:T(8,128)(2,1)} %get-tuple-element.52), channel_id=1, source_target_pairs={{0,3},{1,2},{2,1},{3,0},{4,7},{5,6},{6,5},{7,4},{8,11},{9,10},{10,... | collective-permute-start | bytes 393224 | tf_op jit(solution)/shard_map/ppermute | solution.py:286
  70.3 7.0 %copy-start.4 = (bf16[512,128]{1,0:T(8,128)(2,1)}, bf16[512,128]{1,0:T(8,128)(2,1)S(1)}, u32[]{:S(2)}) copy-start(bf16[512,128]{1,0:T(8,128)(2,1)S(1)} %collective-permute-done.15.refs_1_) | copy-start | bytes 393220
  70.3 22.1 %collective-permute-start.20 = (bf16[512,128]{1,0:T(8,128)(2,1)}, bf16[512,128]{1,0:T(8,128)(2,1)S(1)}, u32[]{:S(2)}, u32[]{:S(2)}) collective-permute-start(bf16[512,128]{1,0:T(8,128)(2,1)} %get-tuple-element.53), channel_id=1, source_target_pairs={{0,7},{1,6},{2,5},{3,4},{4,3},{5,2},{6,1},{7,0},{8,15},{9,14},{10,... | collective-permute-start | bytes 393224 | tf_op jit(solution)/shard_map/ppermute | solution.py:286
  85.5 8.3 %copy-start.8 = (bf16[512,128]{1,0:T(8,128)(2,1)}, bf16[512,128]{1,0:T(8,128)(2,1)S(1)}, u32[]{:S(2)}) copy-start(bf16[512,128]{1,0:T(8,128)(2,1)S(1)} %collective-permute-done.16.refs_2_) | copy-start | bytes 393220
  85.5 15.7 %collective-permute-start.10 = (bf16[512,128]{1,0:T(8,128)(2,1)}, bf16[512,128]{1,0:T(8,128)(2,1)S(1)}, u32[]{:S(2)}, u32[]{:S(2)}) collective-permute-start(bf16[512,128]{1,0:T(8,128)(2,1)} %get-tuple-element.42), channel_id=1, source_target_pairs={{0,2},{1,3},{2,0},{3,1},{4,6},{5,7},{6,4},{7,5},{8,10},{9,11},{10,... | collective-permute-start | bytes 393224 | tf_op jit(solution)/shard_map/ppermute | solution.py:286
  87.5 6.3 %copy-start.12 = (bf16[512,128]{1,0:T(8,128)(2,1)}, bf16[512,128]{1,0:T(8,128)(2,1)S(1)}, u32[]{:S(2)}) copy-start(bf16[512,128]{1,0:T(8,128)(2,1)S(1)} %collective-permute-done.17.refs_3_) | copy-start | bytes 393220
  87.5 13.8 %collective-permute-start.11 = (bf16[512,128]{1,0:T(8,128)(2,1)}, bf16[512,128]{1,0:T(8,128)(2,1)S(1)}, u32[]{:S(2)}, u32[]{:S(2)}) collective-permute-start(bf16[512,128]{1,0:T(8,128)(2,1)} %get-tuple-element.43), channel_id=1, source_target_pairs={{0,6},{1,7},{2,4},{3,5},{4,2},{5,3},{6,0},{7,1},{8,14},{9,15},{10,... | collective-permute-start | bytes 393224 | tf_op jit(solution)/shard_map/ppermute | solution.py:286
  89.4 4.4 %copy-start.14 = (bf16[512,128]{1,0:T(8,128)(2,1)}, bf16[512,128]{1,0:T(8,128)(2,1)S(1)}, u32[]{:S(2)}) copy-start(bf16[512,128]{1,0:T(8,128)(2,1)S(1)} %collective-permute-done.18.refs_4_) | copy-start | bytes 393220
  89.4 13.4 %collective-permute-start.12 = (bf16[512,128]{1,0:T(8,128)(2,1)}, bf16[512,128]{1,0:T(8,128)(2,1)S(1)}, u32[]{:S(2)}, u32[]{:S(2)}) collective-permute-start(bf16[512,128]{1,0:T(8,128)(2,1)} %get-tuple-element.44), channel_id=1, source_target_pairs={{0,3},{1,2},{2,1},{3,0},{4,7},{5,6},{6,5},{7,4},{8,11},{9,10},{10,... | collective-permute-start | bytes 393224 | tf_op jit(solution)/shard_map/ppermute | solution.py:286
  90.5 3.4 %copy-start.16 = (bf16[512,128]{1,0:T(8,128)(2,1)}, bf16[512,128]{1,0:T(8,128)(2,1)S(1)}, u32[]{:S(2)}) copy-start(bf16[512,128]{1,0:T(8,128)(2,1)S(1)} %collective-permute-done.19.refs_5_) | copy-start | bytes 393220
  90.5 12.7 %collective-permute-start.13 = (bf16[512,128]{1,0:T(8,128)(2,1)}, bf16[512,128]{1,0:T(8,128)(2,1)S(1)}, u32[]{:S(2)}, u32[]{:S(2)}) collective-permute-start(bf16[512,128]{1,0:T(8,128)(2,1)} %get-tuple-element.45), channel_id=1, source_target_pairs={{0,7},{1,6},{2,5},{3,4},{4,3},{5,2},{6,1},{7,0},{8,15},{9,14},{10,... | collective-permute-start | bytes 393224 | tf_op jit(solution)/shard_map/ppermute | solution.py:286
  92.3 1.5 copy-start.19
  92.3 13.3 %collective-permute-start.7 = (bf16[512,128]{1,0:T(8,128)(2,1)}, bf16[512,128]{1,0:T(8,128)(2,1)S(1)}, u32[]{:S(2)}, u32[]{:S(2)}) collective-permute-start(bf16[512,128]{1,0:T(8,128)(2,1)} %get-tuple-element.39), channel_id=1, source_target_pairs={{0,4},{1,5},{2,6},{3,7},{4,0},{5,1},{6,2},{7,3},{8,12},{9,13},{10,... | collective-permute-start | bytes 393224 | tf_op jit(solution)/shard_map/ppermute | solution.py:286
  93.8 9.3 %copy-start.25 = (bf16[512,128]{1,0:T(8,128)(2,1)S(1)}, bf16[512,128]{1,0:T(8,128)(2,1)}, u32[]{:S(2)}) copy-start(bf16[512,128]{1,0:T(8,128)(2,1)} %get-tuple-element.40) | copy-start | bytes 393220
  93.9 11.8 %copy-start.24 = (bf16[512,128]{1,0:T(8,128)(2,1)S(1)}, bf16[512,128]{1,0:T(8,128)(2,1)}, u32[]{:S(2)}) copy-start(bf16[512,128]{1,0:T(8,128)(2,1)} %get-tuple-element.41) | copy-start | bytes 393220
  101.2 14.1 %copy-start.10 = (bf16[512,128]{1,0:T(8,128)(2,1)}, bf16[512,128]{1,0:T(8,128)(2,1)S(1)}, u32[]{:S(2)}) copy-start(bf16[512,128]{1,0:T(8,128)(2,1)S(1)} %collective-permute-done.10.refs_3_) | copy-start | bytes 393220
  101.2 48.4 %collective-permute-start.21 = (bf16[512,256]{1,0:T(8,128)(2,1)}, bf16[512,256]{1,0:T(8,128)(2,1)S(1)}, u32[]{:S(2)}, u32[]{:S(2)}) collective-permute-start(bf16[512,256]{1,0:T(8,128)(2,1)} %get-tuple-element.57), channel_id=1, source_target_pairs={{0,8},{8,0},{16,24},{24,16},{1,9},{9,1},{17,25},{25,17},{2,10},{10... | collective-permute-start | bytes 786440 | tf_op jit(solution)/shard_map/ppermute | solution.py:286
  101.3 14.0 %copy-start.13 = (bf16[512,128]{1,0:T(8,128)(2,1)}, bf16[512,128]{1,0:T(8,128)(2,1)S(1)}, u32[]{:S(2)}) copy-start(bf16[512,128]{1,0:T(8,128)(2,1)S(1)} %collective-permute-done.11.refs_4_) | copy-start | bytes 393220
  101.3 48.3 %collective-permute-start.22 = (bf16[512,256]{1,0:T(8,128)(2,1)}, bf16[512,256]{1,0:T(8,128)(2,1)S(1)}, u32[]{:S(2)}, u32[]{:S(2)}) collective-permute-start(bf16[512,256]{1,0:T(8,128)(2,1)} %get-tuple-element.58), channel_id=1, source_target_pairs={{0,16},{8,24},{16,0},{24,8},{1,17},{9,25},{17,1},{25,9},{2,18},{10... | collective-permute-start | bytes 786440 | tf_op jit(solution)/shard_map/ppermute | solution.py:286
  102.9 12.5 %copy-start.15 = (bf16[512,128]{1,0:T(8,128)(2,1)}, bf16[512,128]{1,0:T(8,128)(2,1)S(1)}, u32[]{:S(2)}) copy-start(bf16[512,128]{1,0:T(8,128)(2,1)S(1)} %collective-permute-done.12.refs_5_) | copy-start | bytes 393220
  102.9 46.8 %collective-permute-start.23 = (bf16[512,256]{1,0:T(8,128)(2,1)}, bf16[512,256]{1,0:T(8,128)(2,1)S(1)}, u32[]{:S(2)}, u32[]{:S(2)}) collective-permute-start(bf16[512,256]{1,0:T(8,128)(2,1)} %get-tuple-element.59), channel_id=1, source_target_pairs={{0,24},{8,16},{16,8},{24,0},{1,25},{9,17},{17,9},{25,1},{2,26},{10... | collective-permute-start | bytes 786440 | tf_op jit(solution)/shard_map/ppermute | solution.py:286
  103.1 12.2 %copy-start.18 = (bf16[512,128]{1,0:T(8,128)(2,1)}, bf16[512,128]{1,0:T(8,128)(2,1)S(1)}, u32[]{:S(2)}) copy-start(bf16[512,128]{1,0:T(8,128)(2,1)S(1)} %collective-permute-done.13.refs_6_) | copy-start | bytes 393220
  103.2 6.5 %collective-permute-start.8 = (bf16[512,128]{1,0:T(8,128)(2,1)S(1)}, bf16[512,128]{1,0:T(8,128)(2,1)S(1)}, u32[]{:S(2)}, u32[]{:S(2)}) collective-permute-start(bf16[512,128]{1,0:T(8,128)(2,1)S(1)} %copy-done.25), channel_id=1, source_target_pairs={{0,1},{1,0},{2,3},{3,2},{4,5},{5,4},{6,7},{7,6},{8,9},{9,8},{10,11... | collective-permute-start | bytes 393224 | tf_op jit(solution)/shard_map/ppermute | solution.py:286
  105.7 9.7 %copy-start.21 = (bf16[512,128]{1,0:T(8,128)(2,1)}, bf16[512,128]{1,0:T(8,128)(2,1)S(1)}, u32[]{:S(2)}) copy-start(bf16[512,128]{1,0:T(8,128)(2,1)S(1)} %collective-permute-done.7.refs_0_) | copy-start | bytes 393220
  105.7 9.7 %collective-permute-start.9 = (bf16[512,128]{1,0:T(8,128)(2,1)S(1)}, bf16[512,128]{1,0:T(8,128)(2,1)S(1)}, u32[]{:S(2)}, u32[]{:S(2)}) collective-permute-start(bf16[512,128]{1,0:T(8,128)(2,1)S(1)} %copy-done.24), channel_id=1, source_target_pairs={{0,5},{1,4},{2,7},{3,6},{4,1},{5,0},{6,3},{7,2},{8,13},{9,12},{10,... | collective-permute-start | bytes 393224 | tf_op jit(solution)/shard_map/ppermute | solution.py:286
  109.7 5.7 %copy-start.22 = (bf16[512,128]{1,0:T(8,128)(2,1)}, bf16[512,128]{1,0:T(8,128)(2,1)S(1)}, u32[]{:S(2)}) copy-start(bf16[512,128]{1,0:T(8,128)(2,1)S(1)} %collective-permute-done.8.refs_1_) | copy-start | bytes 393220
  115.3 0.6 copy-start.23
  149.6 0.7 copy-start
  149.6 0.8 copy-start.1
  149.6 0.9 copy-start.2

commit v4 on v2

--- a/solution.py
+++ b/solution.py
@@ -139,8 +139,29 @@
     rows_loop(rows, body)
 
 
+def piece_at(ref, where, k, rows):
+    start = pl.multiple_of(lax.bitwise_xor(where[0], k) * rows, rows)
+    return ref.at[pl.ds(start, rows), :]
+
+
 def gate_kernel(gate, upper, out):
     out[...] = (gate[...].astype(jnp.float32) * upper[...].astype(jnp.float32)).astype(jnp.bfloat16)
+
+
+def pick_kernel(order, where, whole, *refs):
+    outs, (slots, sems, out_sems) = refs[: len(order)], refs[len(order) :]
+    rows = outs[0].shape[0]
+    loads, stores = [], []
+    for i, k in enumerate(order):
+        start = pl.multiple_of(lax.bitwise_xor(where[0], k) * rows, rows)
+        loads.append(pltpu.make_async_copy(whole.at[pl.ds(start, rows), :], slots.at[i], sems.at[i]))
+        loads[-1].start()
+    for i, out in enumerate(outs):
+        loads[i].wait()
+        stores.append(pltpu.make_async_copy(slots.at[i], out, out_sems.at[i]))
+        stores[-1].start()
+    for copy in stores:
+        copy.wait()
 
 
 def taps_kernel(taps, forward, out, mid):
@@ -150,26 +171,29 @@
         out[r] = spectrum(mid, forward, r, width).astype(out.dtype)
 
 
-def ordered(blocks, held):
+def ordered(order, where, refs, held):
+    span = refs[0].shape[1]
+    for k, ref in zip(order, refs):
+        start = pl.multiple_of(lax.bitwise_xor(where[0], k) * span, span)
+        held[:, pl.ds(start, span)] = ref[...]
+
+
+def block_of(held, width):
+    return lambda p, at: held[at, p * width : (p + 1) * width].astype(jnp.float32)
+
+
+def block_into(held, width):
+    def store(p, at, value):
+        held[at, p * width : (p + 1) * width] = value.astype(jnp.bfloat16)
+
+    return store
+
+
+def back_kernel(blocks, taps_spec, forward, backward, out, grad_spec, held, mid, wide):
+    rows, width = held.shape[0], held.shape[1] // BLOCKS
     span = blocks.shape[2]
     for p in range(blocks.shape[0]):
         held[:, p * span : (p + 1) * span] = blocks[p]
-
-
-def block_of(held, width):
-    return lambda p, at: held[at, p * width : (p + 1) * width].astype(jnp.float32)
-
-
-def block_into(held, width):
-    def store(p, at, value):
-        held[at, p * width : (p + 1) * width] = value.astype(jnp.bfloat16)
-
-    return store
-
-
-def back_kernel(blocks, taps_spec, forward, backward, out, grad_spec, held, mid, wide):
-    rows, width = held.shape[0], held.shape[1] // BLOCKS
-    ordered(blocks, held)
     split_rows(block_of(held, width), mid, rows, width)
     for r in range(GROUPS):
         grad = spectrum(mid, forward, r, width)
@@ -179,15 +203,15 @@
         product = jnp.concatenate([hr * gr + hi * gi, hr * gi - hi * gr], axis=1)
         invert_group(product.astype(jnp.bfloat16), backward, r, width, wide)
     merge_rows(wide, block_into(held, width), rows, width)
-    span = out.shape[2]
     for p in range(out.shape[0]):
         out[p] = held[:, p * span : (p + 1) * span]
 
 
-def cross_kernel(where, blocks, grad_spec, forward, backward, *refs):
-    outs, (held, mid, wide) = refs[:-3], refs[-3:]
+def cross_kernel(order, where, *refs):
+    blocks, refs = refs[: len(order)], refs[len(order) :]
+    grad_spec, forward, backward, *outs, held, mid, wide = refs
     rows, width = held.shape[0], held.shape[1] // BLOCKS
-    ordered(blocks, held)
+    ordered(order, where, blocks, held)
     split_rows(block_of(held, width), mid, rows, width)
     for r in range(GROUPS):
         signal = spectrum(mid, forward, r, width)
@@ -198,7 +222,7 @@
     merge_rows(wide, block_into(held, width), rows, width)
     part = held.shape[1] // len(outs)
     for k, out in enumerate(outs):
-        start = pl.multiple_of(lax.rem(where[0] + k, len(outs)) * part, part)
+        start = pl.multiple_of(lax.bitwise_xor(where[1], k) * part, part)
         out[...] = held[:, pl.ds(start, part)]
 
 
@@ -209,8 +233,9 @@
     refs[-1][...] = total * scale
 
 
-def call(kernel, operands, outs, scratch=(), scalar=True, flops=0):
-    specs = [pl.BlockSpec(memory_space=pltpu.VMEM)] * len(operands)
+def call(kernel, operands, outs, scratch=(), scalar=True, flops=0, stream=False):
+    space = pl.ANY if stream else pltpu.VMEM
+    specs = [pl.BlockSpec(memory_space=space)] * len(operands)
     if scalar:
         specs[0] = pl.BlockSpec(memory_space=pltpu.SMEM)
     size = sum(math.prod(o.shape) * o.dtype.itemsize for o in list(operands) + list(outs))
@@ -218,18 +243,22 @@
         kernel,
         out_shape=list(outs),
         in_specs=specs,
-        out_specs=[pl.BlockSpec(memory_space=pltpu.VMEM)] * len(outs),
+        out_specs=[pl.BlockSpec(memory_space=space)] * len(outs),
         scratch_shapes=list(scratch),
         compiler_params=pltpu.CompilerParams(vmem_limit_bytes=LIMIT),
         cost_estimate=pl.CostEstimate(flops=flops, bytes_accessed=size, transcendentals=0),
     )(*operands)
 
 
-def exchange(pieces, axis, size):
-    moved = [pieces[0]]
-    for k in range(1, size):
-        pairs = [(i, (i + k) % size) for i in range(size)]
-        moved.append(lax.ppermute(pieces[k], axis, pairs))
+def far_first(size):
+    half = size // 2
+    return [k for pair in zip(range(half, size), [*range(1, half), 0]) for k in pair]
+
+
+def exchange(pieces, order, axis, size):
+    moved = []
+    for k, piece in zip(order, pieces):
+        moved.append(lax.ppermute(piece, axis, [(i, i ^ k) for i in range(size)]) if k else piece)
     return moved
 
 
@@ -242,20 +271,30 @@
     channels, span = saved_input.shape[1:]
     rows, length = long_filter.shape
     width = length // BLOCKS
-    where = lax.axis_index("dp").astype(jnp.int32)[None]
+    order = far_first(count)
+    where = jnp.stack([lax.axis_index("ctx"), lax.axis_index("dp")]).astype(jnp.int32)
     forward, backward = (jnp.asarray(t) for t in transform_tables(width))
     half, full = jnp.bfloat16, jnp.float32
+    piece = jax.ShapeDtypeStruct((rows, span), half)
     blocks = jax.ShapeDtypeStruct((count, rows, span), half)
     spec = jax.ShapeDtypeStruct((GROUPS, rows, 2 * width), half)
     held = pltpu.VMEM((rows, length), half)
     mid = pltpu.VMEM((GROUPS, rows, 2 * width), half)
     wide = pltpu.VMEM((GROUPS, rows, 2 * width), full)
+    sems = pltpu.SemaphoreType.DMA
     work = 2 * GROUPS * rows * 4 * width * width
 
-    saved_input, out_gate, grad_out = (x.reshape(blocks.shape) for x in (saved_input, out_gate, grad_out))
+    input_pieces = call(
+        functools.partial(pick_kernel, order),
+        [where, saved_input[0]],
+        [piece] * count,
+        [pltpu.VMEM(blocks.shape, half), sems((count,)), sems((count,))],
+        stream=True,
+    )
+    input_blocks = exchange(input_pieces, order, "ctx", count)
+    out_gate, grad_out = (x.reshape(blocks.shape) for x in (out_gate, grad_out))
     (conv_grad,) = call(gate_kernel, [out_gate, grad_out], [blocks], scalar=False)
     grad_blocks = swap(conv_grad)
-    input_blocks = swap(saved_input)
     (taps_spec,) = call(taps_kernel, [long_filter, forward], [spec], [mid], scalar=False, flops=work)
     back, grad_spec = call(
         back_kernel,
@@ -268,13 +307,13 @@
     grad_input = swap(back)
     share = jax.ShapeDtypeStruct((rows, length // shares), half)
     cross = call(
-        cross_kernel,
-        [where, input_blocks, grad_spec, forward, backward],
+        functools.partial(cross_kernel, order),
+        [where, *input_blocks, grad_spec, forward, backward],
         [share] * shares,
         [held, mid, wide],
         flops=2 * work,
     )
-    cross_blocks = exchange(cross, "dp", shares)
+    cross_blocks = exchange(cross, range(shares), "dp", shares)
     scale = 1.0 / math.sqrt(shares * length)
     (grad_filter,) = call(
         functools.partial(sum_kernel, scale),

time: 96.4 us -> 122 us (1.27)
  waiting for transfers between devices: 25.9 us -> 65.8 us
  blocking collectives: 33.2 us -> 0 us
  starting transfers between devices: 10.1 us -> 23.6 us
  Pallas kernels: 24.6 us -> 27.5 us
  local copies, waits for them, and re-layouts: 1.67 us -> 3.32 us
    ppermute x3 -> x10, waiting for transfers between devices: 10.6 us -> 44.8 us  [exchange(): lax.ppermute(piece, axis, [(i, i ^ k) for i in range(size)])]
    all_to_all x1 -> x0, blocking collectives: 33.2 us -> none  [swap(): lax.all_to_all(blocks, 'ctx', split_axis=0, concat_axis=0, tiled=True)]
    ppermute x3 -> x10, starting transfers between devices: 2.96 us -> 12.7 us  [exchange(): lax.ppermute(piece, axis, [(i, i ^ k) for i in range(size)])]
    all_to_all x2, waiting for transfers between devices: 15.3 us -> 21 us  [swap(): lax.all_to_all(blocks, 'ctx', split_axis=0, concat_axis=0, tiled=True)]
    all_to_all x2, starting transfers between devices: 7.15 us -> 10.9 us  [swap(): lax.all_to_all(blocks, 'ctx', split_axis=0, concat_axis=0, tiled=True)]
    pallas_call x5 -> x6, Pallas kernels: 24.6 us -> 27.5 us  [call(): pl.pallas_call(kernel, out_shape=list(outs), in_specs=specs, out_specs=[p...]
    unnamed x9 -> x23, local copies, waits for them, and re-layouts: 1.67 us -> 3.32 us
  transfers between devices with their start and end apart: 5 -> 12, of which waited for: 5 -> 6; matrix products, arithmetic and copies ran while one was open for 0% -> 0% of each run, Pallas kernels for 23% -> 14%
where the time goes in v4:
time: 122 us; the launch traced here: 121 us
  waiting for transfers between devices  65.8 us (54%)
  Pallas kernels  27.5 us (23%)
  starting transfers between devices  23.6 us (19%)
  local copies, waits for them, and re-layouts  3.32 us (3%)
    ppermute x10, waiting for transfers between devices, exchange(): lax.ppermute(piece, axis, [(i, i ^ k) for i in range(size)])  44.8 us
    pallas_call x6, Pallas kernels, call(): pl.pallas_call(kernel, out_shape=list(outs), in_specs=specs, out_specs=[p...  27.5 us
    all_to_all x2, waiting for transfers between devices, swap(): lax.all_to_all(blocks, 'ctx', split_axis=0, concat_axis=0, tiled=True)  21 us
    ppermute x10, starting transfers between devices, exchange(): lax.ppermute(piece, axis, [(i, i ^ k) for i in range(size)])  12.7 us
    all_to_all x2, starting transfers between devices, swap(): lax.all_to_all(blocks, 'ctx', split_axis=0, concat_axis=0, tiled=True)  10.9 us
    unnamed x23, local copies, waits for them, and re-layouts  3.32 us
  transfers between devices with their start and end apart: 12, of which 6 were waited for; matrix products, arithmetic and copies ran while one was open for 0% of the time, Pallas kernels for 14%

profile of v4, /device:TPU:0, one launch (start us, length us, event | category | flops | bytes accessed | tf_op | source)
XLA Modules:
  0.0 121.4 jit_solution(4387530716298197958)
XLA Ops:
  0.6 2.7 %shard_map.77 = bf16[8,512,128]{2,1,0:T(8,128)(2,1)} custom-call(bf16[8,512,128]{2,1,0:T(8,128)(2,1)} %bitcast.7, bf16[8,512,128]{2,1,0:T(8,128)(2,1)} %bitcast.8), custom_call_target="tpu_custom_call" | custom-call | bytes 3145728 | tf_op jit(solution)/shard_map/pallas_call | solution.py:242
  3.4 7.3 %all-to-all-start = ((bf16[8,512,128]{2,1,0:T(8,128)(2,1)}), bf16[8,512,128]{2,1,0:T(8,128)(2,1)S(1)}, u32[]{:S(2)}, u32[]{:S(2)}) async-start(bf16[8,512,128]{2,1,0:T(8,128)(2,1)} %shard_map.77), calls=%async_computation | async-start | bytes 2097152 | tf_op jit(solution)/shard_map/all_to_all | solution.py:266
  10.7 4.8 %shard_map.78.taps_spec = bf16[9,512,256]{2,1,0:T(8,128)(2,1)} custom-call(f32[512,1024]{1,0:T(8,128)} %taps.1, bf16[9,256,256]{2,1,0:T(8,128)(2,1)} %constant.12.clone.forward.refs_9_), custom_call_target="tpu_custom_call" | custom-call | flops 603979776 | bytes 5636096 | tf_op jit(solution)/shard_map/pallas_call | solution.py:242
  15.5 21.0 %all-to-all-done.blocks = bf16[8,512,128]{2,1,0:T(8,128)(2,1)S(1)} async-done(((bf16[8,512,128]{2,1,0:T(8,128)(2,1)}), bf16[8,512,128]{2,1,0:T(8,128)(2,1)S(1)}, u32[]{:S(2)}, u32[]{:S(2)}) %all-to-all-start) | async-done | bytes 1048608 | tf_op jit(solution)/shard_map/all_to_all | solution.py:266
  36.4 0.0 copy-start
  36.4 1.0 copy-done
  37.4 7.8 %shard_map.79 = (bf16[8,512,128]{2,1,0:T(8,128)(2,1)}, bf16[9,512,256]{2,1,0:T(8,128)(2,1)}) custom-call(bf16[8,512,128]{2,1,0:T(8,128)(2,1)} %copy-done, bf16[9,512,256]{2,1,0:T(8,128)(2,1)} %shard_map.78.taps_spec, bf16[9,256,256]{2,1,0:T(8,128)(2,1)} %constant.12.clone.forward.refs_9_, bf16[9,256,256]{2,1,0:T(8,128)(2,1)} %constant.13.clone.backward.refs_10_), custom_call_target="tpu_custom_call" | custom-call | flops 1207959552 | bytes 9175040 | tf_op jit(solution)/shard_map/pallas_call | solution.py:242
  45.2 3.6 %all-to-all-start.1 = ((bf16[8,512,128]{2,1,0:T(8,128)(2,1)}), bf16[8,512,128]{2,1,0:T(8,128)(2,1)S(1)}, u32[]{:S(2)}, u32[]{:S(2)}) async-start(bf16[8,512,128]{2,1,0:T(8,128)(2,1)} %get-tuple-element.16), calls=%async_computation.1 | async-start | bytes 2097152 | tf_op jit(solution)/shard_map/all_to_all | solution.py:266
  48.7 0.6 pad_add_fusion.where
  49.3 2.7 %shard_map.80 = (bf16[512,128]{1,0:T(8,128)(2,1)}, bf16[512,128]{1,0:T(8,128)(2,1)}, bf16[512,128]{1,0:T(8,128)(2,1)}, bf16[512,128]{1,0:T(8,128)(2,1)}, bf16[51...) custom-call(s32[2]{0:T(128)} %pad_add_fusion.where, ...), custom_call_target="tpu_custom_call" | custom-call | bytes 2097160 | tf_op jit(solution)/shard_map/pallas_call | solution.py:242
  52.1 3.0 %collective-permute-start = (bf16[512,128]{1,0:T(8,128)(2,1)}, bf16[512,128]{1,0:T(8,128)(2,1)S(1)}, u32[]{:S(2)}, u32[]{:S(2)}) collective-permute-start(bf16[512,128]{1,0:T(8,128)(2,1)} %get-tuple-element.17), channel_id=1, source_target_pairs={{0,4},{1,5},{2,6},{3,7},{4,0},{5,1},{6,2},{7,3},{8,12},{9,13},{10,... | collective-permute-start | bytes 393224 | tf_op jit(solution)/shard_map/ppermute | solution.py:261
  55.1 1.5 %collective-permute-start.1 = (bf16[512,128]{1,0:T(8,128)(2,1)}, bf16[512,128]{1,0:T(8,128)(2,1)S(1)}, u32[]{:S(2)}, u32[]{:S(2)}) collective-permute-start(bf16[512,128]{1,0:T(8,128)(2,1)} %get-tuple-element.18), channel_id=1, source_target_pairs={{0,1},{1,0},{2,3},{3,2},{4,5},{5,4},{6,7},{7,6},{8,9},{9,8},{10,11... | collective-permute-start | bytes 393224 | tf_op jit(solution)/shard_map/ppermute | solution.py:261
  56.5 0.1 collective-permute-start.2
  56.6 1.9 %collective-permute-start.3 = (bf16[512,128]{1,0:T(8,128)(2,1)}, bf16[512,128]{1,0:T(8,128)(2,1)S(1)}, u32[]{:S(2)}, u32[]{:S(2)}) collective-permute-start(bf16[512,128]{1,0:T(8,128)(2,1)} %get-tuple-element.20), channel_id=1, source_target_pairs={{0,2},{1,3},{2,0},{3,1},{4,6},{5,7},{6,4},{7,5},{8,10},{9,11},{10,... | collective-permute-start | bytes 393224 | tf_op jit(solution)/shard_map/ppermute | solution.py:261
  58.6 2.4 %collective-permute-start.4 = (bf16[512,128]{1,0:T(8,128)(2,1)}, bf16[512,128]{1,0:T(8,128)(2,1)S(1)}, u32[]{:S(2)}, u32[]{:S(2)}) collective-permute-start(bf16[512,128]{1,0:T(8,128)(2,1)} %get-tuple-element.21), channel_id=1, source_target_pairs={{0,6},{1,7},{2,4},{3,5},{4,2},{5,3},{6,0},{7,1},{8,14},{9,15},{10,... | collective-permute-start | bytes 393224 | tf_op jit(solution)/shard_map/ppermute | solution.py:261
  60.9 26.2 %collective-permute-done.refs_0_ = bf16[512,128]{1,0:T(8,128)(2,1)S(1)} collective-permute-done((bf16[512,128]{1,0:T(8,128)(2,1)}, bf16[512,128]{1,0:T(8,128)(2,1)S(1)}, u32[]{:S(2)}, u32[]{:S(2)}) %collective-permute-start) | collective-permute-done | bytes 131104 | tf_op jit(solution)/shard_map/ppermute | solution.py:261
  87.1 0.0 copy-start.4
  87.2 0.0 collective-permute-start.5
  87.2 0.0 collective-permute-done.1.refs_1_
  87.2 0.0 copy-start.5
  87.2 2.0 %collective-permute-start.6 = (bf16[512,128]{1,0:T(8,128)(2,1)}, bf16[512,128]{1,0:T(8,128)(2,1)S(1)}, u32[]{:S(2)}, u32[]{:S(2)}) collective-permute-start(bf16[512,128]{1,0:T(8,128)(2,1)} %get-tuple-element.23), channel_id=1, source_target_pairs={{0,7},{1,6},{2,5},{3,4},{4,3},{5,2},{6,1},{7,0},{8,15},{9,14},{10,... | collective-permute-start | bytes 393224 | tf_op jit(solution)/shard_map/ppermute | solution.py:261
  89.2 1.5 %collective-permute-done.2.refs_2_ = bf16[512,128]{1,0:T(8,128)(2,1)S(1)} collective-permute-done((bf16[512,128]{1,0:T(8,128)(2,1)}, bf16[512,128]{1,0:T(8,128)(2,1)S(1)}, u32[]{:S(2)}, u32[]{:S(2)}) %collective-permute-start.2) | collective-permute-done | bytes 131104 | tf_op jit(solution)/shard_map/ppermute | solution.py:261
  90.6 0.0 copy-start.6
  90.6 0.0 collective-permute-done.3.refs_3_
  90.6 0.0 copy-start.7
  90.6 0.0 collective-permute-done.4.refs_4_
  90.6 0.0 copy-start.8
  90.6 4.9 %collective-permute-done.5.refs_5_ = bf16[512,128]{1,0:T(8,128)(2,1)S(1)} collective-permute-done((bf16[512,128]{1,0:T(8,128)(2,1)}, bf16[512,128]{1,0:T(8,128)(2,1)S(1)}, u32[]{:S(2)}, u32[]{:S(2)}) %collective-permute-start.5) | collective-permute-done | bytes 131104 | tf_op jit(solution)/shard_map/ppermute | solution.py:261
  95.5 0.0 copy-start.9
  95.5 0.0 collective-permute-done.6.refs_6_
  95.5 0.0 copy-start.10
  95.5 0.0 copy-done.4
  95.6 0.0 copy-done.5
  95.6 0.0 copy-done.6
  95.6 0.0 copy-done.7
  95.6 0.0 copy-done.8
  95.6 0.6 copy-done.9
  96.2 0.0 copy-done.10
  96.2 7.3 %shard_map.81 = (bf16[512,256]{1,0:T(8,128)(2,1)}, bf16[512,256]{1,0:T(8,128)(2,1)}, bf16[512,256]{1,0:T(8,128)(2,1)}, bf16[512,256]{1,0:T(8,128)(2,1)}) custom-call(s32[2]{0:T(128)} %pad_add_fusion.where, bf16[512,128]{1,0:T(8,128)(2,1)} %copy-done.4, bf16[512,128]{1,0:T(8,128)(2,1)} %copy-done.5, bf16[512,128]{1,0:T(8,128)(2,1)} %copy-done.6, ...), custom_call_target="tpu_custom_call" | custom-call | flops 1207959552 | bytes 6815752 | tf_op jit(solution)/shard_map/pallas_call | solution.py:242
  103.5 0.0 collective-permute-start.7
  103.5 1.6 %collective-permute-start.8 = (bf16[512,256]{1,0:T(8,128)(2,1)}, bf16[512,256]{1,0:T(8,128)(2,1)S(1)}, u32[]{:S(2)}, u32[]{:S(2)}) collective-permute-start(bf16[512,256]{1,0:T(8,128)(2,1)} %get-tuple-element.28), channel_id=1, source_target_pairs={{0,16},{8,24},{16,0},{24,8},{1,17},{9,25},{17,1},{25,9},{2,18},{10... | collective-permute-start | bytes 786440 | tf_op jit(solution)/shard_map/ppermute | solution.py:261
  105.1 0.3 collective-permute-start.9
  105.4 0.0 collective-permute-done.7.refs_1_
  105.4 0.0 copy-start.1
  105.4 7.5 %collective-permute-done.8.refs_2_ = bf16[512,256]{1,0:T(8,128)(2,1)S(1)} collective-permute-done((bf16[512,256]{1,0:T(8,128)(2,1)}, bf16[512,256]{1,0:T(8,128)(2,1)S(1)}, u32[]{:S(2)}, u32[]{:S(2)}) %collective-permute-start.8) | collective-permute-done | bytes 262176 | tf_op jit(solution)/shard_map/ppermute | solution.py:261
  112.9 0.0 copy-start.2
  112.9 4.7 %collective-permute-done.9.refs_3_ = bf16[512,256]{1,0:T(8,128)(2,1)S(1)} collective-permute-done((bf16[512,256]{1,0:T(8,128)(2,1)}, bf16[512,256]{1,0:T(8,128)(2,1)S(1)}, u32[]{:S(2)}, u32[]{:S(2)}) %collective-permute-start.9) | collective-permute-done | bytes 262176 | tf_op jit(solution)/shard_map/ppermute | solution.py:261
  117.6 0.0 copy-start.3
  117.6 0.0 copy-done.1
  117.6 0.0 copy-done.2
  117.6 0.7 copy-done.3
  118.3 2.1 %shard_map.82 = f32[512,256]{1,0:T(8,128)} custom-call(bf16[512,256]{1,0:T(8,128)(2,1)} %get-tuple-element.26.refs_0_, bf16[512,256]{1,0:T(8,128)(2,1)} %copy-done.1, bf16[512,256]{1,0:T(8,128)(2,1)} %copy-done.2, bf16[512,256]{1,0:T(8,128)(2,1)} %copy-done.3), custom_call_target="tpu_custom_call" | custom-call | bytes 1572864 | tf_op jit(solution)/shard_map/pallas_call | solution.py:242
  120.5 0.0 all-to-all-done.1
  120.5 1.0 copy.9
Async XLA Ops:
  3.4 33.0 %all-to-all-start = ((bf16[8,512,128]{2,1,0:T(8,128)(2,1)}), bf16[8,512,128]{2,1,0:T(8,128)(2,1)S(1)}, u32[]{:S(2)}, u32[]{:S(2)}) async-start(bf16[8,512,128]{2,1,0:T(8,128)(2,1)} %shard_map.77), calls=%async_computation | async-start | bytes 2097152 | tf_op jit(solution)/shard_map/all_to_all | solution.py:266
  36.4 1.0 copy-start
  45.2 75.3 %all-to-all-start.1 = ((bf16[8,512,128]{2,1,0:T(8,128)(2,1)}), bf16[8,512,128]{2,1,0:T(8,128)(2,1)S(1)}, u32[]{:S(2)}, u32[]{:S(2)}) async-start(bf16[8,512,128]{2,1,0:T(8,128)(2,1)} %get-tuple-element.16), calls=%async_computation.1 | async-start | bytes 2097152 | tf_op jit(solution)/shard_map/all_to_all | solution.py:266
  52.1 35.1 %collective-permute-start = (bf16[512,128]{1,0:T(8,128)(2,1)}, bf16[512,128]{1,0:T(8,128)(2,1)S(1)}, u32[]{:S(2)}, u32[]{:S(2)}) collective-permute-start(bf16[512,128]{1,0:T(8,128)(2,1)} %get-tuple-element.17), channel_id=1, source_target_pairs={{0,4},{1,5},{2,6},{3,7},{4,0},{5,1},{6,2},{7,3},{8,12},{9,13},{10,... | collective-permute-start | bytes 393224 | tf_op jit(solution)/shard_map/ppermute | solution.py:261
  55.1 32.1 %collective-permute-start.1 = (bf16[512,128]{1,0:T(8,128)(2,1)}, bf16[512,128]{1,0:T(8,128)(2,1)S(1)}, u32[]{:S(2)}, u32[]{:S(2)}) collective-permute-start(bf16[512,128]{1,0:T(8,128)(2,1)} %get-tuple-element.18), channel_id=1, source_target_pairs={{0,1},{1,0},{2,3},{3,2},{4,5},{5,4},{6,7},{7,6},{8,9},{9,8},{10,11... | collective-permute-start | bytes 393224 | tf_op jit(solution)/shard_map/ppermute | solution.py:261
  56.5 34.1 %collective-permute-start.2 = (bf16[512,128]{1,0:T(8,128)(2,1)}, bf16[512,128]{1,0:T(8,128)(2,1)S(1)}, u32[]{:S(2)}, u32[]{:S(2)}) collective-permute-start(bf16[512,128]{1,0:T(8,128)(2,1)} %get-tuple-element.19), channel_id=1, source_target_pairs={{0,5},{1,4},{2,7},{3,6},{4,1},{5,0},{6,3},{7,2},{8,13},{9,12},{10,... | collective-permute-start | bytes 393224 | tf_op jit(solution)/shard_map/ppermute | solution.py:261
  56.6 34.0 %collective-permute-start.3 = (bf16[512,128]{1,0:T(8,128)(2,1)}, bf16[512,128]{1,0:T(8,128)(2,1)S(1)}, u32[]{:S(2)}, u32[]{:S(2)}) collective-permute-start(bf16[512,128]{1,0:T(8,128)(2,1)} %get-tuple-element.20), channel_id=1, source_target_pairs={{0,2},{1,3},{2,0},{3,1},{4,6},{5,7},{6,4},{7,5},{8,10},{9,11},{10,... | collective-permute-start | bytes 393224 | tf_op jit(solution)/shard_map/ppermute | solution.py:261
  58.6 32.1 %collective-permute-start.4 = (bf16[512,128]{1,0:T(8,128)(2,1)}, bf16[512,128]{1,0:T(8,128)(2,1)S(1)}, u32[]{:S(2)}, u32[]{:S(2)}) collective-permute-start(bf16[512,128]{1,0:T(8,128)(2,1)} %get-tuple-element.21), channel_id=1, source_target_pairs={{0,6},{1,7},{2,4},{3,5},{4,2},{5,3},{6,0},{7,1},{8,14},{9,15},{10,... | collective-permute-start | bytes 393224 | tf_op jit(solution)/shard_map/ppermute | solution.py:261
  87.1 8.4 %copy-start.4 = (bf16[512,128]{1,0:T(8,128)(2,1)}, bf16[512,128]{1,0:T(8,128)(2,1)S(1)}, u32[]{:S(2)}) copy-start(bf16[512,128]{1,0:T(8,128)(2,1)S(1)} %collective-permute-done.refs_0_) | copy-start | bytes 393220
  87.2 8.4 %collective-permute-start.5 = (bf16[512,128]{1,0:T(8,128)(2,1)}, bf16[512,128]{1,0:T(8,128)(2,1)S(1)}, u32[]{:S(2)}, u32[]{:S(2)}) collective-permute-start(bf16[512,128]{1,0:T(8,128)(2,1)} %get-tuple-element.22), channel_id=1, source_target_pairs={{0,3},{1,2},{2,1},{3,0},{4,7},{5,6},{6,5},{7,4},{8,11},{9,10},{10,... | collective-permute-start | bytes 393224 | tf_op jit(solution)/shard_map/ppermute | solution.py:261
  87.2 8.4 %copy-start.5 = (bf16[512,128]{1,0:T(8,128)(2,1)}, bf16[512,128]{1,0:T(8,128)(2,1)S(1)}, u32[]{:S(2)}) copy-start(bf16[512,128]{1,0:T(8,128)(2,1)S(1)} %collective-permute-done.1.refs_1_) | copy-start | bytes 393220
  87.2 8.4 %collective-permute-start.6 = (bf16[512,128]{1,0:T(8,128)(2,1)}, bf16[512,128]{1,0:T(8,128)(2,1)S(1)}, u32[]{:S(2)}, u32[]{:S(2)}) collective-permute-start(bf16[512,128]{1,0:T(8,128)(2,1)} %get-tuple-element.23), channel_id=1, source_target_pairs={{0,7},{1,6},{2,5},{3,4},{4,3},{5,2},{6,1},{7,0},{8,15},{9,14},{10,... | collective-permute-start | bytes 393224 | tf_op jit(solution)/shard_map/ppermute | solution.py:261
  90.6 4.9 %copy-start.6 = (bf16[512,128]{1,0:T(8,128)(2,1)}, bf16[512,128]{1,0:T(8,128)(2,1)S(1)}, u32[]{:S(2)}) copy-start(bf16[512,128]{1,0:T(8,128)(2,1)S(1)} %collective-permute-done.2.refs_2_) | copy-start | bytes 393220
  90.6 4.9 %copy-start.7 = (bf16[512,128]{1,0:T(8,128)(2,1)}, bf16[512,128]{1,0:T(8,128)(2,1)S(1)}, u32[]{:S(2)}) copy-start(bf16[512,128]{1,0:T(8,128)(2,1)S(1)} %collective-permute-done.3.refs_3_) | copy-start | bytes 393220
  90.6 4.9 %copy-start.8 = (bf16[512,128]{1,0:T(8,128)(2,1)}, bf16[512,128]{1,0:T(8,128)(2,1)S(1)}, u32[]{:S(2)}) copy-start(bf16[512,128]{1,0:T(8,128)(2,1)S(1)} %collective-permute-done.4.refs_4_) | copy-start | bytes 393220
  95.5 0.7 copy-start.9
  95.5 0.7 copy-start.10
  103.5 1.9 %collective-permute-start.7 = (bf16[512,256]{1,0:T(8,128)(2,1)}, bf16[512,256]{1,0:T(8,128)(2,1)S(1)}, u32[]{:S(2)}, u32[]{:S(2)}) collective-permute-start(bf16[512,256]{1,0:T(8,128)(2,1)} %get-tuple-element.27), channel_id=1, source_target_pairs={{0,8},{8,0},{16,24},{24,16},{1,9},{9,1},{17,25},{25,17},{2,10},{10... | collective-permute-start | bytes 786440 | tf_op jit(solution)/shard_map/ppermute | solution.py:261
  103.5 9.4 %collective-permute-start.8 = (bf16[512,256]{1,0:T(8,128)(2,1)}, bf16[512,256]{1,0:T(8,128)(2,1)S(1)}, u32[]{:S(2)}, u32[]{:S(2)}) collective-permute-start(bf16[512,256]{1,0:T(8,128)(2,1)} %get-tuple-element.28), channel_id=1, source_target_pairs={{0,16},{8,24},{16,0},{24,8},{1,17},{9,25},{17,1},{25,9},{2,18},{10... | collective-permute-start | bytes 786440 | tf_op jit(solution)/shard_map/ppermute | solution.py:261
  105.1 12.5 %collective-permute-start.9 = (bf16[512,256]{1,0:T(8,128)(2,1)}, bf16[512,256]{1,0:T(8,128)(2,1)S(1)}, u32[]{:S(2)}, u32[]{:S(2)}) collective-permute-start(bf16[512,256]{1,0:T(8,128)(2,1)} %get-tuple-element.29), channel_id=1, source_target_pairs={{0,24},{8,16},{16,8},{24,0},{1,25},{9,17},{17,9},{25,1},{2,26},{10... | collective-permute-start | bytes 786440 | tf_op jit(solution)/shard_map/ppermute | solution.py:261
  105.4 12.2 %copy-start.1 = (bf16[512,256]{1,0:T(8,128)(2,1)}, bf16[512,256]{1,0:T(8,128)(2,1)S(1)}, u32[]{:S(2)}) copy-start(bf16[512,256]{1,0:T(8,128)(2,1)S(1)} %collective-permute-done.7.refs_1_) | copy-start | bytes 786436
  112.9 4.7 %copy-start.2 = (bf16[512,256]{1,0:T(8,128)(2,1)}, bf16[512,256]{1,0:T(8,128)(2,1)S(1)}, u32[]{:S(2)}) copy-start(bf16[512,256]{1,0:T(8,128)(2,1)S(1)} %collective-permute-done.8.refs_2_) | copy-start | bytes 786436
  117.6 0.7 copy-start.3

commit v5 on v3

--- a/solution.py
+++ b/solution.py
@@ -167,31 +167,36 @@
         copy.wait()
 
 
-def pick_kernel(order, where, whole, *refs):
-    outs, sems = refs[:-1], refs[-1]
-    copies = []
+def place_kernel(order, where, *refs):
+    pieces, (whole, slots, sems, out_sems) = refs[: len(order)], refs[len(order) :]
+    loads = [pltpu.make_async_copy(piece, slots.at[i], sems.at[i]) for i, piece in enumerate(pieces)]
+    for copy in loads:
+        copy.start()
+    stores = []
     for i, k in enumerate(order):
-        copies.append(pltpu.make_async_copy(piece_at(whole, where, k, outs[0].shape[0]), outs[i], sems.at[i]))
-        copies[-1].start()
-    for copy in copies:
+        loads[i].wait()
+        stores.append(pltpu.make_async_copy(slots.at[i], piece_at(whole, where, k, slots.shape[1]), out_sems.at[i]))
+        stores[-1].start()
+    for copy in stores:
         copy.wait()
 
 
-def place_kernel(order, where, *refs):
-    pieces, whole, sems = refs[: len(order)], refs[-2], refs[-1]
-    copies = []
+def taps_kernel(order, where, whole, taps, forward, *refs):
+    outs, (taps_spec, slots, mid, sems, out_sems) = refs[: len(order)], refs[len(order) :]
+    rows, width = (taps.shape[0], taps.shape[1] // BLOCKS)
+    loads, stores = [], []
     for i, k in enumerate(order):
-        copies.append(pltpu.make_async_copy(pieces[i], piece_at(whole, where, k, pieces[i].shape[0]), sems.at[i]))
-        copies[-1].start()
-    for copy in copies:
-        copy.wait()
-
-
-def taps_kernel(taps, forward, out, mid):
-    rows, width = (taps.shape[0], taps.shape[1] // BLOCKS)
+        loads.append(pltpu.make_async_copy(piece_at(whole, where, k, rows), slots.at[i], sems.at[i]))
+        loads[-1].start()
+    for i, out in enumerate(outs):
+        loads[i].wait()
+        stores.append(pltpu.make_async_copy(slots.at[i], out, out_sems.at[i]))
+        stores[-1].start()
     split_rows(lambda p, at: taps[at, p * width : (p + 1) * width], mid, rows, width)
     for r in range(GROUPS):
-        out[r] = spectrum(mid, forward, r, width).astype(out.dtype)
+        taps_spec[r] = spectrum(mid, forward, r, width).astype(taps_spec.dtype)
+    for copy in stores:
+        copy.wait()
 
 
 def ordered(order, where, refs, held):
@@ -212,7 +217,7 @@
     return store
 
 
-def back_kernel(order, where, *refs):
+def back_kernel(order, back_order, where, *refs):
     blocks, refs = refs[: len(order)], refs[len(order) :]
     taps_spec, forward, backward, *outs, grad_spec, held, mid, wide = refs
     rows, width = held.shape[0], held.shape[1] // BLOCKS
@@ -227,14 +232,15 @@
         invert_group(product.astype(jnp.bfloat16), backward, r, width, wide)
     merge_rows(wide, block_into(held, width), rows, width)
     span = outs[0].shape[1]
-    for k, out in zip(order, outs):
+    for k, out in zip(back_order, outs):
         start = pl.multiple_of(lax.bitwise_xor(where[0], k) * span, span)
         out[...] = held[:, pl.ds(start, span)]
 
 
-def cross_kernel(order, where, *refs):
-    blocks, refs = refs[: len(order)], refs[len(order) :]
+def cross_kernel(order, near, where, *refs):
+    blocks, refs = refs[: len(order)], refs[len(order) + near :]
     grad_spec, forward, backward, *outs, held, mid, wide = refs
+    outs = outs[near:]
     rows, width = held.shape[0], held.shape[1] // BLOCKS
     ordered(order, where, blocks, held)
     split_rows(block_of(held, width), mid, rows, width)
@@ -258,26 +264,33 @@
     refs[-1][...] = total * scale
 
 
-def call(kernel, operands, outs, scratch=(), scalar=True, flops=0, stream=False):
-    space = pl.ANY if stream else pltpu.VMEM
-    specs = [pl.BlockSpec(memory_space=space)] * len(operands)
-    if scalar:
+def call(kernel, operands, outs, scratch=(), flops=0, streams=(), out_streams=(), aliases=None):
+    def spec(stream):
+        return pl.BlockSpec(memory_space=pl.ANY if stream else pltpu.VMEM)
+
+    size = sum(math.prod(o.shape) * o.dtype.itemsize for o in list(operands) + list(outs))
+    specs = [spec(i in streams) for i in range(len(operands))]
+    if operands[0].dtype == jnp.int32:
         specs[0] = pl.BlockSpec(memory_space=pltpu.SMEM)
-    size = sum(math.prod(o.shape) * o.dtype.itemsize for o in list(operands) + list(outs))
     return pl.pallas_call(
         kernel,
         out_shape=list(outs),
         in_specs=specs,
-        out_specs=[pl.BlockSpec(memory_space=space)] * len(outs),
+        out_specs=[spec(i in out_streams) for i in range(len(outs))],
         scratch_shapes=list(scratch),
+        input_output_aliases=aliases or {},
         compiler_params=pltpu.CompilerParams(vmem_limit_bytes=LIMIT),
         cost_estimate=pl.CostEstimate(flops=flops, bytes_accessed=size, transcendentals=0),
     )(*operands)
 
 
 def far_first(size):
-    half = size // 2
-    return [k for pair in zip(range(half, size), [*range(1, half), 0]) for k in pair]
+    return [*range(size // 2, size), *range(1, size // 2), 0]
+
+
+def mixed(size):
+    far = far_first(size)
+    return [k for pair in zip(far[: size // 2], far[size // 2 :]) for k in pair]
 
 
 def exchange(pieces, order, axis, size):
@@ -292,17 +305,17 @@
     channels, span = saved_input.shape[1:]
     rows, length = long_filter.shape
     width = length // BLOCKS
-    order = far_first(count)
+    order, back_order, near = mixed(count), far_first(count), count // 2
+    every = range(count + 8)
     where = jnp.stack([lax.axis_index("ctx"), lax.axis_index("dp")]).astype(jnp.int32)
     forward, backward = (jnp.asarray(t) for t in transform_tables(width))
     half, full = jnp.bfloat16, jnp.float32
     piece = jax.ShapeDtypeStruct((rows, span), half)
-    blocks = jax.ShapeDtypeStruct((count, rows, span), half)
     spec = jax.ShapeDtypeStruct((GROUPS, rows, 2 * width), half)
     held = pltpu.VMEM((rows, length), half)
     mid = pltpu.VMEM((GROUPS, rows, 2 * width), half)
     wide = pltpu.VMEM((GROUPS, rows, 2 * width), full)
-    slots = pltpu.VMEM(blocks.shape, half)
+    slots = pltpu.VMEM((count, rows, span), half)
     sems = pltpu.SemaphoreType.DMA
     work = 2 * GROUPS * rows * 4 * width * width
 
@@ -311,48 +324,53 @@
         [where, out_gate[0], grad_out[0]],
         [piece] * count,
         [slots, slots, slots, sems((2, count)), sems((count,))],
-        stream=True,
+        streams=every,
+        out_streams=every,
     )
     grad_blocks = exchange(grad_pieces, order, "ctx", count)
-    input_pieces = call(
-        functools.partial(pick_kernel, order),
-        [where, saved_input[0]],
-        [piece] * count,
-        [sems((count,))],
-        stream=True,
+    *input_pieces, taps_spec = call(
+        functools.partial(taps_kernel, order),
+        [where, saved_input[0], long_filter, forward],
+        [piece] * count + [spec],
+        [slots, mid, sems((count,)), sems((count,))],
+        flops=work,
+        streams=(1,),
+        out_streams=range(count),
     )
     input_blocks = exchange(input_pieces, order, "ctx", count)
-    (taps_spec,) = call(taps_kernel, [long_filter, forward], [spec], [mid], scalar=False, flops=work)
     *back, grad_spec = call(
-        functools.partial(back_kernel, order),
+        functools.partial(back_kernel, order, back_order),
         [where, *grad_blocks, taps_spec, forward, backward],
         [piece] * count + [spec],
         [held, mid, wide],
         flops=2 * work,
     )
-    back_blocks = exchange(back, order, "ctx", count)
     share = jax.ShapeDtypeStruct((rows, length // shares), half)
     cross = call(
-        functools.partial(cross_kernel, order),
-        [where, *input_blocks, grad_spec, forward, backward],
-        [share] * shares,
+        functools.partial(cross_kernel, order, near),
+        [where, *input_blocks, *back[-near:], grad_spec, forward, backward],
+        [piece] * near + [share] * shares,
         [held, mid, wide],
         flops=2 * work,
-    )
-    cross_blocks = exchange(cross, range(shares), "dp", shares)
+        streams=range(1 + count, 1 + count + near),
+        out_streams=range(near),
+        aliases={1 + count + i: i for i in range(near)},
+    )
+    back_blocks = exchange([*back[:-near], *cross[:near]], back_order, "ctx", count)
+    cross_blocks = exchange(cross[near:], range(shares), "dp", shares)
     scale = 1.0 / math.sqrt(shares * length)
     (grad_filter,) = call(
         functools.partial(sum_kernel, scale),
         cross_blocks,
         [jax.ShapeDtypeStruct((rows, length // shares), full)],
-        scalar=False,
     )
     (grad_input,) = call(
-        functools.partial(place_kernel, order),
+        functools.partial(place_kernel, back_order),
         [where, *back_blocks],
         [jax.ShapeDtypeStruct((channels, span), half)],
-        [sems((count,))],
-        stream=True,
+        [slots, sems((count,)), sems((count,))],
+        streams=every,
+        out_streams=every,
     )
     return (grad_input[None], grad_filter)
 

time: 153 us -> 95.3 us (0.62)
  Pallas kernels: 92.8 us -> 29.8 us
  starting transfers between devices: 36.2 us -> 40.3 us
    pallas_call x7 -> x6, Pallas kernels: 92.8 us -> 29.8 us  [call(): pl.pallas_call(kernel, out_shape=list(outs), in_specs=specs, out_specs=[s...]
    ppermute x24, starting transfers between devices: 36.2 us -> 40.3 us  [exchange(): lax.ppermute(piece, axis, [(i, i ^ k) for i in range(size)])]
  transfers between devices with their start and end apart: 24 -> 24, of which waited for: 5 -> 6; matrix products, arithmetic and copies ran while one was open for 0% -> 0% of each run, Pallas kernels for 57% -> 26%
where the time goes in v5:
time: 95.3 us; the launch traced here: 95 us
  starting transfers between devices  40.3 us (42%)
  Pallas kernels  29.8 us (31%)
  waiting for transfers between devices  21.4 us (22%)
  local copies, waits for them, and re-layouts  2.15 us (2%)
    ppermute x24, starting transfers between devices, exchange(): lax.ppermute(piece, axis, [(i, i ^ k) for i in range(size)])  40.3 us
    pallas_call x6, Pallas kernels, call(): pl.pallas_call(kernel, out_shape=list(outs), in_specs=specs, out_specs=[s...  29.8 us
    ppermute x24, waiting for transfers between devices, exchange(): lax.ppermute(piece, axis, [(i, i ^ k) for i in range(size)])  21.4 us
    unnamed x48, local copies, waits for them, and re-layouts  2.15 us
  transfers between devices with their start and end apart: 24, of which 6 were waited for; matrix products, arithmetic and copies ran while one was open for 0% of the time, Pallas kernels for 26%

profile of v5, /device:TPU:0, one launch (start us, length us, event | category | flops | bytes accessed | tf_op | source)
XLA Modules:
  0.0 95.0 jit_solution(13124328547957055453)
XLA Ops:
  0.6 0.6 pad_add_fusion.where
  1.2 3.2 %shard_map.77 = (bf16[512,128]{1,0:T(8,128)(2,1)}, bf16[512,128]{1,0:T(8,128)(2,1)}, bf16[512,128]{1,0:T(8,128)(2,1)}, bf16[512,128]{1,0:T(8,128)(2,1)}, bf16[51...) custom-call(s32[2]{0:T(128)} %pad_add_fusion.where, ...), custom_call_target="tpu_custom_call" | custom-call | bytes 3145736 | tf_op jit(solution)/shard_map/pallas_call | solution.py:275
  4.4 4.1 %collective-permute-start = (bf16[512,128]{1,0:T(8,128)(2,1)}, bf16[512,128]{1,0:T(8,128)(2,1)S(1)}, u32[]{:S(2)}, u32[]{:S(2)}) collective-permute-start(bf16[512,128]{1,0:T(8,128)(2,1)} %get-tuple-element.36), channel_id=1, source_target_pairs={{0,4},{1,5},{2,6},{3,7},{4,0},{5,1},{6,2},{7,3},{8,12},{9,13},{10,... | collective-permute-start | bytes 393224 | tf_op jit(solution)/shard_map/ppermute | solution.py:299
  8.5 1.5 %collective-permute-start.1 = (bf16[512,128]{1,0:T(8,128)(2,1)}, bf16[512,128]{1,0:T(8,128)(2,1)S(1)}, u32[]{:S(2)}, u32[]{:S(2)}) collective-permute-start(bf16[512,128]{1,0:T(8,128)(2,1)} %get-tuple-element.37), channel_id=1, source_target_pairs={{0,1},{1,0},{2,3},{3,2},{4,5},{5,4},{6,7},{7,6},{8,9},{9,8},{10,11... | collective-permute-start | bytes 393224 | tf_op jit(solution)/shard_map/ppermute | solution.py:299
  10.0 0.0 collective-permute-start.2
  10.0 1.8 %collective-permute-start.3 = (bf16[512,128]{1,0:T(8,128)(2,1)}, bf16[512,128]{1,0:T(8,128)(2,1)S(1)}, u32[]{:S(2)}, u32[]{:S(2)}) collective-permute-start(bf16[512,128]{1,0:T(8,128)(2,1)} %get-tuple-element.39), channel_id=1, source_target_pairs={{0,2},{1,3},{2,0},{3,1},{4,6},{5,7},{6,4},{7,5},{8,10},{9,11},{10,... | collective-permute-start | bytes 393224 | tf_op jit(solution)/shard_map/ppermute | solution.py:299
  11.8 2.5 %collective-permute-start.4 = (bf16[512,128]{1,0:T(8,128)(2,1)}, bf16[512,128]{1,0:T(8,128)(2,1)S(1)}, u32[]{:S(2)}, u32[]{:S(2)}) collective-permute-start(bf16[512,128]{1,0:T(8,128)(2,1)} %get-tuple-element.40), channel_id=1, source_target_pairs={{0,6},{1,7},{2,4},{3,5},{4,2},{5,3},{6,0},{7,1},{8,14},{9,15},{10,... | collective-permute-start | bytes 393224 | tf_op jit(solution)/shard_map/ppermute | solution.py:299
  14.3 5.0 %collective-permute-done.refs_0_ = bf16[512,128]{1,0:T(8,128)(2,1)S(1)} collective-permute-done((bf16[512,128]{1,0:T(8,128)(2,1)}, bf16[512,128]{1,0:T(8,128)(2,1)S(1)}, u32[]{:S(2)}, u32[]{:S(2)}) %collective-permute-start) | collective-permute-done | bytes 131104 | tf_op jit(solution)/shard_map/ppermute | solution.py:299
  19.4 1.3 %collective-permute-start.5 = (bf16[512,128]{1,0:T(8,128)(2,1)}, bf16[512,128]{1,0:T(8,128)(2,1)S(1)}, u32[]{:S(2)}, u32[]{:S(2)}) collective-permute-start(bf16[512,128]{1,0:T(8,128)(2,1)} %get-tuple-element.41), channel_id=1, source_target_pairs={{0,3},{1,2},{2,1},{3,0},{4,7},{5,6},{6,5},{7,4},{8,11},{9,10},{10,... | collective-permute-start | bytes 393224 | tf_op jit(solution)/shard_map/ppermute | solution.py:299
  20.6 0.0 collective-permute-done.1.refs_1_
  20.6 4.5 %collective-permute-start.6 = (bf16[512,128]{1,0:T(8,128)(2,1)}, bf16[512,128]{1,0:T(8,128)(2,1)S(1)}, u32[]{:S(2)}, u32[]{:S(2)}) collective-permute-start(bf16[512,128]{1,0:T(8,128)(2,1)} %get-tuple-element.42), channel_id=1, source_target_pairs={{0,7},{1,6},{2,5},{3,4},{4,3},{5,2},{6,1},{7,0},{8,15},{9,14},{10,... | collective-permute-start | bytes 393224 | tf_op jit(solution)/shard_map/ppermute | solution.py:299
  25.1 6.3 %shard_map.78 = (bf16[512,128]{1,0:T(8,128)(2,1)}, bf16[512,128]{1,0:T(8,128)(2,1)}, bf16[512,128]{1,0:T(8,128)(2,1)}, bf16[512,128]{1,0:T(8,128)(2,1)}, bf16[51...) custom-call(s32[2]{0:T(128)} %pad_add_fusion.where, ...), custom_call_target="tpu_custom_call" | custom-call | flops 603979776 | bytes 7733256 | tf_op jit(solution)/shard_map/pallas_call | solution.py:275
  31.4 0.0 copy-done.5
  31.4 0.0 copy-done.7
  31.4 0.0 collective-permute-done.2.refs_2_
  31.4 0.6 collective-permute-start.11
  32.0 0.0 collective-permute-done.3.refs_3_
  32.0 0.8 collective-permute-start.12
  32.8 0.0 collective-permute-done.4.refs_4_
  32.8 3.1 %collective-permute-start.13 = (bf16[512,128]{1,0:T(8,128)(2,1)}, bf16[512,128]{1,0:T(8,128)(2,1)S(1)}, u32[]{:S(2)}, u32[]{:S(2)}) collective-permute-start(bf16[512,128]{1,0:T(8,128)(2,1)} %get-tuple-element.51), channel_id=1, source_target_pairs={{0,5},{1,4},{2,7},{3,6},{4,1},{5,0},{6,3},{7,2},{8,13},{9,12},{10,... | collective-permute-start | bytes 393224 | tf_op jit(solution)/shard_map/ppermute | solution.py:299
  35.9 0.0 collective-permute-done.5.refs_5_
  35.9 1.2 %collective-permute-start.14 = (bf16[512,128]{1,0:T(8,128)(2,1)}, bf16[512,128]{1,0:T(8,128)(2,1)S(1)}, u32[]{:S(2)}, u32[]{:S(2)}) collective-permute-start(bf16[512,128]{1,0:T(8,128)(2,1)} %get-tuple-element.52), channel_id=1, source_target_pairs={{0,2},{1,3},{2,0},{3,1},{4,6},{5,7},{6,4},{7,5},{8,10},{9,11},{10,... | collective-permute-start | bytes 393224 | tf_op jit(solution)/shard_map/ppermute | solution.py:299
  37.1 0.0 collective-permute-done.6.refs_6_
  37.1 0.8 collective-permute-start.15
  37.9 5.4 %collective-permute-done.11.refs_0_ = bf16[512,128]{1,0:T(8,128)(2,1)S(1)} collective-permute-done((bf16[512,128]{1,0:T(8,128)(2,1)}, bf16[512,128]{1,0:T(8,128)(2,1)S(1)}, u32[]{:S(2)}, u32[]{:S(2)}) %collective-permute-start.11) | collective-permute-done | bytes 131104 | tf_op jit(solution)/shard_map/ppermute | solution.py:299
  43.3 0.5 collective-permute-start.16
  43.8 0.0 collective-permute-done.12.refs_1_
  43.8 2.6 %collective-permute-start.17 = (bf16[512,128]{1,0:T(8,128)(2,1)}, bf16[512,128]{1,0:T(8,128)(2,1)S(1)}, u32[]{:S(2)}, u32[]{:S(2)}) collective-permute-start(bf16[512,128]{1,0:T(8,128)(2,1)} %get-tuple-element.55), channel_id=1, source_target_pairs={{0,7},{1,6},{2,5},{3,4},{4,3},{5,2},{6,1},{7,0},{8,15},{9,14},{10,... | collective-permute-start | bytes 393224 | tf_op jit(solution)/shard_map/ppermute | solution.py:299
  46.4 0.0 copy-done.10
  46.5 8.2 %shard_map.79 = (bf16[512,128]{1,0:T(8,128)(2,1)}, bf16[512,128]{1,0:T(8,128)(2,1)}, bf16[512,128]{1,0:T(8,128)(2,1)}, bf16[512,128]{1,0:T(8,128)(2,1)}, bf16[51...) custom-call(s32[2]{0:T(128)} %pad_add_fusion.where, ...), custom_call_target="tpu_custom_call" | custom-call | flops 1207959552 | bytes 9175048 | tf_op jit(solution)/shard_map/pallas_call | solution.py:275
  54.7 0.0 collective-permute-done.13.refs_2_
  54.7 0.0 copy-start.9
  54.7 1.4 %collective-permute-start.7 = (bf16[512,128]{1,0:T(8,128)(2,1)}, bf16[512,128]{1,0:T(8,128)(2,1)S(1)}, u32[]{:S(2)}, u32[]{:S(2)}) collective-permute-start(bf16[512,128]{1,0:T(8,128)(2,1)} %get-tuple-element.45), channel_id=1, source_target_pairs={{0,4},{1,5},{2,6},{3,7},{4,0},{5,1},{6,2},{7,3},{8,12},{9,13},{10,... | collective-permute-start | bytes 393224 | tf_op jit(solution)/shard_map/ppermute | solution.py:299
  56.1 0.0 collective-permute-done.14.refs_3_
  56.1 2.5 %collective-permute-start.8 = (bf16[512,128]{1,0:T(8,128)(2,1)}, bf16[512,128]{1,0:T(8,128)(2,1)S(1)}, u32[]{:S(2)}, u32[]{:S(2)}) collective-permute-start(bf16[512,128]{1,0:T(8,128)(2,1)} %get-tuple-element.46), channel_id=1, source_target_pairs={{0,5},{1,4},{2,7},{3,6},{4,1},{5,0},{6,3},{7,2},{8,13},{9,12},{10,... | collective-permute-start | bytes 393224 | tf_op jit(solution)/shard_map/ppermute | solution.py:299
  58.6 0.0 collective-permute-done.15.refs_4_
  58.6 1.2 %collective-permute-start.9 = (bf16[512,128]{1,0:T(8,128)(2,1)}, bf16[512,128]{1,0:T(8,128)(2,1)S(1)}, u32[]{:S(2)}, u32[]{:S(2)}) collective-permute-start(bf16[512,128]{1,0:T(8,128)(2,1)} %get-tuple-element.47), channel_id=1, source_target_pairs={{0,6},{1,7},{2,4},{3,5},{4,2},{5,3},{6,0},{7,1},{8,14},{9,15},{10,... | collective-permute-start | bytes 393224 | tf_op jit(solution)/shard_map/ppermute | solution.py:299
  59.8 0.0 collective-permute-done.16.refs_5_
  59.8 2.6 %collective-permute-start.10 = (bf16[512,128]{1,0:T(8,128)(2,1)}, bf16[512,128]{1,0:T(8,128)(2,1)S(1)}, u32[]{:S(2)}, u32[]{:S(2)}) collective-permute-start(bf16[512,128]{1,0:T(8,128)(2,1)} %get-tuple-element.48), channel_id=1, source_target_pairs={{0,7},{1,6},{2,5},{3,4},{4,3},{5,2},{6,1},{7,0},{8,15},{9,14},{10,... | collective-permute-start | bytes 393224 | tf_op jit(solution)/shard_map/ppermute | solution.py:299
  62.4 0.0 collective-permute-done.17.refs_6_
  62.5 0.6 copy-done.20
  63.1 7.3 %shard_map.80 = (bf16[512,128]{1,0:T(8,128)(2,1)}, bf16[512,128]{1,0:T(8,128)(2,1)}, bf16[512,128]{1,0:T(8,128)(2,1)}, bf16[512,128]{1,0:T(8,128)(2,1)}, bf16[51...) custom-call(s32[2]{0:T(128)} %pad_add_fusion.where, ...), custom_call_target="tpu_custom_call", output_to_operand_aliasing={{0}: (9, {}), {1}: (10, {}), {2}: (11, {}), {3}: (12, {})} | custom-call | flops 1207959552 | bytes 7864328 | tf_op jit(solution)/shard_map/pallas_call | solution.py:275
  70.4 1.5 %collective-permute-start.18 = (bf16[512,128]{1,0:T(8,128)(2,1)}, bf16[512,128]{1,0:T(8,128)(2,1)S(1)}, u32[]{:S(2)}, u32[]{:S(2)}) collective-permute-start(bf16[512,128]{1,0:T(8,128)(2,1)} %get-tuple-element.62), channel_id=1, source_target_pairs={{0,1},{1,0},{2,3},{3,2},{4,5},{5,4},{6,7},{7,6},{8,9},{9,8},{10,11... | collective-permute-start | bytes 393224 | tf_op jit(solution)/shard_map/ppermute | solution.py:299
  71.9 0.5 collective-permute-done.7.refs_0_
  72.4 0.0 collective-permute-start.21
  72.4 3.8 %collective-permute-done.8.refs_1_ = bf16[512,128]{1,0:T(8,128)(2,1)S(1)} collective-permute-done((bf16[512,128]{1,0:T(8,128)(2,1)}, bf16[512,128]{1,0:T(8,128)(2,1)S(1)}, u32[]{:S(2)}, u32[]{:S(2)}) %collective-permute-start.8) | collective-permute-done | bytes 131104 | tf_op jit(solution)/shard_map/ppermute | solution.py:299
  76.2 1.5 %collective-permute-start.22 = (bf16[512,256]{1,0:T(8,128)(2,1)}, bf16[512,256]{1,0:T(8,128)(2,1)S(1)}, u32[]{:S(2)}, u32[]{:S(2)}) collective-permute-start(bf16[512,256]{1,0:T(8,128)(2,1)} %get-tuple-element.68), channel_id=1, source_target_pairs={{0,16},{8,24},{16,0},{24,8},{1,17},{9,25},{17,1},{25,9},{2,18},{10... | collective-permute-start | bytes 786440 | tf_op jit(solution)/shard_map/ppermute | solution.py:299
  77.7 0.0 collective-permute-done.9.refs_2_
  77.7 0.0 collective-permute-start.23
  77.7 0.0 collective-permute-done.10.refs_3_
  77.8 3.3 %collective-permute-start.19 = (bf16[512,128]{1,0:T(8,128)(2,1)}, bf16[512,128]{1,0:T(8,128)(2,1)S(1)}, u32[]{:S(2)}, u32[]{:S(2)}) collective-permute-start(bf16[512,128]{1,0:T(8,128)(2,1)} %get-tuple-element.63), channel_id=1, source_target_pairs={{0,2},{1,3},{2,0},{3,1},{4,6},{5,7},{6,4},{7,5},{8,10},{9,11},{10,... | collective-permute-start | bytes 393224 | tf_op jit(solution)/shard_map/ppermute | solution.py:299
  81.1 0.0 collective-permute-done.18.refs_4_
  81.1 1.0 %collective-permute-start.20 = (bf16[512,128]{1,0:T(8,128)(2,1)}, bf16[512,128]{1,0:T(8,128)(2,1)S(1)}, u32[]{:S(2)}, u32[]{:S(2)}) collective-permute-start(bf16[512,128]{1,0:T(8,128)(2,1)} %get-tuple-element.64), channel_id=1, source_target_pairs={{0,3},{1,2},{2,1},{3,0},{4,7},{5,6},{6,5},{7,4},{8,11},{9,10},{10,... | collective-permute-start | bytes 393224 | tf_op jit(solution)/shard_map/ppermute | solution.py:299
  82.1 3.1 %collective-permute-done.19.refs_5_ = bf16[512,128]{1,0:T(8,128)(2,1)S(1)} collective-permute-done((bf16[512,128]{1,0:T(8,128)(2,1)}, bf16[512,128]{1,0:T(8,128)(2,1)S(1)}, u32[]{:S(2)}, u32[]{:S(2)}) %collective-permute-start.19) | collective-permute-done | bytes 131104 | tf_op jit(solution)/shard_map/ppermute | solution.py:299
  85.2 3.4 %collective-permute-done.20.refs_6_ = bf16[512,128]{1,0:T(8,128)(2,1)S(1)} collective-permute-done((bf16[512,128]{1,0:T(8,128)(2,1)}, bf16[512,128]{1,0:T(8,128)(2,1)S(1)}, u32[]{:S(2)}, u32[]{:S(2)}) %collective-permute-start.20) | collective-permute-done | bytes 131104 | tf_op jit(solution)/shard_map/ppermute | solution.py:299
  88.6 0.6 copy-done.23
  89.2 2.7 %shard_map.81 = bf16[4096,128]{1,0:T(8,128)(2,1)} custom-call(s32[2]{0:T(128)} %pad_add_fusion.where, bf16[512,128]{1,0:T(8,128)(2,1)} %copy-done.6, bf16[512,128]{1,0:T(8,128)(2,1)} %copy-done.11, bf16[512,128]{1,0:T(8,128)(2,1)} %copy-done.14, bf16[512,128]{1,0:T(8,128)(2,1)} %copy-done.17, bf16[512,128]{1,0:T(8,128)(2,1)} %copy-done.21, ...), custom_call_target="tpu_custom_call" | custom-call | bytes 2097160 | tf_op jit(solution)/shard_map/pallas_call | solution.py:275
  92.0 0.0 collective-permute-done.21.refs_1_
  92.0 0.0 collective-permute-done.22.refs_2_
  92.0 0.0 collective-permute-done.23.refs_3_
  92.1 0.6 copy-done
  92.7 0.1 copy-done.1
  92.8 0.1 copy-done.2
  92.9 2.1 %shard_map.82 = f32[512,256]{1,0:T(8,128)} custom-call(bf16[512,256]{1,0:T(8,128)(2,1)} %get-tuple-element.66.refs_0_, bf16[512,256]{1,0:T(8,128)(2,1)} %copy-done, bf16[512,256]{1,0:T(8,128)(2,1)} %copy-done.1, bf16[512,256]{1,0:T(8,128)(2,1)} %copy-done.2), custom_call_target="tpu_custom_call" | custom-call | bytes 1572864 | tf_op jit(solution)/shard_map/pallas_call | solution.py:275
  (39 shorter events, 0.1 us)
Async XLA Ops:
  4.4 15.0 %collective-permute-start = (bf16[512,128]{1,0:T(8,128)(2,1)}, bf16[512,128]{1,0:T(8,128)(2,1)S(1)}, u32[]{:S(2)}, u32[]{:S(2)}) collective-permute-start(bf16[512,128]{1,0:T(8,128)(2,1)} %get-tuple-element.36), channel_id=1, source_target_pairs={{0,4},{1,5},{2,6},{3,7},{4,0},{5,1},{6,2},{7,3},{8,12},{9,13},{10,... | collective-permute-start | bytes 393224 | tf_op jit(solution)/shard_map/ppermute | solution.py:299
  8.5 12.2 %collective-permute-start.1 = (bf16[512,128]{1,0:T(8,128)(2,1)}, bf16[512,128]{1,0:T(8,128)(2,1)S(1)}, u32[]{:S(2)}, u32[]{:S(2)}) collective-permute-start(bf16[512,128]{1,0:T(8,128)(2,1)} %get-tuple-element.37), channel_id=1, source_target_pairs={{0,1},{1,0},{2,3},{3,2},{4,5},{5,4},{6,7},{7,6},{8,9},{9,8},{10,11... | collective-permute-start | bytes 393224 | tf_op jit(solution)/shard_map/ppermute | solution.py:299
  10.0 21.4 %collective-permute-start.2 = (bf16[512,128]{1,0:T(8,128)(2,1)}, bf16[512,128]{1,0:T(8,128)(2,1)S(1)}, u32[]{:S(2)}, u32[]{:S(2)}) collective-permute-start(bf16[512,128]{1,0:T(8,128)(2,1)} %get-tuple-element.38), channel_id=1, source_target_pairs={{0,5},{1,4},{2,7},{3,6},{4,1},{5,0},{6,3},{7,2},{8,13},{9,12},{10,... | collective-permute-start | bytes 393224 | tf_op jit(solution)/shard_map/ppermute | solution.py:299
  10.0 22.0 %collective-permute-start.3 = (bf16[512,128]{1,0:T(8,128)(2,1)}, bf16[512,128]{1,0:T(8,128)(2,1)S(1)}, u32[]{:S(2)}, u32[]{:S(2)}) collective-permute-start(bf16[512,128]{1,0:T(8,128)(2,1)} %get-tuple-element.39), channel_id=1, source_target_pairs={{0,2},{1,3},{2,0},{3,1},{4,6},{5,7},{6,4},{7,5},{8,10},{9,11},{10,... | collective-permute-start | bytes 393224 | tf_op jit(solution)/shard_map/ppermute | solution.py:299
  11.8 21.0 %collective-permute-start.4 = (bf16[512,128]{1,0:T(8,128)(2,1)}, bf16[512,128]{1,0:T(8,128)(2,1)S(1)}, u32[]{:S(2)}, u32[]{:S(2)}) collective-permute-start(bf16[512,128]{1,0:T(8,128)(2,1)} %get-tuple-element.40), channel_id=1, source_target_pairs={{0,6},{1,7},{2,4},{3,5},{4,2},{5,3},{6,0},{7,1},{8,14},{9,15},{10,... | collective-permute-start | bytes 393224 | tf_op jit(solution)/shard_map/ppermute | solution.py:299
  19.4 12.0 %copy-start.5 = (bf16[512,128]{1,0:T(8,128)(2,1)}, bf16[512,128]{1,0:T(8,128)(2,1)S(1)}, u32[]{:S(2)}) copy-start(bf16[512,128]{1,0:T(8,128)(2,1)S(1)} %collective-permute-done.refs_0_) | copy-start | bytes 393220
  19.4 16.5 %collective-permute-start.5 = (bf16[512,128]{1,0:T(8,128)(2,1)}, bf16[512,128]{1,0:T(8,128)(2,1)S(1)}, u32[]{:S(2)}, u32[]{:S(2)}) collective-permute-start(bf16[512,128]{1,0:T(8,128)(2,1)} %get-tuple-element.41), channel_id=1, source_target_pairs={{0,3},{1,2},{2,1},{3,0},{4,7},{5,6},{6,5},{7,4},{8,11},{9,10},{10,... | collective-permute-start | bytes 393224 | tf_op jit(solution)/shard_map/ppermute | solution.py:299
  20.6 10.8 %copy-start.7 = (bf16[512,128]{1,0:T(8,128)(2,1)}, bf16[512,128]{1,0:T(8,128)(2,1)S(1)}, u32[]{:S(2)}) copy-start(bf16[512,128]{1,0:T(8,128)(2,1)S(1)} %collective-permute-done.1.refs_1_) | copy-start | bytes 393220
  20.6 16.5 %collective-permute-start.6 = (bf16[512,128]{1,0:T(8,128)(2,1)}, bf16[512,128]{1,0:T(8,128)(2,1)S(1)}, u32[]{:S(2)}, u32[]{:S(2)}) collective-permute-start(bf16[512,128]{1,0:T(8,128)(2,1)} %get-tuple-element.42), channel_id=1, source_target_pairs={{0,7},{1,6},{2,5},{3,4},{4,3},{5,2},{6,1},{7,0},{8,15},{9,14},{10,... | collective-permute-start | bytes 393224 | tf_op jit(solution)/shard_map/ppermute | solution.py:299
  31.4 15.0 %copy-start.8 = (bf16[512,128]{1,0:T(8,128)(2,1)}, bf16[512,128]{1,0:T(8,128)(2,1)S(1)}, u32[]{:S(2)}) copy-start(bf16[512,128]{1,0:T(8,128)(2,1)S(1)} %collective-permute-done.2.refs_2_) | copy-start | bytes 393220
  31.4 11.9 %collective-permute-start.11 = (bf16[512,128]{1,0:T(8,128)(2,1)}, bf16[512,128]{1,0:T(8,128)(2,1)S(1)}, u32[]{:S(2)}, u32[]{:S(2)}) collective-permute-start(bf16[512,128]{1,0:T(8,128)(2,1)} %get-tuple-element.49), channel_id=1, source_target_pairs={{0,4},{1,5},{2,6},{3,7},{4,0},{5,1},{6,2},{7,3},{8,12},{9,13},{10,... | collective-permute-start | bytes 393224 | tf_op jit(solution)/shard_map/ppermute | solution.py:299
  32.0 14.4 %copy-start.10 = (bf16[512,128]{1,0:T(8,128)(2,1)}, bf16[512,128]{1,0:T(8,128)(2,1)S(1)}, u32[]{:S(2)}) copy-start(bf16[512,128]{1,0:T(8,128)(2,1)S(1)} %collective-permute-done.3.refs_3_) | copy-start | bytes 393220
  32.0 11.8 %collective-permute-start.12 = (bf16[512,128]{1,0:T(8,128)(2,1)}, bf16[512,128]{1,0:T(8,128)(2,1)S(1)}, u32[]{:S(2)}, u32[]{:S(2)}) collective-permute-start(bf16[512,128]{1,0:T(8,128)(2,1)} %get-tuple-element.50), channel_id=1, source_target_pairs={{0,1},{1,0},{2,3},{3,2},{4,5},{5,4},{6,7},{7,6},{8,9},{9,8},{10,11... | collective-permute-start | bytes 393224 | tf_op jit(solution)/shard_map/ppermute | solution.py:299
  32.8 13.6 %copy-start.12 = (bf16[512,128]{1,0:T(8,128)(2,1)}, bf16[512,128]{1,0:T(8,128)(2,1)S(1)}, u32[]{:S(2)}) copy-start(bf16[512,128]{1,0:T(8,128)(2,1)S(1)} %collective-permute-done.4.refs_4_) | copy-start | bytes 393220
  32.8 21.9 %collective-permute-start.13 = (bf16[512,128]{1,0:T(8,128)(2,1)}, bf16[512,128]{1,0:T(8,128)(2,1)S(1)}, u32[]{:S(2)}, u32[]{:S(2)}) collective-permute-start(bf16[512,128]{1,0:T(8,128)(2,1)} %get-tuple-element.51), channel_id=1, source_target_pairs={{0,5},{1,4},{2,7},{3,6},{4,1},{5,0},{6,3},{7,2},{8,13},{9,12},{10,... | collective-permute-start | bytes 393224 | tf_op jit(solution)/shard_map/ppermute | solution.py:299
  35.9 10.6 %copy-start.15 = (bf16[512,128]{1,0:T(8,128)(2,1)}, bf16[512,128]{1,0:T(8,128)(2,1)S(1)}, u32[]{:S(2)}) copy-start(bf16[512,128]{1,0:T(8,128)(2,1)S(1)} %collective-permute-done.5.refs_5_) | copy-start | bytes 393220
  35.9 20.2 %collective-permute-start.14 = (bf16[512,128]{1,0:T(8,128)(2,1)}, bf16[512,128]{1,0:T(8,128)(2,1)S(1)}, u32[]{:S(2)}, u32[]{:S(2)}) collective-permute-start(bf16[512,128]{1,0:T(8,128)(2,1)} %get-tuple-element.52), channel_id=1, source_target_pairs={{0,2},{1,3},{2,0},{3,1},{4,6},{5,7},{6,4},{7,5},{8,10},{9,11},{10,... | collective-permute-start | bytes 393224 | tf_op jit(solution)/shard_map/ppermute | solution.py:299
  37.1 9.3 %copy-start.18 = (bf16[512,128]{1,0:T(8,128)(2,1)}, bf16[512,128]{1,0:T(8,128)(2,1)S(1)}, u32[]{:S(2)}) copy-start(bf16[512,128]{1,0:T(8,128)(2,1)S(1)} %collective-permute-done.6.refs_6_) | copy-start | bytes 393220
  37.1 21.5 %collective-permute-start.15 = (bf16[512,128]{1,0:T(8,128)(2,1)}, bf16[512,128]{1,0:T(8,128)(2,1)S(1)}, u32[]{:S(2)}, u32[]{:S(2)}) collective-permute-start(bf16[512,128]{1,0:T(8,128)(2,1)} %get-tuple-element.53), channel_id=1, source_target_pairs={{0,6},{1,7},{2,4},{3,5},{4,2},{5,3},{6,0},{7,1},{8,14},{9,15},{10,... | collective-permute-start | bytes 393224 | tf_op jit(solution)/shard_map/ppermute | solution.py:299
  43.3 11.3 %copy-start.3 = (bf16[512,128]{1,0:T(8,128)(2,1)}, bf16[512,128]{1,0:T(8,128)(2,1)S(1)}, u32[]{:S(2)}) copy-start(bf16[512,128]{1,0:T(8,128)(2,1)S(1)} %collective-permute-done.11.refs_0_) | copy-start | bytes 393220
  43.3 16.5 %collective-permute-start.16 = (bf16[512,128]{1,0:T(8,128)(2,1)}, bf16[512,128]{1,0:T(8,128)(2,1)S(1)}, u32[]{:S(2)}, u32[]{:S(2)}) collective-permute-start(bf16[512,128]{1,0:T(8,128)(2,1)} %get-tuple-element.54), channel_id=1, source_target_pairs={{0,3},{1,2},{2,1},{3,0},{4,7},{5,6},{6,5},{7,4},{8,11},{9,10},{10,... | collective-permute-start | bytes 393224 | tf_op jit(solution)/shard_map/ppermute | solution.py:299
  43.8 10.9 %copy-start.4 = (bf16[512,128]{1,0:T(8,128)(2,1)}, bf16[512,128]{1,0:T(8,128)(2,1)S(1)}, u32[]{:S(2)}) copy-start(bf16[512,128]{1,0:T(8,128)(2,1)S(1)} %collective-permute-done.12.refs_1_) | copy-start | bytes 393220
  43.8 18.6 %collective-permute-start.17 = (bf16[512,128]{1,0:T(8,128)(2,1)}, bf16[512,128]{1,0:T(8,128)(2,1)S(1)}, u32[]{:S(2)}, u32[]{:S(2)}) collective-permute-start(bf16[512,128]{1,0:T(8,128)(2,1)} %get-tuple-element.55), channel_id=1, source_target_pairs={{0,7},{1,6},{2,5},{3,4},{4,3},{5,2},{6,1},{7,0},{8,15},{9,14},{10,... | collective-permute-start | bytes 393224 | tf_op jit(solution)/shard_map/ppermute | solution.py:299
  54.7 7.8 %copy-start.9 = (bf16[512,128]{1,0:T(8,128)(2,1)}, bf16[512,128]{1,0:T(8,128)(2,1)S(1)}, u32[]{:S(2)}) copy-start(bf16[512,128]{1,0:T(8,128)(2,1)S(1)} %collective-permute-done.13.refs_2_) | copy-start | bytes 393220
  54.7 17.7 %collective-permute-start.7 = (bf16[512,128]{1,0:T(8,128)(2,1)}, bf16[512,128]{1,0:T(8,128)(2,1)S(1)}, u32[]{:S(2)}, u32[]{:S(2)}) collective-permute-start(bf16[512,128]{1,0:T(8,128)(2,1)} %get-tuple-element.45), channel_id=1, source_target_pairs={{0,4},{1,5},{2,6},{3,7},{4,0},{5,1},{6,2},{7,3},{8,12},{9,13},{10,... | collective-permute-start | bytes 393224 | tf_op jit(solution)/shard_map/ppermute | solution.py:299
  56.1 6.4 %copy-start.13 = (bf16[512,128]{1,0:T(8,128)(2,1)}, bf16[512,128]{1,0:T(8,128)(2,1)S(1)}, u32[]{:S(2)}) copy-start(bf16[512,128]{1,0:T(8,128)(2,1)S(1)} %collective-permute-done.14.refs_3_) | copy-start | bytes 393220
  56.1 20.1 %collective-permute-start.8 = (bf16[512,128]{1,0:T(8,128)(2,1)}, bf16[512,128]{1,0:T(8,128)(2,1)S(1)}, u32[]{:S(2)}, u32[]{:S(2)}) collective-permute-start(bf16[512,128]{1,0:T(8,128)(2,1)} %get-tuple-element.46), channel_id=1, source_target_pairs={{0,5},{1,4},{2,7},{3,6},{4,1},{5,0},{6,3},{7,2},{8,13},{9,12},{10,... | collective-permute-start | bytes 393224 | tf_op jit(solution)/shard_map/ppermute | solution.py:299
  58.6 3.9 %copy-start.16 = (bf16[512,128]{1,0:T(8,128)(2,1)}, bf16[512,128]{1,0:T(8,128)(2,1)S(1)}, u32[]{:S(2)}) copy-start(bf16[512,128]{1,0:T(8,128)(2,1)S(1)} %collective-permute-done.15.refs_4_) | copy-start | bytes 393220
  58.6 19.1 %collective-permute-start.9 = (bf16[512,128]{1,0:T(8,128)(2,1)}, bf16[512,128]{1,0:T(8,128)(2,1)S(1)}, u32[]{:S(2)}, u32[]{:S(2)}) collective-permute-start(bf16[512,128]{1,0:T(8,128)(2,1)} %get-tuple-element.47), channel_id=1, source_target_pairs={{0,6},{1,7},{2,4},{3,5},{4,2},{5,3},{6,0},{7,1},{8,14},{9,15},{10,... | collective-permute-start | bytes 393224 | tf_op jit(solution)/shard_map/ppermute | solution.py:299
  59.8 2.6 %copy-start.19 = (bf16[512,128]{1,0:T(8,128)(2,1)}, bf16[512,128]{1,0:T(8,128)(2,1)S(1)}, u32[]{:S(2)}) copy-start(bf16[512,128]{1,0:T(8,128)(2,1)S(1)} %collective-permute-done.16.refs_5_) | copy-start | bytes 393220
  59.8 17.9 %collective-permute-start.10 = (bf16[512,128]{1,0:T(8,128)(2,1)}, bf16[512,128]{1,0:T(8,128)(2,1)S(1)}, u32[]{:S(2)}, u32[]{:S(2)}) collective-permute-start(bf16[512,128]{1,0:T(8,128)(2,1)} %get-tuple-element.48), channel_id=1, source_target_pairs={{0,7},{1,6},{2,5},{3,4},{4,3},{5,2},{6,1},{7,0},{8,15},{9,14},{10,... | collective-permute-start | bytes 393224 | tf_op jit(solution)/shard_map/ppermute | solution.py:299
  62.4 0.7 copy-start.20
  70.4 10.7 %collective-permute-start.18 = (bf16[512,128]{1,0:T(8,128)(2,1)}, bf16[512,128]{1,0:T(8,128)(2,1)S(1)}, u32[]{:S(2)}, u32[]{:S(2)}) collective-permute-start(bf16[512,128]{1,0:T(8,128)(2,1)} %get-tuple-element.62), channel_id=1, source_target_pairs={{0,1},{1,0},{2,3},{3,2},{4,5},{5,4},{6,7},{7,6},{8,9},{9,8},{10,11... | collective-permute-start | bytes 393224 | tf_op jit(solution)/shard_map/ppermute | solution.py:299
  72.4 16.2 %copy-start.6 = (bf16[512,128]{1,0:T(8,128)(2,1)}, bf16[512,128]{1,0:T(8,128)(2,1)S(1)}, u32[]{:S(2)}) copy-start(bf16[512,128]{1,0:T(8,128)(2,1)S(1)} %collective-permute-done.7.refs_0_) | copy-start | bytes 393220
  72.4 19.6 %collective-permute-start.21 = (bf16[512,256]{1,0:T(8,128)(2,1)}, bf16[512,256]{1,0:T(8,128)(2,1)S(1)}, u32[]{:S(2)}, u32[]{:S(2)}) collective-permute-start(bf16[512,256]{1,0:T(8,128)(2,1)} %get-tuple-element.67), channel_id=1, source_target_pairs={{0,8},{8,0},{16,24},{24,16},{1,9},{9,1},{17,25},{25,17},{2,10},{10... | collective-permute-start | bytes 786440 | tf_op jit(solution)/shard_map/ppermute | solution.py:299
  76.2 12.4 %copy-start.11 = (bf16[512,128]{1,0:T(8,128)(2,1)}, bf16[512,128]{1,0:T(8,128)(2,1)S(1)}, u32[]{:S(2)}) copy-start(bf16[512,128]{1,0:T(8,128)(2,1)S(1)} %collective-permute-done.8.refs_1_) | copy-start | bytes 393220
  76.2 15.8 %collective-permute-start.22 = (bf16[512,256]{1,0:T(8,128)(2,1)}, bf16[512,256]{1,0:T(8,128)(2,1)S(1)}, u32[]{:S(2)}, u32[]{:S(2)}) collective-permute-start(bf16[512,256]{1,0:T(8,128)(2,1)} %get-tuple-element.68), channel_id=1, source_target_pairs={{0,16},{8,24},{16,0},{24,8},{1,17},{9,25},{17,1},{25,9},{2,18},{10... | collective-permute-start | bytes 786440 | tf_op jit(solution)/shard_map/ppermute | solution.py:299
  77.7 10.9 %copy-start.14 = (bf16[512,128]{1,0:T(8,128)(2,1)}, bf16[512,128]{1,0:T(8,128)(2,1)S(1)}, u32[]{:S(2)}) copy-start(bf16[512,128]{1,0:T(8,128)(2,1)S(1)} %collective-permute-done.9.refs_2_) | copy-start | bytes 393220
  77.7 14.3 %collective-permute-start.23 = (bf16[512,256]{1,0:T(8,128)(2,1)}, bf16[512,256]{1,0:T(8,128)(2,1)S(1)}, u32[]{:S(2)}, u32[]{:S(2)}) collective-permute-start(bf16[512,256]{1,0:T(8,128)(2,1)} %get-tuple-element.69), channel_id=1, source_target_pairs={{0,24},{8,16},{16,8},{24,0},{1,25},{9,17},{17,9},{25,1},{2,26},{10... | collective-permute-start | bytes 786440 | tf_op jit(solution)/shard_map/ppermute | solution.py:299
  77.7 10.9 %copy-start.17 = (bf16[512,128]{1,0:T(8,128)(2,1)}, bf16[512,128]{1,0:T(8,128)(2,1)S(1)}, u32[]{:S(2)}) copy-start(bf16[512,128]{1,0:T(8,128)(2,1)S(1)} %collective-permute-done.10.refs_3_) | copy-start | bytes 393220
  77.8 7.5 %collective-permute-start.19 = (bf16[512,128]{1,0:T(8,128)(2,1)}, bf16[512,128]{1,0:T(8,128)(2,1)S(1)}, u32[]{:S(2)}, u32[]{:S(2)}) collective-permute-start(bf16[512,128]{1,0:T(8,128)(2,1)} %get-tuple-element.63), channel_id=1, source_target_pairs={{0,2},{1,3},{2,0},{3,1},{4,6},{5,7},{6,4},{7,5},{8,10},{9,11},{10,... | collective-permute-start | bytes 393224 | tf_op jit(solution)/shard_map/ppermute | solution.py:299
  81.1 7.5 %copy-start.21 = (bf16[512,128]{1,0:T(8,128)(2,1)}, bf16[512,128]{1,0:T(8,128)(2,1)S(1)}, u32[]{:S(2)}) copy-start(bf16[512,128]{1,0:T(8,128)(2,1)S(1)} %collective-permute-done.18.refs_4_) | copy-start | bytes 393220
  81.1 7.5 %collective-permute-start.20 = (bf16[512,128]{1,0:T(8,128)(2,1)}, bf16[512,128]{1,0:T(8,128)(2,1)S(1)}, u32[]{:S(2)}, u32[]{:S(2)}) collective-permute-start(bf16[512,128]{1,0:T(8,128)(2,1)} %get-tuple-element.64), channel_id=1, source_target_pairs={{0,3},{1,2},{2,1},{3,0},{4,7},{5,6},{6,5},{7,4},{8,11},{9,10},{10,... | collective-permute-start | bytes 393224 | tf_op jit(solution)/shard_map/ppermute | solution.py:299
  85.2 3.4 %copy-start.22 = (bf16[512,128]{1,0:T(8,128)(2,1)}, bf16[512,128]{1,0:T(8,128)(2,1)S(1)}, u32[]{:S(2)}) copy-start(bf16[512,128]{1,0:T(8,128)(2,1)S(1)} %collective-permute-done.19.refs_5_) | copy-start | bytes 393220
  88.6 0.7 copy-start.23
  92.0 0.7 copy-start
  92.0 0.8 copy-start.1
  92.0 0.8 copy-start.2

commit v6 on v5

--- a/solution.py
+++ b/solution.py
@@ -217,9 +217,10 @@
     return store
 
 
-def back_kernel(order, back_order, where, *refs):
-    blocks, refs = refs[: len(order)], refs[len(order) :]
+def back_kernel(order, back_order, late, where, *refs):
+    blocks, refs = refs[: len(order)], refs[len(order) + late :]
     taps_spec, forward, backward, *outs, grad_spec, held, mid, wide = refs
+    outs = outs[late:]
     rows, width = held.shape[0], held.shape[1] // BLOCKS
     ordered(order, where, blocks, held)
     split_rows(block_of(held, width), mid, rows, width)
@@ -288,6 +289,10 @@
     return [*range(size // 2, size), *range(1, size // 2), 0]
 
 
+def near_first(size):
+    return [*range(1, size), 0]
+
+
 def mixed(size):
     far = far_first(size)
     return [k for pair in zip(far[: size // 2], far[size // 2 :]) for k in pair]
@@ -305,7 +310,8 @@
     channels, span = saved_input.shape[1:]
     rows, length = long_filter.shape
     width = length // BLOCKS
-    order, back_order, near = mixed(count), far_first(count), count // 2
+    order, back_order, near = mixed(count), near_first(count), 0
+    late, at = 2, count - 1 - 2
     every = range(count + 8)
     where = jnp.stack([lax.axis_index("ctx"), lax.axis_index("dp")]).astype(jnp.int32)
     forward, backward = (jnp.asarray(t) for t in transform_tables(width))
@@ -337,18 +343,22 @@
         streams=(1,),
         out_streams=range(count),
     )
-    input_blocks = exchange(input_pieces, order, "ctx", count)
     *back, grad_spec = call(
-        functools.partial(back_kernel, order, back_order),
-        [where, *grad_blocks, taps_spec, forward, backward],
-        [piece] * count + [spec],
+        functools.partial(back_kernel, order, back_order, late),
+        [where, *grad_blocks, *input_pieces[at : at + late], taps_spec, forward, backward],
+        [piece] * (late + count) + [spec],
         [held, mid, wide],
         flops=2 * work,
-    )
+        streams=range(1 + count, 1 + count + late),
+        out_streams=range(late),
+        aliases={1 + count + i: i for i in range(late)},
+    )
+    input_pieces[at : at + late], back = back[:late], back[late:]
+    input_blocks = exchange(input_pieces, order, "ctx", count)
     share = jax.ShapeDtypeStruct((rows, length // shares), half)
     cross = call(
         functools.partial(cross_kernel, order, near),
-        [where, *input_blocks, *back[-near:], grad_spec, forward, backward],
+        [where, *input_blocks, *back[count - near :], grad_spec, forward, backward],
         [piece] * near + [share] * shares,
         [held, mid, wide],
         flops=2 * work,
@@ -356,7 +366,7 @@
         out_streams=range(near),
         aliases={1 + count + i: i for i in range(near)},
     )
-    back_blocks = exchange([*back[:-near], *cross[:near]], back_order, "ctx", count)
+    back_blocks = exchange([*back[: count - near], *cross[:near]], back_order, "ctx", count)
     cross_blocks = exchange(cross[near:], range(shares), "dp", shares)
     scale = 1.0 / math.sqrt(shares * length)
     (grad_filter,) = call(

time: 95.3 us -> 89.6 us (0.940)
  the two profiles are of different devices: /device:TPU:0 before, /device:TPU:9 now
where the time goes in v6:
time: 89.6 us; the launch traced here: 89.4 us
  starting transfers between devices  38.3 us (43%)
  Pallas kernels  29.8 us (33%)
  waiting for transfers between devices  18.1 us (20%)
  local copies, waits for them, and re-layouts  1.55 us (2%)
  between operations  0.92 us (1%)
    ppermute x24, starting transfers between devices, exchange(): lax.ppermute(piece, axis, [(i, i ^ k) for i in range(size)])  38.3 us
    pallas_call x6, Pallas kernels, call(): pl.pallas_call(kernel, out_shape=list(outs), in_specs=specs, out_specs=[s...  29.8 us
    ppermute x24, waiting for transfers between devices, exchange(): lax.ppermute(piece, axis, [(i, i ^ k) for i in range(size)])  18.1 us
  transfers between devices with their start and end apart: 24, of which 5 were waited for; matrix products, arithmetic and copies ran while one was open for 0% of the time, Pallas kernels for 27%

profile of v6, /device:TPU:9, one launch (start us, length us, event | category | flops | bytes accessed | tf_op | source)
XLA Modules:
  0.0 89.4 jit_solution(10399060631822427234)
XLA Ops:
  0.6 0.6 pad_add_fusion.where
  1.3 3.1 %shard_map.77 = (bf16[512,128]{1,0:T(8,128)(2,1)}, bf16[512,128]{1,0:T(8,128)(2,1)}, bf16[512,128]{1,0:T(8,128)(2,1)}, bf16[512,128]{1,0:T(8,128)(2,1)}, bf16[51...) custom-call(s32[2]{0:T(128)} %pad_add_fusion.where, ...), custom_call_target="tpu_custom_call" | custom-call | bytes 3145736 | tf_op jit(solution)/shard_map/pallas_call | solution.py:276
  4.4 2.4 %collective-permute-start = (bf16[512,128]{1,0:T(8,128)(2,1)}, bf16[512,128]{1,0:T(8,128)(2,1)S(1)}, u32[]{:S(2)}, u32[]{:S(2)}) collective-permute-start(bf16[512,128]{1,0:T(8,128)(2,1)} %get-tuple-element.34), channel_id=1, source_target_pairs={{0,4},{1,5},{2,6},{3,7},{4,0},{5,1},{6,2},{7,3},{8,12},{9,13},{10,... | collective-permute-start | bytes 393224 | tf_op jit(solution)/shard_map/ppermute | solution.py:304
  6.8 1.2 %collective-permute-start.1 = (bf16[512,128]{1,0:T(8,128)(2,1)}, bf16[512,128]{1,0:T(8,128)(2,1)S(1)}, u32[]{:S(2)}, u32[]{:S(2)}) collective-permute-start(bf16[512,128]{1,0:T(8,128)(2,1)} %get-tuple-element.35), channel_id=1, source_target_pairs={{0,1},{1,0},{2,3},{3,2},{4,5},{5,4},{6,7},{7,6},{8,9},{9,8},{10,11... | collective-permute-start | bytes 393224 | tf_op jit(solution)/shard_map/ppermute | solution.py:304
  8.0 0.0 collective-permute-start.2
  8.1 0.2 collective-permute-start.3
  8.2 2.4 %collective-permute-start.4 = (bf16[512,128]{1,0:T(8,128)(2,1)}, bf16[512,128]{1,0:T(8,128)(2,1)S(1)}, u32[]{:S(2)}, u32[]{:S(2)}) collective-permute-start(bf16[512,128]{1,0:T(8,128)(2,1)} %get-tuple-element.38), channel_id=1, source_target_pairs={{0,6},{1,7},{2,4},{3,5},{4,2},{5,3},{6,0},{7,1},{8,14},{9,15},{10,... | collective-permute-start | bytes 393224 | tf_op jit(solution)/shard_map/ppermute | solution.py:304
  10.6 5.8 %collective-permute-done.refs_0_ = bf16[512,128]{1,0:T(8,128)(2,1)S(1)} collective-permute-done((bf16[512,128]{1,0:T(8,128)(2,1)}, bf16[512,128]{1,0:T(8,128)(2,1)S(1)}, u32[]{:S(2)}, u32[]{:S(2)}) %collective-permute-start) | collective-permute-done | bytes 131104 | tf_op jit(solution)/shard_map/ppermute | solution.py:304
  16.4 0.0 collective-permute-start.5
  16.4 0.0 collective-permute-done.1.refs_1_
  16.5 4.7 %collective-permute-start.6 = (bf16[512,128]{1,0:T(8,128)(2,1)}, bf16[512,128]{1,0:T(8,128)(2,1)S(1)}, u32[]{:S(2)}, u32[]{:S(2)}) collective-permute-start(bf16[512,128]{1,0:T(8,128)(2,1)} %get-tuple-element.40), channel_id=1, source_target_pairs={{0,7},{1,6},{2,5},{3,4},{4,3},{5,2},{6,1},{7,0},{8,15},{9,14},{10,... | collective-permute-start | bytes 393224 | tf_op jit(solution)/shard_map/ppermute | solution.py:304
  21.1 6.3 %shard_map.78 = (bf16[512,128]{1,0:T(8,128)(2,1)}, bf16[512,128]{1,0:T(8,128)(2,1)}, bf16[512,128]{1,0:T(8,128)(2,1)}, bf16[512,128]{1,0:T(8,128)(2,1)}, bf16[51...) custom-call(s32[2]{0:T(128)} %pad_add_fusion.where, ...), custom_call_target="tpu_custom_call" | custom-call | flops 603979776 | bytes 7733256 | tf_op jit(solution)/shard_map/pallas_call | solution.py:276
  27.4 0.0 copy-done.8
  27.4 0.0 collective-permute-done.2.refs_2_
  27.4 0.1 collective-permute-start.14
  27.5 0.0 collective-permute-done.3.refs_3_
  27.5 1.3 %collective-permute-start.15 = (bf16[512,128]{1,0:T(8,128)(2,1)}, bf16[512,128]{1,0:T(8,128)(2,1)S(1)}, u32[]{:S(2)}, u32[]{:S(2)}) collective-permute-start(bf16[512,128]{1,0:T(8,128)(2,1)} %get-tuple-element.54), channel_id=1, source_target_pairs={{0,1},{1,0},{2,3},{3,2},{4,5},{5,4},{6,7},{7,6},{8,9},{9,8},{10,11... | collective-permute-start | bytes 393224 | tf_op jit(solution)/shard_map/ppermute | solution.py:304
  28.8 0.0 collective-permute-done.4.refs_4_
  28.8 2.2 %collective-permute-start.16 = (bf16[512,128]{1,0:T(8,128)(2,1)}, bf16[512,128]{1,0:T(8,128)(2,1)S(1)}, u32[]{:S(2)}, u32[]{:S(2)}) collective-permute-start(bf16[512,128]{1,0:T(8,128)(2,1)} %get-tuple-element.55), channel_id=1, source_target_pairs={{0,5},{1,4},{2,7},{3,6},{4,1},{5,0},{6,3},{7,2},{8,13},{9,12},{10,... | collective-permute-start | bytes 393224 | tf_op jit(solution)/shard_map/ppermute | solution.py:304
  31.1 0.0 collective-permute-done.5.refs_5_
  31.1 1.0 %collective-permute-start.17 = (bf16[512,128]{1,0:T(8,128)(2,1)}, bf16[512,128]{1,0:T(8,128)(2,1)S(1)}, u32[]{:S(2)}, u32[]{:S(2)}) collective-permute-start(bf16[512,128]{1,0:T(8,128)(2,1)} %get-tuple-element.56), channel_id=1, source_target_pairs={{0,2},{1,3},{2,0},{3,1},{4,6},{5,7},{6,4},{7,5},{8,10},{9,11},{10,... | collective-permute-start | bytes 393224 | tf_op jit(solution)/shard_map/ppermute | solution.py:304
  32.1 0.0 collective-permute-done.6.refs_6_
  32.1 2.3 %collective-permute-start.18 = (bf16[512,128]{1,0:T(8,128)(2,1)}, bf16[512,128]{1,0:T(8,128)(2,1)S(1)}, u32[]{:S(2)}, u32[]{:S(2)}) collective-permute-start(bf16[512,128]{1,0:T(8,128)(2,1)} %get-tuple-element.57), channel_id=1, source_target_pairs={{0,6},{1,7},{2,4},{3,5},{4,2},{5,3},{6,0},{7,1},{8,14},{9,15},{10,... | collective-permute-start | bytes 393224 | tf_op jit(solution)/shard_map/ppermute | solution.py:304
  34.4 0.0 copy-done.13
  34.4 0.0 copy-done.17
  34.5 8.2 %shard_map.79 = (bf16[512,128]{1,0:T(8,128)(2,1)}, bf16[512,128]{1,0:T(8,128)(2,1)}, bf16[512,128]{1,0:T(8,128)(2,1)}, bf16[512,128]{1,0:T(8,128)(2,1)}, bf16[51...) custom-call(s32[2]{0:T(128)} %pad_add_fusion.where, ...), custom_call_target="tpu_custom_call", output_to_operand_aliasing={{0}: (9, {}), {1}: (10, {})} | custom-call | flops 1207959552 | bytes 9699336 | tf_op jit(solution)/shard_map/pallas_call | solution.py:276
  42.7 0.0 collective-permute-done.14.refs_0_
  42.7 0.0 copy-start.3
  42.7 0.1 collective-permute-start.19
  42.8 0.0 collective-permute-done.15.refs_1_
  42.8 1.3 %collective-permute-start.20 = (bf16[512,128]{1,0:T(8,128)(2,1)}, bf16[512,128]{1,0:T(8,128)(2,1)S(1)}, u32[]{:S(2)}, u32[]{:S(2)}) collective-permute-start(bf16[512,128]{1,0:T(8,128)(2,1)} %get-tuple-element.59), channel_id=1, source_target_pairs={{0,7},{1,6},{2,5},{3,4},{4,3},{5,2},{6,1},{7,0},{8,15},{9,14},{10,... | collective-permute-start | bytes 393224 | tf_op jit(solution)/shard_map/ppermute | solution.py:304
  44.1 0.0 collective-permute-done.16.refs_2_
  44.1 1.2 %collective-permute-start.7 = (bf16[512,128]{1,0:T(8,128)(2,1)}, bf16[512,128]{1,0:T(8,128)(2,1)S(1)}, u32[]{:S(2)}, u32[]{:S(2)}) collective-permute-start(bf16[512,128]{1,0:T(8,128)(2,1)} %get-tuple-element.45), channel_id=1, source_target_pairs={{0,1},{1,0},{2,3},{3,2},{4,5},{5,4},{6,7},{7,6},{8,9},{9,8},{10,11... | collective-permute-start | bytes 393224 | tf_op jit(solution)/shard_map/ppermute | solution.py:304
  45.4 0.0 collective-permute-done.17.refs_3_
  45.4 1.9 %collective-permute-start.8 = (bf16[512,128]{1,0:T(8,128)(2,1)}, bf16[512,128]{1,0:T(8,128)(2,1)S(1)}, u32[]{:S(2)}, u32[]{:S(2)}) collective-permute-start(bf16[512,128]{1,0:T(8,128)(2,1)} %get-tuple-element.46), channel_id=1, source_target_pairs={{0,2},{1,3},{2,0},{3,1},{4,6},{5,7},{6,4},{7,5},{8,10},{9,11},{10,... | collective-permute-start | bytes 393224 | tf_op jit(solution)/shard_map/ppermute | solution.py:304
  47.3 0.4 collective-permute-done.18.refs_4_
  47.8 0.2 collective-permute-start.9
  48.0 0.5 collective-permute-done.19.refs_5_
  48.5 4.0 %collective-permute-start.10 = (bf16[512,128]{1,0:T(8,128)(2,1)}, bf16[512,128]{1,0:T(8,128)(2,1)S(1)}, u32[]{:S(2)}, u32[]{:S(2)}) collective-permute-start(bf16[512,128]{1,0:T(8,128)(2,1)} %get-tuple-element.48), channel_id=1, source_target_pairs={{0,4},{1,5},{2,6},{3,7},{4,0},{5,1},{6,2},{7,3},{8,12},{9,13},{10,... | collective-permute-start | bytes 393224 | tf_op jit(solution)/shard_map/ppermute | solution.py:304
  52.5 0.0 collective-permute-done.20.refs_6_
  52.5 1.1 %collective-permute-start.11 = (bf16[512,128]{1,0:T(8,128)(2,1)}, bf16[512,128]{1,0:T(8,128)(2,1)S(1)}, u32[]{:S(2)}, u32[]{:S(2)}) collective-permute-start(bf16[512,128]{1,0:T(8,128)(2,1)} %get-tuple-element.49), channel_id=1, source_target_pairs={{0,5},{1,4},{2,7},{3,6},{4,1},{5,0},{6,3},{7,2},{8,13},{9,12},{10,... | collective-permute-start | bytes 393224 | tf_op jit(solution)/shard_map/ppermute | solution.py:304
  53.6 7.3 %shard_map.81 = (bf16[512,256]{1,0:T(8,128)(2,1)}, bf16[512,256]{1,0:T(8,128)(2,1)}, bf16[512,256]{1,0:T(8,128)(2,1)}, bf16[512,256]{1,0:T(8,128)(2,1)}) custom-call(s32[2]{0:T(128)} %pad_add_fusion.where, bf16[512,128]{1,0:T(8,128)(2,1)} %copy-done.3, bf16[512,128]{1,0:T(8,128)(2,1)} %copy-done.4, bf16[512,128]{1,0:T(8,128)(2,1)} %copy-done.5, ...), custom_call_target="tpu_custom_call" | custom-call | flops 1207959552 | bytes 6815752 | tf_op jit(solution)/shard_map/pallas_call | solution.py:276
  60.9 0.0 collective-permute-done.7.refs_0_
  61.0 5.4 %collective-permute-start.21 = (bf16[512,256]{1,0:T(8,128)(2,1)}, bf16[512,256]{1,0:T(8,128)(2,1)S(1)}, u32[]{:S(2)}, u32[]{:S(2)}) collective-permute-start(bf16[512,256]{1,0:T(8,128)(2,1)} %get-tuple-element.63), channel_id=1, source_target_pairs={{0,8},{8,0},{16,24},{24,16},{1,9},{9,1},{17,25},{25,17},{2,10},{10... | collective-permute-start | bytes 786440 | tf_op jit(solution)/shard_map/ppermute | solution.py:304
  66.4 0.0 collective-permute-done.8.refs_1_
  66.4 1.2 %collective-permute-start.22 = (bf16[512,256]{1,0:T(8,128)(2,1)}, bf16[512,256]{1,0:T(8,128)(2,1)S(1)}, u32[]{:S(2)}, u32[]{:S(2)}) collective-permute-start(bf16[512,256]{1,0:T(8,128)(2,1)} %get-tuple-element.64), channel_id=1, source_target_pairs={{0,16},{8,24},{16,0},{24,8},{1,17},{9,25},{17,1},{25,9},{2,18},{10... | collective-permute-start | bytes 786440 | tf_op jit(solution)/shard_map/ppermute | solution.py:304
  67.6 0.0 collective-permute-done.9.refs_2_
  67.6 0.5 collective-permute-start.23
  68.1 0.0 collective-permute-done.10.refs_3_
  68.1 0.3 collective-permute-start.12
  68.4 0.0 collective-permute-done.11.refs_4_
  68.4 3.2 %collective-permute-start.13 = (bf16[512,128]{1,0:T(8,128)(2,1)S(1)}, bf16[512,128]{1,0:T(8,128)(2,1)S(1)}, u32[]{:S(2)}, u32[]{:S(2)}) collective-permute-start(bf16[512,128]{1,0:T(8,128)(2,1)S(1)} %copy-done.24), channel_id=1, source_target_pairs={{0,7},{1,6},{2,5},{3,4},{4,3},{5,2},{6,1},{7,0},{8,15},{9,14},{10,... | collective-permute-start | bytes 393224 | tf_op jit(solution)/shard_map/ppermute | solution.py:304
  71.6 7.2 %collective-permute-done.12.refs_5_ = bf16[512,128]{1,0:T(8,128)(2,1)S(1)} collective-permute-done((bf16[512,128]{1,0:T(8,128)(2,1)S(1)}, bf16[512,128]{1,0:T(8,128)(2,1)S(1)}, u32[]{:S(2)}, u32[]{:S(2)}) %collective-permute-start.12) | collective-permute-done | bytes 131104 | tf_op jit(solution)/shard_map/ppermute | solution.py:304
  78.8 4.1 %collective-permute-done.13.refs_6_ = bf16[512,128]{1,0:T(8,128)(2,1)S(1)} collective-permute-done((bf16[512,128]{1,0:T(8,128)(2,1)S(1)}, bf16[512,128]{1,0:T(8,128)(2,1)S(1)}, u32[]{:S(2)}, u32[]{:S(2)}) %collective-permute-start.13) | collective-permute-done | bytes 131104 | tf_op jit(solution)/shard_map/ppermute | solution.py:304
  83.0 0.0 copy-done.9
  83.0 0.6 copy-done.23
  83.6 2.7 %shard_map.80 = bf16[4096,128]{1,0:T(8,128)(2,1)} custom-call(s32[2]{0:T(128)} %pad_add_fusion.where, bf16[512,128]{1,0:T(8,128)(2,1)} %copy-done.6, bf16[512,128]{1,0:T(8,128)(2,1)} %copy-done.9, bf16[512,128]{1,0:T(8,128)(2,1)} %copy-done.14, bf16[512,128]{1,0:T(8,128)(2,1)} %copy-done.16, bf16[512,128]{1,0:T(8,128)(2,1)} %copy-done.18, ...), custom_call_target="tpu_custom_call" | custom-call | bytes 2097160 | tf_op jit(solution)/shard_map/pallas_call | solution.py:276
  86.4 0.0 collective-permute-done.21.refs_1_
  86.4 0.0 collective-permute-done.22.refs_2_
  86.4 0.0 collective-permute-done.23.refs_3_
  86.4 0.7 copy-done
  87.1 0.1 copy-done.1
  87.2 0.1 copy-done.2
  87.3 2.1 %shard_map.82 = f32[512,256]{1,0:T(8,128)} custom-call(bf16[512,256]{1,0:T(8,128)(2,1)} %get-tuple-element.62.refs_0_, bf16[512,256]{1,0:T(8,128)(2,1)} %copy-done, bf16[512,256]{1,0:T(8,128)(2,1)} %copy-done.1, bf16[512,256]{1,0:T(8,128)(2,1)} %copy-done.2), custom_call_target="tpu_custom_call" | custom-call | bytes 1572864 | tf_op jit(solution)/shard_map/pallas_call | solution.py:276
  (43 shorter events, 0.1 us)
Async XLA Ops:
  4.4 12.0 %collective-permute-start = (bf16[512,128]{1,0:T(8,128)(2,1)}, bf16[512,128]{1,0:T(8,128)(2,1)S(1)}, u32[]{:S(2)}, u32[]{:S(2)}) collective-permute-start(bf16[512,128]{1,0:T(8,128)(2,1)} %get-tuple-element.34), channel_id=1, source_target_pairs={{0,4},{1,5},{2,6},{3,7},{4,0},{5,1},{6,2},{7,3},{8,12},{9,13},{10,... | collective-permute-start | bytes 393224 | tf_op jit(solution)/shard_map/ppermute | solution.py:304
  6.8 9.6 %collective-permute-start.1 = (bf16[512,128]{1,0:T(8,128)(2,1)}, bf16[512,128]{1,0:T(8,128)(2,1)S(1)}, u32[]{:S(2)}, u32[]{:S(2)}) collective-permute-start(bf16[512,128]{1,0:T(8,128)(2,1)} %get-tuple-element.35), channel_id=1, source_target_pairs={{0,1},{1,0},{2,3},{3,2},{4,5},{5,4},{6,7},{7,6},{8,9},{9,8},{10,11... | collective-permute-start | bytes 393224 | tf_op jit(solution)/shard_map/ppermute | solution.py:304
  8.0 19.4 %collective-permute-start.2 = (bf16[512,128]{1,0:T(8,128)(2,1)}, bf16[512,128]{1,0:T(8,128)(2,1)S(1)}, u32[]{:S(2)}, u32[]{:S(2)}) collective-permute-start(bf16[512,128]{1,0:T(8,128)(2,1)} %get-tuple-element.36), channel_id=1, source_target_pairs={{0,5},{1,4},{2,7},{3,6},{4,1},{5,0},{6,3},{7,2},{8,13},{9,12},{10,... | collective-permute-start | bytes 393224 | tf_op jit(solution)/shard_map/ppermute | solution.py:304
  8.1 19.4 %collective-permute-start.3 = (bf16[512,128]{1,0:T(8,128)(2,1)}, bf16[512,128]{1,0:T(8,128)(2,1)S(1)}, u32[]{:S(2)}, u32[]{:S(2)}) collective-permute-start(bf16[512,128]{1,0:T(8,128)(2,1)} %get-tuple-element.37), channel_id=1, source_target_pairs={{0,2},{1,3},{2,0},{3,1},{4,6},{5,7},{6,4},{7,5},{8,10},{9,11},{10,... | collective-permute-start | bytes 393224 | tf_op jit(solution)/shard_map/ppermute | solution.py:304
  8.2 20.6 %collective-permute-start.4 = (bf16[512,128]{1,0:T(8,128)(2,1)}, bf16[512,128]{1,0:T(8,128)(2,1)S(1)}, u32[]{:S(2)}, u32[]{:S(2)}) collective-permute-start(bf16[512,128]{1,0:T(8,128)(2,1)} %get-tuple-element.38), channel_id=1, source_target_pairs={{0,6},{1,7},{2,4},{3,5},{4,2},{5,3},{6,0},{7,1},{8,14},{9,15},{10,... | collective-permute-start | bytes 393224 | tf_op jit(solution)/shard_map/ppermute | solution.py:304
  16.4 11.0 %copy-start.8 = (bf16[512,128]{1,0:T(8,128)(2,1)}, bf16[512,128]{1,0:T(8,128)(2,1)S(1)}, u32[]{:S(2)}) copy-start(bf16[512,128]{1,0:T(8,128)(2,1)S(1)} %collective-permute-done.refs_0_) | copy-start | bytes 393220
  16.4 14.6 %collective-permute-start.5 = (bf16[512,128]{1,0:T(8,128)(2,1)}, bf16[512,128]{1,0:T(8,128)(2,1)S(1)}, u32[]{:S(2)}, u32[]{:S(2)}) collective-permute-start(bf16[512,128]{1,0:T(8,128)(2,1)} %get-tuple-element.39), channel_id=1, source_target_pairs={{0,3},{1,2},{2,1},{3,0},{4,7},{5,6},{6,5},{7,4},{8,11},{9,10},{10,... | collective-permute-start | bytes 393224 | tf_op jit(solution)/shard_map/ppermute | solution.py:304
  16.5 11.0 %copy-start.10 = (bf16[512,128]{1,0:T(8,128)(2,1)}, bf16[512,128]{1,0:T(8,128)(2,1)S(1)}, u32[]{:S(2)}) copy-start(bf16[512,128]{1,0:T(8,128)(2,1)S(1)} %collective-permute-done.1.refs_1_) | copy-start | bytes 393220
  16.5 15.6 %collective-permute-start.6 = (bf16[512,128]{1,0:T(8,128)(2,1)}, bf16[512,128]{1,0:T(8,128)(2,1)S(1)}, u32[]{:S(2)}, u32[]{:S(2)}) collective-permute-start(bf16[512,128]{1,0:T(8,128)(2,1)} %get-tuple-element.40), channel_id=1, source_target_pairs={{0,7},{1,6},{2,5},{3,4},{4,3},{5,2},{6,1},{7,0},{8,15},{9,14},{10,... | collective-permute-start | bytes 393224 | tf_op jit(solution)/shard_map/ppermute | solution.py:304
  27.4 7.0 %copy-start.12 = (bf16[512,128]{1,0:T(8,128)(2,1)}, bf16[512,128]{1,0:T(8,128)(2,1)S(1)}, u32[]{:S(2)}) copy-start(bf16[512,128]{1,0:T(8,128)(2,1)S(1)} %collective-permute-done.2.refs_2_) | copy-start | bytes 393220
  27.4 15.3 %collective-permute-start.14 = (bf16[512,128]{1,0:T(8,128)(2,1)}, bf16[512,128]{1,0:T(8,128)(2,1)S(1)}, u32[]{:S(2)}, u32[]{:S(2)}) collective-permute-start(bf16[512,128]{1,0:T(8,128)(2,1)} %get-tuple-element.53), channel_id=1, source_target_pairs={{0,4},{1,5},{2,6},{3,7},{4,0},{5,1},{6,2},{7,3},{8,12},{9,13},{10,... | collective-permute-start | bytes 393224 | tf_op jit(solution)/shard_map/ppermute | solution.py:304
  27.5 6.9 %copy-start.13 = (bf16[512,128]{1,0:T(8,128)(2,1)}, bf16[512,128]{1,0:T(8,128)(2,1)S(1)}, u32[]{:S(2)}) copy-start(bf16[512,128]{1,0:T(8,128)(2,1)S(1)} %collective-permute-done.3.refs_3_) | copy-start | bytes 393220
  27.5 15.3 %collective-permute-start.15 = (bf16[512,128]{1,0:T(8,128)(2,1)}, bf16[512,128]{1,0:T(8,128)(2,1)S(1)}, u32[]{:S(2)}, u32[]{:S(2)}) collective-permute-start(bf16[512,128]{1,0:T(8,128)(2,1)} %get-tuple-element.54), channel_id=1, source_target_pairs={{0,1},{1,0},{2,3},{3,2},{4,5},{5,4},{6,7},{7,6},{8,9},{9,8},{10,11... | collective-permute-start | bytes 393224 | tf_op jit(solution)/shard_map/ppermute | solution.py:304
  28.8 5.6 %copy-start.15 = (bf16[512,128]{1,0:T(8,128)(2,1)}, bf16[512,128]{1,0:T(8,128)(2,1)S(1)}, u32[]{:S(2)}) copy-start(bf16[512,128]{1,0:T(8,128)(2,1)S(1)} %collective-permute-done.4.refs_4_) | copy-start | bytes 393220
  28.8 15.3 %collective-permute-start.16 = (bf16[512,128]{1,0:T(8,128)(2,1)}, bf16[512,128]{1,0:T(8,128)(2,1)S(1)}, u32[]{:S(2)}, u32[]{:S(2)}) collective-permute-start(bf16[512,128]{1,0:T(8,128)(2,1)} %get-tuple-element.55), channel_id=1, source_target_pairs={{0,5},{1,4},{2,7},{3,6},{4,1},{5,0},{6,3},{7,2},{8,13},{9,12},{10,... | collective-permute-start | bytes 393224 | tf_op jit(solution)/shard_map/ppermute | solution.py:304
  31.1 3.4 %copy-start.17 = (bf16[512,128]{1,0:T(8,128)(2,1)}, bf16[512,128]{1,0:T(8,128)(2,1)S(1)}, u32[]{:S(2)}) copy-start(bf16[512,128]{1,0:T(8,128)(2,1)S(1)} %collective-permute-done.5.refs_5_) | copy-start | bytes 393220
  31.1 14.3 %collective-permute-start.17 = (bf16[512,128]{1,0:T(8,128)(2,1)}, bf16[512,128]{1,0:T(8,128)(2,1)S(1)}, u32[]{:S(2)}, u32[]{:S(2)}) collective-permute-start(bf16[512,128]{1,0:T(8,128)(2,1)} %get-tuple-element.56), channel_id=1, source_target_pairs={{0,2},{1,3},{2,0},{3,1},{4,6},{5,7},{6,4},{7,5},{8,10},{9,11},{10,... | collective-permute-start | bytes 393224 | tf_op jit(solution)/shard_map/ppermute | solution.py:304
  32.1 2.4 %copy-start.19 = (bf16[512,128]{1,0:T(8,128)(2,1)}, bf16[512,128]{1,0:T(8,128)(2,1)S(1)}, u32[]{:S(2)}) copy-start(bf16[512,128]{1,0:T(8,128)(2,1)S(1)} %collective-permute-done.6.refs_6_) | copy-start | bytes 393220
  32.1 15.7 %collective-permute-start.18 = (bf16[512,128]{1,0:T(8,128)(2,1)}, bf16[512,128]{1,0:T(8,128)(2,1)S(1)}, u32[]{:S(2)}, u32[]{:S(2)}) collective-permute-start(bf16[512,128]{1,0:T(8,128)(2,1)} %get-tuple-element.57), channel_id=1, source_target_pairs={{0,6},{1,7},{2,4},{3,5},{4,2},{5,3},{6,0},{7,1},{8,14},{9,15},{10,... | collective-permute-start | bytes 393224 | tf_op jit(solution)/shard_map/ppermute | solution.py:304
  42.7 10.9 %copy-start.3 = (bf16[512,128]{1,0:T(8,128)(2,1)}, bf16[512,128]{1,0:T(8,128)(2,1)S(1)}, u32[]{:S(2)}) copy-start(bf16[512,128]{1,0:T(8,128)(2,1)S(1)} %collective-permute-done.14.refs_0_) | copy-start | bytes 393220
  42.7 5.8 %collective-permute-start.19 = (bf16[512,128]{1,0:T(8,128)(2,1)}, bf16[512,128]{1,0:T(8,128)(2,1)S(1)}, u32[]{:S(2)}, u32[]{:S(2)}) collective-permute-start(bf16[512,128]{1,0:T(8,128)(2,1)} %get-tuple-element.58), channel_id=1, source_target_pairs={{0,3},{1,2},{2,1},{3,0},{4,7},{5,6},{6,5},{7,4},{8,11},{9,10},{10,... | collective-permute-start | bytes 393224 | tf_op jit(solution)/shard_map/ppermute | solution.py:304
  42.8 10.8 %copy-start.4 = (bf16[512,128]{1,0:T(8,128)(2,1)}, bf16[512,128]{1,0:T(8,128)(2,1)S(1)}, u32[]{:S(2)}) copy-start(bf16[512,128]{1,0:T(8,128)(2,1)S(1)} %collective-permute-done.15.refs_1_) | copy-start | bytes 393220
  42.8 9.7 %collective-permute-start.20 = (bf16[512,128]{1,0:T(8,128)(2,1)}, bf16[512,128]{1,0:T(8,128)(2,1)S(1)}, u32[]{:S(2)}, u32[]{:S(2)}) collective-permute-start(bf16[512,128]{1,0:T(8,128)(2,1)} %get-tuple-element.59), channel_id=1, source_target_pairs={{0,7},{1,6},{2,5},{3,4},{4,3},{5,2},{6,1},{7,0},{8,15},{9,14},{10,... | collective-permute-start | bytes 393224 | tf_op jit(solution)/shard_map/ppermute | solution.py:304
  44.1 9.4 %copy-start.5 = (bf16[512,128]{1,0:T(8,128)(2,1)}, bf16[512,128]{1,0:T(8,128)(2,1)S(1)}, u32[]{:S(2)}) copy-start(bf16[512,128]{1,0:T(8,128)(2,1)S(1)} %collective-permute-done.16.refs_2_) | copy-start | bytes 393220
  44.1 16.8 %collective-permute-start.7 = (bf16[512,128]{1,0:T(8,128)(2,1)}, bf16[512,128]{1,0:T(8,128)(2,1)S(1)}, u32[]{:S(2)}, u32[]{:S(2)}) collective-permute-start(bf16[512,128]{1,0:T(8,128)(2,1)} %get-tuple-element.45), channel_id=1, source_target_pairs={{0,1},{1,0},{2,3},{3,2},{4,5},{5,4},{6,7},{7,6},{8,9},{9,8},{10,11... | collective-permute-start | bytes 393224 | tf_op jit(solution)/shard_map/ppermute | solution.py:304
  45.4 8.2 %copy-start.7 = (bf16[512,128]{1,0:T(8,128)(2,1)}, bf16[512,128]{1,0:T(8,128)(2,1)S(1)}, u32[]{:S(2)}) copy-start(bf16[512,128]{1,0:T(8,128)(2,1)S(1)} %collective-permute-done.17.refs_3_) | copy-start | bytes 393220
  45.4 21.0 %collective-permute-start.8 = (bf16[512,128]{1,0:T(8,128)(2,1)}, bf16[512,128]{1,0:T(8,128)(2,1)S(1)}, u32[]{:S(2)}, u32[]{:S(2)}) collective-permute-start(bf16[512,128]{1,0:T(8,128)(2,1)} %get-tuple-element.46), channel_id=1, source_target_pairs={{0,2},{1,3},{2,0},{3,1},{4,6},{5,7},{6,4},{7,5},{8,10},{9,11},{10,... | collective-permute-start | bytes 393224 | tf_op jit(solution)/shard_map/ppermute | solution.py:304
  47.8 5.8 %copy-start.11 = (bf16[512,128]{1,0:T(8,128)(2,1)}, bf16[512,128]{1,0:T(8,128)(2,1)S(1)}, u32[]{:S(2)}) copy-start(bf16[512,128]{1,0:T(8,128)(2,1)S(1)} %collective-permute-done.18.refs_4_) | copy-start | bytes 393220
  47.8 19.8 %collective-permute-start.9 = (bf16[512,128]{1,0:T(8,128)(2,1)}, bf16[512,128]{1,0:T(8,128)(2,1)S(1)}, u32[]{:S(2)}, u32[]{:S(2)}) collective-permute-start(bf16[512,128]{1,0:T(8,128)(2,1)} %get-tuple-element.47), channel_id=1, source_target_pairs={{0,3},{1,2},{2,1},{3,0},{4,7},{5,6},{6,5},{7,4},{8,11},{9,10},{10,... | collective-permute-start | bytes 393224 | tf_op jit(solution)/shard_map/ppermute | solution.py:304
  48.5 5.1 %copy-start.20 = (bf16[512,128]{1,0:T(8,128)(2,1)}, bf16[512,128]{1,0:T(8,128)(2,1)S(1)}, u32[]{:S(2)}) copy-start(bf16[512,128]{1,0:T(8,128)(2,1)S(1)} %collective-permute-done.19.refs_5_) | copy-start | bytes 393220
  48.5 19.6 %collective-permute-start.10 = (bf16[512,128]{1,0:T(8,128)(2,1)}, bf16[512,128]{1,0:T(8,128)(2,1)S(1)}, u32[]{:S(2)}, u32[]{:S(2)}) collective-permute-start(bf16[512,128]{1,0:T(8,128)(2,1)} %get-tuple-element.48), channel_id=1, source_target_pairs={{0,4},{1,5},{2,6},{3,7},{4,0},{5,1},{6,2},{7,3},{8,12},{9,13},{10,... | collective-permute-start | bytes 393224 | tf_op jit(solution)/shard_map/ppermute | solution.py:304
  52.5 1.1 %copy-start.21 = (bf16[512,128]{1,0:T(8,128)(2,1)}, bf16[512,128]{1,0:T(8,128)(2,1)S(1)}, u32[]{:S(2)}) copy-start(bf16[512,128]{1,0:T(8,128)(2,1)S(1)} %collective-permute-done.20.refs_6_) | copy-start | bytes 393220
  52.5 15.9 %collective-permute-start.11 = (bf16[512,128]{1,0:T(8,128)(2,1)}, bf16[512,128]{1,0:T(8,128)(2,1)S(1)}, u32[]{:S(2)}, u32[]{:S(2)}) collective-permute-start(bf16[512,128]{1,0:T(8,128)(2,1)} %get-tuple-element.49), channel_id=1, source_target_pairs={{0,5},{1,4},{2,7},{3,6},{4,1},{5,0},{6,3},{7,2},{8,13},{9,12},{10,... | collective-permute-start | bytes 393224 | tf_op jit(solution)/shard_map/ppermute | solution.py:304
  53.6 14.5 %copy-start.25 = (bf16[512,128]{1,0:T(8,128)(2,1)S(1)}, bf16[512,128]{1,0:T(8,128)(2,1)}, u32[]{:S(2)}) copy-start(bf16[512,128]{1,0:T(8,128)(2,1)} %get-tuple-element.50) | copy-start | bytes 393220
  53.6 14.8 %copy-start.24 = (bf16[512,128]{1,0:T(8,128)(2,1)S(1)}, bf16[512,128]{1,0:T(8,128)(2,1)}, u32[]{:S(2)}) copy-start(bf16[512,128]{1,0:T(8,128)(2,1)} %get-tuple-element.51) | copy-start | bytes 393220
  60.9 22.0 %copy-start.6 = (bf16[512,128]{1,0:T(8,128)(2,1)}, bf16[512,128]{1,0:T(8,128)(2,1)S(1)}, u32[]{:S(2)}) copy-start(bf16[512,128]{1,0:T(8,128)(2,1)S(1)} %collective-permute-done.7.refs_0_) | copy-start | bytes 393220
  61.0 25.4 %collective-permute-start.21 = (bf16[512,256]{1,0:T(8,128)(2,1)}, bf16[512,256]{1,0:T(8,128)(2,1)S(1)}, u32[]{:S(2)}, u32[]{:S(2)}) collective-permute-start(bf16[512,256]{1,0:T(8,128)(2,1)} %get-tuple-element.63), channel_id=1, source_target_pairs={{0,8},{8,0},{16,24},{24,16},{1,9},{9,1},{17,25},{25,17},{2,10},{10... | collective-permute-start | bytes 786440 | tf_op jit(solution)/shard_map/ppermute | solution.py:304
  66.4 16.6 %copy-start.9 = (bf16[512,128]{1,0:T(8,128)(2,1)}, bf16[512,128]{1,0:T(8,128)(2,1)S(1)}, u32[]{:S(2)}) copy-start(bf16[512,128]{1,0:T(8,128)(2,1)S(1)} %collective-permute-done.8.refs_1_) | copy-start | bytes 393220
  66.4 20.0 %collective-permute-start.22 = (bf16[512,256]{1,0:T(8,128)(2,1)}, bf16[512,256]{1,0:T(8,128)(2,1)S(1)}, u32[]{:S(2)}, u32[]{:S(2)}) collective-permute-start(bf16[512,256]{1,0:T(8,128)(2,1)} %get-tuple-element.64), channel_id=1, source_target_pairs={{0,16},{8,24},{16,0},{24,8},{1,17},{9,25},{17,1},{25,9},{2,18},{10... | collective-permute-start | bytes 786440 | tf_op jit(solution)/shard_map/ppermute | solution.py:304
  67.6 15.4 %copy-start.14 = (bf16[512,128]{1,0:T(8,128)(2,1)}, bf16[512,128]{1,0:T(8,128)(2,1)S(1)}, u32[]{:S(2)}) copy-start(bf16[512,128]{1,0:T(8,128)(2,1)S(1)} %collective-permute-done.9.refs_2_) | copy-start | bytes 393220
  67.6 18.8 %collective-permute-start.23 = (bf16[512,256]{1,0:T(8,128)(2,1)}, bf16[512,256]{1,0:T(8,128)(2,1)S(1)}, u32[]{:S(2)}, u32[]{:S(2)}) collective-permute-start(bf16[512,256]{1,0:T(8,128)(2,1)} %get-tuple-element.65), channel_id=1, source_target_pairs={{0,24},{8,16},{16,8},{24,0},{1,25},{9,17},{17,9},{25,1},{2,26},{10... | collective-permute-start | bytes 786440 | tf_op jit(solution)/shard_map/ppermute | solution.py:304
  68.1 14.9 %copy-start.16 = (bf16[512,128]{1,0:T(8,128)(2,1)}, bf16[512,128]{1,0:T(8,128)(2,1)S(1)}, u32[]{:S(2)}) copy-start(bf16[512,128]{1,0:T(8,128)(2,1)S(1)} %collective-permute-done.10.refs_3_) | copy-start | bytes 393220
  68.1 10.7 %collective-permute-start.12 = (bf16[512,128]{1,0:T(8,128)(2,1)S(1)}, bf16[512,128]{1,0:T(8,128)(2,1)S(1)}, u32[]{:S(2)}, u32[]{:S(2)}) collective-permute-start(bf16[512,128]{1,0:T(8,128)(2,1)S(1)} %copy-done.25), channel_id=1, source_target_pairs={{0,6},{1,7},{2,4},{3,5},{4,2},{5,3},{6,0},{7,1},{8,14},{9,15},{10,... | collective-permute-start | bytes 393224 | tf_op jit(solution)/shard_map/ppermute | solution.py:304
  68.4 14.6 %copy-start.18 = (bf16[512,128]{1,0:T(8,128)(2,1)}, bf16[512,128]{1,0:T(8,128)(2,1)S(1)}, u32[]{:S(2)}) copy-start(bf16[512,128]{1,0:T(8,128)(2,1)S(1)} %collective-permute-done.11.refs_4_) | copy-start | bytes 393220
  68.4 14.5 %collective-permute-start.13 = (bf16[512,128]{1,0:T(8,128)(2,1)S(1)}, bf16[512,128]{1,0:T(8,128)(2,1)S(1)}, u32[]{:S(2)}, u32[]{:S(2)}) collective-permute-start(bf16[512,128]{1,0:T(8,128)(2,1)S(1)} %copy-done.24), channel_id=1, source_target_pairs={{0,7},{1,6},{2,5},{3,4},{4,3},{5,2},{6,1},{7,0},{8,15},{9,14},{10,... | collective-permute-start | bytes 393224 | tf_op jit(solution)/shard_map/ppermute | solution.py:304
  78.8 4.1 %copy-start.22 = (bf16[512,128]{1,0:T(8,128)(2,1)}, bf16[512,128]{1,0:T(8,128)(2,1)S(1)}, u32[]{:S(2)}) copy-start(bf16[512,128]{1,0:T(8,128)(2,1)S(1)} %collective-permute-done.12.refs_5_) | copy-start | bytes 393220
  82.9 0.7 copy-start.23
  86.4 0.7 copy-start
  86.4 0.8 copy-start.1
  86.4 0.9 copy-start.2

commit v7 on v6

--- a/solution.py
+++ b/solution.py
@@ -16,7 +16,7 @@
 C1 = math.cos(math.pi / 8)
 C2 = math.cos(math.pi / 4)
 C3 = math.cos(3 * math.pi / 8)
-LIMIT = 56 * 1024 * 1024
+LIMIT = 32 * 1024 * 1024
 
 
 def transform_tables(width):
@@ -167,20 +167,6 @@
         copy.wait()
 
 
-def place_kernel(order, where, *refs):
-    pieces, (whole, slots, sems, out_sems) = refs[: len(order)], refs[len(order) :]
-    loads = [pltpu.make_async_copy(piece, slots.at[i], sems.at[i]) for i, piece in enumerate(pieces)]
-    for copy in loads:
-        copy.start()
-    stores = []
-    for i, k in enumerate(order):
-        loads[i].wait()
-        stores.append(pltpu.make_async_copy(slots.at[i], piece_at(whole, where, k, slots.shape[1]), out_sems.at[i]))
-        stores[-1].start()
-    for copy in stores:
-        copy.wait()
-
-
 def taps_kernel(order, where, whole, taps, forward, *refs):
     outs, (taps_spec, slots, mid, sems, out_sems) = refs[: len(order)], refs[len(order) :]
     rows, width = (taps.shape[0], taps.shape[1] // BLOCKS)
@@ -217,10 +203,9 @@
     return store
 
 
-def back_kernel(order, back_order, late, where, *refs):
+def back_kernel(order, late, where, *refs):
     blocks, refs = refs[: len(order)], refs[len(order) + late :]
-    taps_spec, forward, backward, *outs, grad_spec, held, mid, wide = refs
-    outs = outs[late:]
+    taps_spec, forward, backward, *_, out, grad_spec, held, mid, wide = refs
     rows, width = held.shape[0], held.shape[1] // BLOCKS
     ordered(order, where, blocks, held)
     split_rows(block_of(held, width), mid, rows, width)
@@ -232,16 +217,14 @@
         product = jnp.concatenate([hr * gr + hi * gi, hr * gi - hi * gr], axis=1)
         invert_group(product.astype(jnp.bfloat16), backward, r, width, wide)
     merge_rows(wide, block_into(held, width), rows, width)
-    span = outs[0].shape[1]
-    for k, out in zip(back_order, outs):
-        start = pl.multiple_of(lax.bitwise_xor(where[0], k) * span, span)
-        out[...] = held[:, pl.ds(start, span)]
-
-
-def cross_kernel(order, near, where, *refs):
-    blocks, refs = refs[: len(order)], refs[len(order) + near :]
+    span = out.shape[2]
+    for p in range(out.shape[0]):
+        out[p] = held[:, p * span : (p + 1) * span]
+
+
+def cross_kernel(order, where, *refs):
+    blocks, refs = refs[: len(order)], refs[len(order) :]
     grad_spec, forward, backward, *outs, held, mid, wide = refs
-    outs = outs[near:]
     rows, width = held.shape[0], held.shape[1] // BLOCKS
     ordered(order, where, blocks, held)
     split_rows(block_of(held, width), mid, rows, width)
@@ -253,16 +236,9 @@
         invert_group(product.astype(jnp.bfloat16), backward, r, width, wide)
     merge_rows(wide, block_into(held, width), rows, width)
     part = held.shape[1] // len(outs)
-    for k, out in enumerate(outs):
+    for k, out in zip(far_first(len(outs)), outs):
         start = pl.multiple_of(lax.bitwise_xor(where[1], k) * part, part)
         out[...] = held[:, pl.ds(start, part)]
-
-
-def sum_kernel(scale, *refs):
-    total = refs[0][...].astype(jnp.float32)
-    for ref in refs[1:-1]:
-        total = total + ref[...].astype(jnp.float32)
-    refs[-1][...] = total * scale
 
 
 def call(kernel, operands, outs, scratch=(), flops=0, streams=(), out_streams=(), aliases=None):
@@ -289,10 +265,6 @@
     return [*range(size // 2, size), *range(1, size // 2), 0]
 
 
-def near_first(size):
-    return [*range(1, size), 0]
-
-
 def mixed(size):
     far = far_first(size)
     return [k for pair in zip(far[: size // 2], far[size // 2 :]) for k in pair]
@@ -310,8 +282,8 @@
     channels, span = saved_input.shape[1:]
     rows, length = long_filter.shape
     width = length // BLOCKS
-    order, back_order, near = mixed(count), near_first(count), 0
-    late, at = 2, count - 1 - 2
+    order, late = mixed(count), 2
+    at = count - 1 - late
     every = range(count + 8)
     where = jnp.stack([lax.axis_index("ctx"), lax.axis_index("dp")]).astype(jnp.int32)
     forward, backward = (jnp.asarray(t) for t in transform_tables(width))
@@ -343,46 +315,30 @@
         streams=(1,),
         out_streams=range(count),
     )
-    *back, grad_spec = call(
-        functools.partial(back_kernel, order, back_order, late),
+    *input_pieces[at : at + late], back, grad_spec = call(
+        functools.partial(back_kernel, order, late),
         [where, *grad_blocks, *input_pieces[at : at + late], taps_spec, forward, backward],
-        [piece] * (late + count) + [spec],
+        [piece] * late + [jax.ShapeDtypeStruct((count, rows, span), half), spec],
         [held, mid, wide],
         flops=2 * work,
         streams=range(1 + count, 1 + count + late),
         out_streams=range(late),
         aliases={1 + count + i: i for i in range(late)},
     )
-    input_pieces[at : at + late], back = back[:late], back[late:]
     input_blocks = exchange(input_pieces, order, "ctx", count)
+    grad_input = lax.all_to_all(back, "ctx", split_axis=0, concat_axis=0, tiled=True)
     share = jax.ShapeDtypeStruct((rows, length // shares), half)
     cross = call(
-        functools.partial(cross_kernel, order, near),
-        [where, *input_blocks, *back[count - near :], grad_spec, forward, backward],
-        [piece] * near + [share] * shares,
+        functools.partial(cross_kernel, order),
+        [where, *input_blocks, grad_spec, forward, backward],
+        [share] * shares,
         [held, mid, wide],
         flops=2 * work,
-        streams=range(1 + count, 1 + count + near),
-        out_streams=range(near),
-        aliases={1 + count + i: i for i in range(near)},
-    )
-    back_blocks = exchange([*back[: count - near], *cross[:near]], back_order, "ctx", count)
-    cross_blocks = exchange(cross[near:], range(shares), "dp", shares)
+    )
+    cross_blocks = exchange(cross, far_first(shares), "dp", shares)
     scale = 1.0 / math.sqrt(shares * length)
-    (grad_filter,) = call(
-        functools.partial(sum_kernel, scale),
-        cross_blocks,
-        [jax.ShapeDtypeStruct((rows, length // shares), full)],
-    )
-    (grad_input,) = call(
-        functools.partial(place_kernel, back_order),
-        [where, *back_blocks],
-        [jax.ShapeDtypeStruct((channels, span), half)],
-        [slots, sems((count,)), sems((count,))],
-        streams=every,
-        out_streams=every,
-    )
-    return (grad_input[None], grad_filter)
+    grad_filter = sum(x.astype(full) for x in cross_blocks) * scale
+    return (grad_input.reshape(1, channels, span), grad_filter)
 
 
 def solution(mesh):

time: 89.6 us -> 116 us (1.29)
  the two profiles are of different devices: /device:TPU:9 before, /device:TPU:0 now
where the time goes in v7:
time: 116 us; the launch traced here: 114 us
  waiting for transfers between devices  50 us (43%)
  starting transfers between devices  32.5 us (28%)
  Pallas kernels  19.3 us (17%)
  local copies, waits for them, and re-layouts  10.7 us (9%)
    ppermute x17, waiting for transfers between devices, exchange(): lax.ppermute(piece, axis, [(i, i ^ k) for i in range(size)])  50 us
    ppermute x17, starting transfers between devices, exchange(): lax.ppermute(piece, axis, [(i, i ^ k) for i in range(size)])  28.2 us
    pallas_call x4, Pallas kernels, call(): pl.pallas_call(kernel, out_shape=list(outs), in_specs=specs, out_specs=[s...  19.3 us
    unnamed x17, local copies, waits for them, and re-layouts  10.7 us
    all_to_all x1, starting transfers between devices, on_device(): lax.all_to_all(back, 'ctx', split_axis=0, concat_axis=0, tiled=True)  4.24 us
  transfers between devices with their start and end apart: 18, of which 6 were waited for; matrix products, arithmetic and copies ran while one was open for 1% of the time, Pallas kernels for 8%

profile of v7, /device:TPU:0, one launch (start us, length us, event | category | flops | bytes accessed | tf_op | source)
XLA Modules:
  0.0 114.2 jit_solution(6197144752301809945)
XLA Ops:
  0.6 0.0 copy-start
  0.6 0.1 pad_add_fusion.where
  0.7 0.0 copy-start.6
  0.7 1.3 %copy-done.6 = bf16[1,4096,128]{2,1,0:T(8,128)(2,1)S(1)} copy-done((bf16[1,4096,128]{2,1,0:T(8,128)(2,1)S(1)}, bf16[1,4096,128]{2,1,0:T(8,128)(2,1)}, u32[]{:S(2)}) %copy-start.6) | copy-done | bytes 1048600
  2.0 0.0 copy-start.7
  2.0 1.2 %copy-done.7 = bf16[1,4096,128]{2,1,0:T(8,128)(2,1)S(1)} copy-done((bf16[1,4096,128]{2,1,0:T(8,128)(2,1)S(1)}, bf16[1,4096,128]{2,1,0:T(8,128)(2,1)}, u32[]{:S(2)}) %copy-start.7) | copy-done | bytes 1048600
  3.3 5.1 %shard_map.77 = (bf16[512,128]{1,0:T(8,128)(2,1)S(1)}, bf16[512,128]{1,0:T(8,128)(2,1)S(1)}, bf16[512,128]{1,0:T(8,128)(2,1)S(1)}, bf16[512,128]{1,0:T(8,128)(2,...) custom-call(s32[2]{0:T(128)S(1)} %pad_add_fusion.where, ...), custom_call_target="tpu_custom_call" | custom-call | bytes 3145736 | tf_op jit(solution)/shard_map/pallas_call | solution.py:252
  8.4 4.1 %collective-permute-start = (bf16[512,128]{1,0:T(8,128)(2,1)S(1)}, bf16[512,128]{1,0:T(8,128)(2,1)S(1)}, u32[]{:S(2)}, u32[]{:S(2)}) collective-permute-start(bf16[512,128]{1,0:T(8,128)(2,1)S(1)} %get-tuple-element.27), channel_id=1, source_target_pairs={{0,4},{1,5},{2,6},{3,7},{4,0},{5,1},{6,2},{7,3},{8,12},{9,13},{10,... | collective-permute-start | bytes 393224 | tf_op jit(solution)/shard_map/ppermute | solution.py:276
  12.5 1.5 %collective-permute-start.1 = (bf16[512,128]{1,0:T(8,128)(2,1)S(1)}, bf16[512,128]{1,0:T(8,128)(2,1)S(1)}, u32[]{:S(2)}, u32[]{:S(2)}) collective-permute-start(bf16[512,128]{1,0:T(8,128)(2,1)S(1)} %get-tuple-element.28), channel_id=1, source_target_pairs={{0,1},{1,0},{2,3},{3,2},{4,5},{5,4},{6,7},{7,6},{8,9},{9,8},{10,11... | collective-permute-start | bytes 393224 | tf_op jit(solution)/shard_map/ppermute | solution.py:276
  14.0 0.0 collective-permute-start.2
  14.0 1.8 %collective-permute-start.3 = (bf16[512,128]{1,0:T(8,128)(2,1)S(1)}, bf16[512,128]{1,0:T(8,128)(2,1)S(1)}, u32[]{:S(2)}, u32[]{:S(2)}) collective-permute-start(bf16[512,128]{1,0:T(8,128)(2,1)S(1)} %get-tuple-element.30), channel_id=1, source_target_pairs={{0,2},{1,3},{2,0},{3,1},{4,6},{5,7},{6,4},{7,5},{8,10},{9,11},{10,... | collective-permute-start | bytes 393224 | tf_op jit(solution)/shard_map/ppermute | solution.py:276
  15.9 2.5 %collective-permute-start.4 = (bf16[512,128]{1,0:T(8,128)(2,1)S(1)}, bf16[512,128]{1,0:T(8,128)(2,1)S(1)}, u32[]{:S(2)}, u32[]{:S(2)}) collective-permute-start(bf16[512,128]{1,0:T(8,128)(2,1)S(1)} %get-tuple-element.31), channel_id=1, source_target_pairs={{0,6},{1,7},{2,4},{3,5},{4,2},{5,3},{6,0},{7,1},{8,14},{9,15},{10,... | collective-permute-start | bytes 393224 | tf_op jit(solution)/shard_map/ppermute | solution.py:276
  18.3 4.8 %collective-permute-done.refs_0_ = bf16[512,128]{1,0:T(8,128)(2,1)S(1)} collective-permute-done((bf16[512,128]{1,0:T(8,128)(2,1)S(1)}, bf16[512,128]{1,0:T(8,128)(2,1)S(1)}, u32[]{:S(2)}, u32[]{:S(2)}) %collective-permute-start) | collective-permute-done | bytes 131104 | tf_op jit(solution)/shard_map/ppermute | solution.py:276
  23.2 1.1 %collective-permute-start.5 = (bf16[512,128]{1,0:T(8,128)(2,1)S(1)}, bf16[512,128]{1,0:T(8,128)(2,1)S(1)}, u32[]{:S(2)}, u32[]{:S(2)}) collective-permute-start(bf16[512,128]{1,0:T(8,128)(2,1)S(1)} %get-tuple-element.32), channel_id=1, source_target_pairs={{0,3},{1,2},{2,1},{3,0},{4,7},{5,6},{6,5},{7,4},{8,11},{9,10},{10,... | collective-permute-start | bytes 393224 | tf_op jit(solution)/shard_map/ppermute | solution.py:276
  24.3 0.0 collective-permute-done.1.refs_1_
  24.3 4.2 %collective-permute-start.6 = (bf16[512,128]{1,0:T(8,128)(2,1)S(1)}, bf16[512,128]{1,0:T(8,128)(2,1)S(1)}, u32[]{:S(2)}, u32[]{:S(2)}) collective-permute-start(bf16[512,128]{1,0:T(8,128)(2,1)S(1)} %get-tuple-element.33), channel_id=1, source_target_pairs={{0,7},{1,6},{2,5},{3,4},{4,3},{5,2},{6,1},{7,0},{8,15},{9,14},{10,... | collective-permute-start | bytes 393224 | tf_op jit(solution)/shard_map/ppermute | solution.py:276
  28.5 0.0 copy-done
  28.5 0.0 copy-start.4
  28.5 1.6 %copy-done.4 = f32[512,1024]{1,0:T(8,128)S(1)} copy-done((f32[512,1024]{1,0:T(8,128)S(1)}, f32[512,1024]{1,0:T(8,128)}, u32[]{:S(2)}) %copy-start.4) | copy-done | bytes 2097176
  30.1 0.0 copy-start.5
  30.1 1.2 %copy-done.5 = bf16[1,4096,128]{2,1,0:T(8,128)(2,1)S(1)} copy-done((bf16[1,4096,128]{2,1,0:T(8,128)(2,1)S(1)}, bf16[1,4096,128]{2,1,0:T(8,128)(2,1)}, u32[]{:S(2)}) %copy-start.5) | copy-done | bytes 1048600
  31.4 0.0 copy-start.1
  31.4 4.9 %shard_map.78 = (bf16[512,128]{1,0:T(8,128)(2,1)S(1)}, bf16[512,128]{1,0:T(8,128)(2,1)S(1)}, bf16[512,128]{1,0:T(8,128)(2,1)S(1)}, bf16[512,128]{1,0:T(8,128)(2,...) custom-call(s32[2]{0:T(128)S(1)} %pad_add_fusion.where, ...), custom_call_target="tpu_custom_call" | custom-call | flops 603979776 | bytes 7733256 | tf_op jit(solution)/shard_map/pallas_call | solution.py:252
  36.3 0.0 collective-permute-done.2.refs_2_
  36.3 0.0 collective-permute-done.3.refs_3_
  36.3 0.0 collective-permute-done.4.refs_4_
  36.3 0.0 collective-permute-done.5.refs_5_
  36.3 0.0 collective-permute-done.6.refs_6_
  36.3 0.0 copy-done.1
  36.3 5.1 %shard_map.79 = (bf16[512,128]{1,0:T(8,128)(2,1)S(1)}, bf16[512,128]{1,0:T(8,128)(2,1)S(1)}, bf16[8,512,128]{2,1,0:T(8,128)(2,1)}, bf16[9,512,256]{2,1,0:T(8,128)(2,1)S(1)}) custom-call(s32[2]{0:T(128)S(1)} %pad_add_fusion.where, bf16[512,128]{1,0:T(8,128)(2,1)S(1)} %collective-permute-done.refs_0_, ...), custom_call_target="tpu_custom_call", output_to_operand_aliasing={{0}: (9, {}), {1}: (10, {})} | custom-call | flops 1207959552 | bytes 9699336 | tf_op jit(solution)/shard_map/pallas_call | solution.py:252
  41.5 0.0 copy-start.2
  41.5 1.4 %copy-done.2 = bf16[9,512,256]{2,1,0:T(8,128)(2,1)} copy-done((bf16[9,512,256]{2,1,0:T(8,128)(2,1)}, bf16[9,512,256]{2,1,0:T(8,128)(2,1)S(1)}, u32[]{:S(2)}) %copy-start.2) | copy-done | bytes 2359320
  42.9 4.2 %all-to-all-start = ((bf16[8,512,128]{2,1,0:T(8,128)(2,1)}), bf16[8,512,128]{2,1,0:T(8,128)(2,1)}, u32[]{:S(2)}, u32[]{:S(2)}) async-start(bf16[8,512,128]{2,1,0:T(8,128)(2,1)} %get-tuple-element.38), calls=%async_computation | async-start | bytes 2097152 | tf_op jit(solution)/shard_map/all_to_all | solution.py:329
  47.1 3.0 %collective-permute-start.7 = (bf16[512,128]{1,0:T(8,128)(2,1)S(1)}, bf16[512,128]{1,0:T(8,128)(2,1)S(1)}, u32[]{:S(2)}, u32[]{:S(2)}) collective-permute-start(bf16[512,128]{1,0:T(8,128)(2,1)S(1)} %get-tuple-element.39), channel_id=1, source_target_pairs={{0,4},{1,5},{2,6},{3,7},{4,0},{5,1},{6,2},{7,3},{8,12},{9,13},{10,... | collective-permute-start | bytes 393224 | tf_op jit(solution)/shard_map/ppermute | solution.py:276
  50.1 1.4 %collective-permute-start.8 = (bf16[512,128]{1,0:T(8,128)(2,1)S(1)}, bf16[512,128]{1,0:T(8,128)(2,1)S(1)}, u32[]{:S(2)}, u32[]{:S(2)}) collective-permute-start(bf16[512,128]{1,0:T(8,128)(2,1)S(1)} %get-tuple-element.40), channel_id=1, source_target_pairs={{0,1},{1,0},{2,3},{3,2},{4,5},{5,4},{6,7},{7,6},{8,9},{9,8},{10,11... | collective-permute-start | bytes 393224 | tf_op jit(solution)/shard_map/ppermute | solution.py:276
  51.5 0.2 collective-permute-start.9
  51.6 1.9 %collective-permute-start.10 = (bf16[512,128]{1,0:T(8,128)(2,1)S(1)}, bf16[512,128]{1,0:T(8,128)(2,1)S(1)}, u32[]{:S(2)}, u32[]{:S(2)}) collective-permute-start(bf16[512,128]{1,0:T(8,128)(2,1)S(1)} %get-tuple-element.42), channel_id=1, source_target_pairs={{0,2},{1,3},{2,0},{3,1},{4,6},{5,7},{6,4},{7,5},{8,10},{9,11},{10,... | collective-permute-start | bytes 393224 | tf_op jit(solution)/shard_map/ppermute | solution.py:276
  53.5 2.4 %collective-permute-start.11 = (bf16[512,128]{1,0:T(8,128)(2,1)S(1)}, bf16[512,128]{1,0:T(8,128)(2,1)S(1)}, u32[]{:S(2)}, u32[]{:S(2)}) collective-permute-start(bf16[512,128]{1,0:T(8,128)(2,1)S(1)} %get-tuple-element.43), channel_id=1, source_target_pairs={{0,6},{1,7},{2,4},{3,5},{4,2},{5,3},{6,0},{7,1},{8,14},{9,15},{10,... | collective-permute-start | bytes 393224 | tf_op jit(solution)/shard_map/ppermute | solution.py:276
  56.0 29.8 %collective-permute-done.7.refs_0_ = bf16[512,128]{1,0:T(8,128)(2,1)S(1)} collective-permute-done((bf16[512,128]{1,0:T(8,128)(2,1)S(1)}, bf16[512,128]{1,0:T(8,128)(2,1)S(1)}, u32[]{:S(2)}, u32[]{:S(2)}) %collective-permute-start.7) | collective-permute-done | bytes 131104 | tf_op jit(solution)/shard_map/ppermute | solution.py:276
  85.8 0.0 collective-permute-start.12
  85.8 0.0 collective-permute-done.8.refs_1_
  85.8 1.9 %collective-permute-start.13 = (bf16[512,128]{1,0:T(8,128)(2,1)S(1)}, bf16[512,128]{1,0:T(8,128)(2,1)S(1)}, u32[]{:S(2)}, u32[]{:S(2)}) collective-permute-start(bf16[512,128]{1,0:T(8,128)(2,1)S(1)} %get-tuple-element.45), channel_id=1, source_target_pairs={{0,7},{1,6},{2,5},{3,4},{4,3},{5,2},{6,1},{7,0},{8,15},{9,14},{10,... | collective-permute-start | bytes 393224 | tf_op jit(solution)/shard_map/ppermute | solution.py:276
  87.7 1.3 %collective-permute-done.9.refs_2_ = bf16[512,128]{1,0:T(8,128)(2,1)S(1)} collective-permute-done((bf16[512,128]{1,0:T(8,128)(2,1)S(1)}, bf16[512,128]{1,0:T(8,128)(2,1)S(1)}, u32[]{:S(2)}, u32[]{:S(2)}) %collective-permute-start.9) | collective-permute-done | bytes 131104 | tf_op jit(solution)/shard_map/ppermute | solution.py:276
  89.0 0.0 collective-permute-done.10.refs_3_
  89.0 0.0 collective-permute-done.11.refs_4_
  89.0 5.2 %collective-permute-done.12.refs_5_ = bf16[512,128]{1,0:T(8,128)(2,1)S(1)} collective-permute-done((bf16[512,128]{1,0:T(8,128)(2,1)S(1)}, bf16[512,128]{1,0:T(8,128)(2,1)S(1)}, u32[]{:S(2)}, u32[]{:S(2)}) %collective-permute-start.12) | collective-permute-done | bytes 131104 | tf_op jit(solution)/shard_map/ppermute | solution.py:276
  94.2 0.0 collective-permute-done.13.refs_6_
  94.2 0.0 copy-start.3
  94.2 1.7 %copy-done.3 = bf16[9,512,256]{2,1,0:T(8,128)(2,1)S(1)} copy-done((bf16[9,512,256]{2,1,0:T(8,128)(2,1)S(1)}, bf16[9,512,256]{2,1,0:T(8,128)(2,1)}, u32[]{:S(2)}) %copy-start.3) | copy-done | bytes 2359320
  95.9 4.1 %shard_map.80 = (bf16[512,256]{1,0:T(8,128)(2,1)S(1)}, bf16[512,256]{1,0:T(8,128)(2,1)S(1)}, bf16[512,256]{1,0:T(8,128)(2,1)S(1)}, bf16[512,256]{1,0:T(8,128)(2,1)S(1)}) custom-call(s32[2]{0:T(128)S(1)} %pad_add_fusion.where, bf16[512,128]{1,0:T(8,128)(2,1)S(1)} %collective-permute-done.7.refs_0_, bf16[512,128]{1,0:T(8,128)(2,1)S(1)} %collective-permute-done.8.refs_1_, ...), custom_call_target="tpu_custom_call" | custom-call | flops 1207959552 | bytes 6815752 | tf_op jit(solution)/shard_map/pallas_call | solution.py:252
  100.0 1.6 %collective-permute-start.14 = (bf16[512,256]{1,0:T(8,128)(2,1)S(1)}, bf16[512,256]{1,0:T(8,128)(2,1)S(1)}, u32[]{:S(2)}, u32[]{:S(2)}) collective-permute-start(bf16[512,256]{1,0:T(8,128)(2,1)S(1)} %get-tuple-element.48), channel_id=1, source_target_pairs={{0,16},{8,24},{16,0},{24,8},{1,17},{9,25},{17,1},{25,9},{2,18},{10... | collective-permute-start | bytes 786440 | tf_op jit(solution)/shard_map/ppermute | solution.py:276
  101.5 0.0 collective-permute-start.15
  101.5 0.6 collective-permute-start.16
  102.2 6.1 %collective-permute-done.14 = bf16[512,256]{1,0:T(8,128)(2,1)S(1)} collective-permute-done((bf16[512,256]{1,0:T(8,128)(2,1)S(1)}, bf16[512,256]{1,0:T(8,128)(2,1)S(1)}, u32[]{:S(2)}, u32[]{:S(2)}) %collective-permute-start.14) | collective-permute-done | bytes 262176 | tf_op jit(solution)/shard_map/ppermute | solution.py:276
  108.3 2.7 %collective-permute-done.15 = bf16[512,256]{1,0:T(8,128)(2,1)S(1)} collective-permute-done((bf16[512,256]{1,0:T(8,128)(2,1)S(1)}, bf16[512,256]{1,0:T(8,128)(2,1)S(1)}, u32[]{:S(2)}, u32[]{:S(2)}) %collective-permute-start.15) | collective-permute-done | bytes 262176 | tf_op jit(solution)/shard_map/ppermute | solution.py:276
  111.0 0.0 collective-permute-done.16
  111.0 0.9 add_multiply_fusion
  111.9 0.0 all-to-all-done
  111.9 2.3 %copy.13 = bf16[1,4096,128]{2,1,0:T(8,128)(2,1)} copy(bf16[1,4096,128]{2,1,0:T(8,128)(2,1)} %bitcast.5) | data formatting | bytes 2097152
Async XLA Ops:
  0.6 27.9 %copy-start = (bf16[9,256,256]{2,1,0:T(8,128)(2,1)S(1)}, bf16[9,256,256]{2,1,0:T(8,128)(2,1)}, u32[]{:S(2)}) copy-start(bf16[9,256,256]{2,1,0:T(8,128)(2,1)} %constant.14.clone.forward.refs_11_.refs_9_) | copy-start | bytes 3538948
  0.7 1.3 %copy-start.6 = (bf16[1,4096,128]{2,1,0:T(8,128)(2,1)S(1)}, bf16[1,4096,128]{2,1,0:T(8,128)(2,1)}, u32[]{:S(2)}) copy-start(bf16[1,4096,128]{2,1,0:T(8,128)(2,1)} %param.7) | copy-start | bytes 3145732
  2.0 1.2 %copy-start.7 = (bf16[1,4096,128]{2,1,0:T(8,128)(2,1)S(1)}, bf16[1,4096,128]{2,1,0:T(8,128)(2,1)}, u32[]{:S(2)}) copy-start(bf16[1,4096,128]{2,1,0:T(8,128)(2,1)} %param.8) | copy-start | bytes 3145732
  8.4 14.8 %collective-permute-start = (bf16[512,128]{1,0:T(8,128)(2,1)S(1)}, bf16[512,128]{1,0:T(8,128)(2,1)S(1)}, u32[]{:S(2)}, u32[]{:S(2)}) collective-permute-start(bf16[512,128]{1,0:T(8,128)(2,1)S(1)} %get-tuple-element.27), channel_id=1, source_target_pairs={{0,4},{1,5},{2,6},{3,7},{4,0},{5,1},{6,2},{7,3},{8,12},{9,13},{10,... | collective-permute-start | bytes 393224 | tf_op jit(solution)/shard_map/ppermute | solution.py:276
  12.5 11.8 %collective-permute-start.1 = (bf16[512,128]{1,0:T(8,128)(2,1)S(1)}, bf16[512,128]{1,0:T(8,128)(2,1)S(1)}, u32[]{:S(2)}, u32[]{:S(2)}) collective-permute-start(bf16[512,128]{1,0:T(8,128)(2,1)S(1)} %get-tuple-element.28), channel_id=1, source_target_pairs={{0,1},{1,0},{2,3},{3,2},{4,5},{5,4},{6,7},{7,6},{8,9},{9,8},{10,11... | collective-permute-start | bytes 393224 | tf_op jit(solution)/shard_map/ppermute | solution.py:276
  14.0 22.3 %collective-permute-start.2 = (bf16[512,128]{1,0:T(8,128)(2,1)S(1)}, bf16[512,128]{1,0:T(8,128)(2,1)S(1)}, u32[]{:S(2)}, u32[]{:S(2)}) collective-permute-start(bf16[512,128]{1,0:T(8,128)(2,1)S(1)} %get-tuple-element.29), channel_id=1, source_target_pairs={{0,5},{1,4},{2,7},{3,6},{4,1},{5,0},{6,3},{7,2},{8,13},{9,12},{10,... | collective-permute-start | bytes 393224 | tf_op jit(solution)/shard_map/ppermute | solution.py:276
  14.0 22.3 %collective-permute-start.3 = (bf16[512,128]{1,0:T(8,128)(2,1)S(1)}, bf16[512,128]{1,0:T(8,128)(2,1)S(1)}, u32[]{:S(2)}, u32[]{:S(2)}) collective-permute-start(bf16[512,128]{1,0:T(8,128)(2,1)S(1)} %get-tuple-element.30), channel_id=1, source_target_pairs={{0,2},{1,3},{2,0},{3,1},{4,6},{5,7},{6,4},{7,5},{8,10},{9,11},{10,... | collective-permute-start | bytes 393224 | tf_op jit(solution)/shard_map/ppermute | solution.py:276
  15.9 20.4 %collective-permute-start.4 = (bf16[512,128]{1,0:T(8,128)(2,1)S(1)}, bf16[512,128]{1,0:T(8,128)(2,1)S(1)}, u32[]{:S(2)}, u32[]{:S(2)}) collective-permute-start(bf16[512,128]{1,0:T(8,128)(2,1)S(1)} %get-tuple-element.31), channel_id=1, source_target_pairs={{0,6},{1,7},{2,4},{3,5},{4,2},{5,3},{6,0},{7,1},{8,14},{9,15},{10,... | collective-permute-start | bytes 393224 | tf_op jit(solution)/shard_map/ppermute | solution.py:276
  23.2 13.1 %collective-permute-start.5 = (bf16[512,128]{1,0:T(8,128)(2,1)S(1)}, bf16[512,128]{1,0:T(8,128)(2,1)S(1)}, u32[]{:S(2)}, u32[]{:S(2)}) collective-permute-start(bf16[512,128]{1,0:T(8,128)(2,1)S(1)} %get-tuple-element.32), channel_id=1, source_target_pairs={{0,3},{1,2},{2,1},{3,0},{4,7},{5,6},{6,5},{7,4},{8,11},{9,10},{10,... | collective-permute-start | bytes 393224 | tf_op jit(solution)/shard_map/ppermute | solution.py:276
  24.3 12.0 %collective-permute-start.6 = (bf16[512,128]{1,0:T(8,128)(2,1)S(1)}, bf16[512,128]{1,0:T(8,128)(2,1)S(1)}, u32[]{:S(2)}, u32[]{:S(2)}) collective-permute-start(bf16[512,128]{1,0:T(8,128)(2,1)S(1)} %get-tuple-element.33), channel_id=1, source_target_pairs={{0,7},{1,6},{2,5},{3,4},{4,3},{5,2},{6,1},{7,0},{8,15},{9,14},{10,... | collective-permute-start | bytes 393224 | tf_op jit(solution)/shard_map/ppermute | solution.py:276
  28.5 1.6 %copy-start.4 = (f32[512,1024]{1,0:T(8,128)S(1)}, f32[512,1024]{1,0:T(8,128)}, u32[]{:S(2)}) copy-start(f32[512,1024]{1,0:T(8,128)} %taps.1) | copy-start | bytes 6291460
  30.1 1.2 %copy-start.5 = (bf16[1,4096,128]{2,1,0:T(8,128)(2,1)S(1)}, bf16[1,4096,128]{2,1,0:T(8,128)(2,1)}, u32[]{:S(2)}) copy-start(bf16[1,4096,128]{2,1,0:T(8,128)(2,1)} %param.6) | copy-start | bytes 3145732
  31.4 5.0 %copy-start.1 = (bf16[9,256,256]{2,1,0:T(8,128)(2,1)S(1)}, bf16[9,256,256]{2,1,0:T(8,128)(2,1)}, u32[]{:S(2)}) copy-start(bf16[9,256,256]{2,1,0:T(8,128)(2,1)} %constant.15.clone.refs_12_.refs_10_) | copy-start | bytes 3538948
  41.5 1.4 %copy-start.2 = (bf16[9,512,256]{2,1,0:T(8,128)(2,1)}, bf16[9,512,256]{2,1,0:T(8,128)(2,1)S(1)}, u32[]{:S(2)}) copy-start(bf16[9,512,256]{2,1,0:T(8,128)(2,1)S(1)} %get-tuple-element.47.refs_8_) | copy-start | bytes 7077892
  42.9 69.0 %all-to-all-start = ((bf16[8,512,128]{2,1,0:T(8,128)(2,1)}), bf16[8,512,128]{2,1,0:T(8,128)(2,1)}, u32[]{:S(2)}, u32[]{:S(2)}) async-start(bf16[8,512,128]{2,1,0:T(8,128)(2,1)} %get-tuple-element.38), calls=%async_computation | async-start | bytes 2097152 | tf_op jit(solution)/shard_map/all_to_all | solution.py:329
  47.1 38.6 %collective-permute-start.7 = (bf16[512,128]{1,0:T(8,128)(2,1)S(1)}, bf16[512,128]{1,0:T(8,128)(2,1)S(1)}, u32[]{:S(2)}, u32[]{:S(2)}) collective-permute-start(bf16[512,128]{1,0:T(8,128)(2,1)S(1)} %get-tuple-element.39), channel_id=1, source_target_pairs={{0,4},{1,5},{2,6},{3,7},{4,0},{5,1},{6,2},{7,3},{8,12},{9,13},{10,... | collective-permute-start | bytes 393224 | tf_op jit(solution)/shard_map/ppermute | solution.py:276
  50.1 35.7 %collective-permute-start.8 = (bf16[512,128]{1,0:T(8,128)(2,1)S(1)}, bf16[512,128]{1,0:T(8,128)(2,1)S(1)}, u32[]{:S(2)}, u32[]{:S(2)}) collective-permute-start(bf16[512,128]{1,0:T(8,128)(2,1)S(1)} %get-tuple-element.40), channel_id=1, source_target_pairs={{0,1},{1,0},{2,3},{3,2},{4,5},{5,4},{6,7},{7,6},{8,9},{9,8},{10,11... | collective-permute-start | bytes 393224 | tf_op jit(solution)/shard_map/ppermute | solution.py:276
  51.5 37.5 %collective-permute-start.9 = (bf16[512,128]{1,0:T(8,128)(2,1)S(1)}, bf16[512,128]{1,0:T(8,128)(2,1)S(1)}, u32[]{:S(2)}, u32[]{:S(2)}) collective-permute-start(bf16[512,128]{1,0:T(8,128)(2,1)S(1)} %get-tuple-element.41), channel_id=1, source_target_pairs={{0,5},{1,4},{2,7},{3,6},{4,1},{5,0},{6,3},{7,2},{8,13},{9,12},{10,... | collective-permute-start | bytes 393224 | tf_op jit(solution)/shard_map/ppermute | solution.py:276
  51.6 37.3 %collective-permute-start.10 = (bf16[512,128]{1,0:T(8,128)(2,1)S(1)}, bf16[512,128]{1,0:T(8,128)(2,1)S(1)}, u32[]{:S(2)}, u32[]{:S(2)}) collective-permute-start(bf16[512,128]{1,0:T(8,128)(2,1)S(1)} %get-tuple-element.42), channel_id=1, source_target_pairs={{0,2},{1,3},{2,0},{3,1},{4,6},{5,7},{6,4},{7,5},{8,10},{9,11},{10,... | collective-permute-start | bytes 393224 | tf_op jit(solution)/shard_map/ppermute | solution.py:276
  53.5 35.5 %collective-permute-start.11 = (bf16[512,128]{1,0:T(8,128)(2,1)S(1)}, bf16[512,128]{1,0:T(8,128)(2,1)S(1)}, u32[]{:S(2)}, u32[]{:S(2)}) collective-permute-start(bf16[512,128]{1,0:T(8,128)(2,1)S(1)} %get-tuple-element.43), channel_id=1, source_target_pairs={{0,6},{1,7},{2,4},{3,5},{4,2},{5,3},{6,0},{7,1},{8,14},{9,15},{10,... | collective-permute-start | bytes 393224 | tf_op jit(solution)/shard_map/ppermute | solution.py:276
  85.8 8.4 %collective-permute-start.12 = (bf16[512,128]{1,0:T(8,128)(2,1)S(1)}, bf16[512,128]{1,0:T(8,128)(2,1)S(1)}, u32[]{:S(2)}, u32[]{:S(2)}) collective-permute-start(bf16[512,128]{1,0:T(8,128)(2,1)S(1)} %get-tuple-element.44), channel_id=1, source_target_pairs={{0,3},{1,2},{2,1},{3,0},{4,7},{5,6},{6,5},{7,4},{8,11},{9,10},{10,... | collective-permute-start | bytes 393224 | tf_op jit(solution)/shard_map/ppermute | solution.py:276
  85.8 8.4 %collective-permute-start.13 = (bf16[512,128]{1,0:T(8,128)(2,1)S(1)}, bf16[512,128]{1,0:T(8,128)(2,1)S(1)}, u32[]{:S(2)}, u32[]{:S(2)}) collective-permute-start(bf16[512,128]{1,0:T(8,128)(2,1)S(1)} %get-tuple-element.45), channel_id=1, source_target_pairs={{0,7},{1,6},{2,5},{3,4},{4,3},{5,2},{6,1},{7,0},{8,15},{9,14},{10,... | collective-permute-start | bytes 393224 | tf_op jit(solution)/shard_map/ppermute | solution.py:276
  94.2 1.7 %copy-start.3 = (bf16[9,512,256]{2,1,0:T(8,128)(2,1)S(1)}, bf16[9,512,256]{2,1,0:T(8,128)(2,1)}, u32[]{:S(2)}) copy-start(bf16[9,512,256]{2,1,0:T(8,128)(2,1)} %copy-done.2) | copy-start | bytes 7077892
  100.0 8.3 %collective-permute-start.14 = (bf16[512,256]{1,0:T(8,128)(2,1)S(1)}, bf16[512,256]{1,0:T(8,128)(2,1)S(1)}, u32[]{:S(2)}, u32[]{:S(2)}) collective-permute-start(bf16[512,256]{1,0:T(8,128)(2,1)S(1)} %get-tuple-element.48), channel_id=1, source_target_pairs={{0,16},{8,24},{16,0},{24,8},{1,17},{9,25},{17,1},{25,9},{2,18},{10... | collective-permute-start | bytes 786440 | tf_op jit(solution)/shard_map/ppermute | solution.py:276
  101.5 9.5 %collective-permute-start.15 = (bf16[512,256]{1,0:T(8,128)(2,1)S(1)}, bf16[512,256]{1,0:T(8,128)(2,1)S(1)}, u32[]{:S(2)}, u32[]{:S(2)}) collective-permute-start(bf16[512,256]{1,0:T(8,128)(2,1)S(1)} %get-tuple-element.49), channel_id=1, source_target_pairs={{0,24},{8,16},{16,8},{24,0},{1,25},{9,17},{17,9},{25,1},{2,26},{10... | collective-permute-start | bytes 786440 | tf_op jit(solution)/shard_map/ppermute | solution.py:276
  101.5 9.5 %collective-permute-start.16 = (bf16[512,256]{1,0:T(8,128)(2,1)S(1)}, bf16[512,256]{1,0:T(8,128)(2,1)S(1)}, u32[]{:S(2)}, u32[]{:S(2)}) collective-permute-start(bf16[512,256]{1,0:T(8,128)(2,1)S(1)} %get-tuple-element.50), channel_id=1, source_target_pairs={{0,8},{8,0},{16,24},{24,16},{1,9},{9,1},{17,25},{25,17},{2,10},{10... | collective-permute-start | bytes 786440 | tf_op jit(solution)/shard_map/ppermute | solution.py:276

commit v8 on v7

--- a/solution.py
+++ b/solution.py
@@ -144,10 +144,11 @@
     return ref.at[pl.ds(start, rows), :]
 
 
-def gate_kernel(order, where, gate, upper, *refs):
-    outs, (left, right, product, sems, out_sems) = refs[: len(order)], refs[len(order) :]
+def gate_kernel(order, where, gate, upper, whole, *refs):
+    outs, picks, refs = refs[: len(order)], refs[len(order) : 2 * len(order)], refs[2 * len(order) :]
+    left, right, sems, pick_sems = refs
     rows = outs[0].shape[0]
-    loads = []
+    loads, moves = [], []
     for i, k in enumerate(order):
         pair = (
             pltpu.make_async_copy(piece_at(gate, where, k, rows), left.at[i], sems.at[0, i]),
@@ -156,33 +157,28 @@
         for copy in pair:
             copy.start()
         loads.append(pair)
-    stores = []
+    for i, k in enumerate(order):
+        moves.append(pltpu.make_async_copy(piece_at(whole, where, k, rows), picks[i], pick_sems.at[i]))
+        moves[-1].start()
     for i, out in enumerate(outs):
         for copy in loads[i]:
             copy.wait()
-        product[i] = (left[i].astype(jnp.float32) * right[i].astype(jnp.float32)).astype(jnp.bfloat16)
-        stores.append(pltpu.make_async_copy(product.at[i], out, out_sems.at[i]))
-        stores[-1].start()
-    for copy in stores:
+        out[...] = (left[i].astype(jnp.float32) * right[i].astype(jnp.float32)).astype(jnp.bfloat16)
+    for copy in moves:
         copy.wait()
 
 
-def taps_kernel(order, where, whole, taps, forward, *refs):
-    outs, (taps_spec, slots, mid, sems, out_sems) = refs[: len(order)], refs[len(order) :]
+def place_kernel(order, where, *refs):
+    pieces, whole = refs[:-1], refs[-1]
+    for k, piece in zip(order, pieces):
+        whole[lax.bitwise_xor(where[0], k)] = piece[...]
+
+
+def taps_kernel(taps, forward, taps_spec, mid):
     rows, width = (taps.shape[0], taps.shape[1] // BLOCKS)
-    loads, stores = [], []
-    for i, k in enumerate(order):
-        loads.append(pltpu.make_async_copy(piece_at(whole, where, k, rows), slots.at[i], sems.at[i]))
-        loads[-1].start()
-    for i, out in enumerate(outs):
-        loads[i].wait()
-        stores.append(pltpu.make_async_copy(slots.at[i], out, out_sems.at[i]))
-        stores[-1].start()
     split_rows(lambda p, at: taps[at, p * width : (p + 1) * width], mid, rows, width)
     for r in range(GROUPS):
         taps_spec[r] = spectrum(mid, forward, r, width).astype(taps_spec.dtype)
-    for copy in stores:
-        copy.wait()
 
 
 def ordered(order, where, refs, held):
@@ -203,9 +199,10 @@
     return store
 
 
-def back_kernel(order, late, where, *refs):
+def back_kernel(order, back_order, late, where, *refs):
     blocks, refs = refs[: len(order)], refs[len(order) + late :]
-    taps_spec, forward, backward, *_, out, grad_spec, held, mid, wide = refs
+    taps_spec, forward, backward, *outs, grad_spec, held, mid, wide = refs
+    outs = outs[late:]
     rows, width = held.shape[0], held.shape[1] // BLOCKS
     ordered(order, where, blocks, held)
     split_rows(block_of(held, width), mid, rows, width)
@@ -217,9 +214,10 @@
         product = jnp.concatenate([hr * gr + hi * gi, hr * gi - hi * gr], axis=1)
         invert_group(product.astype(jnp.bfloat16), backward, r, width, wide)
     merge_rows(wide, block_into(held, width), rows, width)
-    span = out.shape[2]
-    for p in range(out.shape[0]):
-        out[p] = held[:, p * span : (p + 1) * span]
+    span = outs[0].shape[1]
+    for k, out in zip(back_order, outs):
+        start = pl.multiple_of(lax.bitwise_xor(where[0], k) * span, span)
+        out[...] = held[:, pl.ds(start, span)]
 
 
 def cross_kernel(order, where, *refs):
@@ -241,15 +239,17 @@
         out[...] = held[:, pl.ds(start, part)]
 
 
-def call(kernel, operands, outs, scratch=(), flops=0, streams=(), out_streams=(), aliases=None):
+def call(kernel, operands, outs, scratch=(), flops=0, streams=(), out_streams=(), aliases=None, hbm=()):
     def spec(stream):
         return pl.BlockSpec(memory_space=pl.ANY if stream else pltpu.VMEM)
 
     size = sum(math.prod(o.shape) * o.dtype.itemsize for o in list(operands) + list(outs))
     specs = [spec(i in streams) for i in range(len(operands))]
+    for i in hbm:
+        specs[i] = pl.BlockSpec(memory_space=pltpu.HBM)
     if operands[0].dtype == jnp.int32:
         specs[0] = pl.BlockSpec(memory_space=pltpu.SMEM)
-    return pl.pallas_call(
+    outputs = pl.pallas_call(
         kernel,
         out_shape=list(outs),
         in_specs=specs,
@@ -259,6 +259,7 @@
         compiler_params=pltpu.CompilerParams(vmem_limit_bytes=LIMIT),
         cost_estimate=pl.CostEstimate(flops=flops, bytes_accessed=size, transcendentals=0),
     )(*operands)
+    return list(outputs)
 
 
 def far_first(size):
@@ -268,6 +269,12 @@
 def mixed(size):
     far = far_first(size)
     return [k for pair in zip(far[: size // 2], far[size // 2 :]) for k in pair]
+
+
+def back_mixed(size):
+    half = size // 2
+    pairs = [k for pair in zip(range(1, half), range(half, size)) for k in pair]
+    return [*pairs[:-2], size - 2, size - 1, half - 1, 0]
 
 
 def exchange(pieces, order, axis, size):
@@ -282,7 +289,7 @@
     channels, span = saved_input.shape[1:]
     rows, length = long_filter.shape
     width = length // BLOCKS
-    order, late = mixed(count), 2
+    order, back_order, late = mixed(count), back_mixed(count), 2
     at = count - 1 - late
     every = range(count + 8)
     where = jnp.stack([lax.axis_index("ctx"), lax.axis_index("dp")]).astype(jnp.int32)
@@ -297,36 +304,30 @@
     sems = pltpu.SemaphoreType.DMA
     work = 2 * GROUPS * rows * 4 * width * width
 
-    grad_pieces = call(
+    pieces = call(
         functools.partial(gate_kernel, order),
-        [where, out_gate[0], grad_out[0]],
-        [piece] * count,
-        [slots, slots, slots, sems((2, count)), sems((count,))],
-        streams=every,
-        out_streams=every,
-    )
+        [where, *(pltpu.with_memory_space_constraint(x[0], pltpu.HBM) for x in (out_gate, grad_out, saved_input))],
+        [piece] * (2 * count),
+        [slots, slots, sems((2, count)), sems((count,))],
+        hbm=(1, 2, 3),
+    )
+    grad_pieces, input_pieces = pieces[:count], pieces[count:]
     grad_blocks = exchange(grad_pieces, order, "ctx", count)
-    *input_pieces, taps_spec = call(
-        functools.partial(taps_kernel, order),
-        [where, saved_input[0], long_filter, forward],
-        [piece] * count + [spec],
-        [slots, mid, sems((count,)), sems((count,))],
-        flops=work,
-        streams=(1,),
-        out_streams=range(count),
-    )
-    *input_pieces[at : at + late], back, grad_spec = call(
-        functools.partial(back_kernel, order, late),
-        [where, *grad_blocks, *input_pieces[at : at + late], taps_spec, forward, backward],
-        [piece] * late + [jax.ShapeDtypeStruct((count, rows, span), half), spec],
+    (taps_spec,) = call(taps_kernel, [long_filter, forward], [spec], [mid], flops=work)
+    passed = [*input_pieces[at : at + late]]
+    *back, grad_spec = call(
+        functools.partial(back_kernel, order, back_order, late),
+        [where, *grad_blocks, *passed, taps_spec, forward, backward],
+        [piece] * (late + count) + [spec],
         [held, mid, wide],
         flops=2 * work,
         streams=range(1 + count, 1 + count + late),
         out_streams=range(late),
         aliases={1 + count + i: i for i in range(late)},
     )
+    input_pieces[at : at + late], back = back[:late], back[late:]
     input_blocks = exchange(input_pieces, order, "ctx", count)
-    grad_input = lax.all_to_all(back, "ctx", split_axis=0, concat_axis=0, tiled=True)
+    back_blocks = exchange(back, back_order, "ctx", count)
     share = jax.ShapeDtypeStruct((rows, length // shares), half)
     cross = call(
         functools.partial(cross_kernel, order),
@@ -338,7 +339,12 @@
     cross_blocks = exchange(cross, far_first(shares), "dp", shares)
     scale = 1.0 / math.sqrt(shares * length)
     grad_filter = sum(x.astype(full) for x in cross_blocks) * scale
-    return (grad_input.reshape(1, channels, span), grad_filter)
+    (whole,) = call(
+        functools.partial(place_kernel, back_order),
+        [where, *back_blocks],
+        [jax.ShapeDtypeStruct((count, rows, span), half)],
+    )
+    return (whole.reshape(1, channels, span), grad_filter)
 
 
 def solution(mesh):

time: 116 us -> 81.9 us (0.71); the launches traced: 114 us -> 81.8 us
  waiting for transfers between devices: 50 us -> 21.2 us
  starting transfers between devices: 32.5 us -> 43.2 us
  local copies, waits for them, and re-layouts: 10.7 us -> 1.6 us
  Pallas kernels: 19.3 us -> 14.1 us
    ppermute x17 -> x24, waiting for transfers between devices: 50 us -> 21.2 us  [exchange(): lax.ppermute(piece, axis, [(i, i ^ k) for i in range(size)])]
    ppermute x17 -> x24, starting transfers between devices: 28.2 us -> 43.2 us  [exchange(): lax.ppermute(piece, axis, [(i, i ^ k) for i in range(size)])]
    unnamed x17 -> x6, local copies, waits for them, and re-layouts: 10.7 us -> 1.6 us
    pallas_call x4 -> x5, Pallas kernels: 19.3 us -> 14.1 us  [call(): pl.pallas_call(kernel, out_shape=list(outs), in_specs=specs, out_specs=[s...]
    all_to_all x1 -> x0, starting transfers between devices: 4.24 us -> none  [on_device(): lax.all_to_all(back, 'ctx', split_axis=0, concat_axis=0, tiled=True)]
  transfers between devices with their start and end apart: 18 -> 24, of which waited for: 6 -> 7; matrix products, arithmetic and copies ran while one was open for 1% -> 0% of each run, Pallas kernels for 8% -> 14%
where the time goes in v8:
time: 81.9 us; the launch traced here: 81.8 us
  starting transfers between devices  43.2 us (53%)
  waiting for transfers between devices  21.2 us (26%)
  Pallas kernels  14.1 us (17%)
  local copies, waits for them, and re-layouts  1.6 us (2%)
  other arithmetic  1.02 us (1%)
    ppermute x24, starting transfers between devices, exchange(): lax.ppermute(piece, axis, [(i, i ^ k) for i in range(size)])  43.2 us
    ppermute x24, waiting for transfers between devices, exchange(): lax.ppermute(piece, axis, [(i, i ^ k) for i in range(size)])  21.2 us
    pallas_call x5, Pallas kernels, call(): pl.pallas_call(kernel, out_shape=list(outs), in_specs=specs, out_specs=[s...  14.1 us
  transfers between devices with their start and end apart: 24, of which 7 were waited for; matrix products, arithmetic and copies ran while one was open for 0% of the time, Pallas kernels for 14%

profile of v8, /device:TPU:0, one launch (start us, length us, event | category | flops | bytes accessed | tf_op | source)
XLA Modules:
  0.0 81.8 jit_solution(1123907797244685158)
XLA Ops:
  0.6 0.0 copy-start
  0.6 0.1 pad_add_fusion.where
  0.7 2.7 %shard_map.77 = (bf16[512,128]{1,0:T(8,128)(2,1)S(1)}, bf16[512,128]{1,0:T(8,128)(2,1)S(1)}, bf16[512,128]{1,0:T(8,128)(2,1)S(1)}, bf16[512,128]{1,0:T(8,128)(2,...) custom-call(s32[2]{0:T(128)S(1)} %pad_add_fusion.where, ...), custom_call_target="tpu_custom_call" | custom-call | bytes 5242888 | tf_op jit(solution)/shard_map/pallas_call | solution.py:252
  3.4 4.1 %collective-permute-start = (bf16[512,128]{1,0:T(8,128)(2,1)S(1)}, bf16[512,128]{1,0:T(8,128)(2,1)S(1)}, u32[]{:S(2)}, u32[]{:S(2)}) collective-permute-start(bf16[512,128]{1,0:T(8,128)(2,1)S(1)} %get-tuple-element.33), channel_id=1, source_target_pairs={{0,4},{1,5},{2,6},{3,7},{4,0},{5,1},{6,2},{7,3},{8,12},{9,13},{10,... | collective-permute-start | bytes 393224 | tf_op jit(solution)/shard_map/ppermute | solution.py:283
  7.5 1.5 %collective-permute-start.1 = (bf16[512,128]{1,0:T(8,128)(2,1)S(1)}, bf16[512,128]{1,0:T(8,128)(2,1)S(1)}, u32[]{:S(2)}, u32[]{:S(2)}) collective-permute-start(bf16[512,128]{1,0:T(8,128)(2,1)S(1)} %get-tuple-element.34), channel_id=1, source_target_pairs={{0,1},{1,0},{2,3},{3,2},{4,5},{5,4},{6,7},{7,6},{8,9},{9,8},{10,11... | collective-permute-start | bytes 393224 | tf_op jit(solution)/shard_map/ppermute | solution.py:283
  9.0 0.0 collective-permute-start.2
  9.0 1.8 %collective-permute-start.3 = (bf16[512,128]{1,0:T(8,128)(2,1)S(1)}, bf16[512,128]{1,0:T(8,128)(2,1)S(1)}, u32[]{:S(2)}, u32[]{:S(2)}) collective-permute-start(bf16[512,128]{1,0:T(8,128)(2,1)S(1)} %get-tuple-element.36), channel_id=1, source_target_pairs={{0,2},{1,3},{2,0},{3,1},{4,6},{5,7},{6,4},{7,5},{8,10},{9,11},{10,... | collective-permute-start | bytes 393224 | tf_op jit(solution)/shard_map/ppermute | solution.py:283
  10.9 2.5 %collective-permute-start.4 = (bf16[512,128]{1,0:T(8,128)(2,1)S(1)}, bf16[512,128]{1,0:T(8,128)(2,1)S(1)}, u32[]{:S(2)}, u32[]{:S(2)}) collective-permute-start(bf16[512,128]{1,0:T(8,128)(2,1)S(1)} %get-tuple-element.37), channel_id=1, source_target_pairs={{0,6},{1,7},{2,4},{3,5},{4,2},{5,3},{6,0},{7,1},{8,14},{9,15},{10,... | collective-permute-start | bytes 393224 | tf_op jit(solution)/shard_map/ppermute | solution.py:283
  13.4 4.8 %collective-permute-done.refs_0_ = bf16[512,128]{1,0:T(8,128)(2,1)S(1)} collective-permute-done((bf16[512,128]{1,0:T(8,128)(2,1)S(1)}, bf16[512,128]{1,0:T(8,128)(2,1)S(1)}, u32[]{:S(2)}, u32[]{:S(2)}) %collective-permute-start) | collective-permute-done | bytes 131104 | tf_op jit(solution)/shard_map/ppermute | solution.py:283
  18.2 1.1 %collective-permute-start.5 = (bf16[512,128]{1,0:T(8,128)(2,1)S(1)}, bf16[512,128]{1,0:T(8,128)(2,1)S(1)}, u32[]{:S(2)}, u32[]{:S(2)}) collective-permute-start(bf16[512,128]{1,0:T(8,128)(2,1)S(1)} %get-tuple-element.38), channel_id=1, source_target_pairs={{0,3},{1,2},{2,1},{3,0},{4,7},{5,6},{6,5},{7,4},{8,11},{9,10},{10,... | collective-permute-start | bytes 393224 | tf_op jit(solution)/shard_map/ppermute | solution.py:283
  19.3 0.0 collective-permute-done.1.refs_1_
  19.3 4.2 %collective-permute-start.6 = (bf16[512,128]{1,0:T(8,128)(2,1)S(1)}, bf16[512,128]{1,0:T(8,128)(2,1)S(1)}, u32[]{:S(2)}, u32[]{:S(2)}) collective-permute-start(bf16[512,128]{1,0:T(8,128)(2,1)S(1)} %get-tuple-element.39), channel_id=1, source_target_pairs={{0,7},{1,6},{2,5},{3,4},{4,3},{5,2},{6,1},{7,0},{8,15},{9,14},{10,... | collective-permute-start | bytes 393224 | tf_op jit(solution)/shard_map/ppermute | solution.py:283
  23.6 0.8 collective-permute-done.2.refs_2_
  24.4 0.0 collective-permute-start.14
  24.4 0.0 collective-permute-done.3.refs_3_
  24.4 0.0 copy-start.1
  24.4 0.9 %collective-permute-start.15 = (bf16[512,128]{1,0:T(8,128)(2,1)S(1)}, bf16[512,128]{1,0:T(8,128)(2,1)S(1)}, u32[]{:S(2)}, u32[]{:S(2)}) collective-permute-start(bf16[512,128]{1,0:T(8,128)(2,1)S(1)} %get-tuple-element.52), channel_id=1, source_target_pairs={{0,1},{1,0},{2,3},{3,2},{4,5},{5,4},{6,7},{7,6},{8,9},{9,8},{10,11... | collective-permute-start | bytes 393224 | tf_op jit(solution)/shard_map/ppermute | solution.py:283
  25.3 0.0 copy-done
  25.3 0.0 copy-start.2
  25.3 1.6 %copy-done.2 = f32[512,1024]{1,0:T(8,128)S(1)} copy-done((f32[512,1024]{1,0:T(8,128)S(1)}, f32[512,1024]{1,0:T(8,128)}, u32[]{:S(2)}) %copy-start.2) | copy-done | bytes 2097176
  26.9 1.5 %shard_map.78.refs_10_ = bf16[9,512,256]{2,1,0:T(8,128)(2,1)S(1)} custom-call(f32[512,1024]{1,0:T(8,128)S(1)} %copy-done.2, bf16[9,256,256]{2,1,0:T(8,128)(2,1)S(1)} %copy-done), custom_call_target="tpu_custom_call" | custom-call | flops 603979776 | bytes 5636096 | tf_op jit(solution)/shard_map/pallas_call | solution.py:252
  28.3 0.0 collective-permute-done.4.refs_4_
  28.3 6.1 %collective-permute-start.16 = (bf16[512,128]{1,0:T(8,128)(2,1)S(1)}, bf16[512,128]{1,0:T(8,128)(2,1)S(1)}, u32[]{:S(2)}, u32[]{:S(2)}) collective-permute-start(bf16[512,128]{1,0:T(8,128)(2,1)S(1)} %get-tuple-element.53), channel_id=1, source_target_pairs={{0,5},{1,4},{2,7},{3,6},{4,1},{5,0},{6,3},{7,2},{8,13},{9,12},{10,... | collective-permute-start | bytes 393224 | tf_op jit(solution)/shard_map/ppermute | solution.py:283
  34.4 0.0 collective-permute-done.5.refs_5_
  34.4 0.0 collective-permute-start.17
  34.4 0.0 collective-permute-done.6.refs_6_
  34.4 1.4 %collective-permute-start.18 = (bf16[512,128]{1,0:T(8,128)(2,1)S(1)}, bf16[512,128]{1,0:T(8,128)(2,1)S(1)}, u32[]{:S(2)}, u32[]{:S(2)}) collective-permute-start(bf16[512,128]{1,0:T(8,128)(2,1)S(1)} %get-tuple-element.55), channel_id=1, source_target_pairs={{0,6},{1,7},{2,4},{3,5},{4,2},{5,3},{6,0},{7,1},{8,14},{9,15},{10,... | collective-permute-start | bytes 393224 | tf_op jit(solution)/shard_map/ppermute | solution.py:283
  35.8 0.0 copy-done.1
  35.8 4.2 %shard_map.79 = (bf16[512,128]{1,0:T(8,128)(2,1)S(1)}, bf16[512,128]{1,0:T(8,128)(2,1)S(1)}, bf16[512,128]{1,0:T(8,128)(2,1)S(1)}, bf16[512,128]{1,0:T(8,128)(2,...) custom-call(s32[2]{0:T(128)S(1)} %pad_add_fusion.where, ...), custom_call_target="tpu_custom_call", output_to_operand_aliasing={{0}: (9, {}), {1}: (10, {})} | custom-call | flops 1207959552 | bytes 9699336 | tf_op jit(solution)/shard_map/pallas_call | solution.py:252
  40.0 0.7 collective-permute-done.14.refs_0_
  40.8 1.2 %collective-permute-start.19 = (bf16[512,128]{1,0:T(8,128)(2,1)S(1)}, bf16[512,128]{1,0:T(8,128)(2,1)S(1)}, u32[]{:S(2)}, u32[]{:S(2)}) collective-permute-start(bf16[512,128]{1,0:T(8,128)(2,1)S(1)} %get-tuple-element.56), channel_id=1, source_target_pairs={{0,3},{1,2},{2,1},{3,0},{4,7},{5,6},{6,5},{7,4},{8,11},{9,10},{10,... | collective-permute-start | bytes 393224 | tf_op jit(solution)/shard_map/ppermute | solution.py:283
  42.0 0.0 collective-permute-done.15.refs_1_
  42.0 3.8 %collective-permute-start.20 = (bf16[512,128]{1,0:T(8,128)(2,1)S(1)}, bf16[512,128]{1,0:T(8,128)(2,1)S(1)}, u32[]{:S(2)}, u32[]{:S(2)}) collective-permute-start(bf16[512,128]{1,0:T(8,128)(2,1)S(1)} %get-tuple-element.57), channel_id=1, source_target_pairs={{0,7},{1,6},{2,5},{3,4},{4,3},{5,2},{6,1},{7,0},{8,15},{9,14},{10,... | collective-permute-start | bytes 393224 | tf_op jit(solution)/shard_map/ppermute | solution.py:283
  45.8 1.9 %collective-permute-done.16.refs_2_ = bf16[512,128]{1,0:T(8,128)(2,1)S(1)} collective-permute-done((bf16[512,128]{1,0:T(8,128)(2,1)S(1)}, bf16[512,128]{1,0:T(8,128)(2,1)S(1)}, u32[]{:S(2)}, u32[]{:S(2)}) %collective-permute-start.16) | collective-permute-done | bytes 131104 | tf_op jit(solution)/shard_map/ppermute | solution.py:283
  47.7 0.0 collective-permute-start.7
  47.7 0.0 collective-permute-done.17.refs_3_
  47.7 1.4 %collective-permute-start.8 = (bf16[512,128]{1,0:T(8,128)(2,1)S(1)}, bf16[512,128]{1,0:T(8,128)(2,1)S(1)}, u32[]{:S(2)}, u32[]{:S(2)}) collective-permute-start(bf16[512,128]{1,0:T(8,128)(2,1)S(1)} %get-tuple-element.44), channel_id=1, source_target_pairs={{0,4},{1,5},{2,6},{3,7},{4,0},{5,1},{6,2},{7,3},{8,12},{9,13},{10,... | collective-permute-start | bytes 393224 | tf_op jit(solution)/shard_map/ppermute | solution.py:283
  49.1 0.0 collective-permute-done.18.refs_4_
  49.1 5.0 %collective-permute-start.9 = (bf16[512,128]{1,0:T(8,128)(2,1)S(1)}, bf16[512,128]{1,0:T(8,128)(2,1)S(1)}, u32[]{:S(2)}, u32[]{:S(2)}) collective-permute-start(bf16[512,128]{1,0:T(8,128)(2,1)S(1)} %get-tuple-element.45), channel_id=1, source_target_pairs={{0,2},{1,3},{2,0},{3,1},{4,6},{5,7},{6,4},{7,5},{8,10},{9,11},{10,... | collective-permute-start | bytes 393224 | tf_op jit(solution)/shard_map/ppermute | solution.py:283
  54.1 0.0 collective-permute-done.19.refs_5_
  54.1 2.8 %collective-permute-start.10 = (bf16[512,128]{1,0:T(8,128)(2,1)S(1)}, bf16[512,128]{1,0:T(8,128)(2,1)S(1)}, u32[]{:S(2)}, u32[]{:S(2)}) collective-permute-start(bf16[512,128]{1,0:T(8,128)(2,1)S(1)} %get-tuple-element.46), channel_id=1, source_target_pairs={{0,5},{1,4},{2,7},{3,6},{4,1},{5,0},{6,3},{7,2},{8,13},{9,12},{10,... | collective-permute-start | bytes 393224 | tf_op jit(solution)/shard_map/ppermute | solution.py:283
  56.9 0.0 collective-permute-done.20.refs_6_
  56.9 0.6 collective-permute-start.11
  57.5 4.1 %shard_map.81 = (bf16[512,256]{1,0:T(8,128)(2,1)S(1)}, bf16[512,256]{1,0:T(8,128)(2,1)S(1)}, bf16[512,256]{1,0:T(8,128)(2,1)S(1)}, bf16[512,256]{1,0:T(8,128)(2,1)S(1)}) custom-call(s32[2]{0:T(128)S(1)} %pad_add_fusion.where, bf16[512,128]{1,0:T(8,128)(2,1)S(1)} %collective-permute-done.14.refs_0_, bf16[512,128]{1,0:T(8,128)(2,1)S(1)} %collective-permute-done.15.refs_1_, ...), custom_call_target="tpu_custom_call" | custom-call | flops 1207959552 | bytes 6815752 | tf_op jit(solution)/shard_map/pallas_call | solution.py:252
  61.6 0.0 collective-permute-done.7.refs_0_
  61.7 1.6 %collective-permute-start.21 = (bf16[512,256]{1,0:T(8,128)(2,1)S(1)}, bf16[512,256]{1,0:T(8,128)(2,1)S(1)}, u32[]{:S(2)}, u32[]{:S(2)}) collective-permute-start(bf16[512,256]{1,0:T(8,128)(2,1)S(1)} %get-tuple-element.60), channel_id=1, source_target_pairs={{0,16},{8,24},{16,0},{24,8},{1,17},{9,25},{17,1},{25,9},{2,18},{10... | collective-permute-start | bytes 786440 | tf_op jit(solution)/shard_map/ppermute | solution.py:283
  63.2 0.0 collective-permute-done.8.refs_1_
  63.2 0.0 collective-permute-start.22
  63.2 0.0 collective-permute-done.9.refs_2_
  63.2 0.6 collective-permute-start.23
  63.9 5.5 %collective-permute-done.10.refs_3_ = bf16[512,128]{1,0:T(8,128)(2,1)S(1)} collective-permute-done((bf16[512,128]{1,0:T(8,128)(2,1)S(1)}, bf16[512,128]{1,0:T(8,128)(2,1)S(1)}, u32[]{:S(2)}, u32[]{:S(2)}) %collective-permute-start.10) | collective-permute-done | bytes 131104 | tf_op jit(solution)/shard_map/ppermute | solution.py:283
  69.4 2.5 %collective-permute-start.12 = (bf16[512,128]{1,0:T(8,128)(2,1)S(1)}, bf16[512,128]{1,0:T(8,128)(2,1)S(1)}, u32[]{:S(2)}, u32[]{:S(2)}) collective-permute-start(bf16[512,128]{1,0:T(8,128)(2,1)S(1)} %get-tuple-element.48), channel_id=1, source_target_pairs={{0,7},{1,6},{2,5},{3,4},{4,3},{5,2},{6,1},{7,0},{8,15},{9,14},{10,... | collective-permute-start | bytes 393224 | tf_op jit(solution)/shard_map/ppermute | solution.py:283
  71.9 0.0 collective-permute-done.11.refs_4_
  71.9 0.0 collective-permute-start.13
  71.9 6.5 %collective-permute-done.12.refs_5_ = bf16[512,128]{1,0:T(8,128)(2,1)S(1)} collective-permute-done((bf16[512,128]{1,0:T(8,128)(2,1)S(1)}, bf16[512,128]{1,0:T(8,128)(2,1)S(1)}, u32[]{:S(2)}, u32[]{:S(2)}) %collective-permute-start.12) | collective-permute-done | bytes 131104 | tf_op jit(solution)/shard_map/ppermute | solution.py:283
  78.4 0.8 %collective-permute-done.13.refs_6_ = bf16[512,128]{1,0:T(8,128)(2,1)S(1)} collective-permute-done((bf16[512,128]{1,0:T(8,128)(2,1)S(1)}, bf16[512,128]{1,0:T(8,128)(2,1)S(1)}, u32[]{:S(2)}, u32[]{:S(2)}) %collective-permute-start.13) | collective-permute-done | bytes 131104 | tf_op jit(solution)/shard_map/ppermute | solution.py:283
  79.2 1.6 %shard_map.80 = bf16[8,512,128]{2,1,0:T(8,128)(2,1)} custom-call(s32[2]{0:T(128)S(1)} %pad_add_fusion.where, bf16[512,128]{1,0:T(8,128)(2,1)S(1)} %collective-permute-done.7.refs_0_, bf16[512,128]{1,0:T(8,128)(2,1)S(1)} %collective-permute-done.8.refs_1_, bf16[512,128]{1,0:T(8,128)(2,1)S(1)} %collective-permute-done.9.refs_2_, ...), custom_call_target="tpu_custom_call" | custom-call | bytes 2097160 | tf_op jit(solution)/shard_map/pallas_call | solution.py:252
  80.8 0.0 collective-permute-done.21
  80.8 0.0 collective-permute-done.22
  80.8 0.0 collective-permute-done.23
  80.8 0.9 %add_multiply_fusion = f32[512,256]{1,0:T(8,128)} fusion(bf16[512,256]{1,0:T(8,128)(2,1)S(1)} %get-tuple-element.63, bf16[512,256]{1,0:T(8,128)(2,1)S(1)} %collective-permute-done.23, bf16[512,256]{1,0:T(8,128)(2,1)S(1)} %collective-permute-done.22, bf16[512,256]{1,0:T(8,128)(2,1)S(1)} %collective-permute-done.21), kind=kLoop, calls=%fused_computation | loop fusion | flops 1048576 | bytes 1572864 | tf_op jit(solution)/shard_map/mul | solution.py:341
Async XLA Ops:
  0.6 24.6 %copy-start = (bf16[9,256,256]{2,1,0:T(8,128)(2,1)S(1)}, bf16[9,256,256]{2,1,0:T(8,128)(2,1)}, u32[]{:S(2)}) copy-start(bf16[9,256,256]{2,1,0:T(8,128)(2,1)} %constant.14.clone.forward.refs_11_.refs_9_) | copy-start | bytes 3538948
  3.4 14.8 %collective-permute-start = (bf16[512,128]{1,0:T(8,128)(2,1)S(1)}, bf16[512,128]{1,0:T(8,128)(2,1)S(1)}, u32[]{:S(2)}, u32[]{:S(2)}) collective-permute-start(bf16[512,128]{1,0:T(8,128)(2,1)S(1)} %get-tuple-element.33), channel_id=1, source_target_pairs={{0,4},{1,5},{2,6},{3,7},{4,0},{5,1},{6,2},{7,3},{8,12},{9,13},{10,... | collective-permute-start | bytes 393224 | tf_op jit(solution)/shard_map/ppermute | solution.py:283
  7.5 11.8 %collective-permute-start.1 = (bf16[512,128]{1,0:T(8,128)(2,1)S(1)}, bf16[512,128]{1,0:T(8,128)(2,1)S(1)}, u32[]{:S(2)}, u32[]{:S(2)}) collective-permute-start(bf16[512,128]{1,0:T(8,128)(2,1)S(1)} %get-tuple-element.34), channel_id=1, source_target_pairs={{0,1},{1,0},{2,3},{3,2},{4,5},{5,4},{6,7},{7,6},{8,9},{9,8},{10,11... | collective-permute-start | bytes 393224 | tf_op jit(solution)/shard_map/ppermute | solution.py:283
  9.0 15.3 %collective-permute-start.2 = (bf16[512,128]{1,0:T(8,128)(2,1)S(1)}, bf16[512,128]{1,0:T(8,128)(2,1)S(1)}, u32[]{:S(2)}, u32[]{:S(2)}) collective-permute-start(bf16[512,128]{1,0:T(8,128)(2,1)S(1)} %get-tuple-element.35), channel_id=1, source_target_pairs={{0,5},{1,4},{2,7},{3,6},{4,1},{5,0},{6,3},{7,2},{8,13},{9,12},{10,... | collective-permute-start | bytes 393224 | tf_op jit(solution)/shard_map/ppermute | solution.py:283
  9.0 15.3 %collective-permute-start.3 = (bf16[512,128]{1,0:T(8,128)(2,1)S(1)}, bf16[512,128]{1,0:T(8,128)(2,1)S(1)}, u32[]{:S(2)}, u32[]{:S(2)}) collective-permute-start(bf16[512,128]{1,0:T(8,128)(2,1)S(1)} %get-tuple-element.36), channel_id=1, source_target_pairs={{0,2},{1,3},{2,0},{3,1},{4,6},{5,7},{6,4},{7,5},{8,10},{9,11},{10,... | collective-permute-start | bytes 393224 | tf_op jit(solution)/shard_map/ppermute | solution.py:283
  10.9 17.4 %collective-permute-start.4 = (bf16[512,128]{1,0:T(8,128)(2,1)S(1)}, bf16[512,128]{1,0:T(8,128)(2,1)S(1)}, u32[]{:S(2)}, u32[]{:S(2)}) collective-permute-start(bf16[512,128]{1,0:T(8,128)(2,1)S(1)} %get-tuple-element.37), channel_id=1, source_target_pairs={{0,6},{1,7},{2,4},{3,5},{4,2},{5,3},{6,0},{7,1},{8,14},{9,15},{10,... | collective-permute-start | bytes 393224 | tf_op jit(solution)/shard_map/ppermute | solution.py:283
  18.2 16.2 %collective-permute-start.5 = (bf16[512,128]{1,0:T(8,128)(2,1)S(1)}, bf16[512,128]{1,0:T(8,128)(2,1)S(1)}, u32[]{:S(2)}, u32[]{:S(2)}) collective-permute-start(bf16[512,128]{1,0:T(8,128)(2,1)S(1)} %get-tuple-element.38), channel_id=1, source_target_pairs={{0,3},{1,2},{2,1},{3,0},{4,7},{5,6},{6,5},{7,4},{8,11},{9,10},{10,... | collective-permute-start | bytes 393224 | tf_op jit(solution)/shard_map/ppermute | solution.py:283
  19.3 15.1 %collective-permute-start.6 = (bf16[512,128]{1,0:T(8,128)(2,1)S(1)}, bf16[512,128]{1,0:T(8,128)(2,1)S(1)}, u32[]{:S(2)}, u32[]{:S(2)}) collective-permute-start(bf16[512,128]{1,0:T(8,128)(2,1)S(1)} %get-tuple-element.39), channel_id=1, source_target_pairs={{0,7},{1,6},{2,5},{3,4},{4,3},{5,2},{6,1},{7,0},{8,15},{9,14},{10,... | collective-permute-start | bytes 393224 | tf_op jit(solution)/shard_map/ppermute | solution.py:283
  24.4 16.4 %collective-permute-start.14 = (bf16[512,128]{1,0:T(8,128)(2,1)S(1)}, bf16[512,128]{1,0:T(8,128)(2,1)S(1)}, u32[]{:S(2)}, u32[]{:S(2)}) collective-permute-start(bf16[512,128]{1,0:T(8,128)(2,1)S(1)} %get-tuple-element.51), channel_id=1, source_target_pairs={{0,4},{1,5},{2,6},{3,7},{4,0},{5,1},{6,2},{7,3},{8,12},{9,13},{10,... | collective-permute-start | bytes 393224 | tf_op jit(solution)/shard_map/ppermute | solution.py:283
  24.4 11.4 %copy-start.1 = (bf16[9,256,256]{2,1,0:T(8,128)(2,1)S(1)}, bf16[9,256,256]{2,1,0:T(8,128)(2,1)}, u32[]{:S(2)}) copy-start(bf16[9,256,256]{2,1,0:T(8,128)(2,1)} %constant.15.clone.refs_12_.refs_10_) | copy-start | bytes 3538948
  24.4 17.7 %collective-permute-start.15 = (bf16[512,128]{1,0:T(8,128)(2,1)S(1)}, bf16[512,128]{1,0:T(8,128)(2,1)S(1)}, u32[]{:S(2)}, u32[]{:S(2)}) collective-permute-start(bf16[512,128]{1,0:T(8,128)(2,1)S(1)} %get-tuple-element.52), channel_id=1, source_target_pairs={{0,1},{1,0},{2,3},{3,2},{4,5},{5,4},{6,7},{7,6},{8,9},{9,8},{10,11... | collective-permute-start | bytes 393224 | tf_op jit(solution)/shard_map/ppermute | solution.py:283
  25.3 1.6 %copy-start.2 = (f32[512,1024]{1,0:T(8,128)S(1)}, f32[512,1024]{1,0:T(8,128)}, u32[]{:S(2)}) copy-start(f32[512,1024]{1,0:T(8,128)} %taps.1) | copy-start | bytes 6291460
  28.3 19.3 %collective-permute-start.16 = (bf16[512,128]{1,0:T(8,128)(2,1)S(1)}, bf16[512,128]{1,0:T(8,128)(2,1)S(1)}, u32[]{:S(2)}, u32[]{:S(2)}) collective-permute-start(bf16[512,128]{1,0:T(8,128)(2,1)S(1)} %get-tuple-element.53), channel_id=1, source_target_pairs={{0,5},{1,4},{2,7},{3,6},{4,1},{5,0},{6,3},{7,2},{8,13},{9,12},{10,... | collective-permute-start | bytes 393224 | tf_op jit(solution)/shard_map/ppermute | solution.py:283
  34.4 13.3 %collective-permute-start.17 = (bf16[512,128]{1,0:T(8,128)(2,1)S(1)}, bf16[512,128]{1,0:T(8,128)(2,1)S(1)}, u32[]{:S(2)}, u32[]{:S(2)}) collective-permute-start(bf16[512,128]{1,0:T(8,128)(2,1)S(1)} %get-tuple-element.54), channel_id=1, source_target_pairs={{0,2},{1,3},{2,0},{3,1},{4,6},{5,7},{6,4},{7,5},{8,10},{9,11},{10,... | collective-permute-start | bytes 393224 | tf_op jit(solution)/shard_map/ppermute | solution.py:283
  34.4 14.7 %collective-permute-start.18 = (bf16[512,128]{1,0:T(8,128)(2,1)S(1)}, bf16[512,128]{1,0:T(8,128)(2,1)S(1)}, u32[]{:S(2)}, u32[]{:S(2)}) collective-permute-start(bf16[512,128]{1,0:T(8,128)(2,1)S(1)} %get-tuple-element.55), channel_id=1, source_target_pairs={{0,6},{1,7},{2,4},{3,5},{4,2},{5,3},{6,0},{7,1},{8,14},{9,15},{10,... | collective-permute-start | bytes 393224 | tf_op jit(solution)/shard_map/ppermute | solution.py:283
  40.8 13.3 %collective-permute-start.19 = (bf16[512,128]{1,0:T(8,128)(2,1)S(1)}, bf16[512,128]{1,0:T(8,128)(2,1)S(1)}, u32[]{:S(2)}, u32[]{:S(2)}) collective-permute-start(bf16[512,128]{1,0:T(8,128)(2,1)S(1)} %get-tuple-element.56), channel_id=1, source_target_pairs={{0,3},{1,2},{2,1},{3,0},{4,7},{5,6},{6,5},{7,4},{8,11},{9,10},{10,... | collective-permute-start | bytes 393224 | tf_op jit(solution)/shard_map/ppermute | solution.py:283
  42.0 14.9 %collective-permute-start.20 = (bf16[512,128]{1,0:T(8,128)(2,1)S(1)}, bf16[512,128]{1,0:T(8,128)(2,1)S(1)}, u32[]{:S(2)}, u32[]{:S(2)}) collective-permute-start(bf16[512,128]{1,0:T(8,128)(2,1)S(1)} %get-tuple-element.57), channel_id=1, source_target_pairs={{0,7},{1,6},{2,5},{3,4},{4,3},{5,2},{6,1},{7,0},{8,15},{9,14},{10,... | collective-permute-start | bytes 393224 | tf_op jit(solution)/shard_map/ppermute | solution.py:283
  47.7 14.0 %collective-permute-start.7 = (bf16[512,128]{1,0:T(8,128)(2,1)S(1)}, bf16[512,128]{1,0:T(8,128)(2,1)S(1)}, u32[]{:S(2)}, u32[]{:S(2)}) collective-permute-start(bf16[512,128]{1,0:T(8,128)(2,1)S(1)} %get-tuple-element.43), channel_id=1, source_target_pairs={{0,1},{1,0},{2,3},{3,2},{4,5},{5,4},{6,7},{7,6},{8,9},{9,8},{10,11... | collective-permute-start | bytes 393224 | tf_op jit(solution)/shard_map/ppermute | solution.py:283
  47.7 15.5 %collective-permute-start.8 = (bf16[512,128]{1,0:T(8,128)(2,1)S(1)}, bf16[512,128]{1,0:T(8,128)(2,1)S(1)}, u32[]{:S(2)}, u32[]{:S(2)}) collective-permute-start(bf16[512,128]{1,0:T(8,128)(2,1)S(1)} %get-tuple-element.44), channel_id=1, source_target_pairs={{0,4},{1,5},{2,6},{3,7},{4,0},{5,1},{6,2},{7,3},{8,12},{9,13},{10,... | collective-permute-start | bytes 393224 | tf_op jit(solution)/shard_map/ppermute | solution.py:283
  49.1 14.1 %collective-permute-start.9 = (bf16[512,128]{1,0:T(8,128)(2,1)S(1)}, bf16[512,128]{1,0:T(8,128)(2,1)S(1)}, u32[]{:S(2)}, u32[]{:S(2)}) collective-permute-start(bf16[512,128]{1,0:T(8,128)(2,1)S(1)} %get-tuple-element.45), channel_id=1, source_target_pairs={{0,2},{1,3},{2,0},{3,1},{4,6},{5,7},{6,4},{7,5},{8,10},{9,11},{10,... | collective-permute-start | bytes 393224 | tf_op jit(solution)/shard_map/ppermute | solution.py:283
  54.1 15.3 %collective-permute-start.10 = (bf16[512,128]{1,0:T(8,128)(2,1)S(1)}, bf16[512,128]{1,0:T(8,128)(2,1)S(1)}, u32[]{:S(2)}, u32[]{:S(2)}) collective-permute-start(bf16[512,128]{1,0:T(8,128)(2,1)S(1)} %get-tuple-element.46), channel_id=1, source_target_pairs={{0,5},{1,4},{2,7},{3,6},{4,1},{5,0},{6,3},{7,2},{8,13},{9,12},{10,... | collective-permute-start | bytes 393224 | tf_op jit(solution)/shard_map/ppermute | solution.py:283
  56.9 15.0 %collective-permute-start.11 = (bf16[512,128]{1,0:T(8,128)(2,1)S(1)}, bf16[512,128]{1,0:T(8,128)(2,1)S(1)}, u32[]{:S(2)}, u32[]{:S(2)}) collective-permute-start(bf16[512,128]{1,0:T(8,128)(2,1)S(1)} %get-tuple-element.47), channel_id=1, source_target_pairs={{0,6},{1,7},{2,4},{3,5},{4,2},{5,3},{6,0},{7,1},{8,14},{9,15},{10,... | collective-permute-start | bytes 393224 | tf_op jit(solution)/shard_map/ppermute | solution.py:283
  61.7 19.2 %collective-permute-start.21 = (bf16[512,256]{1,0:T(8,128)(2,1)S(1)}, bf16[512,256]{1,0:T(8,128)(2,1)S(1)}, u32[]{:S(2)}, u32[]{:S(2)}) collective-permute-start(bf16[512,256]{1,0:T(8,128)(2,1)S(1)} %get-tuple-element.60), channel_id=1, source_target_pairs={{0,16},{8,24},{16,0},{24,8},{1,17},{9,25},{17,1},{25,9},{2,18},{10... | collective-permute-start | bytes 786440 | tf_op jit(solution)/shard_map/ppermute | solution.py:283
  63.2 17.6 %collective-permute-start.22 = (bf16[512,256]{1,0:T(8,128)(2,1)S(1)}, bf16[512,256]{1,0:T(8,128)(2,1)S(1)}, u32[]{:S(2)}, u32[]{:S(2)}) collective-permute-start(bf16[512,256]{1,0:T(8,128)(2,1)S(1)} %get-tuple-element.61), channel_id=1, source_target_pairs={{0,24},{8,16},{16,8},{24,0},{1,25},{9,17},{17,9},{25,1},{2,26},{10... | collective-permute-start | bytes 786440 | tf_op jit(solution)/shard_map/ppermute | solution.py:283
  63.2 17.6 %collective-permute-start.23 = (bf16[512,256]{1,0:T(8,128)(2,1)S(1)}, bf16[512,256]{1,0:T(8,128)(2,1)S(1)}, u32[]{:S(2)}, u32[]{:S(2)}) collective-permute-start(bf16[512,256]{1,0:T(8,128)(2,1)S(1)} %get-tuple-element.62), channel_id=1, source_target_pairs={{0,8},{8,0},{16,24},{24,16},{1,9},{9,1},{17,25},{25,17},{2,10},{10... | collective-permute-start | bytes 786440 | tf_op jit(solution)/shard_map/ppermute | solution.py:283
  69.4 9.0 %collective-permute-start.12 = (bf16[512,128]{1,0:T(8,128)(2,1)S(1)}, bf16[512,128]{1,0:T(8,128)(2,1)S(1)}, u32[]{:S(2)}, u32[]{:S(2)}) collective-permute-start(bf16[512,128]{1,0:T(8,128)(2,1)S(1)} %get-tuple-element.48), channel_id=1, source_target_pairs={{0,7},{1,6},{2,5},{3,4},{4,3},{5,2},{6,1},{7,0},{8,15},{9,14},{10,... | collective-permute-start | bytes 393224 | tf_op jit(solution)/shard_map/ppermute | solution.py:283
  71.9 7.3 %collective-permute-start.13 = (bf16[512,128]{1,0:T(8,128)(2,1)S(1)}, bf16[512,128]{1,0:T(8,128)(2,1)S(1)}, u32[]{:S(2)}, u32[]{:S(2)}) collective-permute-start(bf16[512,128]{1,0:T(8,128)(2,1)S(1)} %get-tuple-element.49), channel_id=1, source_target_pairs={{0,3},{1,2},{2,1},{3,0},{4,7},{5,6},{6,5},{7,4},{8,11},{9,10},{10,... | collective-permute-start | bytes 393224 | tf_op jit(solution)/shard_map/ppermute | solution.py:283

commit v9 on v8

--- a/solution.py
+++ b/solution.py
@@ -144,11 +144,10 @@
     return ref.at[pl.ds(start, rows), :]
 
 
-def gate_kernel(order, where, gate, upper, whole, *refs):
-    outs, picks, refs = refs[: len(order)], refs[len(order) : 2 * len(order)], refs[2 * len(order) :]
-    left, right, sems, pick_sems = refs
+def gate_kernel(order, where, gate, upper, *refs):
+    outs, (left, right, sems) = refs[: len(order)], refs[len(order) :]
     rows = outs[0].shape[0]
-    loads, moves = [], []
+    loads = []
     for i, k in enumerate(order):
         pair = (
             pltpu.make_async_copy(piece_at(gate, where, k, rows), left.at[i], sems.at[0, i]),
@@ -157,15 +156,10 @@
         for copy in pair:
             copy.start()
         loads.append(pair)
-    for i, k in enumerate(order):
-        moves.append(pltpu.make_async_copy(piece_at(whole, where, k, rows), picks[i], pick_sems.at[i]))
-        moves[-1].start()
     for i, out in enumerate(outs):
         for copy in loads[i]:
             copy.wait()
         out[...] = (left[i].astype(jnp.float32) * right[i].astype(jnp.float32)).astype(jnp.bfloat16)
-    for copy in moves:
-        copy.wait()
 
 
 def place_kernel(order, where, *refs):
@@ -199,10 +193,9 @@
     return store
 
 
-def back_kernel(order, back_order, late, where, *refs):
-    blocks, refs = refs[: len(order)], refs[len(order) + late :]
+def back_kernel(order, back_order, where, *refs):
+    blocks, refs = refs[: len(order)], refs[len(order) :]
     taps_spec, forward, backward, *outs, grad_spec, held, mid, wide = refs
-    outs = outs[late:]
     rows, width = held.shape[0], held.shape[1] // BLOCKS
     ordered(order, where, blocks, held)
     split_rows(block_of(held, width), mid, rows, width)
@@ -220,11 +213,12 @@
         out[...] = held[:, pl.ds(start, span)]
 
 
-def cross_kernel(order, where, *refs):
-    blocks, refs = refs[: len(order)], refs[len(order) :]
-    grad_spec, forward, backward, *outs, held, mid, wide = refs
+def cross_kernel(where, blocks, grad_spec, forward, backward, *refs):
+    *outs, held, mid, wide = refs
     rows, width = held.shape[0], held.shape[1] // BLOCKS
-    ordered(order, where, blocks, held)
+    span = blocks.shape[2]
+    for p in range(blocks.shape[0]):
+        held[:, p * span : (p + 1) * span] = blocks[p]
     split_rows(block_of(held, width), mid, rows, width)
     for r in range(GROUPS):
         signal = spectrum(mid, forward, r, width)
@@ -239,23 +233,17 @@
         out[...] = held[:, pl.ds(start, part)]
 
 
-def call(kernel, operands, outs, scratch=(), flops=0, streams=(), out_streams=(), aliases=None, hbm=()):
-    def spec(stream):
-        return pl.BlockSpec(memory_space=pl.ANY if stream else pltpu.VMEM)
-
+def call(kernel, operands, outs, scratch=(), flops=0, streams=()):
     size = sum(math.prod(o.shape) * o.dtype.itemsize for o in list(operands) + list(outs))
-    specs = [spec(i in streams) for i in range(len(operands))]
-    for i in hbm:
-        specs[i] = pl.BlockSpec(memory_space=pltpu.HBM)
+    specs = [pl.BlockSpec(memory_space=pl.ANY if i in streams else pltpu.VMEM) for i in range(len(operands))]
     if operands[0].dtype == jnp.int32:
         specs[0] = pl.BlockSpec(memory_space=pltpu.SMEM)
     outputs = pl.pallas_call(
         kernel,
         out_shape=list(outs),
         in_specs=specs,
-        out_specs=[spec(i in out_streams) for i in range(len(outs))],
+        out_specs=[pl.BlockSpec(memory_space=pltpu.VMEM)] * len(outs),
         scratch_shapes=list(scratch),
-        input_output_aliases=aliases or {},
         compiler_params=pltpu.CompilerParams(vmem_limit_bytes=LIMIT),
         cost_estimate=pl.CostEstimate(flops=flops, bytes_accessed=size, transcendentals=0),
     )(*operands)
@@ -289,8 +277,7 @@
     channels, span = saved_input.shape[1:]
     rows, length = long_filter.shape
     width = length // BLOCKS
-    order, back_order, late = mixed(count), back_mixed(count), 2
-    at = count - 1 - late
+    order, back_order = mixed(count), back_mixed(count)
     every = range(count + 8)
     where = jnp.stack([lax.axis_index("ctx"), lax.axis_index("dp")]).astype(jnp.int32)
     forward, backward = (jnp.asarray(t) for t in transform_tables(width))
@@ -304,34 +291,29 @@
     sems = pltpu.SemaphoreType.DMA
     work = 2 * GROUPS * rows * 4 * width * width
 
-    pieces = call(
+    grad_pieces = call(
         functools.partial(gate_kernel, order),
-        [where, *(pltpu.with_memory_space_constraint(x[0], pltpu.HBM) for x in (out_gate, grad_out, saved_input))],
-        [piece] * (2 * count),
-        [slots, slots, sems((2, count)), sems((count,))],
-        hbm=(1, 2, 3),
-    )
-    grad_pieces, input_pieces = pieces[:count], pieces[count:]
+        [where, *(pltpu.with_memory_space_constraint(x[0], pltpu.HBM) for x in (out_gate, grad_out))],
+        [piece] * count,
+        [slots, slots, sems((2, count))],
+        streams=(1, 2),
+    )
     grad_blocks = exchange(grad_pieces, order, "ctx", count)
+    whole_input = saved_input.reshape(count, rows, span)
+    input_blocks = lax.all_to_all(whole_input, "ctx", split_axis=0, concat_axis=0, tiled=True)
     (taps_spec,) = call(taps_kernel, [long_filter, forward], [spec], [mid], flops=work)
-    passed = [*input_pieces[at : at + late]]
     *back, grad_spec = call(
-        functools.partial(back_kernel, order, back_order, late),
-        [where, *grad_blocks, *passed, taps_spec, forward, backward],
-        [piece] * (late + count) + [spec],
+        functools.partial(back_kernel, order, back_order),
+        [where, *grad_blocks, taps_spec, forward, backward],
+        [piece] * count + [spec],
         [held, mid, wide],
         flops=2 * work,
-        streams=range(1 + count, 1 + count + late),
-        out_streams=range(late),
-        aliases={1 + count + i: i for i in range(late)},
-    )
-    input_pieces[at : at + late], back = back[:late], back[late:]
-    input_blocks = exchange(input_pieces, order, "ctx", count)
+    )
     back_blocks = exchange(back, back_order, "ctx", count)
     share = jax.ShapeDtypeStruct((rows, length // shares), half)
     cross = call(
-        functools.partial(cross_kernel, order),
-        [where, *input_blocks, grad_spec, forward, backward],
+        cross_kernel,
+        [where, input_blocks, grad_spec, forward, backward],
         [share] * shares,
         [held, mid, wide],
         flops=2 * work,

time: 81.9 us -> 94.2 us (1.15)
  waiting for transfers between devices: 21.2 us -> 41.1 us
  starting transfers between devices: 43.2 us -> 31.6 us
  local copies, waits for them, and re-layouts: 1.6 us -> 4.42 us
  Pallas kernels: 14.1 us -> 15.1 us
    ppermute x24 -> x17, waiting for transfers between devices: 21.2 us -> 41.1 us  [exchange(): lax.ppermute(piece, axis, [(i, i ^ k) for i in range(size)])]
    ppermute x24 -> x17, starting transfers between devices: 43.2 us -> 24.1 us  [exchange(): lax.ppermute(piece, axis, [(i, i ^ k) for i in range(size)])]
    all_to_all x0 -> x1, starting transfers between devices: none -> 7.42 us  [on_device(): lax.all_to_all(whole_input, 'ctx', split_axis=0, concat_axis=0, tiled=True)]
    unnamed x6 -> x18, local copies, waits for them, and re-layouts: 1.6 us -> 4.42 us
    pallas_call x5, Pallas kernels: 14.1 us -> 15.1 us  [call(): pl.pallas_call(kernel, out_shape=list(outs), in_specs=specs, out_specs=[p...]
  transfers between devices with their start and end apart: 24 -> 18, of which waited for: 7 -> 5; matrix products, arithmetic and copies ran while one was open for 0% -> 0% of each run, Pallas kernels for 14% -> 16%
where the time goes in v9:
time: 94.2 us; the launch traced here: 93.9 us
  waiting for transfers between devices  41.1 us (44%)
  starting transfers between devices  31.6 us (34%)
  Pallas kernels  15.1 us (16%)
  local copies, waits for them, and re-layouts  4.42 us (5%)
  other arithmetic  1.01 us (1%)
    ppermute x17, waiting for transfers between devices, exchange(): lax.ppermute(piece, axis, [(i, i ^ k) for i in range(size)])  41.1 us
    ppermute x17, starting transfers between devices, exchange(): lax.ppermute(piece, axis, [(i, i ^ k) for i in range(size)])  24.1 us
    pallas_call x5, Pallas kernels, call(): pl.pallas_call(kernel, out_shape=list(outs), in_specs=specs, out_specs=[p...  15.1 us
    all_to_all x1, starting transfers between devices, on_device(): lax.all_to_all(whole_input, 'ctx', split_axis=0, concat_axis=0, tiled=True)  7.42 us
    unnamed x18, local copies, waits for them, and re-layouts  4.42 us
  transfers between devices with their start and end apart: 18, of which 5 were waited for; matrix products, arithmetic and copies ran while one was open for 0% of the time, Pallas kernels for 16%

profile of v9, /device:TPU:0, one launch (start us, length us, event | category | flops | bytes accessed | tf_op | source)
XLA Modules:
  0.0 93.9 jit_solution(12099371382548075191)
XLA Ops:
  0.6 0.0 copy-start
  0.6 7.4 %all-to-all-start = ((bf16[8,512,128]{2,1,0:T(8,128)(2,1)}), bf16[8,512,128]{2,1,0:T(8,128)(2,1)S(1)}, u32[]{:S(2)}, u32[]{:S(2)}) async-start(bf16[8,512,128]{2,1,0:T(8,128)(2,1)} %bitcast.9), calls=%async_computation | async-start | bytes 2097152 | tf_op jit(solution)/shard_map/all_to_all | solution.py:303
  8.1 0.0 copy-start.4
  8.1 0.1 pad_add_fusion.where
  8.1 2.3 %shard_map.77 = (bf16[512,128]{1,0:T(8,128)(2,1)S(1)}, bf16[512,128]{1,0:T(8,128)(2,1)S(1)}, bf16[512,128]{1,0:T(8,128)(2,1)S(1)}, bf16[512,128]{1,0:T(8,128)(2,...) custom-call(s32[2]{0:T(128)S(1)} %pad_add_fusion.where, ...), custom_call_target="tpu_custom_call" | custom-call | bytes 3145736 | tf_op jit(solution)/shard_map/pallas_call | solution.py:241
  10.5 3.0 %collective-permute-start = (bf16[512,128]{1,0:T(8,128)(2,1)S(1)}, bf16[512,128]{1,0:T(8,128)(2,1)S(1)}, u32[]{:S(2)}, u32[]{:S(2)}) collective-permute-start(bf16[512,128]{1,0:T(8,128)(2,1)S(1)} %get-tuple-element.23), channel_id=1, source_target_pairs={{0,4},{1,5},{2,6},{3,7},{4,0},{5,1},{6,2},{7,3},{8,12},{9,13},{10,... | collective-permute-start | bytes 393224 | tf_op jit(solution)/shard_map/ppermute | solution.py:271
  13.5 1.5 %collective-permute-start.1 = (bf16[512,128]{1,0:T(8,128)(2,1)S(1)}, bf16[512,128]{1,0:T(8,128)(2,1)S(1)}, u32[]{:S(2)}, u32[]{:S(2)}) collective-permute-start(bf16[512,128]{1,0:T(8,128)(2,1)S(1)} %get-tuple-element.24), channel_id=1, source_target_pairs={{0,1},{1,0},{2,3},{3,2},{4,5},{5,4},{6,7},{7,6},{8,9},{9,8},{10,11... | collective-permute-start | bytes 393224 | tf_op jit(solution)/shard_map/ppermute | solution.py:271
  14.9 0.1 collective-permute-start.2
  15.0 1.9 %collective-permute-start.3 = (bf16[512,128]{1,0:T(8,128)(2,1)S(1)}, bf16[512,128]{1,0:T(8,128)(2,1)S(1)}, u32[]{:S(2)}, u32[]{:S(2)}) collective-permute-start(bf16[512,128]{1,0:T(8,128)(2,1)S(1)} %get-tuple-element.26), channel_id=1, source_target_pairs={{0,2},{1,3},{2,0},{3,1},{4,6},{5,7},{6,4},{7,5},{8,10},{9,11},{10,... | collective-permute-start | bytes 393224 | tf_op jit(solution)/shard_map/ppermute | solution.py:271
  17.0 2.4 %collective-permute-start.4 = (bf16[512,128]{1,0:T(8,128)(2,1)S(1)}, bf16[512,128]{1,0:T(8,128)(2,1)S(1)}, u32[]{:S(2)}, u32[]{:S(2)}) collective-permute-start(bf16[512,128]{1,0:T(8,128)(2,1)S(1)} %get-tuple-element.27), channel_id=1, source_target_pairs={{0,6},{1,7},{2,4},{3,5},{4,2},{5,3},{6,0},{7,1},{8,14},{9,15},{10,... | collective-permute-start | bytes 393224 | tf_op jit(solution)/shard_map/ppermute | solution.py:271
  19.3 27.2 %collective-permute-done.refs_0_ = bf16[512,128]{1,0:T(8,128)(2,1)S(1)} collective-permute-done((bf16[512,128]{1,0:T(8,128)(2,1)S(1)}, bf16[512,128]{1,0:T(8,128)(2,1)S(1)}, u32[]{:S(2)}, u32[]{:S(2)}) %collective-permute-start) | collective-permute-done | bytes 131104 | tf_op jit(solution)/shard_map/ppermute | solution.py:271
  46.5 0.0 collective-permute-start.5
  46.5 0.0 collective-permute-done.1.refs_1_
  46.5 0.0 copy-start.1
  46.5 1.9 %collective-permute-start.6 = (bf16[512,128]{1,0:T(8,128)(2,1)S(1)}, bf16[512,128]{1,0:T(8,128)(2,1)S(1)}, u32[]{:S(2)}, u32[]{:S(2)}) collective-permute-start(bf16[512,128]{1,0:T(8,128)(2,1)S(1)} %get-tuple-element.29), channel_id=1, source_target_pairs={{0,7},{1,6},{2,5},{3,4},{4,3},{5,2},{6,1},{7,0},{8,15},{9,14},{10,... | collective-permute-start | bytes 393224 | tf_op jit(solution)/shard_map/ppermute | solution.py:271
  48.4 0.0 copy-done
  48.4 0.0 copy-done.4
  48.4 1.5 %shard_map.78.refs_8_ = bf16[9,512,256]{2,1,0:T(8,128)(2,1)S(1)} custom-call(f32[512,1024]{1,0:T(8,128)S(1)} %copy-done.4, bf16[9,256,256]{2,1,0:T(8,128)(2,1)S(1)} %copy-done), custom_call_target="tpu_custom_call" | custom-call | flops 603979776 | bytes 5636096 | tf_op jit(solution)/shard_map/pallas_call | solution.py:241
  49.9 0.4 collective-permute-done.2.refs_2_
  50.3 0.0 collective-permute-done.3.refs_3_
  50.3 0.0 collective-permute-done.4.refs_4_
  50.3 4.1 %collective-permute-done.5.refs_5_ = bf16[512,128]{1,0:T(8,128)(2,1)S(1)} collective-permute-done((bf16[512,128]{1,0:T(8,128)(2,1)S(1)}, bf16[512,128]{1,0:T(8,128)(2,1)S(1)}, u32[]{:S(2)}, u32[]{:S(2)}) %collective-permute-start.5) | collective-permute-done | bytes 131104 | tf_op jit(solution)/shard_map/ppermute | solution.py:271
  54.4 0.0 collective-permute-done.6.refs_6_
  54.4 0.0 copy-done.1
  54.4 5.0 %shard_map.79 = (bf16[512,128]{1,0:T(8,128)(2,1)}, bf16[512,128]{1,0:T(8,128)(2,1)S(1)}, bf16[512,128]{1,0:T(8,128)(2,1)S(1)}, bf16[512,128]{1,0:T(8,128)(2,1)},...) custom-call(s32[2]{0:T(128)S(1)} %pad_add_fusion.where, ...), custom_call_target="tpu_custom_call" | custom-call | flops 1207959552 | bytes 9175048 | tf_op jit(solution)/shard_map/pallas_call | solution.py:241
  59.4 0.0 copy-start.2
  59.4 1.4 %copy-done.2 = bf16[9,512,256]{2,1,0:T(8,128)(2,1)} copy-done((bf16[9,512,256]{2,1,0:T(8,128)(2,1)}, bf16[9,512,256]{2,1,0:T(8,128)(2,1)S(1)}, u32[]{:S(2)}) %copy-start.2) | copy-done | bytes 2359320
  60.8 0.0 copy-start.5
  60.8 0.6 copy-done.5
  61.4 0.0 copy-start.7
  61.4 0.7 copy-done.7
  62.1 3.1 %collective-permute-start.10 = (bf16[512,128]{1,0:T(8,128)(2,1)}, bf16[512,128]{1,0:T(8,128)(2,1)}, u32[]{:S(2)}, u32[]{:S(2)}) collective-permute-start(bf16[512,128]{1,0:T(8,128)(2,1)} %get-tuple-element.34), channel_id=1, source_target_pairs={{0,5},{1,4},{2,7},{3,6},{4,1},{5,0},{6,3},{7,2},{8,13},{9,12},{10,... | collective-permute-start | bytes 393224 | tf_op jit(solution)/shard_map/ppermute | solution.py:271
  65.2 2.7 %collective-permute-start.11 = (bf16[512,128]{1,0:T(8,128)(2,1)}, bf16[512,128]{1,0:T(8,128)(2,1)}, u32[]{:S(2)}, u32[]{:S(2)}) collective-permute-start(bf16[512,128]{1,0:T(8,128)(2,1)} %get-tuple-element.35), channel_id=1, source_target_pairs={{0,6},{1,7},{2,4},{3,5},{4,2},{5,3},{6,0},{7,1},{8,14},{9,15},{10,... | collective-permute-start | bytes 393224 | tf_op jit(solution)/shard_map/ppermute | solution.py:271
  67.9 2.3 %collective-permute-start.12 = (bf16[512,128]{1,0:T(8,128)(2,1)}, bf16[512,128]{1,0:T(8,128)(2,1)}, u32[]{:S(2)}, u32[]{:S(2)}) collective-permute-start(bf16[512,128]{1,0:T(8,128)(2,1)} %get-tuple-element.36), channel_id=1, source_target_pairs={{0,7},{1,6},{2,5},{3,4},{4,3},{5,2},{6,1},{7,0},{8,15},{9,14},{10,... | collective-permute-start | bytes 393224 | tf_op jit(solution)/shard_map/ppermute | solution.py:271
  70.2 0.0 collective-permute-start.13
  70.2 0.3 collective-permute-start.7
  70.5 0.0 all-to-all-done.blocks
  70.5 0.0 copy-start.3
  70.5 1.7 %copy-done.3 = bf16[9,512,256]{2,1,0:T(8,128)(2,1)S(1)} copy-done((bf16[9,512,256]{2,1,0:T(8,128)(2,1)S(1)}, bf16[9,512,256]{2,1,0:T(8,128)(2,1)}, u32[]{:S(2)}) %copy-start.3) | copy-done | bytes 2359320
  72.1 0.0 copy-start.8
  72.1 0.0 copy-start.6
  72.1 4.1 %shard_map.81 = (bf16[512,256]{1,0:T(8,128)(2,1)S(1)}, bf16[512,256]{1,0:T(8,128)(2,1)S(1)}, bf16[512,256]{1,0:T(8,128)(2,1)S(1)}, bf16[512,256]{1,0:T(8,128)(2,1)S(1)}) custom-call(s32[2]{0:T(128)S(1)} %pad_add_fusion.where, bf16[8,512,128]{2,1,0:T(8,128)(2,1)S(1)} %all-to-all-done.blocks, bf16[9,512,256]{2,1,0:T(8,128)(2,1)S(1)} %copy-done.3, ...), custom_call_target="tpu_custom_call" | custom-call | flops 1207959552 | bytes 6815752 | tf_op jit(solution)/shard_map/pallas_call | solution.py:241
  76.2 2.9 %collective-permute-done.10.refs_3_ = bf16[512,128]{1,0:T(8,128)(2,1)} collective-permute-done((bf16[512,128]{1,0:T(8,128)(2,1)}, bf16[512,128]{1,0:T(8,128)(2,1)}, u32[]{:S(2)}, u32[]{:S(2)}) %collective-permute-start.10) | collective-permute-done | bytes 131104 | tf_op jit(solution)/shard_map/ppermute | solution.py:271
  79.2 1.5 %collective-permute-start.14 = (bf16[512,256]{1,0:T(8,128)(2,1)S(1)}, bf16[512,256]{1,0:T(8,128)(2,1)S(1)}, u32[]{:S(2)}, u32[]{:S(2)}) collective-permute-start(bf16[512,256]{1,0:T(8,128)(2,1)S(1)} %get-tuple-element.40), channel_id=1, source_target_pairs={{0,16},{8,24},{16,0},{24,8},{1,17},{9,25},{17,1},{25,9},{2,18},{10... | collective-permute-start | bytes 786440 | tf_op jit(solution)/shard_map/ppermute | solution.py:271
  80.7 0.0 collective-permute-done.11.refs_4_
  80.7 0.0 collective-permute-start.15
  80.7 0.0 collective-permute-done.12.refs_5_
  80.7 0.7 collective-permute-start.16
  81.3 0.0 collective-permute-done.13.refs_6_
  81.3 0.0 copy-done.8
  81.3 2.9 %collective-permute-start.8 = (bf16[512,128]{1,0:T(8,128)(2,1)S(1)}, bf16[512,128]{1,0:T(8,128)(2,1)S(1)}, u32[]{:S(2)}, u32[]{:S(2)}) collective-permute-start(bf16[512,128]{1,0:T(8,128)(2,1)S(1)} %copy-done.8), channel_id=1, source_target_pairs={{0,4},{1,5},{2,6},{3,7},{4,0},{5,1},{6,2},{7,3},{8,12},{9,13},{10,... | collective-permute-start | bytes 393224 | tf_op jit(solution)/shard_map/ppermute | solution.py:271
  84.2 0.0 collective-permute-done.7.refs_0_
  84.2 0.0 copy-done.6
  84.2 0.0 collective-permute-start.9
  84.2 6.5 %collective-permute-done.8.refs_1_ = bf16[512,128]{1,0:T(8,128)(2,1)S(1)} collective-permute-done((bf16[512,128]{1,0:T(8,128)(2,1)S(1)}, bf16[512,128]{1,0:T(8,128)(2,1)S(1)}, u32[]{:S(2)}, u32[]{:S(2)}) %collective-permute-start.8) | collective-permute-done | bytes 131104 | tf_op jit(solution)/shard_map/ppermute | solution.py:271
  90.8 0.0 collective-permute-done.9.refs_2_
  90.8 2.2 %shard_map.80 = bf16[8,512,128]{2,1,0:T(8,128)(2,1)} custom-call(s32[2]{0:T(128)S(1)} %pad_add_fusion.where, bf16[512,128]{1,0:T(8,128)(2,1)} %collective-permute-done.7.refs_0_, bf16[512,128]{1,0:T(8,128)(2,1)S(1)} %collective-permute-done.8.refs_1_, bf16[512,128]{1,0:T(8,128)(2,1)S(1)} %collective-permute-done.9.refs_2_, ...), custom_call_target="tpu_custom_call" | custom-call | bytes 2097160 | tf_op jit(solution)/shard_map/pallas_call | solution.py:241
  93.0 0.0 collective-permute-done.14
  93.0 0.0 collective-permute-done.15
  93.0 0.0 collective-permute-done.16
  93.0 0.9 add_multiply_fusion
Async XLA Ops:
  0.6 47.8 %copy-start = (bf16[9,256,256]{2,1,0:T(8,128)(2,1)S(1)}, bf16[9,256,256]{2,1,0:T(8,128)(2,1)}, u32[]{:S(2)}) copy-start(bf16[9,256,256]{2,1,0:T(8,128)(2,1)} %constant.14.clone.forward.refs_9_) | copy-start | bytes 3538948
  0.6 69.8 %all-to-all-start = ((bf16[8,512,128]{2,1,0:T(8,128)(2,1)}), bf16[8,512,128]{2,1,0:T(8,128)(2,1)S(1)}, u32[]{:S(2)}, u32[]{:S(2)}) async-start(bf16[8,512,128]{2,1,0:T(8,128)(2,1)} %bitcast.9), calls=%async_computation | async-start | bytes 2097152 | tf_op jit(solution)/shard_map/all_to_all | solution.py:303
  8.1 40.3 %copy-start.4 = (f32[512,1024]{1,0:T(8,128)S(1)}, f32[512,1024]{1,0:T(8,128)}, u32[]{:S(2)}) copy-start(f32[512,1024]{1,0:T(8,128)} %taps.1) | copy-start | bytes 6291460
  10.5 36.0 %collective-permute-start = (bf16[512,128]{1,0:T(8,128)(2,1)S(1)}, bf16[512,128]{1,0:T(8,128)(2,1)S(1)}, u32[]{:S(2)}, u32[]{:S(2)}) collective-permute-start(bf16[512,128]{1,0:T(8,128)(2,1)S(1)} %get-tuple-element.23), channel_id=1, source_target_pairs={{0,4},{1,5},{2,6},{3,7},{4,0},{5,1},{6,2},{7,3},{8,12},{9,13},{10,... | collective-permute-start | bytes 393224 | tf_op jit(solution)/shard_map/ppermute | solution.py:271
  13.5 33.0 %collective-permute-start.1 = (bf16[512,128]{1,0:T(8,128)(2,1)S(1)}, bf16[512,128]{1,0:T(8,128)(2,1)S(1)}, u32[]{:S(2)}, u32[]{:S(2)}) collective-permute-start(bf16[512,128]{1,0:T(8,128)(2,1)S(1)} %get-tuple-element.24), channel_id=1, source_target_pairs={{0,1},{1,0},{2,3},{3,2},{4,5},{5,4},{6,7},{7,6},{8,9},{9,8},{10,11... | collective-permute-start | bytes 393224 | tf_op jit(solution)/shard_map/ppermute | solution.py:271
  14.9 35.3 %collective-permute-start.2 = (bf16[512,128]{1,0:T(8,128)(2,1)S(1)}, bf16[512,128]{1,0:T(8,128)(2,1)S(1)}, u32[]{:S(2)}, u32[]{:S(2)}) collective-permute-start(bf16[512,128]{1,0:T(8,128)(2,1)S(1)} %get-tuple-element.25), channel_id=1, source_target_pairs={{0,5},{1,4},{2,7},{3,6},{4,1},{5,0},{6,3},{7,2},{8,13},{9,12},{10,... | collective-permute-start | bytes 393224 | tf_op jit(solution)/shard_map/ppermute | solution.py:271
  15.0 35.2 %collective-permute-start.3 = (bf16[512,128]{1,0:T(8,128)(2,1)S(1)}, bf16[512,128]{1,0:T(8,128)(2,1)S(1)}, u32[]{:S(2)}, u32[]{:S(2)}) collective-permute-start(bf16[512,128]{1,0:T(8,128)(2,1)S(1)} %get-tuple-element.26), channel_id=1, source_target_pairs={{0,2},{1,3},{2,0},{3,1},{4,6},{5,7},{6,4},{7,5},{8,10},{9,11},{10,... | collective-permute-start | bytes 393224 | tf_op jit(solution)/shard_map/ppermute | solution.py:271
  17.0 33.3 %collective-permute-start.4 = (bf16[512,128]{1,0:T(8,128)(2,1)S(1)}, bf16[512,128]{1,0:T(8,128)(2,1)S(1)}, u32[]{:S(2)}, u32[]{:S(2)}) collective-permute-start(bf16[512,128]{1,0:T(8,128)(2,1)S(1)} %get-tuple-element.27), channel_id=1, source_target_pairs={{0,6},{1,7},{2,4},{3,5},{4,2},{5,3},{6,0},{7,1},{8,14},{9,15},{10,... | collective-permute-start | bytes 393224 | tf_op jit(solution)/shard_map/ppermute | solution.py:271
  46.5 7.9 %collective-permute-start.5 = (bf16[512,128]{1,0:T(8,128)(2,1)S(1)}, bf16[512,128]{1,0:T(8,128)(2,1)S(1)}, u32[]{:S(2)}, u32[]{:S(2)}) collective-permute-start(bf16[512,128]{1,0:T(8,128)(2,1)S(1)} %get-tuple-element.28), channel_id=1, source_target_pairs={{0,3},{1,2},{2,1},{3,0},{4,7},{5,6},{6,5},{7,4},{8,11},{9,10},{10,... | collective-permute-start | bytes 393224 | tf_op jit(solution)/shard_map/ppermute | solution.py:271
  46.5 7.9 %copy-start.1 = (bf16[9,256,256]{2,1,0:T(8,128)(2,1)S(1)}, bf16[9,256,256]{2,1,0:T(8,128)(2,1)}, u32[]{:S(2)}) copy-start(bf16[9,256,256]{2,1,0:T(8,128)(2,1)} %constant.15.clone.refs_10_.backward) | copy-start | bytes 3538948
  46.5 7.9 %collective-permute-start.6 = (bf16[512,128]{1,0:T(8,128)(2,1)S(1)}, bf16[512,128]{1,0:T(8,128)(2,1)S(1)}, u32[]{:S(2)}, u32[]{:S(2)}) collective-permute-start(bf16[512,128]{1,0:T(8,128)(2,1)S(1)} %get-tuple-element.29), channel_id=1, source_target_pairs={{0,7},{1,6},{2,5},{3,4},{4,3},{5,2},{6,1},{7,0},{8,15},{9,14},{10,... | collective-permute-start | bytes 393224 | tf_op jit(solution)/shard_map/ppermute | solution.py:271
  59.4 1.4 %copy-start.2 = (bf16[9,512,256]{2,1,0:T(8,128)(2,1)}, bf16[9,512,256]{2,1,0:T(8,128)(2,1)S(1)}, u32[]{:S(2)}) copy-start(bf16[9,512,256]{2,1,0:T(8,128)(2,1)S(1)} %get-tuple-element.39.grad_spec) | copy-start | bytes 7077892
  60.8 0.6 copy-start.5
  61.4 0.7 copy-start.7
  62.1 17.1 %collective-permute-start.10 = (bf16[512,128]{1,0:T(8,128)(2,1)}, bf16[512,128]{1,0:T(8,128)(2,1)}, u32[]{:S(2)}, u32[]{:S(2)}) collective-permute-start(bf16[512,128]{1,0:T(8,128)(2,1)} %get-tuple-element.34), channel_id=1, source_target_pairs={{0,5},{1,4},{2,7},{3,6},{4,1},{5,0},{6,3},{7,2},{8,13},{9,12},{10,... | collective-permute-start | bytes 393224 | tf_op jit(solution)/shard_map/ppermute | solution.py:271
  65.2 15.5 %collective-permute-start.11 = (bf16[512,128]{1,0:T(8,128)(2,1)}, bf16[512,128]{1,0:T(8,128)(2,1)}, u32[]{:S(2)}, u32[]{:S(2)}) collective-permute-start(bf16[512,128]{1,0:T(8,128)(2,1)} %get-tuple-element.35), channel_id=1, source_target_pairs={{0,6},{1,7},{2,4},{3,5},{4,2},{5,3},{6,0},{7,1},{8,14},{9,15},{10,... | collective-permute-start | bytes 393224 | tf_op jit(solution)/shard_map/ppermute | solution.py:271
  67.9 12.8 %collective-permute-start.12 = (bf16[512,128]{1,0:T(8,128)(2,1)}, bf16[512,128]{1,0:T(8,128)(2,1)}, u32[]{:S(2)}, u32[]{:S(2)}) collective-permute-start(bf16[512,128]{1,0:T(8,128)(2,1)} %get-tuple-element.36), channel_id=1, source_target_pairs={{0,7},{1,6},{2,5},{3,4},{4,3},{5,2},{6,1},{7,0},{8,15},{9,14},{10,... | collective-permute-start | bytes 393224 | tf_op jit(solution)/shard_map/ppermute | solution.py:271
  70.2 11.1 %collective-permute-start.13 = (bf16[512,128]{1,0:T(8,128)(2,1)}, bf16[512,128]{1,0:T(8,128)(2,1)}, u32[]{:S(2)}, u32[]{:S(2)}) collective-permute-start(bf16[512,128]{1,0:T(8,128)(2,1)} %get-tuple-element.37), channel_id=1, source_target_pairs={{0,3},{1,2},{2,1},{3,0},{4,7},{5,6},{6,5},{7,4},{8,11},{9,10},{10,... | collective-permute-start | bytes 393224 | tf_op jit(solution)/shard_map/ppermute | solution.py:271
  70.2 14.0 %collective-permute-start.7 = (bf16[512,128]{1,0:T(8,128)(2,1)}, bf16[512,128]{1,0:T(8,128)(2,1)}, u32[]{:S(2)}, u32[]{:S(2)}) collective-permute-start(bf16[512,128]{1,0:T(8,128)(2,1)} %get-tuple-element.31), channel_id=1, source_target_pairs={{0,1},{1,0},{2,3},{3,2},{4,5},{5,4},{6,7},{7,6},{8,9},{9,8},{10,11... | collective-permute-start | bytes 393224 | tf_op jit(solution)/shard_map/ppermute | solution.py:271
  70.5 1.7 %copy-start.3 = (bf16[9,512,256]{2,1,0:T(8,128)(2,1)S(1)}, bf16[9,512,256]{2,1,0:T(8,128)(2,1)}, u32[]{:S(2)}) copy-start(bf16[9,512,256]{2,1,0:T(8,128)(2,1)} %copy-done.2) | copy-start | bytes 7077892
  72.1 9.2 %copy-start.8 = (bf16[512,128]{1,0:T(8,128)(2,1)S(1)}, bf16[512,128]{1,0:T(8,128)(2,1)}, u32[]{:S(2)}) copy-start(bf16[512,128]{1,0:T(8,128)(2,1)} %copy-done.7) | copy-start | bytes 393220
  72.1 12.1 %copy-start.6 = (bf16[512,128]{1,0:T(8,128)(2,1)S(1)}, bf16[512,128]{1,0:T(8,128)(2,1)}, u32[]{:S(2)}) copy-start(bf16[512,128]{1,0:T(8,128)(2,1)} %copy-done.5) | copy-start | bytes 393220
  79.2 13.8 %collective-permute-start.14 = (bf16[512,256]{1,0:T(8,128)(2,1)S(1)}, bf16[512,256]{1,0:T(8,128)(2,1)S(1)}, u32[]{:S(2)}, u32[]{:S(2)}) collective-permute-start(bf16[512,256]{1,0:T(8,128)(2,1)S(1)} %get-tuple-element.40), channel_id=1, source_target_pairs={{0,16},{8,24},{16,0},{24,8},{1,17},{9,25},{17,1},{25,9},{2,18},{10... | collective-permute-start | bytes 786440 | tf_op jit(solution)/shard_map/ppermute | solution.py:271
  80.7 12.3 %collective-permute-start.15 = (bf16[512,256]{1,0:T(8,128)(2,1)S(1)}, bf16[512,256]{1,0:T(8,128)(2,1)S(1)}, u32[]{:S(2)}, u32[]{:S(2)}) collective-permute-start(bf16[512,256]{1,0:T(8,128)(2,1)S(1)} %get-tuple-element.41), channel_id=1, source_target_pairs={{0,24},{8,16},{16,8},{24,0},{1,25},{9,17},{17,9},{25,1},{2,26},{10... | collective-permute-start | bytes 786440 | tf_op jit(solution)/shard_map/ppermute | solution.py:271
  80.7 12.3 %collective-permute-start.16 = (bf16[512,256]{1,0:T(8,128)(2,1)S(1)}, bf16[512,256]{1,0:T(8,128)(2,1)S(1)}, u32[]{:S(2)}, u32[]{:S(2)}) collective-permute-start(bf16[512,256]{1,0:T(8,128)(2,1)S(1)} %get-tuple-element.42), channel_id=1, source_target_pairs={{0,8},{8,0},{16,24},{24,16},{1,9},{9,1},{17,25},{25,17},{2,10},{10... | collective-permute-start | bytes 786440 | tf_op jit(solution)/shard_map/ppermute | solution.py:271
  81.3 9.4 %collective-permute-start.8 = (bf16[512,128]{1,0:T(8,128)(2,1)S(1)}, bf16[512,128]{1,0:T(8,128)(2,1)S(1)}, u32[]{:S(2)}, u32[]{:S(2)}) collective-permute-start(bf16[512,128]{1,0:T(8,128)(2,1)S(1)} %copy-done.8), channel_id=1, source_target_pairs={{0,4},{1,5},{2,6},{3,7},{4,0},{5,1},{6,2},{7,3},{8,12},{9,13},{10,... | collective-permute-start | bytes 393224 | tf_op jit(solution)/shard_map/ppermute | solution.py:271
  84.2 6.5 %collective-permute-start.9 = (bf16[512,128]{1,0:T(8,128)(2,1)S(1)}, bf16[512,128]{1,0:T(8,128)(2,1)S(1)}, u32[]{:S(2)}, u32[]{:S(2)}) collective-permute-start(bf16[512,128]{1,0:T(8,128)(2,1)S(1)} %copy-done.6), channel_id=1, source_target_pairs={{0,2},{1,3},{2,0},{3,1},{4,6},{5,7},{6,4},{7,5},{8,10},{9,11},{10,... | collective-permute-start | bytes 393224 | tf_op jit(solution)/shard_map/ppermute | solution.py:271

commit v10 on v9

--- a/solution.py
+++ b/solution.py
@@ -213,12 +213,13 @@
         out[...] = held[:, pl.ds(start, span)]
 
 
-def cross_kernel(where, blocks, grad_spec, forward, backward, *refs):
+def cross_kernel(where, upper, lower, grad_spec, forward, backward, *refs):
     *outs, held, mid, wide = refs
     rows, width = held.shape[0], held.shape[1] // BLOCKS
-    span = blocks.shape[2]
-    for p in range(blocks.shape[0]):
-        held[:, p * span : (p + 1) * span] = blocks[p]
+    span = upper.shape[2]
+    for p in range(upper.shape[0]):
+        held[: rows // 2, p * span : (p + 1) * span] = upper[p]
+        held[rows // 2 :, p * span : (p + 1) * span] = lower[p]
     split_rows(block_of(held, width), mid, rows, width)
     for r in range(GROUPS):
         signal = spectrum(mid, forward, r, width)
@@ -254,17 +255,6 @@
     return [*range(size // 2, size), *range(1, size // 2), 0]
 
 
-def mixed(size):
-    far = far_first(size)
-    return [k for pair in zip(far[: size // 2], far[size // 2 :]) for k in pair]
-
-
-def back_mixed(size):
-    half = size // 2
-    pairs = [k for pair in zip(range(1, half), range(half, size)) for k in pair]
-    return [*pairs[:-2], size - 2, size - 1, half - 1, 0]
-
-
 def exchange(pieces, order, axis, size):
     moved = []
     for k, piece in zip(order, pieces):
@@ -277,7 +267,7 @@
     channels, span = saved_input.shape[1:]
     rows, length = long_filter.shape
     width = length // BLOCKS
-    order, back_order = mixed(count), back_mixed(count)
+    order, back_order = far_first(count), far_first(count)
     every = range(count + 8)
     where = jnp.stack([lax.axis_index("ctx"), lax.axis_index("dp")]).astype(jnp.int32)
     forward, backward = (jnp.asarray(t) for t in transform_tables(width))
@@ -300,7 +290,10 @@
     )
     grad_blocks = exchange(grad_pieces, order, "ctx", count)
     whole_input = saved_input.reshape(count, rows, span)
-    input_blocks = lax.all_to_all(whole_input, "ctx", split_axis=0, concat_axis=0, tiled=True)
+    input_parts = [
+        lax.all_to_all(part, "ctx", split_axis=0, concat_axis=0, tiled=True)
+        for part in (whole_input[:, : rows // 2], whole_input[:, rows // 2 :])
+    ]
     (taps_spec,) = call(taps_kernel, [long_filter, forward], [spec], [mid], flops=work)
     *back, grad_spec = call(
         functools.partial(back_kernel, order, back_order),
@@ -313,7 +306,7 @@
     share = jax.ShapeDtypeStruct((rows, length // shares), half)
     cross = call(
         cross_kernel,
-        [where, input_blocks, grad_spec, forward, backward],
+        [where, *input_parts, grad_spec, forward, backward],
         [share] * shares,
         [held, mid, wide],
         flops=2 * work,

time: 94.2 us -> 106 us (1.13)
  blocking collectives: 0 us -> 21.7 us
  waiting for transfers between devices: 41.1 us -> 34.4 us
  starting transfers between devices: 31.6 us -> 26.7 us
  local copies, waits for them, and re-layouts: 4.42 us -> 6.49 us
    all_to_all x0 -> x1, blocking collectives: none -> 21.7 us  [on_device(): lax.all_to_all(part, 'ctx', split_axis=0, concat_axis=0, tiled=True)]
    ppermute x17, waiting for transfers between devices: 41.1 us -> 34.4 us  [exchange(): lax.ppermute(piece, axis, [(i, i ^ k) for i in range(size)])]
    all_to_all x1, starting transfers between devices: 7.42 us -> 3.59 us  [on_device(): lax.all_to_all(part, 'ctx', split_axis=0, concat_axis=0, tiled=True)]
    slice x0 -> x1, local copies, waits for them, and re-layouts: none -> 2.09 us  [on_device(): whole_input[:, rows // 2:]]
  transfers between devices with their start and end apart: 18 -> 18, of which waited for: 5 -> 5; matrix products, arithmetic and copies ran while one was open for 0% -> 0% of each run, Pallas kernels for 16% -> 14%
where the time goes in v10:
time: 106 us
  waiting for transfers between devices  34.4 us (32%)
  starting transfers between devices  26.7 us (25%)
  blocking collectives  21.7 us (20%)
  Pallas kernels  15.1 us (14%)
  local copies, waits for them, and re-layouts  6.49 us (6%)
    ppermute x17, waiting for transfers between devices, exchange(): lax.ppermute(piece, axis, [(i, i ^ k) for i in range(size)])  34.4 us
    ppermute x17, starting transfers between devices, exchange(): lax.ppermute(piece, axis, [(i, i ^ k) for i in range(size)])  23.1 us
    all_to_all x1, blocking collectives, on_device(): lax.all_to_all(part, 'ctx', split_axis=0, concat_axis=0, tiled=True)  21.7 us
    pallas_call x5, Pallas kernels, call(): pl.pallas_call(kernel, out_shape=list(outs), in_specs=specs, out_specs=[p...  15.1 us
    unnamed x18, local copies, waits for them, and re-layouts  4.4 us
    all_to_all x1, starting transfers between devices, on_device(): lax.all_to_all(part, 'ctx', split_axis=0, concat_axis=0, tiled=True)  3.59 us
  transfers between devices with their start and end apart: 18, of which 5 were waited for; matrix products, arithmetic and copies ran while one was open for 0% of the time, Pallas kernels for 14%

profile of v10, /device:TPU:0, one launch (start us, length us, event | category | flops | bytes accessed | tf_op | source)
XLA Modules:
  0.0 106.1 jit_solution(14248849845240685614)
XLA Ops:
  0.6 2.1 %fusion = (bf16[8,256,128]{2,1,0:T(8,128)(2,1)}, bf16[8,256,128]{2,1,0:T(8,128)(2,1)S(1)}) fusion(bf16[8,512,128]{2,1,0:T(8,128)(2,1)} %bitcast.9), kind=kLoop, calls=%fused_computation.2 | loop fusion | bytes 2097152 | tf_op jit(solution)/shard_map/slice | solution.py:295
  2.7 0.0 copy-start
  2.7 21.7 %all_to_all.10.upper = bf16[8,256,128]{2,1,0:T(8,128)(2,1)S(1)} all-to-all(bf16[8,256,128]{2,1,0:T(8,128)(2,1)S(1)} %get-tuple-element.45), channel_id=1, replica_groups=mesh['dp'=4,'ctx'=8] {'ctx'}, dimensions={0} | all-to-all | bytes 1048576 | tf_op jit(solution)/shard_map/all_to_all | solution.py:294
  24.5 3.6 %all-to-all-start.1 = ((bf16[8,256,128]{2,1,0:T(8,128)(2,1)}), bf16[8,256,128]{2,1,0:T(8,128)(2,1)S(1)}, u32[]{:S(2)}, u32[]{:S(2)}) async-start(bf16[8,256,128]{2,1,0:T(8,128)(2,1)} %get-tuple-element.44), calls=%async_computation.1 | async-start | bytes 1048576 | tf_op jit(solution)/shard_map/all_to_all | solution.py:294
  28.0 0.0 copy-start.4
  28.0 0.1 pad_add_fusion.where
  28.1 2.3 %shard_map.77 = (bf16[512,128]{1,0:T(8,128)(2,1)S(1)}, bf16[512,128]{1,0:T(8,128)(2,1)S(1)}, bf16[512,128]{1,0:T(8,128)(2,1)S(1)}, bf16[512,128]{1,0:T(8,128)(2,...) custom-call(s32[2]{0:T(128)S(1)} %pad_add_fusion.where, ...), custom_call_target="tpu_custom_call" | custom-call | bytes 3145736 | tf_op jit(solution)/shard_map/pallas_call | solution.py:242
  30.5 3.0 %collective-permute-start = (bf16[512,128]{1,0:T(8,128)(2,1)S(1)}, bf16[512,128]{1,0:T(8,128)(2,1)S(1)}, u32[]{:S(2)}, u32[]{:S(2)}) collective-permute-start(bf16[512,128]{1,0:T(8,128)(2,1)S(1)} %get-tuple-element.23), channel_id=1, source_target_pairs={{0,4},{1,5},{2,6},{3,7},{4,0},{5,1},{6,2},{7,3},{8,12},{9,13},{10,... | collective-permute-start | bytes 393224 | tf_op jit(solution)/shard_map/ppermute | solution.py:261
  33.5 1.5 %collective-permute-start.1 = (bf16[512,128]{1,0:T(8,128)(2,1)S(1)}, bf16[512,128]{1,0:T(8,128)(2,1)S(1)}, u32[]{:S(2)}, u32[]{:S(2)}) collective-permute-start(bf16[512,128]{1,0:T(8,128)(2,1)S(1)} %get-tuple-element.24), channel_id=1, source_target_pairs={{0,5},{1,4},{2,7},{3,6},{4,1},{5,0},{6,3},{7,2},{8,13},{9,12},{10,... | collective-permute-start | bytes 393224 | tf_op jit(solution)/shard_map/ppermute | solution.py:261
  34.9 3.3 %collective-permute-start.2 = (bf16[512,128]{1,0:T(8,128)(2,1)S(1)}, bf16[512,128]{1,0:T(8,128)(2,1)S(1)}, u32[]{:S(2)}, u32[]{:S(2)}) collective-permute-start(bf16[512,128]{1,0:T(8,128)(2,1)S(1)} %get-tuple-element.25), channel_id=1, source_target_pairs={{0,6},{1,7},{2,4},{3,5},{4,2},{5,3},{6,0},{7,1},{8,14},{9,15},{10,... | collective-permute-start | bytes 393224 | tf_op jit(solution)/shard_map/ppermute | solution.py:261
  38.2 0.1 collective-permute-start.3
  38.3 1.9 %collective-permute-start.4 = (bf16[512,128]{1,0:T(8,128)(2,1)S(1)}, bf16[512,128]{1,0:T(8,128)(2,1)S(1)}, u32[]{:S(2)}, u32[]{:S(2)}) collective-permute-start(bf16[512,128]{1,0:T(8,128)(2,1)S(1)} %get-tuple-element.27), channel_id=1, source_target_pairs={{0,1},{1,0},{2,3},{3,2},{4,5},{5,4},{6,7},{7,6},{8,9},{9,8},{10,11... | collective-permute-start | bytes 393224 | tf_op jit(solution)/shard_map/ppermute | solution.py:261
  40.2 17.8 %collective-permute-done.refs_0_ = bf16[512,128]{1,0:T(8,128)(2,1)S(1)} collective-permute-done((bf16[512,128]{1,0:T(8,128)(2,1)S(1)}, bf16[512,128]{1,0:T(8,128)(2,1)S(1)}, u32[]{:S(2)}, u32[]{:S(2)}) %collective-permute-start) | collective-permute-done | bytes 131104 | tf_op jit(solution)/shard_map/ppermute | solution.py:261
  58.0 0.0 collective-permute-start.5
  58.0 3.0 %collective-permute-done.1.refs_1_ = bf16[512,128]{1,0:T(8,128)(2,1)S(1)} collective-permute-done((bf16[512,128]{1,0:T(8,128)(2,1)S(1)}, bf16[512,128]{1,0:T(8,128)(2,1)S(1)}, u32[]{:S(2)}, u32[]{:S(2)}) %collective-permute-start.1) | collective-permute-done | bytes 131104 | tf_op jit(solution)/shard_map/ppermute | solution.py:261
  61.1 0.0 copy-start.1
  61.1 0.0 collective-permute-start.6
  61.1 0.0 copy-done
  61.1 0.0 copy-done.4
  61.1 1.5 %shard_map.78.refs_8_ = bf16[9,512,256]{2,1,0:T(8,128)(2,1)S(1)} custom-call(f32[512,1024]{1,0:T(8,128)S(1)} %copy-done.4, bf16[9,256,256]{2,1,0:T(8,128)(2,1)S(1)} %copy-done), custom_call_target="tpu_custom_call" | custom-call | flops 603979776 | bytes 5636096 | tf_op jit(solution)/shard_map/pallas_call | solution.py:242
  62.6 0.0 collective-permute-done.2.refs_2_
  62.6 0.0 collective-permute-done.3.refs_3_
  62.6 0.0 collective-permute-done.4.refs_4_
  62.6 1.0 collective-permute-done.5.refs_5_
  63.5 3.4 %collective-permute-done.6.refs_6_ = bf16[512,128]{1,0:T(8,128)(2,1)S(1)} collective-permute-done((bf16[512,128]{1,0:T(8,128)(2,1)S(1)}, bf16[512,128]{1,0:T(8,128)(2,1)S(1)}, u32[]{:S(2)}, u32[]{:S(2)}) %collective-permute-start.6) | collective-permute-done | bytes 131104 | tf_op jit(solution)/shard_map/ppermute | solution.py:261
  66.9 0.0 copy-done.1
  66.9 5.0 %shard_map.79 = (bf16[512,128]{1,0:T(8,128)(2,1)}, bf16[512,128]{1,0:T(8,128)(2,1)S(1)}, bf16[512,128]{1,0:T(8,128)(2,1)S(1)}, bf16[512,128]{1,0:T(8,128)(2,1)},...) custom-call(s32[2]{0:T(128)S(1)} %pad_add_fusion.where, ...), custom_call_target="tpu_custom_call" | custom-call | flops 1207959552 | bytes 9175048 | tf_op jit(solution)/shard_map/pallas_call | solution.py:242
  71.9 0.0 copy-start.2
  71.9 1.4 %copy-done.2 = bf16[9,512,256]{2,1,0:T(8,128)(2,1)} copy-done((bf16[9,512,256]{2,1,0:T(8,128)(2,1)}, bf16[9,512,256]{2,1,0:T(8,128)(2,1)S(1)}, u32[]{:S(2)}) %copy-start.2) | copy-done | bytes 2359320
  73.3 0.0 copy-start.5
  73.3 0.7 copy-done.5
  74.0 0.0 copy-start.7
  74.0 0.6 copy-done.7
  74.6 0.9 collective-permute-start.10
  75.5 1.3 %collective-permute-start.11 = (bf16[512,128]{1,0:T(8,128)(2,1)}, bf16[512,128]{1,0:T(8,128)(2,1)}, u32[]{:S(2)}, u32[]{:S(2)}) collective-permute-start(bf16[512,128]{1,0:T(8,128)(2,1)} %get-tuple-element.35), channel_id=1, source_target_pairs={{0,1},{1,0},{2,3},{3,2},{4,5},{5,4},{6,7},{7,6},{8,9},{9,8},{10,11... | collective-permute-start | bytes 393224 | tf_op jit(solution)/shard_map/ppermute | solution.py:261
  76.8 0.9 collective-permute-start.12
  77.7 1.3 %collective-permute-start.13 = (bf16[512,128]{1,0:T(8,128)(2,1)}, bf16[512,128]{1,0:T(8,128)(2,1)}, u32[]{:S(2)}, u32[]{:S(2)}) collective-permute-start(bf16[512,128]{1,0:T(8,128)(2,1)} %get-tuple-element.37), channel_id=1, source_target_pairs={{0,3},{1,2},{2,1},{3,0},{4,7},{5,6},{6,5},{7,4},{8,11},{9,10},{10,... | collective-permute-start | bytes 393224 | tf_op jit(solution)/shard_map/ppermute | solution.py:261
  79.0 2.1 %collective-permute-start.7 = (bf16[512,128]{1,0:T(8,128)(2,1)}, bf16[512,128]{1,0:T(8,128)(2,1)}, u32[]{:S(2)}, u32[]{:S(2)}) collective-permute-start(bf16[512,128]{1,0:T(8,128)(2,1)} %get-tuple-element.31), channel_id=1, source_target_pairs={{0,4},{1,5},{2,6},{3,7},{4,0},{5,1},{6,2},{7,3},{8,12},{9,13},{10,... | collective-permute-start | bytes 393224 | tf_op jit(solution)/shard_map/ppermute | solution.py:261
  81.2 0.0 all-to-all-done.1.lower
  81.2 0.0 copy-start.3
  81.2 1.7 %copy-done.3 = bf16[9,512,256]{2,1,0:T(8,128)(2,1)S(1)} copy-done((bf16[9,512,256]{2,1,0:T(8,128)(2,1)S(1)}, bf16[9,512,256]{2,1,0:T(8,128)(2,1)}, u32[]{:S(2)}) %copy-start.3) | copy-done | bytes 2359320
  82.8 0.0 copy-start.8
  82.8 0.0 copy-start.6
  82.8 4.1 %shard_map.81 = (bf16[512,256]{1,0:T(8,128)(2,1)S(1)}, bf16[512,256]{1,0:T(8,128)(2,1)S(1)}, bf16[512,256]{1,0:T(8,128)(2,1)S(1)}, bf16[512,256]{1,0:T(8,128)(2,1)S(1)}) custom-call(s32[2]{0:T(128)S(1)} %pad_add_fusion.where, bf16[8,256,128]{2,1,0:T(8,128)(2,1)S(1)} %all_to_all.10.upper, bf16[8,256,128]{2,1,0:T(8,128)(2,1)S(1)} %all-to-all-done.1.lower, ...), custom_call_target="tpu_custom_call" | custom-call | flops 1207959552 | bytes 6815752 | tf_op jit(solution)/shard_map/pallas_call | solution.py:242
  86.9 0.0 collective-permute-done.10.refs_3_
  86.9 1.6 %collective-permute-start.14 = (bf16[512,256]{1,0:T(8,128)(2,1)S(1)}, bf16[512,256]{1,0:T(8,128)(2,1)S(1)}, u32[]{:S(2)}, u32[]{:S(2)}) collective-permute-start(bf16[512,256]{1,0:T(8,128)(2,1)S(1)} %get-tuple-element.40), channel_id=1, source_target_pairs={{0,16},{8,24},{16,0},{24,8},{1,17},{9,25},{17,1},{25,9},{2,18},{10... | collective-permute-start | bytes 786440 | tf_op jit(solution)/shard_map/ppermute | solution.py:261
  88.5 0.0 collective-permute-done.11.refs_4_
  88.5 0.0 collective-permute-start.15
  88.5 0.0 collective-permute-done.12.refs_5_
  88.5 0.6 collective-permute-start.16
  89.2 0.0 collective-permute-done.13.refs_6_
  89.2 0.0 copy-done.8
  89.2 1.5 %collective-permute-start.8 = (bf16[512,128]{1,0:T(8,128)(2,1)S(1)}, bf16[512,128]{1,0:T(8,128)(2,1)S(1)}, u32[]{:S(2)}, u32[]{:S(2)}) collective-permute-start(bf16[512,128]{1,0:T(8,128)(2,1)S(1)} %copy-done.8), channel_id=1, source_target_pairs={{0,5},{1,4},{2,7},{3,6},{4,1},{5,0},{6,3},{7,2},{8,13},{9,12},{10,... | collective-permute-start | bytes 393224 | tf_op jit(solution)/shard_map/ppermute | solution.py:261
  90.6 0.0 collective-permute-done.7.refs_0_
  90.6 0.0 copy-done.6
  90.7 3.1 %collective-permute-start.9 = (bf16[512,128]{1,0:T(8,128)(2,1)S(1)}, bf16[512,128]{1,0:T(8,128)(2,1)S(1)}, u32[]{:S(2)}, u32[]{:S(2)}) collective-permute-start(bf16[512,128]{1,0:T(8,128)(2,1)S(1)} %copy-done.6), channel_id=1, source_target_pairs={{0,6},{1,7},{2,4},{3,5},{4,2},{5,3},{6,0},{7,1},{8,14},{9,15},{10,... | collective-permute-start | bytes 393224 | tf_op jit(solution)/shard_map/ppermute | solution.py:261
  93.8 9.2 %collective-permute-done.8.refs_1_ = bf16[512,128]{1,0:T(8,128)(2,1)S(1)} collective-permute-done((bf16[512,128]{1,0:T(8,128)(2,1)S(1)}, bf16[512,128]{1,0:T(8,128)(2,1)S(1)}, u32[]{:S(2)}, u32[]{:S(2)}) %collective-permute-start.8) | collective-permute-done | bytes 131104 | tf_op jit(solution)/shard_map/ppermute | solution.py:261
  102.9 0.0 collective-permute-done.9.refs_2_
  102.9 2.2 %shard_map.80 = bf16[8,512,128]{2,1,0:T(8,128)(2,1)} custom-call(s32[2]{0:T(128)S(1)} %pad_add_fusion.where, bf16[512,128]{1,0:T(8,128)(2,1)} %collective-permute-done.7.refs_0_, bf16[512,128]{1,0:T(8,128)(2,1)S(1)} %collective-permute-done.8.refs_1_, bf16[512,128]{1,0:T(8,128)(2,1)S(1)} %collective-permute-done.9.refs_2_, ...), custom_call_target="tpu_custom_call" | custom-call | bytes 2097160 | tf_op jit(solution)/shard_map/pallas_call | solution.py:242
  105.1 0.0 collective-permute-done.14
  105.2 0.0 collective-permute-done.15
  105.2 0.0 collective-permute-done.16
  105.2 0.9 add_multiply_fusion
Async XLA Ops:
  2.7 58.3 %copy-start = (bf16[9,256,256]{2,1,0:T(8,128)(2,1)S(1)}, bf16[9,256,256]{2,1,0:T(8,128)(2,1)}, u32[]{:S(2)}) copy-start(bf16[9,256,256]{2,1,0:T(8,128)(2,1)} %constant.14.clone.forward.refs_9_) | copy-start | bytes 3538948
  24.5 56.7 %all-to-all-start.1 = ((bf16[8,256,128]{2,1,0:T(8,128)(2,1)}), bf16[8,256,128]{2,1,0:T(8,128)(2,1)S(1)}, u32[]{:S(2)}, u32[]{:S(2)}) async-start(bf16[8,256,128]{2,1,0:T(8,128)(2,1)} %get-tuple-element.44), calls=%async_computation.1 | async-start | bytes 1048576 | tf_op jit(solution)/shard_map/all_to_all | solution.py:294
  28.0 33.0 %copy-start.4 = (f32[512,1024]{1,0:T(8,128)S(1)}, f32[512,1024]{1,0:T(8,128)}, u32[]{:S(2)}) copy-start(f32[512,1024]{1,0:T(8,128)} %taps.1) | copy-start | bytes 6291460
  30.5 27.6 %collective-permute-start = (bf16[512,128]{1,0:T(8,128)(2,1)S(1)}, bf16[512,128]{1,0:T(8,128)(2,1)S(1)}, u32[]{:S(2)}, u32[]{:S(2)}) collective-permute-start(bf16[512,128]{1,0:T(8,128)(2,1)S(1)} %get-tuple-element.23), channel_id=1, source_target_pairs={{0,4},{1,5},{2,6},{3,7},{4,0},{5,1},{6,2},{7,3},{8,12},{9,13},{10,... | collective-permute-start | bytes 393224 | tf_op jit(solution)/shard_map/ppermute | solution.py:261
  33.5 27.6 %collective-permute-start.1 = (bf16[512,128]{1,0:T(8,128)(2,1)S(1)}, bf16[512,128]{1,0:T(8,128)(2,1)S(1)}, u32[]{:S(2)}, u32[]{:S(2)}) collective-permute-start(bf16[512,128]{1,0:T(8,128)(2,1)S(1)} %get-tuple-element.24), channel_id=1, source_target_pairs={{0,5},{1,4},{2,7},{3,6},{4,1},{5,0},{6,3},{7,2},{8,13},{9,12},{10,... | collective-permute-start | bytes 393224 | tf_op jit(solution)/shard_map/ppermute | solution.py:261
  34.9 27.6 %collective-permute-start.2 = (bf16[512,128]{1,0:T(8,128)(2,1)S(1)}, bf16[512,128]{1,0:T(8,128)(2,1)S(1)}, u32[]{:S(2)}, u32[]{:S(2)}) collective-permute-start(bf16[512,128]{1,0:T(8,128)(2,1)S(1)} %get-tuple-element.25), channel_id=1, source_target_pairs={{0,6},{1,7},{2,4},{3,5},{4,2},{5,3},{6,0},{7,1},{8,14},{9,15},{10,... | collective-permute-start | bytes 393224 | tf_op jit(solution)/shard_map/ppermute | solution.py:261
  38.2 24.4 %collective-permute-start.3 = (bf16[512,128]{1,0:T(8,128)(2,1)S(1)}, bf16[512,128]{1,0:T(8,128)(2,1)S(1)}, u32[]{:S(2)}, u32[]{:S(2)}) collective-permute-start(bf16[512,128]{1,0:T(8,128)(2,1)S(1)} %get-tuple-element.26), channel_id=1, source_target_pairs={{0,7},{1,6},{2,5},{3,4},{4,3},{5,2},{6,1},{7,0},{8,15},{9,14},{10,... | collective-permute-start | bytes 393224 | tf_op jit(solution)/shard_map/ppermute | solution.py:261
  38.3 24.3 %collective-permute-start.4 = (bf16[512,128]{1,0:T(8,128)(2,1)S(1)}, bf16[512,128]{1,0:T(8,128)(2,1)S(1)}, u32[]{:S(2)}, u32[]{:S(2)}) collective-permute-start(bf16[512,128]{1,0:T(8,128)(2,1)S(1)} %get-tuple-element.27), channel_id=1, source_target_pairs={{0,1},{1,0},{2,3},{3,2},{4,5},{5,4},{6,7},{7,6},{8,9},{9,8},{10,11... | collective-permute-start | bytes 393224 | tf_op jit(solution)/shard_map/ppermute | solution.py:261
  58.0 5.5 %collective-permute-start.5 = (bf16[512,128]{1,0:T(8,128)(2,1)S(1)}, bf16[512,128]{1,0:T(8,128)(2,1)S(1)}, u32[]{:S(2)}, u32[]{:S(2)}) collective-permute-start(bf16[512,128]{1,0:T(8,128)(2,1)S(1)} %get-tuple-element.28), channel_id=1, source_target_pairs={{0,2},{1,3},{2,0},{3,1},{4,6},{5,7},{6,4},{7,5},{8,10},{9,11},{10,... | collective-permute-start | bytes 393224 | tf_op jit(solution)/shard_map/ppermute | solution.py:261
  61.1 5.9 %copy-start.1 = (bf16[9,256,256]{2,1,0:T(8,128)(2,1)S(1)}, bf16[9,256,256]{2,1,0:T(8,128)(2,1)}, u32[]{:S(2)}) copy-start(bf16[9,256,256]{2,1,0:T(8,128)(2,1)} %constant.15.clone.refs_10_.backward) | copy-start | bytes 3538948
  61.1 5.9 %collective-permute-start.6 = (bf16[512,128]{1,0:T(8,128)(2,1)S(1)}, bf16[512,128]{1,0:T(8,128)(2,1)S(1)}, u32[]{:S(2)}, u32[]{:S(2)}) collective-permute-start(bf16[512,128]{1,0:T(8,128)(2,1)S(1)} %get-tuple-element.29), channel_id=1, source_target_pairs={{0,3},{1,2},{2,1},{3,0},{4,7},{5,6},{6,5},{7,4},{8,11},{9,10},{10,... | collective-permute-start | bytes 393224 | tf_op jit(solution)/shard_map/ppermute | solution.py:261
  71.9 1.4 %copy-start.2 = (bf16[9,512,256]{2,1,0:T(8,128)(2,1)}, bf16[9,512,256]{2,1,0:T(8,128)(2,1)S(1)}, u32[]{:S(2)}) copy-start(bf16[9,512,256]{2,1,0:T(8,128)(2,1)S(1)} %get-tuple-element.39.grad_spec) | copy-start | bytes 7077892
  73.3 0.7 copy-start.5
  74.0 0.6 copy-start.7
  74.6 12.3 %collective-permute-start.10 = (bf16[512,128]{1,0:T(8,128)(2,1)}, bf16[512,128]{1,0:T(8,128)(2,1)}, u32[]{:S(2)}, u32[]{:S(2)}) collective-permute-start(bf16[512,128]{1,0:T(8,128)(2,1)} %get-tuple-element.34), channel_id=1, source_target_pairs={{0,7},{1,6},{2,5},{3,4},{4,3},{5,2},{6,1},{7,0},{8,15},{9,14},{10,... | collective-permute-start | bytes 393224 | tf_op jit(solution)/shard_map/ppermute | solution.py:261
  75.5 13.0 %collective-permute-start.11 = (bf16[512,128]{1,0:T(8,128)(2,1)}, bf16[512,128]{1,0:T(8,128)(2,1)}, u32[]{:S(2)}, u32[]{:S(2)}) collective-permute-start(bf16[512,128]{1,0:T(8,128)(2,1)} %get-tuple-element.35), channel_id=1, source_target_pairs={{0,1},{1,0},{2,3},{3,2},{4,5},{5,4},{6,7},{7,6},{8,9},{9,8},{10,11... | collective-permute-start | bytes 393224 | tf_op jit(solution)/shard_map/ppermute | solution.py:261
  76.8 11.7 %collective-permute-start.12 = (bf16[512,128]{1,0:T(8,128)(2,1)}, bf16[512,128]{1,0:T(8,128)(2,1)}, u32[]{:S(2)}, u32[]{:S(2)}) collective-permute-start(bf16[512,128]{1,0:T(8,128)(2,1)} %get-tuple-element.36), channel_id=1, source_target_pairs={{0,2},{1,3},{2,0},{3,1},{4,6},{5,7},{6,4},{7,5},{8,10},{9,11},{10,... | collective-permute-start | bytes 393224 | tf_op jit(solution)/shard_map/ppermute | solution.py:261
  77.7 11.4 %collective-permute-start.13 = (bf16[512,128]{1,0:T(8,128)(2,1)}, bf16[512,128]{1,0:T(8,128)(2,1)}, u32[]{:S(2)}, u32[]{:S(2)}) collective-permute-start(bf16[512,128]{1,0:T(8,128)(2,1)} %get-tuple-element.37), channel_id=1, source_target_pairs={{0,3},{1,2},{2,1},{3,0},{4,7},{5,6},{6,5},{7,4},{8,11},{9,10},{10,... | collective-permute-start | bytes 393224 | tf_op jit(solution)/shard_map/ppermute | solution.py:261
  79.0 11.6 %collective-permute-start.7 = (bf16[512,128]{1,0:T(8,128)(2,1)}, bf16[512,128]{1,0:T(8,128)(2,1)}, u32[]{:S(2)}, u32[]{:S(2)}) collective-permute-start(bf16[512,128]{1,0:T(8,128)(2,1)} %get-tuple-element.31), channel_id=1, source_target_pairs={{0,4},{1,5},{2,6},{3,7},{4,0},{5,1},{6,2},{7,3},{8,12},{9,13},{10,... | collective-permute-start | bytes 393224 | tf_op jit(solution)/shard_map/ppermute | solution.py:261
  81.2 1.7 %copy-start.3 = (bf16[9,512,256]{2,1,0:T(8,128)(2,1)S(1)}, bf16[9,512,256]{2,1,0:T(8,128)(2,1)}, u32[]{:S(2)}) copy-start(bf16[9,512,256]{2,1,0:T(8,128)(2,1)} %copy-done.2) | copy-start | bytes 7077892
  82.8 6.3 %copy-start.8 = (bf16[512,128]{1,0:T(8,128)(2,1)S(1)}, bf16[512,128]{1,0:T(8,128)(2,1)}, u32[]{:S(2)}) copy-start(bf16[512,128]{1,0:T(8,128)(2,1)} %copy-done.7) | copy-start | bytes 393220
  82.8 7.8 %copy-start.6 = (bf16[512,128]{1,0:T(8,128)(2,1)S(1)}, bf16[512,128]{1,0:T(8,128)(2,1)}, u32[]{:S(2)}) copy-start(bf16[512,128]{1,0:T(8,128)(2,1)} %copy-done.5) | copy-start | bytes 393220
  86.9 18.2 %collective-permute-start.14 = (bf16[512,256]{1,0:T(8,128)(2,1)S(1)}, bf16[512,256]{1,0:T(8,128)(2,1)S(1)}, u32[]{:S(2)}, u32[]{:S(2)}) collective-permute-start(bf16[512,256]{1,0:T(8,128)(2,1)S(1)} %get-tuple-element.40), channel_id=1, source_target_pairs={{0,16},{8,24},{16,0},{24,8},{1,17},{9,25},{17,1},{25,9},{2,18},{10... | collective-permute-start | bytes 786440 | tf_op jit(solution)/shard_map/ppermute | solution.py:261
  88.5 16.7 %collective-permute-start.15 = (bf16[512,256]{1,0:T(8,128)(2,1)S(1)}, bf16[512,256]{1,0:T(8,128)(2,1)S(1)}, u32[]{:S(2)}, u32[]{:S(2)}) collective-permute-start(bf16[512,256]{1,0:T(8,128)(2,1)S(1)} %get-tuple-element.41), channel_id=1, source_target_pairs={{0,24},{8,16},{16,8},{24,0},{1,25},{9,17},{17,9},{25,1},{2,26},{10... | collective-permute-start | bytes 786440 | tf_op jit(solution)/shard_map/ppermute | solution.py:261
  88.5 16.6 %collective-permute-start.16 = (bf16[512,256]{1,0:T(8,128)(2,1)S(1)}, bf16[512,256]{1,0:T(8,128)(2,1)S(1)}, u32[]{:S(2)}, u32[]{:S(2)}) collective-permute-start(bf16[512,256]{1,0:T(8,128)(2,1)S(1)} %get-tuple-element.42), channel_id=1, source_target_pairs={{0,8},{8,0},{16,24},{24,16},{1,9},{9,1},{17,25},{25,17},{2,10},{10... | collective-permute-start | bytes 786440 | tf_op jit(solution)/shard_map/ppermute | solution.py:261
  89.2 13.8 %collective-permute-start.8 = (bf16[512,128]{1,0:T(8,128)(2,1)S(1)}, bf16[512,128]{1,0:T(8,128)(2,1)S(1)}, u32[]{:S(2)}, u32[]{:S(2)}) collective-permute-start(bf16[512,128]{1,0:T(8,128)(2,1)S(1)} %copy-done.8), channel_id=1, source_target_pairs={{0,5},{1,4},{2,7},{3,6},{4,1},{5,0},{6,3},{7,2},{8,13},{9,12},{10,... | collective-permute-start | bytes 393224 | tf_op jit(solution)/shard_map/ppermute | solution.py:261
  90.7 12.3 %collective-permute-start.9 = (bf16[512,128]{1,0:T(8,128)(2,1)S(1)}, bf16[512,128]{1,0:T(8,128)(2,1)S(1)}, u32[]{:S(2)}, u32[]{:S(2)}) collective-permute-start(bf16[512,128]{1,0:T(8,128)(2,1)S(1)} %copy-done.6), channel_id=1, source_target_pairs={{0,6},{1,7},{2,4},{3,5},{4,2},{5,3},{6,0},{7,1},{8,14},{9,15},{10,... | collective-permute-start | bytes 393224 | tf_op jit(solution)/shard_map/ppermute | solution.py:261

commit v11 on v8

--- a/solution.py
+++ b/solution.py
@@ -144,7 +144,7 @@
     return ref.at[pl.ds(start, rows), :]
 
 
-def gate_kernel(order, where, gate, upper, whole, *refs):
+def gate_kernel(order, input_order, where, gate, upper, whole, *refs):
     outs, picks, refs = refs[: len(order)], refs[len(order) : 2 * len(order)], refs[2 * len(order) :]
     left, right, sems, pick_sems = refs
     rows = outs[0].shape[0]
@@ -157,7 +157,7 @@
         for copy in pair:
             copy.start()
         loads.append(pair)
-    for i, k in enumerate(order):
+    for i, k in enumerate(input_order):
         moves.append(pltpu.make_async_copy(piece_at(whole, where, k, rows), picks[i], pick_sems.at[i]))
         moves[-1].start()
     for i, out in enumerate(outs):
@@ -266,15 +266,9 @@
     return [*range(size // 2, size), *range(1, size // 2), 0]
 
 
-def mixed(size):
-    far = far_first(size)
-    return [k for pair in zip(far[: size // 2], far[size // 2 :]) for k in pair]
-
-
-def back_mixed(size):
-    half = size // 2
-    pairs = [k for pair in zip(range(1, half), range(half, size)) for k in pair]
-    return [*pairs[:-2], size - 2, size - 1, half - 1, 0]
+def spread(size, order):
+    part = size // 8
+    return [k * part + i for k in order for i in range(part)] + [*range(1, part), 0]
 
 
 def exchange(pieces, order, axis, size):
@@ -289,7 +283,8 @@
     channels, span = saved_input.shape[1:]
     rows, length = long_filter.shape
     width = length // BLOCKS
-    order, back_order, late = mixed(count), back_mixed(count), 2
+    grad_order, input_order, back_order = (spread(count, o) for o in ((1, 2, 4, 5, 6, 7, 3), (4, 5, 1, 6, 2, 7, 3), (1, 2, 3, 4, 5, 6, 7)))
+    late = 2
     at = count - 1 - late
     every = range(count + 8)
     where = jnp.stack([lax.axis_index("ctx"), lax.axis_index("dp")]).astype(jnp.int32)
@@ -305,18 +300,18 @@
     work = 2 * GROUPS * rows * 4 * width * width
 
     pieces = call(
-        functools.partial(gate_kernel, order),
+        functools.partial(gate_kernel, grad_order, input_order),
         [where, *(pltpu.with_memory_space_constraint(x[0], pltpu.HBM) for x in (out_gate, grad_out, saved_input))],
         [piece] * (2 * count),
         [slots, slots, sems((2, count)), sems((count,))],
         hbm=(1, 2, 3),
     )
     grad_pieces, input_pieces = pieces[:count], pieces[count:]
-    grad_blocks = exchange(grad_pieces, order, "ctx", count)
+    grad_blocks = exchange(grad_pieces, grad_order, "ctx", count)
     (taps_spec,) = call(taps_kernel, [long_filter, forward], [spec], [mid], flops=work)
     passed = [*input_pieces[at : at + late]]
     *back, grad_spec = call(
-        functools.partial(back_kernel, order, back_order, late),
+        functools.partial(back_kernel, grad_order, back_order, late),
         [where, *grad_blocks, *passed, taps_spec, forward, backward],
         [piece] * (late + count) + [spec],
         [held, mid, wide],
@@ -326,11 +321,11 @@
         aliases={1 + count + i: i for i in range(late)},
     )
     input_pieces[at : at + late], back = back[:late], back[late:]
-    input_blocks = exchange(input_pieces, order, "ctx", count)
+    input_blocks = exchange(input_pieces, input_order, "ctx", count)
     back_blocks = exchange(back, back_order, "ctx", count)
     share = jax.ShapeDtypeStruct((rows, length // shares), half)
     cross = call(
-        functools.partial(cross_kernel, order),
+        functools.partial(cross_kernel, input_order),
         [where, *input_blocks, grad_spec, forward, backward],
         [share] * shares,
         [held, mid, wide],

time: 81.9 us -> 84.2 us (1.028)
  the two profiles are of different devices: /device:TPU:0 before, /device:TPU:9 now
where the time goes in v11:
time: 84.2 us; the launch traced here: 84 us
  starting transfers between devices  37.6 us (45%)
  waiting for transfers between devices  29 us (34%)
  Pallas kernels  14.1 us (17%)
  local copies, waits for them, and re-layouts  1.6 us (2%)
  other arithmetic  1.02 us (1%)
    ppermute x24, starting transfers between devices, exchange(): lax.ppermute(piece, axis, [(i, i ^ k) for i in range(size)])  37.6 us
    ppermute x24, waiting for transfers between devices, exchange(): lax.ppermute(piece, axis, [(i, i ^ k) for i in range(size)])  29 us
    pallas_call x5, Pallas kernels, call(): pl.pallas_call(kernel, out_shape=list(outs), in_specs=specs, out_specs=[s...  14.1 us
  transfers between devices with their start and end apart: 24, of which 6 were waited for; matrix products, arithmetic and copies ran while one was open for 0% of the time, Pallas kernels for 14%

profile of v11, /device:TPU:9, one launch (start us, length us, event | category | flops | bytes accessed | tf_op | source)
XLA Modules:
  0.0 84.0 jit_solution(9892270480584603181)
XLA Ops:
  0.6 0.0 copy-start
  0.6 0.1 pad_add_fusion.where
  0.7 2.7 %shard_map.77 = (bf16[512,128]{1,0:T(8,128)(2,1)S(1)}, bf16[512,128]{1,0:T(8,128)(2,1)S(1)}, bf16[512,128]{1,0:T(8,128)(2,1)S(1)}, bf16[512,128]{1,0:T(8,128)(2,...) custom-call(s32[2]{0:T(128)S(1)} %pad_add_fusion.where, ...), custom_call_target="tpu_custom_call" | custom-call | bytes 5242888 | tf_op jit(solution)/shard_map/pallas_call | solution.py:252
  3.4 1.3 %collective-permute-start = (bf16[512,128]{1,0:T(8,128)(2,1)S(1)}, bf16[512,128]{1,0:T(8,128)(2,1)S(1)}, u32[]{:S(2)}, u32[]{:S(2)}) collective-permute-start(bf16[512,128]{1,0:T(8,128)(2,1)S(1)} %get-tuple-element.33), channel_id=1, source_target_pairs={{0,1},{1,0},{2,3},{3,2},{4,5},{5,4},{6,7},{7,6},{8,9},{9,8},{10,11... | collective-permute-start | bytes 393224 | tf_op jit(solution)/shard_map/ppermute | solution.py:277
  4.7 0.2 collective-permute-start.1
  4.9 2.3 %collective-permute-start.2 = (bf16[512,128]{1,0:T(8,128)(2,1)S(1)}, bf16[512,128]{1,0:T(8,128)(2,1)S(1)}, u32[]{:S(2)}, u32[]{:S(2)}) collective-permute-start(bf16[512,128]{1,0:T(8,128)(2,1)S(1)} %get-tuple-element.35), channel_id=1, source_target_pairs={{0,4},{1,5},{2,6},{3,7},{4,0},{5,1},{6,2},{7,3},{8,12},{9,13},{10,... | collective-permute-start | bytes 393224 | tf_op jit(solution)/shard_map/ppermute | solution.py:277
  7.2 0.0 collective-permute-start.3
  7.2 2.4 %collective-permute-start.4 = (bf16[512,128]{1,0:T(8,128)(2,1)S(1)}, bf16[512,128]{1,0:T(8,128)(2,1)S(1)}, u32[]{:S(2)}, u32[]{:S(2)}) collective-permute-start(bf16[512,128]{1,0:T(8,128)(2,1)S(1)} %get-tuple-element.37), channel_id=1, source_target_pairs={{0,6},{1,7},{2,4},{3,5},{4,2},{5,3},{6,0},{7,1},{8,14},{9,15},{10,... | collective-permute-start | bytes 393224 | tf_op jit(solution)/shard_map/ppermute | solution.py:277
  9.6 0.0 collective-permute-done.refs_0_
  9.6 1.0 %collective-permute-start.5 = (bf16[512,128]{1,0:T(8,128)(2,1)S(1)}, bf16[512,128]{1,0:T(8,128)(2,1)S(1)}, u32[]{:S(2)}, u32[]{:S(2)}) collective-permute-start(bf16[512,128]{1,0:T(8,128)(2,1)S(1)} %get-tuple-element.38), channel_id=1, source_target_pairs={{0,7},{1,6},{2,5},{3,4},{4,3},{5,2},{6,1},{7,0},{8,15},{9,14},{10,... | collective-permute-start | bytes 393224 | tf_op jit(solution)/shard_map/ppermute | solution.py:277
  10.6 0.0 collective-permute-done.1.refs_1_
  10.6 2.1 %collective-permute-start.6 = (bf16[512,128]{1,0:T(8,128)(2,1)S(1)}, bf16[512,128]{1,0:T(8,128)(2,1)S(1)}, u32[]{:S(2)}, u32[]{:S(2)}) collective-permute-start(bf16[512,128]{1,0:T(8,128)(2,1)S(1)} %get-tuple-element.39), channel_id=1, source_target_pairs={{0,3},{1,2},{2,1},{3,0},{4,7},{5,6},{6,5},{7,4},{8,11},{9,10},{10,... | collective-permute-start | bytes 393224 | tf_op jit(solution)/shard_map/ppermute | solution.py:277
  12.7 0.0 collective-permute-done.2.refs_2_
  12.7 1.1 %collective-permute-start.14 = (bf16[512,128]{1,0:T(8,128)(2,1)S(1)}, bf16[512,128]{1,0:T(8,128)(2,1)S(1)}, u32[]{:S(2)}, u32[]{:S(2)}) collective-permute-start(bf16[512,128]{1,0:T(8,128)(2,1)S(1)} %get-tuple-element.51), channel_id=1, source_target_pairs={{0,4},{1,5},{2,6},{3,7},{4,0},{5,1},{6,2},{7,3},{8,12},{9,13},{10,... | collective-permute-start | bytes 393224 | tf_op jit(solution)/shard_map/ppermute | solution.py:277
  13.8 10.2 %collective-permute-done.3.refs_3_ = bf16[512,128]{1,0:T(8,128)(2,1)S(1)} collective-permute-done((bf16[512,128]{1,0:T(8,128)(2,1)S(1)}, bf16[512,128]{1,0:T(8,128)(2,1)S(1)}, u32[]{:S(2)}, u32[]{:S(2)}) %collective-permute-start.3) | collective-permute-done | bytes 131104 | tf_op jit(solution)/shard_map/ppermute | solution.py:277
  24.0 0.0 copy-start.1
  24.0 4.5 %collective-permute-start.15 = (bf16[512,128]{1,0:T(8,128)(2,1)S(1)}, bf16[512,128]{1,0:T(8,128)(2,1)S(1)}, u32[]{:S(2)}, u32[]{:S(2)}) collective-permute-start(bf16[512,128]{1,0:T(8,128)(2,1)S(1)} %get-tuple-element.52), channel_id=1, source_target_pairs={{0,5},{1,4},{2,7},{3,6},{4,1},{5,0},{6,3},{7,2},{8,13},{9,12},{10,... | collective-permute-start | bytes 393224 | tf_op jit(solution)/shard_map/ppermute | solution.py:277
  28.5 0.0 copy-done
  28.5 0.0 copy-start.2
  28.5 1.6 %copy-done.2 = f32[512,1024]{1,0:T(8,128)S(1)} copy-done((f32[512,1024]{1,0:T(8,128)S(1)}, f32[512,1024]{1,0:T(8,128)}, u32[]{:S(2)}) %copy-start.2) | copy-done | bytes 2097176
  30.1 1.5 %shard_map.78.refs_10_ = bf16[9,512,256]{2,1,0:T(8,128)(2,1)S(1)} custom-call(f32[512,1024]{1,0:T(8,128)S(1)} %copy-done.2, bf16[9,256,256]{2,1,0:T(8,128)(2,1)S(1)} %copy-done), custom_call_target="tpu_custom_call" | custom-call | flops 603979776 | bytes 5636096 | tf_op jit(solution)/shard_map/pallas_call | solution.py:252
  31.6 0.1 collective-permute-done.4.refs_4_
  31.7 0.3 collective-permute-start.16
  32.0 3.9 %collective-permute-done.5.refs_5_ = bf16[512,128]{1,0:T(8,128)(2,1)S(1)} collective-permute-done((bf16[512,128]{1,0:T(8,128)(2,1)S(1)}, bf16[512,128]{1,0:T(8,128)(2,1)S(1)}, u32[]{:S(2)}, u32[]{:S(2)}) %collective-permute-start.5) | collective-permute-done | bytes 131104 | tf_op jit(solution)/shard_map/ppermute | solution.py:277
  35.9 2.1 %collective-permute-start.17 = (bf16[512,128]{1,0:T(8,128)(2,1)S(1)}, bf16[512,128]{1,0:T(8,128)(2,1)S(1)}, u32[]{:S(2)}, u32[]{:S(2)}) collective-permute-start(bf16[512,128]{1,0:T(8,128)(2,1)S(1)} %get-tuple-element.54), channel_id=1, source_target_pairs={{0,6},{1,7},{2,4},{3,5},{4,2},{5,3},{6,0},{7,1},{8,14},{9,15},{10,... | collective-permute-start | bytes 393224 | tf_op jit(solution)/shard_map/ppermute | solution.py:277
  38.0 0.0 collective-permute-done.6.refs_6_
  38.1 0.0 collective-permute-start.18
  38.1 0.0 copy-done.1
  38.1 4.3 %shard_map.79 = (bf16[512,128]{1,0:T(8,128)(2,1)S(1)}, bf16[512,128]{1,0:T(8,128)(2,1)S(1)}, bf16[512,128]{1,0:T(8,128)(2,1)S(1)}, bf16[512,128]{1,0:T(8,128)(2,...) custom-call(s32[2]{0:T(128)S(1)} %pad_add_fusion.where, ...), custom_call_target="tpu_custom_call", output_to_operand_aliasing={{0}: (9, {}), {1}: (10, {})} | custom-call | flops 1207959552 | bytes 9699336 | tf_op jit(solution)/shard_map/pallas_call | solution.py:252
  42.3 0.0 collective-permute-done.14.refs_0_
  42.3 1.4 %collective-permute-start.19 = (bf16[512,128]{1,0:T(8,128)(2,1)S(1)}, bf16[512,128]{1,0:T(8,128)(2,1)S(1)}, u32[]{:S(2)}, u32[]{:S(2)}) collective-permute-start(bf16[512,128]{1,0:T(8,128)(2,1)S(1)} %get-tuple-element.56), channel_id=1, source_target_pairs={{0,7},{1,6},{2,5},{3,4},{4,3},{5,2},{6,1},{7,0},{8,15},{9,14},{10,... | collective-permute-start | bytes 393224 | tf_op jit(solution)/shard_map/ppermute | solution.py:277
  43.7 0.0 collective-permute-done.15.refs_1_
  43.8 2.4 %collective-permute-start.20 = (bf16[512,128]{1,0:T(8,128)(2,1)S(1)}, bf16[512,128]{1,0:T(8,128)(2,1)S(1)}, u32[]{:S(2)}, u32[]{:S(2)}) collective-permute-start(bf16[512,128]{1,0:T(8,128)(2,1)S(1)} %get-tuple-element.57), channel_id=1, source_target_pairs={{0,3},{1,2},{2,1},{3,0},{4,7},{5,6},{6,5},{7,4},{8,11},{9,10},{10,... | collective-permute-start | bytes 393224 | tf_op jit(solution)/shard_map/ppermute | solution.py:277
  46.2 0.0 collective-permute-done.16.refs_2_
  46.2 1.1 %collective-permute-start.7 = (bf16[512,128]{1,0:T(8,128)(2,1)S(1)}, bf16[512,128]{1,0:T(8,128)(2,1)S(1)}, u32[]{:S(2)}, u32[]{:S(2)}) collective-permute-start(bf16[512,128]{1,0:T(8,128)(2,1)S(1)} %get-tuple-element.43), channel_id=1, source_target_pairs={{0,1},{1,0},{2,3},{3,2},{4,5},{5,4},{6,7},{7,6},{8,9},{9,8},{10,11... | collective-permute-start | bytes 393224 | tf_op jit(solution)/shard_map/ppermute | solution.py:277
  47.3 0.0 collective-permute-done.17.refs_3_
  47.3 0.0 collective-permute-start.8
  47.3 0.0 collective-permute-done.18.refs_4_
  47.3 1.7 %collective-permute-start.9 = (bf16[512,128]{1,0:T(8,128)(2,1)S(1)}, bf16[512,128]{1,0:T(8,128)(2,1)S(1)}, u32[]{:S(2)}, u32[]{:S(2)}) collective-permute-start(bf16[512,128]{1,0:T(8,128)(2,1)S(1)} %get-tuple-element.45), channel_id=1, source_target_pairs={{0,3},{1,2},{2,1},{3,0},{4,7},{5,6},{6,5},{7,4},{8,11},{9,10},{10,... | collective-permute-start | bytes 393224 | tf_op jit(solution)/shard_map/ppermute | solution.py:277
  49.0 2.7 %collective-permute-done.19.refs_5_ = bf16[512,128]{1,0:T(8,128)(2,1)S(1)} collective-permute-done((bf16[512,128]{1,0:T(8,128)(2,1)S(1)}, bf16[512,128]{1,0:T(8,128)(2,1)S(1)}, u32[]{:S(2)}, u32[]{:S(2)}) %collective-permute-start.19) | collective-permute-done | bytes 131104 | tf_op jit(solution)/shard_map/ppermute | solution.py:277
  51.7 0.0 collective-permute-start.10
  51.8 0.0 collective-permute-done.20.refs_6_
  51.8 2.6 %collective-permute-start.11 = (bf16[512,128]{1,0:T(8,128)(2,1)S(1)}, bf16[512,128]{1,0:T(8,128)(2,1)S(1)}, u32[]{:S(2)}, u32[]{:S(2)}) collective-permute-start(bf16[512,128]{1,0:T(8,128)(2,1)S(1)} %get-tuple-element.47), channel_id=1, source_target_pairs={{0,5},{1,4},{2,7},{3,6},{4,1},{5,0},{6,3},{7,2},{8,13},{9,12},{10,... | collective-permute-start | bytes 393224 | tf_op jit(solution)/shard_map/ppermute | solution.py:277
  54.4 4.1 %shard_map.81 = (bf16[512,256]{1,0:T(8,128)(2,1)S(1)}, bf16[512,256]{1,0:T(8,128)(2,1)S(1)}, bf16[512,256]{1,0:T(8,128)(2,1)S(1)}, bf16[512,256]{1,0:T(8,128)(2,1)S(1)}) custom-call(s32[2]{0:T(128)S(1)} %pad_add_fusion.where, bf16[512,128]{1,0:T(8,128)(2,1)S(1)} %collective-permute-done.14.refs_0_, bf16[512,128]{1,0:T(8,128)(2,1)S(1)} %collective-permute-done.15.refs_1_, ...), custom_call_target="tpu_custom_call" | custom-call | flops 1207959552 | bytes 6815752 | tf_op jit(solution)/shard_map/pallas_call | solution.py:252
  58.5 0.0 collective-permute-done.7.refs_0_
  58.5 1.3 %collective-permute-start.21 = (bf16[512,256]{1,0:T(8,128)(2,1)S(1)}, bf16[512,256]{1,0:T(8,128)(2,1)S(1)}, u32[]{:S(2)}, u32[]{:S(2)}) collective-permute-start(bf16[512,256]{1,0:T(8,128)(2,1)S(1)} %get-tuple-element.60), channel_id=1, source_target_pairs={{0,16},{8,24},{16,0},{24,8},{1,17},{9,25},{17,1},{25,9},{2,18},{10... | collective-permute-start | bytes 786440 | tf_op jit(solution)/shard_map/ppermute | solution.py:277
  59.8 0.0 collective-permute-done.8.refs_1_
  59.8 8.4 %collective-permute-start.22 = (bf16[512,256]{1,0:T(8,128)(2,1)S(1)}, bf16[512,256]{1,0:T(8,128)(2,1)S(1)}, u32[]{:S(2)}, u32[]{:S(2)}) collective-permute-start(bf16[512,256]{1,0:T(8,128)(2,1)S(1)} %get-tuple-element.61), channel_id=1, source_target_pairs={{0,24},{8,16},{16,8},{24,0},{1,25},{9,17},{17,9},{25,1},{2,26},{10... | collective-permute-start | bytes 786440 | tf_op jit(solution)/shard_map/ppermute | solution.py:277
  68.2 0.0 collective-permute-done.9.refs_2_
  68.2 0.0 collective-permute-start.23
  68.2 0.0 collective-permute-done.10.refs_3_
  68.2 0.1 collective-permute-start.12
  68.3 0.0 collective-permute-done.11.refs_4_
  68.3 1.2 %collective-permute-start.13 = (bf16[512,128]{1,0:T(8,128)(2,1)S(1)}, bf16[512,128]{1,0:T(8,128)(2,1)S(1)}, u32[]{:S(2)}, u32[]{:S(2)}) collective-permute-start(bf16[512,128]{1,0:T(8,128)(2,1)S(1)} %get-tuple-element.49), channel_id=1, source_target_pairs={{0,7},{1,6},{2,5},{3,4},{4,3},{5,2},{6,1},{7,0},{8,15},{9,14},{10,... | collective-permute-start | bytes 393224 | tf_op jit(solution)/shard_map/ppermute | solution.py:277
  69.5 9.1 %collective-permute-done.12.refs_5_ = bf16[512,128]{1,0:T(8,128)(2,1)S(1)} collective-permute-done((bf16[512,128]{1,0:T(8,128)(2,1)S(1)}, bf16[512,128]{1,0:T(8,128)(2,1)S(1)}, u32[]{:S(2)}, u32[]{:S(2)}) %collective-permute-start.12) | collective-permute-done | bytes 131104 | tf_op jit(solution)/shard_map/ppermute | solution.py:277
  78.6 2.9 %collective-permute-done.13.refs_6_ = bf16[512,128]{1,0:T(8,128)(2,1)S(1)} collective-permute-done((bf16[512,128]{1,0:T(8,128)(2,1)S(1)}, bf16[512,128]{1,0:T(8,128)(2,1)S(1)}, u32[]{:S(2)}, u32[]{:S(2)}) %collective-permute-start.13) | collective-permute-done | bytes 131104 | tf_op jit(solution)/shard_map/ppermute | solution.py:277
  81.5 1.6 %shard_map.80 = bf16[8,512,128]{2,1,0:T(8,128)(2,1)} custom-call(s32[2]{0:T(128)S(1)} %pad_add_fusion.where, bf16[512,128]{1,0:T(8,128)(2,1)S(1)} %collective-permute-done.7.refs_0_, bf16[512,128]{1,0:T(8,128)(2,1)S(1)} %collective-permute-done.8.refs_1_, bf16[512,128]{1,0:T(8,128)(2,1)S(1)} %collective-permute-done.9.refs_2_, ...), custom_call_target="tpu_custom_call" | custom-call | bytes 2097160 | tf_op jit(solution)/shard_map/pallas_call | solution.py:252
  83.1 0.0 collective-permute-done.21
  83.1 0.0 collective-permute-done.22
  83.1 0.0 collective-permute-done.23
  83.1 0.9 %add_multiply_fusion = f32[512,256]{1,0:T(8,128)} fusion(bf16[512,256]{1,0:T(8,128)(2,1)S(1)} %get-tuple-element.63, bf16[512,256]{1,0:T(8,128)(2,1)S(1)} %collective-permute-done.23, bf16[512,256]{1,0:T(8,128)(2,1)S(1)} %collective-permute-done.22, bf16[512,256]{1,0:T(8,128)(2,1)S(1)} %collective-permute-done.21), kind=kLoop, calls=%fused_computation | loop fusion | flops 1048576 | bytes 1572864 | tf_op jit(solution)/shard_map/mul | solution.py:336
Async XLA Ops:
  0.6 27.9 %copy-start = (bf16[9,256,256]{2,1,0:T(8,128)(2,1)S(1)}, bf16[9,256,256]{2,1,0:T(8,128)(2,1)}, u32[]{:S(2)}) copy-start(bf16[9,256,256]{2,1,0:T(8,128)(2,1)} %constant.14.clone.forward.refs_11_.refs_9_) | copy-start | bytes 3538948
  3.4 6.2 %collective-permute-start = (bf16[512,128]{1,0:T(8,128)(2,1)S(1)}, bf16[512,128]{1,0:T(8,128)(2,1)S(1)}, u32[]{:S(2)}, u32[]{:S(2)}) collective-permute-start(bf16[512,128]{1,0:T(8,128)(2,1)S(1)} %get-tuple-element.33), channel_id=1, source_target_pairs={{0,1},{1,0},{2,3},{3,2},{4,5},{5,4},{6,7},{7,6},{8,9},{9,8},{10,11... | collective-permute-start | bytes 393224 | tf_op jit(solution)/shard_map/ppermute | solution.py:277
  4.7 5.9 %collective-permute-start.1 = (bf16[512,128]{1,0:T(8,128)(2,1)S(1)}, bf16[512,128]{1,0:T(8,128)(2,1)S(1)}, u32[]{:S(2)}, u32[]{:S(2)}) collective-permute-start(bf16[512,128]{1,0:T(8,128)(2,1)S(1)} %get-tuple-element.34), channel_id=1, source_target_pairs={{0,2},{1,3},{2,0},{3,1},{4,6},{5,7},{6,4},{7,5},{8,10},{9,11},{10,... | collective-permute-start | bytes 393224 | tf_op jit(solution)/shard_map/ppermute | solution.py:277
  4.9 7.8 %collective-permute-start.2 = (bf16[512,128]{1,0:T(8,128)(2,1)S(1)}, bf16[512,128]{1,0:T(8,128)(2,1)S(1)}, u32[]{:S(2)}, u32[]{:S(2)}) collective-permute-start(bf16[512,128]{1,0:T(8,128)(2,1)S(1)} %get-tuple-element.35), channel_id=1, source_target_pairs={{0,4},{1,5},{2,6},{3,7},{4,0},{5,1},{6,2},{7,3},{8,12},{9,13},{10,... | collective-permute-start | bytes 393224 | tf_op jit(solution)/shard_map/ppermute | solution.py:277
  7.2 16.8 %collective-permute-start.3 = (bf16[512,128]{1,0:T(8,128)(2,1)S(1)}, bf16[512,128]{1,0:T(8,128)(2,1)S(1)}, u32[]{:S(2)}, u32[]{:S(2)}) collective-permute-start(bf16[512,128]{1,0:T(8,128)(2,1)S(1)} %get-tuple-element.36), channel_id=1, source_target_pairs={{0,5},{1,4},{2,7},{3,6},{4,1},{5,0},{6,3},{7,2},{8,13},{9,12},{10,... | collective-permute-start | bytes 393224 | tf_op jit(solution)/shard_map/ppermute | solution.py:277
  7.2 24.5 %collective-permute-start.4 = (bf16[512,128]{1,0:T(8,128)(2,1)S(1)}, bf16[512,128]{1,0:T(8,128)(2,1)S(1)}, u32[]{:S(2)}, u32[]{:S(2)}) collective-permute-start(bf16[512,128]{1,0:T(8,128)(2,1)S(1)} %get-tuple-element.37), channel_id=1, source_target_pairs={{0,6},{1,7},{2,4},{3,5},{4,2},{5,3},{6,0},{7,1},{8,14},{9,15},{10,... | collective-permute-start | bytes 393224 | tf_op jit(solution)/shard_map/ppermute | solution.py:277
  9.6 26.3 %collective-permute-start.5 = (bf16[512,128]{1,0:T(8,128)(2,1)S(1)}, bf16[512,128]{1,0:T(8,128)(2,1)S(1)}, u32[]{:S(2)}, u32[]{:S(2)}) collective-permute-start(bf16[512,128]{1,0:T(8,128)(2,1)S(1)} %get-tuple-element.38), channel_id=1, source_target_pairs={{0,7},{1,6},{2,5},{3,4},{4,3},{5,2},{6,1},{7,0},{8,15},{9,14},{10,... | collective-permute-start | bytes 393224 | tf_op jit(solution)/shard_map/ppermute | solution.py:277
  10.6 27.5 %collective-permute-start.6 = (bf16[512,128]{1,0:T(8,128)(2,1)S(1)}, bf16[512,128]{1,0:T(8,128)(2,1)S(1)}, u32[]{:S(2)}, u32[]{:S(2)}) collective-permute-start(bf16[512,128]{1,0:T(8,128)(2,1)S(1)} %get-tuple-element.39), channel_id=1, source_target_pairs={{0,3},{1,2},{2,1},{3,0},{4,7},{5,6},{6,5},{7,4},{8,11},{9,10},{10,... | collective-permute-start | bytes 393224 | tf_op jit(solution)/shard_map/ppermute | solution.py:277
  12.7 29.7 %collective-permute-start.14 = (bf16[512,128]{1,0:T(8,128)(2,1)S(1)}, bf16[512,128]{1,0:T(8,128)(2,1)S(1)}, u32[]{:S(2)}, u32[]{:S(2)}) collective-permute-start(bf16[512,128]{1,0:T(8,128)(2,1)S(1)} %get-tuple-element.51), channel_id=1, source_target_pairs={{0,4},{1,5},{2,6},{3,7},{4,0},{5,1},{6,2},{7,3},{8,12},{9,13},{10,... | collective-permute-start | bytes 393224 | tf_op jit(solution)/shard_map/ppermute | solution.py:277
  24.0 14.0 %copy-start.1 = (bf16[9,256,256]{2,1,0:T(8,128)(2,1)S(1)}, bf16[9,256,256]{2,1,0:T(8,128)(2,1)}, u32[]{:S(2)}) copy-start(bf16[9,256,256]{2,1,0:T(8,128)(2,1)} %constant.15.clone.refs_12_.refs_10_) | copy-start | bytes 3538948
  24.0 19.7 %collective-permute-start.15 = (bf16[512,128]{1,0:T(8,128)(2,1)S(1)}, bf16[512,128]{1,0:T(8,128)(2,1)S(1)}, u32[]{:S(2)}, u32[]{:S(2)}) collective-permute-start(bf16[512,128]{1,0:T(8,128)(2,1)S(1)} %get-tuple-element.52), channel_id=1, source_target_pairs={{0,5},{1,4},{2,7},{3,6},{4,1},{5,0},{6,3},{7,2},{8,13},{9,12},{10,... | collective-permute-start | bytes 393224 | tf_op jit(solution)/shard_map/ppermute | solution.py:277
  28.5 1.6 %copy-start.2 = (f32[512,1024]{1,0:T(8,128)S(1)}, f32[512,1024]{1,0:T(8,128)}, u32[]{:S(2)}) copy-start(f32[512,1024]{1,0:T(8,128)} %taps.1) | copy-start | bytes 6291460
  31.7 14.5 %collective-permute-start.16 = (bf16[512,128]{1,0:T(8,128)(2,1)S(1)}, bf16[512,128]{1,0:T(8,128)(2,1)S(1)}, u32[]{:S(2)}, u32[]{:S(2)}) collective-permute-start(bf16[512,128]{1,0:T(8,128)(2,1)S(1)} %get-tuple-element.53), channel_id=1, source_target_pairs={{0,1},{1,0},{2,3},{3,2},{4,5},{5,4},{6,7},{7,6},{8,9},{9,8},{10,11... | collective-permute-start | bytes 393224 | tf_op jit(solution)/shard_map/ppermute | solution.py:277
  35.9 11.4 %collective-permute-start.17 = (bf16[512,128]{1,0:T(8,128)(2,1)S(1)}, bf16[512,128]{1,0:T(8,128)(2,1)S(1)}, u32[]{:S(2)}, u32[]{:S(2)}) collective-permute-start(bf16[512,128]{1,0:T(8,128)(2,1)S(1)} %get-tuple-element.54), channel_id=1, source_target_pairs={{0,6},{1,7},{2,4},{3,5},{4,2},{5,3},{6,0},{7,1},{8,14},{9,15},{10,... | collective-permute-start | bytes 393224 | tf_op jit(solution)/shard_map/ppermute | solution.py:277
  38.1 9.2 %collective-permute-start.18 = (bf16[512,128]{1,0:T(8,128)(2,1)S(1)}, bf16[512,128]{1,0:T(8,128)(2,1)S(1)}, u32[]{:S(2)}, u32[]{:S(2)}) collective-permute-start(bf16[512,128]{1,0:T(8,128)(2,1)S(1)} %get-tuple-element.55), channel_id=1, source_target_pairs={{0,2},{1,3},{2,0},{3,1},{4,6},{5,7},{6,4},{7,5},{8,10},{9,11},{10,... | collective-permute-start | bytes 393224 | tf_op jit(solution)/shard_map/ppermute | solution.py:277
  42.3 9.4 %collective-permute-start.19 = (bf16[512,128]{1,0:T(8,128)(2,1)S(1)}, bf16[512,128]{1,0:T(8,128)(2,1)S(1)}, u32[]{:S(2)}, u32[]{:S(2)}) collective-permute-start(bf16[512,128]{1,0:T(8,128)(2,1)S(1)} %get-tuple-element.56), channel_id=1, source_target_pairs={{0,7},{1,6},{2,5},{3,4},{4,3},{5,2},{6,1},{7,0},{8,15},{9,14},{10,... | collective-permute-start | bytes 393224 | tf_op jit(solution)/shard_map/ppermute | solution.py:277
  43.8 8.0 %collective-permute-start.20 = (bf16[512,128]{1,0:T(8,128)(2,1)S(1)}, bf16[512,128]{1,0:T(8,128)(2,1)S(1)}, u32[]{:S(2)}, u32[]{:S(2)}) collective-permute-start(bf16[512,128]{1,0:T(8,128)(2,1)S(1)} %get-tuple-element.57), channel_id=1, source_target_pairs={{0,3},{1,2},{2,1},{3,0},{4,7},{5,6},{6,5},{7,4},{8,11},{9,10},{10,... | collective-permute-start | bytes 393224 | tf_op jit(solution)/shard_map/ppermute | solution.py:277
  46.2 12.3 %collective-permute-start.7 = (bf16[512,128]{1,0:T(8,128)(2,1)S(1)}, bf16[512,128]{1,0:T(8,128)(2,1)S(1)}, u32[]{:S(2)}, u32[]{:S(2)}) collective-permute-start(bf16[512,128]{1,0:T(8,128)(2,1)S(1)} %get-tuple-element.43), channel_id=1, source_target_pairs={{0,1},{1,0},{2,3},{3,2},{4,5},{5,4},{6,7},{7,6},{8,9},{9,8},{10,11... | collective-permute-start | bytes 393224 | tf_op jit(solution)/shard_map/ppermute | solution.py:277
  47.3 12.5 %collective-permute-start.8 = (bf16[512,128]{1,0:T(8,128)(2,1)S(1)}, bf16[512,128]{1,0:T(8,128)(2,1)S(1)}, u32[]{:S(2)}, u32[]{:S(2)}) collective-permute-start(bf16[512,128]{1,0:T(8,128)(2,1)S(1)} %get-tuple-element.44), channel_id=1, source_target_pairs={{0,2},{1,3},{2,0},{3,1},{4,6},{5,7},{6,4},{7,5},{8,10},{9,11},{10,... | collective-permute-start | bytes 393224 | tf_op jit(solution)/shard_map/ppermute | solution.py:277
  47.3 20.9 %collective-permute-start.9 = (bf16[512,128]{1,0:T(8,128)(2,1)S(1)}, bf16[512,128]{1,0:T(8,128)(2,1)S(1)}, u32[]{:S(2)}, u32[]{:S(2)}) collective-permute-start(bf16[512,128]{1,0:T(8,128)(2,1)S(1)} %get-tuple-element.45), channel_id=1, source_target_pairs={{0,3},{1,2},{2,1},{3,0},{4,7},{5,6},{6,5},{7,4},{8,11},{9,10},{10,... | collective-permute-start | bytes 393224 | tf_op jit(solution)/shard_map/ppermute | solution.py:277
  51.7 16.4 %collective-permute-start.10 = (bf16[512,128]{1,0:T(8,128)(2,1)S(1)}, bf16[512,128]{1,0:T(8,128)(2,1)S(1)}, u32[]{:S(2)}, u32[]{:S(2)}) collective-permute-start(bf16[512,128]{1,0:T(8,128)(2,1)S(1)} %get-tuple-element.46), channel_id=1, source_target_pairs={{0,4},{1,5},{2,6},{3,7},{4,0},{5,1},{6,2},{7,3},{8,12},{9,13},{10,... | collective-permute-start | bytes 393224 | tf_op jit(solution)/shard_map/ppermute | solution.py:277
  51.8 16.5 %collective-permute-start.11 = (bf16[512,128]{1,0:T(8,128)(2,1)S(1)}, bf16[512,128]{1,0:T(8,128)(2,1)S(1)}, u32[]{:S(2)}, u32[]{:S(2)}) collective-permute-start(bf16[512,128]{1,0:T(8,128)(2,1)S(1)} %get-tuple-element.47), channel_id=1, source_target_pairs={{0,5},{1,4},{2,7},{3,6},{4,1},{5,0},{6,3},{7,2},{8,13},{9,12},{10,... | collective-permute-start | bytes 393224 | tf_op jit(solution)/shard_map/ppermute | solution.py:277
  58.5 24.6 %collective-permute-start.21 = (bf16[512,256]{1,0:T(8,128)(2,1)S(1)}, bf16[512,256]{1,0:T(8,128)(2,1)S(1)}, u32[]{:S(2)}, u32[]{:S(2)}) collective-permute-start(bf16[512,256]{1,0:T(8,128)(2,1)S(1)} %get-tuple-element.60), channel_id=1, source_target_pairs={{0,16},{8,24},{16,0},{24,8},{1,17},{9,25},{17,1},{25,9},{2,18},{10... | collective-permute-start | bytes 786440 | tf_op jit(solution)/shard_map/ppermute | solution.py:277
  59.8 23.3 %collective-permute-start.22 = (bf16[512,256]{1,0:T(8,128)(2,1)S(1)}, bf16[512,256]{1,0:T(8,128)(2,1)S(1)}, u32[]{:S(2)}, u32[]{:S(2)}) collective-permute-start(bf16[512,256]{1,0:T(8,128)(2,1)S(1)} %get-tuple-element.61), channel_id=1, source_target_pairs={{0,24},{8,16},{16,8},{24,0},{1,25},{9,17},{17,9},{25,1},{2,26},{10... | collective-permute-start | bytes 786440 | tf_op jit(solution)/shard_map/ppermute | solution.py:277
  68.2 14.9 %collective-permute-start.23 = (bf16[512,256]{1,0:T(8,128)(2,1)S(1)}, bf16[512,256]{1,0:T(8,128)(2,1)S(1)}, u32[]{:S(2)}, u32[]{:S(2)}) collective-permute-start(bf16[512,256]{1,0:T(8,128)(2,1)S(1)} %get-tuple-element.62), channel_id=1, source_target_pairs={{0,8},{8,0},{16,24},{24,16},{1,9},{9,1},{17,25},{25,17},{2,10},{10... | collective-permute-start | bytes 786440 | tf_op jit(solution)/shard_map/ppermute | solution.py:277
  68.2 10.4 %collective-permute-start.12 = (bf16[512,128]{1,0:T(8,128)(2,1)S(1)}, bf16[512,128]{1,0:T(8,128)(2,1)S(1)}, u32[]{:S(2)}, u32[]{:S(2)}) collective-permute-start(bf16[512,128]{1,0:T(8,128)(2,1)S(1)} %get-tuple-element.48), channel_id=1, source_target_pairs={{0,6},{1,7},{2,4},{3,5},{4,2},{5,3},{6,0},{7,1},{8,14},{9,15},{10,... | collective-permute-start | bytes 393224 | tf_op jit(solution)/shard_map/ppermute | solution.py:277
  68.3 13.2 %collective-permute-start.13 = (bf16[512,128]{1,0:T(8,128)(2,1)S(1)}, bf16[512,128]{1,0:T(8,128)(2,1)S(1)}, u32[]{:S(2)}, u32[]{:S(2)}) collective-permute-start(bf16[512,128]{1,0:T(8,128)(2,1)S(1)} %get-tuple-element.49), channel_id=1, source_target_pairs={{0,7},{1,6},{2,5},{3,4},{4,3},{5,2},{6,1},{7,0},{8,15},{9,14},{10,... | collective-permute-start | bytes 393224 | tf_op jit(solution)/shard_map/ppermute | solution.py:277

commit v12 on v11

--- a/solution.py
+++ b/solution.py
@@ -182,10 +182,11 @@
 
 
 def ordered(order, where, refs, held):
-    span = refs[0].shape[1]
+    span = refs[0].shape[-1]
     for k, ref in zip(order, refs):
-        start = pl.multiple_of(lax.bitwise_xor(where[0], k) * span, span)
-        held[:, pl.ds(start, span)] = ref[...]
+        other = lax.bitwise_xor(where[0], k)
+        block = ref[...] if len(ref.shape) == 2 else ref[(other > where[0]).astype(jnp.int32)]
+        held[:, pl.ds(pl.multiple_of(other * span, span), span)] = block
 
 
 def block_of(held, width):
@@ -199,10 +200,9 @@
     return store
 
 
-def back_kernel(order, back_order, late, where, *refs):
-    blocks, refs = refs[: len(order)], refs[len(order) + late :]
+def back_kernel(order, back_order, where, *refs):
+    blocks, refs = refs[: len(order)], refs[len(order) :]
     taps_spec, forward, backward, *outs, grad_spec, held, mid, wide = refs
-    outs = outs[late:]
     rows, width = held.shape[0], held.shape[1] // BLOCKS
     ordered(order, where, blocks, held)
     split_rows(block_of(held, width), mid, rows, width)
@@ -278,14 +278,20 @@
     return moved
 
 
+def gather_pairs(pieces, order, axis, size):
+    moved = []
+    for k, piece in zip(order, pieces):
+        pairs = [(i, i ^ k) for i in range(size) if i < i ^ k]
+        moved.append(lax.all_gather(piece, axis, axis_index_groups=pairs, axis=0, tiled=False) if k else piece)
+    return moved
+
+
 def on_device(saved_input, out_gate, grad_out, long_filter):
     count, shares = lax.axis_size("ctx"), lax.axis_size("dp")
     channels, span = saved_input.shape[1:]
     rows, length = long_filter.shape
     width = length // BLOCKS
-    grad_order, input_order, back_order = (spread(count, o) for o in ((1, 2, 4, 5, 6, 7, 3), (4, 5, 1, 6, 2, 7, 3), (1, 2, 3, 4, 5, 6, 7)))
-    late = 2
-    at = count - 1 - late
+    grad_order, input_order, back_order = (spread(count, o) for o in ((4, 5, 6, 7, 1, 2, 3), (4, 5, 6, 7, 1, 2, 3), (6, 7, 3, 1, 2, 4, 5)))
     every = range(count + 8)
     where = jnp.stack([lax.axis_index("ctx"), lax.axis_index("dp")]).astype(jnp.int32)
     forward, backward = (jnp.asarray(t) for t in transform_tables(width))
@@ -309,19 +315,14 @@
     grad_pieces, input_pieces = pieces[:count], pieces[count:]
     grad_blocks = exchange(grad_pieces, grad_order, "ctx", count)
     (taps_spec,) = call(taps_kernel, [long_filter, forward], [spec], [mid], flops=work)
-    passed = [*input_pieces[at : at + late]]
     *back, grad_spec = call(
-        functools.partial(back_kernel, grad_order, back_order, late),
-        [where, *grad_blocks, *passed, taps_spec, forward, backward],
-        [piece] * (late + count) + [spec],
+        functools.partial(back_kernel, grad_order, back_order),
+        [where, *grad_blocks, taps_spec, forward, backward],
+        [piece] * count + [spec],
         [held, mid, wide],
         flops=2 * work,
-        streams=range(1 + count, 1 + count + late),
-        out_streams=range(late),
-        aliases={1 + count + i: i for i in range(late)},
-    )
-    input_pieces[at : at + late], back = back[:late], back[late:]
-    input_blocks = exchange(input_pieces, input_order, "ctx", count)
+    )
+    input_blocks = gather_pairs(input_pieces, input_order, "ctx", count)
     back_blocks = exchange(back, back_order, "ctx", count)
     share = jax.ShapeDtypeStruct((rows, length // shares), half)
     cross = call(

time: 84.2 us -> 113 us (1.34)
  the two profiles are of different devices: /device:TPU:9 before, /device:TPU:0 now
where the time goes in v12:
time: 113 us
  blocking collectives  56.7 us (50%)
  starting transfers between devices  31.2 us (28%)
  Pallas kernels  14.4 us (13%)
  waiting for transfers between devices  8.69 us (8%)
    all_gather x7, blocking collectives, gather_pairs(): lax.all_gather(piece, axis, axis_index_groups=pairs, axis=0, tiled=False)  56.7 us
    ppermute x17, starting transfers between devices, exchange(): lax.ppermute(piece, axis, [(i, i ^ k) for i in range(size)])  31.2 us
    pallas_call x5, Pallas kernels, call(): pl.pallas_call(kernel, out_shape=list(outs), in_specs=specs, out_specs=[s...  14.4 us
    ppermute x17, waiting for transfers between devices, exchange(): lax.ppermute(piece, axis, [(i, i ^ k) for i in range(size)])  8.69 us
  transfers between devices with their start and end apart: 17, of which 2 were waited for; matrix products, arithmetic and copies ran while one was open for 0% of the time, Pallas kernels for 6%

profile of v12, /device:TPU:0, one launch (start us, length us, event | category | flops | bytes accessed | tf_op | source)
XLA Modules:
  0.0 112.8 jit_solution(8463924724056751816)
XLA Ops:
  0.6 0.0 copy-start
  0.6 0.0 copy-start.2
  0.7 0.1 pad_add_fusion.where
  0.7 3.0 %shard_map.77 = (bf16[512,128]{1,0:T(8,128)(2,1)S(1)}, bf16[512,128]{1,0:T(8,128)(2,1)S(1)}, bf16[512,128]{1,0:T(8,128)(2,1)S(1)}, bf16[512,128]{1,0:T(8,128)(2,...) custom-call(s32[2]{0:T(128)S(1)} %pad_add_fusion.where, ...), custom_call_target="tpu_custom_call" | custom-call | bytes 5242888 | tf_op jit(solution)/shard_map/pallas_call | solution.py:252
  3.7 4.1 %collective-permute-start = (bf16[512,128]{1,0:T(8,128)(2,1)S(1)}, bf16[512,128]{1,0:T(8,128)(2,1)S(1)}, u32[]{:S(2)}, u32[]{:S(2)}) collective-permute-start(bf16[512,128]{1,0:T(8,128)(2,1)S(1)} %get-tuple-element.31), channel_id=1, source_target_pairs={{0,4},{1,5},{2,6},{3,7},{4,0},{5,1},{6,2},{7,3},{8,12},{9,13},{10,... | collective-permute-start | bytes 393224 | tf_op jit(solution)/shard_map/ppermute | solution.py:277
  7.8 1.3 %collective-permute-start.1 = (bf16[512,128]{1,0:T(8,128)(2,1)S(1)}, bf16[512,128]{1,0:T(8,128)(2,1)S(1)}, u32[]{:S(2)}, u32[]{:S(2)}) collective-permute-start(bf16[512,128]{1,0:T(8,128)(2,1)S(1)} %get-tuple-element.32), channel_id=1, source_target_pairs={{0,5},{1,4},{2,7},{3,6},{4,1},{5,0},{6,3},{7,2},{8,13},{9,12},{10,... | collective-permute-start | bytes 393224 | tf_op jit(solution)/shard_map/ppermute | solution.py:277
  9.1 3.6 %collective-permute-start.2 = (bf16[512,128]{1,0:T(8,128)(2,1)S(1)}, bf16[512,128]{1,0:T(8,128)(2,1)S(1)}, u32[]{:S(2)}, u32[]{:S(2)}) collective-permute-start(bf16[512,128]{1,0:T(8,128)(2,1)S(1)} %get-tuple-element.33), channel_id=1, source_target_pairs={{0,6},{1,7},{2,4},{3,5},{4,2},{5,3},{6,0},{7,1},{8,14},{9,15},{10,... | collective-permute-start | bytes 393224 | tf_op jit(solution)/shard_map/ppermute | solution.py:277
  12.7 0.0 collective-permute-start.3
  12.7 1.7 %collective-permute-start.4 = (bf16[512,128]{1,0:T(8,128)(2,1)S(1)}, bf16[512,128]{1,0:T(8,128)(2,1)S(1)}, u32[]{:S(2)}, u32[]{:S(2)}) collective-permute-start(bf16[512,128]{1,0:T(8,128)(2,1)S(1)} %get-tuple-element.35), channel_id=1, source_target_pairs={{0,1},{1,0},{2,3},{3,2},{4,5},{5,4},{6,7},{7,6},{8,9},{9,8},{10,11... | collective-permute-start | bytes 393224 | tf_op jit(solution)/shard_map/ppermute | solution.py:277
  14.4 9.4 %all-gather.4 = bf16[1024,128]{1,0:T(8,128)(2,1)S(1)} all-gather(bf16[512,128]{1,0:T(8,128)(2,1)S(1)} %get-tuple-element.51), channel_id=6, replica_groups={{0,1},{2,3},{4,5},{6,7},{8,9},{10,11},{12,13},{14,15},{16,17},{18,19},{..., dimensions={0}, use_global_device_ids=true | all-gather | bytes 393216 | tf_op jit(solution)/shard_map/all_gather | solution.py:285
  23.8 5.6 %all-gather.5 = bf16[1024,128]{1,0:T(8,128)(2,1)S(1)} all-gather(bf16[512,128]{1,0:T(8,128)(2,1)S(1)} %get-tuple-element.52), channel_id=7, replica_groups={{0,2},{1,3},{4,6},{5,7},{8,10},{9,11},{12,14},{13,15},{16,18},{17,19},{..., dimensions={0}, use_global_device_ids=true | all-gather | bytes 393216 | tf_op jit(solution)/shard_map/all_gather | solution.py:285
  29.5 0.0 copy-done
  29.5 0.0 copy-done.2
  29.5 1.5 %shard_map.78.refs_8_ = bf16[9,512,256]{2,1,0:T(8,128)(2,1)S(1)} custom-call(f32[512,1024]{1,0:T(8,128)S(1)} %copy-done.2, bf16[9,256,256]{2,1,0:T(8,128)(2,1)S(1)} %copy-done), custom_call_target="tpu_custom_call" | custom-call | flops 603979776 | bytes 5636096 | tf_op jit(solution)/shard_map/pallas_call | solution.py:252
  30.9 0.0 copy-start.1
  31.0 6.7 %all-gather.6 = bf16[1024,128]{1,0:T(8,128)(2,1)S(1)} all-gather(bf16[512,128]{1,0:T(8,128)(2,1)S(1)} %get-tuple-element.53), channel_id=8, replica_groups={{0,3},{1,2},{4,7},{5,6},{8,11},{9,10},{12,15},{13,14},{16,19},{17,18},{..., dimensions={0}, use_global_device_ids=true | all-gather | bytes 393216 | tf_op jit(solution)/shard_map/all_gather | solution.py:285
  37.6 8.5 %all-gather = bf16[1024,128]{1,0:T(8,128)(2,1)S(1)} all-gather(bf16[512,128]{1,0:T(8,128)(2,1)S(1)} %get-tuple-element.47), channel_id=2, replica_groups={{0,4},{1,5},{2,6},{3,7},{8,12},{9,13},{10,14},{11,15},{16,20},{17,21},{..., dimensions={0}, use_global_device_ids=true | all-gather | bytes 393216 | tf_op jit(solution)/shard_map/all_gather | solution.py:285
  46.2 0.0 collective-permute-done.refs_0_
  46.2 0.0 collective-permute-start.5
  46.2 0.0 collective-permute-done.1.refs_1_
  46.2 6.2 %collective-permute-start.6 = (bf16[512,128]{1,0:T(8,128)(2,1)S(1)}, bf16[512,128]{1,0:T(8,128)(2,1)S(1)}, u32[]{:S(2)}, u32[]{:S(2)}) collective-permute-start(bf16[512,128]{1,0:T(8,128)(2,1)S(1)} %get-tuple-element.37), channel_id=1, source_target_pairs={{0,3},{1,2},{2,1},{3,0},{4,7},{5,6},{6,5},{7,4},{8,11},{9,10},{10,... | collective-permute-start | bytes 393224 | tf_op jit(solution)/shard_map/ppermute | solution.py:277
  52.3 7.4 %all-gather.1 = bf16[1024,128]{1,0:T(8,128)(2,1)S(1)} all-gather(bf16[512,128]{1,0:T(8,128)(2,1)S(1)} %get-tuple-element.48), channel_id=3, replica_groups={{0,5},{1,4},{2,7},{3,6},{8,13},{9,12},{10,15},{11,14},{16,21},{17,20},{..., dimensions={0}, use_global_device_ids=true | all-gather | bytes 393216 | tf_op jit(solution)/shard_map/all_gather | solution.py:285
  59.8 10.6 %all-gather.2 = bf16[1024,128]{1,0:T(8,128)(2,1)S(1)} all-gather(bf16[512,128]{1,0:T(8,128)(2,1)S(1)} %get-tuple-element.49), channel_id=4, replica_groups={{0,6},{1,7},{2,4},{3,5},{8,14},{9,15},{10,12},{11,13},{16,22},{17,23},{..., dimensions={0}, use_global_device_ids=true | all-gather | bytes 393216 | tf_op jit(solution)/shard_map/all_gather | solution.py:285
  70.4 0.0 collective-permute-done.2.refs_2_
  70.4 0.0 collective-permute-done.3.refs_3_
  70.4 0.0 collective-permute-done.4.refs_4_
  70.4 0.0 collective-permute-done.5.refs_5_
  70.4 0.0 collective-permute-done.6.refs_6_
  70.4 0.0 copy-done.1
  70.4 4.3 %shard_map.79 = (bf16[512,128]{1,0:T(8,128)(2,1)S(1)}, bf16[512,128]{1,0:T(8,128)(2,1)S(1)}, bf16[512,128]{1,0:T(8,128)(2,1)S(1)}, bf16[512,128]{1,0:T(8,128)(2,...) custom-call(s32[2]{0:T(128)S(1)} %pad_add_fusion.where, ...), custom_call_target="tpu_custom_call" | custom-call | flops 1207959552 | bytes 9175048 | tf_op jit(solution)/shard_map/pallas_call | solution.py:252
  74.7 0.1 collective-permute-start.10
  74.8 0.3 collective-permute-start.11
  75.1 4.2 %collective-permute-start.12 = (bf16[512,128]{1,0:T(8,128)(2,1)S(1)}, bf16[512,128]{1,0:T(8,128)(2,1)S(1)}, u32[]{:S(2)}, u32[]{:S(2)}) collective-permute-start(bf16[512,128]{1,0:T(8,128)(2,1)S(1)} %get-tuple-element.44), channel_id=1, source_target_pairs={{0,4},{1,5},{2,6},{3,7},{4,0},{5,1},{6,2},{7,3},{8,12},{9,13},{10,... | collective-permute-start | bytes 393224 | tf_op jit(solution)/shard_map/ppermute | solution.py:277
  79.3 8.4 %all-gather.3 = bf16[1024,128]{1,0:T(8,128)(2,1)S(1)} all-gather(bf16[512,128]{1,0:T(8,128)(2,1)S(1)} %get-tuple-element.50), channel_id=5, replica_groups={{0,7},{1,6},{2,5},{3,4},{8,15},{9,14},{10,13},{11,12},{16,23},{17,22},{..., dimensions={0}, use_global_device_ids=true | all-gather | bytes 393216 | tf_op jit(solution)/shard_map/all_gather | solution.py:285
  87.8 3.1 %collective-permute-start.13 = (bf16[512,128]{1,0:T(8,128)(2,1)S(1)}, bf16[512,128]{1,0:T(8,128)(2,1)S(1)}, u32[]{:S(2)}, u32[]{:S(2)}) collective-permute-start(bf16[512,128]{1,0:T(8,128)(2,1)S(1)} %get-tuple-element.45), channel_id=1, source_target_pairs={{0,5},{1,4},{2,7},{3,6},{4,1},{5,0},{6,3},{7,2},{8,13},{9,12},{10,... | collective-permute-start | bytes 393224 | tf_op jit(solution)/shard_map/ppermute | solution.py:277
  90.8 2.0 %collective-permute-start.7 = (bf16[512,128]{1,0:T(8,128)(2,1)S(1)}, bf16[512,128]{1,0:T(8,128)(2,1)S(1)}, u32[]{:S(2)}, u32[]{:S(2)}) collective-permute-start(bf16[512,128]{1,0:T(8,128)(2,1)S(1)} %get-tuple-element.39), channel_id=1, source_target_pairs={{0,6},{1,7},{2,4},{3,5},{4,2},{5,3},{6,0},{7,1},{8,14},{9,15},{10,... | collective-permute-start | bytes 393224 | tf_op jit(solution)/shard_map/ppermute | solution.py:277
  92.8 4.1 %shard_map.81 = (bf16[512,256]{1,0:T(8,128)(2,1)S(1)}, bf16[512,256]{1,0:T(8,128)(2,1)S(1)}, bf16[512,256]{1,0:T(8,128)(2,1)S(1)}, bf16[512,256]{1,0:T(8,128)(2,1)S(1)}) custom-call(s32[2]{0:T(128)S(1)} %pad_add_fusion.where, bf16[2,512,128]{2,1,0:T(8,128)(2,1)S(1)} %bitcast.16, bf16[2,512,128]{2,1,0:T(8,128)(2,1)S(1)} %bitcast.17, ...), custom_call_target="tpu_custom_call" | custom-call | flops 1207959552 | bytes 7733256 | tf_op jit(solution)/shard_map/pallas_call | solution.py:252
  97.0 0.0 collective-permute-done.10.refs_3_
  97.0 1.6 %collective-permute-start.14 = (bf16[512,256]{1,0:T(8,128)(2,1)S(1)}, bf16[512,256]{1,0:T(8,128)(2,1)S(1)}, u32[]{:S(2)}, u32[]{:S(2)}) collective-permute-start(bf16[512,256]{1,0:T(8,128)(2,1)S(1)} %get-tuple-element.56), channel_id=1, source_target_pairs={{0,16},{8,24},{16,0},{24,8},{1,17},{9,25},{17,1},{25,9},{2,18},{10... | collective-permute-start | bytes 786440 | tf_op jit(solution)/shard_map/ppermute | solution.py:277
  98.5 0.0 collective-permute-done.11.refs_4_
  98.5 0.0 collective-permute-start.15
  98.5 0.0 collective-permute-done.12.refs_5_
  98.5 0.6 collective-permute-start.16
  99.2 0.0 collective-permute-done.13.refs_6_
  99.2 2.4 %collective-permute-start.8 = (bf16[512,128]{1,0:T(8,128)(2,1)S(1)}, bf16[512,128]{1,0:T(8,128)(2,1)S(1)}, u32[]{:S(2)}, u32[]{:S(2)}) collective-permute-start(bf16[512,128]{1,0:T(8,128)(2,1)S(1)} %get-tuple-element.40), channel_id=1, source_target_pairs={{0,7},{1,6},{2,5},{3,4},{4,3},{5,2},{6,1},{7,0},{8,15},{9,14},{10,... | collective-permute-start | bytes 393224 | tf_op jit(solution)/shard_map/ppermute | solution.py:277
  101.6 0.0 collective-permute-done.7.refs_0_
  101.6 0.0 collective-permute-start.9
  101.6 6.7 %collective-permute-done.8.refs_1_ = bf16[512,128]{1,0:T(8,128)(2,1)S(1)} collective-permute-done((bf16[512,128]{1,0:T(8,128)(2,1)S(1)}, bf16[512,128]{1,0:T(8,128)(2,1)S(1)}, u32[]{:S(2)}, u32[]{:S(2)}) %collective-permute-start.8) | collective-permute-done | bytes 131104 | tf_op jit(solution)/shard_map/ppermute | solution.py:277
  108.3 2.0 %collective-permute-done.9.refs_2_ = bf16[512,128]{1,0:T(8,128)(2,1)S(1)} collective-permute-done((bf16[512,128]{1,0:T(8,128)(2,1)S(1)}, bf16[512,128]{1,0:T(8,128)(2,1)S(1)}, u32[]{:S(2)}, u32[]{:S(2)}) %collective-permute-start.9) | collective-permute-done | bytes 131104 | tf_op jit(solution)/shard_map/ppermute | solution.py:277
  110.3 1.6 %shard_map.80 = bf16[8,512,128]{2,1,0:T(8,128)(2,1)} custom-call(s32[2]{0:T(128)S(1)} %pad_add_fusion.where, bf16[512,128]{1,0:T(8,128)(2,1)S(1)} %collective-permute-done.7.refs_0_, bf16[512,128]{1,0:T(8,128)(2,1)S(1)} %collective-permute-done.8.refs_1_, bf16[512,128]{1,0:T(8,128)(2,1)S(1)} %collective-permute-done.9.refs_2_, ...), custom_call_target="tpu_custom_call" | custom-call | bytes 2097160 | tf_op jit(solution)/shard_map/pallas_call | solution.py:252
  111.8 0.0 collective-permute-done.14
  111.8 0.0 collective-permute-done.15
  111.8 0.0 collective-permute-done.16
  111.9 0.9 add_multiply_fusion
Async XLA Ops:
  0.6 28.8 %copy-start = (bf16[9,256,256]{2,1,0:T(8,128)(2,1)S(1)}, bf16[9,256,256]{2,1,0:T(8,128)(2,1)}, u32[]{:S(2)}) copy-start(bf16[9,256,256]{2,1,0:T(8,128)(2,1)} %constant.14.clone.forward.refs_9_) | copy-start | bytes 3538948
  0.6 28.8 %copy-start.2 = (f32[512,1024]{1,0:T(8,128)S(1)}, f32[512,1024]{1,0:T(8,128)}, u32[]{:S(2)}) copy-start(f32[512,1024]{1,0:T(8,128)} %taps.1) | copy-start | bytes 6291460
  3.7 42.4 %collective-permute-start = (bf16[512,128]{1,0:T(8,128)(2,1)S(1)}, bf16[512,128]{1,0:T(8,128)(2,1)S(1)}, u32[]{:S(2)}, u32[]{:S(2)}) collective-permute-start(bf16[512,128]{1,0:T(8,128)(2,1)S(1)} %get-tuple-element.31), channel_id=1, source_target_pairs={{0,4},{1,5},{2,6},{3,7},{4,0},{5,1},{6,2},{7,3},{8,12},{9,13},{10,... | collective-permute-start | bytes 393224 | tf_op jit(solution)/shard_map/ppermute | solution.py:277
  7.8 38.4 %collective-permute-start.1 = (bf16[512,128]{1,0:T(8,128)(2,1)S(1)}, bf16[512,128]{1,0:T(8,128)(2,1)S(1)}, u32[]{:S(2)}, u32[]{:S(2)}) collective-permute-start(bf16[512,128]{1,0:T(8,128)(2,1)S(1)} %get-tuple-element.32), channel_id=1, source_target_pairs={{0,5},{1,4},{2,7},{3,6},{4,1},{5,0},{6,3},{7,2},{8,13},{9,12},{10,... | collective-permute-start | bytes 393224 | tf_op jit(solution)/shard_map/ppermute | solution.py:277
  9.1 61.3 %collective-permute-start.2 = (bf16[512,128]{1,0:T(8,128)(2,1)S(1)}, bf16[512,128]{1,0:T(8,128)(2,1)S(1)}, u32[]{:S(2)}, u32[]{:S(2)}) collective-permute-start(bf16[512,128]{1,0:T(8,128)(2,1)S(1)} %get-tuple-element.33), channel_id=1, source_target_pairs={{0,6},{1,7},{2,4},{3,5},{4,2},{5,3},{6,0},{7,1},{8,14},{9,15},{10,... | collective-permute-start | bytes 393224 | tf_op jit(solution)/shard_map/ppermute | solution.py:277
  12.7 57.7 %collective-permute-start.3 = (bf16[512,128]{1,0:T(8,128)(2,1)S(1)}, bf16[512,128]{1,0:T(8,128)(2,1)S(1)}, u32[]{:S(2)}, u32[]{:S(2)}) collective-permute-start(bf16[512,128]{1,0:T(8,128)(2,1)S(1)} %get-tuple-element.34), channel_id=1, source_target_pairs={{0,7},{1,6},{2,5},{3,4},{4,3},{5,2},{6,1},{7,0},{8,15},{9,14},{10,... | collective-permute-start | bytes 393224 | tf_op jit(solution)/shard_map/ppermute | solution.py:277
  12.7 57.7 %collective-permute-start.4 = (bf16[512,128]{1,0:T(8,128)(2,1)S(1)}, bf16[512,128]{1,0:T(8,128)(2,1)S(1)}, u32[]{:S(2)}, u32[]{:S(2)}) collective-permute-start(bf16[512,128]{1,0:T(8,128)(2,1)S(1)} %get-tuple-element.35), channel_id=1, source_target_pairs={{0,1},{1,0},{2,3},{3,2},{4,5},{5,4},{6,7},{7,6},{8,9},{9,8},{10,11... | collective-permute-start | bytes 393224 | tf_op jit(solution)/shard_map/ppermute | solution.py:277
  30.9 39.5 %copy-start.1 = (bf16[9,256,256]{2,1,0:T(8,128)(2,1)S(1)}, bf16[9,256,256]{2,1,0:T(8,128)(2,1)}, u32[]{:S(2)}) copy-start(bf16[9,256,256]{2,1,0:T(8,128)(2,1)} %constant.15.clone.refs_10_) | copy-start | bytes 3538948
  46.2 24.2 %collective-permute-start.5 = (bf16[512,128]{1,0:T(8,128)(2,1)S(1)}, bf16[512,128]{1,0:T(8,128)(2,1)S(1)}, u32[]{:S(2)}, u32[]{:S(2)}) collective-permute-start(bf16[512,128]{1,0:T(8,128)(2,1)S(1)} %get-tuple-element.36), channel_id=1, source_target_pairs={{0,2},{1,3},{2,0},{3,1},{4,6},{5,7},{6,4},{7,5},{8,10},{9,11},{10,... | collective-permute-start | bytes 393224 | tf_op jit(solution)/shard_map/ppermute | solution.py:277
  46.2 24.2 %collective-permute-start.6 = (bf16[512,128]{1,0:T(8,128)(2,1)S(1)}, bf16[512,128]{1,0:T(8,128)(2,1)S(1)}, u32[]{:S(2)}, u32[]{:S(2)}) collective-permute-start(bf16[512,128]{1,0:T(8,128)(2,1)S(1)} %get-tuple-element.37), channel_id=1, source_target_pairs={{0,3},{1,2},{2,1},{3,0},{4,7},{5,6},{6,5},{7,4},{8,11},{9,10},{10,... | collective-permute-start | bytes 393224 | tf_op jit(solution)/shard_map/ppermute | solution.py:277
  74.7 22.3 %collective-permute-start.10 = (bf16[512,128]{1,0:T(8,128)(2,1)S(1)}, bf16[512,128]{1,0:T(8,128)(2,1)S(1)}, u32[]{:S(2)}, u32[]{:S(2)}) collective-permute-start(bf16[512,128]{1,0:T(8,128)(2,1)S(1)} %get-tuple-element.42), channel_id=1, source_target_pairs={{0,1},{1,0},{2,3},{3,2},{4,5},{5,4},{6,7},{7,6},{8,9},{9,8},{10,11... | collective-permute-start | bytes 393224 | tf_op jit(solution)/shard_map/ppermute | solution.py:277
  74.8 23.7 %collective-permute-start.11 = (bf16[512,128]{1,0:T(8,128)(2,1)S(1)}, bf16[512,128]{1,0:T(8,128)(2,1)S(1)}, u32[]{:S(2)}, u32[]{:S(2)}) collective-permute-start(bf16[512,128]{1,0:T(8,128)(2,1)S(1)} %get-tuple-element.43), channel_id=1, source_target_pairs={{0,2},{1,3},{2,0},{3,1},{4,6},{5,7},{6,4},{7,5},{8,10},{9,11},{10,... | collective-permute-start | bytes 393224 | tf_op jit(solution)/shard_map/ppermute | solution.py:277
  75.1 23.4 %collective-permute-start.12 = (bf16[512,128]{1,0:T(8,128)(2,1)S(1)}, bf16[512,128]{1,0:T(8,128)(2,1)S(1)}, u32[]{:S(2)}, u32[]{:S(2)}) collective-permute-start(bf16[512,128]{1,0:T(8,128)(2,1)S(1)} %get-tuple-element.44), channel_id=1, source_target_pairs={{0,4},{1,5},{2,6},{3,7},{4,0},{5,1},{6,2},{7,3},{8,12},{9,13},{10,... | collective-permute-start | bytes 393224 | tf_op jit(solution)/shard_map/ppermute | solution.py:277
  87.8 11.4 %collective-permute-start.13 = (bf16[512,128]{1,0:T(8,128)(2,1)S(1)}, bf16[512,128]{1,0:T(8,128)(2,1)S(1)}, u32[]{:S(2)}, u32[]{:S(2)}) collective-permute-start(bf16[512,128]{1,0:T(8,128)(2,1)S(1)} %get-tuple-element.45), channel_id=1, source_target_pairs={{0,5},{1,4},{2,7},{3,6},{4,1},{5,0},{6,3},{7,2},{8,13},{9,12},{10,... | collective-permute-start | bytes 393224 | tf_op jit(solution)/shard_map/ppermute | solution.py:277
  90.8 10.8 %collective-permute-start.7 = (bf16[512,128]{1,0:T(8,128)(2,1)S(1)}, bf16[512,128]{1,0:T(8,128)(2,1)S(1)}, u32[]{:S(2)}, u32[]{:S(2)}) collective-permute-start(bf16[512,128]{1,0:T(8,128)(2,1)S(1)} %get-tuple-element.39), channel_id=1, source_target_pairs={{0,6},{1,7},{2,4},{3,5},{4,2},{5,3},{6,0},{7,1},{8,14},{9,15},{10,... | collective-permute-start | bytes 393224 | tf_op jit(solution)/shard_map/ppermute | solution.py:277
  97.0 14.9 %collective-permute-start.14 = (bf16[512,256]{1,0:T(8,128)(2,1)S(1)}, bf16[512,256]{1,0:T(8,128)(2,1)S(1)}, u32[]{:S(2)}, u32[]{:S(2)}) collective-permute-start(bf16[512,256]{1,0:T(8,128)(2,1)S(1)} %get-tuple-element.56), channel_id=1, source_target_pairs={{0,16},{8,24},{16,0},{24,8},{1,17},{9,25},{17,1},{25,9},{2,18},{10... | collective-permute-start | bytes 786440 | tf_op jit(solution)/shard_map/ppermute | solution.py:277
  98.5 13.3 %collective-permute-start.15 = (bf16[512,256]{1,0:T(8,128)(2,1)S(1)}, bf16[512,256]{1,0:T(8,128)(2,1)S(1)}, u32[]{:S(2)}, u32[]{:S(2)}) collective-permute-start(bf16[512,256]{1,0:T(8,128)(2,1)S(1)} %get-tuple-element.57), channel_id=1, source_target_pairs={{0,24},{8,16},{16,8},{24,0},{1,25},{9,17},{17,9},{25,1},{2,26},{10... | collective-permute-start | bytes 786440 | tf_op jit(solution)/shard_map/ppermute | solution.py:277
  98.5 13.3 %collective-permute-start.16 = (bf16[512,256]{1,0:T(8,128)(2,1)S(1)}, bf16[512,256]{1,0:T(8,128)(2,1)S(1)}, u32[]{:S(2)}, u32[]{:S(2)}) collective-permute-start(bf16[512,256]{1,0:T(8,128)(2,1)S(1)} %get-tuple-element.58), channel_id=1, source_target_pairs={{0,8},{8,0},{16,24},{24,16},{1,9},{9,1},{17,25},{25,17},{2,10},{10... | collective-permute-start | bytes 786440 | tf_op jit(solution)/shard_map/ppermute | solution.py:277
  99.2 9.1 %collective-permute-start.8 = (bf16[512,128]{1,0:T(8,128)(2,1)S(1)}, bf16[512,128]{1,0:T(8,128)(2,1)S(1)}, u32[]{:S(2)}, u32[]{:S(2)}) collective-permute-start(bf16[512,128]{1,0:T(8,128)(2,1)S(1)} %get-tuple-element.40), channel_id=1, source_target_pairs={{0,7},{1,6},{2,5},{3,4},{4,3},{5,2},{6,1},{7,0},{8,15},{9,14},{10,... | collective-permute-start | bytes 393224 | tf_op jit(solution)/shard_map/ppermute | solution.py:277
  101.6 8.7 %collective-permute-start.9 = (bf16[512,128]{1,0:T(8,128)(2,1)S(1)}, bf16[512,128]{1,0:T(8,128)(2,1)S(1)}, u32[]{:S(2)}, u32[]{:S(2)}) collective-permute-start(bf16[512,128]{1,0:T(8,128)(2,1)S(1)} %get-tuple-element.41), channel_id=1, source_target_pairs={{0,3},{1,2},{2,1},{3,0},{4,7},{5,6},{6,5},{7,4},{8,11},{9,10},{10,... | collective-permute-start | bytes 393224 | tf_op jit(solution)/shard_map/ppermute | solution.py:277

commit v13 on v12

--- a/solution.py
+++ b/solution.py
@@ -144,10 +144,10 @@
     return ref.at[pl.ds(start, rows), :]
 
 
-def gate_kernel(order, input_order, where, gate, upper, whole, *refs):
-    outs, picks, refs = refs[: len(order)], refs[len(order) : 2 * len(order)], refs[2 * len(order) :]
+def gate_kernel(order, alone, where, gate, upper, whole, *refs):
+    outs, picks, refs = refs[: len(order)], refs[len(order) : -4], refs[-4:]
     left, right, sems, pick_sems = refs
-    rows = outs[0].shape[0]
+    rows = left.shape[1]
     loads, moves = [], []
     for i, k in enumerate(order):
         pair = (
@@ -157,13 +157,18 @@
         for copy in pair:
             copy.start()
         loads.append(pair)
-    for i, k in enumerate(input_order):
-        moves.append(pltpu.make_async_copy(piece_at(whole, where, k, rows), picks[i], pick_sems.at[i]))
+    for i, k in enumerate(order):
+        target = picks[alone.index(k)] if k in alone else outs[i].at[1]
+        moves.append(pltpu.make_async_copy(piece_at(whole, where, k, rows), target, pick_sems.at[i]))
         moves[-1].start()
-    for i, out in enumerate(outs):
+    for i, k in enumerate(order):
         for copy in loads[i]:
             copy.wait()
-        out[...] = (left[i].astype(jnp.float32) * right[i].astype(jnp.float32)).astype(jnp.bfloat16)
+        product = (left[i].astype(jnp.float32) * right[i].astype(jnp.float32)).astype(jnp.bfloat16)
+        if k in alone:
+            outs[i][...] = product
+        else:
+            outs[i][0] = product
     for copy in moves:
         copy.wait()
 
@@ -181,12 +186,11 @@
         taps_spec[r] = spectrum(mid, forward, r, width).astype(taps_spec.dtype)
 
 
-def ordered(order, where, refs, held):
+def ordered(order, part, where, refs, held):
     span = refs[0].shape[-1]
     for k, ref in zip(order, refs):
-        other = lax.bitwise_xor(where[0], k)
-        block = ref[...] if len(ref.shape) == 2 else ref[(other > where[0]).astype(jnp.int32)]
-        held[:, pl.ds(pl.multiple_of(other * span, span), span)] = block
+        start = pl.multiple_of(lax.bitwise_xor(where[0], k) * span, span)
+        held[:, pl.ds(start, span)] = ref[...] if len(ref.shape) == 2 else ref[part]
 
 
 def block_of(held, width):
@@ -204,7 +208,7 @@
     blocks, refs = refs[: len(order)], refs[len(order) :]
     taps_spec, forward, backward, *outs, grad_spec, held, mid, wide = refs
     rows, width = held.shape[0], held.shape[1] // BLOCKS
-    ordered(order, where, blocks, held)
+    ordered(order, 0, where, blocks, held)
     split_rows(block_of(held, width), mid, rows, width)
     for r in range(GROUPS):
         grad = spectrum(mid, forward, r, width)
@@ -224,7 +228,7 @@
     blocks, refs = refs[: len(order)], refs[len(order) :]
     grad_spec, forward, backward, *outs, held, mid, wide = refs
     rows, width = held.shape[0], held.shape[1] // BLOCKS
-    ordered(order, where, blocks, held)
+    ordered(order, 1, where, blocks, held)
     split_rows(block_of(held, width), mid, rows, width)
     for r in range(GROUPS):
         signal = spectrum(mid, forward, r, width)
@@ -239,23 +243,17 @@
         out[...] = held[:, pl.ds(start, part)]
 
 
-def call(kernel, operands, outs, scratch=(), flops=0, streams=(), out_streams=(), aliases=None, hbm=()):
-    def spec(stream):
-        return pl.BlockSpec(memory_space=pl.ANY if stream else pltpu.VMEM)
-
+def call(kernel, operands, outs, scratch=(), flops=0, streams=()):
     size = sum(math.prod(o.shape) * o.dtype.itemsize for o in list(operands) + list(outs))
-    specs = [spec(i in streams) for i in range(len(operands))]
-    for i in hbm:
-        specs[i] = pl.BlockSpec(memory_space=pltpu.HBM)
+    specs = [pl.BlockSpec(memory_space=pl.ANY if i in streams else pltpu.VMEM) for i in range(len(operands))]
     if operands[0].dtype == jnp.int32:
         specs[0] = pl.BlockSpec(memory_space=pltpu.SMEM)
     outputs = pl.pallas_call(
         kernel,
         out_shape=list(outs),
         in_specs=specs,
-        out_specs=[spec(i in out_streams) for i in range(len(outs))],
+        out_specs=[pl.BlockSpec(memory_space=pltpu.VMEM)] * len(outs),
         scratch_shapes=list(scratch),
-        input_output_aliases=aliases or {},
         compiler_params=pltpu.CompilerParams(vmem_limit_bytes=LIMIT),
         cost_estimate=pl.CostEstimate(flops=flops, bytes_accessed=size, transcendentals=0),
     )(*operands)
@@ -278,21 +276,13 @@
     return moved
 
 
-def gather_pairs(pieces, order, axis, size):
-    moved = []
-    for k, piece in zip(order, pieces):
-        pairs = [(i, i ^ k) for i in range(size) if i < i ^ k]
-        moved.append(lax.all_gather(piece, axis, axis_index_groups=pairs, axis=0, tiled=False) if k else piece)
-    return moved
-
-
 def on_device(saved_input, out_gate, grad_out, long_filter):
     count, shares = lax.axis_size("ctx"), lax.axis_size("dp")
     channels, span = saved_input.shape[1:]
     rows, length = long_filter.shape
     width = length // BLOCKS
-    grad_order, input_order, back_order = (spread(count, o) for o in ((4, 5, 6, 7, 1, 2, 3), (4, 5, 6, 7, 1, 2, 3), (6, 7, 3, 1, 2, 4, 5)))
-    every = range(count + 8)
+    order, back_order = (spread(count, o) for o in ((1, 6, 7, 4, 5, 2, 3), (1, 4, 5, 6, 7, 2, 3)))
+    alone = spread(count, (6, 7))[: count // 4]
     where = jnp.stack([lax.axis_index("ctx"), lax.axis_index("dp")]).astype(jnp.int32)
     forward, backward = (jnp.asarray(t) for t in transform_tables(width))
     half, full = jnp.bfloat16, jnp.float32
@@ -305,28 +295,29 @@
     sems = pltpu.SemaphoreType.DMA
     work = 2 * GROUPS * rows * 4 * width * width
 
+    both = jax.ShapeDtypeStruct((2, rows, span), half)
     pieces = call(
-        functools.partial(gate_kernel, grad_order, input_order),
+        functools.partial(gate_kernel, order, alone),
         [where, *(pltpu.with_memory_space_constraint(x[0], pltpu.HBM) for x in (out_gate, grad_out, saved_input))],
-        [piece] * (2 * count),
+        [piece if k in alone else both for k in order] + [piece] * len(alone),
         [slots, slots, sems((2, count)), sems((count,))],
-        hbm=(1, 2, 3),
-    )
-    grad_pieces, input_pieces = pieces[:count], pieces[count:]
-    grad_blocks = exchange(grad_pieces, grad_order, "ctx", count)
+        streams=(1, 2, 3),
+    )
+    grad_blocks = exchange(pieces[:count], order, "ctx", count)
+    late_blocks = exchange(pieces[count:], alone, "ctx", count)
     (taps_spec,) = call(taps_kernel, [long_filter, forward], [spec], [mid], flops=work)
     *back, grad_spec = call(
-        functools.partial(back_kernel, grad_order, back_order),
+        functools.partial(back_kernel, order, back_order),
         [where, *grad_blocks, taps_spec, forward, backward],
         [piece] * count + [spec],
         [held, mid, wide],
         flops=2 * work,
     )
-    input_blocks = gather_pairs(input_pieces, input_order, "ctx", count)
+    input_blocks = [late_blocks[alone.index(k)] if k in alone else both for k, both in zip(order, grad_blocks)]
     back_blocks = exchange(back, back_order, "ctx", count)
     share = jax.ShapeDtypeStruct((rows, length // shares), half)
     cross = call(
-        functools.partial(cross_kernel, input_order),
+        functools.partial(cross_kernel, order),
         [where, *input_blocks, grad_spec, forward, backward],
         [share] * shares,
         [held, mid, wide],

time: 113 us -> 93 us (0.82)
  blocking collectives: 56.7 us -> 0 us
  starting transfers between devices: 31.2 us -> 49.6 us
  waiting for transfers between devices: 8.69 us -> 25.8 us
  local copies, waits for them, and re-layouts: 0.02 us -> 1.6 us
    all_gather x7 -> x0, blocking collectives: 56.7 us -> none  [gather_pairs(): lax.all_gather(piece, axis, axis_index_groups=pairs, axis=0, tiled=False)]
    ppermute x17 -> x19, starting transfers between devices: 31.2 us -> 49.6 us  [exchange(): lax.ppermute(piece, axis, [(i, i ^ k) for i in range(size)])]
    ppermute x17 -> x19, waiting for transfers between devices: 8.69 us -> 25.8 us  [exchange(): lax.ppermute(piece, axis, [(i, i ^ k) for i in range(size)])]
    unnamed x6, local copies, waits for them, and re-layouts: 0.02 us -> 1.6 us
  transfers between devices with their start and end apart: 17 -> 19, of which waited for: 2 -> 7; matrix products, arithmetic and copies ran while one was open for 0% -> 0% of each run, Pallas kernels for 6% -> 12%
where the time goes in v13:
time: 93 us; the launch traced here: 92.8 us
  starting transfers between devices  49.6 us (53%)
  waiting for transfers between devices  25.8 us (28%)
  Pallas kernels  14.1 us (15%)
  local copies, waits for them, and re-layouts  1.6 us (2%)
  other arithmetic  1.01 us (1%)
    ppermute x19, starting transfers between devices, exchange(): lax.ppermute(piece, axis, [(i, i ^ k) for i in range(size)])  49.6 us
    ppermute x19, waiting for transfers between devices, exchange(): lax.ppermute(piece, axis, [(i, i ^ k) for i in range(size)])  25.8 us
    pallas_call x5, Pallas kernels, call(): pl.pallas_call(kernel, out_shape=list(outs), in_specs=specs, out_specs=[p...  14.1 us
  transfers between devices with their start and end apart: 19, of which 7 were waited for; matrix products, arithmetic and copies ran while one was open for 0% of the time, Pallas kernels for 12%

profile of v13, /device:TPU:0, one launch (start us, length us, event | category | flops | bytes accessed | tf_op | source)
XLA Modules:
  0.0 92.8 jit_solution(10431071975961436697)
XLA Ops:
  0.6 0.0 copy-start
  0.6 0.1 pad_add_fusion.where
  0.7 2.7 %shard_map.77 = (bf16[2,512,128]{2,1,0:T(8,128)(2,1)S(1)}, bf16[512,128]{1,0:T(8,128)(2,1)S(1)}, bf16[512,128]{1,0:T(8,128)(2,1)S(1)}, bf16[2,512,128]{2,1,0:T(8...) custom-call(s32[2]{0:T(128)S(1)} %pad_add_fusion.where, ...), custom_call_target="tpu_custom_call" | custom-call | bytes 5242888 | tf_op jit(solution)/shard_map/pallas_call | solution.py:251
  3.4 5.1 %collective-permute-start.1 = (bf16[512,128]{1,0:T(8,128)(2,1)S(1)}, bf16[512,128]{1,0:T(8,128)(2,1)S(1)}, u32[]{:S(2)}, u32[]{:S(2)}) collective-permute-start(bf16[512,128]{1,0:T(8,128)(2,1)S(1)} %get-tuple-element.26), channel_id=1, source_target_pairs={{0,6},{1,7},{2,4},{3,5},{4,2},{5,3},{6,0},{7,1},{8,14},{9,15},{10,... | collective-permute-start | bytes 393224 | tf_op jit(solution)/shard_map/ppermute | solution.py:275
  8.5 1.2 %collective-permute-start.2 = (bf16[512,128]{1,0:T(8,128)(2,1)S(1)}, bf16[512,128]{1,0:T(8,128)(2,1)S(1)}, u32[]{:S(2)}, u32[]{:S(2)}) collective-permute-start(bf16[512,128]{1,0:T(8,128)(2,1)S(1)} %get-tuple-element.27), channel_id=1, source_target_pairs={{0,7},{1,6},{2,5},{3,4},{4,3},{5,2},{6,1},{7,0},{8,15},{9,14},{10,... | collective-permute-start | bytes 393224 | tf_op jit(solution)/shard_map/ppermute | solution.py:275
  9.7 0.4 collective-permute-start
  10.1 0.9 %collective-permute-start.3 = (bf16[2,512,128]{2,1,0:T(8,128)(2,1)S(1)}, bf16[2,512,128]{2,1,0:T(8,128)(2,1)S(1)}, u32[]{:S(2)}, u32[]{:S(2)}) collective-permute-start(bf16[2,512,128]{2,1,0:T(8,128)(2,1)S(1)} %get-tuple-element.28), channel_id=1, source_target_pairs={{0,4},{1,5},{2,6},{3,7},{4,0},{5,1},{6,2},{7,3},{8,12},{9,13},{10,... | collective-permute-start | bytes 786440 | tf_op jit(solution)/shard_map/ppermute | solution.py:275
  11.0 3.1 %collective-permute-start.4 = (bf16[2,512,128]{2,1,0:T(8,128)(2,1)S(1)}, bf16[2,512,128]{2,1,0:T(8,128)(2,1)S(1)}, u32[]{:S(2)}, u32[]{:S(2)}) collective-permute-start(bf16[2,512,128]{2,1,0:T(8,128)(2,1)S(1)} %get-tuple-element.29), channel_id=1, source_target_pairs={{0,5},{1,4},{2,7},{3,6},{4,1},{5,0},{6,3},{7,2},{8,13},{9,12},{10,... | collective-permute-start | bytes 786440 | tf_op jit(solution)/shard_map/ppermute | solution.py:275
  14.1 0.0 collective-permute-done.1.refs_1_
  14.1 15.5 %collective-permute-start.5 = (bf16[2,512,128]{2,1,0:T(8,128)(2,1)S(1)}, bf16[2,512,128]{2,1,0:T(8,128)(2,1)S(1)}, u32[]{:S(2)}, u32[]{:S(2)}) collective-permute-start(bf16[2,512,128]{2,1,0:T(8,128)(2,1)S(1)} %get-tuple-element.30), channel_id=1, source_target_pairs={{0,2},{1,3},{2,0},{3,1},{4,6},{5,7},{6,4},{7,5},{8,10},{9,11},{10,... | collective-permute-start | bytes 786440 | tf_op jit(solution)/shard_map/ppermute | solution.py:275
  29.5 0.0 collective-permute-done.2.refs_2_
  29.5 0.0 copy-start.1
  29.5 3.7 %collective-permute-start.6 = (bf16[2,512,128]{2,1,0:T(8,128)(2,1)S(1)}, bf16[2,512,128]{2,1,0:T(8,128)(2,1)S(1)}, u32[]{:S(2)}, u32[]{:S(2)}) collective-permute-start(bf16[2,512,128]{2,1,0:T(8,128)(2,1)S(1)} %get-tuple-element.31), channel_id=1, source_target_pairs={{0,3},{1,2},{2,1},{3,0},{4,7},{5,6},{6,5},{7,4},{8,11},{9,10},{10,... | collective-permute-start | bytes 786440 | tf_op jit(solution)/shard_map/ppermute | solution.py:275
  33.3 0.0 copy-done
  33.3 0.0 copy-start.2
  33.3 1.6 %copy-done.2 = f32[512,1024]{1,0:T(8,128)S(1)} copy-done((f32[512,1024]{1,0:T(8,128)S(1)}, f32[512,1024]{1,0:T(8,128)}, u32[]{:S(2)}) %copy-start.2) | copy-done | bytes 2097176
  34.8 1.5 %shard_map.78.refs_8_ = bf16[9,512,256]{2,1,0:T(8,128)(2,1)S(1)} custom-call(f32[512,1024]{1,0:T(8,128)S(1)} %copy-done.2, bf16[9,256,256]{2,1,0:T(8,128)(2,1)S(1)} %copy-done), custom_call_target="tpu_custom_call" | custom-call | flops 603979776 | bytes 5636096 | tf_op jit(solution)/shard_map/pallas_call | solution.py:251
  36.3 0.0 collective-permute-done.refs_0_
  36.3 2.7 %collective-permute-start.14 = (bf16[512,128]{1,0:T(8,128)(2,1)S(1)}, bf16[512,128]{1,0:T(8,128)(2,1)S(1)}, u32[]{:S(2)}, u32[]{:S(2)}) collective-permute-start(bf16[512,128]{1,0:T(8,128)(2,1)S(1)} %get-tuple-element.41), channel_id=1, source_target_pairs={{0,6},{1,7},{2,4},{3,5},{4,2},{5,3},{6,0},{7,1},{8,14},{9,15},{10,... | collective-permute-start | bytes 393224 | tf_op jit(solution)/shard_map/ppermute | solution.py:275
  39.0 0.0 collective-permute-done.3.refs_3_
  39.0 2.1 %collective-permute-start.15 = (bf16[512,128]{1,0:T(8,128)(2,1)S(1)}, bf16[512,128]{1,0:T(8,128)(2,1)S(1)}, u32[]{:S(2)}, u32[]{:S(2)}) collective-permute-start(bf16[512,128]{1,0:T(8,128)(2,1)S(1)} %get-tuple-element.42), channel_id=1, source_target_pairs={{0,7},{1,6},{2,5},{3,4},{4,3},{5,2},{6,1},{7,0},{8,15},{9,14},{10,... | collective-permute-start | bytes 393224 | tf_op jit(solution)/shard_map/ppermute | solution.py:275
  41.2 8.5 %collective-permute-done.4.refs_4_ = bf16[2,512,128]{2,1,0:T(8,128)(2,1)S(1)} collective-permute-done((bf16[2,512,128]{2,1,0:T(8,128)(2,1)S(1)}, bf16[2,512,128]{2,1,0:T(8,128)(2,1)S(1)}, u32[]{:S(2)}, u32[]{:S(2)}) %collective-permute-start.4) | collective-permute-done | bytes 262176 | tf_op jit(solution)/shard_map/ppermute | solution.py:275
  49.6 2.8 %collective-permute-done.5.refs_5_ = bf16[2,512,128]{2,1,0:T(8,128)(2,1)S(1)} collective-permute-done((bf16[2,512,128]{2,1,0:T(8,128)(2,1)S(1)}, bf16[2,512,128]{2,1,0:T(8,128)(2,1)S(1)}, u32[]{:S(2)}, u32[]{:S(2)}) %collective-permute-start.5) | collective-permute-done | bytes 262176 | tf_op jit(solution)/shard_map/ppermute | solution.py:275
  52.5 5.2 %collective-permute-done.6.refs_6_ = bf16[2,512,128]{2,1,0:T(8,128)(2,1)S(1)} collective-permute-done((bf16[2,512,128]{2,1,0:T(8,128)(2,1)S(1)}, bf16[2,512,128]{2,1,0:T(8,128)(2,1)S(1)}, u32[]{:S(2)}, u32[]{:S(2)}) %collective-permute-start.6) | collective-permute-done | bytes 262176 | tf_op jit(solution)/shard_map/ppermute | solution.py:275
  57.6 0.0 copy-done.1
  57.6 4.2 %shard_map.79 = (bf16[512,128]{1,0:T(8,128)(2,1)S(1)}, bf16[512,128]{1,0:T(8,128)(2,1)S(1)}, bf16[512,128]{1,0:T(8,128)(2,1)S(1)}, bf16[512,128]{1,0:T(8,128)(2,...) custom-call(s32[2]{0:T(128)S(1)} %pad_add_fusion.where, ...), custom_call_target="tpu_custom_call" | custom-call | flops 1207959552 | bytes 9961480 | tf_op jit(solution)/shard_map/pallas_call | solution.py:251
  61.9 0.1 collective-permute-start.7
  62.0 0.1 collective-permute-start.8
  62.1 4.2 %collective-permute-start.9 = (bf16[512,128]{1,0:T(8,128)(2,1)S(1)}, bf16[512,128]{1,0:T(8,128)(2,1)S(1)}, u32[]{:S(2)}, u32[]{:S(2)}) collective-permute-start(bf16[512,128]{1,0:T(8,128)(2,1)S(1)} %get-tuple-element.35), channel_id=1, source_target_pairs={{0,5},{1,4},{2,7},{3,6},{4,1},{5,0},{6,3},{7,2},{8,13},{9,12},{10,... | collective-permute-start | bytes 393224 | tf_op jit(solution)/shard_map/ppermute | solution.py:275
  66.3 0.0 collective-permute-done.14.refs_1_
  66.3 1.5 %collective-permute-start.10 = (bf16[512,128]{1,0:T(8,128)(2,1)S(1)}, bf16[512,128]{1,0:T(8,128)(2,1)S(1)}, u32[]{:S(2)}, u32[]{:S(2)}) collective-permute-start(bf16[512,128]{1,0:T(8,128)(2,1)S(1)} %get-tuple-element.36), channel_id=1, source_target_pairs={{0,6},{1,7},{2,4},{3,5},{4,2},{5,3},{6,0},{7,1},{8,14},{9,15},{10,... | collective-permute-start | bytes 393224 | tf_op jit(solution)/shard_map/ppermute | solution.py:275
  67.8 0.0 collective-permute-done.15.refs_2_
  67.8 1.8 %collective-permute-start.11 = (bf16[512,128]{1,0:T(8,128)(2,1)S(1)}, bf16[512,128]{1,0:T(8,128)(2,1)S(1)}, u32[]{:S(2)}, u32[]{:S(2)}) collective-permute-start(bf16[512,128]{1,0:T(8,128)(2,1)S(1)} %get-tuple-element.37), channel_id=1, source_target_pairs={{0,7},{1,6},{2,5},{3,4},{4,3},{5,2},{6,1},{7,0},{8,15},{9,14},{10,... | collective-permute-start | bytes 393224 | tf_op jit(solution)/shard_map/ppermute | solution.py:275
  69.7 4.1 %shard_map.81 = (bf16[512,256]{1,0:T(8,128)(2,1)S(1)}, bf16[512,256]{1,0:T(8,128)(2,1)S(1)}, bf16[512,256]{1,0:T(8,128)(2,1)S(1)}, bf16[512,256]{1,0:T(8,128)(2,1)S(1)}) custom-call(s32[2]{0:T(128)S(1)} %pad_add_fusion.where, bf16[2,512,128]{2,1,0:T(8,128)(2,1)S(1)} %collective-permute-done.refs_0_, bf16[512,128]{1,0:T(8,128)(2,1)S(1)} %collective-permute-done.14.refs_1_, ...), custom_call_target="tpu_custom_call" | custom-call | flops 1207959552 | bytes 7602184 | tf_op jit(solution)/shard_map/pallas_call | solution.py:251
  73.8 0.0 collective-permute-done.7.refs_0_
  73.8 1.6 %collective-permute-start.16 = (bf16[512,256]{1,0:T(8,128)(2,1)S(1)}, bf16[512,256]{1,0:T(8,128)(2,1)S(1)}, u32[]{:S(2)}, u32[]{:S(2)}) collective-permute-start(bf16[512,256]{1,0:T(8,128)(2,1)S(1)} %get-tuple-element.44), channel_id=1, source_target_pairs={{0,16},{8,24},{16,0},{24,8},{1,17},{9,25},{17,1},{25,9},{2,18},{10... | collective-permute-start | bytes 786440 | tf_op jit(solution)/shard_map/ppermute | solution.py:275
  75.4 2.2 %collective-permute-done.8.refs_1_ = bf16[512,128]{1,0:T(8,128)(2,1)S(1)} collective-permute-done((bf16[512,128]{1,0:T(8,128)(2,1)S(1)}, bf16[512,128]{1,0:T(8,128)(2,1)S(1)}, u32[]{:S(2)}, u32[]{:S(2)}) %collective-permute-start.8) | collective-permute-done | bytes 131104 | tf_op jit(solution)/shard_map/ppermute | solution.py:275
  77.6 0.0 collective-permute-start.17
  77.6 3.6 %collective-permute-done.9.refs_2_ = bf16[512,128]{1,0:T(8,128)(2,1)S(1)} collective-permute-done((bf16[512,128]{1,0:T(8,128)(2,1)S(1)}, bf16[512,128]{1,0:T(8,128)(2,1)S(1)}, u32[]{:S(2)}, u32[]{:S(2)}) %collective-permute-start.9) | collective-permute-done | bytes 131104 | tf_op jit(solution)/shard_map/ppermute | solution.py:275
  81.2 0.0 collective-permute-start.18
  81.2 0.0 collective-permute-done.10.refs_3_
  81.2 2.6 %collective-permute-start.12 = (bf16[512,128]{1,0:T(8,128)(2,1)S(1)}, bf16[512,128]{1,0:T(8,128)(2,1)S(1)}, u32[]{:S(2)}, u32[]{:S(2)}) collective-permute-start(bf16[512,128]{1,0:T(8,128)(2,1)S(1)} %get-tuple-element.38), channel_id=1, source_target_pairs={{0,2},{1,3},{2,0},{3,1},{4,6},{5,7},{6,4},{7,5},{8,10},{9,11},{10,... | collective-permute-start | bytes 393224 | tf_op jit(solution)/shard_map/ppermute | solution.py:275
  83.8 0.0 collective-permute-done.11.refs_4_
  83.8 3.0 %collective-permute-start.13 = (bf16[512,128]{1,0:T(8,128)(2,1)S(1)}, bf16[512,128]{1,0:T(8,128)(2,1)S(1)}, u32[]{:S(2)}, u32[]{:S(2)}) collective-permute-start(bf16[512,128]{1,0:T(8,128)(2,1)S(1)} %get-tuple-element.39), channel_id=1, source_target_pairs={{0,3},{1,2},{2,1},{3,0},{4,7},{5,6},{6,5},{7,4},{8,11},{9,10},{10,... | collective-permute-start | bytes 393224 | tf_op jit(solution)/shard_map/ppermute | solution.py:275
  86.8 1.0 %collective-permute-done.12.refs_5_ = bf16[512,128]{1,0:T(8,128)(2,1)S(1)} collective-permute-done((bf16[512,128]{1,0:T(8,128)(2,1)S(1)}, bf16[512,128]{1,0:T(8,128)(2,1)S(1)}, u32[]{:S(2)}, u32[]{:S(2)}) %collective-permute-start.12) | collective-permute-done | bytes 131104 | tf_op jit(solution)/shard_map/ppermute | solution.py:275
  87.8 2.5 %collective-permute-done.13.refs_6_ = bf16[512,128]{1,0:T(8,128)(2,1)S(1)} collective-permute-done((bf16[512,128]{1,0:T(8,128)(2,1)S(1)}, bf16[512,128]{1,0:T(8,128)(2,1)S(1)}, u32[]{:S(2)}, u32[]{:S(2)}) %collective-permute-start.13) | collective-permute-done | bytes 131104 | tf_op jit(solution)/shard_map/ppermute | solution.py:275
  90.3 1.6 %shard_map.80 = bf16[8,512,128]{2,1,0:T(8,128)(2,1)} custom-call(s32[2]{0:T(128)S(1)} %pad_add_fusion.where, bf16[512,128]{1,0:T(8,128)(2,1)S(1)} %collective-permute-done.7.refs_0_, bf16[512,128]{1,0:T(8,128)(2,1)S(1)} %collective-permute-done.8.refs_1_, bf16[512,128]{1,0:T(8,128)(2,1)S(1)} %collective-permute-done.9.refs_2_, ...), custom_call_target="tpu_custom_call" | custom-call | bytes 2097160 | tf_op jit(solution)/shard_map/pallas_call | solution.py:251
  91.9 0.0 collective-permute-done.16
  91.9 0.0 collective-permute-done.17
  91.9 0.0 collective-permute-done.18
  91.9 0.9 %add_multiply_fusion = f32[512,256]{1,0:T(8,128)} fusion(bf16[512,256]{1,0:T(8,128)(2,1)S(1)} %get-tuple-element.47, bf16[512,256]{1,0:T(8,128)(2,1)S(1)} %collective-permute-done.18, bf16[512,256]{1,0:T(8,128)(2,1)S(1)} %collective-permute-done.17, bf16[512,256]{1,0:T(8,128)(2,1)S(1)} %collective-permute-done.16), kind=kLoop, calls=%fused_computation | loop fusion | flops 1048576 | bytes 1572864 | tf_op jit(solution)/shard_map/mul | solution.py:328
Async XLA Ops:
  0.6 32.6 %copy-start = (bf16[9,256,256]{2,1,0:T(8,128)(2,1)S(1)}, bf16[9,256,256]{2,1,0:T(8,128)(2,1)}, u32[]{:S(2)}) copy-start(bf16[9,256,256]{2,1,0:T(8,128)(2,1)} %constant.14.clone.forward.refs_9_) | copy-start | bytes 3538948
  3.4 10.7 %collective-permute-start.1 = (bf16[512,128]{1,0:T(8,128)(2,1)S(1)}, bf16[512,128]{1,0:T(8,128)(2,1)S(1)}, u32[]{:S(2)}, u32[]{:S(2)}) collective-permute-start(bf16[512,128]{1,0:T(8,128)(2,1)S(1)} %get-tuple-element.26), channel_id=1, source_target_pairs={{0,6},{1,7},{2,4},{3,5},{4,2},{5,3},{6,0},{7,1},{8,14},{9,15},{10,... | collective-permute-start | bytes 393224 | tf_op jit(solution)/shard_map/ppermute | solution.py:275
  8.5 21.0 %collective-permute-start.2 = (bf16[512,128]{1,0:T(8,128)(2,1)S(1)}, bf16[512,128]{1,0:T(8,128)(2,1)S(1)}, u32[]{:S(2)}, u32[]{:S(2)}) collective-permute-start(bf16[512,128]{1,0:T(8,128)(2,1)S(1)} %get-tuple-element.27), channel_id=1, source_target_pairs={{0,7},{1,6},{2,5},{3,4},{4,3},{5,2},{6,1},{7,0},{8,15},{9,14},{10,... | collective-permute-start | bytes 393224 | tf_op jit(solution)/shard_map/ppermute | solution.py:275
  9.7 26.6 %collective-permute-start = (bf16[2,512,128]{2,1,0:T(8,128)(2,1)S(1)}, bf16[2,512,128]{2,1,0:T(8,128)(2,1)S(1)}, u32[]{:S(2)}, u32[]{:S(2)}) collective-permute-start(bf16[2,512,128]{2,1,0:T(8,128)(2,1)S(1)} %get-tuple-element.25), channel_id=1, source_target_pairs={{0,1},{1,0},{2,3},{3,2},{4,5},{5,4},{6,7},{7,6},{8,9},{9,8},{10,11... | collective-permute-start | bytes 786440 | tf_op jit(solution)/shard_map/ppermute | solution.py:275
  10.1 29.0 %collective-permute-start.3 = (bf16[2,512,128]{2,1,0:T(8,128)(2,1)S(1)}, bf16[2,512,128]{2,1,0:T(8,128)(2,1)S(1)}, u32[]{:S(2)}, u32[]{:S(2)}) collective-permute-start(bf16[2,512,128]{2,1,0:T(8,128)(2,1)S(1)} %get-tuple-element.28), channel_id=1, source_target_pairs={{0,4},{1,5},{2,6},{3,7},{4,0},{5,1},{6,2},{7,3},{8,12},{9,13},{10,... | collective-permute-start | bytes 786440 | tf_op jit(solution)/shard_map/ppermute | solution.py:275
  11.0 38.6 %collective-permute-start.4 = (bf16[2,512,128]{2,1,0:T(8,128)(2,1)S(1)}, bf16[2,512,128]{2,1,0:T(8,128)(2,1)S(1)}, u32[]{:S(2)}, u32[]{:S(2)}) collective-permute-start(bf16[2,512,128]{2,1,0:T(8,128)(2,1)S(1)} %get-tuple-element.29), channel_id=1, source_target_pairs={{0,5},{1,4},{2,7},{3,6},{4,1},{5,0},{6,3},{7,2},{8,13},{9,12},{10,... | collective-permute-start | bytes 786440 | tf_op jit(solution)/shard_map/ppermute | solution.py:275
  14.1 38.4 %collective-permute-start.5 = (bf16[2,512,128]{2,1,0:T(8,128)(2,1)S(1)}, bf16[2,512,128]{2,1,0:T(8,128)(2,1)S(1)}, u32[]{:S(2)}, u32[]{:S(2)}) collective-permute-start(bf16[2,512,128]{2,1,0:T(8,128)(2,1)S(1)} %get-tuple-element.30), channel_id=1, source_target_pairs={{0,2},{1,3},{2,0},{3,1},{4,6},{5,7},{6,4},{7,5},{8,10},{9,11},{10,... | collective-permute-start | bytes 786440 | tf_op jit(solution)/shard_map/ppermute | solution.py:275
  29.5 28.1 %copy-start.1 = (bf16[9,256,256]{2,1,0:T(8,128)(2,1)S(1)}, bf16[9,256,256]{2,1,0:T(8,128)(2,1)}, u32[]{:S(2)}) copy-start(bf16[9,256,256]{2,1,0:T(8,128)(2,1)} %constant.15.clone.refs_10_) | copy-start | bytes 3538948
  29.5 28.1 %collective-permute-start.6 = (bf16[2,512,128]{2,1,0:T(8,128)(2,1)S(1)}, bf16[2,512,128]{2,1,0:T(8,128)(2,1)S(1)}, u32[]{:S(2)}, u32[]{:S(2)}) collective-permute-start(bf16[2,512,128]{2,1,0:T(8,128)(2,1)S(1)} %get-tuple-element.31), channel_id=1, source_target_pairs={{0,3},{1,2},{2,1},{3,0},{4,7},{5,6},{6,5},{7,4},{8,11},{9,10},{10,... | collective-permute-start | bytes 786440 | tf_op jit(solution)/shard_map/ppermute | solution.py:275
  33.3 1.6 %copy-start.2 = (f32[512,1024]{1,0:T(8,128)S(1)}, f32[512,1024]{1,0:T(8,128)}, u32[]{:S(2)}) copy-start(f32[512,1024]{1,0:T(8,128)} %taps.1) | copy-start | bytes 6291460
  36.3 30.0 %collective-permute-start.14 = (bf16[512,128]{1,0:T(8,128)(2,1)S(1)}, bf16[512,128]{1,0:T(8,128)(2,1)S(1)}, u32[]{:S(2)}, u32[]{:S(2)}) collective-permute-start(bf16[512,128]{1,0:T(8,128)(2,1)S(1)} %get-tuple-element.41), channel_id=1, source_target_pairs={{0,6},{1,7},{2,4},{3,5},{4,2},{5,3},{6,0},{7,1},{8,14},{9,15},{10,... | collective-permute-start | bytes 393224 | tf_op jit(solution)/shard_map/ppermute | solution.py:275
  39.0 28.8 %collective-permute-start.15 = (bf16[512,128]{1,0:T(8,128)(2,1)S(1)}, bf16[512,128]{1,0:T(8,128)(2,1)S(1)}, u32[]{:S(2)}, u32[]{:S(2)}) collective-permute-start(bf16[512,128]{1,0:T(8,128)(2,1)S(1)} %get-tuple-element.42), channel_id=1, source_target_pairs={{0,7},{1,6},{2,5},{3,4},{4,3},{5,2},{6,1},{7,0},{8,15},{9,14},{10,... | collective-permute-start | bytes 393224 | tf_op jit(solution)/shard_map/ppermute | solution.py:275
  61.9 11.9 %collective-permute-start.7 = (bf16[512,128]{1,0:T(8,128)(2,1)S(1)}, bf16[512,128]{1,0:T(8,128)(2,1)S(1)}, u32[]{:S(2)}, u32[]{:S(2)}) collective-permute-start(bf16[512,128]{1,0:T(8,128)(2,1)S(1)} %get-tuple-element.33), channel_id=1, source_target_pairs={{0,1},{1,0},{2,3},{3,2},{4,5},{5,4},{6,7},{7,6},{8,9},{9,8},{10,11... | collective-permute-start | bytes 393224 | tf_op jit(solution)/shard_map/ppermute | solution.py:275
  62.0 15.6 %collective-permute-start.8 = (bf16[512,128]{1,0:T(8,128)(2,1)S(1)}, bf16[512,128]{1,0:T(8,128)(2,1)S(1)}, u32[]{:S(2)}, u32[]{:S(2)}) collective-permute-start(bf16[512,128]{1,0:T(8,128)(2,1)S(1)} %get-tuple-element.34), channel_id=1, source_target_pairs={{0,4},{1,5},{2,6},{3,7},{4,0},{5,1},{6,2},{7,3},{8,12},{9,13},{10,... | collective-permute-start | bytes 393224 | tf_op jit(solution)/shard_map/ppermute | solution.py:275
  62.1 19.1 %collective-permute-start.9 = (bf16[512,128]{1,0:T(8,128)(2,1)S(1)}, bf16[512,128]{1,0:T(8,128)(2,1)S(1)}, u32[]{:S(2)}, u32[]{:S(2)}) collective-permute-start(bf16[512,128]{1,0:T(8,128)(2,1)S(1)} %get-tuple-element.35), channel_id=1, source_target_pairs={{0,5},{1,4},{2,7},{3,6},{4,1},{5,0},{6,3},{7,2},{8,13},{9,12},{10,... | collective-permute-start | bytes 393224 | tf_op jit(solution)/shard_map/ppermute | solution.py:275
  66.3 14.9 %collective-permute-start.10 = (bf16[512,128]{1,0:T(8,128)(2,1)S(1)}, bf16[512,128]{1,0:T(8,128)(2,1)S(1)}, u32[]{:S(2)}, u32[]{:S(2)}) collective-permute-start(bf16[512,128]{1,0:T(8,128)(2,1)S(1)} %get-tuple-element.36), channel_id=1, source_target_pairs={{0,6},{1,7},{2,4},{3,5},{4,2},{5,3},{6,0},{7,1},{8,14},{9,15},{10,... | collective-permute-start | bytes 393224 | tf_op jit(solution)/shard_map/ppermute | solution.py:275
  67.8 15.9 %collective-permute-start.11 = (bf16[512,128]{1,0:T(8,128)(2,1)S(1)}, bf16[512,128]{1,0:T(8,128)(2,1)S(1)}, u32[]{:S(2)}, u32[]{:S(2)}) collective-permute-start(bf16[512,128]{1,0:T(8,128)(2,1)S(1)} %get-tuple-element.37), channel_id=1, source_target_pairs={{0,7},{1,6},{2,5},{3,4},{4,3},{5,2},{6,1},{7,0},{8,15},{9,14},{10,... | collective-permute-start | bytes 393224 | tf_op jit(solution)/shard_map/ppermute | solution.py:275
  73.8 18.1 %collective-permute-start.16 = (bf16[512,256]{1,0:T(8,128)(2,1)S(1)}, bf16[512,256]{1,0:T(8,128)(2,1)S(1)}, u32[]{:S(2)}, u32[]{:S(2)}) collective-permute-start(bf16[512,256]{1,0:T(8,128)(2,1)S(1)} %get-tuple-element.44), channel_id=1, source_target_pairs={{0,16},{8,24},{16,0},{24,8},{1,17},{9,25},{17,1},{25,9},{2,18},{10... | collective-permute-start | bytes 786440 | tf_op jit(solution)/shard_map/ppermute | solution.py:275
  77.6 14.3 %collective-permute-start.17 = (bf16[512,256]{1,0:T(8,128)(2,1)S(1)}, bf16[512,256]{1,0:T(8,128)(2,1)S(1)}, u32[]{:S(2)}, u32[]{:S(2)}) collective-permute-start(bf16[512,256]{1,0:T(8,128)(2,1)S(1)} %get-tuple-element.45), channel_id=1, source_target_pairs={{0,24},{8,16},{16,8},{24,0},{1,25},{9,17},{17,9},{25,1},{2,26},{10... | collective-permute-start | bytes 786440 | tf_op jit(solution)/shard_map/ppermute | solution.py:275
  81.2 10.7 %collective-permute-start.18 = (bf16[512,256]{1,0:T(8,128)(2,1)S(1)}, bf16[512,256]{1,0:T(8,128)(2,1)S(1)}, u32[]{:S(2)}, u32[]{:S(2)}) collective-permute-start(bf16[512,256]{1,0:T(8,128)(2,1)S(1)} %get-tuple-element.46), channel_id=1, source_target_pairs={{0,8},{8,0},{16,24},{24,16},{1,9},{9,1},{17,25},{25,17},{2,10},{10... | collective-permute-start | bytes 786440 | tf_op jit(solution)/shard_map/ppermute | solution.py:275
  81.2 6.6 %collective-permute-start.12 = (bf16[512,128]{1,0:T(8,128)(2,1)S(1)}, bf16[512,128]{1,0:T(8,128)(2,1)S(1)}, u32[]{:S(2)}, u32[]{:S(2)}) collective-permute-start(bf16[512,128]{1,0:T(8,128)(2,1)S(1)} %get-tuple-element.38), channel_id=1, source_target_pairs={{0,2},{1,3},{2,0},{3,1},{4,6},{5,7},{6,4},{7,5},{8,10},{9,11},{10,... | collective-permute-start | bytes 393224 | tf_op jit(solution)/shard_map/ppermute | solution.py:275
  83.8 6.5 %collective-permute-start.13 = (bf16[512,128]{1,0:T(8,128)(2,1)S(1)}, bf16[512,128]{1,0:T(8,128)(2,1)S(1)}, u32[]{:S(2)}, u32[]{:S(2)}) collective-permute-start(bf16[512,128]{1,0:T(8,128)(2,1)S(1)} %get-tuple-element.39), channel_id=1, source_target_pairs={{0,3},{1,2},{2,1},{3,0},{4,7},{5,6},{6,5},{7,4},{8,11},{9,10},{10,... | collective-permute-start | bytes 393224 | tf_op jit(solution)/shard_map/ppermute | solution.py:275

commit v14 on v13

--- a/solution.py
+++ b/solution.py
@@ -281,8 +281,8 @@
     channels, span = saved_input.shape[1:]
     rows, length = long_filter.shape
     width = length // BLOCKS
-    order, back_order = (spread(count, o) for o in ((1, 6, 7, 4, 5, 2, 3), (1, 4, 5, 6, 7, 2, 3)))
-    alone = spread(count, (6, 7))[: count // 4]
+    order, back_order = (spread(count, o) for o in ((4, 1, 5, 2, 6, 7, 3), (1, 4, 2, 5, 6, 7, 3)))
+    alone = spread(count, (4, 5, 6, 7))[: count // 2]
     where = jnp.stack([lax.axis_index("ctx"), lax.axis_index("dp")]).astype(jnp.int32)
     forward, backward = (jnp.asarray(t) for t in transform_tables(width))
     half, full = jnp.bfloat16, jnp.float32

time: 93 us -> 83.6 us (0.90)
  starting transfers between devices: 49.6 us -> 40.6 us
  waiting for transfers between devices: 25.8 us -> 24.6 us
    ppermute x19 -> x21, starting transfers between devices: 49.6 us -> 40.6 us  [exchange(): lax.ppermute(piece, axis, [(i, i ^ k) for i in range(size)])]
    ppermute x19 -> x21, waiting for transfers between devices: 25.8 us -> 24.6 us  [exchange(): lax.ppermute(piece, axis, [(i, i ^ k) for i in range(size)])]
  transfers between devices with their start and end apart: 19 -> 21, of which waited for: 7 -> 10; matrix products, arithmetic and copies ran while one was open for 0% -> 0% of each run, Pallas kernels for 12% -> 14%
where the time goes in v14:
time: 83.6 us; the launch traced here: 82.6 us
  starting transfers between devices  40.6 us (49%)
  waiting for transfers between devices  24.6 us (29%)
  Pallas kernels  14.1 us (17%)
  local copies, waits for them, and re-layouts  1.6 us (2%)
  other arithmetic  1.02 us (1%)
    ppermute x21, starting transfers between devices, exchange(): lax.ppermute(piece, axis, [(i, i ^ k) for i in range(size)])  40.6 us
    ppermute x21, waiting for transfers between devices, exchange(): lax.ppermute(piece, axis, [(i, i ^ k) for i in range(size)])  24.6 us
    pallas_call x5, Pallas kernels, call(): pl.pallas_call(kernel, out_shape=list(outs), in_specs=specs, out_specs=[p...  14.1 us
  transfers between devices with their start and end apart: 21, of which 10 were waited for; matrix products, arithmetic and copies ran while one was open for 0% of the time, Pallas kernels for 14%

profile of v14, /device:TPU:0, one launch (start us, length us, event | category | flops | bytes accessed | tf_op | source)
XLA Modules:
  0.0 82.6 jit_solution(16723809198091635299)
XLA Ops:
  0.6 0.0 copy-start
  0.6 0.1 pad_add_fusion.where
  0.7 2.7 %shard_map.77 = (bf16[512,128]{1,0:T(8,128)(2,1)S(1)}, bf16[2,512,128]{2,1,0:T(8,128)(2,1)S(1)}, bf16[512,128]{1,0:T(8,128)(2,1)S(1)}, bf16[2,512,128]{2,1,0:T(8...) custom-call(s32[2]{0:T(128)S(1)} %pad_add_fusion.where, ...), custom_call_target="tpu_custom_call" | custom-call | bytes 5242888 | tf_op jit(solution)/shard_map/pallas_call | solution.py:251
  3.4 4.1 %collective-permute-start = (bf16[512,128]{1,0:T(8,128)(2,1)S(1)}, bf16[512,128]{1,0:T(8,128)(2,1)S(1)}, u32[]{:S(2)}, u32[]{:S(2)}) collective-permute-start(bf16[512,128]{1,0:T(8,128)(2,1)S(1)} %get-tuple-element.27), channel_id=1, source_target_pairs={{0,4},{1,5},{2,6},{3,7},{4,0},{5,1},{6,2},{7,3},{8,12},{9,13},{10,... | collective-permute-start | bytes 393224 | tf_op jit(solution)/shard_map/ppermute | solution.py:275
  7.5 1.3 %collective-permute-start.2 = (bf16[512,128]{1,0:T(8,128)(2,1)S(1)}, bf16[512,128]{1,0:T(8,128)(2,1)S(1)}, u32[]{:S(2)}, u32[]{:S(2)}) collective-permute-start(bf16[512,128]{1,0:T(8,128)(2,1)S(1)} %get-tuple-element.29), channel_id=1, source_target_pairs={{0,5},{1,4},{2,7},{3,6},{4,1},{5,0},{6,3},{7,2},{8,13},{9,12},{10,... | collective-permute-start | bytes 393224 | tf_op jit(solution)/shard_map/ppermute | solution.py:275
  8.8 0.2 collective-permute-start.1
  9.0 1.8 %collective-permute-start.3 = (bf16[2,512,128]{2,1,0:T(8,128)(2,1)S(1)}, bf16[2,512,128]{2,1,0:T(8,128)(2,1)S(1)}, u32[]{:S(2)}, u32[]{:S(2)}) collective-permute-start(bf16[2,512,128]{2,1,0:T(8,128)(2,1)S(1)} %get-tuple-element.30), channel_id=1, source_target_pairs={{0,2},{1,3},{2,0},{3,1},{4,6},{5,7},{6,4},{7,5},{8,10},{9,11},{10,... | collective-permute-start | bytes 786440 | tf_op jit(solution)/shard_map/ppermute | solution.py:275
  10.9 1.4 %collective-permute-start.6 = (bf16[2,512,128]{2,1,0:T(8,128)(2,1)S(1)}, bf16[2,512,128]{2,1,0:T(8,128)(2,1)S(1)}, u32[]{:S(2)}, u32[]{:S(2)}) collective-permute-start(bf16[2,512,128]{2,1,0:T(8,128)(2,1)S(1)} %get-tuple-element.33), channel_id=1, source_target_pairs={{0,3},{1,2},{2,1},{3,0},{4,7},{5,6},{6,5},{7,4},{8,11},{9,10},{10,... | collective-permute-start | bytes 786440 | tf_op jit(solution)/shard_map/ppermute | solution.py:275
  12.3 5.2 %collective-permute-done.refs_0_ = bf16[512,128]{1,0:T(8,128)(2,1)S(1)} collective-permute-done((bf16[512,128]{1,0:T(8,128)(2,1)S(1)}, bf16[512,128]{1,0:T(8,128)(2,1)S(1)}, u32[]{:S(2)}, u32[]{:S(2)}) %collective-permute-start) | collective-permute-done | bytes 131104 | tf_op jit(solution)/shard_map/ppermute | solution.py:275
  17.5 2.9 %collective-permute-start.4 = (bf16[512,128]{1,0:T(8,128)(2,1)S(1)}, bf16[512,128]{1,0:T(8,128)(2,1)S(1)}, u32[]{:S(2)}, u32[]{:S(2)}) collective-permute-start(bf16[512,128]{1,0:T(8,128)(2,1)S(1)} %get-tuple-element.31), channel_id=1, source_target_pairs={{0,6},{1,7},{2,4},{3,5},{4,2},{5,3},{6,0},{7,1},{8,14},{9,15},{10,... | collective-permute-start | bytes 393224 | tf_op jit(solution)/shard_map/ppermute | solution.py:275
  20.3 0.1 collective-permute-done.2.refs_2_
  20.4 3.6 %collective-permute-start.5 = (bf16[512,128]{1,0:T(8,128)(2,1)S(1)}, bf16[512,128]{1,0:T(8,128)(2,1)S(1)}, u32[]{:S(2)}, u32[]{:S(2)}) collective-permute-start(bf16[512,128]{1,0:T(8,128)(2,1)S(1)} %get-tuple-element.32), channel_id=1, source_target_pairs={{0,7},{1,6},{2,5},{3,4},{4,3},{5,2},{6,1},{7,0},{8,15},{9,14},{10,... | collective-permute-start | bytes 393224 | tf_op jit(solution)/shard_map/ppermute | solution.py:275
  24.0 6.8 %collective-permute-done.4.refs_4_ = bf16[512,128]{1,0:T(8,128)(2,1)S(1)} collective-permute-done((bf16[512,128]{1,0:T(8,128)(2,1)S(1)}, bf16[512,128]{1,0:T(8,128)(2,1)S(1)}, u32[]{:S(2)}, u32[]{:S(2)}) %collective-permute-start.4) | collective-permute-done | bytes 131104 | tf_op jit(solution)/shard_map/ppermute | solution.py:275
  30.8 0.0 collective-permute-start.14
  30.8 1.9 %collective-permute-done.5.refs_5_ = bf16[512,128]{1,0:T(8,128)(2,1)S(1)} collective-permute-done((bf16[512,128]{1,0:T(8,128)(2,1)S(1)}, bf16[512,128]{1,0:T(8,128)(2,1)S(1)}, u32[]{:S(2)}, u32[]{:S(2)}) %collective-permute-start.5) | collective-permute-done | bytes 131104 | tf_op jit(solution)/shard_map/ppermute | solution.py:275
  32.8 0.0 copy-start.1
  32.8 1.2 %collective-permute-start.15 = (bf16[512,128]{1,0:T(8,128)(2,1)S(1)}, bf16[512,128]{1,0:T(8,128)(2,1)S(1)}, u32[]{:S(2)}, u32[]{:S(2)}) collective-permute-start(bf16[512,128]{1,0:T(8,128)(2,1)S(1)} %get-tuple-element.44), channel_id=1, source_target_pairs={{0,5},{1,4},{2,7},{3,6},{4,1},{5,0},{6,3},{7,2},{8,13},{9,12},{10,... | collective-permute-start | bytes 393224 | tf_op jit(solution)/shard_map/ppermute | solution.py:275
  34.0 0.0 copy-done
  34.0 0.0 copy-start.2
  34.0 1.6 %copy-done.2 = f32[512,1024]{1,0:T(8,128)S(1)} copy-done((f32[512,1024]{1,0:T(8,128)S(1)}, f32[512,1024]{1,0:T(8,128)}, u32[]{:S(2)}) %copy-start.2) | copy-done | bytes 2097176
  35.6 1.5 %shard_map.78.refs_8_ = bf16[9,512,256]{2,1,0:T(8,128)(2,1)S(1)} custom-call(f32[512,1024]{1,0:T(8,128)S(1)} %copy-done.2, bf16[9,256,256]{2,1,0:T(8,128)(2,1)S(1)} %copy-done), custom_call_target="tpu_custom_call" | custom-call | flops 603979776 | bytes 5636096 | tf_op jit(solution)/shard_map/pallas_call | solution.py:251
  37.1 0.0 collective-permute-done.1.refs_1_
  37.1 4.5 %collective-permute-start.16 = (bf16[512,128]{1,0:T(8,128)(2,1)S(1)}, bf16[512,128]{1,0:T(8,128)(2,1)S(1)}, u32[]{:S(2)}, u32[]{:S(2)}) collective-permute-start(bf16[512,128]{1,0:T(8,128)(2,1)S(1)} %get-tuple-element.45), channel_id=1, source_target_pairs={{0,6},{1,7},{2,4},{3,5},{4,2},{5,3},{6,0},{7,1},{8,14},{9,15},{10,... | collective-permute-start | bytes 393224 | tf_op jit(solution)/shard_map/ppermute | solution.py:275
  41.6 0.0 collective-permute-done.3.refs_3_
  41.6 0.0 collective-permute-start.17
  41.6 0.0 collective-permute-done.6.refs_6_
  41.6 0.0 copy-done.1
  41.6 4.3 %shard_map.79 = (bf16[512,128]{1,0:T(8,128)(2,1)S(1)}, bf16[512,128]{1,0:T(8,128)(2,1)S(1)}, bf16[512,128]{1,0:T(8,128)(2,1)S(1)}, bf16[512,128]{1,0:T(8,128)(2,...) custom-call(s32[2]{0:T(128)S(1)} %pad_add_fusion.where, ...), custom_call_target="tpu_custom_call" | custom-call | flops 1207959552 | bytes 9699336 | tf_op jit(solution)/shard_map/pallas_call | solution.py:251
  45.9 1.6 %collective-permute-start.7 = (bf16[512,128]{1,0:T(8,128)(2,1)S(1)}, bf16[512,128]{1,0:T(8,128)(2,1)S(1)}, u32[]{:S(2)}, u32[]{:S(2)}) collective-permute-start(bf16[512,128]{1,0:T(8,128)(2,1)S(1)} %get-tuple-element.35), channel_id=1, source_target_pairs={{0,1},{1,0},{2,3},{3,2},{4,5},{5,4},{6,7},{7,6},{8,9},{9,8},{10,11... | collective-permute-start | bytes 393224 | tf_op jit(solution)/shard_map/ppermute | solution.py:275
  47.5 0.2 collective-permute-done.14.refs_0_
  47.7 1.6 %collective-permute-start.8 = (bf16[512,128]{1,0:T(8,128)(2,1)S(1)}, bf16[512,128]{1,0:T(8,128)(2,1)S(1)}, u32[]{:S(2)}, u32[]{:S(2)}) collective-permute-start(bf16[512,128]{1,0:T(8,128)(2,1)S(1)} %get-tuple-element.36), channel_id=1, source_target_pairs={{0,4},{1,5},{2,6},{3,7},{4,0},{5,1},{6,2},{7,3},{8,12},{9,13},{10,... | collective-permute-start | bytes 393224 | tf_op jit(solution)/shard_map/ppermute | solution.py:275
  49.3 1.4 %collective-permute-done.15.refs_2_ = bf16[512,128]{1,0:T(8,128)(2,1)S(1)} collective-permute-done((bf16[512,128]{1,0:T(8,128)(2,1)S(1)}, bf16[512,128]{1,0:T(8,128)(2,1)S(1)}, u32[]{:S(2)}, u32[]{:S(2)}) %collective-permute-start.15) | collective-permute-done | bytes 131104 | tf_op jit(solution)/shard_map/ppermute | solution.py:275
  50.7 1.1 %collective-permute-start.9 = (bf16[512,128]{1,0:T(8,128)(2,1)S(1)}, bf16[512,128]{1,0:T(8,128)(2,1)S(1)}, u32[]{:S(2)}, u32[]{:S(2)}) collective-permute-start(bf16[512,128]{1,0:T(8,128)(2,1)S(1)} %get-tuple-element.37), channel_id=1, source_target_pairs={{0,2},{1,3},{2,0},{3,1},{4,6},{5,7},{6,4},{7,5},{8,10},{9,11},{10,... | collective-permute-start | bytes 393224 | tf_op jit(solution)/shard_map/ppermute | solution.py:275
  51.8 0.0 collective-permute-done.16.refs_4_
  51.8 6.9 %collective-permute-start.10 = (bf16[512,128]{1,0:T(8,128)(2,1)S(1)}, bf16[512,128]{1,0:T(8,128)(2,1)S(1)}, u32[]{:S(2)}, u32[]{:S(2)}) collective-permute-start(bf16[512,128]{1,0:T(8,128)(2,1)S(1)} %get-tuple-element.38), channel_id=1, source_target_pairs={{0,5},{1,4},{2,7},{3,6},{4,1},{5,0},{6,3},{7,2},{8,13},{9,12},{10,... | collective-permute-start | bytes 393224 | tf_op jit(solution)/shard_map/ppermute | solution.py:275
  58.7 0.0 collective-permute-done.17.refs_5_
  58.7 0.4 collective-permute-start.11
  59.2 4.1 %shard_map.81 = (bf16[512,256]{1,0:T(8,128)(2,1)S(1)}, bf16[512,256]{1,0:T(8,128)(2,1)S(1)}, bf16[512,256]{1,0:T(8,128)(2,1)S(1)}, bf16[512,256]{1,0:T(8,128)(2,1)S(1)}) custom-call(s32[2]{0:T(128)S(1)} %pad_add_fusion.where, bf16[512,128]{1,0:T(8,128)(2,1)S(1)} %collective-permute-done.14.refs_0_, bf16[2,512,128]{2,1,0:T(8,128)(2,1)S(1)} %collective-permute-done.1.refs_1_, ...), custom_call_target="tpu_custom_call" | custom-call | flops 1207959552 | bytes 7340040 | tf_op jit(solution)/shard_map/pallas_call | solution.py:251
  63.3 0.0 collective-permute-done.7.refs_0_
  63.3 1.6 %collective-permute-start.18 = (bf16[512,256]{1,0:T(8,128)(2,1)S(1)}, bf16[512,256]{1,0:T(8,128)(2,1)S(1)}, u32[]{:S(2)}, u32[]{:S(2)}) collective-permute-start(bf16[512,256]{1,0:T(8,128)(2,1)S(1)} %get-tuple-element.48), channel_id=1, source_target_pairs={{0,16},{8,24},{16,0},{24,8},{1,17},{9,25},{17,1},{25,9},{2,18},{10... | collective-permute-start | bytes 786440 | tf_op jit(solution)/shard_map/ppermute | solution.py:275
  64.9 2.5 %collective-permute-done.8.refs_1_ = bf16[512,128]{1,0:T(8,128)(2,1)S(1)} collective-permute-done((bf16[512,128]{1,0:T(8,128)(2,1)S(1)}, bf16[512,128]{1,0:T(8,128)(2,1)S(1)}, u32[]{:S(2)}, u32[]{:S(2)}) %collective-permute-start.8) | collective-permute-done | bytes 131104 | tf_op jit(solution)/shard_map/ppermute | solution.py:275
  67.3 0.0 collective-permute-start.19
  67.3 0.0 collective-permute-done.9.refs_2_
  67.3 1.6 %collective-permute-start.20 = (bf16[512,256]{1,0:T(8,128)(2,1)S(1)}, bf16[512,256]{1,0:T(8,128)(2,1)S(1)}, u32[]{:S(2)}, u32[]{:S(2)}) collective-permute-start(bf16[512,256]{1,0:T(8,128)(2,1)S(1)} %get-tuple-element.50), channel_id=1, source_target_pairs={{0,8},{8,0},{16,24},{24,16},{1,9},{9,1},{17,25},{25,17},{2,10},{10... | collective-permute-start | bytes 786440 | tf_op jit(solution)/shard_map/ppermute | solution.py:275
  68.9 1.4 %collective-permute-done.10.refs_3_ = bf16[512,128]{1,0:T(8,128)(2,1)S(1)} collective-permute-done((bf16[512,128]{1,0:T(8,128)(2,1)S(1)}, bf16[512,128]{1,0:T(8,128)(2,1)S(1)}, u32[]{:S(2)}, u32[]{:S(2)}) %collective-permute-start.10) | collective-permute-done | bytes 131104 | tf_op jit(solution)/shard_map/ppermute | solution.py:275
  70.3 2.4 %collective-permute-start.12 = (bf16[512,128]{1,0:T(8,128)(2,1)S(1)}, bf16[512,128]{1,0:T(8,128)(2,1)S(1)}, u32[]{:S(2)}, u32[]{:S(2)}) collective-permute-start(bf16[512,128]{1,0:T(8,128)(2,1)S(1)} %get-tuple-element.40), channel_id=1, source_target_pairs={{0,7},{1,6},{2,5},{3,4},{4,3},{5,2},{6,1},{7,0},{8,15},{9,14},{10,... | collective-permute-start | bytes 393224 | tf_op jit(solution)/shard_map/ppermute | solution.py:275
  72.7 0.0 collective-permute-done.11.refs_4_
  72.7 2.3 %collective-permute-start.13 = (bf16[512,128]{1,0:T(8,128)(2,1)S(1)}, bf16[512,128]{1,0:T(8,128)(2,1)S(1)}, u32[]{:S(2)}, u32[]{:S(2)}) collective-permute-start(bf16[512,128]{1,0:T(8,128)(2,1)S(1)} %get-tuple-element.41), channel_id=1, source_target_pairs={{0,3},{1,2},{2,1},{3,0},{4,7},{5,6},{6,5},{7,4},{8,11},{9,10},{10,... | collective-permute-start | bytes 393224 | tf_op jit(solution)/shard_map/ppermute | solution.py:275
  75.0 4.4 %collective-permute-done.12.refs_5_ = bf16[512,128]{1,0:T(8,128)(2,1)S(1)} collective-permute-done((bf16[512,128]{1,0:T(8,128)(2,1)S(1)}, bf16[512,128]{1,0:T(8,128)(2,1)S(1)}, u32[]{:S(2)}, u32[]{:S(2)}) %collective-permute-start.12) | collective-permute-done | bytes 131104 | tf_op jit(solution)/shard_map/ppermute | solution.py:275
  79.4 0.7 collective-permute-done.13.refs_6_
  80.1 1.6 %shard_map.80 = bf16[8,512,128]{2,1,0:T(8,128)(2,1)} custom-call(s32[2]{0:T(128)S(1)} %pad_add_fusion.where, bf16[512,128]{1,0:T(8,128)(2,1)S(1)} %collective-permute-done.7.refs_0_, bf16[512,128]{1,0:T(8,128)(2,1)S(1)} %collective-permute-done.8.refs_1_, bf16[512,128]{1,0:T(8,128)(2,1)S(1)} %collective-permute-done.9.refs_2_, ...), custom_call_target="tpu_custom_call" | custom-call | bytes 2097160 | tf_op jit(solution)/shard_map/pallas_call | solution.py:251
  81.6 0.0 collective-permute-done.18
  81.6 0.0 collective-permute-done.19
  81.6 0.0 collective-permute-done.20
  81.6 0.9 %add_multiply_fusion = f32[512,256]{1,0:T(8,128)} fusion(bf16[512,256]{1,0:T(8,128)(2,1)S(1)} %get-tuple-element.51, bf16[512,256]{1,0:T(8,128)(2,1)S(1)} %collective-permute-done.20, bf16[512,256]{1,0:T(8,128)(2,1)S(1)} %collective-permute-done.19, bf16[512,256]{1,0:T(8,128)(2,1)S(1)} %collective-permute-done.18), kind=kLoop, calls=%fused_computation | loop fusion | flops 1048576 | bytes 1572864 | tf_op jit(solution)/shard_map/mul | solution.py:328
Async XLA Ops:
  0.6 33.4 %copy-start = (bf16[9,256,256]{2,1,0:T(8,128)(2,1)S(1)}, bf16[9,256,256]{2,1,0:T(8,128)(2,1)}, u32[]{:S(2)}) copy-start(bf16[9,256,256]{2,1,0:T(8,128)(2,1)} %constant.14.clone.forward.refs_9_) | copy-start | bytes 3538948
  3.4 14.1 %collective-permute-start = (bf16[512,128]{1,0:T(8,128)(2,1)S(1)}, bf16[512,128]{1,0:T(8,128)(2,1)S(1)}, u32[]{:S(2)}, u32[]{:S(2)}) collective-permute-start(bf16[512,128]{1,0:T(8,128)(2,1)S(1)} %get-tuple-element.27), channel_id=1, source_target_pairs={{0,4},{1,5},{2,6},{3,7},{4,0},{5,1},{6,2},{7,3},{8,12},{9,13},{10,... | collective-permute-start | bytes 393224 | tf_op jit(solution)/shard_map/ppermute | solution.py:275
  7.5 12.9 %collective-permute-start.2 = (bf16[512,128]{1,0:T(8,128)(2,1)S(1)}, bf16[512,128]{1,0:T(8,128)(2,1)S(1)}, u32[]{:S(2)}, u32[]{:S(2)}) collective-permute-start(bf16[512,128]{1,0:T(8,128)(2,1)S(1)} %get-tuple-element.29), channel_id=1, source_target_pairs={{0,5},{1,4},{2,7},{3,6},{4,1},{5,0},{6,3},{7,2},{8,13},{9,12},{10,... | collective-permute-start | bytes 393224 | tf_op jit(solution)/shard_map/ppermute | solution.py:275
  8.8 28.3 %collective-permute-start.1 = (bf16[2,512,128]{2,1,0:T(8,128)(2,1)S(1)}, bf16[2,512,128]{2,1,0:T(8,128)(2,1)S(1)}, u32[]{:S(2)}, u32[]{:S(2)}) collective-permute-start(bf16[2,512,128]{2,1,0:T(8,128)(2,1)S(1)} %get-tuple-element.28), channel_id=1, source_target_pairs={{0,1},{1,0},{2,3},{3,2},{4,5},{5,4},{6,7},{7,6},{8,9},{9,8},{10,11... | collective-permute-start | bytes 786440 | tf_op jit(solution)/shard_map/ppermute | solution.py:275
  9.0 32.6 %collective-permute-start.3 = (bf16[2,512,128]{2,1,0:T(8,128)(2,1)S(1)}, bf16[2,512,128]{2,1,0:T(8,128)(2,1)S(1)}, u32[]{:S(2)}, u32[]{:S(2)}) collective-permute-start(bf16[2,512,128]{2,1,0:T(8,128)(2,1)S(1)} %get-tuple-element.30), channel_id=1, source_target_pairs={{0,2},{1,3},{2,0},{3,1},{4,6},{5,7},{6,4},{7,5},{8,10},{9,11},{10,... | collective-permute-start | bytes 786440 | tf_op jit(solution)/shard_map/ppermute | solution.py:275
  10.9 30.7 %collective-permute-start.6 = (bf16[2,512,128]{2,1,0:T(8,128)(2,1)S(1)}, bf16[2,512,128]{2,1,0:T(8,128)(2,1)S(1)}, u32[]{:S(2)}, u32[]{:S(2)}) collective-permute-start(bf16[2,512,128]{2,1,0:T(8,128)(2,1)S(1)} %get-tuple-element.33), channel_id=1, source_target_pairs={{0,3},{1,2},{2,1},{3,0},{4,7},{5,6},{6,5},{7,4},{8,11},{9,10},{10,... | collective-permute-start | bytes 786440 | tf_op jit(solution)/shard_map/ppermute | solution.py:275
  17.5 13.3 %collective-permute-start.4 = (bf16[512,128]{1,0:T(8,128)(2,1)S(1)}, bf16[512,128]{1,0:T(8,128)(2,1)S(1)}, u32[]{:S(2)}, u32[]{:S(2)}) collective-permute-start(bf16[512,128]{1,0:T(8,128)(2,1)S(1)} %get-tuple-element.31), channel_id=1, source_target_pairs={{0,6},{1,7},{2,4},{3,5},{4,2},{5,3},{6,0},{7,1},{8,14},{9,15},{10,... | collective-permute-start | bytes 393224 | tf_op jit(solution)/shard_map/ppermute | solution.py:275
  20.4 12.3 %collective-permute-start.5 = (bf16[512,128]{1,0:T(8,128)(2,1)S(1)}, bf16[512,128]{1,0:T(8,128)(2,1)S(1)}, u32[]{:S(2)}, u32[]{:S(2)}) collective-permute-start(bf16[512,128]{1,0:T(8,128)(2,1)S(1)} %get-tuple-element.32), channel_id=1, source_target_pairs={{0,7},{1,6},{2,5},{3,4},{4,3},{5,2},{6,1},{7,0},{8,15},{9,14},{10,... | collective-permute-start | bytes 393224 | tf_op jit(solution)/shard_map/ppermute | solution.py:275
  30.8 16.8 %collective-permute-start.14 = (bf16[512,128]{1,0:T(8,128)(2,1)S(1)}, bf16[512,128]{1,0:T(8,128)(2,1)S(1)}, u32[]{:S(2)}, u32[]{:S(2)}) collective-permute-start(bf16[512,128]{1,0:T(8,128)(2,1)S(1)} %get-tuple-element.43), channel_id=1, source_target_pairs={{0,4},{1,5},{2,6},{3,7},{4,0},{5,1},{6,2},{7,3},{8,12},{9,13},{10,... | collective-permute-start | bytes 393224 | tf_op jit(solution)/shard_map/ppermute | solution.py:275
  32.8 8.8 %copy-start.1 = (bf16[9,256,256]{2,1,0:T(8,128)(2,1)S(1)}, bf16[9,256,256]{2,1,0:T(8,128)(2,1)}, u32[]{:S(2)}) copy-start(bf16[9,256,256]{2,1,0:T(8,128)(2,1)} %constant.15.clone.refs_10_) | copy-start | bytes 3538948
  32.8 17.9 %collective-permute-start.15 = (bf16[512,128]{1,0:T(8,128)(2,1)S(1)}, bf16[512,128]{1,0:T(8,128)(2,1)S(1)}, u32[]{:S(2)}, u32[]{:S(2)}) collective-permute-start(bf16[512,128]{1,0:T(8,128)(2,1)S(1)} %get-tuple-element.44), channel_id=1, source_target_pairs={{0,5},{1,4},{2,7},{3,6},{4,1},{5,0},{6,3},{7,2},{8,13},{9,12},{10,... | collective-permute-start | bytes 393224 | tf_op jit(solution)/shard_map/ppermute | solution.py:275
  34.0 1.6 %copy-start.2 = (f32[512,1024]{1,0:T(8,128)S(1)}, f32[512,1024]{1,0:T(8,128)}, u32[]{:S(2)}) copy-start(f32[512,1024]{1,0:T(8,128)} %taps.1) | copy-start | bytes 6291460
  37.1 14.7 %collective-permute-start.16 = (bf16[512,128]{1,0:T(8,128)(2,1)S(1)}, bf16[512,128]{1,0:T(8,128)(2,1)S(1)}, u32[]{:S(2)}, u32[]{:S(2)}) collective-permute-start(bf16[512,128]{1,0:T(8,128)(2,1)S(1)} %get-tuple-element.45), channel_id=1, source_target_pairs={{0,6},{1,7},{2,4},{3,5},{4,2},{5,3},{6,0},{7,1},{8,14},{9,15},{10,... | collective-permute-start | bytes 393224 | tf_op jit(solution)/shard_map/ppermute | solution.py:275
  41.6 17.1 %collective-permute-start.17 = (bf16[512,128]{1,0:T(8,128)(2,1)S(1)}, bf16[512,128]{1,0:T(8,128)(2,1)S(1)}, u32[]{:S(2)}, u32[]{:S(2)}) collective-permute-start(bf16[512,128]{1,0:T(8,128)(2,1)S(1)} %get-tuple-element.46), channel_id=1, source_target_pairs={{0,7},{1,6},{2,5},{3,4},{4,3},{5,2},{6,1},{7,0},{8,15},{9,14},{10,... | collective-permute-start | bytes 393224 | tf_op jit(solution)/shard_map/ppermute | solution.py:275
  45.9 17.4 %collective-permute-start.7 = (bf16[512,128]{1,0:T(8,128)(2,1)S(1)}, bf16[512,128]{1,0:T(8,128)(2,1)S(1)}, u32[]{:S(2)}, u32[]{:S(2)}) collective-permute-start(bf16[512,128]{1,0:T(8,128)(2,1)S(1)} %get-tuple-element.35), channel_id=1, source_target_pairs={{0,1},{1,0},{2,3},{3,2},{4,5},{5,4},{6,7},{7,6},{8,9},{9,8},{10,11... | collective-permute-start | bytes 393224 | tf_op jit(solution)/shard_map/ppermute | solution.py:275
  47.7 19.7 %collective-permute-start.8 = (bf16[512,128]{1,0:T(8,128)(2,1)S(1)}, bf16[512,128]{1,0:T(8,128)(2,1)S(1)}, u32[]{:S(2)}, u32[]{:S(2)}) collective-permute-start(bf16[512,128]{1,0:T(8,128)(2,1)S(1)} %get-tuple-element.36), channel_id=1, source_target_pairs={{0,4},{1,5},{2,6},{3,7},{4,0},{5,1},{6,2},{7,3},{8,12},{9,13},{10,... | collective-permute-start | bytes 393224 | tf_op jit(solution)/shard_map/ppermute | solution.py:275
  50.7 16.7 %collective-permute-start.9 = (bf16[512,128]{1,0:T(8,128)(2,1)S(1)}, bf16[512,128]{1,0:T(8,128)(2,1)S(1)}, u32[]{:S(2)}, u32[]{:S(2)}) collective-permute-start(bf16[512,128]{1,0:T(8,128)(2,1)S(1)} %get-tuple-element.37), channel_id=1, source_target_pairs={{0,2},{1,3},{2,0},{3,1},{4,6},{5,7},{6,4},{7,5},{8,10},{9,11},{10,... | collective-permute-start | bytes 393224 | tf_op jit(solution)/shard_map/ppermute | solution.py:275
  51.8 18.5 %collective-permute-start.10 = (bf16[512,128]{1,0:T(8,128)(2,1)S(1)}, bf16[512,128]{1,0:T(8,128)(2,1)S(1)}, u32[]{:S(2)}, u32[]{:S(2)}) collective-permute-start(bf16[512,128]{1,0:T(8,128)(2,1)S(1)} %get-tuple-element.38), channel_id=1, source_target_pairs={{0,5},{1,4},{2,7},{3,6},{4,1},{5,0},{6,3},{7,2},{8,13},{9,12},{10,... | collective-permute-start | bytes 393224 | tf_op jit(solution)/shard_map/ppermute | solution.py:275
  58.7 14.0 %collective-permute-start.11 = (bf16[512,128]{1,0:T(8,128)(2,1)S(1)}, bf16[512,128]{1,0:T(8,128)(2,1)S(1)}, u32[]{:S(2)}, u32[]{:S(2)}) collective-permute-start(bf16[512,128]{1,0:T(8,128)(2,1)S(1)} %get-tuple-element.39), channel_id=1, source_target_pairs={{0,6},{1,7},{2,4},{3,5},{4,2},{5,3},{6,0},{7,1},{8,14},{9,15},{10,... | collective-permute-start | bytes 393224 | tf_op jit(solution)/shard_map/ppermute | solution.py:275
  63.3 18.3 %collective-permute-start.18 = (bf16[512,256]{1,0:T(8,128)(2,1)S(1)}, bf16[512,256]{1,0:T(8,128)(2,1)S(1)}, u32[]{:S(2)}, u32[]{:S(2)}) collective-permute-start(bf16[512,256]{1,0:T(8,128)(2,1)S(1)} %get-tuple-element.48), channel_id=1, source_target_pairs={{0,16},{8,24},{16,0},{24,8},{1,17},{9,25},{17,1},{25,9},{2,18},{10... | collective-permute-start | bytes 786440 | tf_op jit(solution)/shard_map/ppermute | solution.py:275
  67.3 14.3 %collective-permute-start.19 = (bf16[512,256]{1,0:T(8,128)(2,1)S(1)}, bf16[512,256]{1,0:T(8,128)(2,1)S(1)}, u32[]{:S(2)}, u32[]{:S(2)}) collective-permute-start(bf16[512,256]{1,0:T(8,128)(2,1)S(1)} %get-tuple-element.49), channel_id=1, source_target_pairs={{0,24},{8,16},{16,8},{24,0},{1,25},{9,17},{17,9},{25,1},{2,26},{10... | collective-permute-start | bytes 786440 | tf_op jit(solution)/shard_map/ppermute | solution.py:275
  67.3 14.3 %collective-permute-start.20 = (bf16[512,256]{1,0:T(8,128)(2,1)S(1)}, bf16[512,256]{1,0:T(8,128)(2,1)S(1)}, u32[]{:S(2)}, u32[]{:S(2)}) collective-permute-start(bf16[512,256]{1,0:T(8,128)(2,1)S(1)} %get-tuple-element.50), channel_id=1, source_target_pairs={{0,8},{8,0},{16,24},{24,16},{1,9},{9,1},{17,25},{25,17},{2,10},{10... | collective-permute-start | bytes 786440 | tf_op jit(solution)/shard_map/ppermute | solution.py:275
  70.3 9.1 %collective-permute-start.12 = (bf16[512,128]{1,0:T(8,128)(2,1)S(1)}, bf16[512,128]{1,0:T(8,128)(2,1)S(1)}, u32[]{:S(2)}, u32[]{:S(2)}) collective-permute-start(bf16[512,128]{1,0:T(8,128)(2,1)S(1)} %get-tuple-element.40), channel_id=1, source_target_pairs={{0,7},{1,6},{2,5},{3,4},{4,3},{5,2},{6,1},{7,0},{8,15},{9,14},{10,... | collective-permute-start | bytes 393224 | tf_op jit(solution)/shard_map/ppermute | solution.py:275
  72.7 7.3 %collective-permute-start.13 = (bf16[512,128]{1,0:T(8,128)(2,1)S(1)}, bf16[512,128]{1,0:T(8,128)(2,1)S(1)}, u32[]{:S(2)}, u32[]{:S(2)}) collective-permute-start(bf16[512,128]{1,0:T(8,128)(2,1)S(1)} %get-tuple-element.41), channel_id=1, source_target_pairs={{0,3},{1,2},{2,1},{3,0},{4,7},{5,6},{6,5},{7,4},{8,11},{9,10},{10,... | collective-permute-start | bytes 393224 | tf_op jit(solution)/shard_map/ppermute | solution.py:275

commit v15 on v11

--- a/solution.py
+++ b/solution.py
@@ -168,10 +168,18 @@
         copy.wait()
 
 
-def place_kernel(order, where, *refs):
-    pieces, whole = refs[:-1], refs[-1]
-    for k, piece in zip(order, pieces):
-        whole[lax.bitwise_xor(where[0], k)] = piece[...]
+def finish_kernel(order, scale, where, *refs):
+    pieces, shares, (whole, total, sems) = refs[: len(order)], refs[len(order) : -3], refs[-3:]
+    copies = []
+    for i, k in enumerate(order):
+        copies.append(pltpu.make_async_copy(pieces[i], whole.at[lax.bitwise_xor(where[0], k)], sems.at[i]))
+        copies[-1].start()
+    added = shares[0][...].astype(jnp.float32)
+    for share in shares[1:]:
+        added = added + share[...].astype(jnp.float32)
+    total[...] = added * scale
+    for copy in copies:
+        copy.wait()
 
 
 def taps_kernel(taps, forward, taps_spec, mid):
@@ -283,7 +291,7 @@
     channels, span = saved_input.shape[1:]
     rows, length = long_filter.shape
     width = length // BLOCKS
-    grad_order, input_order, back_order = (spread(count, o) for o in ((1, 2, 4, 5, 6, 7, 3), (4, 5, 1, 6, 2, 7, 3), (1, 2, 3, 4, 5, 6, 7)))
+    grad_order, input_order, back_order = (spread(count, o) for o in ((4, 1, 5, 2, 6, 3, 7), (4, 1, 5, 2, 6, 3, 7), (1, 4, 5, 6, 7, 2, 3)))
     late = 2
     at = count - 1 - late
     every = range(count + 8)
@@ -333,11 +341,12 @@
     )
     cross_blocks = exchange(cross, far_first(shares), "dp", shares)
     scale = 1.0 / math.sqrt(shares * length)
-    grad_filter = sum(x.astype(full) for x in cross_blocks) * scale
-    (whole,) = call(
-        functools.partial(place_kernel, back_order),
-        [where, *back_blocks],
-        [jax.ShapeDtypeStruct((count, rows, span), half)],
+    whole, grad_filter = call(
+        functools.partial(finish_kernel, back_order, scale),
+        [where, *back_blocks, *cross_blocks],
+        [jax.ShapeDtypeStruct((count, rows, span), half), jax.ShapeDtypeStruct((rows, length // shares), full)],
+        [sems((count,))],
+        out_streams=(0,),
     )
     return (whole.reshape(1, channels, span), grad_filter)
 

time: 84.2 us -> 84.1 us (level)
  the two profiles are of different devices: /device:TPU:9 before, /device:TPU:0 now
where the time goes in v15:
time: 84.1 us; the launch traced here: 83.7 us
  starting transfers between devices  48.5 us (58%)
  waiting for transfers between devices  18 us (21%)
  Pallas kernels  14.8 us (18%)
  local copies, waits for them, and re-layouts  1.6 us (2%)
    ppermute x24, starting transfers between devices, exchange(): lax.ppermute(piece, axis, [(i, i ^ k) for i in range(size)])  48.5 us
    ppermute x24, waiting for transfers between devices, exchange(): lax.ppermute(piece, axis, [(i, i ^ k) for i in range(size)])  18 us
    pallas_call x5, Pallas kernels, call(): pl.pallas_call(kernel, out_shape=list(outs), in_specs=specs, out_specs=[s...  14.8 us
  transfers between devices with their start and end apart: 24, of which 8 were waited for; matrix products, arithmetic and copies ran while one was open for 0% of the time, Pallas kernels for 12%

profile of v15, /device:TPU:0, one launch (start us, length us, event | category | flops | bytes accessed | tf_op | source)
XLA Modules:
  0.0 83.7 jit_solution(10053153846448264688)
XLA Ops:
  0.6 0.0 copy-start
  0.6 0.1 pad_add_fusion.where
  0.7 2.7 %shard_map.77 = (bf16[512,128]{1,0:T(8,128)(2,1)S(1)}, bf16[512,128]{1,0:T(8,128)(2,1)S(1)}, bf16[512,128]{1,0:T(8,128)(2,1)S(1)}, bf16[512,128]{1,0:T(8,128)(2,...) custom-call(s32[2]{0:T(128)S(1)} %pad_add_fusion.where, ...), custom_call_target="tpu_custom_call" | custom-call | bytes 5242888 | tf_op jit(solution)/shard_map/pallas_call | solution.py:260
  3.4 4.1 %collective-permute-start = (bf16[512,128]{1,0:T(8,128)(2,1)S(1)}, bf16[512,128]{1,0:T(8,128)(2,1)S(1)}, u32[]{:S(2)}, u32[]{:S(2)}) collective-permute-start(bf16[512,128]{1,0:T(8,128)(2,1)S(1)} %get-tuple-element.35), channel_id=1, source_target_pairs={{0,4},{1,5},{2,6},{3,7},{4,0},{5,1},{6,2},{7,3},{8,12},{9,13},{10,... | collective-permute-start | bytes 393224 | tf_op jit(solution)/shard_map/ppermute | solution.py:285
  7.5 1.5 %collective-permute-start.1 = (bf16[512,128]{1,0:T(8,128)(2,1)S(1)}, bf16[512,128]{1,0:T(8,128)(2,1)S(1)}, u32[]{:S(2)}, u32[]{:S(2)}) collective-permute-start(bf16[512,128]{1,0:T(8,128)(2,1)S(1)} %get-tuple-element.36), channel_id=1, source_target_pairs={{0,1},{1,0},{2,3},{3,2},{4,5},{5,4},{6,7},{7,6},{8,9},{9,8},{10,11... | collective-permute-start | bytes 393224 | tf_op jit(solution)/shard_map/ppermute | solution.py:285
  9.0 0.0 collective-permute-start.2
  9.0 1.8 %collective-permute-start.3 = (bf16[512,128]{1,0:T(8,128)(2,1)S(1)}, bf16[512,128]{1,0:T(8,128)(2,1)S(1)}, u32[]{:S(2)}, u32[]{:S(2)}) collective-permute-start(bf16[512,128]{1,0:T(8,128)(2,1)S(1)} %get-tuple-element.38), channel_id=1, source_target_pairs={{0,2},{1,3},{2,0},{3,1},{4,6},{5,7},{6,4},{7,5},{8,10},{9,11},{10,... | collective-permute-start | bytes 393224 | tf_op jit(solution)/shard_map/ppermute | solution.py:285
  10.9 2.5 %collective-permute-start.4 = (bf16[512,128]{1,0:T(8,128)(2,1)S(1)}, bf16[512,128]{1,0:T(8,128)(2,1)S(1)}, u32[]{:S(2)}, u32[]{:S(2)}) collective-permute-start(bf16[512,128]{1,0:T(8,128)(2,1)S(1)} %get-tuple-element.39), channel_id=1, source_target_pairs={{0,6},{1,7},{2,4},{3,5},{4,2},{5,3},{6,0},{7,1},{8,14},{9,15},{10,... | collective-permute-start | bytes 393224 | tf_op jit(solution)/shard_map/ppermute | solution.py:285
  13.4 4.8 %collective-permute-done.refs_0_ = bf16[512,128]{1,0:T(8,128)(2,1)S(1)} collective-permute-done((bf16[512,128]{1,0:T(8,128)(2,1)S(1)}, bf16[512,128]{1,0:T(8,128)(2,1)S(1)}, u32[]{:S(2)}, u32[]{:S(2)}) %collective-permute-start) | collective-permute-done | bytes 131104 | tf_op jit(solution)/shard_map/ppermute | solution.py:285
  18.2 1.1 %collective-permute-start.5 = (bf16[512,128]{1,0:T(8,128)(2,1)S(1)}, bf16[512,128]{1,0:T(8,128)(2,1)S(1)}, u32[]{:S(2)}, u32[]{:S(2)}) collective-permute-start(bf16[512,128]{1,0:T(8,128)(2,1)S(1)} %get-tuple-element.40), channel_id=1, source_target_pairs={{0,3},{1,2},{2,1},{3,0},{4,7},{5,6},{6,5},{7,4},{8,11},{9,10},{10,... | collective-permute-start | bytes 393224 | tf_op jit(solution)/shard_map/ppermute | solution.py:285
  19.3 0.0 collective-permute-done.1.refs_1_
  19.3 4.2 %collective-permute-start.6 = (bf16[512,128]{1,0:T(8,128)(2,1)S(1)}, bf16[512,128]{1,0:T(8,128)(2,1)S(1)}, u32[]{:S(2)}, u32[]{:S(2)}) collective-permute-start(bf16[512,128]{1,0:T(8,128)(2,1)S(1)} %get-tuple-element.41), channel_id=1, source_target_pairs={{0,7},{1,6},{2,5},{3,4},{4,3},{5,2},{6,1},{7,0},{8,15},{9,14},{10,... | collective-permute-start | bytes 393224 | tf_op jit(solution)/shard_map/ppermute | solution.py:285
  23.6 0.8 collective-permute-done.2.refs_2_
  24.4 0.0 collective-permute-start.14
  24.4 0.0 collective-permute-done.3.refs_3_
  24.4 0.0 copy-start.1
  24.4 0.9 %collective-permute-start.15 = (bf16[512,128]{1,0:T(8,128)(2,1)S(1)}, bf16[512,128]{1,0:T(8,128)(2,1)S(1)}, u32[]{:S(2)}, u32[]{:S(2)}) collective-permute-start(bf16[512,128]{1,0:T(8,128)(2,1)S(1)} %get-tuple-element.54), channel_id=1, source_target_pairs={{0,1},{1,0},{2,3},{3,2},{4,5},{5,4},{6,7},{7,6},{8,9},{9,8},{10,11... | collective-permute-start | bytes 393224 | tf_op jit(solution)/shard_map/ppermute | solution.py:285
  25.3 0.0 copy-done
  25.3 0.0 copy-start.2
  25.3 1.6 %copy-done.2 = f32[512,1024]{1,0:T(8,128)S(1)} copy-done((f32[512,1024]{1,0:T(8,128)S(1)}, f32[512,1024]{1,0:T(8,128)}, u32[]{:S(2)}) %copy-start.2) | copy-done | bytes 2097176
  26.9 1.5 %shard_map.78.refs_10_ = bf16[9,512,256]{2,1,0:T(8,128)(2,1)S(1)} custom-call(f32[512,1024]{1,0:T(8,128)S(1)} %copy-done.2, bf16[9,256,256]{2,1,0:T(8,128)(2,1)S(1)} %copy-done), custom_call_target="tpu_custom_call" | custom-call | flops 603979776 | bytes 5636096 | tf_op jit(solution)/shard_map/pallas_call | solution.py:260
  28.3 0.0 collective-permute-done.4.refs_4_
  28.3 6.1 %collective-permute-start.16 = (bf16[512,128]{1,0:T(8,128)(2,1)S(1)}, bf16[512,128]{1,0:T(8,128)(2,1)S(1)}, u32[]{:S(2)}, u32[]{:S(2)}) collective-permute-start(bf16[512,128]{1,0:T(8,128)(2,1)S(1)} %get-tuple-element.55), channel_id=1, source_target_pairs={{0,5},{1,4},{2,7},{3,6},{4,1},{5,0},{6,3},{7,2},{8,13},{9,12},{10,... | collective-permute-start | bytes 393224 | tf_op jit(solution)/shard_map/ppermute | solution.py:285
  34.4 0.0 collective-permute-done.5.refs_5_
  34.4 0.0 collective-permute-start.17
  34.4 0.0 collective-permute-done.6.refs_6_
  34.4 1.4 %collective-permute-start.18 = (bf16[512,128]{1,0:T(8,128)(2,1)S(1)}, bf16[512,128]{1,0:T(8,128)(2,1)S(1)}, u32[]{:S(2)}, u32[]{:S(2)}) collective-permute-start(bf16[512,128]{1,0:T(8,128)(2,1)S(1)} %get-tuple-element.57), channel_id=1, source_target_pairs={{0,6},{1,7},{2,4},{3,5},{4,2},{5,3},{6,0},{7,1},{8,14},{9,15},{10,... | collective-permute-start | bytes 393224 | tf_op jit(solution)/shard_map/ppermute | solution.py:285
  35.8 0.0 copy-done.1
  35.8 4.2 %shard_map.79 = (bf16[512,128]{1,0:T(8,128)(2,1)S(1)}, bf16[512,128]{1,0:T(8,128)(2,1)S(1)}, bf16[512,128]{1,0:T(8,128)(2,1)S(1)}, bf16[512,128]{1,0:T(8,128)(2,...) custom-call(s32[2]{0:T(128)S(1)} %pad_add_fusion.where, ...), custom_call_target="tpu_custom_call", output_to_operand_aliasing={{0}: (9, {}), {1}: (10, {})} | custom-call | flops 1207959552 | bytes 9699336 | tf_op jit(solution)/shard_map/pallas_call | solution.py:260
  40.0 0.7 collective-permute-done.14.refs_0_
  40.8 1.2 %collective-permute-start.19 = (bf16[512,128]{1,0:T(8,128)(2,1)S(1)}, bf16[512,128]{1,0:T(8,128)(2,1)S(1)}, u32[]{:S(2)}, u32[]{:S(2)}) collective-permute-start(bf16[512,128]{1,0:T(8,128)(2,1)S(1)} %get-tuple-element.58), channel_id=1, source_target_pairs={{0,3},{1,2},{2,1},{3,0},{4,7},{5,6},{6,5},{7,4},{8,11},{9,10},{10,... | collective-permute-start | bytes 393224 | tf_op jit(solution)/shard_map/ppermute | solution.py:285
  42.0 0.0 collective-permute-done.15.refs_1_
  42.0 3.8 %collective-permute-start.20 = (bf16[512,128]{1,0:T(8,128)(2,1)S(1)}, bf16[512,128]{1,0:T(8,128)(2,1)S(1)}, u32[]{:S(2)}, u32[]{:S(2)}) collective-permute-start(bf16[512,128]{1,0:T(8,128)(2,1)S(1)} %get-tuple-element.59), channel_id=1, source_target_pairs={{0,7},{1,6},{2,5},{3,4},{4,3},{5,2},{6,1},{7,0},{8,15},{9,14},{10,... | collective-permute-start | bytes 393224 | tf_op jit(solution)/shard_map/ppermute | solution.py:285
  45.8 1.9 %collective-permute-done.16.refs_2_ = bf16[512,128]{1,0:T(8,128)(2,1)S(1)} collective-permute-done((bf16[512,128]{1,0:T(8,128)(2,1)S(1)}, bf16[512,128]{1,0:T(8,128)(2,1)S(1)}, u32[]{:S(2)}, u32[]{:S(2)}) %collective-permute-start.16) | collective-permute-done | bytes 131104 | tf_op jit(solution)/shard_map/ppermute | solution.py:285
  47.7 0.0 collective-permute-start.7
  47.7 0.0 collective-permute-done.17.refs_3_
  47.7 1.4 %collective-permute-start.8 = (bf16[512,128]{1,0:T(8,128)(2,1)S(1)}, bf16[512,128]{1,0:T(8,128)(2,1)S(1)}, u32[]{:S(2)}, u32[]{:S(2)}) collective-permute-start(bf16[512,128]{1,0:T(8,128)(2,1)S(1)} %get-tuple-element.46), channel_id=1, source_target_pairs={{0,4},{1,5},{2,6},{3,7},{4,0},{5,1},{6,2},{7,3},{8,12},{9,13},{10,... | collective-permute-start | bytes 393224 | tf_op jit(solution)/shard_map/ppermute | solution.py:285
  49.1 0.0 collective-permute-done.18.refs_4_
  49.1 7.8 %collective-permute-start.9 = (bf16[512,128]{1,0:T(8,128)(2,1)S(1)}, bf16[512,128]{1,0:T(8,128)(2,1)S(1)}, u32[]{:S(2)}, u32[]{:S(2)}) collective-permute-start(bf16[512,128]{1,0:T(8,128)(2,1)S(1)} %get-tuple-element.47), channel_id=1, source_target_pairs={{0,5},{1,4},{2,7},{3,6},{4,1},{5,0},{6,3},{7,2},{8,13},{9,12},{10,... | collective-permute-start | bytes 393224 | tf_op jit(solution)/shard_map/ppermute | solution.py:285
  56.9 0.0 collective-permute-done.19.refs_5_
  56.9 0.4 collective-permute-start.10
  57.4 0.0 collective-permute-done.20.refs_6_
  57.4 3.4 %collective-permute-start.11 = (bf16[512,128]{1,0:T(8,128)(2,1)S(1)}, bf16[512,128]{1,0:T(8,128)(2,1)S(1)}, u32[]{:S(2)}, u32[]{:S(2)}) collective-permute-start(bf16[512,128]{1,0:T(8,128)(2,1)S(1)} %get-tuple-element.49), channel_id=1, source_target_pairs={{0,7},{1,6},{2,5},{3,4},{4,3},{5,2},{6,1},{7,0},{8,15},{9,14},{10,... | collective-permute-start | bytes 393224 | tf_op jit(solution)/shard_map/ppermute | solution.py:285
  60.7 4.1 %shard_map.80 = (bf16[512,256]{1,0:T(8,128)(2,1)S(1)}, bf16[512,256]{1,0:T(8,128)(2,1)S(1)}, bf16[512,256]{1,0:T(8,128)(2,1)S(1)}, bf16[512,256]{1,0:T(8,128)(2,1)S(1)}) custom-call(s32[2]{0:T(128)S(1)} %pad_add_fusion.where, bf16[512,128]{1,0:T(8,128)(2,1)S(1)} %collective-permute-done.14.refs_0_, bf16[512,128]{1,0:T(8,128)(2,1)S(1)} %collective-permute-done.15.refs_1_, ...), custom_call_target="tpu_custom_call" | custom-call | flops 1207959552 | bytes 6815752 | tf_op jit(solution)/shard_map/pallas_call | solution.py:260
  64.8 0.0 collective-permute-done.7.refs_0_
  64.8 1.6 %collective-permute-start.21 = (bf16[512,256]{1,0:T(8,128)(2,1)S(1)}, bf16[512,256]{1,0:T(8,128)(2,1)S(1)}, u32[]{:S(2)}, u32[]{:S(2)}) collective-permute-start(bf16[512,256]{1,0:T(8,128)(2,1)S(1)} %get-tuple-element.62), channel_id=1, source_target_pairs={{0,16},{8,24},{16,0},{24,8},{1,17},{9,25},{17,1},{25,9},{2,18},{10... | collective-permute-start | bytes 786440 | tf_op jit(solution)/shard_map/ppermute | solution.py:285
  66.4 1.6 %collective-permute-done.8.refs_1_ = bf16[512,128]{1,0:T(8,128)(2,1)S(1)} collective-permute-done((bf16[512,128]{1,0:T(8,128)(2,1)S(1)}, bf16[512,128]{1,0:T(8,128)(2,1)S(1)}, u32[]{:S(2)}, u32[]{:S(2)}) %collective-permute-start.8) | collective-permute-done | bytes 131104 | tf_op jit(solution)/shard_map/ppermute | solution.py:285
  68.0 0.0 collective-permute-start.22
  68.0 4.2 %collective-permute-done.9.refs_2_ = bf16[512,128]{1,0:T(8,128)(2,1)S(1)} collective-permute-done((bf16[512,128]{1,0:T(8,128)(2,1)S(1)}, bf16[512,128]{1,0:T(8,128)(2,1)S(1)}, u32[]{:S(2)}, u32[]{:S(2)}) %collective-permute-start.9) | collective-permute-done | bytes 131104 | tf_op jit(solution)/shard_map/ppermute | solution.py:285
  72.2 0.0 collective-permute-start.23
  72.2 0.0 collective-permute-done.10.refs_3_
  72.2 2.0 %collective-permute-start.12 = (bf16[512,128]{1,0:T(8,128)(2,1)S(1)}, bf16[512,128]{1,0:T(8,128)(2,1)S(1)}, u32[]{:S(2)}, u32[]{:S(2)}) collective-permute-start(bf16[512,128]{1,0:T(8,128)(2,1)S(1)} %get-tuple-element.50), channel_id=1, source_target_pairs={{0,2},{1,3},{2,0},{3,1},{4,6},{5,7},{6,4},{7,5},{8,10},{9,11},{10,... | collective-permute-start | bytes 393224 | tf_op jit(solution)/shard_map/ppermute | solution.py:285
  74.2 0.0 collective-permute-done.11.refs_4_
  74.2 3.2 %collective-permute-start.13 = (bf16[512,128]{1,0:T(8,128)(2,1)S(1)}, bf16[512,128]{1,0:T(8,128)(2,1)S(1)}, u32[]{:S(2)}, u32[]{:S(2)}) collective-permute-start(bf16[512,128]{1,0:T(8,128)(2,1)S(1)} %get-tuple-element.51), channel_id=1, source_target_pairs={{0,3},{1,2},{2,1},{3,0},{4,7},{5,6},{6,5},{7,4},{8,11},{9,10},{10,... | collective-permute-start | bytes 393224 | tf_op jit(solution)/shard_map/ppermute | solution.py:285
  77.4 1.1 %collective-permute-done.12.refs_5_ = bf16[512,128]{1,0:T(8,128)(2,1)S(1)} collective-permute-done((bf16[512,128]{1,0:T(8,128)(2,1)S(1)}, bf16[512,128]{1,0:T(8,128)(2,1)S(1)}, u32[]{:S(2)}, u32[]{:S(2)}) %collective-permute-start.12) | collective-permute-done | bytes 131104 | tf_op jit(solution)/shard_map/ppermute | solution.py:285
  78.5 2.8 %collective-permute-done.13.refs_6_ = bf16[512,128]{1,0:T(8,128)(2,1)S(1)} collective-permute-done((bf16[512,128]{1,0:T(8,128)(2,1)S(1)}, bf16[512,128]{1,0:T(8,128)(2,1)S(1)}, u32[]{:S(2)}, u32[]{:S(2)}) %collective-permute-start.13) | collective-permute-done | bytes 131104 | tf_op jit(solution)/shard_map/ppermute | solution.py:285
  81.3 0.0 collective-permute-done.21.refs_8_
  81.3 0.0 collective-permute-done.22.refs_9_
  81.3 0.0 collective-permute-done.23.refs_10_
  81.3 2.4 %shard_map.81 = (bf16[8,512,128]{2,1,0:T(8,128)(2,1)}, f32[512,256]{1,0:T(8,128)}) custom-call(s32[2]{0:T(128)S(1)} %pad_add_fusion.where, bf16[512,128]{1,0:T(8,128)(2,1)S(1)} %collective-permute-done.7.refs_0_, bf16[512,128]{1,0:T(8,128)(2,1)S(1)} %collective-permute-done.8.refs_1_, bf16[512,128]{1,0:T(8,128)(2,1)S(1)} %collective-permute-done.9.refs_2_, ...), custom_call_target="tpu_custom_call" | custom-call | bytes 3670024 | tf_op jit(solution)/shard_map/pallas_call | solution.py:260
Async XLA Ops:
  0.6 24.6 %copy-start = (bf16[9,256,256]{2,1,0:T(8,128)(2,1)S(1)}, bf16[9,256,256]{2,1,0:T(8,128)(2,1)}, u32[]{:S(2)}) copy-start(bf16[9,256,256]{2,1,0:T(8,128)(2,1)} %constant.12.clone.forward.refs_11_.refs_9_) | copy-start | bytes 3538948
  3.4 14.8 %collective-permute-start = (bf16[512,128]{1,0:T(8,128)(2,1)S(1)}, bf16[512,128]{1,0:T(8,128)(2,1)S(1)}, u32[]{:S(2)}, u32[]{:S(2)}) collective-permute-start(bf16[512,128]{1,0:T(8,128)(2,1)S(1)} %get-tuple-element.35), channel_id=1, source_target_pairs={{0,4},{1,5},{2,6},{3,7},{4,0},{5,1},{6,2},{7,3},{8,12},{9,13},{10,... | collective-permute-start | bytes 393224 | tf_op jit(solution)/shard_map/ppermute | solution.py:285
  7.5 11.8 %collective-permute-start.1 = (bf16[512,128]{1,0:T(8,128)(2,1)S(1)}, bf16[512,128]{1,0:T(8,128)(2,1)S(1)}, u32[]{:S(2)}, u32[]{:S(2)}) collective-permute-start(bf16[512,128]{1,0:T(8,128)(2,1)S(1)} %get-tuple-element.36), channel_id=1, source_target_pairs={{0,1},{1,0},{2,3},{3,2},{4,5},{5,4},{6,7},{7,6},{8,9},{9,8},{10,11... | collective-permute-start | bytes 393224 | tf_op jit(solution)/shard_map/ppermute | solution.py:285
  9.0 15.3 %collective-permute-start.2 = (bf16[512,128]{1,0:T(8,128)(2,1)S(1)}, bf16[512,128]{1,0:T(8,128)(2,1)S(1)}, u32[]{:S(2)}, u32[]{:S(2)}) collective-permute-start(bf16[512,128]{1,0:T(8,128)(2,1)S(1)} %get-tuple-element.37), channel_id=1, source_target_pairs={{0,5},{1,4},{2,7},{3,6},{4,1},{5,0},{6,3},{7,2},{8,13},{9,12},{10,... | collective-permute-start | bytes 393224 | tf_op jit(solution)/shard_map/ppermute | solution.py:285
  9.0 15.3 %collective-permute-start.3 = (bf16[512,128]{1,0:T(8,128)(2,1)S(1)}, bf16[512,128]{1,0:T(8,128)(2,1)S(1)}, u32[]{:S(2)}, u32[]{:S(2)}) collective-permute-start(bf16[512,128]{1,0:T(8,128)(2,1)S(1)} %get-tuple-element.38), channel_id=1, source_target_pairs={{0,2},{1,3},{2,0},{3,1},{4,6},{5,7},{6,4},{7,5},{8,10},{9,11},{10,... | collective-permute-start | bytes 393224 | tf_op jit(solution)/shard_map/ppermute | solution.py:285
  10.9 17.4 %collective-permute-start.4 = (bf16[512,128]{1,0:T(8,128)(2,1)S(1)}, bf16[512,128]{1,0:T(8,128)(2,1)S(1)}, u32[]{:S(2)}, u32[]{:S(2)}) collective-permute-start(bf16[512,128]{1,0:T(8,128)(2,1)S(1)} %get-tuple-element.39), channel_id=1, source_target_pairs={{0,6},{1,7},{2,4},{3,5},{4,2},{5,3},{6,0},{7,1},{8,14},{9,15},{10,... | collective-permute-start | bytes 393224 | tf_op jit(solution)/shard_map/ppermute | solution.py:285
  18.2 16.2 %collective-permute-start.5 = (bf16[512,128]{1,0:T(8,128)(2,1)S(1)}, bf16[512,128]{1,0:T(8,128)(2,1)S(1)}, u32[]{:S(2)}, u32[]{:S(2)}) collective-permute-start(bf16[512,128]{1,0:T(8,128)(2,1)S(1)} %get-tuple-element.40), channel_id=1, source_target_pairs={{0,3},{1,2},{2,1},{3,0},{4,7},{5,6},{6,5},{7,4},{8,11},{9,10},{10,... | collective-permute-start | bytes 393224 | tf_op jit(solution)/shard_map/ppermute | solution.py:285
  19.3 15.1 %collective-permute-start.6 = (bf16[512,128]{1,0:T(8,128)(2,1)S(1)}, bf16[512,128]{1,0:T(8,128)(2,1)S(1)}, u32[]{:S(2)}, u32[]{:S(2)}) collective-permute-start(bf16[512,128]{1,0:T(8,128)(2,1)S(1)} %get-tuple-element.41), channel_id=1, source_target_pairs={{0,7},{1,6},{2,5},{3,4},{4,3},{5,2},{6,1},{7,0},{8,15},{9,14},{10,... | collective-permute-start | bytes 393224 | tf_op jit(solution)/shard_map/ppermute | solution.py:285
  24.4 16.4 %collective-permute-start.14 = (bf16[512,128]{1,0:T(8,128)(2,1)S(1)}, bf16[512,128]{1,0:T(8,128)(2,1)S(1)}, u32[]{:S(2)}, u32[]{:S(2)}) collective-permute-start(bf16[512,128]{1,0:T(8,128)(2,1)S(1)} %get-tuple-element.53), channel_id=1, source_target_pairs={{0,4},{1,5},{2,6},{3,7},{4,0},{5,1},{6,2},{7,3},{8,12},{9,13},{10,... | collective-permute-start | bytes 393224 | tf_op jit(solution)/shard_map/ppermute | solution.py:285
  24.4 11.4 %copy-start.1 = (bf16[9,256,256]{2,1,0:T(8,128)(2,1)S(1)}, bf16[9,256,256]{2,1,0:T(8,128)(2,1)}, u32[]{:S(2)}) copy-start(bf16[9,256,256]{2,1,0:T(8,128)(2,1)} %constant.13.clone.refs_12_.refs_10_) | copy-start | bytes 3538948
  24.4 17.7 %collective-permute-start.15 = (bf16[512,128]{1,0:T(8,128)(2,1)S(1)}, bf16[512,128]{1,0:T(8,128)(2,1)S(1)}, u32[]{:S(2)}, u32[]{:S(2)}) collective-permute-start(bf16[512,128]{1,0:T(8,128)(2,1)S(1)} %get-tuple-element.54), channel_id=1, source_target_pairs={{0,1},{1,0},{2,3},{3,2},{4,5},{5,4},{6,7},{7,6},{8,9},{9,8},{10,11... | collective-permute-start | bytes 393224 | tf_op jit(solution)/shard_map/ppermute | solution.py:285
  25.3 1.6 %copy-start.2 = (f32[512,1024]{1,0:T(8,128)S(1)}, f32[512,1024]{1,0:T(8,128)}, u32[]{:S(2)}) copy-start(f32[512,1024]{1,0:T(8,128)} %taps.1) | copy-start | bytes 6291460
  28.3 19.3 %collective-permute-start.16 = (bf16[512,128]{1,0:T(8,128)(2,1)S(1)}, bf16[512,128]{1,0:T(8,128)(2,1)S(1)}, u32[]{:S(2)}, u32[]{:S(2)}) collective-permute-start(bf16[512,128]{1,0:T(8,128)(2,1)S(1)} %get-tuple-element.55), channel_id=1, source_target_pairs={{0,5},{1,4},{2,7},{3,6},{4,1},{5,0},{6,3},{7,2},{8,13},{9,12},{10,... | collective-permute-start | bytes 393224 | tf_op jit(solution)/shard_map/ppermute | solution.py:285
  34.4 13.3 %collective-permute-start.17 = (bf16[512,128]{1,0:T(8,128)(2,1)S(1)}, bf16[512,128]{1,0:T(8,128)(2,1)S(1)}, u32[]{:S(2)}, u32[]{:S(2)}) collective-permute-start(bf16[512,128]{1,0:T(8,128)(2,1)S(1)} %get-tuple-element.56), channel_id=1, source_target_pairs={{0,2},{1,3},{2,0},{3,1},{4,6},{5,7},{6,4},{7,5},{8,10},{9,11},{10,... | collective-permute-start | bytes 393224 | tf_op jit(solution)/shard_map/ppermute | solution.py:285
  34.4 14.7 %collective-permute-start.18 = (bf16[512,128]{1,0:T(8,128)(2,1)S(1)}, bf16[512,128]{1,0:T(8,128)(2,1)S(1)}, u32[]{:S(2)}, u32[]{:S(2)}) collective-permute-start(bf16[512,128]{1,0:T(8,128)(2,1)S(1)} %get-tuple-element.57), channel_id=1, source_target_pairs={{0,6},{1,7},{2,4},{3,5},{4,2},{5,3},{6,0},{7,1},{8,14},{9,15},{10,... | collective-permute-start | bytes 393224 | tf_op jit(solution)/shard_map/ppermute | solution.py:285
  40.8 16.1 %collective-permute-start.19 = (bf16[512,128]{1,0:T(8,128)(2,1)S(1)}, bf16[512,128]{1,0:T(8,128)(2,1)S(1)}, u32[]{:S(2)}, u32[]{:S(2)}) collective-permute-start(bf16[512,128]{1,0:T(8,128)(2,1)S(1)} %get-tuple-element.58), channel_id=1, source_target_pairs={{0,3},{1,2},{2,1},{3,0},{4,7},{5,6},{6,5},{7,4},{8,11},{9,10},{10,... | collective-permute-start | bytes 393224 | tf_op jit(solution)/shard_map/ppermute | solution.py:285
  42.0 15.3 %collective-permute-start.20 = (bf16[512,128]{1,0:T(8,128)(2,1)S(1)}, bf16[512,128]{1,0:T(8,128)(2,1)S(1)}, u32[]{:S(2)}, u32[]{:S(2)}) collective-permute-start(bf16[512,128]{1,0:T(8,128)(2,1)S(1)} %get-tuple-element.59), channel_id=1, source_target_pairs={{0,7},{1,6},{2,5},{3,4},{4,3},{5,2},{6,1},{7,0},{8,15},{9,14},{10,... | collective-permute-start | bytes 393224 | tf_op jit(solution)/shard_map/ppermute | solution.py:285
  47.7 17.2 %collective-permute-start.7 = (bf16[512,128]{1,0:T(8,128)(2,1)S(1)}, bf16[512,128]{1,0:T(8,128)(2,1)S(1)}, u32[]{:S(2)}, u32[]{:S(2)}) collective-permute-start(bf16[512,128]{1,0:T(8,128)(2,1)S(1)} %get-tuple-element.45), channel_id=1, source_target_pairs={{0,1},{1,0},{2,3},{3,2},{4,5},{5,4},{6,7},{7,6},{8,9},{9,8},{10,11... | collective-permute-start | bytes 393224 | tf_op jit(solution)/shard_map/ppermute | solution.py:285
  47.7 20.3 %collective-permute-start.8 = (bf16[512,128]{1,0:T(8,128)(2,1)S(1)}, bf16[512,128]{1,0:T(8,128)(2,1)S(1)}, u32[]{:S(2)}, u32[]{:S(2)}) collective-permute-start(bf16[512,128]{1,0:T(8,128)(2,1)S(1)} %get-tuple-element.46), channel_id=1, source_target_pairs={{0,4},{1,5},{2,6},{3,7},{4,0},{5,1},{6,2},{7,3},{8,12},{9,13},{10,... | collective-permute-start | bytes 393224 | tf_op jit(solution)/shard_map/ppermute | solution.py:285
  49.1 23.1 %collective-permute-start.9 = (bf16[512,128]{1,0:T(8,128)(2,1)S(1)}, bf16[512,128]{1,0:T(8,128)(2,1)S(1)}, u32[]{:S(2)}, u32[]{:S(2)}) collective-permute-start(bf16[512,128]{1,0:T(8,128)(2,1)S(1)} %get-tuple-element.47), channel_id=1, source_target_pairs={{0,5},{1,4},{2,7},{3,6},{4,1},{5,0},{6,3},{7,2},{8,13},{9,12},{10,... | collective-permute-start | bytes 393224 | tf_op jit(solution)/shard_map/ppermute | solution.py:285
  56.9 15.3 %collective-permute-start.10 = (bf16[512,128]{1,0:T(8,128)(2,1)S(1)}, bf16[512,128]{1,0:T(8,128)(2,1)S(1)}, u32[]{:S(2)}, u32[]{:S(2)}) collective-permute-start(bf16[512,128]{1,0:T(8,128)(2,1)S(1)} %get-tuple-element.48), channel_id=1, source_target_pairs={{0,6},{1,7},{2,4},{3,5},{4,2},{5,3},{6,0},{7,1},{8,14},{9,15},{10,... | collective-permute-start | bytes 393224 | tf_op jit(solution)/shard_map/ppermute | solution.py:285
  57.4 16.8 %collective-permute-start.11 = (bf16[512,128]{1,0:T(8,128)(2,1)S(1)}, bf16[512,128]{1,0:T(8,128)(2,1)S(1)}, u32[]{:S(2)}, u32[]{:S(2)}) collective-permute-start(bf16[512,128]{1,0:T(8,128)(2,1)S(1)} %get-tuple-element.49), channel_id=1, source_target_pairs={{0,7},{1,6},{2,5},{3,4},{4,3},{5,2},{6,1},{7,0},{8,15},{9,14},{10,... | collective-permute-start | bytes 393224 | tf_op jit(solution)/shard_map/ppermute | solution.py:285
  64.8 16.4 %collective-permute-start.21 = (bf16[512,256]{1,0:T(8,128)(2,1)S(1)}, bf16[512,256]{1,0:T(8,128)(2,1)S(1)}, u32[]{:S(2)}, u32[]{:S(2)}) collective-permute-start(bf16[512,256]{1,0:T(8,128)(2,1)S(1)} %get-tuple-element.62), channel_id=1, source_target_pairs={{0,16},{8,24},{16,0},{24,8},{1,17},{9,25},{17,1},{25,9},{2,18},{10... | collective-permute-start | bytes 786440 | tf_op jit(solution)/shard_map/ppermute | solution.py:285
  68.0 13.3 %collective-permute-start.22 = (bf16[512,256]{1,0:T(8,128)(2,1)S(1)}, bf16[512,256]{1,0:T(8,128)(2,1)S(1)}, u32[]{:S(2)}, u32[]{:S(2)}) collective-permute-start(bf16[512,256]{1,0:T(8,128)(2,1)S(1)} %get-tuple-element.63), channel_id=1, source_target_pairs={{0,24},{8,16},{16,8},{24,0},{1,25},{9,17},{17,9},{25,1},{2,26},{10... | collective-permute-start | bytes 786440 | tf_op jit(solution)/shard_map/ppermute | solution.py:285
  72.2 9.1 %collective-permute-start.23 = (bf16[512,256]{1,0:T(8,128)(2,1)S(1)}, bf16[512,256]{1,0:T(8,128)(2,1)S(1)}, u32[]{:S(2)}, u32[]{:S(2)}) collective-permute-start(bf16[512,256]{1,0:T(8,128)(2,1)S(1)} %get-tuple-element.64), channel_id=1, source_target_pairs={{0,8},{8,0},{16,24},{24,16},{1,9},{9,1},{17,25},{25,17},{2,10},{10... | collective-permute-start | bytes 786440 | tf_op jit(solution)/shard_map/ppermute | solution.py:285
  72.2 6.3 %collective-permute-start.12 = (bf16[512,128]{1,0:T(8,128)(2,1)S(1)}, bf16[512,128]{1,0:T(8,128)(2,1)S(1)}, u32[]{:S(2)}, u32[]{:S(2)}) collective-permute-start(bf16[512,128]{1,0:T(8,128)(2,1)S(1)} %get-tuple-element.50), channel_id=1, source_target_pairs={{0,2},{1,3},{2,0},{3,1},{4,6},{5,7},{6,4},{7,5},{8,10},{9,11},{10,... | collective-permute-start | bytes 393224 | tf_op jit(solution)/shard_map/ppermute | solution.py:285
  74.2 7.1 %collective-permute-start.13 = (bf16[512,128]{1,0:T(8,128)(2,1)S(1)}, bf16[512,128]{1,0:T(8,128)(2,1)S(1)}, u32[]{:S(2)}, u32[]{:S(2)}) collective-permute-start(bf16[512,128]{1,0:T(8,128)(2,1)S(1)} %get-tuple-element.51), channel_id=1, source_target_pairs={{0,3},{1,2},{2,1},{3,0},{4,7},{5,6},{6,5},{7,4},{8,11},{9,10},{10,... | collective-permute-start | bytes 393224 | tf_op jit(solution)/shard_map/ppermute | solution.py:285

commit v16 on v9

--- a/solution.py
+++ b/solution.py
@@ -168,11 +168,15 @@
         whole[lax.bitwise_xor(where[0], k)] = piece[...]
 
 
-def taps_kernel(taps, forward, taps_spec, mid):
+def taps_kernel(whole, taps, forward, *refs):
+    taps_spec, copied, mid, sem = refs[-4:]
     rows, width = (taps.shape[0], taps.shape[1] // BLOCKS)
+    copy = pltpu.make_async_copy(whole, copied, sem.at[0])
+    copy.start()
     split_rows(lambda p, at: taps[at, p * width : (p + 1) * width], mid, rows, width)
     for r in range(GROUPS):
         taps_spec[r] = spectrum(mid, forward, r, width).astype(taps_spec.dtype)
+    copy.wait()
 
 
 def ordered(order, where, refs, held):
@@ -254,15 +258,9 @@
     return [*range(size // 2, size), *range(1, size // 2), 0]
 
 
-def mixed(size):
-    far = far_first(size)
-    return [k for pair in zip(far[: size // 2], far[size // 2 :]) for k in pair]
-
-
-def back_mixed(size):
-    half = size // 2
-    pairs = [k for pair in zip(range(1, half), range(half, size)) for k in pair]
-    return [*pairs[:-2], size - 2, size - 1, half - 1, 0]
+def spread(size, order):
+    part = size // 8
+    return [k * part + i for k in order for i in range(part)] + [*range(1, part), 0]
 
 
 def exchange(pieces, order, axis, size):
@@ -277,7 +275,8 @@
     channels, span = saved_input.shape[1:]
     rows, length = long_filter.shape
     width = length // BLOCKS
-    order, back_order = mixed(count), back_mixed(count)
+    order, back_order, tied = (spread(count, o) for o in ((4, 1, 5, 2, 6, 7, 3), (4, 1, 5, 2, 6, 7, 3), (4, 5, 6)))
+    tied = tied[: 3 * count // 8]
     every = range(count + 8)
     where = jnp.stack([lax.axis_index("ctx"), lax.axis_index("dp")]).astype(jnp.int32)
     forward, backward = (jnp.asarray(t) for t in transform_tables(width))
@@ -299,9 +298,17 @@
         streams=(1, 2),
     )
     grad_blocks = exchange(grad_pieces, order, "ctx", count)
-    whole_input = saved_input.reshape(count, rows, span)
-    input_blocks = lax.all_to_all(whole_input, "ctx", split_axis=0, concat_axis=0, tiled=True)
-    (taps_spec,) = call(taps_kernel, [long_filter, forward], [spec], [mid], flops=work)
+    whole_input = pltpu.with_memory_space_constraint(saved_input.reshape(count, rows, span), pltpu.HBM)
+    waited = [block for k, block in zip(order, grad_blocks) if k in tied]
+    taps_spec, copied = call(
+        taps_kernel,
+        [whole_input, long_filter, forward, *waited],
+        [spec, jax.ShapeDtypeStruct((count, rows, span), half)],
+        [mid, sems((1,))],
+        flops=work,
+        streams=(0, *range(3, 3 + len(waited))),
+    )
+    input_blocks = lax.all_to_all(copied, "ctx", split_axis=0, concat_axis=0, tiled=True)
     *back, grad_spec = call(
         functools.partial(back_kernel, order, back_order),
         [where, *grad_blocks, taps_spec, forward, backward],

time: 94.2 us -> 114 us (1.21)
  local copies, waits for them, and re-layouts: 4.42 us -> 16.8 us
  starting transfers between devices: 31.6 us -> 37.6 us
  waiting for transfers between devices: 41.1 us -> 42.3 us
    unnamed x18 -> x48, local copies, waits for them, and re-layouts: 4.42 us -> 16.8 us
    ppermute x17, starting transfers between devices: 24.1 us -> 32 us  [exchange(): lax.ppermute(piece, axis, [(i, i ^ k) for i in range(size)])]
    all_to_all x1, starting transfers between devices: 7.42 us -> 5.62 us  [on_device(): lax.all_to_all(copied, 'ctx', split_axis=0, concat_axis=0, tiled=True)]
    ppermute x17, waiting for transfers between devices: 41.1 us -> 42.3 us  [exchange(): lax.ppermute(piece, axis, [(i, i ^ k) for i in range(size)])]
  transfers between devices with their start and end apart: 18 -> 18, of which waited for: 5 -> 8; matrix products, arithmetic and copies ran while one was open for 0% -> 0% of each run, Pallas kernels for 16% -> 10%
where the time goes in v16:
time: 114 us; the launch traced here: 113 us
  waiting for transfers between devices  42.3 us (37%)
  starting transfers between devices  37.6 us (33%)
  local copies, waits for them, and re-layouts  16.8 us (15%)
  Pallas kernels  15 us (13%)
    ppermute x17, waiting for transfers between devices, exchange(): lax.ppermute(piece, axis, [(i, i ^ k) for i in range(size)])  42.3 us
    ppermute x17, starting transfers between devices, exchange(): lax.ppermute(piece, axis, [(i, i ^ k) for i in range(size)])  32 us
    unnamed x48, local copies, waits for them, and re-layouts  16.8 us
    pallas_call x5, Pallas kernels, call(): pl.pallas_call(kernel, out_shape=list(outs), in_specs=specs, out_specs=[p...  15 us
    all_to_all x1, starting transfers between devices, on_device(): lax.all_to_all(copied, 'ctx', split_axis=0, concat_axis=0, tiled=True)  5.62 us
  transfers between devices with their start and end apart: 18, of which 8 were waited for; matrix products, arithmetic and copies ran while one was open for 0% of the time, Pallas kernels for 10%

profile of v16, /device:TPU:0, one launch (start us, length us, event | category | flops | bytes accessed | tf_op | source)
XLA Modules:
  0.0 113.5 jit_solution(4920946012007398283)
XLA Ops:
  0.6 0.0 copy-start
  0.6 0.1 pad_add_fusion.where
  0.7 2.3 %shard_map.77 = (bf16[512,128]{1,0:T(8,128)(2,1)S(1)}, bf16[512,128]{1,0:T(8,128)(2,1)S(1)}, bf16[512,128]{1,0:T(8,128)(2,1)S(1)}, bf16[512,128]{1,0:T(8,128)(2,...) custom-call(s32[2]{0:T(128)S(1)} %pad_add_fusion.where, ...), custom_call_target="tpu_custom_call" | custom-call | bytes 3145736 | tf_op jit(solution)/shard_map/pallas_call | solution.py:245
  3.0 0.0 copy-start.14
  3.1 0.7 copy-done.14
  3.7 0.6 copy-done.20
  4.4 0.6 copy-done.21
  5.0 0.6 copy-done.22
  5.6 0.7 copy-done.23
  6.3 4.0 %collective-permute-start = (bf16[512,128]{1,0:T(8,128)(2,1)S(1)}, bf16[512,128]{1,0:T(8,128)(2,1)S(1)}, u32[]{:S(2)}, u32[]{:S(2)}) collective-permute-start(bf16[512,128]{1,0:T(8,128)(2,1)S(1)} %get-tuple-element.25), channel_id=1, source_target_pairs={{0,4},{1,5},{2,6},{3,7},{4,0},{5,1},{6,2},{7,3},{8,12},{9,13},{10,... | collective-permute-start | bytes 393224 | tf_op jit(solution)/shard_map/ppermute | solution.py:269
  10.3 1.3 %collective-permute-start.2 = (bf16[512,128]{1,0:T(8,128)(2,1)S(1)}, bf16[512,128]{1,0:T(8,128)(2,1)S(1)}, u32[]{:S(2)}, u32[]{:S(2)}) collective-permute-start(bf16[512,128]{1,0:T(8,128)(2,1)S(1)} %get-tuple-element.27), channel_id=1, source_target_pairs={{0,5},{1,4},{2,7},{3,6},{4,1},{5,0},{6,3},{7,2},{8,13},{9,12},{10,... | collective-permute-start | bytes 393224 | tf_op jit(solution)/shard_map/ppermute | solution.py:269
  11.6 3.6 %collective-permute-start.4 = (bf16[512,128]{1,0:T(8,128)(2,1)S(1)}, bf16[512,128]{1,0:T(8,128)(2,1)S(1)}, u32[]{:S(2)}, u32[]{:S(2)}) collective-permute-start(bf16[512,128]{1,0:T(8,128)(2,1)S(1)} %get-tuple-element.29), channel_id=1, source_target_pairs={{0,6},{1,7},{2,4},{3,5},{4,2},{5,3},{6,0},{7,1},{8,14},{9,15},{10,... | collective-permute-start | bytes 393224 | tf_op jit(solution)/shard_map/ppermute | solution.py:269
  15.2 7.9 %collective-permute-done.refs_0_ = bf16[512,128]{1,0:T(8,128)(2,1)S(1)} collective-permute-done((bf16[512,128]{1,0:T(8,128)(2,1)S(1)}, bf16[512,128]{1,0:T(8,128)(2,1)S(1)}, u32[]{:S(2)}, u32[]{:S(2)}) %collective-permute-start) | collective-permute-done | bytes 131104 | tf_op jit(solution)/shard_map/ppermute | solution.py:269
  23.1 4.1 %collective-permute-done.2.refs_1_.refs_2_ = bf16[512,128]{1,0:T(8,128)(2,1)S(1)} collective-permute-done((bf16[512,128]{1,0:T(8,128)(2,1)S(1)}, bf16[512,128]{1,0:T(8,128)(2,1)S(1)}, u32[]{:S(2)}, u32[]{:S(2)}) %collective-permute-start.2) | collective-permute-done | bytes 131104 | tf_op jit(solution)/shard_map/ppermute | solution.py:269
  27.2 0.0 collective-permute-done.4.refs_2_.refs_4_
  27.2 0.0 copy-start.6
  27.2 1.7 %copy-done.6 = f32[512,1024]{1,0:T(8,128)S(1)} copy-done((f32[512,1024]{1,0:T(8,128)S(1)}, f32[512,1024]{1,0:T(8,128)}, u32[]{:S(2)}) %copy-start.6) | copy-done | bytes 2097176
  28.9 1.5 %shard_map.78 = (bf16[9,512,256]{2,1,0:T(8,128)(2,1)S(1)}, bf16[8,512,128]{2,1,0:T(8,128)(2,1)S(1)}) custom-call(bf16[8,512,128]{2,1,0:T(8,128)(2,1)} %bitcast.9, f32[512,1024]{1,0:T(8,128)S(1)} %copy-done.6, bf16[9,256,256]{2,1,0:T(8,128)(2,1)S(1)} %copy-done, bf16[512,128]{1,0:T(8,128)(2,1)S(1)} %collective-permute-done.refs_0_, ...), custom_call_target="tpu_custom_call" | custom-call | flops 603979776 | bytes 8126464 | tf_op jit(solution)/shard_map/pallas_call | solution.py:245
  30.4 1.4 %copy-done.2 = bf16[9,512,256]{2,1,0:T(8,128)(2,1)} copy-done((bf16[9,512,256]{2,1,0:T(8,128)(2,1)}, bf16[9,512,256]{2,1,0:T(8,128)(2,1)S(1)}, u32[]{:S(2)}) %copy-start.2) | copy-done | bytes 2359320
  31.8 1.0 copy-done.7
  32.8 5.6 %all-to-all-start = ((bf16[8,512,128]{2,1,0:T(8,128)(2,1)}), bf16[8,512,128]{2,1,0:T(8,128)(2,1)S(1)}, u32[]{:S(2)}, u32[]{:S(2)}) async-start(bf16[8,512,128]{2,1,0:T(8,128)(2,1)} %copy-done.7), calls=%async_computation | async-start | bytes 2097152 | tf_op jit(solution)/shard_map/all_to_all | solution.py:311
  38.4 2.0 %collective-permute-start.1 = (bf16[512,128]{1,0:T(8,128)(2,1)}, bf16[512,128]{1,0:T(8,128)(2,1)S(1)}, u32[]{:S(2)}, u32[]{:S(2)}) collective-permute-start(bf16[512,128]{1,0:T(8,128)(2,1)} %copy-done.23), channel_id=1, source_target_pairs={{0,1},{1,0},{2,3},{3,2},{4,5},{5,4},{6,7},{7,6},{8,9},{9,8},{10,11... | collective-permute-start | bytes 393224 | tf_op jit(solution)/shard_map/ppermute | solution.py:269
  40.5 1.5 %collective-permute-start.3 = (bf16[512,128]{1,0:T(8,128)(2,1)}, bf16[512,128]{1,0:T(8,128)(2,1)S(1)}, u32[]{:S(2)}, u32[]{:S(2)}) collective-permute-start(bf16[512,128]{1,0:T(8,128)(2,1)} %copy-done.22), channel_id=1, source_target_pairs={{0,2},{1,3},{2,0},{3,1},{4,6},{5,7},{6,4},{7,5},{8,10},{9,11},{10,... | collective-permute-start | bytes 393224 | tf_op jit(solution)/shard_map/ppermute | solution.py:269
  41.9 2.4 %collective-permute-start.5 = (bf16[512,128]{1,0:T(8,128)(2,1)}, bf16[512,128]{1,0:T(8,128)(2,1)S(1)}, u32[]{:S(2)}, u32[]{:S(2)}) collective-permute-start(bf16[512,128]{1,0:T(8,128)(2,1)} %copy-done.21), channel_id=1, source_target_pairs={{0,7},{1,6},{2,5},{3,4},{4,3},{5,2},{6,1},{7,0},{8,15},{9,14},{10,... | collective-permute-start | bytes 393224 | tf_op jit(solution)/shard_map/ppermute | solution.py:269
  44.3 1.5 %collective-permute-start.6 = (bf16[512,128]{1,0:T(8,128)(2,1)}, bf16[512,128]{1,0:T(8,128)(2,1)S(1)}, u32[]{:S(2)}, u32[]{:S(2)}) collective-permute-start(bf16[512,128]{1,0:T(8,128)(2,1)} %copy-done.20), channel_id=1, source_target_pairs={{0,3},{1,2},{2,1},{3,0},{4,7},{5,6},{6,5},{7,4},{8,11},{9,10},{10,... | collective-permute-start | bytes 393224 | tf_op jit(solution)/shard_map/ppermute | solution.py:269
  45.7 5.5 %collective-permute-done.1.refs_1_ = bf16[512,128]{1,0:T(8,128)(2,1)S(1)} collective-permute-done((bf16[512,128]{1,0:T(8,128)(2,1)}, bf16[512,128]{1,0:T(8,128)(2,1)S(1)}, u32[]{:S(2)}, u32[]{:S(2)}) %collective-permute-start.1) | collective-permute-done | bytes 131104 | tf_op jit(solution)/shard_map/ppermute | solution.py:269
  51.3 8.7 %collective-permute-done.3.refs_3_ = bf16[512,128]{1,0:T(8,128)(2,1)S(1)} collective-permute-done((bf16[512,128]{1,0:T(8,128)(2,1)}, bf16[512,128]{1,0:T(8,128)(2,1)S(1)}, u32[]{:S(2)}, u32[]{:S(2)}) %collective-permute-start.3) | collective-permute-done | bytes 131104 | tf_op jit(solution)/shard_map/ppermute | solution.py:269
  60.0 7.4 %collective-permute-done.5.refs_5_ = bf16[512,128]{1,0:T(8,128)(2,1)S(1)} collective-permute-done((bf16[512,128]{1,0:T(8,128)(2,1)}, bf16[512,128]{1,0:T(8,128)(2,1)S(1)}, u32[]{:S(2)}, u32[]{:S(2)}) %collective-permute-start.5) | collective-permute-done | bytes 131104 | tf_op jit(solution)/shard_map/ppermute | solution.py:269
  67.4 0.0 collective-permute-done.6.refs_6_
  67.4 1.7 %copy-done.3 = bf16[9,512,256]{2,1,0:T(8,128)(2,1)S(1)} copy-done((bf16[9,512,256]{2,1,0:T(8,128)(2,1)S(1)}, bf16[9,512,256]{2,1,0:T(8,128)(2,1)}, u32[]{:S(2)}) %copy-start.3) | copy-done | bytes 2359320
  69.1 0.9 copy-done.9
  70.0 0.9 copy-done.11
  70.9 0.9 copy-done.15
  71.8 5.0 %shard_map.79 = (bf16[512,128]{1,0:T(8,128)(2,1)}, bf16[512,128]{1,0:T(8,128)(2,1)}, bf16[512,128]{1,0:T(8,128)(2,1)}, bf16[512,128]{1,0:T(8,128)(2,1)}, bf16[51...) custom-call(s32[2]{0:T(128)S(1)} %pad_add_fusion.where, ...), custom_call_target="tpu_custom_call" | custom-call | flops 1207959552 | bytes 9175048 | tf_op jit(solution)/shard_map/pallas_call | solution.py:245
  76.8 1.4 %copy-done.4 = bf16[9,512,256]{2,1,0:T(8,128)(2,1)} copy-done((bf16[9,512,256]{2,1,0:T(8,128)(2,1)}, bf16[9,512,256]{2,1,0:T(8,128)(2,1)S(1)}, u32[]{:S(2)}) %copy-start.4) | copy-done | bytes 2359320
  78.2 0.6 copy-done.12
  78.9 0.6 copy-done.16
  79.5 0.7 copy-done.18
  80.2 5.0 %collective-permute-start.7 = (bf16[512,128]{1,0:T(8,128)(2,1)}, bf16[512,128]{1,0:T(8,128)(2,1)S(1)}, u32[]{:S(2)}, u32[]{:S(2)}) collective-permute-start(bf16[512,128]{1,0:T(8,128)(2,1)} %get-tuple-element.34), channel_id=1, source_target_pairs={{0,4},{1,5},{2,6},{3,7},{4,0},{5,1},{6,2},{7,3},{8,12},{9,13},{10,... | collective-permute-start | bytes 393224 | tf_op jit(solution)/shard_map/ppermute | solution.py:269
  85.1 0.6 collective-permute-start.8
  85.7 0.9 collective-permute-start.9
  86.6 2.0 %collective-permute-start.10 = (bf16[512,128]{1,0:T(8,128)(2,1)}, bf16[512,128]{1,0:T(8,128)(2,1)}, u32[]{:S(2)}, u32[]{:S(2)}) collective-permute-start(bf16[512,128]{1,0:T(8,128)(2,1)} %get-tuple-element.37), channel_id=1, source_target_pairs={{0,2},{1,3},{2,0},{3,1},{4,6},{5,7},{6,4},{7,5},{8,10},{9,11},{10,... | collective-permute-start | bytes 393224 | tf_op jit(solution)/shard_map/ppermute | solution.py:269
  88.6 2.4 %collective-permute-start.11 = (bf16[512,128]{1,0:T(8,128)(2,1)}, bf16[512,128]{1,0:T(8,128)(2,1)}, u32[]{:S(2)}, u32[]{:S(2)}) collective-permute-start(bf16[512,128]{1,0:T(8,128)(2,1)} %get-tuple-element.38), channel_id=1, source_target_pairs={{0,6},{1,7},{2,4},{3,5},{4,2},{5,3},{6,0},{7,1},{8,14},{9,15},{10,... | collective-permute-start | bytes 393224 | tf_op jit(solution)/shard_map/ppermute | solution.py:269
  91.0 0.0 all-to-all-done.blocks
  91.0 1.7 %copy-done.5 = bf16[9,512,256]{2,1,0:T(8,128)(2,1)S(1)} copy-done((bf16[9,512,256]{2,1,0:T(8,128)(2,1)S(1)}, bf16[9,512,256]{2,1,0:T(8,128)(2,1)}, u32[]{:S(2)}) %copy-start.5) | copy-done | bytes 2359320
  92.7 4.1 %shard_map.81 = (bf16[512,256]{1,0:T(8,128)(2,1)S(1)}, bf16[512,256]{1,0:T(8,128)(2,1)S(1)}, bf16[512,256]{1,0:T(8,128)(2,1)S(1)}, bf16[512,256]{1,0:T(8,128)(2,1)S(1)}) custom-call(s32[2]{0:T(128)S(1)} %pad_add_fusion.where, bf16[8,512,128]{2,1,0:T(8,128)(2,1)S(1)} %all-to-all-done.blocks, bf16[9,512,256]{2,1,0:T(8,128)(2,1)S(1)} %copy-done.5, ...), custom_call_target="tpu_custom_call" | custom-call | flops 1207959552 | bytes 6815752 | tf_op jit(solution)/shard_map/pallas_call | solution.py:245
  96.8 0.0 collective-permute-done.7.refs_0_
  96.8 1.6 %collective-permute-start.14 = (bf16[512,256]{1,0:T(8,128)(2,1)S(1)}, bf16[512,256]{1,0:T(8,128)(2,1)S(1)}, u32[]{:S(2)}, u32[]{:S(2)}) collective-permute-start(bf16[512,256]{1,0:T(8,128)(2,1)S(1)} %get-tuple-element.44), channel_id=1, source_target_pairs={{0,16},{8,24},{16,0},{24,8},{1,17},{9,25},{17,1},{25,9},{2,18},{10... | collective-permute-start | bytes 786440 | tf_op jit(solution)/shard_map/ppermute | solution.py:269
  98.3 0.0 collective-permute-done.8.refs_1_
  98.3 0.0 collective-permute-start.15
  98.3 2.3 %collective-permute-done.9.refs_2_ = bf16[512,128]{1,0:T(8,128)(2,1)} collective-permute-done((bf16[512,128]{1,0:T(8,128)(2,1)}, bf16[512,128]{1,0:T(8,128)(2,1)}, u32[]{:S(2)}, u32[]{:S(2)}) %collective-permute-start.9) | collective-permute-done | bytes 131104 | tf_op jit(solution)/shard_map/ppermute | solution.py:269
  100.6 0.0 collective-permute-start.16
  100.6 0.0 collective-permute-done.10.refs_3_
  100.6 0.1 collective-permute-start.12
  100.7 0.0 collective-permute-done.11.refs_4_
  100.7 0.0 copy-done.17
  100.7 3.3 %collective-permute-start.13 = (bf16[512,128]{1,0:T(8,128)(2,1)S(1)}, bf16[512,128]{1,0:T(8,128)(2,1)S(1)}, u32[]{:S(2)}, u32[]{:S(2)}) collective-permute-start(bf16[512,128]{1,0:T(8,128)(2,1)S(1)} %copy-done.17), channel_id=1, source_target_pairs={{0,3},{1,2},{2,1},{3,0},{4,7},{5,6},{6,5},{7,4},{8,11},{9,10},{10,... | collective-permute-start | bytes 393224 | tf_op jit(solution)/shard_map/ppermute | solution.py:269
  104.0 5.7 %collective-permute-done.12.refs_5_ = bf16[512,128]{1,0:T(8,128)(2,1)S(1)} collective-permute-done((bf16[512,128]{1,0:T(8,128)(2,1)S(1)}, bf16[512,128]{1,0:T(8,128)(2,1)S(1)}, u32[]{:S(2)}, u32[]{:S(2)}) %collective-permute-start.12) | collective-permute-done | bytes 131104 | tf_op jit(solution)/shard_map/ppermute | solution.py:269
  109.7 0.7 collective-permute-done.13.refs_6_
  110.4 2.1 %shard_map.80 = bf16[8,512,128]{2,1,0:T(8,128)(2,1)} custom-call(s32[2]{0:T(128)S(1)} %pad_add_fusion.where, bf16[512,128]{1,0:T(8,128)(2,1)S(1)} %collective-permute-done.7.refs_0_, bf16[512,128]{1,0:T(8,128)(2,1)} %collective-permute-done.8.refs_1_, bf16[512,128]{1,0:T(8,128)(2,1)} %collective-permute-done.9.refs_2_, ...), custom_call_target="tpu_custom_call" | custom-call | bytes 2097160 | tf_op jit(solution)/shard_map/pallas_call | solution.py:245
  112.5 0.0 collective-permute-done.14
  112.5 0.0 collective-permute-done.15
  112.5 0.0 collective-permute-done.16
  112.5 0.9 add_multiply_fusion
  (27 shorter events, 0.0 us)
Async XLA Ops:
  0.6 26.6 %copy-start = (bf16[9,256,256]{2,1,0:T(8,128)(2,1)S(1)}, bf16[9,256,256]{2,1,0:T(8,128)(2,1)}, u32[]{:S(2)}) copy-start(bf16[9,256,256]{2,1,0:T(8,128)(2,1)} %constant.14.clone.forward.refs_9_) | copy-start | bytes 3538948
  3.0 0.7 copy-start.14
  3.7 0.6 copy-start.20
  4.4 0.6 copy-start.21
  5.0 0.6 copy-start.22
  5.6 0.7 copy-start.23
  6.3 16.8 %collective-permute-start = (bf16[512,128]{1,0:T(8,128)(2,1)S(1)}, bf16[512,128]{1,0:T(8,128)(2,1)S(1)}, u32[]{:S(2)}, u32[]{:S(2)}) collective-permute-start(bf16[512,128]{1,0:T(8,128)(2,1)S(1)} %get-tuple-element.25), channel_id=1, source_target_pairs={{0,4},{1,5},{2,6},{3,7},{4,0},{5,1},{6,2},{7,3},{8,12},{9,13},{10,... | collective-permute-start | bytes 393224 | tf_op jit(solution)/shard_map/ppermute | solution.py:269
  10.3 16.9 %collective-permute-start.2 = (bf16[512,128]{1,0:T(8,128)(2,1)S(1)}, bf16[512,128]{1,0:T(8,128)(2,1)S(1)}, u32[]{:S(2)}, u32[]{:S(2)}) collective-permute-start(bf16[512,128]{1,0:T(8,128)(2,1)S(1)} %get-tuple-element.27), channel_id=1, source_target_pairs={{0,5},{1,4},{2,7},{3,6},{4,1},{5,0},{6,3},{7,2},{8,13},{9,12},{10,... | collective-permute-start | bytes 393224 | tf_op jit(solution)/shard_map/ppermute | solution.py:269
  11.6 15.6 %collective-permute-start.4 = (bf16[512,128]{1,0:T(8,128)(2,1)S(1)}, bf16[512,128]{1,0:T(8,128)(2,1)S(1)}, u32[]{:S(2)}, u32[]{:S(2)}) collective-permute-start(bf16[512,128]{1,0:T(8,128)(2,1)S(1)} %get-tuple-element.29), channel_id=1, source_target_pairs={{0,6},{1,7},{2,4},{3,5},{4,2},{5,3},{6,0},{7,1},{8,14},{9,15},{10,... | collective-permute-start | bytes 393224 | tf_op jit(solution)/shard_map/ppermute | solution.py:269
  27.2 3.2 %copy-start.8 = (bf16[512,128]{1,0:T(8,128)(2,1)}, bf16[512,128]{1,0:T(8,128)(2,1)S(1)}, u32[]{:S(2)}) copy-start(bf16[512,128]{1,0:T(8,128)(2,1)S(1)} %collective-permute-done.2.refs_1_.refs_2_) | copy-start | bytes 393220
  27.2 3.2 %copy-start.10 = (bf16[512,128]{1,0:T(8,128)(2,1)}, bf16[512,128]{1,0:T(8,128)(2,1)S(1)}, u32[]{:S(2)}) copy-start(bf16[512,128]{1,0:T(8,128)(2,1)S(1)} %collective-permute-done.4.refs_2_.refs_4_) | copy-start | bytes 393220
  27.2 1.7 %copy-start.6 = (f32[512,1024]{1,0:T(8,128)S(1)}, f32[512,1024]{1,0:T(8,128)}, u32[]{:S(2)}) copy-start(f32[512,1024]{1,0:T(8,128)} %taps.1) | copy-start | bytes 6291460
  30.4 1.4 %copy-start.2 = (bf16[9,512,256]{2,1,0:T(8,128)(2,1)}, bf16[9,512,256]{2,1,0:T(8,128)(2,1)S(1)}, u32[]{:S(2)}) copy-start(bf16[9,512,256]{2,1,0:T(8,128)(2,1)S(1)} %get-tuple-element.33.refs_8_) | copy-start | bytes 7077892
  31.8 1.0 copy-start.7
  32.8 34.6 %copy-start.1 = (bf16[9,256,256]{2,1,0:T(8,128)(2,1)S(1)}, bf16[9,256,256]{2,1,0:T(8,128)(2,1)}, u32[]{:S(2)}) copy-start(bf16[9,256,256]{2,1,0:T(8,128)(2,1)} %constant.15.clone.refs_10_.backward) | copy-start | bytes 3538948
  32.8 58.2 %all-to-all-start = ((bf16[8,512,128]{2,1,0:T(8,128)(2,1)}), bf16[8,512,128]{2,1,0:T(8,128)(2,1)S(1)}, u32[]{:S(2)}, u32[]{:S(2)}) async-start(bf16[8,512,128]{2,1,0:T(8,128)(2,1)} %copy-done.7), calls=%async_computation | async-start | bytes 2097152 | tf_op jit(solution)/shard_map/all_to_all | solution.py:311
  38.4 12.9 %collective-permute-start.1 = (bf16[512,128]{1,0:T(8,128)(2,1)}, bf16[512,128]{1,0:T(8,128)(2,1)S(1)}, u32[]{:S(2)}, u32[]{:S(2)}) collective-permute-start(bf16[512,128]{1,0:T(8,128)(2,1)} %copy-done.23), channel_id=1, source_target_pairs={{0,1},{1,0},{2,3},{3,2},{4,5},{5,4},{6,7},{7,6},{8,9},{9,8},{10,11... | collective-permute-start | bytes 393224 | tf_op jit(solution)/shard_map/ppermute | solution.py:269
  40.5 19.5 %collective-permute-start.3 = (bf16[512,128]{1,0:T(8,128)(2,1)}, bf16[512,128]{1,0:T(8,128)(2,1)S(1)}, u32[]{:S(2)}, u32[]{:S(2)}) collective-permute-start(bf16[512,128]{1,0:T(8,128)(2,1)} %copy-done.22), channel_id=1, source_target_pairs={{0,2},{1,3},{2,0},{3,1},{4,6},{5,7},{6,4},{7,5},{8,10},{9,11},{10,... | collective-permute-start | bytes 393224 | tf_op jit(solution)/shard_map/ppermute | solution.py:269
  41.9 25.5 %collective-permute-start.5 = (bf16[512,128]{1,0:T(8,128)(2,1)}, bf16[512,128]{1,0:T(8,128)(2,1)S(1)}, u32[]{:S(2)}, u32[]{:S(2)}) collective-permute-start(bf16[512,128]{1,0:T(8,128)(2,1)} %copy-done.21), channel_id=1, source_target_pairs={{0,7},{1,6},{2,5},{3,4},{4,3},{5,2},{6,1},{7,0},{8,15},{9,14},{10,... | collective-permute-start | bytes 393224 | tf_op jit(solution)/shard_map/ppermute | solution.py:269
  44.3 23.1 %collective-permute-start.6 = (bf16[512,128]{1,0:T(8,128)(2,1)}, bf16[512,128]{1,0:T(8,128)(2,1)S(1)}, u32[]{:S(2)}, u32[]{:S(2)}) collective-permute-start(bf16[512,128]{1,0:T(8,128)(2,1)} %copy-done.20), channel_id=1, source_target_pairs={{0,3},{1,2},{2,1},{3,0},{4,7},{5,6},{6,5},{7,4},{8,11},{9,10},{10,... | collective-permute-start | bytes 393224 | tf_op jit(solution)/shard_map/ppermute | solution.py:269
  67.4 1.7 %copy-start.3 = (bf16[9,512,256]{2,1,0:T(8,128)(2,1)S(1)}, bf16[9,512,256]{2,1,0:T(8,128)(2,1)}, u32[]{:S(2)}) copy-start(bf16[9,512,256]{2,1,0:T(8,128)(2,1)} %copy-done.2) | copy-start | bytes 7077892
  69.1 0.9 copy-start.9
  70.0 0.9 copy-start.11
  70.9 0.9 copy-start.15
  76.8 1.4 %copy-start.4 = (bf16[9,512,256]{2,1,0:T(8,128)(2,1)}, bf16[9,512,256]{2,1,0:T(8,128)(2,1)S(1)}, u32[]{:S(2)}) copy-start(bf16[9,512,256]{2,1,0:T(8,128)(2,1)S(1)} %get-tuple-element.43.grad_spec) | copy-start | bytes 7077892
  78.2 0.6 copy-start.12
  78.9 0.6 copy-start.16
  79.5 0.7 copy-start.18
  80.2 16.6 %collective-permute-start.7 = (bf16[512,128]{1,0:T(8,128)(2,1)}, bf16[512,128]{1,0:T(8,128)(2,1)S(1)}, u32[]{:S(2)}, u32[]{:S(2)}) collective-permute-start(bf16[512,128]{1,0:T(8,128)(2,1)} %get-tuple-element.34), channel_id=1, source_target_pairs={{0,4},{1,5},{2,6},{3,7},{4,0},{5,1},{6,2},{7,3},{8,12},{9,13},{10,... | collective-permute-start | bytes 393224 | tf_op jit(solution)/shard_map/ppermute | solution.py:269
  85.1 13.2 %collective-permute-start.8 = (bf16[512,128]{1,0:T(8,128)(2,1)}, bf16[512,128]{1,0:T(8,128)(2,1)}, u32[]{:S(2)}, u32[]{:S(2)}) collective-permute-start(bf16[512,128]{1,0:T(8,128)(2,1)} %get-tuple-element.35), channel_id=1, source_target_pairs={{0,1},{1,0},{2,3},{3,2},{4,5},{5,4},{6,7},{7,6},{8,9},{9,8},{10,11... | collective-permute-start | bytes 393224 | tf_op jit(solution)/shard_map/ppermute | solution.py:269
  85.7 14.9 %collective-permute-start.9 = (bf16[512,128]{1,0:T(8,128)(2,1)}, bf16[512,128]{1,0:T(8,128)(2,1)}, u32[]{:S(2)}, u32[]{:S(2)}) collective-permute-start(bf16[512,128]{1,0:T(8,128)(2,1)} %get-tuple-element.36), channel_id=1, source_target_pairs={{0,5},{1,4},{2,7},{3,6},{4,1},{5,0},{6,3},{7,2},{8,13},{9,12},{10,... | collective-permute-start | bytes 393224 | tf_op jit(solution)/shard_map/ppermute | solution.py:269
  86.6 14.0 %collective-permute-start.10 = (bf16[512,128]{1,0:T(8,128)(2,1)}, bf16[512,128]{1,0:T(8,128)(2,1)}, u32[]{:S(2)}, u32[]{:S(2)}) collective-permute-start(bf16[512,128]{1,0:T(8,128)(2,1)} %get-tuple-element.37), channel_id=1, source_target_pairs={{0,2},{1,3},{2,0},{3,1},{4,6},{5,7},{6,4},{7,5},{8,10},{9,11},{10,... | collective-permute-start | bytes 393224 | tf_op jit(solution)/shard_map/ppermute | solution.py:269
  88.6 12.1 %collective-permute-start.11 = (bf16[512,128]{1,0:T(8,128)(2,1)}, bf16[512,128]{1,0:T(8,128)(2,1)}, u32[]{:S(2)}, u32[]{:S(2)}) collective-permute-start(bf16[512,128]{1,0:T(8,128)(2,1)} %get-tuple-element.38), channel_id=1, source_target_pairs={{0,6},{1,7},{2,4},{3,5},{4,2},{5,3},{6,0},{7,1},{8,14},{9,15},{10,... | collective-permute-start | bytes 393224 | tf_op jit(solution)/shard_map/ppermute | solution.py:269
  91.0 1.7 %copy-start.5 = (bf16[9,512,256]{2,1,0:T(8,128)(2,1)S(1)}, bf16[9,512,256]{2,1,0:T(8,128)(2,1)}, u32[]{:S(2)}) copy-start(bf16[9,512,256]{2,1,0:T(8,128)(2,1)} %copy-done.4) | copy-start | bytes 7077892
  92.7 8.0 %copy-start.19 = (bf16[512,128]{1,0:T(8,128)(2,1)S(1)}, bf16[512,128]{1,0:T(8,128)(2,1)}, u32[]{:S(2)}) copy-start(bf16[512,128]{1,0:T(8,128)(2,1)} %copy-done.18) | copy-start | bytes 393220
  92.7 8.1 %copy-start.17 = (bf16[512,128]{1,0:T(8,128)(2,1)S(1)}, bf16[512,128]{1,0:T(8,128)(2,1)}, u32[]{:S(2)}) copy-start(bf16[512,128]{1,0:T(8,128)(2,1)} %copy-done.16) | copy-start | bytes 393220
  92.7 17.7 %copy-start.13 = (bf16[512,128]{1,0:T(8,128)(2,1)S(1)}, bf16[512,128]{1,0:T(8,128)(2,1)}, u32[]{:S(2)}) copy-start(bf16[512,128]{1,0:T(8,128)(2,1)} %copy-done.12) | copy-start | bytes 393220
  96.8 15.7 %collective-permute-start.14 = (bf16[512,256]{1,0:T(8,128)(2,1)S(1)}, bf16[512,256]{1,0:T(8,128)(2,1)S(1)}, u32[]{:S(2)}, u32[]{:S(2)}) collective-permute-start(bf16[512,256]{1,0:T(8,128)(2,1)S(1)} %get-tuple-element.44), channel_id=1, source_target_pairs={{0,16},{8,24},{16,0},{24,8},{1,17},{9,25},{17,1},{25,9},{2,18},{10... | collective-permute-start | bytes 786440 | tf_op jit(solution)/shard_map/ppermute | solution.py:269
  98.3 14.2 %collective-permute-start.15 = (bf16[512,256]{1,0:T(8,128)(2,1)S(1)}, bf16[512,256]{1,0:T(8,128)(2,1)S(1)}, u32[]{:S(2)}, u32[]{:S(2)}) collective-permute-start(bf16[512,256]{1,0:T(8,128)(2,1)S(1)} %get-tuple-element.45), channel_id=1, source_target_pairs={{0,24},{8,16},{16,8},{24,0},{1,25},{9,17},{17,9},{25,1},{2,26},{10... | collective-permute-start | bytes 786440 | tf_op jit(solution)/shard_map/ppermute | solution.py:269
  100.6 11.9 %collective-permute-start.16 = (bf16[512,256]{1,0:T(8,128)(2,1)S(1)}, bf16[512,256]{1,0:T(8,128)(2,1)S(1)}, u32[]{:S(2)}, u32[]{:S(2)}) collective-permute-start(bf16[512,256]{1,0:T(8,128)(2,1)S(1)} %get-tuple-element.46), channel_id=1, source_target_pairs={{0,8},{8,0},{16,24},{24,16},{1,9},{9,1},{17,25},{25,17},{2,10},{10... | collective-permute-start | bytes 786440 | tf_op jit(solution)/shard_map/ppermute | solution.py:269
  100.6 9.1 %collective-permute-start.12 = (bf16[512,128]{1,0:T(8,128)(2,1)S(1)}, bf16[512,128]{1,0:T(8,128)(2,1)S(1)}, u32[]{:S(2)}, u32[]{:S(2)}) collective-permute-start(bf16[512,128]{1,0:T(8,128)(2,1)S(1)} %copy-done.19), channel_id=1, source_target_pairs={{0,7},{1,6},{2,5},{3,4},{4,3},{5,2},{6,1},{7,0},{8,15},{9,14},{10,... | collective-permute-start | bytes 393224 | tf_op jit(solution)/shard_map/ppermute | solution.py:269
  100.7 9.6 %collective-permute-start.13 = (bf16[512,128]{1,0:T(8,128)(2,1)S(1)}, bf16[512,128]{1,0:T(8,128)(2,1)S(1)}, u32[]{:S(2)}, u32[]{:S(2)}) collective-permute-start(bf16[512,128]{1,0:T(8,128)(2,1)S(1)} %copy-done.17), channel_id=1, source_target_pairs={{0,3},{1,2},{2,1},{3,0},{4,7},{5,6},{6,5},{7,4},{8,11},{9,10},{10,... | collective-permute-start | bytes 393224 | tf_op jit(solution)/shard_map/ppermute | solution.py:269

commit v17 on v11

--- a/solution.py
+++ b/solution.py
@@ -140,7 +140,7 @@
 
 
 def piece_at(ref, where, k, rows):
-    start = pl.multiple_of(lax.bitwise_xor(where[0], k) * rows, rows)
+    start = pl.multiple_of(where[k] * rows, rows)
     return ref.at[pl.ds(start, rows), :]
 
 
@@ -171,7 +171,7 @@
 def place_kernel(order, where, *refs):
     pieces, whole = refs[:-1], refs[-1]
     for k, piece in zip(order, pieces):
-        whole[lax.bitwise_xor(where[0], k)] = piece[...]
+        whole[where[k]] = piece[...]
 
 
 def taps_kernel(taps, forward, taps_spec, mid):
@@ -184,7 +184,7 @@
 def ordered(order, where, refs, held):
     span = refs[0].shape[1]
     for k, ref in zip(order, refs):
-        start = pl.multiple_of(lax.bitwise_xor(where[0], k) * span, span)
+        start = pl.multiple_of(where[k] * span, span)
         held[:, pl.ds(start, span)] = ref[...]
 
 
@@ -216,7 +216,7 @@
     merge_rows(wide, block_into(held, width), rows, width)
     span = outs[0].shape[1]
     for k, out in zip(back_order, outs):
-        start = pl.multiple_of(lax.bitwise_xor(where[0], k) * span, span)
+        start = pl.multiple_of(where[k] * span, span)
         out[...] = held[:, pl.ds(start, span)]
 
 
@@ -235,7 +235,7 @@
     merge_rows(wide, block_into(held, width), rows, width)
     part = held.shape[1] // len(outs)
     for k, out in zip(far_first(len(outs)), outs):
-        start = pl.multiple_of(lax.bitwise_xor(where[1], k) * part, part)
+        start = pl.multiple_of(lax.bitwise_xor(where[where.shape[0] - 1], k) * part, part)
         out[...] = held[:, pl.ds(start, part)]
 
 
@@ -266,15 +266,29 @@
     return [*range(size // 2, size), *range(1, size // 2), 0]
 
 
+def pairings(size):
+    if size != 8:
+        return [[i ^ k for i in range(size)] for k in [*range(1, size), 0]]
+    rounds = [[i ^ 4 for i in range(8)]]
+    for k, l in ((0, 1), (2, 3), (0, 2), (1, 3), (0, 3), (1, 2)):
+        i, j = (n for n in range(4) if n not in (k, l))
+        partner = [0] * 8
+        for one, two in ((k, 4 + l), (l, 4 + k), (i, j), (4 + i, 4 + j)):
+            partner[one], partner[two] = two, one
+        rounds.append(partner)
+    return rounds + [list(range(8))]
+
+
 def spread(size, order):
     part = size // 8
-    return [k * part + i for k in order for i in range(part)] + [*range(1, part), 0]
-
-
-def exchange(pieces, order, axis, size):
+    return [k * part + i for k in (*order, 7) for i in range(part)]
+
+
+def exchange(pieces, order, rounds, axis):
     moved = []
     for k, piece in zip(order, pieces):
-        moved.append(lax.ppermute(piece, axis, [(i, i ^ k) for i in range(size)]) if k else piece)
+        pairs = list(enumerate(rounds[k]))
+        moved.append(piece if pairs[0][1] == 0 else lax.ppermute(piece, axis, pairs))
     return moved
 
 
@@ -283,11 +297,14 @@
     channels, span = saved_input.shape[1:]
     rows, length = long_filter.shape
     width = length // BLOCKS
-    grad_order, input_order, back_order = (spread(count, o) for o in ((1, 2, 4, 5, 6, 7, 3), (4, 5, 1, 6, 2, 7, 3), (1, 2, 3, 4, 5, 6, 7)))
+    rounds = pairings(count)
+    grad_order, input_order, back_order = (spread(count, o) for o in ((0, 1, 2, 3, 4, 5, 6), (0, 1, 2, 3, 4, 5, 6), (0, 1, 2, 3, 4, 5, 6)))
     late = 2
     at = count - 1 - late
     every = range(count + 8)
-    where = jnp.stack([lax.axis_index("ctx"), lax.axis_index("dp")]).astype(jnp.int32)
+    me = lax.axis_index("ctx")
+    partners = lax.dynamic_index_in_dim(jnp.asarray(np.array(rounds, np.int32).T), me, 0, keepdims=False)
+    where = jnp.concatenate([partners, jnp.stack([me, lax.axis_index("dp")]).astype(jnp.int32)])
     forward, backward = (jnp.asarray(t) for t in transform_tables(width))
     half, full = jnp.bfloat16, jnp.float32
     piece = jax.ShapeDtypeStruct((rows, span), half)
@@ -307,7 +324,7 @@
         hbm=(1, 2, 3),
     )
     grad_pieces, input_pieces = pieces[:count], pieces[count:]
-    grad_blocks = exchange(grad_pieces, grad_order, "ctx", count)
+    grad_blocks = exchange(grad_pieces, grad_order, rounds, "ctx")
     (taps_spec,) = call(taps_kernel, [long_filter, forward], [spec], [mid], flops=work)
     passed = [*input_pieces[at : at + late]]
     *back, grad_spec = call(
@@ -321,8 +338,8 @@
         aliases={1 + count + i: i for i in range(late)},
     )
     input_pieces[at : at + late], back = back[:late], back[late:]
-    input_blocks = exchange(input_pieces, input_order, "ctx", count)
-    back_blocks = exchange(back, back_order, "ctx", count)
+    input_blocks = exchange(input_pieces, input_order, rounds, "ctx")
+    back_blocks = exchange(back, back_order, rounds, "ctx")
     share = jax.ShapeDtypeStruct((rows, length // shares), half)
     cross = call(
         functools.partial(cross_kernel, input_order),
@@ -331,7 +348,8 @@
         [held, mid, wide],
         flops=2 * work,
     )
-    cross_blocks = exchange(cross, far_first(shares), "dp", shares)
+    swaps = [[i ^ k for i in range(shares)] for k in far_first(shares)]
+    cross_blocks = exchange(cross, range(shares), swaps, "dp")
     scale = 1.0 / math.sqrt(shares * length)
     grad_filter = sum(x.astype(full) for x in cross_blocks) * scale
     (whole,) = call(

time: 84.2 us -> 84.1 us (level)
  the two profiles are of different devices: /device:TPU:9 before, /device:TPU:0 now
where the time goes in v17:
time: 84.1 us; the launch traced here: 84 us
  starting transfers between devices  49.5 us (59%)
  waiting for transfers between devices  16.2 us (19%)
  Pallas kernels  14.1 us (17%)
  local copies, waits for them, and re-layouts  2.4 us (3%)
  other arithmetic  1.02 us (1%)
    ppermute x24, starting transfers between devices, exchange(): lax.ppermute(piece, axis, pairs)  49.5 us
    ppermute x24, waiting for transfers between devices, exchange(): lax.ppermute(piece, axis, pairs)  16.2 us
    pallas_call x5, Pallas kernels, call(): pl.pallas_call(kernel, out_shape=list(outs), in_specs=specs, out_specs=[s...  14.1 us
  transfers between devices with their start and end apart: 24, of which 6 were waited for; matrix products, arithmetic and copies ran while one was open for 0% of the time, Pallas kernels for 14%

profile of v17, /device:TPU:0, one launch (start us, length us, event | category | flops | bytes accessed | tf_op | source)
XLA Modules:
  0.0 84.0 jit_solution(5488710802385076601)
XLA Ops:
  0.6 0.0 copy-start
  0.6 0.8 dynamic-slice_bitcast_fusion
  1.4 0.1 pad_add_fusion.where
  1.5 2.7 %shard_map.86 = (bf16[512,128]{1,0:T(8,128)(2,1)S(1)}, bf16[512,128]{1,0:T(8,128)(2,1)S(1)}, bf16[512,128]{1,0:T(8,128)(2,1)S(1)}, bf16[512,128]{1,0:T(8,128)(2,...) custom-call(s32[10]{0:T(128)S(1)} %pad_add_fusion.where, ...), custom_call_target="tpu_custom_call" | custom-call | bytes 5242920 | tf_op jit(solution)/shard_map/pallas_call | solution.py:252
  4.2 4.1 %collective-permute-start = (bf16[512,128]{1,0:T(8,128)(2,1)S(1)}, bf16[512,128]{1,0:T(8,128)(2,1)S(1)}, u32[]{:S(2)}, u32[]{:S(2)}) collective-permute-start(bf16[512,128]{1,0:T(8,128)(2,1)S(1)} %get-tuple-element.33), channel_id=1, source_target_pairs={{0,4},{1,5},{2,6},{3,7},{4,0},{5,1},{6,2},{7,3},{8,12},{9,13},{10,... | collective-permute-start | bytes 393224 | tf_op jit(solution)/shard_map/ppermute | solution.py:291
  8.3 1.3 %collective-permute-start.1 = (bf16[512,128]{1,0:T(8,128)(2,1)S(1)}, bf16[512,128]{1,0:T(8,128)(2,1)S(1)}, u32[]{:S(2)}, u32[]{:S(2)}) collective-permute-start(bf16[512,128]{1,0:T(8,128)(2,1)S(1)} %get-tuple-element.34), channel_id=1, source_target_pairs={{0,5},{1,4},{2,3},{3,2},{4,1},{5,0},{6,7},{7,6},{8,13},{9,12},{10,... | collective-permute-start | bytes 393224 | tf_op jit(solution)/shard_map/ppermute | solution.py:291
  9.6 0.2 collective-permute-start.2
  9.8 3.9 %collective-permute-start.3 = (bf16[512,128]{1,0:T(8,128)(2,1)S(1)}, bf16[512,128]{1,0:T(8,128)(2,1)S(1)}, u32[]{:S(2)}, u32[]{:S(2)}) collective-permute-start(bf16[512,128]{1,0:T(8,128)(2,1)S(1)} %get-tuple-element.36), channel_id=1, source_target_pairs={{0,6},{1,3},{2,4},{3,1},{4,2},{5,7},{6,0},{7,5},{8,14},{9,11},{10,... | collective-permute-start | bytes 393224 | tf_op jit(solution)/shard_map/ppermute | solution.py:291
  13.7 0.0 collective-permute-start.4
  13.7 7.4 %collective-permute-done.refs_0_ = bf16[512,128]{1,0:T(8,128)(2,1)S(1)} collective-permute-done((bf16[512,128]{1,0:T(8,128)(2,1)S(1)}, bf16[512,128]{1,0:T(8,128)(2,1)S(1)}, u32[]{:S(2)}, u32[]{:S(2)}) %collective-permute-start) | collective-permute-done | bytes 131104 | tf_op jit(solution)/shard_map/ppermute | solution.py:291
  21.1 3.8 %collective-permute-start.5 = (bf16[512,128]{1,0:T(8,128)(2,1)S(1)}, bf16[512,128]{1,0:T(8,128)(2,1)S(1)}, u32[]{:S(2)}, u32[]{:S(2)}) collective-permute-start(bf16[512,128]{1,0:T(8,128)(2,1)S(1)} %get-tuple-element.38), channel_id=1, source_target_pairs={{0,7},{1,2},{2,1},{3,4},{4,3},{5,6},{6,5},{7,0},{8,15},{9,10},{10,... | collective-permute-start | bytes 393224 | tf_op jit(solution)/shard_map/ppermute | solution.py:291
  24.9 1.7 %collective-permute-done.1.refs_1_ = bf16[512,128]{1,0:T(8,128)(2,1)S(1)} collective-permute-done((bf16[512,128]{1,0:T(8,128)(2,1)S(1)}, bf16[512,128]{1,0:T(8,128)(2,1)S(1)}, u32[]{:S(2)}, u32[]{:S(2)}) %collective-permute-start.1) | collective-permute-done | bytes 131104 | tf_op jit(solution)/shard_map/ppermute | solution.py:291
  26.6 0.0 collective-permute-start.6
  26.6 0.0 collective-permute-done.2.refs_2_
  26.6 0.0 collective-permute-start.14
  26.6 0.0 collective-permute-done.3.refs_3_
  26.6 0.0 copy-start.1
  26.6 1.2 %collective-permute-start.15 = (bf16[512,128]{1,0:T(8,128)(2,1)S(1)}, bf16[512,128]{1,0:T(8,128)(2,1)S(1)}, u32[]{:S(2)}, u32[]{:S(2)}) collective-permute-start(bf16[512,128]{1,0:T(8,128)(2,1)S(1)} %get-tuple-element.52), channel_id=1, source_target_pairs={{0,5},{1,4},{2,3},{3,2},{4,1},{5,0},{6,7},{7,6},{8,13},{9,12},{10,... | collective-permute-start | bytes 393224 | tf_op jit(solution)/shard_map/ppermute | solution.py:291
  27.8 0.0 copy-done
  27.8 0.0 copy-start.2
  27.8 1.6 %copy-done.2 = f32[512,1024]{1,0:T(8,128)S(1)} copy-done((f32[512,1024]{1,0:T(8,128)S(1)}, f32[512,1024]{1,0:T(8,128)}, u32[]{:S(2)}) %copy-start.2) | copy-done | bytes 2097176
  29.4 1.5 %shard_map.87.refs_10_ = bf16[9,512,256]{2,1,0:T(8,128)(2,1)S(1)} custom-call(f32[512,1024]{1,0:T(8,128)S(1)} %copy-done.2, bf16[9,256,256]{2,1,0:T(8,128)(2,1)S(1)} %copy-done), custom_call_target="tpu_custom_call" | custom-call | flops 603979776 | bytes 5636096 | tf_op jit(solution)/shard_map/pallas_call | solution.py:252
  30.9 0.0 collective-permute-done.4.refs_4_
  30.9 6.9 %collective-permute-start.16 = (bf16[512,128]{1,0:T(8,128)(2,1)S(1)}, bf16[512,128]{1,0:T(8,128)(2,1)S(1)}, u32[]{:S(2)}, u32[]{:S(2)}) collective-permute-start(bf16[512,128]{1,0:T(8,128)(2,1)S(1)} %get-tuple-element.53), channel_id=1, source_target_pairs={{0,1},{1,0},{2,7},{3,6},{4,5},{5,4},{6,3},{7,2},{8,9},{9,8},{10,15... | collective-permute-start | bytes 393224 | tf_op jit(solution)/shard_map/ppermute | solution.py:291
  37.7 0.0 collective-permute-done.5.refs_5_
  37.7 0.1 collective-permute-start.17
  37.9 0.0 collective-permute-done.6.refs_6_
  37.9 3.6 %collective-permute-start.18 = (bf16[512,128]{1,0:T(8,128)(2,1)S(1)}, bf16[512,128]{1,0:T(8,128)(2,1)S(1)}, u32[]{:S(2)}, u32[]{:S(2)}) collective-permute-start(bf16[512,128]{1,0:T(8,128)(2,1)S(1)} %get-tuple-element.55), channel_id=1, source_target_pairs={{0,2},{1,7},{2,0},{3,5},{4,6},{5,3},{6,4},{7,1},{8,10},{9,15},{10,... | collective-permute-start | bytes 393224 | tf_op jit(solution)/shard_map/ppermute | solution.py:291
  41.4 0.0 copy-done.1
  41.4 4.2 %shard_map.88 = (bf16[512,128]{1,0:T(8,128)(2,1)S(1)}, bf16[512,128]{1,0:T(8,128)(2,1)S(1)}, bf16[512,128]{1,0:T(8,128)(2,1)S(1)}, bf16[512,128]{1,0:T(8,128)(2,...) custom-call(s32[10]{0:T(128)S(1)} %pad_add_fusion.where, ...), custom_call_target="tpu_custom_call", output_to_operand_aliasing={{0}: (9, {}), {1}: (10, {})} | custom-call | flops 1207959552 | bytes 9699368 | tf_op jit(solution)/shard_map/pallas_call | solution.py:252
  45.7 0.0 collective-permute-done.14.refs_0_
  45.7 1.3 %collective-permute-start.19 = (bf16[512,128]{1,0:T(8,128)(2,1)S(1)}, bf16[512,128]{1,0:T(8,128)(2,1)S(1)}, u32[]{:S(2)}, u32[]{:S(2)}) collective-permute-start(bf16[512,128]{1,0:T(8,128)(2,1)S(1)} %get-tuple-element.56), channel_id=1, source_target_pairs={{0,7},{1,2},{2,1},{3,4},{4,3},{5,6},{6,5},{7,0},{8,15},{9,10},{10,... | collective-permute-start | bytes 393224 | tf_op jit(solution)/shard_map/ppermute | solution.py:291
  47.0 0.7 collective-permute-done.15.refs_1_
  47.7 0.2 collective-permute-start.20
  47.9 0.0 collective-permute-done.16.refs_2_
  47.9 3.1 %collective-permute-start.7 = (bf16[512,128]{1,0:T(8,128)(2,1)S(1)}, bf16[512,128]{1,0:T(8,128)(2,1)S(1)}, u32[]{:S(2)}, u32[]{:S(2)}) collective-permute-start(bf16[512,128]{1,0:T(8,128)(2,1)S(1)} %get-tuple-element.43), channel_id=1, source_target_pairs={{0,4},{1,5},{2,6},{3,7},{4,0},{5,1},{6,2},{7,3},{8,12},{9,13},{10,... | collective-permute-start | bytes 393224 | tf_op jit(solution)/shard_map/ppermute | solution.py:291
  51.1 0.0 collective-permute-done.17.refs_3_
  51.1 0.0 collective-permute-start.8
  51.1 0.0 collective-permute-done.18.refs_4_
  51.1 4.0 %collective-permute-start.9 = (bf16[512,128]{1,0:T(8,128)(2,1)S(1)}, bf16[512,128]{1,0:T(8,128)(2,1)S(1)}, u32[]{:S(2)}, u32[]{:S(2)}) collective-permute-start(bf16[512,128]{1,0:T(8,128)(2,1)S(1)} %get-tuple-element.45), channel_id=1, source_target_pairs={{0,1},{1,0},{2,7},{3,6},{4,5},{5,4},{6,3},{7,2},{8,9},{9,8},{10,15... | collective-permute-start | bytes 393224 | tf_op jit(solution)/shard_map/ppermute | solution.py:291
  55.1 0.0 collective-permute-done.19.refs_5_
  55.1 0.4 collective-permute-start.10
  55.5 0.1 collective-permute-done.20.refs_6_
  55.6 8.4 %collective-permute-start.11 = (bf16[512,128]{1,0:T(8,128)(2,1)S(1)}, bf16[512,128]{1,0:T(8,128)(2,1)S(1)}, u32[]{:S(2)}, u32[]{:S(2)}) collective-permute-start(bf16[512,128]{1,0:T(8,128)(2,1)S(1)} %get-tuple-element.47), channel_id=1, source_target_pairs={{0,2},{1,7},{2,0},{3,5},{4,6},{5,3},{6,4},{7,1},{8,10},{9,15},{10,... | collective-permute-start | bytes 393224 | tf_op jit(solution)/shard_map/ppermute | solution.py:291
  63.9 4.1 %shard_map.90 = (bf16[512,256]{1,0:T(8,128)(2,1)S(1)}, bf16[512,256]{1,0:T(8,128)(2,1)S(1)}, bf16[512,256]{1,0:T(8,128)(2,1)S(1)}, bf16[512,256]{1,0:T(8,128)(2,1)S(1)}) custom-call(s32[10]{0:T(128)S(1)} %pad_add_fusion.where, bf16[512,128]{1,0:T(8,128)(2,1)S(1)} %collective-permute-done.14.refs_0_, bf16[512,128]{1,0:T(8,128)(2,1)S(1)} %collective-permute-done.15.refs_1_, ...), custom_call_target="tpu_custom_call" | custom-call | flops 1207959552 | bytes 6815784 | tf_op jit(solution)/shard_map/pallas_call | solution.py:252
  68.1 0.0 collective-permute-done.7.refs_0_
  68.1 1.6 %collective-permute-start.21 = (bf16[512,256]{1,0:T(8,128)(2,1)S(1)}, bf16[512,256]{1,0:T(8,128)(2,1)S(1)}, u32[]{:S(2)}, u32[]{:S(2)}) collective-permute-start(bf16[512,256]{1,0:T(8,128)(2,1)S(1)} %get-tuple-element.60), channel_id=1, source_target_pairs={{0,16},{8,24},{16,0},{24,8},{1,17},{9,25},{17,1},{25,9},{2,18},{10... | collective-permute-start | bytes 786440 | tf_op jit(solution)/shard_map/ppermute | solution.py:291
  69.6 0.0 collective-permute-done.8.refs_1_
  69.6 0.0 collective-permute-start.22
  69.6 0.0 collective-permute-done.9.refs_2_
  69.6 0.7 collective-permute-start.23
  70.3 0.0 collective-permute-done.10.refs_3_
  70.3 4.2 %collective-permute-start.12 = (bf16[512,128]{1,0:T(8,128)(2,1)S(1)}, bf16[512,128]{1,0:T(8,128)(2,1)S(1)}, u32[]{:S(2)}, u32[]{:S(2)}) collective-permute-start(bf16[512,128]{1,0:T(8,128)(2,1)S(1)} %get-tuple-element.48), channel_id=1, source_target_pairs={{0,7},{1,2},{2,1},{3,4},{4,3},{5,6},{6,5},{7,0},{8,15},{9,10},{10,... | collective-permute-start | bytes 393224 | tf_op jit(solution)/shard_map/ppermute | solution.py:291
  74.5 0.0 collective-permute-done.11.refs_4_
  74.5 0.5 collective-permute-start.13
  75.1 4.3 %collective-permute-done.12.refs_5_ = bf16[512,128]{1,0:T(8,128)(2,1)S(1)} collective-permute-done((bf16[512,128]{1,0:T(8,128)(2,1)S(1)}, bf16[512,128]{1,0:T(8,128)(2,1)S(1)}, u32[]{:S(2)}, u32[]{:S(2)}) %collective-permute-start.12) | collective-permute-done | bytes 131104 | tf_op jit(solution)/shard_map/ppermute | solution.py:291
  79.4 2.0 %collective-permute-done.13.refs_6_ = bf16[512,128]{1,0:T(8,128)(2,1)S(1)} collective-permute-done((bf16[512,128]{1,0:T(8,128)(2,1)S(1)}, bf16[512,128]{1,0:T(8,128)(2,1)S(1)}, u32[]{:S(2)}, u32[]{:S(2)}) %collective-permute-start.13) | collective-permute-done | bytes 131104 | tf_op jit(solution)/shard_map/ppermute | solution.py:291
  81.4 1.6 %shard_map.89 = bf16[8,512,128]{2,1,0:T(8,128)(2,1)} custom-call(s32[10]{0:T(128)S(1)} %pad_add_fusion.where, bf16[512,128]{1,0:T(8,128)(2,1)S(1)} %collective-permute-done.7.refs_0_, bf16[512,128]{1,0:T(8,128)(2,1)S(1)} %collective-permute-done.8.refs_1_, bf16[512,128]{1,0:T(8,128)(2,1)S(1)} %collective-permute-done.9.refs_2_, ...), custom_call_target="tpu_custom_call" | custom-call | bytes 2097192 | tf_op jit(solution)/shard_map/pallas_call | solution.py:252
  83.0 0.0 collective-permute-done.21
  83.0 0.0 collective-permute-done.22
  83.0 0.0 collective-permute-done.23
  83.0 0.9 %add_multiply_fusion = f32[512,256]{1,0:T(8,128)} fusion(bf16[512,256]{1,0:T(8,128)(2,1)S(1)} %get-tuple-element.63, bf16[512,256]{1,0:T(8,128)(2,1)S(1)} %collective-permute-done.23, bf16[512,256]{1,0:T(8,128)(2,1)S(1)} %collective-permute-done.22, bf16[512,256]{1,0:T(8,128)(2,1)S(1)} %collective-permute-done.21), kind=kLoop, calls=%fused_computation | loop fusion | flops 1048576 | bytes 1572864 | tf_op jit(solution)/shard_map/mul | solution.py:354
Async XLA Ops:
  0.6 27.2 %copy-start = (bf16[9,256,256]{2,1,0:T(8,128)(2,1)S(1)}, bf16[9,256,256]{2,1,0:T(8,128)(2,1)}, u32[]{:S(2)}) copy-start(bf16[9,256,256]{2,1,0:T(8,128)(2,1)} %constant.23.clone.forward.refs_11_.refs_9_) | copy-start | bytes 3538948
  4.2 16.9 %collective-permute-start = (bf16[512,128]{1,0:T(8,128)(2,1)S(1)}, bf16[512,128]{1,0:T(8,128)(2,1)S(1)}, u32[]{:S(2)}, u32[]{:S(2)}) collective-permute-start(bf16[512,128]{1,0:T(8,128)(2,1)S(1)} %get-tuple-element.33), channel_id=1, source_target_pairs={{0,4},{1,5},{2,6},{3,7},{4,0},{5,1},{6,2},{7,3},{8,12},{9,13},{10,... | collective-permute-start | bytes 393224 | tf_op jit(solution)/shard_map/ppermute | solution.py:291
  8.3 18.3 %collective-permute-start.1 = (bf16[512,128]{1,0:T(8,128)(2,1)S(1)}, bf16[512,128]{1,0:T(8,128)(2,1)S(1)}, u32[]{:S(2)}, u32[]{:S(2)}) collective-permute-start(bf16[512,128]{1,0:T(8,128)(2,1)S(1)} %get-tuple-element.34), channel_id=1, source_target_pairs={{0,5},{1,4},{2,3},{3,2},{4,1},{5,0},{6,7},{7,6},{8,13},{9,12},{10,... | collective-permute-start | bytes 393224 | tf_op jit(solution)/shard_map/ppermute | solution.py:291
  9.6 17.0 %collective-permute-start.2 = (bf16[512,128]{1,0:T(8,128)(2,1)S(1)}, bf16[512,128]{1,0:T(8,128)(2,1)S(1)}, u32[]{:S(2)}, u32[]{:S(2)}) collective-permute-start(bf16[512,128]{1,0:T(8,128)(2,1)S(1)} %get-tuple-element.35), channel_id=1, source_target_pairs={{0,1},{1,0},{2,7},{3,6},{4,5},{5,4},{6,3},{7,2},{8,9},{9,8},{10,15... | collective-permute-start | bytes 393224 | tf_op jit(solution)/shard_map/ppermute | solution.py:291
  9.8 16.7 %collective-permute-start.3 = (bf16[512,128]{1,0:T(8,128)(2,1)S(1)}, bf16[512,128]{1,0:T(8,128)(2,1)S(1)}, u32[]{:S(2)}, u32[]{:S(2)}) collective-permute-start(bf16[512,128]{1,0:T(8,128)(2,1)S(1)} %get-tuple-element.36), channel_id=1, source_target_pairs={{0,6},{1,3},{2,4},{3,1},{4,2},{5,7},{6,0},{7,5},{8,14},{9,11},{10,... | collective-permute-start | bytes 393224 | tf_op jit(solution)/shard_map/ppermute | solution.py:291
  13.7 17.2 %collective-permute-start.4 = (bf16[512,128]{1,0:T(8,128)(2,1)S(1)}, bf16[512,128]{1,0:T(8,128)(2,1)S(1)}, u32[]{:S(2)}, u32[]{:S(2)}) collective-permute-start(bf16[512,128]{1,0:T(8,128)(2,1)S(1)} %get-tuple-element.37), channel_id=1, source_target_pairs={{0,2},{1,7},{2,0},{3,5},{4,6},{5,3},{6,4},{7,1},{8,10},{9,15},{10,... | collective-permute-start | bytes 393224 | tf_op jit(solution)/shard_map/ppermute | solution.py:291
  21.1 16.6 %collective-permute-start.5 = (bf16[512,128]{1,0:T(8,128)(2,1)S(1)}, bf16[512,128]{1,0:T(8,128)(2,1)S(1)}, u32[]{:S(2)}, u32[]{:S(2)}) collective-permute-start(bf16[512,128]{1,0:T(8,128)(2,1)S(1)} %get-tuple-element.38), channel_id=1, source_target_pairs={{0,7},{1,2},{2,1},{3,4},{4,3},{5,6},{6,5},{7,0},{8,15},{9,10},{10,... | collective-permute-start | bytes 393224 | tf_op jit(solution)/shard_map/ppermute | solution.py:291
  26.6 11.3 %collective-permute-start.6 = (bf16[512,128]{1,0:T(8,128)(2,1)S(1)}, bf16[512,128]{1,0:T(8,128)(2,1)S(1)}, u32[]{:S(2)}, u32[]{:S(2)}) collective-permute-start(bf16[512,128]{1,0:T(8,128)(2,1)S(1)} %get-tuple-element.39), channel_id=1, source_target_pairs={{0,3},{1,6},{2,5},{3,0},{4,7},{5,2},{6,1},{7,4},{8,11},{9,14},{10,... | collective-permute-start | bytes 393224 | tf_op jit(solution)/shard_map/ppermute | solution.py:291
  26.6 19.1 %collective-permute-start.14 = (bf16[512,128]{1,0:T(8,128)(2,1)S(1)}, bf16[512,128]{1,0:T(8,128)(2,1)S(1)}, u32[]{:S(2)}, u32[]{:S(2)}) collective-permute-start(bf16[512,128]{1,0:T(8,128)(2,1)S(1)} %get-tuple-element.51), channel_id=1, source_target_pairs={{0,4},{1,5},{2,6},{3,7},{4,0},{5,1},{6,2},{7,3},{8,12},{9,13},{10,... | collective-permute-start | bytes 393224 | tf_op jit(solution)/shard_map/ppermute | solution.py:291
  26.6 14.8 %copy-start.1 = (bf16[9,256,256]{2,1,0:T(8,128)(2,1)S(1)}, bf16[9,256,256]{2,1,0:T(8,128)(2,1)}, u32[]{:S(2)}) copy-start(bf16[9,256,256]{2,1,0:T(8,128)(2,1)} %constant.24.clone.refs_12_.refs_10_) | copy-start | bytes 3538948
  26.6 21.1 %collective-permute-start.15 = (bf16[512,128]{1,0:T(8,128)(2,1)S(1)}, bf16[512,128]{1,0:T(8,128)(2,1)S(1)}, u32[]{:S(2)}, u32[]{:S(2)}) collective-permute-start(bf16[512,128]{1,0:T(8,128)(2,1)S(1)} %get-tuple-element.52), channel_id=1, source_target_pairs={{0,5},{1,4},{2,3},{3,2},{4,1},{5,0},{6,7},{7,6},{8,13},{9,12},{10,... | collective-permute-start | bytes 393224 | tf_op jit(solution)/shard_map/ppermute | solution.py:291
  27.8 1.6 %copy-start.2 = (f32[512,1024]{1,0:T(8,128)S(1)}, f32[512,1024]{1,0:T(8,128)}, u32[]{:S(2)}) copy-start(f32[512,1024]{1,0:T(8,128)} %taps.1) | copy-start | bytes 6291460
  30.9 17.1 %collective-permute-start.16 = (bf16[512,128]{1,0:T(8,128)(2,1)S(1)}, bf16[512,128]{1,0:T(8,128)(2,1)S(1)}, u32[]{:S(2)}, u32[]{:S(2)}) collective-permute-start(bf16[512,128]{1,0:T(8,128)(2,1)S(1)} %get-tuple-element.53), channel_id=1, source_target_pairs={{0,1},{1,0},{2,7},{3,6},{4,5},{5,4},{6,3},{7,2},{8,9},{9,8},{10,15... | collective-permute-start | bytes 393224 | tf_op jit(solution)/shard_map/ppermute | solution.py:291
  37.7 13.3 %collective-permute-start.17 = (bf16[512,128]{1,0:T(8,128)(2,1)S(1)}, bf16[512,128]{1,0:T(8,128)(2,1)S(1)}, u32[]{:S(2)}, u32[]{:S(2)}) collective-permute-start(bf16[512,128]{1,0:T(8,128)(2,1)S(1)} %get-tuple-element.54), channel_id=1, source_target_pairs={{0,6},{1,3},{2,4},{3,1},{4,2},{5,7},{6,0},{7,5},{8,14},{9,11},{10,... | collective-permute-start | bytes 393224 | tf_op jit(solution)/shard_map/ppermute | solution.py:291
  37.9 13.2 %collective-permute-start.18 = (bf16[512,128]{1,0:T(8,128)(2,1)S(1)}, bf16[512,128]{1,0:T(8,128)(2,1)S(1)}, u32[]{:S(2)}, u32[]{:S(2)}) collective-permute-start(bf16[512,128]{1,0:T(8,128)(2,1)S(1)} %get-tuple-element.55), channel_id=1, source_target_pairs={{0,2},{1,7},{2,0},{3,5},{4,6},{5,3},{6,4},{7,1},{8,10},{9,15},{10,... | collective-permute-start | bytes 393224 | tf_op jit(solution)/shard_map/ppermute | solution.py:291
  45.7 9.4 %collective-permute-start.19 = (bf16[512,128]{1,0:T(8,128)(2,1)S(1)}, bf16[512,128]{1,0:T(8,128)(2,1)S(1)}, u32[]{:S(2)}, u32[]{:S(2)}) collective-permute-start(bf16[512,128]{1,0:T(8,128)(2,1)S(1)} %get-tuple-element.56), channel_id=1, source_target_pairs={{0,7},{1,2},{2,1},{3,4},{4,3},{5,6},{6,5},{7,0},{8,15},{9,10},{10,... | collective-permute-start | bytes 393224 | tf_op jit(solution)/shard_map/ppermute | solution.py:291
  47.7 7.8 %collective-permute-start.20 = (bf16[512,128]{1,0:T(8,128)(2,1)S(1)}, bf16[512,128]{1,0:T(8,128)(2,1)S(1)}, u32[]{:S(2)}, u32[]{:S(2)}) collective-permute-start(bf16[512,128]{1,0:T(8,128)(2,1)S(1)} %get-tuple-element.57), channel_id=1, source_target_pairs={{0,3},{1,6},{2,5},{3,0},{4,7},{5,2},{6,1},{7,4},{8,11},{9,14},{10,... | collective-permute-start | bytes 393224 | tf_op jit(solution)/shard_map/ppermute | solution.py:291
  47.9 20.1 %collective-permute-start.7 = (bf16[512,128]{1,0:T(8,128)(2,1)S(1)}, bf16[512,128]{1,0:T(8,128)(2,1)S(1)}, u32[]{:S(2)}, u32[]{:S(2)}) collective-permute-start(bf16[512,128]{1,0:T(8,128)(2,1)S(1)} %get-tuple-element.43), channel_id=1, source_target_pairs={{0,4},{1,5},{2,6},{3,7},{4,0},{5,1},{6,2},{7,3},{8,12},{9,13},{10,... | collective-permute-start | bytes 393224 | tf_op jit(solution)/shard_map/ppermute | solution.py:291
  51.1 18.6 %collective-permute-start.8 = (bf16[512,128]{1,0:T(8,128)(2,1)S(1)}, bf16[512,128]{1,0:T(8,128)(2,1)S(1)}, u32[]{:S(2)}, u32[]{:S(2)}) collective-permute-start(bf16[512,128]{1,0:T(8,128)(2,1)S(1)} %get-tuple-element.44), channel_id=1, source_target_pairs={{0,5},{1,4},{2,3},{3,2},{4,1},{5,0},{6,7},{7,6},{8,13},{9,12},{10,... | collective-permute-start | bytes 393224 | tf_op jit(solution)/shard_map/ppermute | solution.py:291
  51.1 18.6 %collective-permute-start.9 = (bf16[512,128]{1,0:T(8,128)(2,1)S(1)}, bf16[512,128]{1,0:T(8,128)(2,1)S(1)}, u32[]{:S(2)}, u32[]{:S(2)}) collective-permute-start(bf16[512,128]{1,0:T(8,128)(2,1)S(1)} %get-tuple-element.45), channel_id=1, source_target_pairs={{0,1},{1,0},{2,7},{3,6},{4,5},{5,4},{6,3},{7,2},{8,9},{9,8},{10,15... | collective-permute-start | bytes 393224 | tf_op jit(solution)/shard_map/ppermute | solution.py:291
  55.1 15.2 %collective-permute-start.10 = (bf16[512,128]{1,0:T(8,128)(2,1)S(1)}, bf16[512,128]{1,0:T(8,128)(2,1)S(1)}, u32[]{:S(2)}, u32[]{:S(2)}) collective-permute-start(bf16[512,128]{1,0:T(8,128)(2,1)S(1)} %get-tuple-element.46), channel_id=1, source_target_pairs={{0,6},{1,3},{2,4},{3,1},{4,2},{5,7},{6,0},{7,5},{8,14},{9,11},{10,... | collective-permute-start | bytes 393224 | tf_op jit(solution)/shard_map/ppermute | solution.py:291
  55.6 19.0 %collective-permute-start.11 = (bf16[512,128]{1,0:T(8,128)(2,1)S(1)}, bf16[512,128]{1,0:T(8,128)(2,1)S(1)}, u32[]{:S(2)}, u32[]{:S(2)}) collective-permute-start(bf16[512,128]{1,0:T(8,128)(2,1)S(1)} %get-tuple-element.47), channel_id=1, source_target_pairs={{0,2},{1,7},{2,0},{3,5},{4,6},{5,3},{6,4},{7,1},{8,10},{9,15},{10,... | collective-permute-start | bytes 393224 | tf_op jit(solution)/shard_map/ppermute | solution.py:291
  68.1 14.9 %collective-permute-start.21 = (bf16[512,256]{1,0:T(8,128)(2,1)S(1)}, bf16[512,256]{1,0:T(8,128)(2,1)S(1)}, u32[]{:S(2)}, u32[]{:S(2)}) collective-permute-start(bf16[512,256]{1,0:T(8,128)(2,1)S(1)} %get-tuple-element.60), channel_id=1, source_target_pairs={{0,16},{8,24},{16,0},{24,8},{1,17},{9,25},{17,1},{25,9},{2,18},{10... | collective-permute-start | bytes 786440 | tf_op jit(solution)/shard_map/ppermute | solution.py:291
  69.6 13.4 %collective-permute-start.22 = (bf16[512,256]{1,0:T(8,128)(2,1)S(1)}, bf16[512,256]{1,0:T(8,128)(2,1)S(1)}, u32[]{:S(2)}, u32[]{:S(2)}) collective-permute-start(bf16[512,256]{1,0:T(8,128)(2,1)S(1)} %get-tuple-element.61), channel_id=1, source_target_pairs={{0,24},{8,16},{16,8},{24,0},{1,25},{9,17},{17,9},{25,1},{2,26},{10... | collective-permute-start | bytes 786440 | tf_op jit(solution)/shard_map/ppermute | solution.py:291
  69.6 13.4 %collective-permute-start.23 = (bf16[512,256]{1,0:T(8,128)(2,1)S(1)}, bf16[512,256]{1,0:T(8,128)(2,1)S(1)}, u32[]{:S(2)}, u32[]{:S(2)}) collective-permute-start(bf16[512,256]{1,0:T(8,128)(2,1)S(1)} %get-tuple-element.62), channel_id=1, source_target_pairs={{0,8},{8,0},{16,24},{24,16},{1,9},{9,1},{17,25},{25,17},{2,10},{10... | collective-permute-start | bytes 786440 | tf_op jit(solution)/shard_map/ppermute | solution.py:291
  70.3 9.1 %collective-permute-start.12 = (bf16[512,128]{1,0:T(8,128)(2,1)S(1)}, bf16[512,128]{1,0:T(8,128)(2,1)S(1)}, u32[]{:S(2)}, u32[]{:S(2)}) collective-permute-start(bf16[512,128]{1,0:T(8,128)(2,1)S(1)} %get-tuple-element.48), channel_id=1, source_target_pairs={{0,7},{1,2},{2,1},{3,4},{4,3},{5,6},{6,5},{7,0},{8,15},{9,10},{10,... | collective-permute-start | bytes 393224 | tf_op jit(solution)/shard_map/ppermute | solution.py:291
  74.5 6.9 %collective-permute-start.13 = (bf16[512,128]{1,0:T(8,128)(2,1)S(1)}, bf16[512,128]{1,0:T(8,128)(2,1)S(1)}, u32[]{:S(2)}, u32[]{:S(2)}) collective-permute-start(bf16[512,128]{1,0:T(8,128)(2,1)S(1)} %get-tuple-element.49), channel_id=1, source_target_pairs={{0,3},{1,6},{2,5},{3,0},{4,7},{5,2},{6,1},{7,4},{8,11},{9,14},{10,... | collective-permute-start | bytes 393224 | tf_op jit(solution)/shard_map/ppermute | solution.py:291

commit v18 on v11

--- a/solution.py
+++ b/solution.py
@@ -174,7 +174,8 @@
         whole[lax.bitwise_xor(where[0], k)] = piece[...]
 
 
-def taps_kernel(taps, forward, taps_spec, mid):
+def taps_kernel(taps, forward, *refs):
+    taps_spec, mid = refs[-2:]
     rows, width = (taps.shape[0], taps.shape[1] // BLOCKS)
     split_rows(lambda p, at: taps[at, p * width : (p + 1) * width], mid, rows, width)
     for r in range(GROUPS):
@@ -283,7 +284,7 @@
     channels, span = saved_input.shape[1:]
     rows, length = long_filter.shape
     width = length // BLOCKS
-    grad_order, input_order, back_order = (spread(count, o) for o in ((1, 2, 4, 5, 6, 7, 3), (4, 5, 1, 6, 2, 7, 3), (1, 2, 3, 4, 5, 6, 7)))
+    grad_order, input_order, back_order = (spread(count, o) for o in ((4, 1, 5, 2, 6, 7, 3), (4, 1, 5, 2, 6, 3, 7), (1, 4, 2, 5, 6, 7, 3)))
     late = 2
     at = count - 1 - late
     every = range(count + 8)
@@ -308,7 +309,17 @@
     )
     grad_pieces, input_pieces = pieces[:count], pieces[count:]
     grad_blocks = exchange(grad_pieces, grad_order, "ctx", count)
-    (taps_spec,) = call(taps_kernel, [long_filter, forward], [spec], [mid], flops=work)
+    ahead = 5
+    *input_pieces[:ahead], taps_spec = call(
+        taps_kernel,
+        [long_filter, forward, *input_pieces[:ahead]],
+        [piece] * ahead + [spec],
+        [mid],
+        flops=work,
+        streams=range(2, 2 + ahead),
+        out_streams=range(ahead),
+        aliases={2 + i: i for i in range(ahead)},
+    )
     passed = [*input_pieces[at : at + late]]
     *back, grad_spec = call(
         functools.partial(back_kernel, grad_order, back_order, late),

time: 84.2 us -> 82.7 us (0.982)
  the two profiles are of different devices: /device:TPU:9 before, /device:TPU:0 now
where the time goes in v18:
time: 82.7 us; the launch traced here: 82.2 us
  starting transfers between devices  44.1 us (53%)
  waiting for transfers between devices  20.7 us (25%)
  Pallas kernels  14.1 us (17%)
  local copies, waits for them, and re-layouts  1.6 us (2%)
  other arithmetic  1.01 us (1%)
    ppermute x24, starting transfers between devices, exchange(): lax.ppermute(piece, axis, [(i, i ^ k) for i in range(size)])  44.1 us
    ppermute x24, waiting for transfers between devices, exchange(): lax.ppermute(piece, axis, [(i, i ^ k) for i in range(size)])  20.7 us
    pallas_call x5, Pallas kernels, call(): pl.pallas_call(kernel, out_shape=list(outs), in_specs=specs, out_specs=[s...  14.1 us
  transfers between devices with their start and end apart: 24, of which 6 were waited for; matrix products, arithmetic and copies ran while one was open for 0% of the time, Pallas kernels for 14%

profile of v18, /device:TPU:0, one launch (start us, length us, event | category | flops | bytes accessed | tf_op | source)
XLA Modules:
  0.0 82.2 jit_solution(11429158906273492732)
XLA Ops:
  0.6 0.0 copy-start
  0.6 0.1 pad_add_fusion.where
  0.7 2.7 %shard_map.77 = (bf16[512,128]{1,0:T(8,128)(2,1)S(1)}, bf16[512,128]{1,0:T(8,128)(2,1)S(1)}, bf16[512,128]{1,0:T(8,128)(2,1)S(1)}, bf16[512,128]{1,0:T(8,128)(2,...) custom-call(s32[2]{0:T(128)S(1)} %pad_add_fusion.where, ...), custom_call_target="tpu_custom_call" | custom-call | bytes 5242888 | tf_op jit(solution)/shard_map/pallas_call | solution.py:253
  3.4 0.0 copy-start.1
  3.4 4.1 %collective-permute-start = (bf16[512,128]{1,0:T(8,128)(2,1)S(1)}, bf16[512,128]{1,0:T(8,128)(2,1)S(1)}, u32[]{:S(2)}, u32[]{:S(2)}) collective-permute-start(bf16[512,128]{1,0:T(8,128)(2,1)S(1)} %get-tuple-element.39), channel_id=1, source_target_pairs={{0,4},{1,5},{2,6},{3,7},{4,0},{5,1},{6,2},{7,3},{8,12},{9,13},{10,... | collective-permute-start | bytes 393224 | tf_op jit(solution)/shard_map/ppermute | solution.py:278
  7.5 1.5 %collective-permute-start.1 = (bf16[512,128]{1,0:T(8,128)(2,1)S(1)}, bf16[512,128]{1,0:T(8,128)(2,1)S(1)}, u32[]{:S(2)}, u32[]{:S(2)}) collective-permute-start(bf16[512,128]{1,0:T(8,128)(2,1)S(1)} %get-tuple-element.40), channel_id=1, source_target_pairs={{0,1},{1,0},{2,3},{3,2},{4,5},{5,4},{6,7},{7,6},{8,9},{9,8},{10,11... | collective-permute-start | bytes 393224 | tf_op jit(solution)/shard_map/ppermute | solution.py:278
  9.0 0.0 collective-permute-start.2
  9.1 1.8 %collective-permute-start.3 = (bf16[512,128]{1,0:T(8,128)(2,1)S(1)}, bf16[512,128]{1,0:T(8,128)(2,1)S(1)}, u32[]{:S(2)}, u32[]{:S(2)}) collective-permute-start(bf16[512,128]{1,0:T(8,128)(2,1)S(1)} %get-tuple-element.42), channel_id=1, source_target_pairs={{0,2},{1,3},{2,0},{3,1},{4,6},{5,7},{6,4},{7,5},{8,10},{9,11},{10,... | collective-permute-start | bytes 393224 | tf_op jit(solution)/shard_map/ppermute | solution.py:278
  10.9 2.5 %collective-permute-start.4 = (bf16[512,128]{1,0:T(8,128)(2,1)S(1)}, bf16[512,128]{1,0:T(8,128)(2,1)S(1)}, u32[]{:S(2)}, u32[]{:S(2)}) collective-permute-start(bf16[512,128]{1,0:T(8,128)(2,1)S(1)} %get-tuple-element.43), channel_id=1, source_target_pairs={{0,6},{1,7},{2,4},{3,5},{4,2},{5,3},{6,0},{7,1},{8,14},{9,15},{10,... | collective-permute-start | bytes 393224 | tf_op jit(solution)/shard_map/ppermute | solution.py:278
  13.4 4.8 %collective-permute-done.refs_0_ = bf16[512,128]{1,0:T(8,128)(2,1)S(1)} collective-permute-done((bf16[512,128]{1,0:T(8,128)(2,1)S(1)}, bf16[512,128]{1,0:T(8,128)(2,1)S(1)}, u32[]{:S(2)}, u32[]{:S(2)}) %collective-permute-start) | collective-permute-done | bytes 131104 | tf_op jit(solution)/shard_map/ppermute | solution.py:278
  18.2 5.9 %collective-permute-start.5 = (bf16[512,128]{1,0:T(8,128)(2,1)S(1)}, bf16[512,128]{1,0:T(8,128)(2,1)S(1)}, u32[]{:S(2)}, u32[]{:S(2)}) collective-permute-start(bf16[512,128]{1,0:T(8,128)(2,1)S(1)} %get-tuple-element.44), channel_id=1, source_target_pairs={{0,7},{1,6},{2,5},{3,4},{4,3},{5,2},{6,1},{7,0},{8,15},{9,14},{10,... | collective-permute-start | bytes 393224 | tf_op jit(solution)/shard_map/ppermute | solution.py:278
  24.1 0.0 collective-permute-done.1.refs_1_
  24.1 0.0 collective-permute-start.6
  24.1 0.0 copy-done
  24.1 0.0 copy-start.2
  24.1 1.6 %copy-done.2 = f32[512,1024]{1,0:T(8,128)S(1)} copy-done((f32[512,1024]{1,0:T(8,128)S(1)}, f32[512,1024]{1,0:T(8,128)}, u32[]{:S(2)}) %copy-start.2) | copy-done | bytes 2097176
  25.7 1.5 %shard_map.78 = (bf16[512,128]{1,0:T(8,128)(2,1)S(1)}, bf16[512,128]{1,0:T(8,128)(2,1)S(1)}, bf16[512,128]{1,0:T(8,128)(2,1)S(1)}, bf16[512,128]{1,0:T(8,128)(2,...) custom-call(f32[512,1024]{1,0:T(8,128)S(1)} %copy-done.2, ...), custom_call_target="tpu_custom_call", output_to_operand_aliasing={{0}: (2, {}), {1}: (3, {}), {2}: (4, {}), {3}: (5, {}), {4}... | custom-call | flops 603979776 | bytes 6946816 | tf_op jit(solution)/shard_map/pallas_call | solution.py:253
  27.2 0.0 collective-permute-done.2.refs_2_
  27.2 0.6 collective-permute-start.14
  27.8 0.0 collective-permute-done.3.refs_3_
  27.8 1.0 %collective-permute-start.15 = (bf16[512,128]{1,0:T(8,128)(2,1)S(1)}, bf16[512,128]{1,0:T(8,128)(2,1)S(1)}, u32[]{:S(2)}, u32[]{:S(2)}) collective-permute-start(bf16[512,128]{1,0:T(8,128)(2,1)S(1)} %get-tuple-element.64), channel_id=1, source_target_pairs={{0,1},{1,0},{2,3},{3,2},{4,5},{5,4},{6,7},{7,6},{8,9},{9,8},{10,11... | collective-permute-start | bytes 393224 | tf_op jit(solution)/shard_map/ppermute | solution.py:278
  28.8 0.0 collective-permute-done.4.refs_4_
  28.8 5.6 %collective-permute-start.16 = (bf16[512,128]{1,0:T(8,128)(2,1)S(1)}, bf16[512,128]{1,0:T(8,128)(2,1)S(1)}, u32[]{:S(2)}, u32[]{:S(2)}) collective-permute-start(bf16[512,128]{1,0:T(8,128)(2,1)S(1)} %get-tuple-element.65), channel_id=1, source_target_pairs={{0,5},{1,4},{2,7},{3,6},{4,1},{5,0},{6,3},{7,2},{8,13},{9,12},{10,... | collective-permute-start | bytes 393224 | tf_op jit(solution)/shard_map/ppermute | solution.py:278
  34.4 0.0 collective-permute-done.5.refs_5_
  34.4 4.6 %collective-permute-start.17 = (bf16[512,128]{1,0:T(8,128)(2,1)S(1)}, bf16[512,128]{1,0:T(8,128)(2,1)S(1)}, u32[]{:S(2)}, u32[]{:S(2)}) collective-permute-start(bf16[512,128]{1,0:T(8,128)(2,1)S(1)} %get-tuple-element.66), channel_id=1, source_target_pairs={{0,2},{1,3},{2,0},{3,1},{4,6},{5,7},{6,4},{7,5},{8,10},{9,11},{10,... | collective-permute-start | bytes 393224 | tf_op jit(solution)/shard_map/ppermute | solution.py:278
  39.0 0.0 collective-permute-done.6.refs_6_
  39.0 2.5 %collective-permute-start.18 = (bf16[512,128]{1,0:T(8,128)(2,1)S(1)}, bf16[512,128]{1,0:T(8,128)(2,1)S(1)}, u32[]{:S(2)}, u32[]{:S(2)}) collective-permute-start(bf16[512,128]{1,0:T(8,128)(2,1)S(1)} %get-tuple-element.67), channel_id=1, source_target_pairs={{0,6},{1,7},{2,4},{3,5},{4,2},{5,3},{6,0},{7,1},{8,14},{9,15},{10,... | collective-permute-start | bytes 393224 | tf_op jit(solution)/shard_map/ppermute | solution.py:278
  41.5 0.0 copy-done.1
  41.5 4.2 %shard_map.79 = (bf16[512,128]{1,0:T(8,128)(2,1)S(1)}, bf16[512,128]{1,0:T(8,128)(2,1)S(1)}, bf16[512,128]{1,0:T(8,128)(2,1)S(1)}, bf16[512,128]{1,0:T(8,128)(2,...) custom-call(s32[2]{0:T(128)S(1)} %pad_add_fusion.where, ...), custom_call_target="tpu_custom_call", output_to_operand_aliasing={{0}: (9, {}), {1}: (10, {})} | custom-call | flops 1207959552 | bytes 9699336 | tf_op jit(solution)/shard_map/pallas_call | solution.py:253
  45.8 0.0 collective-permute-done.14.refs_0_
  45.8 0.1 collective-permute-start.19
  45.9 0.0 collective-permute-done.15.refs_1_
  45.9 1.3 %collective-permute-start.20 = (bf16[512,128]{1,0:T(8,128)(2,1)S(1)}, bf16[512,128]{1,0:T(8,128)(2,1)S(1)}, u32[]{:S(2)}, u32[]{:S(2)}) collective-permute-start(bf16[512,128]{1,0:T(8,128)(2,1)S(1)} %get-tuple-element.69), channel_id=1, source_target_pairs={{0,7},{1,6},{2,5},{3,4},{4,3},{5,2},{6,1},{7,0},{8,15},{9,14},{10,... | collective-permute-start | bytes 393224 | tf_op jit(solution)/shard_map/ppermute | solution.py:278
  47.2 0.0 collective-permute-done.16.refs_2_
  47.2 1.5 %collective-permute-start.7 = (bf16[512,128]{1,0:T(8,128)(2,1)S(1)}, bf16[512,128]{1,0:T(8,128)(2,1)S(1)}, u32[]{:S(2)}, u32[]{:S(2)}) collective-permute-start(bf16[512,128]{1,0:T(8,128)(2,1)S(1)} %get-tuple-element.55), channel_id=1, source_target_pairs={{0,1},{1,0},{2,3},{3,2},{4,5},{5,4},{6,7},{7,6},{8,9},{9,8},{10,11... | collective-permute-start | bytes 393224 | tf_op jit(solution)/shard_map/ppermute | solution.py:278
  48.7 0.0 collective-permute-done.17.refs_3_
  48.7 1.6 %collective-permute-start.8 = (bf16[512,128]{1,0:T(8,128)(2,1)S(1)}, bf16[512,128]{1,0:T(8,128)(2,1)S(1)}, u32[]{:S(2)}, u32[]{:S(2)}) collective-permute-start(bf16[512,128]{1,0:T(8,128)(2,1)S(1)} %get-tuple-element.56), channel_id=1, source_target_pairs={{0,4},{1,5},{2,6},{3,7},{4,0},{5,1},{6,2},{7,3},{8,12},{9,13},{10,... | collective-permute-start | bytes 393224 | tf_op jit(solution)/shard_map/ppermute | solution.py:278
  50.3 0.0 collective-permute-done.18.refs_4_
  50.3 1.5 %collective-permute-start.9 = (bf16[512,128]{1,0:T(8,128)(2,1)S(1)}, bf16[512,128]{1,0:T(8,128)(2,1)S(1)}, u32[]{:S(2)}, u32[]{:S(2)}) collective-permute-start(bf16[512,128]{1,0:T(8,128)(2,1)S(1)} %get-tuple-element.57), channel_id=1, source_target_pairs={{0,2},{1,3},{2,0},{3,1},{4,6},{5,7},{6,4},{7,5},{8,10},{9,11},{10,... | collective-permute-start | bytes 393224 | tf_op jit(solution)/shard_map/ppermute | solution.py:278
  51.8 3.5 %collective-permute-done.19.refs_5_ = bf16[512,128]{1,0:T(8,128)(2,1)S(1)} collective-permute-done((bf16[512,128]{1,0:T(8,128)(2,1)S(1)}, bf16[512,128]{1,0:T(8,128)(2,1)S(1)}, u32[]{:S(2)}, u32[]{:S(2)}) %collective-permute-start.19) | collective-permute-done | bytes 131104 | tf_op jit(solution)/shard_map/ppermute | solution.py:278
  55.3 0.0 collective-permute-start.10
  55.3 0.0 collective-permute-done.20.refs_6_
  55.3 1.7 %collective-permute-start.11 = (bf16[512,128]{1,0:T(8,128)(2,1)S(1)}, bf16[512,128]{1,0:T(8,128)(2,1)S(1)}, u32[]{:S(2)}, u32[]{:S(2)}) collective-permute-start(bf16[512,128]{1,0:T(8,128)(2,1)S(1)} %get-tuple-element.59), channel_id=1, source_target_pairs={{0,6},{1,7},{2,4},{3,5},{4,2},{5,3},{6,0},{7,1},{8,14},{9,15},{10,... | collective-permute-start | bytes 393224 | tf_op jit(solution)/shard_map/ppermute | solution.py:278
  57.0 4.1 %shard_map.81 = (bf16[512,256]{1,0:T(8,128)(2,1)S(1)}, bf16[512,256]{1,0:T(8,128)(2,1)S(1)}, bf16[512,256]{1,0:T(8,128)(2,1)S(1)}, bf16[512,256]{1,0:T(8,128)(2,1)S(1)}) custom-call(s32[2]{0:T(128)S(1)} %pad_add_fusion.where, bf16[512,128]{1,0:T(8,128)(2,1)S(1)} %collective-permute-done.14.refs_0_, bf16[512,128]{1,0:T(8,128)(2,1)S(1)} %collective-permute-done.15.refs_1_, ...), custom_call_target="tpu_custom_call" | custom-call | flops 1207959552 | bytes 6815752 | tf_op jit(solution)/shard_map/pallas_call | solution.py:253
  61.1 0.0 collective-permute-done.7.refs_0_
  61.1 1.6 %collective-permute-start.21 = (bf16[512,256]{1,0:T(8,128)(2,1)S(1)}, bf16[512,256]{1,0:T(8,128)(2,1)S(1)}, u32[]{:S(2)}, u32[]{:S(2)}) collective-permute-start(bf16[512,256]{1,0:T(8,128)(2,1)S(1)} %get-tuple-element.72), channel_id=1, source_target_pairs={{0,16},{8,24},{16,0},{24,8},{1,17},{9,25},{17,1},{25,9},{2,18},{10... | collective-permute-start | bytes 786440 | tf_op jit(solution)/shard_map/ppermute | solution.py:278
  62.6 4.8 %collective-permute-done.8.refs_1_ = bf16[512,128]{1,0:T(8,128)(2,1)S(1)} collective-permute-done((bf16[512,128]{1,0:T(8,128)(2,1)S(1)}, bf16[512,128]{1,0:T(8,128)(2,1)S(1)}, u32[]{:S(2)}, u32[]{:S(2)}) %collective-permute-start.8) | collective-permute-done | bytes 131104 | tf_op jit(solution)/shard_map/ppermute | solution.py:278
  67.5 0.0 collective-permute-start.22
  67.5 0.0 collective-permute-done.9.refs_2_
  67.5 1.6 %collective-permute-start.23 = (bf16[512,256]{1,0:T(8,128)(2,1)S(1)}, bf16[512,256]{1,0:T(8,128)(2,1)S(1)}, u32[]{:S(2)}, u32[]{:S(2)}) collective-permute-start(bf16[512,256]{1,0:T(8,128)(2,1)S(1)} %get-tuple-element.74), channel_id=1, source_target_pairs={{0,8},{8,0},{16,24},{24,16},{1,9},{9,1},{17,25},{25,17},{2,10},{10... | collective-permute-start | bytes 786440 | tf_op jit(solution)/shard_map/ppermute | solution.py:278
  69.1 0.6 collective-permute-done.10.refs_3_
  69.7 3.1 %collective-permute-start.12 = (bf16[512,128]{1,0:T(8,128)(2,1)S(1)}, bf16[512,128]{1,0:T(8,128)(2,1)S(1)}, u32[]{:S(2)}, u32[]{:S(2)}) collective-permute-start(bf16[512,128]{1,0:T(8,128)(2,1)S(1)} %get-tuple-element.60), channel_id=1, source_target_pairs={{0,7},{1,6},{2,5},{3,4},{4,3},{5,2},{6,1},{7,0},{8,15},{9,14},{10,... | collective-permute-start | bytes 393224 | tf_op jit(solution)/shard_map/ppermute | solution.py:278
  72.8 0.0 collective-permute-done.11.refs_4_
  72.8 0.0 collective-permute-start.13
  72.9 5.3 %collective-permute-done.12.refs_5_ = bf16[512,128]{1,0:T(8,128)(2,1)S(1)} collective-permute-done((bf16[512,128]{1,0:T(8,128)(2,1)S(1)}, bf16[512,128]{1,0:T(8,128)(2,1)S(1)}, u32[]{:S(2)}, u32[]{:S(2)}) %collective-permute-start.12) | collective-permute-done | bytes 131104 | tf_op jit(solution)/shard_map/ppermute | solution.py:278
  78.1 1.6 %collective-permute-done.13.refs_6_ = bf16[512,128]{1,0:T(8,128)(2,1)S(1)} collective-permute-done((bf16[512,128]{1,0:T(8,128)(2,1)S(1)}, bf16[512,128]{1,0:T(8,128)(2,1)S(1)}, u32[]{:S(2)}, u32[]{:S(2)}) %collective-permute-start.13) | collective-permute-done | bytes 131104 | tf_op jit(solution)/shard_map/ppermute | solution.py:278
  79.7 1.6 %shard_map.80 = bf16[8,512,128]{2,1,0:T(8,128)(2,1)} custom-call(s32[2]{0:T(128)S(1)} %pad_add_fusion.where, bf16[512,128]{1,0:T(8,128)(2,1)S(1)} %collective-permute-done.7.refs_0_, bf16[512,128]{1,0:T(8,128)(2,1)S(1)} %collective-permute-done.8.refs_1_, bf16[512,128]{1,0:T(8,128)(2,1)S(1)} %collective-permute-done.9.refs_2_, ...), custom_call_target="tpu_custom_call" | custom-call | bytes 2097160 | tf_op jit(solution)/shard_map/pallas_call | solution.py:253
  81.3 0.0 collective-permute-done.21
  81.3 0.0 collective-permute-done.22
  81.3 0.0 collective-permute-done.23
  81.3 0.9 %add_multiply_fusion = f32[512,256]{1,0:T(8,128)} fusion(bf16[512,256]{1,0:T(8,128)(2,1)S(1)} %get-tuple-element.75, bf16[512,256]{1,0:T(8,128)(2,1)S(1)} %collective-permute-done.23, bf16[512,256]{1,0:T(8,128)(2,1)S(1)} %collective-permute-done.22, bf16[512,256]{1,0:T(8,128)(2,1)S(1)} %collective-permute-done.21), kind=kLoop, calls=%fused_computation | loop fusion | flops 1048576 | bytes 1572864 | tf_op jit(solution)/shard_map/mul | solution.py:347
Async XLA Ops:
  0.6 23.5 %copy-start = (bf16[9,256,256]{2,1,0:T(8,128)(2,1)S(1)}, bf16[9,256,256]{2,1,0:T(8,128)(2,1)}, u32[]{:S(2)}) copy-start(bf16[9,256,256]{2,1,0:T(8,128)(2,1)} %constant.14.clone.forward.refs_11_.refs_9_) | copy-start | bytes 3538948
  3.4 38.1 %copy-start.1 = (bf16[9,256,256]{2,1,0:T(8,128)(2,1)S(1)}, bf16[9,256,256]{2,1,0:T(8,128)(2,1)}, u32[]{:S(2)}) copy-start(bf16[9,256,256]{2,1,0:T(8,128)(2,1)} %constant.15.clone.refs_12_.refs_10_) | copy-start | bytes 3538948
  3.4 14.8 %collective-permute-start = (bf16[512,128]{1,0:T(8,128)(2,1)S(1)}, bf16[512,128]{1,0:T(8,128)(2,1)S(1)}, u32[]{:S(2)}, u32[]{:S(2)}) collective-permute-start(bf16[512,128]{1,0:T(8,128)(2,1)S(1)} %get-tuple-element.39), channel_id=1, source_target_pairs={{0,4},{1,5},{2,6},{3,7},{4,0},{5,1},{6,2},{7,3},{8,12},{9,13},{10,... | collective-permute-start | bytes 393224 | tf_op jit(solution)/shard_map/ppermute | solution.py:278
  7.5 16.6 %collective-permute-start.1 = (bf16[512,128]{1,0:T(8,128)(2,1)S(1)}, bf16[512,128]{1,0:T(8,128)(2,1)S(1)}, u32[]{:S(2)}, u32[]{:S(2)}) collective-permute-start(bf16[512,128]{1,0:T(8,128)(2,1)S(1)} %get-tuple-element.40), channel_id=1, source_target_pairs={{0,1},{1,0},{2,3},{3,2},{4,5},{5,4},{6,7},{7,6},{8,9},{9,8},{10,11... | collective-permute-start | bytes 393224 | tf_op jit(solution)/shard_map/ppermute | solution.py:278
  9.0 18.2 %collective-permute-start.2 = (bf16[512,128]{1,0:T(8,128)(2,1)S(1)}, bf16[512,128]{1,0:T(8,128)(2,1)S(1)}, u32[]{:S(2)}, u32[]{:S(2)}) collective-permute-start(bf16[512,128]{1,0:T(8,128)(2,1)S(1)} %get-tuple-element.41), channel_id=1, source_target_pairs={{0,5},{1,4},{2,7},{3,6},{4,1},{5,0},{6,3},{7,2},{8,13},{9,12},{10,... | collective-permute-start | bytes 393224 | tf_op jit(solution)/shard_map/ppermute | solution.py:278
  9.1 18.8 %collective-permute-start.3 = (bf16[512,128]{1,0:T(8,128)(2,1)S(1)}, bf16[512,128]{1,0:T(8,128)(2,1)S(1)}, u32[]{:S(2)}, u32[]{:S(2)}) collective-permute-start(bf16[512,128]{1,0:T(8,128)(2,1)S(1)} %get-tuple-element.42), channel_id=1, source_target_pairs={{0,2},{1,3},{2,0},{3,1},{4,6},{5,7},{6,4},{7,5},{8,10},{9,11},{10,... | collective-permute-start | bytes 393224 | tf_op jit(solution)/shard_map/ppermute | solution.py:278
  10.9 18.0 %collective-permute-start.4 = (bf16[512,128]{1,0:T(8,128)(2,1)S(1)}, bf16[512,128]{1,0:T(8,128)(2,1)S(1)}, u32[]{:S(2)}, u32[]{:S(2)}) collective-permute-start(bf16[512,128]{1,0:T(8,128)(2,1)S(1)} %get-tuple-element.43), channel_id=1, source_target_pairs={{0,6},{1,7},{2,4},{3,5},{4,2},{5,3},{6,0},{7,1},{8,14},{9,15},{10,... | collective-permute-start | bytes 393224 | tf_op jit(solution)/shard_map/ppermute | solution.py:278
  18.2 16.2 %collective-permute-start.5 = (bf16[512,128]{1,0:T(8,128)(2,1)S(1)}, bf16[512,128]{1,0:T(8,128)(2,1)S(1)}, u32[]{:S(2)}, u32[]{:S(2)}) collective-permute-start(bf16[512,128]{1,0:T(8,128)(2,1)S(1)} %get-tuple-element.44), channel_id=1, source_target_pairs={{0,7},{1,6},{2,5},{3,4},{4,3},{5,2},{6,1},{7,0},{8,15},{9,14},{10,... | collective-permute-start | bytes 393224 | tf_op jit(solution)/shard_map/ppermute | solution.py:278
  24.1 14.9 %collective-permute-start.6 = (bf16[512,128]{1,0:T(8,128)(2,1)S(1)}, bf16[512,128]{1,0:T(8,128)(2,1)S(1)}, u32[]{:S(2)}, u32[]{:S(2)}) collective-permute-start(bf16[512,128]{1,0:T(8,128)(2,1)S(1)} %get-tuple-element.45), channel_id=1, source_target_pairs={{0,3},{1,2},{2,1},{3,0},{4,7},{5,6},{6,5},{7,4},{8,11},{9,10},{10,... | collective-permute-start | bytes 393224 | tf_op jit(solution)/shard_map/ppermute | solution.py:278
  24.1 1.6 %copy-start.2 = (f32[512,1024]{1,0:T(8,128)S(1)}, f32[512,1024]{1,0:T(8,128)}, u32[]{:S(2)}) copy-start(f32[512,1024]{1,0:T(8,128)} %taps.1) | copy-start | bytes 6291460
  27.2 18.6 %collective-permute-start.14 = (bf16[512,128]{1,0:T(8,128)(2,1)S(1)}, bf16[512,128]{1,0:T(8,128)(2,1)S(1)}, u32[]{:S(2)}, u32[]{:S(2)}) collective-permute-start(bf16[512,128]{1,0:T(8,128)(2,1)S(1)} %get-tuple-element.63), channel_id=1, source_target_pairs={{0,4},{1,5},{2,6},{3,7},{4,0},{5,1},{6,2},{7,3},{8,12},{9,13},{10,... | collective-permute-start | bytes 393224 | tf_op jit(solution)/shard_map/ppermute | solution.py:278
  27.8 18.0 %collective-permute-start.15 = (bf16[512,128]{1,0:T(8,128)(2,1)S(1)}, bf16[512,128]{1,0:T(8,128)(2,1)S(1)}, u32[]{:S(2)}, u32[]{:S(2)}) collective-permute-start(bf16[512,128]{1,0:T(8,128)(2,1)S(1)} %get-tuple-element.64), channel_id=1, source_target_pairs={{0,1},{1,0},{2,3},{3,2},{4,5},{5,4},{6,7},{7,6},{8,9},{9,8},{10,11... | collective-permute-start | bytes 393224 | tf_op jit(solution)/shard_map/ppermute | solution.py:278
  28.8 18.3 %collective-permute-start.16 = (bf16[512,128]{1,0:T(8,128)(2,1)S(1)}, bf16[512,128]{1,0:T(8,128)(2,1)S(1)}, u32[]{:S(2)}, u32[]{:S(2)}) collective-permute-start(bf16[512,128]{1,0:T(8,128)(2,1)S(1)} %get-tuple-element.65), channel_id=1, source_target_pairs={{0,5},{1,4},{2,7},{3,6},{4,1},{5,0},{6,3},{7,2},{8,13},{9,12},{10,... | collective-permute-start | bytes 393224 | tf_op jit(solution)/shard_map/ppermute | solution.py:278
  34.4 14.3 %collective-permute-start.17 = (bf16[512,128]{1,0:T(8,128)(2,1)S(1)}, bf16[512,128]{1,0:T(8,128)(2,1)S(1)}, u32[]{:S(2)}, u32[]{:S(2)}) collective-permute-start(bf16[512,128]{1,0:T(8,128)(2,1)S(1)} %get-tuple-element.66), channel_id=1, source_target_pairs={{0,2},{1,3},{2,0},{3,1},{4,6},{5,7},{6,4},{7,5},{8,10},{9,11},{10,... | collective-permute-start | bytes 393224 | tf_op jit(solution)/shard_map/ppermute | solution.py:278
  39.0 11.3 %collective-permute-start.18 = (bf16[512,128]{1,0:T(8,128)(2,1)S(1)}, bf16[512,128]{1,0:T(8,128)(2,1)S(1)}, u32[]{:S(2)}, u32[]{:S(2)}) collective-permute-start(bf16[512,128]{1,0:T(8,128)(2,1)S(1)} %get-tuple-element.67), channel_id=1, source_target_pairs={{0,6},{1,7},{2,4},{3,5},{4,2},{5,3},{6,0},{7,1},{8,14},{9,15},{10,... | collective-permute-start | bytes 393224 | tf_op jit(solution)/shard_map/ppermute | solution.py:278
  45.8 9.5 %collective-permute-start.19 = (bf16[512,128]{1,0:T(8,128)(2,1)S(1)}, bf16[512,128]{1,0:T(8,128)(2,1)S(1)}, u32[]{:S(2)}, u32[]{:S(2)}) collective-permute-start(bf16[512,128]{1,0:T(8,128)(2,1)S(1)} %get-tuple-element.68), channel_id=1, source_target_pairs={{0,3},{1,2},{2,1},{3,0},{4,7},{5,6},{6,5},{7,4},{8,11},{9,10},{10,... | collective-permute-start | bytes 393224 | tf_op jit(solution)/shard_map/ppermute | solution.py:278
  45.9 9.4 %collective-permute-start.20 = (bf16[512,128]{1,0:T(8,128)(2,1)S(1)}, bf16[512,128]{1,0:T(8,128)(2,1)S(1)}, u32[]{:S(2)}, u32[]{:S(2)}) collective-permute-start(bf16[512,128]{1,0:T(8,128)(2,1)S(1)} %get-tuple-element.69), channel_id=1, source_target_pairs={{0,7},{1,6},{2,5},{3,4},{4,3},{5,2},{6,1},{7,0},{8,15},{9,14},{10,... | collective-permute-start | bytes 393224 | tf_op jit(solution)/shard_map/ppermute | solution.py:278
  47.2 13.9 %collective-permute-start.7 = (bf16[512,128]{1,0:T(8,128)(2,1)S(1)}, bf16[512,128]{1,0:T(8,128)(2,1)S(1)}, u32[]{:S(2)}, u32[]{:S(2)}) collective-permute-start(bf16[512,128]{1,0:T(8,128)(2,1)S(1)} %get-tuple-element.55), channel_id=1, source_target_pairs={{0,1},{1,0},{2,3},{3,2},{4,5},{5,4},{6,7},{7,6},{8,9},{9,8},{10,11... | collective-permute-start | bytes 393224 | tf_op jit(solution)/shard_map/ppermute | solution.py:278
  48.7 18.7 %collective-permute-start.8 = (bf16[512,128]{1,0:T(8,128)(2,1)S(1)}, bf16[512,128]{1,0:T(8,128)(2,1)S(1)}, u32[]{:S(2)}, u32[]{:S(2)}) collective-permute-start(bf16[512,128]{1,0:T(8,128)(2,1)S(1)} %get-tuple-element.56), channel_id=1, source_target_pairs={{0,4},{1,5},{2,6},{3,7},{4,0},{5,1},{6,2},{7,3},{8,12},{9,13},{10,... | collective-permute-start | bytes 393224 | tf_op jit(solution)/shard_map/ppermute | solution.py:278
  50.3 17.1 %collective-permute-start.9 = (bf16[512,128]{1,0:T(8,128)(2,1)S(1)}, bf16[512,128]{1,0:T(8,128)(2,1)S(1)}, u32[]{:S(2)}, u32[]{:S(2)}) collective-permute-start(bf16[512,128]{1,0:T(8,128)(2,1)S(1)} %get-tuple-element.57), channel_id=1, source_target_pairs={{0,2},{1,3},{2,0},{3,1},{4,6},{5,7},{6,4},{7,5},{8,10},{9,11},{10,... | collective-permute-start | bytes 393224 | tf_op jit(solution)/shard_map/ppermute | solution.py:278
  55.3 14.4 %collective-permute-start.10 = (bf16[512,128]{1,0:T(8,128)(2,1)S(1)}, bf16[512,128]{1,0:T(8,128)(2,1)S(1)}, u32[]{:S(2)}, u32[]{:S(2)}) collective-permute-start(bf16[512,128]{1,0:T(8,128)(2,1)S(1)} %get-tuple-element.58), channel_id=1, source_target_pairs={{0,5},{1,4},{2,7},{3,6},{4,1},{5,0},{6,3},{7,2},{8,13},{9,12},{10,... | collective-permute-start | bytes 393224 | tf_op jit(solution)/shard_map/ppermute | solution.py:278
  55.3 17.5 %collective-permute-start.11 = (bf16[512,128]{1,0:T(8,128)(2,1)S(1)}, bf16[512,128]{1,0:T(8,128)(2,1)S(1)}, u32[]{:S(2)}, u32[]{:S(2)}) collective-permute-start(bf16[512,128]{1,0:T(8,128)(2,1)S(1)} %get-tuple-element.59), channel_id=1, source_target_pairs={{0,6},{1,7},{2,4},{3,5},{4,2},{5,3},{6,0},{7,1},{8,14},{9,15},{10,... | collective-permute-start | bytes 393224 | tf_op jit(solution)/shard_map/ppermute | solution.py:278
  61.1 20.2 %collective-permute-start.21 = (bf16[512,256]{1,0:T(8,128)(2,1)S(1)}, bf16[512,256]{1,0:T(8,128)(2,1)S(1)}, u32[]{:S(2)}, u32[]{:S(2)}) collective-permute-start(bf16[512,256]{1,0:T(8,128)(2,1)S(1)} %get-tuple-element.72), channel_id=1, source_target_pairs={{0,16},{8,24},{16,0},{24,8},{1,17},{9,25},{17,1},{25,9},{2,18},{10... | collective-permute-start | bytes 786440 | tf_op jit(solution)/shard_map/ppermute | solution.py:278
  67.5 13.8 %collective-permute-start.22 = (bf16[512,256]{1,0:T(8,128)(2,1)S(1)}, bf16[512,256]{1,0:T(8,128)(2,1)S(1)}, u32[]{:S(2)}, u32[]{:S(2)}) collective-permute-start(bf16[512,256]{1,0:T(8,128)(2,1)S(1)} %get-tuple-element.73), channel_id=1, source_target_pairs={{0,24},{8,16},{16,8},{24,0},{1,25},{9,17},{17,9},{25,1},{2,26},{10... | collective-permute-start | bytes 786440 | tf_op jit(solution)/shard_map/ppermute | solution.py:278
  67.5 13.8 %collective-permute-start.23 = (bf16[512,256]{1,0:T(8,128)(2,1)S(1)}, bf16[512,256]{1,0:T(8,128)(2,1)S(1)}, u32[]{:S(2)}, u32[]{:S(2)}) collective-permute-start(bf16[512,256]{1,0:T(8,128)(2,1)S(1)} %get-tuple-element.74), channel_id=1, source_target_pairs={{0,8},{8,0},{16,24},{24,16},{1,9},{9,1},{17,25},{25,17},{2,10},{10... | collective-permute-start | bytes 786440 | tf_op jit(solution)/shard_map/ppermute | solution.py:278
  69.7 8.4 %collective-permute-start.12 = (bf16[512,128]{1,0:T(8,128)(2,1)S(1)}, bf16[512,128]{1,0:T(8,128)(2,1)S(1)}, u32[]{:S(2)}, u32[]{:S(2)}) collective-permute-start(bf16[512,128]{1,0:T(8,128)(2,1)S(1)} %get-tuple-element.60), channel_id=1, source_target_pairs={{0,7},{1,6},{2,5},{3,4},{4,3},{5,2},{6,1},{7,0},{8,15},{9,14},{10,... | collective-permute-start | bytes 393224 | tf_op jit(solution)/shard_map/ppermute | solution.py:278
  72.8 6.9 %collective-permute-start.13 = (bf16[512,128]{1,0:T(8,128)(2,1)S(1)}, bf16[512,128]{1,0:T(8,128)(2,1)S(1)}, u32[]{:S(2)}, u32[]{:S(2)}) collective-permute-start(bf16[512,128]{1,0:T(8,128)(2,1)S(1)} %get-tuple-element.61), channel_id=1, source_target_pairs={{0,3},{1,2},{2,1},{3,0},{4,7},{5,6},{6,5},{7,4},{8,11},{9,10},{10,... | collective-permute-start | bytes 393224 | tf_op jit(solution)/shard_map/ppermute | solution.py:278

commit v19 on v11

--- a/solution.py
+++ b/solution.py
@@ -144,11 +144,10 @@
     return ref.at[pl.ds(start, rows), :]
 
 
-def gate_kernel(order, input_order, where, gate, upper, whole, *refs):
-    outs, picks, refs = refs[: len(order)], refs[len(order) : 2 * len(order)], refs[2 * len(order) :]
-    left, right, sems, pick_sems = refs
+def gate_kernel(order, where, gate, upper, *refs):
+    outs, (left, right, sems) = refs[: len(order)], refs[len(order) :]
     rows = outs[0].shape[0]
-    loads, moves = [], []
+    loads = []
     for i, k in enumerate(order):
         pair = (
             pltpu.make_async_copy(piece_at(gate, where, k, rows), left.at[i], sems.at[0, i]),
@@ -157,15 +156,10 @@
         for copy in pair:
             copy.start()
         loads.append(pair)
-    for i, k in enumerate(input_order):
-        moves.append(pltpu.make_async_copy(piece_at(whole, where, k, rows), picks[i], pick_sems.at[i]))
-        moves[-1].start()
     for i, out in enumerate(outs):
         for copy in loads[i]:
             copy.wait()
         out[...] = (left[i].astype(jnp.float32) * right[i].astype(jnp.float32)).astype(jnp.bfloat16)
-    for copy in moves:
-        copy.wait()
 
 
 def place_kernel(order, where, *refs):
@@ -174,11 +168,18 @@
         whole[lax.bitwise_xor(where[0], k)] = piece[...]
 
 
-def taps_kernel(taps, forward, taps_spec, mid):
+def taps_kernel(order, where, whole, taps, forward, *refs):
+    picks, (taps_spec, mid, sems) = refs[: len(order)], refs[len(order) :]
     rows, width = (taps.shape[0], taps.shape[1] // BLOCKS)
+    moves = []
+    for i, k in enumerate(order):
+        moves.append(pltpu.make_async_copy(piece_at(whole, where, k, rows), picks[i], sems.at[i]))
+        moves[-1].start()
     split_rows(lambda p, at: taps[at, p * width : (p + 1) * width], mid, rows, width)
     for r in range(GROUPS):
         taps_spec[r] = spectrum(mid, forward, r, width).astype(taps_spec.dtype)
+    for copy in moves:
+        copy.wait()
 
 
 def ordered(order, where, refs, held):
@@ -283,7 +284,7 @@
     channels, span = saved_input.shape[1:]
     rows, length = long_filter.shape
     width = length // BLOCKS
-    grad_order, input_order, back_order = (spread(count, o) for o in ((1, 2, 4, 5, 6, 7, 3), (4, 5, 1, 6, 2, 7, 3), (1, 2, 3, 4, 5, 6, 7)))
+    grad_order, input_order, back_order = (spread(count, o) for o in ((4, 1, 5, 2, 6, 7, 3), (4, 5, 6, 1, 2, 7, 3), (1, 4, 2, 5, 6, 7, 3)))
     late = 2
     at = count - 1 - late
     every = range(count + 8)
@@ -299,16 +300,23 @@
     sems = pltpu.SemaphoreType.DMA
     work = 2 * GROUPS * rows * 4 * width * width
 
-    pieces = call(
-        functools.partial(gate_kernel, grad_order, input_order),
-        [where, *(pltpu.with_memory_space_constraint(x[0], pltpu.HBM) for x in (out_gate, grad_out, saved_input))],
-        [piece] * (2 * count),
-        [slots, slots, sems((2, count)), sems((count,))],
-        hbm=(1, 2, 3),
-    )
-    grad_pieces, input_pieces = pieces[:count], pieces[count:]
+    stay = [pltpu.with_memory_space_constraint(x[0], pltpu.HBM) for x in (out_gate, grad_out, saved_input)]
+    grad_pieces = call(
+        functools.partial(gate_kernel, grad_order),
+        [where, *stay[:2]],
+        [piece] * count,
+        [slots, slots, sems((2, count))],
+        hbm=(1, 2),
+    )
     grad_blocks = exchange(grad_pieces, grad_order, "ctx", count)
-    (taps_spec,) = call(taps_kernel, [long_filter, forward], [spec], [mid], flops=work)
+    *input_pieces, taps_spec = call(
+        functools.partial(taps_kernel, input_order),
+        [where, stay[2], long_filter, forward],
+        [piece] * count + [spec],
+        [mid, sems((count,))],
+        flops=work,
+        hbm=(1,),
+    )
     passed = [*input_pieces[at : at + late]]
     *back, grad_spec = call(
         functools.partial(back_kernel, grad_order, back_order, late),

time: 84.2 us -> 82.1 us (0.975)
  the two profiles are of different devices: /device:TPU:9 before, /device:TPU:0 now
where the time goes in v19:
time: 82.1 us; the launch traced here: 81.9 us
  starting transfers between devices  49.2 us (60%)
  waiting for transfers between devices  15.1 us (18%)
  Pallas kernels  14.4 us (18%)
  local copies, waits for them, and re-layouts  1.6 us (2%)
  other arithmetic  1.01 us (1%)
    ppermute x24, starting transfers between devices, exchange(): lax.ppermute(piece, axis, [(i, i ^ k) for i in range(size)])  49.2 us
    ppermute x24, waiting for transfers between devices, exchange(): lax.ppermute(piece, axis, [(i, i ^ k) for i in range(size)])  15.1 us
    pallas_call x5, Pallas kernels, call(): pl.pallas_call(kernel, out_shape=list(outs), in_specs=specs, out_specs=[s...  14.4 us
  transfers between devices with their start and end apart: 24, of which 6 were waited for; matrix products, arithmetic and copies ran while one was open for 0% of the time, Pallas kernels for 15%

profile of v19, /device:TPU:0, one launch (start us, length us, event | category | flops | bytes accessed | tf_op | source)
XLA Modules:
  0.0 81.9 jit_solution(2775233583857129539)
XLA Ops:
  0.6 0.0 copy-start
  0.6 0.1 pad_add_fusion.where
  0.7 2.3 %shard_map.77 = (bf16[512,128]{1,0:T(8,128)(2,1)S(1)}, bf16[512,128]{1,0:T(8,128)(2,1)S(1)}, bf16[512,128]{1,0:T(8,128)(2,1)S(1)}, bf16[512,128]{1,0:T(8,128)(2,...) custom-call(s32[2]{0:T(128)S(1)} %pad_add_fusion.where, ...), custom_call_target="tpu_custom_call" | custom-call | bytes 3145736 | tf_op jit(solution)/shard_map/pallas_call | solution.py:253
  3.0 4.1 %collective-permute-start = (bf16[512,128]{1,0:T(8,128)(2,1)S(1)}, bf16[512,128]{1,0:T(8,128)(2,1)S(1)}, u32[]{:S(2)}, u32[]{:S(2)}) collective-permute-start(bf16[512,128]{1,0:T(8,128)(2,1)S(1)} %get-tuple-element.34), channel_id=1, source_target_pairs={{0,4},{1,5},{2,6},{3,7},{4,0},{5,1},{6,2},{7,3},{8,12},{9,13},{10,... | collective-permute-start | bytes 393224 | tf_op jit(solution)/shard_map/ppermute | solution.py:278
  7.1 1.5 %collective-permute-start.1 = (bf16[512,128]{1,0:T(8,128)(2,1)S(1)}, bf16[512,128]{1,0:T(8,128)(2,1)S(1)}, u32[]{:S(2)}, u32[]{:S(2)}) collective-permute-start(bf16[512,128]{1,0:T(8,128)(2,1)S(1)} %get-tuple-element.35), channel_id=1, source_target_pairs={{0,1},{1,0},{2,3},{3,2},{4,5},{5,4},{6,7},{7,6},{8,9},{9,8},{10,11... | collective-permute-start | bytes 393224 | tf_op jit(solution)/shard_map/ppermute | solution.py:278
  8.7 0.0 collective-permute-start.2
  8.7 1.8 %collective-permute-start.3 = (bf16[512,128]{1,0:T(8,128)(2,1)S(1)}, bf16[512,128]{1,0:T(8,128)(2,1)S(1)}, u32[]{:S(2)}, u32[]{:S(2)}) collective-permute-start(bf16[512,128]{1,0:T(8,128)(2,1)S(1)} %get-tuple-element.37), channel_id=1, source_target_pairs={{0,2},{1,3},{2,0},{3,1},{4,6},{5,7},{6,4},{7,5},{8,10},{9,11},{10,... | collective-permute-start | bytes 393224 | tf_op jit(solution)/shard_map/ppermute | solution.py:278
  10.5 2.5 %collective-permute-start.4 = (bf16[512,128]{1,0:T(8,128)(2,1)S(1)}, bf16[512,128]{1,0:T(8,128)(2,1)S(1)}, u32[]{:S(2)}, u32[]{:S(2)}) collective-permute-start(bf16[512,128]{1,0:T(8,128)(2,1)S(1)} %get-tuple-element.38), channel_id=1, source_target_pairs={{0,6},{1,7},{2,4},{3,5},{4,2},{5,3},{6,0},{7,1},{8,14},{9,15},{10,... | collective-permute-start | bytes 393224 | tf_op jit(solution)/shard_map/ppermute | solution.py:278
  13.0 4.8 %collective-permute-done.refs_0_ = bf16[512,128]{1,0:T(8,128)(2,1)S(1)} collective-permute-done((bf16[512,128]{1,0:T(8,128)(2,1)S(1)}, bf16[512,128]{1,0:T(8,128)(2,1)S(1)}, u32[]{:S(2)}, u32[]{:S(2)}) %collective-permute-start) | collective-permute-done | bytes 131104 | tf_op jit(solution)/shard_map/ppermute | solution.py:278
  17.8 5.9 %collective-permute-start.5 = (bf16[512,128]{1,0:T(8,128)(2,1)S(1)}, bf16[512,128]{1,0:T(8,128)(2,1)S(1)}, u32[]{:S(2)}, u32[]{:S(2)}) collective-permute-start(bf16[512,128]{1,0:T(8,128)(2,1)S(1)} %get-tuple-element.39), channel_id=1, source_target_pairs={{0,7},{1,6},{2,5},{3,4},{4,3},{5,2},{6,1},{7,0},{8,15},{9,14},{10,... | collective-permute-start | bytes 393224 | tf_op jit(solution)/shard_map/ppermute | solution.py:278
  23.8 0.0 collective-permute-done.1.refs_1_
  23.8 0.0 collective-permute-start.6
  23.8 0.0 copy-done
  23.8 0.0 copy-start.2
  23.8 1.6 %copy-done.2 = f32[512,1024]{1,0:T(8,128)S(1)} copy-done((f32[512,1024]{1,0:T(8,128)S(1)}, f32[512,1024]{1,0:T(8,128)}, u32[]{:S(2)}) %copy-start.2) | copy-done | bytes 2097176
  25.4 0.0 copy-start.1
  25.4 2.1 %shard_map.78 = (bf16[512,128]{1,0:T(8,128)(2,1)S(1)}, bf16[512,128]{1,0:T(8,128)(2,1)S(1)}, bf16[512,128]{1,0:T(8,128)(2,1)S(1)}, bf16[512,128]{1,0:T(8,128)(2,...) custom-call(s32[2]{0:T(128)S(1)} %pad_add_fusion.where, ...), custom_call_target="tpu_custom_call" | custom-call | flops 603979776 | bytes 7733256 | tf_op jit(solution)/shard_map/pallas_call | solution.py:253
  27.5 0.0 collective-permute-done.2.refs_2_
  27.5 0.6 collective-permute-start.14
  28.1 0.0 collective-permute-done.3.refs_3_
  28.1 2.3 %collective-permute-start.15 = (bf16[512,128]{1,0:T(8,128)(2,1)S(1)}, bf16[512,128]{1,0:T(8,128)(2,1)S(1)}, u32[]{:S(2)}, u32[]{:S(2)}) collective-permute-start(bf16[512,128]{1,0:T(8,128)(2,1)S(1)} %get-tuple-element.54), channel_id=1, source_target_pairs={{0,5},{1,4},{2,7},{3,6},{4,1},{5,0},{6,3},{7,2},{8,13},{9,12},{10,... | collective-permute-start | bytes 393224 | tf_op jit(solution)/shard_map/ppermute | solution.py:278
  30.4 0.0 collective-permute-done.4.refs_4_
  30.4 2.5 %collective-permute-start.16 = (bf16[512,128]{1,0:T(8,128)(2,1)S(1)}, bf16[512,128]{1,0:T(8,128)(2,1)S(1)}, u32[]{:S(2)}, u32[]{:S(2)}) collective-permute-start(bf16[512,128]{1,0:T(8,128)(2,1)S(1)} %get-tuple-element.55), channel_id=1, source_target_pairs={{0,6},{1,7},{2,4},{3,5},{4,2},{5,3},{6,0},{7,1},{8,14},{9,15},{10,... | collective-permute-start | bytes 393224 | tf_op jit(solution)/shard_map/ppermute | solution.py:278
  32.9 0.0 collective-permute-done.5.refs_5_
  32.9 0.5 collective-permute-start.17
  33.5 0.0 collective-permute-done.6.refs_6_
  33.5 8.1 %collective-permute-start.18 = (bf16[512,128]{1,0:T(8,128)(2,1)S(1)}, bf16[512,128]{1,0:T(8,128)(2,1)S(1)}, u32[]{:S(2)}, u32[]{:S(2)}) collective-permute-start(bf16[512,128]{1,0:T(8,128)(2,1)S(1)} %get-tuple-element.57), channel_id=1, source_target_pairs={{0,2},{1,3},{2,0},{3,1},{4,6},{5,7},{6,4},{7,5},{8,10},{9,11},{10,... | collective-permute-start | bytes 393224 | tf_op jit(solution)/shard_map/ppermute | solution.py:278
  41.6 0.0 copy-done.1
  41.6 4.2 %shard_map.79 = (bf16[512,128]{1,0:T(8,128)(2,1)S(1)}, bf16[512,128]{1,0:T(8,128)(2,1)S(1)}, bf16[512,128]{1,0:T(8,128)(2,1)S(1)}, bf16[512,128]{1,0:T(8,128)(2,...) custom-call(s32[2]{0:T(128)S(1)} %pad_add_fusion.where, ...), custom_call_target="tpu_custom_call", output_to_operand_aliasing={{0}: (9, {}), {1}: (10, {})} | custom-call | flops 1207959552 | bytes 9699336 | tf_op jit(solution)/shard_map/pallas_call | solution.py:253
  45.8 0.0 collective-permute-done.14.refs_0_
  45.8 3.9 %collective-permute-start.19 = (bf16[512,128]{1,0:T(8,128)(2,1)S(1)}, bf16[512,128]{1,0:T(8,128)(2,1)S(1)}, u32[]{:S(2)}, u32[]{:S(2)}) collective-permute-start(bf16[512,128]{1,0:T(8,128)(2,1)S(1)} %get-tuple-element.58), channel_id=1, source_target_pairs={{0,7},{1,6},{2,5},{3,4},{4,3},{5,2},{6,1},{7,0},{8,15},{9,14},{10,... | collective-permute-start | bytes 393224 | tf_op jit(solution)/shard_map/ppermute | solution.py:278
  49.7 0.0 collective-permute-done.15.refs_1_
  49.7 0.0 collective-permute-start.20
  49.7 0.0 collective-permute-done.16.refs_2_
  49.7 0.6 collective-permute-start.7
  50.3 0.0 collective-permute-done.17.refs_3_
  50.3 2.8 %collective-permute-start.8 = (bf16[512,128]{1,0:T(8,128)(2,1)S(1)}, bf16[512,128]{1,0:T(8,128)(2,1)S(1)}, u32[]{:S(2)}, u32[]{:S(2)}) collective-permute-start(bf16[512,128]{1,0:T(8,128)(2,1)S(1)} %get-tuple-element.46), channel_id=1, source_target_pairs={{0,4},{1,5},{2,6},{3,7},{4,0},{5,1},{6,2},{7,3},{8,12},{9,13},{10,... | collective-permute-start | bytes 393224 | tf_op jit(solution)/shard_map/ppermute | solution.py:278
  53.1 0.0 collective-permute-done.18.refs_4_
  53.1 0.2 collective-permute-start.9
  53.3 1.2 %collective-permute-done.19.refs_5_ = bf16[512,128]{1,0:T(8,128)(2,1)S(1)} collective-permute-done((bf16[512,128]{1,0:T(8,128)(2,1)S(1)}, bf16[512,128]{1,0:T(8,128)(2,1)S(1)}, u32[]{:S(2)}, u32[]{:S(2)}) %collective-permute-start.19) | collective-permute-done | bytes 131104 | tf_op jit(solution)/shard_map/ppermute | solution.py:278
  54.5 4.0 %collective-permute-start.10 = (bf16[512,128]{1,0:T(8,128)(2,1)S(1)}, bf16[512,128]{1,0:T(8,128)(2,1)S(1)}, u32[]{:S(2)}, u32[]{:S(2)}) collective-permute-start(bf16[512,128]{1,0:T(8,128)(2,1)S(1)} %get-tuple-element.48), channel_id=1, source_target_pairs={{0,5},{1,4},{2,7},{3,6},{4,1},{5,0},{6,3},{7,2},{8,13},{9,12},{10,... | collective-permute-start | bytes 393224 | tf_op jit(solution)/shard_map/ppermute | solution.py:278
  58.6 1.6 %collective-permute-done.20.refs_6_ = bf16[512,128]{1,0:T(8,128)(2,1)S(1)} collective-permute-done((bf16[512,128]{1,0:T(8,128)(2,1)S(1)}, bf16[512,128]{1,0:T(8,128)(2,1)S(1)}, u32[]{:S(2)}, u32[]{:S(2)}) %collective-permute-start.20) | collective-permute-done | bytes 131104 | tf_op jit(solution)/shard_map/ppermute | solution.py:278
  60.1 1.8 %collective-permute-start.11 = (bf16[512,128]{1,0:T(8,128)(2,1)S(1)}, bf16[512,128]{1,0:T(8,128)(2,1)S(1)}, u32[]{:S(2)}, u32[]{:S(2)}) collective-permute-start(bf16[512,128]{1,0:T(8,128)(2,1)S(1)} %get-tuple-element.49), channel_id=1, source_target_pairs={{0,6},{1,7},{2,4},{3,5},{4,2},{5,3},{6,0},{7,1},{8,14},{9,15},{10,... | collective-permute-start | bytes 393224 | tf_op jit(solution)/shard_map/ppermute | solution.py:278
  62.0 4.1 %shard_map.81 = (bf16[512,256]{1,0:T(8,128)(2,1)S(1)}, bf16[512,256]{1,0:T(8,128)(2,1)S(1)}, bf16[512,256]{1,0:T(8,128)(2,1)S(1)}, bf16[512,256]{1,0:T(8,128)(2,1)S(1)}) custom-call(s32[2]{0:T(128)S(1)} %pad_add_fusion.where, bf16[512,128]{1,0:T(8,128)(2,1)S(1)} %collective-permute-done.14.refs_0_, bf16[512,128]{1,0:T(8,128)(2,1)S(1)} %collective-permute-done.15.refs_1_, ...), custom_call_target="tpu_custom_call" | custom-call | flops 1207959552 | bytes 6815752 | tf_op jit(solution)/shard_map/pallas_call | solution.py:253
  66.1 0.0 collective-permute-done.7.refs_0_
  66.1 1.6 %collective-permute-start.21 = (bf16[512,256]{1,0:T(8,128)(2,1)S(1)}, bf16[512,256]{1,0:T(8,128)(2,1)S(1)}, u32[]{:S(2)}, u32[]{:S(2)}) collective-permute-start(bf16[512,256]{1,0:T(8,128)(2,1)S(1)} %get-tuple-element.62), channel_id=1, source_target_pairs={{0,16},{8,24},{16,0},{24,8},{1,17},{9,25},{17,1},{25,9},{2,18},{10... | collective-permute-start | bytes 786440 | tf_op jit(solution)/shard_map/ppermute | solution.py:278
  67.7 0.0 collective-permute-done.8.refs_1_
  67.7 0.0 collective-permute-start.22
  67.7 0.0 collective-permute-done.9.refs_2_
  67.7 0.6 collective-permute-start.23
  68.3 1.0 %collective-permute-done.10.refs_3_ = bf16[512,128]{1,0:T(8,128)(2,1)S(1)} collective-permute-done((bf16[512,128]{1,0:T(8,128)(2,1)S(1)}, bf16[512,128]{1,0:T(8,128)(2,1)S(1)}, u32[]{:S(2)}, u32[]{:S(2)}) %collective-permute-start.10) | collective-permute-done | bytes 131104 | tf_op jit(solution)/shard_map/ppermute | solution.py:278
  69.3 3.7 %collective-permute-start.12 = (bf16[512,128]{1,0:T(8,128)(2,1)S(1)}, bf16[512,128]{1,0:T(8,128)(2,1)S(1)}, u32[]{:S(2)}, u32[]{:S(2)}) collective-permute-start(bf16[512,128]{1,0:T(8,128)(2,1)S(1)} %get-tuple-element.50), channel_id=1, source_target_pairs={{0,7},{1,6},{2,5},{3,4},{4,3},{5,2},{6,1},{7,0},{8,15},{9,14},{10,... | collective-permute-start | bytes 393224 | tf_op jit(solution)/shard_map/ppermute | solution.py:278
  73.0 0.0 collective-permute-done.11.refs_4_
  73.0 0.0 collective-permute-start.13
  73.0 5.3 %collective-permute-done.12.refs_5_ = bf16[512,128]{1,0:T(8,128)(2,1)S(1)} collective-permute-done((bf16[512,128]{1,0:T(8,128)(2,1)S(1)}, bf16[512,128]{1,0:T(8,128)(2,1)S(1)}, u32[]{:S(2)}, u32[]{:S(2)}) %collective-permute-start.12) | collective-permute-done | bytes 131104 | tf_op jit(solution)/shard_map/ppermute | solution.py:278
  78.2 1.2 %collective-permute-done.13.refs_6_ = bf16[512,128]{1,0:T(8,128)(2,1)S(1)} collective-permute-done((bf16[512,128]{1,0:T(8,128)(2,1)S(1)}, bf16[512,128]{1,0:T(8,128)(2,1)S(1)}, u32[]{:S(2)}, u32[]{:S(2)}) %collective-permute-start.13) | collective-permute-done | bytes 131104 | tf_op jit(solution)/shard_map/ppermute | solution.py:278
  79.4 1.6 %shard_map.80 = bf16[8,512,128]{2,1,0:T(8,128)(2,1)} custom-call(s32[2]{0:T(128)S(1)} %pad_add_fusion.where, bf16[512,128]{1,0:T(8,128)(2,1)S(1)} %collective-permute-done.7.refs_0_, bf16[512,128]{1,0:T(8,128)(2,1)S(1)} %collective-permute-done.8.refs_1_, bf16[512,128]{1,0:T(8,128)(2,1)S(1)} %collective-permute-done.9.refs_2_, ...), custom_call_target="tpu_custom_call" | custom-call | bytes 2097160 | tf_op jit(solution)/shard_map/pallas_call | solution.py:253
  81.0 0.0 collective-permute-done.21
  81.0 0.0 collective-permute-done.22
  81.0 0.0 collective-permute-done.23
  81.0 0.9 %add_multiply_fusion = f32[512,256]{1,0:T(8,128)} fusion(bf16[512,256]{1,0:T(8,128)(2,1)S(1)} %get-tuple-element.65, bf16[512,256]{1,0:T(8,128)(2,1)S(1)} %collective-permute-done.23, bf16[512,256]{1,0:T(8,128)(2,1)S(1)} %collective-permute-done.22, bf16[512,256]{1,0:T(8,128)(2,1)S(1)} %collective-permute-done.21), kind=kLoop, calls=%fused_computation | loop fusion | flops 1048576 | bytes 1572864 | tf_op jit(solution)/shard_map/mul | solution.py:344
Async XLA Ops:
  0.6 23.1 %copy-start = (bf16[9,256,256]{2,1,0:T(8,128)(2,1)S(1)}, bf16[9,256,256]{2,1,0:T(8,128)(2,1)}, u32[]{:S(2)}) copy-start(bf16[9,256,256]{2,1,0:T(8,128)(2,1)} %constant.14.clone.forward.refs_11_.refs_9_) | copy-start | bytes 3538948
  3.0 14.8 %collective-permute-start = (bf16[512,128]{1,0:T(8,128)(2,1)S(1)}, bf16[512,128]{1,0:T(8,128)(2,1)S(1)}, u32[]{:S(2)}, u32[]{:S(2)}) collective-permute-start(bf16[512,128]{1,0:T(8,128)(2,1)S(1)} %get-tuple-element.34), channel_id=1, source_target_pairs={{0,4},{1,5},{2,6},{3,7},{4,0},{5,1},{6,2},{7,3},{8,12},{9,13},{10,... | collective-permute-start | bytes 393224 | tf_op jit(solution)/shard_map/ppermute | solution.py:278
  7.1 16.6 %collective-permute-start.1 = (bf16[512,128]{1,0:T(8,128)(2,1)S(1)}, bf16[512,128]{1,0:T(8,128)(2,1)S(1)}, u32[]{:S(2)}, u32[]{:S(2)}) collective-permute-start(bf16[512,128]{1,0:T(8,128)(2,1)S(1)} %get-tuple-element.35), channel_id=1, source_target_pairs={{0,1},{1,0},{2,3},{3,2},{4,5},{5,4},{6,7},{7,6},{8,9},{9,8},{10,11... | collective-permute-start | bytes 393224 | tf_op jit(solution)/shard_map/ppermute | solution.py:278
  8.7 18.8 %collective-permute-start.2 = (bf16[512,128]{1,0:T(8,128)(2,1)S(1)}, bf16[512,128]{1,0:T(8,128)(2,1)S(1)}, u32[]{:S(2)}, u32[]{:S(2)}) collective-permute-start(bf16[512,128]{1,0:T(8,128)(2,1)S(1)} %get-tuple-element.36), channel_id=1, source_target_pairs={{0,5},{1,4},{2,7},{3,6},{4,1},{5,0},{6,3},{7,2},{8,13},{9,12},{10,... | collective-permute-start | bytes 393224 | tf_op jit(solution)/shard_map/ppermute | solution.py:278
  8.7 19.4 %collective-permute-start.3 = (bf16[512,128]{1,0:T(8,128)(2,1)S(1)}, bf16[512,128]{1,0:T(8,128)(2,1)S(1)}, u32[]{:S(2)}, u32[]{:S(2)}) collective-permute-start(bf16[512,128]{1,0:T(8,128)(2,1)S(1)} %get-tuple-element.37), channel_id=1, source_target_pairs={{0,2},{1,3},{2,0},{3,1},{4,6},{5,7},{6,4},{7,5},{8,10},{9,11},{10,... | collective-permute-start | bytes 393224 | tf_op jit(solution)/shard_map/ppermute | solution.py:278
  10.5 19.9 %collective-permute-start.4 = (bf16[512,128]{1,0:T(8,128)(2,1)S(1)}, bf16[512,128]{1,0:T(8,128)(2,1)S(1)}, u32[]{:S(2)}, u32[]{:S(2)}) collective-permute-start(bf16[512,128]{1,0:T(8,128)(2,1)S(1)} %get-tuple-element.38), channel_id=1, source_target_pairs={{0,6},{1,7},{2,4},{3,5},{4,2},{5,3},{6,0},{7,1},{8,14},{9,15},{10,... | collective-permute-start | bytes 393224 | tf_op jit(solution)/shard_map/ppermute | solution.py:278
  17.8 15.1 %collective-permute-start.5 = (bf16[512,128]{1,0:T(8,128)(2,1)S(1)}, bf16[512,128]{1,0:T(8,128)(2,1)S(1)}, u32[]{:S(2)}, u32[]{:S(2)}) collective-permute-start(bf16[512,128]{1,0:T(8,128)(2,1)S(1)} %get-tuple-element.39), channel_id=1, source_target_pairs={{0,7},{1,6},{2,5},{3,4},{4,3},{5,2},{6,1},{7,0},{8,15},{9,14},{10,... | collective-permute-start | bytes 393224 | tf_op jit(solution)/shard_map/ppermute | solution.py:278
  23.8 9.7 %collective-permute-start.6 = (bf16[512,128]{1,0:T(8,128)(2,1)S(1)}, bf16[512,128]{1,0:T(8,128)(2,1)S(1)}, u32[]{:S(2)}, u32[]{:S(2)}) collective-permute-start(bf16[512,128]{1,0:T(8,128)(2,1)S(1)} %get-tuple-element.40), channel_id=1, source_target_pairs={{0,3},{1,2},{2,1},{3,0},{4,7},{5,6},{6,5},{7,4},{8,11},{9,10},{10,... | collective-permute-start | bytes 393224 | tf_op jit(solution)/shard_map/ppermute | solution.py:278
  23.8 1.6 %copy-start.2 = (f32[512,1024]{1,0:T(8,128)S(1)}, f32[512,1024]{1,0:T(8,128)}, u32[]{:S(2)}) copy-start(f32[512,1024]{1,0:T(8,128)} %taps.1) | copy-start | bytes 6291460
  25.4 16.2 %copy-start.1 = (bf16[9,256,256]{2,1,0:T(8,128)(2,1)S(1)}, bf16[9,256,256]{2,1,0:T(8,128)(2,1)}, u32[]{:S(2)}) copy-start(bf16[9,256,256]{2,1,0:T(8,128)(2,1)} %constant.15.clone.refs_12_.refs_10_) | copy-start | bytes 3538948
  27.5 18.3 %collective-permute-start.14 = (bf16[512,128]{1,0:T(8,128)(2,1)S(1)}, bf16[512,128]{1,0:T(8,128)(2,1)S(1)}, u32[]{:S(2)}, u32[]{:S(2)}) collective-permute-start(bf16[512,128]{1,0:T(8,128)(2,1)S(1)} %get-tuple-element.53), channel_id=1, source_target_pairs={{0,4},{1,5},{2,6},{3,7},{4,0},{5,1},{6,2},{7,3},{8,12},{9,13},{10,... | collective-permute-start | bytes 393224 | tf_op jit(solution)/shard_map/ppermute | solution.py:278
  28.1 21.6 %collective-permute-start.15 = (bf16[512,128]{1,0:T(8,128)(2,1)S(1)}, bf16[512,128]{1,0:T(8,128)(2,1)S(1)}, u32[]{:S(2)}, u32[]{:S(2)}) collective-permute-start(bf16[512,128]{1,0:T(8,128)(2,1)S(1)} %get-tuple-element.54), channel_id=1, source_target_pairs={{0,5},{1,4},{2,7},{3,6},{4,1},{5,0},{6,3},{7,2},{8,13},{9,12},{10,... | collective-permute-start | bytes 393224 | tf_op jit(solution)/shard_map/ppermute | solution.py:278
  30.4 19.3 %collective-permute-start.16 = (bf16[512,128]{1,0:T(8,128)(2,1)S(1)}, bf16[512,128]{1,0:T(8,128)(2,1)S(1)}, u32[]{:S(2)}, u32[]{:S(2)}) collective-permute-start(bf16[512,128]{1,0:T(8,128)(2,1)S(1)} %get-tuple-element.55), channel_id=1, source_target_pairs={{0,6},{1,7},{2,4},{3,5},{4,2},{5,3},{6,0},{7,1},{8,14},{9,15},{10,... | collective-permute-start | bytes 393224 | tf_op jit(solution)/shard_map/ppermute | solution.py:278
  32.9 17.4 %collective-permute-start.17 = (bf16[512,128]{1,0:T(8,128)(2,1)S(1)}, bf16[512,128]{1,0:T(8,128)(2,1)S(1)}, u32[]{:S(2)}, u32[]{:S(2)}) collective-permute-start(bf16[512,128]{1,0:T(8,128)(2,1)S(1)} %get-tuple-element.56), channel_id=1, source_target_pairs={{0,1},{1,0},{2,3},{3,2},{4,5},{5,4},{6,7},{7,6},{8,9},{9,8},{10,11... | collective-permute-start | bytes 393224 | tf_op jit(solution)/shard_map/ppermute | solution.py:278
  33.5 19.6 %collective-permute-start.18 = (bf16[512,128]{1,0:T(8,128)(2,1)S(1)}, bf16[512,128]{1,0:T(8,128)(2,1)S(1)}, u32[]{:S(2)}, u32[]{:S(2)}) collective-permute-start(bf16[512,128]{1,0:T(8,128)(2,1)S(1)} %get-tuple-element.57), channel_id=1, source_target_pairs={{0,2},{1,3},{2,0},{3,1},{4,6},{5,7},{6,4},{7,5},{8,10},{9,11},{10,... | collective-permute-start | bytes 393224 | tf_op jit(solution)/shard_map/ppermute | solution.py:278
  45.8 8.7 %collective-permute-start.19 = (bf16[512,128]{1,0:T(8,128)(2,1)S(1)}, bf16[512,128]{1,0:T(8,128)(2,1)S(1)}, u32[]{:S(2)}, u32[]{:S(2)}) collective-permute-start(bf16[512,128]{1,0:T(8,128)(2,1)S(1)} %get-tuple-element.58), channel_id=1, source_target_pairs={{0,7},{1,6},{2,5},{3,4},{4,3},{5,2},{6,1},{7,0},{8,15},{9,14},{10,... | collective-permute-start | bytes 393224 | tf_op jit(solution)/shard_map/ppermute | solution.py:278
  49.7 10.4 %collective-permute-start.20 = (bf16[512,128]{1,0:T(8,128)(2,1)S(1)}, bf16[512,128]{1,0:T(8,128)(2,1)S(1)}, u32[]{:S(2)}, u32[]{:S(2)}) collective-permute-start(bf16[512,128]{1,0:T(8,128)(2,1)S(1)} %get-tuple-element.59), channel_id=1, source_target_pairs={{0,3},{1,2},{2,1},{3,0},{4,7},{5,6},{6,5},{7,4},{8,11},{9,10},{10,... | collective-permute-start | bytes 393224 | tf_op jit(solution)/shard_map/ppermute | solution.py:278
  49.7 16.4 %collective-permute-start.7 = (bf16[512,128]{1,0:T(8,128)(2,1)S(1)}, bf16[512,128]{1,0:T(8,128)(2,1)S(1)}, u32[]{:S(2)}, u32[]{:S(2)}) collective-permute-start(bf16[512,128]{1,0:T(8,128)(2,1)S(1)} %get-tuple-element.45), channel_id=1, source_target_pairs={{0,1},{1,0},{2,3},{3,2},{4,5},{5,4},{6,7},{7,6},{8,9},{9,8},{10,11... | collective-permute-start | bytes 393224 | tf_op jit(solution)/shard_map/ppermute | solution.py:278
  50.3 17.4 %collective-permute-start.8 = (bf16[512,128]{1,0:T(8,128)(2,1)S(1)}, bf16[512,128]{1,0:T(8,128)(2,1)S(1)}, u32[]{:S(2)}, u32[]{:S(2)}) collective-permute-start(bf16[512,128]{1,0:T(8,128)(2,1)S(1)} %get-tuple-element.46), channel_id=1, source_target_pairs={{0,4},{1,5},{2,6},{3,7},{4,0},{5,1},{6,2},{7,3},{8,12},{9,13},{10,... | collective-permute-start | bytes 393224 | tf_op jit(solution)/shard_map/ppermute | solution.py:278
  53.1 14.6 %collective-permute-start.9 = (bf16[512,128]{1,0:T(8,128)(2,1)S(1)}, bf16[512,128]{1,0:T(8,128)(2,1)S(1)}, u32[]{:S(2)}, u32[]{:S(2)}) collective-permute-start(bf16[512,128]{1,0:T(8,128)(2,1)S(1)} %get-tuple-element.47), channel_id=1, source_target_pairs={{0,2},{1,3},{2,0},{3,1},{4,6},{5,7},{6,4},{7,5},{8,10},{9,11},{10,... | collective-permute-start | bytes 393224 | tf_op jit(solution)/shard_map/ppermute | solution.py:278
  54.5 14.8 %collective-permute-start.10 = (bf16[512,128]{1,0:T(8,128)(2,1)S(1)}, bf16[512,128]{1,0:T(8,128)(2,1)S(1)}, u32[]{:S(2)}, u32[]{:S(2)}) collective-permute-start(bf16[512,128]{1,0:T(8,128)(2,1)S(1)} %get-tuple-element.48), channel_id=1, source_target_pairs={{0,5},{1,4},{2,7},{3,6},{4,1},{5,0},{6,3},{7,2},{8,13},{9,12},{10,... | collective-permute-start | bytes 393224 | tf_op jit(solution)/shard_map/ppermute | solution.py:278
  60.1 12.9 %collective-permute-start.11 = (bf16[512,128]{1,0:T(8,128)(2,1)S(1)}, bf16[512,128]{1,0:T(8,128)(2,1)S(1)}, u32[]{:S(2)}, u32[]{:S(2)}) collective-permute-start(bf16[512,128]{1,0:T(8,128)(2,1)S(1)} %get-tuple-element.49), channel_id=1, source_target_pairs={{0,6},{1,7},{2,4},{3,5},{4,2},{5,3},{6,0},{7,1},{8,14},{9,15},{10,... | collective-permute-start | bytes 393224 | tf_op jit(solution)/shard_map/ppermute | solution.py:278
  66.1 14.9 %collective-permute-start.21 = (bf16[512,256]{1,0:T(8,128)(2,1)S(1)}, bf16[512,256]{1,0:T(8,128)(2,1)S(1)}, u32[]{:S(2)}, u32[]{:S(2)}) collective-permute-start(bf16[512,256]{1,0:T(8,128)(2,1)S(1)} %get-tuple-element.62), channel_id=1, source_target_pairs={{0,16},{8,24},{16,0},{24,8},{1,17},{9,25},{17,1},{25,9},{2,18},{10... | collective-permute-start | bytes 786440 | tf_op jit(solution)/shard_map/ppermute | solution.py:278
  67.7 13.3 %collective-permute-start.22 = (bf16[512,256]{1,0:T(8,128)(2,1)S(1)}, bf16[512,256]{1,0:T(8,128)(2,1)S(1)}, u32[]{:S(2)}, u32[]{:S(2)}) collective-permute-start(bf16[512,256]{1,0:T(8,128)(2,1)S(1)} %get-tuple-element.63), channel_id=1, source_target_pairs={{0,24},{8,16},{16,8},{24,0},{1,25},{9,17},{17,9},{25,1},{2,26},{10... | collective-permute-start | bytes 786440 | tf_op jit(solution)/shard_map/ppermute | solution.py:278
  67.7 13.3 %collective-permute-start.23 = (bf16[512,256]{1,0:T(8,128)(2,1)S(1)}, bf16[512,256]{1,0:T(8,128)(2,1)S(1)}, u32[]{:S(2)}, u32[]{:S(2)}) collective-permute-start(bf16[512,256]{1,0:T(8,128)(2,1)S(1)} %get-tuple-element.64), channel_id=1, source_target_pairs={{0,8},{8,0},{16,24},{24,16},{1,9},{9,1},{17,25},{25,17},{2,10},{10... | collective-permute-start | bytes 786440 | tf_op jit(solution)/shard_map/ppermute | solution.py:278
  69.3 8.9 %collective-permute-start.12 = (bf16[512,128]{1,0:T(8,128)(2,1)S(1)}, bf16[512,128]{1,0:T(8,128)(2,1)S(1)}, u32[]{:S(2)}, u32[]{:S(2)}) collective-permute-start(bf16[512,128]{1,0:T(8,128)(2,1)S(1)} %get-tuple-element.50), channel_id=1, source_target_pairs={{0,7},{1,6},{2,5},{3,4},{4,3},{5,2},{6,1},{7,0},{8,15},{9,14},{10,... | collective-permute-start | bytes 393224 | tf_op jit(solution)/shard_map/ppermute | solution.py:278
  73.0 6.4 %collective-permute-start.13 = (bf16[512,128]{1,0:T(8,128)(2,1)S(1)}, bf16[512,128]{1,0:T(8,128)(2,1)S(1)}, u32[]{:S(2)}, u32[]{:S(2)}) collective-permute-start(bf16[512,128]{1,0:T(8,128)(2,1)S(1)} %get-tuple-element.51), channel_id=1, source_target_pairs={{0,3},{1,2},{2,1},{3,0},{4,7},{5,6},{6,5},{7,4},{8,11},{9,10},{10,... | collective-permute-start | bytes 393224 | tf_op jit(solution)/shard_map/ppermute | solution.py:278

commit v20 on v19

--- a/solution.py
+++ b/solution.py
@@ -162,8 +162,12 @@
         out[...] = (left[i].astype(jnp.float32) * right[i].astype(jnp.float32)).astype(jnp.bfloat16)
 
 
-def place_kernel(order, where, *refs):
-    pieces, whole = refs[:-1], refs[-1]
+def finish_kernel(order, scale, where, *refs):
+    pieces, shares, (whole, total) = refs[: len(order)], refs[len(order) : -2], refs[-2:]
+    added = shares[0][...].astype(jnp.float32)
+    for share in shares[1:]:
+        added = added + share[...].astype(jnp.float32)
+    total[...] = added * scale
     for k, piece in zip(order, pieces):
         whole[lax.bitwise_xor(where[0], k)] = piece[...]
 
@@ -284,8 +288,8 @@
     channels, span = saved_input.shape[1:]
     rows, length = long_filter.shape
     width = length // BLOCKS
-    grad_order, input_order, back_order = (spread(count, o) for o in ((4, 1, 5, 2, 6, 7, 3), (4, 5, 6, 1, 2, 7, 3), (1, 4, 2, 5, 6, 7, 3)))
-    late = 2
+    grad_order, input_order, back_order = (spread(count, o) for o in ((4, 1, 5, 2, 6, 7, 3), (4, 5, 6, 1, 7, 2, 3), (1, 4, 2, 5, 6, 7, 3)))
+    late = 3
     at = count - 1 - late
     every = range(count + 8)
     where = jnp.stack([lax.axis_index("ctx"), lax.axis_index("dp")]).astype(jnp.int32)
@@ -341,11 +345,10 @@
     )
     cross_blocks = exchange(cross, far_first(shares), "dp", shares)
     scale = 1.0 / math.sqrt(shares * length)
-    grad_filter = sum(x.astype(full) for x in cross_blocks) * scale
-    (whole,) = call(
-        functools.partial(place_kernel, back_order),
-        [where, *back_blocks],
-        [jax.ShapeDtypeStruct((count, rows, span), half)],
+    whole, grad_filter = call(
+        functools.partial(finish_kernel, back_order, scale),
+        [where, *back_blocks, *cross_blocks],
+        [jax.ShapeDtypeStruct((count, rows, span), half), jax.ShapeDtypeStruct((rows, length // shares), full)],
     )
     return (whole.reshape(1, channels, span), grad_filter)
 

time: 82.1 us -> 81.2 us (0.989)
  starting transfers between devices: 49.2 us -> 46 us
  waiting for transfers between devices: 15.1 us -> 18.1 us
  other arithmetic: 1.01 us -> 0.08 us
    ppermute x24, starting transfers between devices: 49.2 us -> 46 us  [exchange(): lax.ppermute(piece, axis, [(i, i ^ k) for i in range(size)])]
    ppermute x24, waiting for transfers between devices: 15.1 us -> 18.1 us  [exchange(): lax.ppermute(piece, axis, [(i, i ^ k) for i in range(size)])]
    mul x1 -> x0, other arithmetic: 0.93 us -> none  [on_device(): grad_filter = sum((x.astype(full) for x in cross_blocks)) * scale]
  transfers between devices with their start and end apart: 24 -> 24, of which waited for: 6 -> 6; matrix products, arithmetic and copies ran while one was open for 0% -> 0% of each run, Pallas kernels for 15% -> 13%
where the time goes in v20:
time: 81.2 us; the launch traced here: 81.1 us
  starting transfers between devices  46 us (57%)
  waiting for transfers between devices  18.1 us (22%)
  Pallas kernels  14.6 us (18%)
  local copies, waits for them, and re-layouts  1.6 us (2%)
    ppermute x24, starting transfers between devices, exchange(): lax.ppermute(piece, axis, [(i, i ^ k) for i in range(size)])  46 us
    ppermute x24, waiting for transfers between devices, exchange(): lax.ppermute(piece, axis, [(i, i ^ k) for i in range(size)])  18.1 us
    pallas_call x5, Pallas kernels, call(): pl.pallas_call(kernel, out_shape=list(outs), in_specs=specs, out_specs=[s...  14.6 us
  transfers between devices with their start and end apart: 24, of which 6 were waited for; matrix products, arithmetic and copies ran while one was open for 0% of the time, Pallas kernels for 13%

profile of v20, /device:TPU:0, one launch (start us, length us, event | category | flops | bytes accessed | tf_op | source)
XLA Modules:
  0.0 81.1 jit_solution(5179226076243625149)
XLA Ops:
  0.6 0.0 copy-start
  0.6 0.1 pad_add_fusion.where
  0.7 2.3 %shard_map.77 = (bf16[512,128]{1,0:T(8,128)(2,1)S(1)}, bf16[512,128]{1,0:T(8,128)(2,1)S(1)}, bf16[512,128]{1,0:T(8,128)(2,1)S(1)}, bf16[512,128]{1,0:T(8,128)(2,...) custom-call(s32[2]{0:T(128)S(1)} %pad_add_fusion.where, ...), custom_call_target="tpu_custom_call" | custom-call | bytes 3145736 | tf_op jit(solution)/shard_map/pallas_call | solution.py:257
  3.0 4.1 %collective-permute-start = (bf16[512,128]{1,0:T(8,128)(2,1)S(1)}, bf16[512,128]{1,0:T(8,128)(2,1)S(1)}, u32[]{:S(2)}, u32[]{:S(2)}) collective-permute-start(bf16[512,128]{1,0:T(8,128)(2,1)S(1)} %get-tuple-element.37), channel_id=1, source_target_pairs={{0,4},{1,5},{2,6},{3,7},{4,0},{5,1},{6,2},{7,3},{8,12},{9,13},{10,... | collective-permute-start | bytes 393224 | tf_op jit(solution)/shard_map/ppermute | solution.py:282
  7.1 1.5 %collective-permute-start.1 = (bf16[512,128]{1,0:T(8,128)(2,1)S(1)}, bf16[512,128]{1,0:T(8,128)(2,1)S(1)}, u32[]{:S(2)}, u32[]{:S(2)}) collective-permute-start(bf16[512,128]{1,0:T(8,128)(2,1)S(1)} %get-tuple-element.38), channel_id=1, source_target_pairs={{0,1},{1,0},{2,3},{3,2},{4,5},{5,4},{6,7},{7,6},{8,9},{9,8},{10,11... | collective-permute-start | bytes 393224 | tf_op jit(solution)/shard_map/ppermute | solution.py:282
  8.7 0.0 collective-permute-start.2
  8.7 1.8 %collective-permute-start.3 = (bf16[512,128]{1,0:T(8,128)(2,1)S(1)}, bf16[512,128]{1,0:T(8,128)(2,1)S(1)}, u32[]{:S(2)}, u32[]{:S(2)}) collective-permute-start(bf16[512,128]{1,0:T(8,128)(2,1)S(1)} %get-tuple-element.40), channel_id=1, source_target_pairs={{0,2},{1,3},{2,0},{3,1},{4,6},{5,7},{6,4},{7,5},{8,10},{9,11},{10,... | collective-permute-start | bytes 393224 | tf_op jit(solution)/shard_map/ppermute | solution.py:282
  10.5 2.5 %collective-permute-start.4 = (bf16[512,128]{1,0:T(8,128)(2,1)S(1)}, bf16[512,128]{1,0:T(8,128)(2,1)S(1)}, u32[]{:S(2)}, u32[]{:S(2)}) collective-permute-start(bf16[512,128]{1,0:T(8,128)(2,1)S(1)} %get-tuple-element.41), channel_id=1, source_target_pairs={{0,6},{1,7},{2,4},{3,5},{4,2},{5,3},{6,0},{7,1},{8,14},{9,15},{10,... | collective-permute-start | bytes 393224 | tf_op jit(solution)/shard_map/ppermute | solution.py:282
  13.0 4.8 %collective-permute-done.refs_0_ = bf16[512,128]{1,0:T(8,128)(2,1)S(1)} collective-permute-done((bf16[512,128]{1,0:T(8,128)(2,1)S(1)}, bf16[512,128]{1,0:T(8,128)(2,1)S(1)}, u32[]{:S(2)}, u32[]{:S(2)}) %collective-permute-start) | collective-permute-done | bytes 131104 | tf_op jit(solution)/shard_map/ppermute | solution.py:282
  17.8 5.9 %collective-permute-start.5 = (bf16[512,128]{1,0:T(8,128)(2,1)S(1)}, bf16[512,128]{1,0:T(8,128)(2,1)S(1)}, u32[]{:S(2)}, u32[]{:S(2)}) collective-permute-start(bf16[512,128]{1,0:T(8,128)(2,1)S(1)} %get-tuple-element.42), channel_id=1, source_target_pairs={{0,7},{1,6},{2,5},{3,4},{4,3},{5,2},{6,1},{7,0},{8,15},{9,14},{10,... | collective-permute-start | bytes 393224 | tf_op jit(solution)/shard_map/ppermute | solution.py:282
  23.8 0.0 collective-permute-done.1.refs_1_
  23.8 0.0 collective-permute-start.6
  23.8 0.0 copy-done
  23.8 0.0 copy-start.2
  23.8 1.6 %copy-done.2 = f32[512,1024]{1,0:T(8,128)S(1)} copy-done((f32[512,1024]{1,0:T(8,128)S(1)}, f32[512,1024]{1,0:T(8,128)}, u32[]{:S(2)}) %copy-start.2) | copy-done | bytes 2097176
  25.4 0.0 copy-start.1
  25.4 2.1 %shard_map.78 = (bf16[512,128]{1,0:T(8,128)(2,1)S(1)}, bf16[512,128]{1,0:T(8,128)(2,1)S(1)}, bf16[512,128]{1,0:T(8,128)(2,1)S(1)}, bf16[512,128]{1,0:T(8,128)(2,...) custom-call(s32[2]{0:T(128)S(1)} %pad_add_fusion.where, ...), custom_call_target="tpu_custom_call" | custom-call | flops 603979776 | bytes 7733256 | tf_op jit(solution)/shard_map/pallas_call | solution.py:257
  27.5 0.0 collective-permute-done.2.refs_2_
  27.5 0.6 collective-permute-start.14
  28.1 0.0 collective-permute-done.3.refs_3_
  28.1 2.3 %collective-permute-start.15 = (bf16[512,128]{1,0:T(8,128)(2,1)S(1)}, bf16[512,128]{1,0:T(8,128)(2,1)S(1)}, u32[]{:S(2)}, u32[]{:S(2)}) collective-permute-start(bf16[512,128]{1,0:T(8,128)(2,1)S(1)} %get-tuple-element.58), channel_id=1, source_target_pairs={{0,5},{1,4},{2,7},{3,6},{4,1},{5,0},{6,3},{7,2},{8,13},{9,12},{10,... | collective-permute-start | bytes 393224 | tf_op jit(solution)/shard_map/ppermute | solution.py:282
  30.4 0.0 collective-permute-done.4.refs_4_
  30.4 2.5 %collective-permute-start.16 = (bf16[512,128]{1,0:T(8,128)(2,1)S(1)}, bf16[512,128]{1,0:T(8,128)(2,1)S(1)}, u32[]{:S(2)}, u32[]{:S(2)}) collective-permute-start(bf16[512,128]{1,0:T(8,128)(2,1)S(1)} %get-tuple-element.59), channel_id=1, source_target_pairs={{0,6},{1,7},{2,4},{3,5},{4,2},{5,3},{6,0},{7,1},{8,14},{9,15},{10,... | collective-permute-start | bytes 393224 | tf_op jit(solution)/shard_map/ppermute | solution.py:282
  32.9 0.0 collective-permute-done.5.refs_5_
  32.9 0.5 collective-permute-start.17
  33.5 0.0 collective-permute-done.6.refs_6_
  33.5 0.0 copy-done.1
  33.5 4.2 %shard_map.79 = (bf16[512,128]{1,0:T(8,128)(2,1)S(1)}, bf16[512,128]{1,0:T(8,128)(2,1)S(1)}, bf16[512,128]{1,0:T(8,128)(2,1)S(1)}, bf16[512,128]{1,0:T(8,128)(2,...) custom-call(s32[2]{0:T(128)S(1)} %pad_add_fusion.where, ...), custom_call_target="tpu_custom_call", output_to_operand_aliasing={{0}: (9, {}), {1}: (10, {}), {2}: (11, {})} | custom-call | flops 1207959552 | bytes 9961480 | tf_op jit(solution)/shard_map/pallas_call | solution.py:257
  37.7 2.3 %collective-permute-start.18 = (bf16[512,128]{1,0:T(8,128)(2,1)S(1)}, bf16[512,128]{1,0:T(8,128)(2,1)S(1)}, u32[]{:S(2)}, u32[]{:S(2)}) collective-permute-start(bf16[512,128]{1,0:T(8,128)(2,1)S(1)} %get-tuple-element.61), channel_id=1, source_target_pairs={{0,7},{1,6},{2,5},{3,4},{4,3},{5,2},{6,1},{7,0},{8,15},{9,14},{10,... | collective-permute-start | bytes 393224 | tf_op jit(solution)/shard_map/ppermute | solution.py:282
  40.0 3.7 %collective-permute-done.14.refs_0_ = bf16[512,128]{1,0:T(8,128)(2,1)S(1)} collective-permute-done((bf16[512,128]{1,0:T(8,128)(2,1)S(1)}, bf16[512,128]{1,0:T(8,128)(2,1)S(1)}, u32[]{:S(2)}, u32[]{:S(2)}) %collective-permute-start.14) | collective-permute-done | bytes 131104 | tf_op jit(solution)/shard_map/ppermute | solution.py:282
  43.8 6.4 %collective-permute-start.19 = (bf16[512,128]{1,0:T(8,128)(2,1)S(1)}, bf16[512,128]{1,0:T(8,128)(2,1)S(1)}, u32[]{:S(2)}, u32[]{:S(2)}) collective-permute-start(bf16[512,128]{1,0:T(8,128)(2,1)S(1)} %get-tuple-element.62), channel_id=1, source_target_pairs={{0,2},{1,3},{2,0},{3,1},{4,6},{5,7},{6,4},{7,5},{8,10},{9,11},{10,... | collective-permute-start | bytes 393224 | tf_op jit(solution)/shard_map/ppermute | solution.py:282
  50.2 0.0 collective-permute-done.15.refs_1_
  50.2 0.0 collective-permute-start.20
  50.2 0.0 collective-permute-done.16.refs_2_
  50.2 1.5 %collective-permute-start.7 = (bf16[512,128]{1,0:T(8,128)(2,1)S(1)}, bf16[512,128]{1,0:T(8,128)(2,1)S(1)}, u32[]{:S(2)}, u32[]{:S(2)}) collective-permute-start(bf16[512,128]{1,0:T(8,128)(2,1)S(1)} %get-tuple-element.49), channel_id=1, source_target_pairs={{0,1},{1,0},{2,3},{3,2},{4,5},{5,4},{6,7},{7,6},{8,9},{9,8},{10,11... | collective-permute-start | bytes 393224 | tf_op jit(solution)/shard_map/ppermute | solution.py:282
  51.8 0.0 collective-permute-done.17.refs_3_
  51.8 2.5 %collective-permute-start.8 = (bf16[512,128]{1,0:T(8,128)(2,1)S(1)}, bf16[512,128]{1,0:T(8,128)(2,1)S(1)}, u32[]{:S(2)}, u32[]{:S(2)}) collective-permute-start(bf16[512,128]{1,0:T(8,128)(2,1)S(1)} %get-tuple-element.50), channel_id=1, source_target_pairs={{0,4},{1,5},{2,6},{3,7},{4,0},{5,1},{6,2},{7,3},{8,12},{9,13},{10,... | collective-permute-start | bytes 393224 | tf_op jit(solution)/shard_map/ppermute | solution.py:282
  54.3 0.0 collective-permute-done.18.refs_4_
  54.3 0.7 collective-permute-start.9
  55.0 0.0 collective-permute-done.19.refs_5_
  55.0 3.2 %collective-permute-start.10 = (bf16[512,128]{1,0:T(8,128)(2,1)S(1)}, bf16[512,128]{1,0:T(8,128)(2,1)S(1)}, u32[]{:S(2)}, u32[]{:S(2)}) collective-permute-start(bf16[512,128]{1,0:T(8,128)(2,1)S(1)} %get-tuple-element.52), channel_id=1, source_target_pairs={{0,5},{1,4},{2,7},{3,6},{4,1},{5,0},{6,3},{7,2},{8,13},{9,12},{10,... | collective-permute-start | bytes 393224 | tf_op jit(solution)/shard_map/ppermute | solution.py:282
  58.1 1.4 %collective-permute-done.20.refs_6_ = bf16[512,128]{1,0:T(8,128)(2,1)S(1)} collective-permute-done((bf16[512,128]{1,0:T(8,128)(2,1)S(1)}, bf16[512,128]{1,0:T(8,128)(2,1)S(1)}, u32[]{:S(2)}, u32[]{:S(2)}) %collective-permute-start.20) | collective-permute-done | bytes 131104 | tf_op jit(solution)/shard_map/ppermute | solution.py:282
  59.6 0.5 collective-permute-start.11
  60.1 4.1 %shard_map.80 = (bf16[512,256]{1,0:T(8,128)(2,1)S(1)}, bf16[512,256]{1,0:T(8,128)(2,1)S(1)}, bf16[512,256]{1,0:T(8,128)(2,1)S(1)}, bf16[512,256]{1,0:T(8,128)(2,1)S(1)}) custom-call(s32[2]{0:T(128)S(1)} %pad_add_fusion.where, bf16[512,128]{1,0:T(8,128)(2,1)S(1)} %collective-permute-done.14.refs_0_, bf16[512,128]{1,0:T(8,128)(2,1)S(1)} %collective-permute-done.15.refs_1_, ...), custom_call_target="tpu_custom_call" | custom-call | flops 1207959552 | bytes 6815752 | tf_op jit(solution)/shard_map/pallas_call | solution.py:257
  64.2 0.0 collective-permute-done.7.refs_0_
  64.2 1.6 %collective-permute-start.21 = (bf16[512,256]{1,0:T(8,128)(2,1)S(1)}, bf16[512,256]{1,0:T(8,128)(2,1)S(1)}, u32[]{:S(2)}, u32[]{:S(2)}) collective-permute-start(bf16[512,256]{1,0:T(8,128)(2,1)S(1)} %get-tuple-element.66), channel_id=1, source_target_pairs={{0,16},{8,24},{16,0},{24,8},{1,17},{9,25},{17,1},{25,9},{2,18},{10... | collective-permute-start | bytes 786440 | tf_op jit(solution)/shard_map/ppermute | solution.py:282
  65.7 0.0 collective-permute-done.8.refs_1_
  65.8 0.0 collective-permute-start.22
  65.8 0.0 collective-permute-done.9.refs_2_
  65.8 0.6 collective-permute-start.23
  66.4 2.9 %collective-permute-done.10.refs_3_ = bf16[512,128]{1,0:T(8,128)(2,1)S(1)} collective-permute-done((bf16[512,128]{1,0:T(8,128)(2,1)S(1)}, bf16[512,128]{1,0:T(8,128)(2,1)S(1)}, u32[]{:S(2)}, u32[]{:S(2)}) %collective-permute-start.10) | collective-permute-done | bytes 131104 | tf_op jit(solution)/shard_map/ppermute | solution.py:282
  69.3 4.0 %collective-permute-start.12 = (bf16[512,128]{1,0:T(8,128)(2,1)S(1)}, bf16[512,128]{1,0:T(8,128)(2,1)S(1)}, u32[]{:S(2)}, u32[]{:S(2)}) collective-permute-start(bf16[512,128]{1,0:T(8,128)(2,1)S(1)} %get-tuple-element.54), channel_id=1, source_target_pairs={{0,7},{1,6},{2,5},{3,4},{4,3},{5,2},{6,1},{7,0},{8,15},{9,14},{10,... | collective-permute-start | bytes 393224 | tf_op jit(solution)/shard_map/ppermute | solution.py:282
  73.4 0.0 collective-permute-done.11.refs_4_
  73.4 0.8 collective-permute-start.13
  74.1 3.3 %collective-permute-done.12.refs_5_ = bf16[512,128]{1,0:T(8,128)(2,1)S(1)} collective-permute-done((bf16[512,128]{1,0:T(8,128)(2,1)S(1)}, bf16[512,128]{1,0:T(8,128)(2,1)S(1)}, u32[]{:S(2)}, u32[]{:S(2)}) %collective-permute-start.12) | collective-permute-done | bytes 131104 | tf_op jit(solution)/shard_map/ppermute | solution.py:282
  77.4 1.8 %collective-permute-done.13.refs_6_ = bf16[512,128]{1,0:T(8,128)(2,1)S(1)} collective-permute-done((bf16[512,128]{1,0:T(8,128)(2,1)S(1)}, bf16[512,128]{1,0:T(8,128)(2,1)S(1)}, u32[]{:S(2)}, u32[]{:S(2)}) %collective-permute-start.13) | collective-permute-done | bytes 131104 | tf_op jit(solution)/shard_map/ppermute | solution.py:282
  79.2 0.0 collective-permute-done.21.refs_8_
  79.2 0.0 collective-permute-done.22.refs_9_
  79.2 0.0 collective-permute-done.23.refs_10_
  79.2 1.8 %shard_map.81 = (bf16[8,512,128]{2,1,0:T(8,128)(2,1)}, f32[512,256]{1,0:T(8,128)}) custom-call(s32[2]{0:T(128)S(1)} %pad_add_fusion.where, bf16[512,128]{1,0:T(8,128)(2,1)S(1)} %collective-permute-done.7.refs_0_, bf16[512,128]{1,0:T(8,128)(2,1)S(1)} %collective-permute-done.8.refs_1_, bf16[512,128]{1,0:T(8,128)(2,1)S(1)} %collective-permute-done.9.refs_2_, ...), custom_call_target="tpu_custom_call" | custom-call | bytes 3670024 | tf_op jit(solution)/shard_map/pallas_call | solution.py:257
Async XLA Ops:
  0.6 23.1 %copy-start = (bf16[9,256,256]{2,1,0:T(8,128)(2,1)S(1)}, bf16[9,256,256]{2,1,0:T(8,128)(2,1)}, u32[]{:S(2)}) copy-start(bf16[9,256,256]{2,1,0:T(8,128)(2,1)} %constant.12.clone.forward.refs_12_.refs_9_) | copy-start | bytes 3538948
  3.0 14.8 %collective-permute-start = (bf16[512,128]{1,0:T(8,128)(2,1)S(1)}, bf16[512,128]{1,0:T(8,128)(2,1)S(1)}, u32[]{:S(2)}, u32[]{:S(2)}) collective-permute-start(bf16[512,128]{1,0:T(8,128)(2,1)S(1)} %get-tuple-element.37), channel_id=1, source_target_pairs={{0,4},{1,5},{2,6},{3,7},{4,0},{5,1},{6,2},{7,3},{8,12},{9,13},{10,... | collective-permute-start | bytes 393224 | tf_op jit(solution)/shard_map/ppermute | solution.py:282
  7.1 16.6 %collective-permute-start.1 = (bf16[512,128]{1,0:T(8,128)(2,1)S(1)}, bf16[512,128]{1,0:T(8,128)(2,1)S(1)}, u32[]{:S(2)}, u32[]{:S(2)}) collective-permute-start(bf16[512,128]{1,0:T(8,128)(2,1)S(1)} %get-tuple-element.38), channel_id=1, source_target_pairs={{0,1},{1,0},{2,3},{3,2},{4,5},{5,4},{6,7},{7,6},{8,9},{9,8},{10,11... | collective-permute-start | bytes 393224 | tf_op jit(solution)/shard_map/ppermute | solution.py:282
  8.7 18.8 %collective-permute-start.2 = (bf16[512,128]{1,0:T(8,128)(2,1)S(1)}, bf16[512,128]{1,0:T(8,128)(2,1)S(1)}, u32[]{:S(2)}, u32[]{:S(2)}) collective-permute-start(bf16[512,128]{1,0:T(8,128)(2,1)S(1)} %get-tuple-element.39), channel_id=1, source_target_pairs={{0,5},{1,4},{2,7},{3,6},{4,1},{5,0},{6,3},{7,2},{8,13},{9,12},{10,... | collective-permute-start | bytes 393224 | tf_op jit(solution)/shard_map/ppermute | solution.py:282
  8.7 19.4 %collective-permute-start.3 = (bf16[512,128]{1,0:T(8,128)(2,1)S(1)}, bf16[512,128]{1,0:T(8,128)(2,1)S(1)}, u32[]{:S(2)}, u32[]{:S(2)}) collective-permute-start(bf16[512,128]{1,0:T(8,128)(2,1)S(1)} %get-tuple-element.40), channel_id=1, source_target_pairs={{0,2},{1,3},{2,0},{3,1},{4,6},{5,7},{6,4},{7,5},{8,10},{9,11},{10,... | collective-permute-start | bytes 393224 | tf_op jit(solution)/shard_map/ppermute | solution.py:282
  10.5 19.9 %collective-permute-start.4 = (bf16[512,128]{1,0:T(8,128)(2,1)S(1)}, bf16[512,128]{1,0:T(8,128)(2,1)S(1)}, u32[]{:S(2)}, u32[]{:S(2)}) collective-permute-start(bf16[512,128]{1,0:T(8,128)(2,1)S(1)} %get-tuple-element.41), channel_id=1, source_target_pairs={{0,6},{1,7},{2,4},{3,5},{4,2},{5,3},{6,0},{7,1},{8,14},{9,15},{10,... | collective-permute-start | bytes 393224 | tf_op jit(solution)/shard_map/ppermute | solution.py:282
  17.8 15.1 %collective-permute-start.5 = (bf16[512,128]{1,0:T(8,128)(2,1)S(1)}, bf16[512,128]{1,0:T(8,128)(2,1)S(1)}, u32[]{:S(2)}, u32[]{:S(2)}) collective-permute-start(bf16[512,128]{1,0:T(8,128)(2,1)S(1)} %get-tuple-element.42), channel_id=1, source_target_pairs={{0,7},{1,6},{2,5},{3,4},{4,3},{5,2},{6,1},{7,0},{8,15},{9,14},{10,... | collective-permute-start | bytes 393224 | tf_op jit(solution)/shard_map/ppermute | solution.py:282
  23.8 9.7 %collective-permute-start.6 = (bf16[512,128]{1,0:T(8,128)(2,1)S(1)}, bf16[512,128]{1,0:T(8,128)(2,1)S(1)}, u32[]{:S(2)}, u32[]{:S(2)}) collective-permute-start(bf16[512,128]{1,0:T(8,128)(2,1)S(1)} %get-tuple-element.43), channel_id=1, source_target_pairs={{0,3},{1,2},{2,1},{3,0},{4,7},{5,6},{6,5},{7,4},{8,11},{9,10},{10,... | collective-permute-start | bytes 393224 | tf_op jit(solution)/shard_map/ppermute | solution.py:282
  23.8 1.6 %copy-start.2 = (f32[512,1024]{1,0:T(8,128)S(1)}, f32[512,1024]{1,0:T(8,128)}, u32[]{:S(2)}) copy-start(f32[512,1024]{1,0:T(8,128)} %taps.1) | copy-start | bytes 6291460
  25.4 8.1 %copy-start.1 = (bf16[9,256,256]{2,1,0:T(8,128)(2,1)S(1)}, bf16[9,256,256]{2,1,0:T(8,128)(2,1)}, u32[]{:S(2)}) copy-start(bf16[9,256,256]{2,1,0:T(8,128)(2,1)} %constant.13.clone.refs_13_.refs_10_) | copy-start | bytes 3538948
  27.5 16.3 %collective-permute-start.14 = (bf16[512,128]{1,0:T(8,128)(2,1)S(1)}, bf16[512,128]{1,0:T(8,128)(2,1)S(1)}, u32[]{:S(2)}, u32[]{:S(2)}) collective-permute-start(bf16[512,128]{1,0:T(8,128)(2,1)S(1)} %get-tuple-element.57), channel_id=1, source_target_pairs={{0,4},{1,5},{2,6},{3,7},{4,0},{5,1},{6,2},{7,3},{8,12},{9,13},{10,... | collective-permute-start | bytes 393224 | tf_op jit(solution)/shard_map/ppermute | solution.py:282
  28.1 22.1 %collective-permute-start.15 = (bf16[512,128]{1,0:T(8,128)(2,1)S(1)}, bf16[512,128]{1,0:T(8,128)(2,1)S(1)}, u32[]{:S(2)}, u32[]{:S(2)}) collective-permute-start(bf16[512,128]{1,0:T(8,128)(2,1)S(1)} %get-tuple-element.58), channel_id=1, source_target_pairs={{0,5},{1,4},{2,7},{3,6},{4,1},{5,0},{6,3},{7,2},{8,13},{9,12},{10,... | collective-permute-start | bytes 393224 | tf_op jit(solution)/shard_map/ppermute | solution.py:282
  30.4 19.8 %collective-permute-start.16 = (bf16[512,128]{1,0:T(8,128)(2,1)S(1)}, bf16[512,128]{1,0:T(8,128)(2,1)S(1)}, u32[]{:S(2)}, u32[]{:S(2)}) collective-permute-start(bf16[512,128]{1,0:T(8,128)(2,1)S(1)} %get-tuple-element.59), channel_id=1, source_target_pairs={{0,6},{1,7},{2,4},{3,5},{4,2},{5,3},{6,0},{7,1},{8,14},{9,15},{10,... | collective-permute-start | bytes 393224 | tf_op jit(solution)/shard_map/ppermute | solution.py:282
  32.9 18.8 %collective-permute-start.17 = (bf16[512,128]{1,0:T(8,128)(2,1)S(1)}, bf16[512,128]{1,0:T(8,128)(2,1)S(1)}, u32[]{:S(2)}, u32[]{:S(2)}) collective-permute-start(bf16[512,128]{1,0:T(8,128)(2,1)S(1)} %get-tuple-element.60), channel_id=1, source_target_pairs={{0,1},{1,0},{2,3},{3,2},{4,5},{5,4},{6,7},{7,6},{8,9},{9,8},{10,11... | collective-permute-start | bytes 393224 | tf_op jit(solution)/shard_map/ppermute | solution.py:282
  37.7 16.5 %collective-permute-start.18 = (bf16[512,128]{1,0:T(8,128)(2,1)S(1)}, bf16[512,128]{1,0:T(8,128)(2,1)S(1)}, u32[]{:S(2)}, u32[]{:S(2)}) collective-permute-start(bf16[512,128]{1,0:T(8,128)(2,1)S(1)} %get-tuple-element.61), channel_id=1, source_target_pairs={{0,7},{1,6},{2,5},{3,4},{4,3},{5,2},{6,1},{7,0},{8,15},{9,14},{10,... | collective-permute-start | bytes 393224 | tf_op jit(solution)/shard_map/ppermute | solution.py:282
  43.8 11.2 %collective-permute-start.19 = (bf16[512,128]{1,0:T(8,128)(2,1)S(1)}, bf16[512,128]{1,0:T(8,128)(2,1)S(1)}, u32[]{:S(2)}, u32[]{:S(2)}) collective-permute-start(bf16[512,128]{1,0:T(8,128)(2,1)S(1)} %get-tuple-element.62), channel_id=1, source_target_pairs={{0,2},{1,3},{2,0},{3,1},{4,6},{5,7},{6,4},{7,5},{8,10},{9,11},{10,... | collective-permute-start | bytes 393224 | tf_op jit(solution)/shard_map/ppermute | solution.py:282
  50.2 9.4 %collective-permute-start.20 = (bf16[512,128]{1,0:T(8,128)(2,1)S(1)}, bf16[512,128]{1,0:T(8,128)(2,1)S(1)}, u32[]{:S(2)}, u32[]{:S(2)}) collective-permute-start(bf16[512,128]{1,0:T(8,128)(2,1)S(1)} %get-tuple-element.63), channel_id=1, source_target_pairs={{0,3},{1,2},{2,1},{3,0},{4,7},{5,6},{6,5},{7,4},{8,11},{9,10},{10,... | collective-permute-start | bytes 393224 | tf_op jit(solution)/shard_map/ppermute | solution.py:282
  50.2 13.9 %collective-permute-start.7 = (bf16[512,128]{1,0:T(8,128)(2,1)S(1)}, bf16[512,128]{1,0:T(8,128)(2,1)S(1)}, u32[]{:S(2)}, u32[]{:S(2)}) collective-permute-start(bf16[512,128]{1,0:T(8,128)(2,1)S(1)} %get-tuple-element.49), channel_id=1, source_target_pairs={{0,1},{1,0},{2,3},{3,2},{4,5},{5,4},{6,7},{7,6},{8,9},{9,8},{10,11... | collective-permute-start | bytes 393224 | tf_op jit(solution)/shard_map/ppermute | solution.py:282
  51.8 14.0 %collective-permute-start.8 = (bf16[512,128]{1,0:T(8,128)(2,1)S(1)}, bf16[512,128]{1,0:T(8,128)(2,1)S(1)}, u32[]{:S(2)}, u32[]{:S(2)}) collective-permute-start(bf16[512,128]{1,0:T(8,128)(2,1)S(1)} %get-tuple-element.50), channel_id=1, source_target_pairs={{0,4},{1,5},{2,6},{3,7},{4,0},{5,1},{6,2},{7,3},{8,12},{9,13},{10,... | collective-permute-start | bytes 393224 | tf_op jit(solution)/shard_map/ppermute | solution.py:282
  54.3 11.5 %collective-permute-start.9 = (bf16[512,128]{1,0:T(8,128)(2,1)S(1)}, bf16[512,128]{1,0:T(8,128)(2,1)S(1)}, u32[]{:S(2)}, u32[]{:S(2)}) collective-permute-start(bf16[512,128]{1,0:T(8,128)(2,1)S(1)} %get-tuple-element.51), channel_id=1, source_target_pairs={{0,2},{1,3},{2,0},{3,1},{4,6},{5,7},{6,4},{7,5},{8,10},{9,11},{10,... | collective-permute-start | bytes 393224 | tf_op jit(solution)/shard_map/ppermute | solution.py:282
  55.0 14.4 %collective-permute-start.10 = (bf16[512,128]{1,0:T(8,128)(2,1)S(1)}, bf16[512,128]{1,0:T(8,128)(2,1)S(1)}, u32[]{:S(2)}, u32[]{:S(2)}) collective-permute-start(bf16[512,128]{1,0:T(8,128)(2,1)S(1)} %get-tuple-element.52), channel_id=1, source_target_pairs={{0,5},{1,4},{2,7},{3,6},{4,1},{5,0},{6,3},{7,2},{8,13},{9,12},{10,... | collective-permute-start | bytes 393224 | tf_op jit(solution)/shard_map/ppermute | solution.py:282
  59.6 13.8 %collective-permute-start.11 = (bf16[512,128]{1,0:T(8,128)(2,1)S(1)}, bf16[512,128]{1,0:T(8,128)(2,1)S(1)}, u32[]{:S(2)}, u32[]{:S(2)}) collective-permute-start(bf16[512,128]{1,0:T(8,128)(2,1)S(1)} %get-tuple-element.53), channel_id=1, source_target_pairs={{0,6},{1,7},{2,4},{3,5},{4,2},{5,3},{6,0},{7,1},{8,14},{9,15},{10,... | collective-permute-start | bytes 393224 | tf_op jit(solution)/shard_map/ppermute | solution.py:282
  64.2 15.0 %collective-permute-start.21 = (bf16[512,256]{1,0:T(8,128)(2,1)S(1)}, bf16[512,256]{1,0:T(8,128)(2,1)S(1)}, u32[]{:S(2)}, u32[]{:S(2)}) collective-permute-start(bf16[512,256]{1,0:T(8,128)(2,1)S(1)} %get-tuple-element.66), channel_id=1, source_target_pairs={{0,16},{8,24},{16,0},{24,8},{1,17},{9,25},{17,1},{25,9},{2,18},{10... | collective-permute-start | bytes 786440 | tf_op jit(solution)/shard_map/ppermute | solution.py:282
  65.8 13.5 %collective-permute-start.22 = (bf16[512,256]{1,0:T(8,128)(2,1)S(1)}, bf16[512,256]{1,0:T(8,128)(2,1)S(1)}, u32[]{:S(2)}, u32[]{:S(2)}) collective-permute-start(bf16[512,256]{1,0:T(8,128)(2,1)S(1)} %get-tuple-element.67), channel_id=1, source_target_pairs={{0,24},{8,16},{16,8},{24,0},{1,25},{9,17},{17,9},{25,1},{2,26},{10... | collective-permute-start | bytes 786440 | tf_op jit(solution)/shard_map/ppermute | solution.py:282
  65.8 13.5 %collective-permute-start.23 = (bf16[512,256]{1,0:T(8,128)(2,1)S(1)}, bf16[512,256]{1,0:T(8,128)(2,1)S(1)}, u32[]{:S(2)}, u32[]{:S(2)}) collective-permute-start(bf16[512,256]{1,0:T(8,128)(2,1)S(1)} %get-tuple-element.68), channel_id=1, source_target_pairs={{0,8},{8,0},{16,24},{24,16},{1,9},{9,1},{17,25},{25,17},{2,10},{10... | collective-permute-start | bytes 786440 | tf_op jit(solution)/shard_map/ppermute | solution.py:282
  69.3 8.0 %collective-permute-start.12 = (bf16[512,128]{1,0:T(8,128)(2,1)S(1)}, bf16[512,128]{1,0:T(8,128)(2,1)S(1)}, u32[]{:S(2)}, u32[]{:S(2)}) collective-permute-start(bf16[512,128]{1,0:T(8,128)(2,1)S(1)} %get-tuple-element.54), channel_id=1, source_target_pairs={{0,7},{1,6},{2,5},{3,4},{4,3},{5,2},{6,1},{7,0},{8,15},{9,14},{10,... | collective-permute-start | bytes 393224 | tf_op jit(solution)/shard_map/ppermute | solution.py:282
  73.4 5.9 %collective-permute-start.13 = (bf16[512,128]{1,0:T(8,128)(2,1)S(1)}, bf16[512,128]{1,0:T(8,128)(2,1)S(1)}, u32[]{:S(2)}, u32[]{:S(2)}) collective-permute-start(bf16[512,128]{1,0:T(8,128)(2,1)S(1)} %get-tuple-element.55), channel_id=1, source_target_pairs={{0,3},{1,2},{2,1},{3,0},{4,7},{5,6},{6,5},{7,4},{8,11},{9,10},{10,... | collective-permute-start | bytes 393224 | tf_op jit(solution)/shard_map/ppermute | solution.py:282

commit v21 on v20

--- a/solution.py
+++ b/solution.py
@@ -288,7 +288,7 @@
     channels, span = saved_input.shape[1:]
     rows, length = long_filter.shape
     width = length // BLOCKS
-    grad_order, input_order, back_order = (spread(count, o) for o in ((4, 1, 5, 2, 6, 7, 3), (4, 5, 6, 1, 7, 2, 3), (1, 4, 2, 5, 6, 7, 3)))
+    grad_order, input_order, back_order = (spread(count, o) for o in ((1, 2, 4, 5, 6, 7, 3), (1, 4, 5, 6, 7, 2, 3), (1, 4, 2, 5, 6, 7, 3)))
     late = 3
     at = count - 1 - late
     every = range(count + 8)

time: 81.2 us -> 82.2 us (1.012)
  starting transfers between devices: 46 us -> 47.4 us
    ppermute x24, starting transfers between devices: 46 us -> 47.4 us  [exchange(): lax.ppermute(piece, axis, [(i, i ^ k) for i in range(size)])]
  transfers between devices with their start and end apart: 24 -> 24, of which waited for: 6 -> 5; matrix products, arithmetic and copies ran while one was open for 0% -> 0% of each run, Pallas kernels for 13% -> 13%
where the time goes in v21:
time: 82.2 us; the launch traced here: 82.1 us
  starting transfers between devices  47.4 us (58%)
  waiting for transfers between devices  17.6 us (21%)
  Pallas kernels  14.6 us (18%)
  local copies, waits for them, and re-layouts  1.6 us (2%)
    ppermute x24, starting transfers between devices, exchange(): lax.ppermute(piece, axis, [(i, i ^ k) for i in range(size)])  47.4 us
    ppermute x24, waiting for transfers between devices, exchange(): lax.ppermute(piece, axis, [(i, i ^ k) for i in range(size)])  17.6 us
    pallas_call x5, Pallas kernels, call(): pl.pallas_call(kernel, out_shape=list(outs), in_specs=specs, out_specs=[s...  14.6 us
  transfers between devices with their start and end apart: 24, of which 5 were waited for; matrix products, arithmetic and copies ran while one was open for 0% of the time, Pallas kernels for 13%

profile of v21, /device:TPU:0, one launch (start us, length us, event | category | flops | bytes accessed | tf_op | source)
XLA Modules:
  0.0 82.1 jit_solution(16643323271912767883)
XLA Ops:
  0.6 0.0 copy-start
  0.6 0.1 pad_add_fusion.where
  0.7 2.3 %shard_map.77 = (bf16[512,128]{1,0:T(8,128)(2,1)S(1)}, bf16[512,128]{1,0:T(8,128)(2,1)S(1)}, bf16[512,128]{1,0:T(8,128)(2,1)S(1)}, bf16[512,128]{1,0:T(8,128)(2,...) custom-call(s32[2]{0:T(128)S(1)} %pad_add_fusion.where, ...), custom_call_target="tpu_custom_call" | custom-call | bytes 3145736 | tf_op jit(solution)/shard_map/pallas_call | solution.py:257
  3.0 3.0 %collective-permute-start = (bf16[512,128]{1,0:T(8,128)(2,1)S(1)}, bf16[512,128]{1,0:T(8,128)(2,1)S(1)}, u32[]{:S(2)}, u32[]{:S(2)}) collective-permute-start(bf16[512,128]{1,0:T(8,128)(2,1)S(1)} %get-tuple-element.37), channel_id=1, source_target_pairs={{0,1},{1,0},{2,3},{3,2},{4,5},{5,4},{6,7},{7,6},{8,9},{9,8},{10,11... | collective-permute-start | bytes 393224 | tf_op jit(solution)/shard_map/ppermute | solution.py:282
  6.1 1.6 %collective-permute-start.1 = (bf16[512,128]{1,0:T(8,128)(2,1)S(1)}, bf16[512,128]{1,0:T(8,128)(2,1)S(1)}, u32[]{:S(2)}, u32[]{:S(2)}) collective-permute-start(bf16[512,128]{1,0:T(8,128)(2,1)S(1)} %get-tuple-element.38), channel_id=1, source_target_pairs={{0,2},{1,3},{2,0},{3,1},{4,6},{5,7},{6,4},{7,5},{8,10},{9,11},{10,... | collective-permute-start | bytes 393224 | tf_op jit(solution)/shard_map/ppermute | solution.py:282
  7.7 2.6 %collective-permute-start.2 = (bf16[512,128]{1,0:T(8,128)(2,1)S(1)}, bf16[512,128]{1,0:T(8,128)(2,1)S(1)}, u32[]{:S(2)}, u32[]{:S(2)}) collective-permute-start(bf16[512,128]{1,0:T(8,128)(2,1)S(1)} %get-tuple-element.39), channel_id=1, source_target_pairs={{0,4},{1,5},{2,6},{3,7},{4,0},{5,1},{6,2},{7,3},{8,12},{9,13},{10,... | collective-permute-start | bytes 393224 | tf_op jit(solution)/shard_map/ppermute | solution.py:282
  10.2 0.3 collective-permute-start.3
  10.5 2.5 %collective-permute-start.4 = (bf16[512,128]{1,0:T(8,128)(2,1)S(1)}, bf16[512,128]{1,0:T(8,128)(2,1)S(1)}, u32[]{:S(2)}, u32[]{:S(2)}) collective-permute-start(bf16[512,128]{1,0:T(8,128)(2,1)S(1)} %get-tuple-element.41), channel_id=1, source_target_pairs={{0,6},{1,7},{2,4},{3,5},{4,2},{5,3},{6,0},{7,1},{8,14},{9,15},{10,... | collective-permute-start | bytes 393224 | tf_op jit(solution)/shard_map/ppermute | solution.py:282
  13.0 0.0 collective-permute-done.refs_0_
  13.0 2.3 %collective-permute-start.5 = (bf16[512,128]{1,0:T(8,128)(2,1)S(1)}, bf16[512,128]{1,0:T(8,128)(2,1)S(1)}, u32[]{:S(2)}, u32[]{:S(2)}) collective-permute-start(bf16[512,128]{1,0:T(8,128)(2,1)S(1)} %get-tuple-element.42), channel_id=1, source_target_pairs={{0,7},{1,6},{2,5},{3,4},{4,3},{5,2},{6,1},{7,0},{8,15},{9,14},{10,... | collective-permute-start | bytes 393224 | tf_op jit(solution)/shard_map/ppermute | solution.py:282
  15.3 0.0 collective-permute-done.1.refs_1_
  15.3 0.0 collective-permute-start.6
  15.3 0.0 copy-done
  15.3 0.0 copy-start.2
  15.3 1.6 %copy-done.2 = f32[512,1024]{1,0:T(8,128)S(1)} copy-done((f32[512,1024]{1,0:T(8,128)S(1)}, f32[512,1024]{1,0:T(8,128)}, u32[]{:S(2)}) %copy-start.2) | copy-done | bytes 2097176
  16.9 0.0 copy-start.1
  16.9 2.1 %shard_map.78 = (bf16[512,128]{1,0:T(8,128)(2,1)S(1)}, bf16[512,128]{1,0:T(8,128)(2,1)S(1)}, bf16[512,128]{1,0:T(8,128)(2,1)S(1)}, bf16[512,128]{1,0:T(8,128)(2,...) custom-call(s32[2]{0:T(128)S(1)} %pad_add_fusion.where, ...), custom_call_target="tpu_custom_call" | custom-call | flops 603979776 | bytes 7733256 | tf_op jit(solution)/shard_map/pallas_call | solution.py:257
  19.0 6.7 %collective-permute-done.2.refs_2_ = bf16[512,128]{1,0:T(8,128)(2,1)S(1)} collective-permute-done((bf16[512,128]{1,0:T(8,128)(2,1)S(1)}, bf16[512,128]{1,0:T(8,128)(2,1)S(1)}, u32[]{:S(2)}, u32[]{:S(2)}) %collective-permute-start.2) | collective-permute-done | bytes 131104 | tf_op jit(solution)/shard_map/ppermute | solution.py:282
  25.7 0.0 collective-permute-start.14
  25.7 2.2 %collective-permute-done.3.refs_3_ = bf16[512,128]{1,0:T(8,128)(2,1)S(1)} collective-permute-done((bf16[512,128]{1,0:T(8,128)(2,1)S(1)}, bf16[512,128]{1,0:T(8,128)(2,1)S(1)}, u32[]{:S(2)}, u32[]{:S(2)}) %collective-permute-start.3) | collective-permute-done | bytes 131104 | tf_op jit(solution)/shard_map/ppermute | solution.py:282
  27.9 0.2 collective-permute-start.15
  28.1 0.0 collective-permute-done.4.refs_4_
  28.1 10.6 %collective-permute-start.16 = (bf16[512,128]{1,0:T(8,128)(2,1)S(1)}, bf16[512,128]{1,0:T(8,128)(2,1)S(1)}, u32[]{:S(2)}, u32[]{:S(2)}) collective-permute-start(bf16[512,128]{1,0:T(8,128)(2,1)S(1)} %get-tuple-element.59), channel_id=1, source_target_pairs={{0,5},{1,4},{2,7},{3,6},{4,1},{5,0},{6,3},{7,2},{8,13},{9,12},{10,... | collective-permute-start | bytes 393224 | tf_op jit(solution)/shard_map/ppermute | solution.py:282
  38.7 0.0 collective-permute-done.5.refs_5_
  38.7 0.3 collective-permute-start.17
  39.0 0.0 collective-permute-done.6.refs_6_
  39.0 0.0 copy-done.1
  39.0 4.2 %shard_map.79 = (bf16[512,128]{1,0:T(8,128)(2,1)S(1)}, bf16[512,128]{1,0:T(8,128)(2,1)S(1)}, bf16[512,128]{1,0:T(8,128)(2,1)S(1)}, bf16[512,128]{1,0:T(8,128)(2,...) custom-call(s32[2]{0:T(128)S(1)} %pad_add_fusion.where, ...), custom_call_target="tpu_custom_call", output_to_operand_aliasing={{0}: (9, {}), {1}: (10, {}), {2}: (11, {})} | custom-call | flops 1207959552 | bytes 9961480 | tf_op jit(solution)/shard_map/pallas_call | solution.py:257
  43.2 4.5 %collective-permute-start.18 = (bf16[512,128]{1,0:T(8,128)(2,1)S(1)}, bf16[512,128]{1,0:T(8,128)(2,1)S(1)}, u32[]{:S(2)}, u32[]{:S(2)}) collective-permute-start(bf16[512,128]{1,0:T(8,128)(2,1)S(1)} %get-tuple-element.61), channel_id=1, source_target_pairs={{0,7},{1,6},{2,5},{3,4},{4,3},{5,2},{6,1},{7,0},{8,15},{9,14},{10,... | collective-permute-start | bytes 393224 | tf_op jit(solution)/shard_map/ppermute | solution.py:282
  47.8 0.0 collective-permute-done.14.refs_0_
  47.8 0.0 collective-permute-start.19
  47.8 0.0 collective-permute-done.15.refs_1_
  47.8 2.0 %collective-permute-start.20 = (bf16[512,128]{1,0:T(8,128)(2,1)S(1)}, bf16[512,128]{1,0:T(8,128)(2,1)S(1)}, u32[]{:S(2)}, u32[]{:S(2)}) collective-permute-start(bf16[512,128]{1,0:T(8,128)(2,1)S(1)} %get-tuple-element.63), channel_id=1, source_target_pairs={{0,3},{1,2},{2,1},{3,0},{4,7},{5,6},{6,5},{7,4},{8,11},{9,10},{10,... | collective-permute-start | bytes 393224 | tf_op jit(solution)/shard_map/ppermute | solution.py:282
  49.8 0.0 collective-permute-done.16.refs_2_
  49.8 1.5 %collective-permute-start.7 = (bf16[512,128]{1,0:T(8,128)(2,1)S(1)}, bf16[512,128]{1,0:T(8,128)(2,1)S(1)}, u32[]{:S(2)}, u32[]{:S(2)}) collective-permute-start(bf16[512,128]{1,0:T(8,128)(2,1)S(1)} %get-tuple-element.49), channel_id=1, source_target_pairs={{0,1},{1,0},{2,3},{3,2},{4,5},{5,4},{6,7},{7,6},{8,9},{9,8},{10,11... | collective-permute-start | bytes 393224 | tf_op jit(solution)/shard_map/ppermute | solution.py:282
  51.3 0.0 collective-permute-done.17.refs_3_
  51.3 4.8 %collective-permute-start.8 = (bf16[512,128]{1,0:T(8,128)(2,1)S(1)}, bf16[512,128]{1,0:T(8,128)(2,1)S(1)}, u32[]{:S(2)}, u32[]{:S(2)}) collective-permute-start(bf16[512,128]{1,0:T(8,128)(2,1)S(1)} %get-tuple-element.50), channel_id=1, source_target_pairs={{0,4},{1,5},{2,6},{3,7},{4,0},{5,1},{6,2},{7,3},{8,12},{9,13},{10,... | collective-permute-start | bytes 393224 | tf_op jit(solution)/shard_map/ppermute | solution.py:282
  56.1 0.0 collective-permute-done.18.refs_4_
  56.1 2.0 %collective-permute-start.9 = (bf16[512,128]{1,0:T(8,128)(2,1)S(1)}, bf16[512,128]{1,0:T(8,128)(2,1)S(1)}, u32[]{:S(2)}, u32[]{:S(2)}) collective-permute-start(bf16[512,128]{1,0:T(8,128)(2,1)S(1)} %get-tuple-element.51), channel_id=1, source_target_pairs={{0,2},{1,3},{2,0},{3,1},{4,6},{5,7},{6,4},{7,5},{8,10},{9,11},{10,... | collective-permute-start | bytes 393224 | tf_op jit(solution)/shard_map/ppermute | solution.py:282
  58.1 0.0 collective-permute-done.19.refs_5_
  58.1 2.6 %collective-permute-start.10 = (bf16[512,128]{1,0:T(8,128)(2,1)S(1)}, bf16[512,128]{1,0:T(8,128)(2,1)S(1)}, u32[]{:S(2)}, u32[]{:S(2)}) collective-permute-start(bf16[512,128]{1,0:T(8,128)(2,1)S(1)} %get-tuple-element.52), channel_id=1, source_target_pairs={{0,5},{1,4},{2,7},{3,6},{4,1},{5,0},{6,3},{7,2},{8,13},{9,12},{10,... | collective-permute-start | bytes 393224 | tf_op jit(solution)/shard_map/ppermute | solution.py:282
  60.7 0.0 collective-permute-done.20.refs_6_
  60.7 1.1 %collective-permute-start.11 = (bf16[512,128]{1,0:T(8,128)(2,1)S(1)}, bf16[512,128]{1,0:T(8,128)(2,1)S(1)}, u32[]{:S(2)}, u32[]{:S(2)}) collective-permute-start(bf16[512,128]{1,0:T(8,128)(2,1)S(1)} %get-tuple-element.53), channel_id=1, source_target_pairs={{0,6},{1,7},{2,4},{3,5},{4,2},{5,3},{6,0},{7,1},{8,14},{9,15},{10,... | collective-permute-start | bytes 393224 | tf_op jit(solution)/shard_map/ppermute | solution.py:282
  61.9 4.1 %shard_map.80 = (bf16[512,256]{1,0:T(8,128)(2,1)S(1)}, bf16[512,256]{1,0:T(8,128)(2,1)S(1)}, bf16[512,256]{1,0:T(8,128)(2,1)S(1)}, bf16[512,256]{1,0:T(8,128)(2,1)S(1)}) custom-call(s32[2]{0:T(128)S(1)} %pad_add_fusion.where, bf16[512,128]{1,0:T(8,128)(2,1)S(1)} %collective-permute-done.14.refs_0_, bf16[512,128]{1,0:T(8,128)(2,1)S(1)} %collective-permute-done.15.refs_1_, ...), custom_call_target="tpu_custom_call" | custom-call | flops 1207959552 | bytes 6815752 | tf_op jit(solution)/shard_map/pallas_call | solution.py:257
  66.0 0.0 collective-permute-done.7.refs_0_
  66.0 1.6 %collective-permute-start.21 = (bf16[512,256]{1,0:T(8,128)(2,1)S(1)}, bf16[512,256]{1,0:T(8,128)(2,1)S(1)}, u32[]{:S(2)}, u32[]{:S(2)}) collective-permute-start(bf16[512,256]{1,0:T(8,128)(2,1)S(1)} %get-tuple-element.66), channel_id=1, source_target_pairs={{0,16},{8,24},{16,0},{24,8},{1,17},{9,25},{17,1},{25,9},{2,18},{10... | collective-permute-start | bytes 786440 | tf_op jit(solution)/shard_map/ppermute | solution.py:282
  67.5 0.0 collective-permute-done.8.refs_1_
  67.5 0.0 collective-permute-start.22
  67.5 0.0 collective-permute-done.9.refs_2_
  67.6 0.6 collective-permute-start.23
  68.2 2.3 %collective-permute-done.10.refs_3_ = bf16[512,128]{1,0:T(8,128)(2,1)S(1)} collective-permute-done((bf16[512,128]{1,0:T(8,128)(2,1)S(1)}, bf16[512,128]{1,0:T(8,128)(2,1)S(1)}, u32[]{:S(2)}, u32[]{:S(2)}) %collective-permute-start.10) | collective-permute-done | bytes 131104 | tf_op jit(solution)/shard_map/ppermute | solution.py:282
  70.5 3.3 %collective-permute-start.12 = (bf16[512,128]{1,0:T(8,128)(2,1)S(1)}, bf16[512,128]{1,0:T(8,128)(2,1)S(1)}, u32[]{:S(2)}, u32[]{:S(2)}) collective-permute-start(bf16[512,128]{1,0:T(8,128)(2,1)S(1)} %get-tuple-element.54), channel_id=1, source_target_pairs={{0,7},{1,6},{2,5},{3,4},{4,3},{5,2},{6,1},{7,0},{8,15},{9,14},{10,... | collective-permute-start | bytes 393224 | tf_op jit(solution)/shard_map/ppermute | solution.py:282
  73.8 0.0 collective-permute-done.11.refs_4_
  73.8 0.0 collective-permute-start.13
  73.8 5.1 %collective-permute-done.12.refs_5_ = bf16[512,128]{1,0:T(8,128)(2,1)S(1)} collective-permute-done((bf16[512,128]{1,0:T(8,128)(2,1)S(1)}, bf16[512,128]{1,0:T(8,128)(2,1)S(1)}, u32[]{:S(2)}, u32[]{:S(2)}) %collective-permute-start.12) | collective-permute-done | bytes 131104 | tf_op jit(solution)/shard_map/ppermute | solution.py:282
  78.9 1.4 %collective-permute-done.13.refs_6_ = bf16[512,128]{1,0:T(8,128)(2,1)S(1)} collective-permute-done((bf16[512,128]{1,0:T(8,128)(2,1)S(1)}, bf16[512,128]{1,0:T(8,128)(2,1)S(1)}, u32[]{:S(2)}, u32[]{:S(2)}) %collective-permute-start.13) | collective-permute-done | bytes 131104 | tf_op jit(solution)/shard_map/ppermute | solution.py:282
  80.3 0.0 collective-permute-done.21.refs_8_
  80.3 0.0 collective-permute-done.22.refs_9_
  80.3 0.0 collective-permute-done.23.refs_10_
  80.3 1.8 %shard_map.81 = (bf16[8,512,128]{2,1,0:T(8,128)(2,1)}, f32[512,256]{1,0:T(8,128)}) custom-call(s32[2]{0:T(128)S(1)} %pad_add_fusion.where, bf16[512,128]{1,0:T(8,128)(2,1)S(1)} %collective-permute-done.7.refs_0_, bf16[512,128]{1,0:T(8,128)(2,1)S(1)} %collective-permute-done.8.refs_1_, bf16[512,128]{1,0:T(8,128)(2,1)S(1)} %collective-permute-done.9.refs_2_, ...), custom_call_target="tpu_custom_call" | custom-call | bytes 3670024 | tf_op jit(solution)/shard_map/pallas_call | solution.py:257
Async XLA Ops:
  0.6 14.7 %copy-start = (bf16[9,256,256]{2,1,0:T(8,128)(2,1)S(1)}, bf16[9,256,256]{2,1,0:T(8,128)(2,1)}, u32[]{:S(2)}) copy-start(bf16[9,256,256]{2,1,0:T(8,128)(2,1)} %constant.12.clone.forward.refs_12_.refs_9_) | copy-start | bytes 3538948
  3.0 10.0 %collective-permute-start = (bf16[512,128]{1,0:T(8,128)(2,1)S(1)}, bf16[512,128]{1,0:T(8,128)(2,1)S(1)}, u32[]{:S(2)}, u32[]{:S(2)}) collective-permute-start(bf16[512,128]{1,0:T(8,128)(2,1)S(1)} %get-tuple-element.37), channel_id=1, source_target_pairs={{0,1},{1,0},{2,3},{3,2},{4,5},{5,4},{6,7},{7,6},{8,9},{9,8},{10,11... | collective-permute-start | bytes 393224 | tf_op jit(solution)/shard_map/ppermute | solution.py:282
  6.1 9.2 %collective-permute-start.1 = (bf16[512,128]{1,0:T(8,128)(2,1)S(1)}, bf16[512,128]{1,0:T(8,128)(2,1)S(1)}, u32[]{:S(2)}, u32[]{:S(2)}) collective-permute-start(bf16[512,128]{1,0:T(8,128)(2,1)S(1)} %get-tuple-element.38), channel_id=1, source_target_pairs={{0,2},{1,3},{2,0},{3,1},{4,6},{5,7},{6,4},{7,5},{8,10},{9,11},{10,... | collective-permute-start | bytes 393224 | tf_op jit(solution)/shard_map/ppermute | solution.py:282
  7.7 18.0 %collective-permute-start.2 = (bf16[512,128]{1,0:T(8,128)(2,1)S(1)}, bf16[512,128]{1,0:T(8,128)(2,1)S(1)}, u32[]{:S(2)}, u32[]{:S(2)}) collective-permute-start(bf16[512,128]{1,0:T(8,128)(2,1)S(1)} %get-tuple-element.39), channel_id=1, source_target_pairs={{0,4},{1,5},{2,6},{3,7},{4,0},{5,1},{6,2},{7,3},{8,12},{9,13},{10,... | collective-permute-start | bytes 393224 | tf_op jit(solution)/shard_map/ppermute | solution.py:282
  10.2 17.6 %collective-permute-start.3 = (bf16[512,128]{1,0:T(8,128)(2,1)S(1)}, bf16[512,128]{1,0:T(8,128)(2,1)S(1)}, u32[]{:S(2)}, u32[]{:S(2)}) collective-permute-start(bf16[512,128]{1,0:T(8,128)(2,1)S(1)} %get-tuple-element.40), channel_id=1, source_target_pairs={{0,5},{1,4},{2,7},{3,6},{4,1},{5,0},{6,3},{7,2},{8,13},{9,12},{10,... | collective-permute-start | bytes 393224 | tf_op jit(solution)/shard_map/ppermute | solution.py:282
  10.5 17.5 %collective-permute-start.4 = (bf16[512,128]{1,0:T(8,128)(2,1)S(1)}, bf16[512,128]{1,0:T(8,128)(2,1)S(1)}, u32[]{:S(2)}, u32[]{:S(2)}) collective-permute-start(bf16[512,128]{1,0:T(8,128)(2,1)S(1)} %get-tuple-element.41), channel_id=1, source_target_pairs={{0,6},{1,7},{2,4},{3,5},{4,2},{5,3},{6,0},{7,1},{8,14},{9,15},{10,... | collective-permute-start | bytes 393224 | tf_op jit(solution)/shard_map/ppermute | solution.py:282
  13.0 25.7 %collective-permute-start.5 = (bf16[512,128]{1,0:T(8,128)(2,1)S(1)}, bf16[512,128]{1,0:T(8,128)(2,1)S(1)}, u32[]{:S(2)}, u32[]{:S(2)}) collective-permute-start(bf16[512,128]{1,0:T(8,128)(2,1)S(1)} %get-tuple-element.42), channel_id=1, source_target_pairs={{0,7},{1,6},{2,5},{3,4},{4,3},{5,2},{6,1},{7,0},{8,15},{9,14},{10,... | collective-permute-start | bytes 393224 | tf_op jit(solution)/shard_map/ppermute | solution.py:282
  15.3 23.7 %collective-permute-start.6 = (bf16[512,128]{1,0:T(8,128)(2,1)S(1)}, bf16[512,128]{1,0:T(8,128)(2,1)S(1)}, u32[]{:S(2)}, u32[]{:S(2)}) collective-permute-start(bf16[512,128]{1,0:T(8,128)(2,1)S(1)} %get-tuple-element.43), channel_id=1, source_target_pairs={{0,3},{1,2},{2,1},{3,0},{4,7},{5,6},{6,5},{7,4},{8,11},{9,10},{10,... | collective-permute-start | bytes 393224 | tf_op jit(solution)/shard_map/ppermute | solution.py:282
  15.3 1.6 %copy-start.2 = (f32[512,1024]{1,0:T(8,128)S(1)}, f32[512,1024]{1,0:T(8,128)}, u32[]{:S(2)}) copy-start(f32[512,1024]{1,0:T(8,128)} %taps.1) | copy-start | bytes 6291460
  16.9 22.1 %copy-start.1 = (bf16[9,256,256]{2,1,0:T(8,128)(2,1)S(1)}, bf16[9,256,256]{2,1,0:T(8,128)(2,1)}, u32[]{:S(2)}) copy-start(bf16[9,256,256]{2,1,0:T(8,128)(2,1)} %constant.13.clone.refs_13_.refs_10_) | copy-start | bytes 3538948
  25.7 22.1 %collective-permute-start.14 = (bf16[512,128]{1,0:T(8,128)(2,1)S(1)}, bf16[512,128]{1,0:T(8,128)(2,1)S(1)}, u32[]{:S(2)}, u32[]{:S(2)}) collective-permute-start(bf16[512,128]{1,0:T(8,128)(2,1)S(1)} %get-tuple-element.57), channel_id=1, source_target_pairs={{0,1},{1,0},{2,3},{3,2},{4,5},{5,4},{6,7},{7,6},{8,9},{9,8},{10,11... | collective-permute-start | bytes 393224 | tf_op jit(solution)/shard_map/ppermute | solution.py:282
  27.9 19.9 %collective-permute-start.15 = (bf16[512,128]{1,0:T(8,128)(2,1)S(1)}, bf16[512,128]{1,0:T(8,128)(2,1)S(1)}, u32[]{:S(2)}, u32[]{:S(2)}) collective-permute-start(bf16[512,128]{1,0:T(8,128)(2,1)S(1)} %get-tuple-element.58), channel_id=1, source_target_pairs={{0,4},{1,5},{2,6},{3,7},{4,0},{5,1},{6,2},{7,3},{8,12},{9,13},{10,... | collective-permute-start | bytes 393224 | tf_op jit(solution)/shard_map/ppermute | solution.py:282
  28.1 21.7 %collective-permute-start.16 = (bf16[512,128]{1,0:T(8,128)(2,1)S(1)}, bf16[512,128]{1,0:T(8,128)(2,1)S(1)}, u32[]{:S(2)}, u32[]{:S(2)}) collective-permute-start(bf16[512,128]{1,0:T(8,128)(2,1)S(1)} %get-tuple-element.59), channel_id=1, source_target_pairs={{0,5},{1,4},{2,7},{3,6},{4,1},{5,0},{6,3},{7,2},{8,13},{9,12},{10,... | collective-permute-start | bytes 393224 | tf_op jit(solution)/shard_map/ppermute | solution.py:282
  38.7 12.6 %collective-permute-start.17 = (bf16[512,128]{1,0:T(8,128)(2,1)S(1)}, bf16[512,128]{1,0:T(8,128)(2,1)S(1)}, u32[]{:S(2)}, u32[]{:S(2)}) collective-permute-start(bf16[512,128]{1,0:T(8,128)(2,1)S(1)} %get-tuple-element.60), channel_id=1, source_target_pairs={{0,6},{1,7},{2,4},{3,5},{4,2},{5,3},{6,0},{7,1},{8,14},{9,15},{10,... | collective-permute-start | bytes 393224 | tf_op jit(solution)/shard_map/ppermute | solution.py:282
  43.2 12.8 %collective-permute-start.18 = (bf16[512,128]{1,0:T(8,128)(2,1)S(1)}, bf16[512,128]{1,0:T(8,128)(2,1)S(1)}, u32[]{:S(2)}, u32[]{:S(2)}) collective-permute-start(bf16[512,128]{1,0:T(8,128)(2,1)S(1)} %get-tuple-element.61), channel_id=1, source_target_pairs={{0,7},{1,6},{2,5},{3,4},{4,3},{5,2},{6,1},{7,0},{8,15},{9,14},{10,... | collective-permute-start | bytes 393224 | tf_op jit(solution)/shard_map/ppermute | solution.py:282
  47.8 10.3 %collective-permute-start.19 = (bf16[512,128]{1,0:T(8,128)(2,1)S(1)}, bf16[512,128]{1,0:T(8,128)(2,1)S(1)}, u32[]{:S(2)}, u32[]{:S(2)}) collective-permute-start(bf16[512,128]{1,0:T(8,128)(2,1)S(1)} %get-tuple-element.62), channel_id=1, source_target_pairs={{0,2},{1,3},{2,0},{3,1},{4,6},{5,7},{6,4},{7,5},{8,10},{9,11},{10,... | collective-permute-start | bytes 393224 | tf_op jit(solution)/shard_map/ppermute | solution.py:282
  47.8 12.9 %collective-permute-start.20 = (bf16[512,128]{1,0:T(8,128)(2,1)S(1)}, bf16[512,128]{1,0:T(8,128)(2,1)S(1)}, u32[]{:S(2)}, u32[]{:S(2)}) collective-permute-start(bf16[512,128]{1,0:T(8,128)(2,1)S(1)} %get-tuple-element.63), channel_id=1, source_target_pairs={{0,3},{1,2},{2,1},{3,0},{4,7},{5,6},{6,5},{7,4},{8,11},{9,10},{10,... | collective-permute-start | bytes 393224 | tf_op jit(solution)/shard_map/ppermute | solution.py:282
  49.8 16.2 %collective-permute-start.7 = (bf16[512,128]{1,0:T(8,128)(2,1)S(1)}, bf16[512,128]{1,0:T(8,128)(2,1)S(1)}, u32[]{:S(2)}, u32[]{:S(2)}) collective-permute-start(bf16[512,128]{1,0:T(8,128)(2,1)S(1)} %get-tuple-element.49), channel_id=1, source_target_pairs={{0,1},{1,0},{2,3},{3,2},{4,5},{5,4},{6,7},{7,6},{8,9},{9,8},{10,11... | collective-permute-start | bytes 393224 | tf_op jit(solution)/shard_map/ppermute | solution.py:282
  51.3 16.3 %collective-permute-start.8 = (bf16[512,128]{1,0:T(8,128)(2,1)S(1)}, bf16[512,128]{1,0:T(8,128)(2,1)S(1)}, u32[]{:S(2)}, u32[]{:S(2)}) collective-permute-start(bf16[512,128]{1,0:T(8,128)(2,1)S(1)} %get-tuple-element.50), channel_id=1, source_target_pairs={{0,4},{1,5},{2,6},{3,7},{4,0},{5,1},{6,2},{7,3},{8,12},{9,13},{10,... | collective-permute-start | bytes 393224 | tf_op jit(solution)/shard_map/ppermute | solution.py:282
  56.1 11.5 %collective-permute-start.9 = (bf16[512,128]{1,0:T(8,128)(2,1)S(1)}, bf16[512,128]{1,0:T(8,128)(2,1)S(1)}, u32[]{:S(2)}, u32[]{:S(2)}) collective-permute-start(bf16[512,128]{1,0:T(8,128)(2,1)S(1)} %get-tuple-element.51), channel_id=1, source_target_pairs={{0,2},{1,3},{2,0},{3,1},{4,6},{5,7},{6,4},{7,5},{8,10},{9,11},{10,... | collective-permute-start | bytes 393224 | tf_op jit(solution)/shard_map/ppermute | solution.py:282
  58.1 12.4 %collective-permute-start.10 = (bf16[512,128]{1,0:T(8,128)(2,1)S(1)}, bf16[512,128]{1,0:T(8,128)(2,1)S(1)}, u32[]{:S(2)}, u32[]{:S(2)}) collective-permute-start(bf16[512,128]{1,0:T(8,128)(2,1)S(1)} %get-tuple-element.52), channel_id=1, source_target_pairs={{0,5},{1,4},{2,7},{3,6},{4,1},{5,0},{6,3},{7,2},{8,13},{9,12},{10,... | collective-permute-start | bytes 393224 | tf_op jit(solution)/shard_map/ppermute | solution.py:282
  60.7 13.0 %collective-permute-start.11 = (bf16[512,128]{1,0:T(8,128)(2,1)S(1)}, bf16[512,128]{1,0:T(8,128)(2,1)S(1)}, u32[]{:S(2)}, u32[]{:S(2)}) collective-permute-start(bf16[512,128]{1,0:T(8,128)(2,1)S(1)} %get-tuple-element.53), channel_id=1, source_target_pairs={{0,6},{1,7},{2,4},{3,5},{4,2},{5,3},{6,0},{7,1},{8,14},{9,15},{10,... | collective-permute-start | bytes 393224 | tf_op jit(solution)/shard_map/ppermute | solution.py:282
  66.0 14.3 %collective-permute-start.21 = (bf16[512,256]{1,0:T(8,128)(2,1)S(1)}, bf16[512,256]{1,0:T(8,128)(2,1)S(1)}, u32[]{:S(2)}, u32[]{:S(2)}) collective-permute-start(bf16[512,256]{1,0:T(8,128)(2,1)S(1)} %get-tuple-element.66), channel_id=1, source_target_pairs={{0,16},{8,24},{16,0},{24,8},{1,17},{9,25},{17,1},{25,9},{2,18},{10... | collective-permute-start | bytes 786440 | tf_op jit(solution)/shard_map/ppermute | solution.py:282
  67.5 12.7 %collective-permute-start.22 = (bf16[512,256]{1,0:T(8,128)(2,1)S(1)}, bf16[512,256]{1,0:T(8,128)(2,1)S(1)}, u32[]{:S(2)}, u32[]{:S(2)}) collective-permute-start(bf16[512,256]{1,0:T(8,128)(2,1)S(1)} %get-tuple-element.67), channel_id=1, source_target_pairs={{0,24},{8,16},{16,8},{24,0},{1,25},{9,17},{17,9},{25,1},{2,26},{10... | collective-permute-start | bytes 786440 | tf_op jit(solution)/shard_map/ppermute | solution.py:282
  67.6 12.7 %collective-permute-start.23 = (bf16[512,256]{1,0:T(8,128)(2,1)S(1)}, bf16[512,256]{1,0:T(8,128)(2,1)S(1)}, u32[]{:S(2)}, u32[]{:S(2)}) collective-permute-start(bf16[512,256]{1,0:T(8,128)(2,1)S(1)} %get-tuple-element.68), channel_id=1, source_target_pairs={{0,8},{8,0},{16,24},{24,16},{1,9},{9,1},{17,25},{25,17},{2,10},{10... | collective-permute-start | bytes 786440 | tf_op jit(solution)/shard_map/ppermute | solution.py:282
  70.5 8.4 %collective-permute-start.12 = (bf16[512,128]{1,0:T(8,128)(2,1)S(1)}, bf16[512,128]{1,0:T(8,128)(2,1)S(1)}, u32[]{:S(2)}, u32[]{:S(2)}) collective-permute-start(bf16[512,128]{1,0:T(8,128)(2,1)S(1)} %get-tuple-element.54), channel_id=1, source_target_pairs={{0,7},{1,6},{2,5},{3,4},{4,3},{5,2},{6,1},{7,0},{8,15},{9,14},{10,... | collective-permute-start | bytes 393224 | tf_op jit(solution)/shard_map/ppermute | solution.py:282
  73.8 6.5 %collective-permute-start.13 = (bf16[512,128]{1,0:T(8,128)(2,1)S(1)}, bf16[512,128]{1,0:T(8,128)(2,1)S(1)}, u32[]{:S(2)}, u32[]{:S(2)}) collective-permute-start(bf16[512,128]{1,0:T(8,128)(2,1)S(1)} %get-tuple-element.55), channel_id=1, source_target_pairs={{0,3},{1,2},{2,1},{3,0},{4,7},{5,6},{6,5},{7,4},{8,11},{9,10},{10,... | collective-permute-start | bytes 393224 | tf_op jit(solution)/shard_map/ppermute | solution.py:282

commit v22 on v20

--- a/solution.py
+++ b/solution.py
@@ -300,18 +300,20 @@
     held = pltpu.VMEM((rows, length), half)
     mid = pltpu.VMEM((GROUPS, rows, 2 * width), half)
     wide = pltpu.VMEM((GROUPS, rows, 2 * width), full)
-    slots = pltpu.VMEM((count, rows, span), half)
     sems = pltpu.SemaphoreType.DMA
     work = 2 * GROUPS * rows * 4 * width * width
 
     stay = [pltpu.with_memory_space_constraint(x[0], pltpu.HBM) for x in (out_gate, grad_out, saved_input)]
-    grad_pieces = call(
-        functools.partial(gate_kernel, grad_order),
-        [where, *stay[:2]],
-        [piece] * count,
-        [slots, slots, sems((2, count))],
-        hbm=(1, 2),
-    )
+    grad_pieces, cut = [], 1 * count // 8
+    for some in (grad_order[:cut], grad_order[cut:]):
+        held_some = pltpu.VMEM((len(some), rows, span), half)
+        grad_pieces += call(
+            functools.partial(gate_kernel, some),
+            [where, *stay[:2]],
+            [piece] * len(some),
+            [held_some, held_some, sems((2, len(some)))],
+            hbm=(1, 2),
+        )
     grad_blocks = exchange(grad_pieces, grad_order, "ctx", count)
     *input_pieces, taps_spec = call(
         functools.partial(taps_kernel, input_order),

time: 81.2 us -> 82.4 us (1.015)
  waiting for transfers between devices: 18.1 us -> 20.3 us
  Pallas kernels: 14.6 us -> 16.3 us
  local copies, waits for them, and re-layouts: 1.6 us -> 0.01 us
  starting transfers between devices: 46 us -> 44.8 us
    ppermute x24, waiting for transfers between devices: 18.1 us -> 20.3 us  [exchange(): lax.ppermute(piece, axis, [(i, i ^ k) for i in range(size)])]
    pallas_call x5 -> x6, Pallas kernels: 14.6 us -> 16.3 us  [call(): pl.pallas_call(kernel, out_shape=list(outs), in_specs=specs, out_specs=[s...]
    unnamed x6, local copies, waits for them, and re-layouts: 1.6 us -> 0.01 us
    ppermute x24, starting transfers between devices: 46 us -> 44.8 us  [exchange(): lax.ppermute(piece, axis, [(i, i ^ k) for i in range(size)])]
  transfers between devices with their start and end apart: 24 -> 24, of which waited for: 6 -> 6; matrix products, arithmetic and copies ran while one was open for 0% -> 0% of each run, Pallas kernels for 13% -> 15%
where the time goes in v22:
time: 82.4 us; the launch traced here: 82.3 us
  starting transfers between devices  44.8 us (54%)
  waiting for transfers between devices  20.3 us (25%)
  Pallas kernels  16.3 us (20%)
    ppermute x24, starting transfers between devices, exchange(): lax.ppermute(piece, axis, [(i, i ^ k) for i in range(size)])  44.8 us
    ppermute x24, waiting for transfers between devices, exchange(): lax.ppermute(piece, axis, [(i, i ^ k) for i in range(size)])  20.3 us
    pallas_call x6, Pallas kernels, call(): pl.pallas_call(kernel, out_shape=list(outs), in_specs=specs, out_specs=[s...  16.3 us
  transfers between devices with their start and end apart: 24, of which 6 were waited for; matrix products, arithmetic and copies ran while one was open for 0% of the time, Pallas kernels for 15%

profile of v22, /device:TPU:0, one launch (start us, length us, event | category | flops | bytes accessed | tf_op | source)
XLA Modules:
  0.0 82.3 jit_solution(10155822509667701685)
XLA Ops:
  0.6 0.1 pad_add_fusion.where
  0.7 0.0 copy-start
  0.7 0.0 copy-start.2
  0.7 1.8 %shard_map.77 = bf16[512,128]{1,0:T(8,128)(2,1)S(1)} custom-call(s32[2]{0:T(128)S(1)} %pad_add_fusion.where, bf16[4096,128]{1,0:T(8,128)(2,1)} %bitcast.6, bf16[4096,128]{1,0:T(8,128)(2,1)} %bitcast.8), custom_call_target="tpu_custom_call" | custom-call | bytes 2228232 | tf_op jit(solution)/shard_map/pallas_call | solution.py:257
  2.5 4.1 %collective-permute-start = (bf16[512,128]{1,0:T(8,128)(2,1)S(1)}, bf16[512,128]{1,0:T(8,128)(2,1)S(1)}, u32[]{:S(2)}, u32[]{:S(2)}) collective-permute-start(bf16[512,128]{1,0:T(8,128)(2,1)S(1)} %shard_map.77), channel_id=1, source_target_pairs={{0,4},{1,5},{2,6},{3,7},{4,0},{5,1},{6,2},{7,3},{8,12},{9,13},{10,... | collective-permute-start | bytes 393224 | tf_op jit(solution)/shard_map/ppermute | solution.py:282
  6.7 2.2 %shard_map.78 = (bf16[512,128]{1,0:T(8,128)(2,1)S(1)}, bf16[512,128]{1,0:T(8,128)(2,1)S(1)}, bf16[512,128]{1,0:T(8,128)(2,1)S(1)}, bf16[512,128]{1,0:T(8,128)(2,...) custom-call(s32[2]{0:T(128)S(1)} %pad_add_fusion.where, ...), custom_call_target="tpu_custom_call" | custom-call | bytes 3014664 | tf_op jit(solution)/shard_map/pallas_call | solution.py:257
  8.9 1.6 %collective-permute-start.1 = (bf16[512,128]{1,0:T(8,128)(2,1)S(1)}, bf16[512,128]{1,0:T(8,128)(2,1)S(1)}, u32[]{:S(2)}, u32[]{:S(2)}) collective-permute-start(bf16[512,128]{1,0:T(8,128)(2,1)S(1)} %get-tuple-element.36), channel_id=1, source_target_pairs={{0,1},{1,0},{2,3},{3,2},{4,5},{5,4},{6,7},{7,6},{8,9},{9,8},{10,11... | collective-permute-start | bytes 393224 | tf_op jit(solution)/shard_map/ppermute | solution.py:282
  10.5 0.0 collective-permute-start.2
  10.5 1.9 %collective-permute-start.3 = (bf16[512,128]{1,0:T(8,128)(2,1)S(1)}, bf16[512,128]{1,0:T(8,128)(2,1)S(1)}, u32[]{:S(2)}, u32[]{:S(2)}) collective-permute-start(bf16[512,128]{1,0:T(8,128)(2,1)S(1)} %get-tuple-element.38), channel_id=1, source_target_pairs={{0,2},{1,3},{2,0},{3,1},{4,6},{5,7},{6,4},{7,5},{8,10},{9,11},{10,... | collective-permute-start | bytes 393224 | tf_op jit(solution)/shard_map/ppermute | solution.py:282
  12.3 2.5 %collective-permute-start.4 = (bf16[512,128]{1,0:T(8,128)(2,1)S(1)}, bf16[512,128]{1,0:T(8,128)(2,1)S(1)}, u32[]{:S(2)}, u32[]{:S(2)}) collective-permute-start(bf16[512,128]{1,0:T(8,128)(2,1)S(1)} %get-tuple-element.39), channel_id=1, source_target_pairs={{0,6},{1,7},{2,4},{3,5},{4,2},{5,3},{6,0},{7,1},{8,14},{9,15},{10,... | collective-permute-start | bytes 393224 | tf_op jit(solution)/shard_map/ppermute | solution.py:282
  14.8 0.0 collective-permute-done.refs_0_
  14.8 6.6 %collective-permute-start.5 = (bf16[512,128]{1,0:T(8,128)(2,1)S(1)}, bf16[512,128]{1,0:T(8,128)(2,1)S(1)}, u32[]{:S(2)}, u32[]{:S(2)}) collective-permute-start(bf16[512,128]{1,0:T(8,128)(2,1)S(1)} %get-tuple-element.40), channel_id=1, source_target_pairs={{0,7},{1,6},{2,5},{3,4},{4,3},{5,2},{6,1},{7,0},{8,15},{9,14},{10,... | collective-permute-start | bytes 393224 | tf_op jit(solution)/shard_map/ppermute | solution.py:282
  21.4 0.0 collective-permute-done.1.refs_1_
  21.4 0.0 collective-permute-start.6
  21.5 0.0 copy-done
  21.5 0.0 copy-done.2
  21.5 0.0 copy-start.1
  21.5 2.1 %shard_map.79 = (bf16[512,128]{1,0:T(8,128)(2,1)S(1)}, bf16[512,128]{1,0:T(8,128)(2,1)S(1)}, bf16[512,128]{1,0:T(8,128)(2,1)S(1)}, bf16[512,128]{1,0:T(8,128)(2,...) custom-call(s32[2]{0:T(128)S(1)} %pad_add_fusion.where, ...), custom_call_target="tpu_custom_call" | custom-call | flops 603979776 | bytes 7733256 | tf_op jit(solution)/shard_map/pallas_call | solution.py:257
  23.6 1.5 %collective-permute-done.2.refs_2_ = bf16[512,128]{1,0:T(8,128)(2,1)S(1)} collective-permute-done((bf16[512,128]{1,0:T(8,128)(2,1)S(1)}, bf16[512,128]{1,0:T(8,128)(2,1)S(1)}, u32[]{:S(2)}, u32[]{:S(2)}) %collective-permute-start.2) | collective-permute-done | bytes 131104 | tf_op jit(solution)/shard_map/ppermute | solution.py:282
  25.1 0.0 collective-permute-start.14
  25.1 0.0 collective-permute-done.3.refs_3_
  25.1 4.0 %collective-permute-start.15 = (bf16[512,128]{1,0:T(8,128)(2,1)S(1)}, bf16[512,128]{1,0:T(8,128)(2,1)S(1)}, u32[]{:S(2)}, u32[]{:S(2)}) collective-permute-start(bf16[512,128]{1,0:T(8,128)(2,1)S(1)} %get-tuple-element.56), channel_id=1, source_target_pairs={{0,5},{1,4},{2,7},{3,6},{4,1},{5,0},{6,3},{7,2},{8,13},{9,12},{10,... | collective-permute-start | bytes 393224 | tf_op jit(solution)/shard_map/ppermute | solution.py:282
  29.1 0.0 collective-permute-done.4.refs_4_
  29.1 1.1 %collective-permute-start.16 = (bf16[512,128]{1,0:T(8,128)(2,1)S(1)}, bf16[512,128]{1,0:T(8,128)(2,1)S(1)}, u32[]{:S(2)}, u32[]{:S(2)}) collective-permute-start(bf16[512,128]{1,0:T(8,128)(2,1)S(1)} %get-tuple-element.57), channel_id=1, source_target_pairs={{0,6},{1,7},{2,4},{3,5},{4,2},{5,3},{6,0},{7,1},{8,14},{9,15},{10,... | collective-permute-start | bytes 393224 | tf_op jit(solution)/shard_map/ppermute | solution.py:282
  30.2 0.0 collective-permute-done.5.refs_5_
  30.2 2.3 %collective-permute-start.17 = (bf16[512,128]{1,0:T(8,128)(2,1)S(1)}, bf16[512,128]{1,0:T(8,128)(2,1)S(1)}, u32[]{:S(2)}, u32[]{:S(2)}) collective-permute-start(bf16[512,128]{1,0:T(8,128)(2,1)S(1)} %get-tuple-element.58), channel_id=1, source_target_pairs={{0,1},{1,0},{2,3},{3,2},{4,5},{5,4},{6,7},{7,6},{8,9},{9,8},{10,11... | collective-permute-start | bytes 393224 | tf_op jit(solution)/shard_map/ppermute | solution.py:282
  32.6 0.0 collective-permute-done.6.refs_6_
  32.6 0.0 copy-done.1
  32.6 4.2 %shard_map.80 = (bf16[512,128]{1,0:T(8,128)(2,1)S(1)}, bf16[512,128]{1,0:T(8,128)(2,1)S(1)}, bf16[512,128]{1,0:T(8,128)(2,1)S(1)}, bf16[512,128]{1,0:T(8,128)(2,...) custom-call(s32[2]{0:T(128)S(1)} %pad_add_fusion.where, ...), custom_call_target="tpu_custom_call", output_to_operand_aliasing={{0}: (9, {}), {1}: (10, {}), {2}: (11, {})} | custom-call | flops 1207959552 | bytes 9961480 | tf_op jit(solution)/shard_map/pallas_call | solution.py:257
  36.8 1.9 %collective-permute-start.18 = (bf16[512,128]{1,0:T(8,128)(2,1)S(1)}, bf16[512,128]{1,0:T(8,128)(2,1)S(1)}, u32[]{:S(2)}, u32[]{:S(2)}) collective-permute-start(bf16[512,128]{1,0:T(8,128)(2,1)S(1)} %get-tuple-element.59), channel_id=1, source_target_pairs={{0,7},{1,6},{2,5},{3,4},{4,3},{5,2},{6,1},{7,0},{8,15},{9,14},{10,... | collective-permute-start | bytes 393224 | tf_op jit(solution)/shard_map/ppermute | solution.py:282
  38.7 6.5 %collective-permute-done.14.refs_0_ = bf16[512,128]{1,0:T(8,128)(2,1)S(1)} collective-permute-done((bf16[512,128]{1,0:T(8,128)(2,1)S(1)}, bf16[512,128]{1,0:T(8,128)(2,1)S(1)}, u32[]{:S(2)}, u32[]{:S(2)}) %collective-permute-start.14) | collective-permute-done | bytes 131104 | tf_op jit(solution)/shard_map/ppermute | solution.py:282
  45.2 5.8 %collective-permute-start.19 = (bf16[512,128]{1,0:T(8,128)(2,1)S(1)}, bf16[512,128]{1,0:T(8,128)(2,1)S(1)}, u32[]{:S(2)}, u32[]{:S(2)}) collective-permute-start(bf16[512,128]{1,0:T(8,128)(2,1)S(1)} %get-tuple-element.60), channel_id=1, source_target_pairs={{0,2},{1,3},{2,0},{3,1},{4,6},{5,7},{6,4},{7,5},{8,10},{9,11},{10,... | collective-permute-start | bytes 393224 | tf_op jit(solution)/shard_map/ppermute | solution.py:282
  51.1 0.0 collective-permute-done.15.refs_1_
  51.1 0.0 collective-permute-start.20
  51.1 0.0 collective-permute-done.16.refs_2_
  51.1 1.5 %collective-permute-start.7 = (bf16[512,128]{1,0:T(8,128)(2,1)S(1)}, bf16[512,128]{1,0:T(8,128)(2,1)S(1)}, u32[]{:S(2)}, u32[]{:S(2)}) collective-permute-start(bf16[512,128]{1,0:T(8,128)(2,1)S(1)} %get-tuple-element.47), channel_id=1, source_target_pairs={{0,1},{1,0},{2,3},{3,2},{4,5},{5,4},{6,7},{7,6},{8,9},{9,8},{10,11... | collective-permute-start | bytes 393224 | tf_op jit(solution)/shard_map/ppermute | solution.py:282
  52.6 0.0 collective-permute-done.17.refs_3_
  52.6 1.1 %collective-permute-start.8 = (bf16[512,128]{1,0:T(8,128)(2,1)S(1)}, bf16[512,128]{1,0:T(8,128)(2,1)S(1)}, u32[]{:S(2)}, u32[]{:S(2)}) collective-permute-start(bf16[512,128]{1,0:T(8,128)(2,1)S(1)} %get-tuple-element.48), channel_id=1, source_target_pairs={{0,4},{1,5},{2,6},{3,7},{4,0},{5,1},{6,2},{7,3},{8,12},{9,13},{10,... | collective-permute-start | bytes 393224 | tf_op jit(solution)/shard_map/ppermute | solution.py:282
  53.7 0.0 collective-permute-done.18.refs_4_
  53.7 1.4 %collective-permute-start.9 = (bf16[512,128]{1,0:T(8,128)(2,1)S(1)}, bf16[512,128]{1,0:T(8,128)(2,1)S(1)}, u32[]{:S(2)}, u32[]{:S(2)}) collective-permute-start(bf16[512,128]{1,0:T(8,128)(2,1)S(1)} %get-tuple-element.49), channel_id=1, source_target_pairs={{0,2},{1,3},{2,0},{3,1},{4,6},{5,7},{6,4},{7,5},{8,10},{9,11},{10,... | collective-permute-start | bytes 393224 | tf_op jit(solution)/shard_map/ppermute | solution.py:282
  55.1 0.0 collective-permute-done.19.refs_5_
  55.1 2.9 %collective-permute-start.10 = (bf16[512,128]{1,0:T(8,128)(2,1)S(1)}, bf16[512,128]{1,0:T(8,128)(2,1)S(1)}, u32[]{:S(2)}, u32[]{:S(2)}) collective-permute-start(bf16[512,128]{1,0:T(8,128)(2,1)S(1)} %get-tuple-element.50), channel_id=1, source_target_pairs={{0,5},{1,4},{2,7},{3,6},{4,1},{5,0},{6,3},{7,2},{8,13},{9,12},{10,... | collective-permute-start | bytes 393224 | tf_op jit(solution)/shard_map/ppermute | solution.py:282
  58.0 3.1 %collective-permute-done.20.refs_6_ = bf16[512,128]{1,0:T(8,128)(2,1)S(1)} collective-permute-done((bf16[512,128]{1,0:T(8,128)(2,1)S(1)}, bf16[512,128]{1,0:T(8,128)(2,1)S(1)}, u32[]{:S(2)}, u32[]{:S(2)}) %collective-permute-start.20) | collective-permute-done | bytes 131104 | tf_op jit(solution)/shard_map/ppermute | solution.py:282
  61.1 0.0 collective-permute-start.11
  61.1 4.1 %shard_map.81 = (bf16[512,256]{1,0:T(8,128)(2,1)S(1)}, bf16[512,256]{1,0:T(8,128)(2,1)S(1)}, bf16[512,256]{1,0:T(8,128)(2,1)S(1)}, bf16[512,256]{1,0:T(8,128)(2,1)S(1)}) custom-call(s32[2]{0:T(128)S(1)} %pad_add_fusion.where, bf16[512,128]{1,0:T(8,128)(2,1)S(1)} %collective-permute-done.14.refs_0_, bf16[512,128]{1,0:T(8,128)(2,1)S(1)} %collective-permute-done.15.refs_1_, ...), custom_call_target="tpu_custom_call" | custom-call | flops 1207959552 | bytes 6815752 | tf_op jit(solution)/shard_map/pallas_call | solution.py:257
  65.2 0.0 collective-permute-done.7.refs_0_
  65.2 2.3 %collective-permute-start.21 = (bf16[512,256]{1,0:T(8,128)(2,1)S(1)}, bf16[512,256]{1,0:T(8,128)(2,1)S(1)}, u32[]{:S(2)}, u32[]{:S(2)}) collective-permute-start(bf16[512,256]{1,0:T(8,128)(2,1)S(1)} %get-tuple-element.64), channel_id=1, source_target_pairs={{0,16},{8,24},{16,0},{24,8},{1,17},{9,25},{17,1},{25,9},{2,18},{10... | collective-permute-start | bytes 786440 | tf_op jit(solution)/shard_map/ppermute | solution.py:282
  67.6 0.0 collective-permute-done.8.refs_1_
  67.6 0.0 collective-permute-start.22
  67.6 0.0 collective-permute-done.9.refs_2_
  67.6 0.2 collective-permute-start.23
  67.8 1.8 %collective-permute-done.10.refs_3_ = bf16[512,128]{1,0:T(8,128)(2,1)S(1)} collective-permute-done((bf16[512,128]{1,0:T(8,128)(2,1)S(1)}, bf16[512,128]{1,0:T(8,128)(2,1)S(1)}, u32[]{:S(2)}, u32[]{:S(2)}) %collective-permute-start.10) | collective-permute-done | bytes 131104 | tf_op jit(solution)/shard_map/ppermute | solution.py:282
  69.6 3.5 %collective-permute-start.12 = (bf16[512,128]{1,0:T(8,128)(2,1)S(1)}, bf16[512,128]{1,0:T(8,128)(2,1)S(1)}, u32[]{:S(2)}, u32[]{:S(2)}) collective-permute-start(bf16[512,128]{1,0:T(8,128)(2,1)S(1)} %get-tuple-element.52), channel_id=1, source_target_pairs={{0,7},{1,6},{2,5},{3,4},{4,3},{5,2},{6,1},{7,0},{8,15},{9,14},{10,... | collective-permute-start | bytes 393224 | tf_op jit(solution)/shard_map/ppermute | solution.py:282
  73.1 0.0 collective-permute-done.11.refs_4_
  73.1 0.0 collective-permute-start.13
  73.1 5.4 %collective-permute-done.12.refs_5_ = bf16[512,128]{1,0:T(8,128)(2,1)S(1)} collective-permute-done((bf16[512,128]{1,0:T(8,128)(2,1)S(1)}, bf16[512,128]{1,0:T(8,128)(2,1)S(1)}, u32[]{:S(2)}, u32[]{:S(2)}) %collective-permute-start.12) | collective-permute-done | bytes 131104 | tf_op jit(solution)/shard_map/ppermute | solution.py:282
  78.5 1.9 %collective-permute-done.13.refs_6_ = bf16[512,128]{1,0:T(8,128)(2,1)S(1)} collective-permute-done((bf16[512,128]{1,0:T(8,128)(2,1)S(1)}, bf16[512,128]{1,0:T(8,128)(2,1)S(1)}, u32[]{:S(2)}, u32[]{:S(2)}) %collective-permute-start.13) | collective-permute-done | bytes 131104 | tf_op jit(solution)/shard_map/ppermute | solution.py:282
  80.4 0.0 collective-permute-done.21.refs_8_
  80.5 0.0 collective-permute-done.22.refs_9_
  80.5 0.0 collective-permute-done.23.refs_10_
  80.5 1.8 %shard_map.82 = (bf16[8,512,128]{2,1,0:T(8,128)(2,1)}, f32[512,256]{1,0:T(8,128)}) custom-call(s32[2]{0:T(128)S(1)} %pad_add_fusion.where, bf16[512,128]{1,0:T(8,128)(2,1)S(1)} %collective-permute-done.7.refs_0_, bf16[512,128]{1,0:T(8,128)(2,1)S(1)} %collective-permute-done.8.refs_1_, bf16[512,128]{1,0:T(8,128)(2,1)S(1)} %collective-permute-done.9.refs_2_, ...), custom_call_target="tpu_custom_call" | custom-call | bytes 3670024 | tf_op jit(solution)/shard_map/pallas_call | solution.py:257
Async XLA Ops:
  0.7 20.7 %copy-start = (bf16[9,256,256]{2,1,0:T(8,128)(2,1)S(1)}, bf16[9,256,256]{2,1,0:T(8,128)(2,1)}, u32[]{:S(2)}) copy-start(bf16[9,256,256]{2,1,0:T(8,128)(2,1)} %constant.12.clone.forward.refs_12_.refs_9_) | copy-start | bytes 3538948
  0.7 20.7 %copy-start.2 = (f32[512,1024]{1,0:T(8,128)S(1)}, f32[512,1024]{1,0:T(8,128)}, u32[]{:S(2)}) copy-start(f32[512,1024]{1,0:T(8,128)} %taps.1) | copy-start | bytes 6291460
  2.5 12.2 %collective-permute-start = (bf16[512,128]{1,0:T(8,128)(2,1)S(1)}, bf16[512,128]{1,0:T(8,128)(2,1)S(1)}, u32[]{:S(2)}, u32[]{:S(2)}) collective-permute-start(bf16[512,128]{1,0:T(8,128)(2,1)S(1)} %shard_map.77), channel_id=1, source_target_pairs={{0,4},{1,5},{2,6},{3,7},{4,0},{5,1},{6,2},{7,3},{8,12},{9,13},{10,... | collective-permute-start | bytes 393224 | tf_op jit(solution)/shard_map/ppermute | solution.py:282
  8.9 12.6 %collective-permute-start.1 = (bf16[512,128]{1,0:T(8,128)(2,1)S(1)}, bf16[512,128]{1,0:T(8,128)(2,1)S(1)}, u32[]{:S(2)}, u32[]{:S(2)}) collective-permute-start(bf16[512,128]{1,0:T(8,128)(2,1)S(1)} %get-tuple-element.36), channel_id=1, source_target_pairs={{0,1},{1,0},{2,3},{3,2},{4,5},{5,4},{6,7},{7,6},{8,9},{9,8},{10,11... | collective-permute-start | bytes 393224 | tf_op jit(solution)/shard_map/ppermute | solution.py:282
  10.5 14.6 %collective-permute-start.2 = (bf16[512,128]{1,0:T(8,128)(2,1)S(1)}, bf16[512,128]{1,0:T(8,128)(2,1)S(1)}, u32[]{:S(2)}, u32[]{:S(2)}) collective-permute-start(bf16[512,128]{1,0:T(8,128)(2,1)S(1)} %get-tuple-element.37), channel_id=1, source_target_pairs={{0,5},{1,4},{2,7},{3,6},{4,1},{5,0},{6,3},{7,2},{8,13},{9,12},{10,... | collective-permute-start | bytes 393224 | tf_op jit(solution)/shard_map/ppermute | solution.py:282
  10.5 14.6 %collective-permute-start.3 = (bf16[512,128]{1,0:T(8,128)(2,1)S(1)}, bf16[512,128]{1,0:T(8,128)(2,1)S(1)}, u32[]{:S(2)}, u32[]{:S(2)}) collective-permute-start(bf16[512,128]{1,0:T(8,128)(2,1)S(1)} %get-tuple-element.38), channel_id=1, source_target_pairs={{0,2},{1,3},{2,0},{3,1},{4,6},{5,7},{6,4},{7,5},{8,10},{9,11},{10,... | collective-permute-start | bytes 393224 | tf_op jit(solution)/shard_map/ppermute | solution.py:282
  12.3 16.8 %collective-permute-start.4 = (bf16[512,128]{1,0:T(8,128)(2,1)S(1)}, bf16[512,128]{1,0:T(8,128)(2,1)S(1)}, u32[]{:S(2)}, u32[]{:S(2)}) collective-permute-start(bf16[512,128]{1,0:T(8,128)(2,1)S(1)} %get-tuple-element.39), channel_id=1, source_target_pairs={{0,6},{1,7},{2,4},{3,5},{4,2},{5,3},{6,0},{7,1},{8,14},{9,15},{10,... | collective-permute-start | bytes 393224 | tf_op jit(solution)/shard_map/ppermute | solution.py:282
  14.8 15.4 %collective-permute-start.5 = (bf16[512,128]{1,0:T(8,128)(2,1)S(1)}, bf16[512,128]{1,0:T(8,128)(2,1)S(1)}, u32[]{:S(2)}, u32[]{:S(2)}) collective-permute-start(bf16[512,128]{1,0:T(8,128)(2,1)S(1)} %get-tuple-element.40), channel_id=1, source_target_pairs={{0,7},{1,6},{2,5},{3,4},{4,3},{5,2},{6,1},{7,0},{8,15},{9,14},{10,... | collective-permute-start | bytes 393224 | tf_op jit(solution)/shard_map/ppermute | solution.py:282
  21.4 11.1 %collective-permute-start.6 = (bf16[512,128]{1,0:T(8,128)(2,1)S(1)}, bf16[512,128]{1,0:T(8,128)(2,1)S(1)}, u32[]{:S(2)}, u32[]{:S(2)}) collective-permute-start(bf16[512,128]{1,0:T(8,128)(2,1)S(1)} %get-tuple-element.41), channel_id=1, source_target_pairs={{0,3},{1,2},{2,1},{3,0},{4,7},{5,6},{6,5},{7,4},{8,11},{9,10},{10,... | collective-permute-start | bytes 393224 | tf_op jit(solution)/shard_map/ppermute | solution.py:282
  21.5 11.1 %copy-start.1 = (bf16[9,256,256]{2,1,0:T(8,128)(2,1)S(1)}, bf16[9,256,256]{2,1,0:T(8,128)(2,1)}, u32[]{:S(2)}) copy-start(bf16[9,256,256]{2,1,0:T(8,128)(2,1)} %constant.13.clone.refs_13_.refs_10_) | copy-start | bytes 3538948
  25.1 20.2 %collective-permute-start.14 = (bf16[512,128]{1,0:T(8,128)(2,1)S(1)}, bf16[512,128]{1,0:T(8,128)(2,1)S(1)}, u32[]{:S(2)}, u32[]{:S(2)}) collective-permute-start(bf16[512,128]{1,0:T(8,128)(2,1)S(1)} %get-tuple-element.55), channel_id=1, source_target_pairs={{0,4},{1,5},{2,6},{3,7},{4,0},{5,1},{6,2},{7,3},{8,12},{9,13},{10,... | collective-permute-start | bytes 393224 | tf_op jit(solution)/shard_map/ppermute | solution.py:282
  25.1 26.0 %collective-permute-start.15 = (bf16[512,128]{1,0:T(8,128)(2,1)S(1)}, bf16[512,128]{1,0:T(8,128)(2,1)S(1)}, u32[]{:S(2)}, u32[]{:S(2)}) collective-permute-start(bf16[512,128]{1,0:T(8,128)(2,1)S(1)} %get-tuple-element.56), channel_id=1, source_target_pairs={{0,5},{1,4},{2,7},{3,6},{4,1},{5,0},{6,3},{7,2},{8,13},{9,12},{10,... | collective-permute-start | bytes 393224 | tf_op jit(solution)/shard_map/ppermute | solution.py:282
  29.1 22.0 %collective-permute-start.16 = (bf16[512,128]{1,0:T(8,128)(2,1)S(1)}, bf16[512,128]{1,0:T(8,128)(2,1)S(1)}, u32[]{:S(2)}, u32[]{:S(2)}) collective-permute-start(bf16[512,128]{1,0:T(8,128)(2,1)S(1)} %get-tuple-element.57), channel_id=1, source_target_pairs={{0,6},{1,7},{2,4},{3,5},{4,2},{5,3},{6,0},{7,1},{8,14},{9,15},{10,... | collective-permute-start | bytes 393224 | tf_op jit(solution)/shard_map/ppermute | solution.py:282
  30.2 22.4 %collective-permute-start.17 = (bf16[512,128]{1,0:T(8,128)(2,1)S(1)}, bf16[512,128]{1,0:T(8,128)(2,1)S(1)}, u32[]{:S(2)}, u32[]{:S(2)}) collective-permute-start(bf16[512,128]{1,0:T(8,128)(2,1)S(1)} %get-tuple-element.58), channel_id=1, source_target_pairs={{0,1},{1,0},{2,3},{3,2},{4,5},{5,4},{6,7},{7,6},{8,9},{9,8},{10,11... | collective-permute-start | bytes 393224 | tf_op jit(solution)/shard_map/ppermute | solution.py:282
  36.8 16.9 %collective-permute-start.18 = (bf16[512,128]{1,0:T(8,128)(2,1)S(1)}, bf16[512,128]{1,0:T(8,128)(2,1)S(1)}, u32[]{:S(2)}, u32[]{:S(2)}) collective-permute-start(bf16[512,128]{1,0:T(8,128)(2,1)S(1)} %get-tuple-element.59), channel_id=1, source_target_pairs={{0,7},{1,6},{2,5},{3,4},{4,3},{5,2},{6,1},{7,0},{8,15},{9,14},{10,... | collective-permute-start | bytes 393224 | tf_op jit(solution)/shard_map/ppermute | solution.py:282
  45.2 9.9 %collective-permute-start.19 = (bf16[512,128]{1,0:T(8,128)(2,1)S(1)}, bf16[512,128]{1,0:T(8,128)(2,1)S(1)}, u32[]{:S(2)}, u32[]{:S(2)}) collective-permute-start(bf16[512,128]{1,0:T(8,128)(2,1)S(1)} %get-tuple-element.60), channel_id=1, source_target_pairs={{0,2},{1,3},{2,0},{3,1},{4,6},{5,7},{6,4},{7,5},{8,10},{9,11},{10,... | collective-permute-start | bytes 393224 | tf_op jit(solution)/shard_map/ppermute | solution.py:282
  51.1 10.0 %collective-permute-start.20 = (bf16[512,128]{1,0:T(8,128)(2,1)S(1)}, bf16[512,128]{1,0:T(8,128)(2,1)S(1)}, u32[]{:S(2)}, u32[]{:S(2)}) collective-permute-start(bf16[512,128]{1,0:T(8,128)(2,1)S(1)} %get-tuple-element.61), channel_id=1, source_target_pairs={{0,3},{1,2},{2,1},{3,0},{4,7},{5,6},{6,5},{7,4},{8,11},{9,10},{10,... | collective-permute-start | bytes 393224 | tf_op jit(solution)/shard_map/ppermute | solution.py:282
  51.1 14.2 %collective-permute-start.7 = (bf16[512,128]{1,0:T(8,128)(2,1)S(1)}, bf16[512,128]{1,0:T(8,128)(2,1)S(1)}, u32[]{:S(2)}, u32[]{:S(2)}) collective-permute-start(bf16[512,128]{1,0:T(8,128)(2,1)S(1)} %get-tuple-element.47), channel_id=1, source_target_pairs={{0,1},{1,0},{2,3},{3,2},{4,5},{5,4},{6,7},{7,6},{8,9},{9,8},{10,11... | collective-permute-start | bytes 393224 | tf_op jit(solution)/shard_map/ppermute | solution.py:282
  52.6 15.0 %collective-permute-start.8 = (bf16[512,128]{1,0:T(8,128)(2,1)S(1)}, bf16[512,128]{1,0:T(8,128)(2,1)S(1)}, u32[]{:S(2)}, u32[]{:S(2)}) collective-permute-start(bf16[512,128]{1,0:T(8,128)(2,1)S(1)} %get-tuple-element.48), channel_id=1, source_target_pairs={{0,4},{1,5},{2,6},{3,7},{4,0},{5,1},{6,2},{7,3},{8,12},{9,13},{10,... | collective-permute-start | bytes 393224 | tf_op jit(solution)/shard_map/ppermute | solution.py:282
  53.7 13.9 %collective-permute-start.9 = (bf16[512,128]{1,0:T(8,128)(2,1)S(1)}, bf16[512,128]{1,0:T(8,128)(2,1)S(1)}, u32[]{:S(2)}, u32[]{:S(2)}) collective-permute-start(bf16[512,128]{1,0:T(8,128)(2,1)S(1)} %get-tuple-element.49), channel_id=1, source_target_pairs={{0,2},{1,3},{2,0},{3,1},{4,6},{5,7},{6,4},{7,5},{8,10},{9,11},{10,... | collective-permute-start | bytes 393224 | tf_op jit(solution)/shard_map/ppermute | solution.py:282
  55.1 14.5 %collective-permute-start.10 = (bf16[512,128]{1,0:T(8,128)(2,1)S(1)}, bf16[512,128]{1,0:T(8,128)(2,1)S(1)}, u32[]{:S(2)}, u32[]{:S(2)}) collective-permute-start(bf16[512,128]{1,0:T(8,128)(2,1)S(1)} %get-tuple-element.50), channel_id=1, source_target_pairs={{0,5},{1,4},{2,7},{3,6},{4,1},{5,0},{6,3},{7,2},{8,13},{9,12},{10,... | collective-permute-start | bytes 393224 | tf_op jit(solution)/shard_map/ppermute | solution.py:282
  61.1 12.0 %collective-permute-start.11 = (bf16[512,128]{1,0:T(8,128)(2,1)S(1)}, bf16[512,128]{1,0:T(8,128)(2,1)S(1)}, u32[]{:S(2)}, u32[]{:S(2)}) collective-permute-start(bf16[512,128]{1,0:T(8,128)(2,1)S(1)} %get-tuple-element.51), channel_id=1, source_target_pairs={{0,6},{1,7},{2,4},{3,5},{4,2},{5,3},{6,0},{7,1},{8,14},{9,15},{10,... | collective-permute-start | bytes 393224 | tf_op jit(solution)/shard_map/ppermute | solution.py:282
  65.2 15.2 %collective-permute-start.21 = (bf16[512,256]{1,0:T(8,128)(2,1)S(1)}, bf16[512,256]{1,0:T(8,128)(2,1)S(1)}, u32[]{:S(2)}, u32[]{:S(2)}) collective-permute-start(bf16[512,256]{1,0:T(8,128)(2,1)S(1)} %get-tuple-element.64), channel_id=1, source_target_pairs={{0,16},{8,24},{16,0},{24,8},{1,17},{9,25},{17,1},{25,9},{2,18},{10... | collective-permute-start | bytes 786440 | tf_op jit(solution)/shard_map/ppermute | solution.py:282
  67.6 12.9 %collective-permute-start.22 = (bf16[512,256]{1,0:T(8,128)(2,1)S(1)}, bf16[512,256]{1,0:T(8,128)(2,1)S(1)}, u32[]{:S(2)}, u32[]{:S(2)}) collective-permute-start(bf16[512,256]{1,0:T(8,128)(2,1)S(1)} %get-tuple-element.65), channel_id=1, source_target_pairs={{0,24},{8,16},{16,8},{24,0},{1,25},{9,17},{17,9},{25,1},{2,26},{10... | collective-permute-start | bytes 786440 | tf_op jit(solution)/shard_map/ppermute | solution.py:282
  67.6 12.9 %collective-permute-start.23 = (bf16[512,256]{1,0:T(8,128)(2,1)S(1)}, bf16[512,256]{1,0:T(8,128)(2,1)S(1)}, u32[]{:S(2)}, u32[]{:S(2)}) collective-permute-start(bf16[512,256]{1,0:T(8,128)(2,1)S(1)} %get-tuple-element.66), channel_id=1, source_target_pairs={{0,8},{8,0},{16,24},{24,16},{1,9},{9,1},{17,25},{25,17},{2,10},{10... | collective-permute-start | bytes 786440 | tf_op jit(solution)/shard_map/ppermute | solution.py:282
  69.6 8.9 %collective-permute-start.12 = (bf16[512,128]{1,0:T(8,128)(2,1)S(1)}, bf16[512,128]{1,0:T(8,128)(2,1)S(1)}, u32[]{:S(2)}, u32[]{:S(2)}) collective-permute-start(bf16[512,128]{1,0:T(8,128)(2,1)S(1)} %get-tuple-element.52), channel_id=1, source_target_pairs={{0,7},{1,6},{2,5},{3,4},{4,3},{5,2},{6,1},{7,0},{8,15},{9,14},{10,... | collective-permute-start | bytes 393224 | tf_op jit(solution)/shard_map/ppermute | solution.py:282
  73.1 7.4 %collective-permute-start.13 = (bf16[512,128]{1,0:T(8,128)(2,1)S(1)}, bf16[512,128]{1,0:T(8,128)(2,1)S(1)}, u32[]{:S(2)}, u32[]{:S(2)}) collective-permute-start(bf16[512,128]{1,0:T(8,128)(2,1)S(1)} %get-tuple-element.53), channel_id=1, source_target_pairs={{0,3},{1,2},{2,1},{3,0},{4,7},{5,6},{6,5},{7,4},{8,11},{9,10},{10,... | collective-permute-start | bytes 393224 | tf_op jit(solution)/shard_map/ppermute | solution.py:282

commit v23 on v21

--- a/solution.py
+++ b/solution.py
@@ -288,7 +288,7 @@
     channels, span = saved_input.shape[1:]
     rows, length = long_filter.shape
     width = length // BLOCKS
-    grad_order, input_order, back_order = (spread(count, o) for o in ((1, 2, 4, 5, 6, 7, 3), (1, 4, 5, 6, 7, 2, 3), (1, 4, 2, 5, 6, 7, 3)))
+    grad_order, input_order, back_order = (spread(count, o) for o in ((4, 1, 5, 2, 6, 7, 3), (1, 4, 5, 6, 7, 2, 3), (1, 4, 2, 5, 6, 7, 3)))
     late = 3
     at = count - 1 - late
     every = range(count + 8)

time: 82.2 us -> 81.4 us (level)
  waiting for transfers between devices: 17.6 us -> 15.1 us
  starting transfers between devices: 47.4 us -> 49.2 us
    ppermute x24, waiting for transfers between devices: 17.6 us -> 15.1 us  [exchange(): lax.ppermute(piece, axis, [(i, i ^ k) for i in range(size)])]
    ppermute x24, starting transfers between devices: 47.4 us -> 49.2 us  [exchange(): lax.ppermute(piece, axis, [(i, i ^ k) for i in range(size)])]
  transfers between devices with their start and end apart: 24 -> 24, of which waited for: 5 -> 4; matrix products, arithmetic and copies ran while one was open for 0% -> 0% of each run, Pallas kernels for 13% -> 13%
where the time goes in v23:
time: 81.4 us; the launch traced here: 81.3 us
  starting transfers between devices  49.2 us (60%)
  waiting for transfers between devices  15.1 us (19%)
  Pallas kernels  14.6 us (18%)
  local copies, waits for them, and re-layouts  1.6 us (2%)
    ppermute x24, starting transfers between devices, exchange(): lax.ppermute(piece, axis, [(i, i ^ k) for i in range(size)])  49.2 us
    ppermute x24, waiting for transfers between devices, exchange(): lax.ppermute(piece, axis, [(i, i ^ k) for i in range(size)])  15.1 us
    pallas_call x5, Pallas kernels, call(): pl.pallas_call(kernel, out_shape=list(outs), in_specs=specs, out_specs=[s...  14.6 us
  transfers between devices with their start and end apart: 24, of which 4 were waited for; matrix products, arithmetic and copies ran while one was open for 0% of the time, Pallas kernels for 13%

profile of v23, /device:TPU:0, one launch (start us, length us, event | category | flops | bytes accessed | tf_op | source)
XLA Modules:
  0.0 81.3 jit_solution(2814322893976680352)
XLA Ops:
  0.6 0.0 copy-start
  0.6 0.1 pad_add_fusion.where
  0.7 2.3 %shard_map.77 = (bf16[512,128]{1,0:T(8,128)(2,1)S(1)}, bf16[512,128]{1,0:T(8,128)(2,1)S(1)}, bf16[512,128]{1,0:T(8,128)(2,1)S(1)}, bf16[512,128]{1,0:T(8,128)(2,...) custom-call(s32[2]{0:T(128)S(1)} %pad_add_fusion.where, ...), custom_call_target="tpu_custom_call" | custom-call | bytes 3145736 | tf_op jit(solution)/shard_map/pallas_call | solution.py:257
  3.0 4.1 %collective-permute-start = (bf16[512,128]{1,0:T(8,128)(2,1)S(1)}, bf16[512,128]{1,0:T(8,128)(2,1)S(1)}, u32[]{:S(2)}, u32[]{:S(2)}) collective-permute-start(bf16[512,128]{1,0:T(8,128)(2,1)S(1)} %get-tuple-element.37), channel_id=1, source_target_pairs={{0,4},{1,5},{2,6},{3,7},{4,0},{5,1},{6,2},{7,3},{8,12},{9,13},{10,... | collective-permute-start | bytes 393224 | tf_op jit(solution)/shard_map/ppermute | solution.py:282
  7.1 1.5 %collective-permute-start.1 = (bf16[512,128]{1,0:T(8,128)(2,1)S(1)}, bf16[512,128]{1,0:T(8,128)(2,1)S(1)}, u32[]{:S(2)}, u32[]{:S(2)}) collective-permute-start(bf16[512,128]{1,0:T(8,128)(2,1)S(1)} %get-tuple-element.38), channel_id=1, source_target_pairs={{0,1},{1,0},{2,3},{3,2},{4,5},{5,4},{6,7},{7,6},{8,9},{9,8},{10,11... | collective-permute-start | bytes 393224 | tf_op jit(solution)/shard_map/ppermute | solution.py:282
  8.7 0.0 collective-permute-start.2
  8.7 1.8 %collective-permute-start.3 = (bf16[512,128]{1,0:T(8,128)(2,1)S(1)}, bf16[512,128]{1,0:T(8,128)(2,1)S(1)}, u32[]{:S(2)}, u32[]{:S(2)}) collective-permute-start(bf16[512,128]{1,0:T(8,128)(2,1)S(1)} %get-tuple-element.40), channel_id=1, source_target_pairs={{0,2},{1,3},{2,0},{3,1},{4,6},{5,7},{6,4},{7,5},{8,10},{9,11},{10,... | collective-permute-start | bytes 393224 | tf_op jit(solution)/shard_map/ppermute | solution.py:282
  10.5 2.5 %collective-permute-start.4 = (bf16[512,128]{1,0:T(8,128)(2,1)S(1)}, bf16[512,128]{1,0:T(8,128)(2,1)S(1)}, u32[]{:S(2)}, u32[]{:S(2)}) collective-permute-start(bf16[512,128]{1,0:T(8,128)(2,1)S(1)} %get-tuple-element.41), channel_id=1, source_target_pairs={{0,6},{1,7},{2,4},{3,5},{4,2},{5,3},{6,0},{7,1},{8,14},{9,15},{10,... | collective-permute-start | bytes 393224 | tf_op jit(solution)/shard_map/ppermute | solution.py:282
  13.0 4.8 %collective-permute-done.refs_0_ = bf16[512,128]{1,0:T(8,128)(2,1)S(1)} collective-permute-done((bf16[512,128]{1,0:T(8,128)(2,1)S(1)}, bf16[512,128]{1,0:T(8,128)(2,1)S(1)}, u32[]{:S(2)}, u32[]{:S(2)}) %collective-permute-start) | collective-permute-done | bytes 131104 | tf_op jit(solution)/shard_map/ppermute | solution.py:282
  17.8 5.9 %collective-permute-start.5 = (bf16[512,128]{1,0:T(8,128)(2,1)S(1)}, bf16[512,128]{1,0:T(8,128)(2,1)S(1)}, u32[]{:S(2)}, u32[]{:S(2)}) collective-permute-start(bf16[512,128]{1,0:T(8,128)(2,1)S(1)} %get-tuple-element.42), channel_id=1, source_target_pairs={{0,7},{1,6},{2,5},{3,4},{4,3},{5,2},{6,1},{7,0},{8,15},{9,14},{10,... | collective-permute-start | bytes 393224 | tf_op jit(solution)/shard_map/ppermute | solution.py:282
  23.8 0.0 collective-permute-done.1.refs_1_
  23.8 0.0 collective-permute-start.6
  23.8 0.0 copy-done
  23.8 0.0 copy-start.2
  23.8 1.6 %copy-done.2 = f32[512,1024]{1,0:T(8,128)S(1)} copy-done((f32[512,1024]{1,0:T(8,128)S(1)}, f32[512,1024]{1,0:T(8,128)}, u32[]{:S(2)}) %copy-start.2) | copy-done | bytes 2097176
  25.4 0.0 copy-start.1
  25.4 2.1 %shard_map.78 = (bf16[512,128]{1,0:T(8,128)(2,1)S(1)}, bf16[512,128]{1,0:T(8,128)(2,1)S(1)}, bf16[512,128]{1,0:T(8,128)(2,1)S(1)}, bf16[512,128]{1,0:T(8,128)(2,...) custom-call(s32[2]{0:T(128)S(1)} %pad_add_fusion.where, ...), custom_call_target="tpu_custom_call" | custom-call | flops 603979776 | bytes 7733256 | tf_op jit(solution)/shard_map/pallas_call | solution.py:257
  27.5 0.0 collective-permute-done.2.refs_2_
  27.5 0.6 collective-permute-start.14
  28.1 0.0 collective-permute-done.3.refs_3_
  28.1 1.1 %collective-permute-start.15 = (bf16[512,128]{1,0:T(8,128)(2,1)S(1)}, bf16[512,128]{1,0:T(8,128)(2,1)S(1)}, u32[]{:S(2)}, u32[]{:S(2)}) collective-permute-start(bf16[512,128]{1,0:T(8,128)(2,1)S(1)} %get-tuple-element.58), channel_id=1, source_target_pairs={{0,4},{1,5},{2,6},{3,7},{4,0},{5,1},{6,2},{7,3},{8,12},{9,13},{10,... | collective-permute-start | bytes 393224 | tf_op jit(solution)/shard_map/ppermute | solution.py:282
  29.1 0.0 collective-permute-done.4.refs_4_
  29.1 3.5 %collective-permute-start.16 = (bf16[512,128]{1,0:T(8,128)(2,1)S(1)}, bf16[512,128]{1,0:T(8,128)(2,1)S(1)}, u32[]{:S(2)}, u32[]{:S(2)}) collective-permute-start(bf16[512,128]{1,0:T(8,128)(2,1)S(1)} %get-tuple-element.59), channel_id=1, source_target_pairs={{0,5},{1,4},{2,7},{3,6},{4,1},{5,0},{6,3},{7,2},{8,13},{9,12},{10,... | collective-permute-start | bytes 393224 | tf_op jit(solution)/shard_map/ppermute | solution.py:282
  32.6 0.0 collective-permute-done.5.refs_5_
  32.6 0.8 %collective-permute-start.17 = (bf16[512,128]{1,0:T(8,128)(2,1)S(1)}, bf16[512,128]{1,0:T(8,128)(2,1)S(1)}, u32[]{:S(2)}, u32[]{:S(2)}) collective-permute-start(bf16[512,128]{1,0:T(8,128)(2,1)S(1)} %get-tuple-element.60), channel_id=1, source_target_pairs={{0,6},{1,7},{2,4},{3,5},{4,2},{5,3},{6,0},{7,1},{8,14},{9,15},{10,... | collective-permute-start | bytes 393224 | tf_op jit(solution)/shard_map/ppermute | solution.py:282
  33.5 0.0 collective-permute-done.6.refs_6_
  33.5 0.0 copy-done.1
  33.5 4.2 %shard_map.79 = (bf16[512,128]{1,0:T(8,128)(2,1)S(1)}, bf16[512,128]{1,0:T(8,128)(2,1)S(1)}, bf16[512,128]{1,0:T(8,128)(2,1)S(1)}, bf16[512,128]{1,0:T(8,128)(2,...) custom-call(s32[2]{0:T(128)S(1)} %pad_add_fusion.where, ...), custom_call_target="tpu_custom_call", output_to_operand_aliasing={{0}: (9, {}), {1}: (10, {}), {2}: (11, {})} | custom-call | flops 1207959552 | bytes 9961480 | tf_op jit(solution)/shard_map/pallas_call | solution.py:257
  37.7 2.3 %collective-permute-start.18 = (bf16[512,128]{1,0:T(8,128)(2,1)S(1)}, bf16[512,128]{1,0:T(8,128)(2,1)S(1)}, u32[]{:S(2)}, u32[]{:S(2)}) collective-permute-start(bf16[512,128]{1,0:T(8,128)(2,1)S(1)} %get-tuple-element.61), channel_id=1, source_target_pairs={{0,7},{1,6},{2,5},{3,4},{4,3},{5,2},{6,1},{7,0},{8,15},{9,14},{10,... | collective-permute-start | bytes 393224 | tf_op jit(solution)/shard_map/ppermute | solution.py:282
  40.0 0.0 collective-permute-done.14.refs_0_
  40.0 7.4 %collective-permute-start.19 = (bf16[512,128]{1,0:T(8,128)(2,1)S(1)}, bf16[512,128]{1,0:T(8,128)(2,1)S(1)}, u32[]{:S(2)}, u32[]{:S(2)}) collective-permute-start(bf16[512,128]{1,0:T(8,128)(2,1)S(1)} %get-tuple-element.62), channel_id=1, source_target_pairs={{0,2},{1,3},{2,0},{3,1},{4,6},{5,7},{6,4},{7,5},{8,10},{9,11},{10,... | collective-permute-start | bytes 393224 | tf_op jit(solution)/shard_map/ppermute | solution.py:282
  47.5 0.0 collective-permute-done.15.refs_1_
  47.5 2.9 %collective-permute-start.20 = (bf16[512,128]{1,0:T(8,128)(2,1)S(1)}, bf16[512,128]{1,0:T(8,128)(2,1)S(1)}, u32[]{:S(2)}, u32[]{:S(2)}) collective-permute-start(bf16[512,128]{1,0:T(8,128)(2,1)S(1)} %get-tuple-element.63), channel_id=1, source_target_pairs={{0,3},{1,2},{2,1},{3,0},{4,7},{5,6},{6,5},{7,4},{8,11},{9,10},{10,... | collective-permute-start | bytes 393224 | tf_op jit(solution)/shard_map/ppermute | solution.py:282
  50.4 0.0 collective-permute-done.16.refs_2_
  50.4 0.6 collective-permute-start.7
  50.9 0.0 collective-permute-done.17.refs_3_
  50.9 1.8 %collective-permute-start.8 = (bf16[512,128]{1,0:T(8,128)(2,1)S(1)}, bf16[512,128]{1,0:T(8,128)(2,1)S(1)}, u32[]{:S(2)}, u32[]{:S(2)}) collective-permute-start(bf16[512,128]{1,0:T(8,128)(2,1)S(1)} %get-tuple-element.50), channel_id=1, source_target_pairs={{0,4},{1,5},{2,6},{3,7},{4,0},{5,1},{6,2},{7,3},{8,12},{9,13},{10,... | collective-permute-start | bytes 393224 | tf_op jit(solution)/shard_map/ppermute | solution.py:282
  52.8 0.0 collective-permute-done.18.refs_4_
  52.8 3.2 %collective-permute-start.9 = (bf16[512,128]{1,0:T(8,128)(2,1)S(1)}, bf16[512,128]{1,0:T(8,128)(2,1)S(1)}, u32[]{:S(2)}, u32[]{:S(2)}) collective-permute-start(bf16[512,128]{1,0:T(8,128)(2,1)S(1)} %get-tuple-element.51), channel_id=1, source_target_pairs={{0,2},{1,3},{2,0},{3,1},{4,6},{5,7},{6,4},{7,5},{8,10},{9,11},{10,... | collective-permute-start | bytes 393224 | tf_op jit(solution)/shard_map/ppermute | solution.py:282
  56.0 0.0 collective-permute-done.19.refs_5_
  56.0 2.0 %collective-permute-start.10 = (bf16[512,128]{1,0:T(8,128)(2,1)S(1)}, bf16[512,128]{1,0:T(8,128)(2,1)S(1)}, u32[]{:S(2)}, u32[]{:S(2)}) collective-permute-start(bf16[512,128]{1,0:T(8,128)(2,1)S(1)} %get-tuple-element.52), channel_id=1, source_target_pairs={{0,5},{1,4},{2,7},{3,6},{4,1},{5,0},{6,3},{7,2},{8,13},{9,12},{10,... | collective-permute-start | bytes 393224 | tf_op jit(solution)/shard_map/ppermute | solution.py:282
  58.0 0.0 collective-permute-done.20.refs_6_
  58.0 1.7 %collective-permute-start.11 = (bf16[512,128]{1,0:T(8,128)(2,1)S(1)}, bf16[512,128]{1,0:T(8,128)(2,1)S(1)}, u32[]{:S(2)}, u32[]{:S(2)}) collective-permute-start(bf16[512,128]{1,0:T(8,128)(2,1)S(1)} %get-tuple-element.53), channel_id=1, source_target_pairs={{0,6},{1,7},{2,4},{3,5},{4,2},{5,3},{6,0},{7,1},{8,14},{9,15},{10,... | collective-permute-start | bytes 393224 | tf_op jit(solution)/shard_map/ppermute | solution.py:282
  59.7 4.1 %shard_map.80 = (bf16[512,256]{1,0:T(8,128)(2,1)S(1)}, bf16[512,256]{1,0:T(8,128)(2,1)S(1)}, bf16[512,256]{1,0:T(8,128)(2,1)S(1)}, bf16[512,256]{1,0:T(8,128)(2,1)S(1)}) custom-call(s32[2]{0:T(128)S(1)} %pad_add_fusion.where, bf16[512,128]{1,0:T(8,128)(2,1)S(1)} %collective-permute-done.14.refs_0_, bf16[512,128]{1,0:T(8,128)(2,1)S(1)} %collective-permute-done.15.refs_1_, ...), custom_call_target="tpu_custom_call" | custom-call | flops 1207959552 | bytes 6815752 | tf_op jit(solution)/shard_map/pallas_call | solution.py:257
  63.8 0.0 collective-permute-done.7.refs_0_
  63.8 1.6 %collective-permute-start.21 = (bf16[512,256]{1,0:T(8,128)(2,1)S(1)}, bf16[512,256]{1,0:T(8,128)(2,1)S(1)}, u32[]{:S(2)}, u32[]{:S(2)}) collective-permute-start(bf16[512,256]{1,0:T(8,128)(2,1)S(1)} %get-tuple-element.66), channel_id=1, source_target_pairs={{0,16},{8,24},{16,0},{24,8},{1,17},{9,25},{17,1},{25,9},{2,18},{10... | collective-permute-start | bytes 786440 | tf_op jit(solution)/shard_map/ppermute | solution.py:282
  65.4 0.0 collective-permute-done.8.refs_1_
  65.4 0.0 collective-permute-start.22
  65.4 0.0 collective-permute-done.9.refs_2_
  65.4 0.6 collective-permute-start.23
  66.1 3.6 %collective-permute-done.10.refs_3_ = bf16[512,128]{1,0:T(8,128)(2,1)S(1)} collective-permute-done((bf16[512,128]{1,0:T(8,128)(2,1)S(1)}, bf16[512,128]{1,0:T(8,128)(2,1)S(1)}, u32[]{:S(2)}, u32[]{:S(2)}) %collective-permute-start.10) | collective-permute-done | bytes 131104 | tf_op jit(solution)/shard_map/ppermute | solution.py:282
  69.7 3.0 %collective-permute-start.12 = (bf16[512,128]{1,0:T(8,128)(2,1)S(1)}, bf16[512,128]{1,0:T(8,128)(2,1)S(1)}, u32[]{:S(2)}, u32[]{:S(2)}) collective-permute-start(bf16[512,128]{1,0:T(8,128)(2,1)S(1)} %get-tuple-element.54), channel_id=1, source_target_pairs={{0,7},{1,6},{2,5},{3,4},{4,3},{5,2},{6,1},{7,0},{8,15},{9,14},{10,... | collective-permute-start | bytes 393224 | tf_op jit(solution)/shard_map/ppermute | solution.py:282
  72.7 0.0 collective-permute-done.11.refs_4_
  72.7 0.1 collective-permute-start.13
  72.8 5.9 %collective-permute-done.12.refs_5_ = bf16[512,128]{1,0:T(8,128)(2,1)S(1)} collective-permute-done((bf16[512,128]{1,0:T(8,128)(2,1)S(1)}, bf16[512,128]{1,0:T(8,128)(2,1)S(1)}, u32[]{:S(2)}, u32[]{:S(2)}) %collective-permute-start.12) | collective-permute-done | bytes 131104 | tf_op jit(solution)/shard_map/ppermute | solution.py:282
  78.7 0.7 collective-permute-done.13.refs_6_
  79.4 0.0 collective-permute-done.21.refs_8_
  79.5 0.0 collective-permute-done.22.refs_9_
  79.5 0.0 collective-permute-done.23.refs_10_
  79.5 1.8 %shard_map.81 = (bf16[8,512,128]{2,1,0:T(8,128)(2,1)}, f32[512,256]{1,0:T(8,128)}) custom-call(s32[2]{0:T(128)S(1)} %pad_add_fusion.where, bf16[512,128]{1,0:T(8,128)(2,1)S(1)} %collective-permute-done.7.refs_0_, bf16[512,128]{1,0:T(8,128)(2,1)S(1)} %collective-permute-done.8.refs_1_, bf16[512,128]{1,0:T(8,128)(2,1)S(1)} %collective-permute-done.9.refs_2_, ...), custom_call_target="tpu_custom_call" | custom-call | bytes 3670024 | tf_op jit(solution)/shard_map/pallas_call | solution.py:257
Async XLA Ops:
  0.6 23.1 %copy-start = (bf16[9,256,256]{2,1,0:T(8,128)(2,1)S(1)}, bf16[9,256,256]{2,1,0:T(8,128)(2,1)}, u32[]{:S(2)}) copy-start(bf16[9,256,256]{2,1,0:T(8,128)(2,1)} %constant.12.clone.forward.refs_12_.refs_9_) | copy-start | bytes 3538948
  3.0 14.8 %collective-permute-start = (bf16[512,128]{1,0:T(8,128)(2,1)S(1)}, bf16[512,128]{1,0:T(8,128)(2,1)S(1)}, u32[]{:S(2)}, u32[]{:S(2)}) collective-permute-start(bf16[512,128]{1,0:T(8,128)(2,1)S(1)} %get-tuple-element.37), channel_id=1, source_target_pairs={{0,4},{1,5},{2,6},{3,7},{4,0},{5,1},{6,2},{7,3},{8,12},{9,13},{10,... | collective-permute-start | bytes 393224 | tf_op jit(solution)/shard_map/ppermute | solution.py:282
  7.1 16.6 %collective-permute-start.1 = (bf16[512,128]{1,0:T(8,128)(2,1)S(1)}, bf16[512,128]{1,0:T(8,128)(2,1)S(1)}, u32[]{:S(2)}, u32[]{:S(2)}) collective-permute-start(bf16[512,128]{1,0:T(8,128)(2,1)S(1)} %get-tuple-element.38), channel_id=1, source_target_pairs={{0,1},{1,0},{2,3},{3,2},{4,5},{5,4},{6,7},{7,6},{8,9},{9,8},{10,11... | collective-permute-start | bytes 393224 | tf_op jit(solution)/shard_map/ppermute | solution.py:282
  8.7 18.8 %collective-permute-start.2 = (bf16[512,128]{1,0:T(8,128)(2,1)S(1)}, bf16[512,128]{1,0:T(8,128)(2,1)S(1)}, u32[]{:S(2)}, u32[]{:S(2)}) collective-permute-start(bf16[512,128]{1,0:T(8,128)(2,1)S(1)} %get-tuple-element.39), channel_id=1, source_target_pairs={{0,5},{1,4},{2,7},{3,6},{4,1},{5,0},{6,3},{7,2},{8,13},{9,12},{10,... | collective-permute-start | bytes 393224 | tf_op jit(solution)/shard_map/ppermute | solution.py:282
  8.7 19.4 %collective-permute-start.3 = (bf16[512,128]{1,0:T(8,128)(2,1)S(1)}, bf16[512,128]{1,0:T(8,128)(2,1)S(1)}, u32[]{:S(2)}, u32[]{:S(2)}) collective-permute-start(bf16[512,128]{1,0:T(8,128)(2,1)S(1)} %get-tuple-element.40), channel_id=1, source_target_pairs={{0,2},{1,3},{2,0},{3,1},{4,6},{5,7},{6,4},{7,5},{8,10},{9,11},{10,... | collective-permute-start | bytes 393224 | tf_op jit(solution)/shard_map/ppermute | solution.py:282
  10.5 18.6 %collective-permute-start.4 = (bf16[512,128]{1,0:T(8,128)(2,1)S(1)}, bf16[512,128]{1,0:T(8,128)(2,1)S(1)}, u32[]{:S(2)}, u32[]{:S(2)}) collective-permute-start(bf16[512,128]{1,0:T(8,128)(2,1)S(1)} %get-tuple-element.41), channel_id=1, source_target_pairs={{0,6},{1,7},{2,4},{3,5},{4,2},{5,3},{6,0},{7,1},{8,14},{9,15},{10,... | collective-permute-start | bytes 393224 | tf_op jit(solution)/shard_map/ppermute | solution.py:282
  17.8 14.8 %collective-permute-start.5 = (bf16[512,128]{1,0:T(8,128)(2,1)S(1)}, bf16[512,128]{1,0:T(8,128)(2,1)S(1)}, u32[]{:S(2)}, u32[]{:S(2)}) collective-permute-start(bf16[512,128]{1,0:T(8,128)(2,1)S(1)} %get-tuple-element.42), channel_id=1, source_target_pairs={{0,7},{1,6},{2,5},{3,4},{4,3},{5,2},{6,1},{7,0},{8,15},{9,14},{10,... | collective-permute-start | bytes 393224 | tf_op jit(solution)/shard_map/ppermute | solution.py:282
  23.8 9.7 %collective-permute-start.6 = (bf16[512,128]{1,0:T(8,128)(2,1)S(1)}, bf16[512,128]{1,0:T(8,128)(2,1)S(1)}, u32[]{:S(2)}, u32[]{:S(2)}) collective-permute-start(bf16[512,128]{1,0:T(8,128)(2,1)S(1)} %get-tuple-element.43), channel_id=1, source_target_pairs={{0,3},{1,2},{2,1},{3,0},{4,7},{5,6},{6,5},{7,4},{8,11},{9,10},{10,... | collective-permute-start | bytes 393224 | tf_op jit(solution)/shard_map/ppermute | solution.py:282
  23.8 1.6 %copy-start.2 = (f32[512,1024]{1,0:T(8,128)S(1)}, f32[512,1024]{1,0:T(8,128)}, u32[]{:S(2)}) copy-start(f32[512,1024]{1,0:T(8,128)} %taps.1) | copy-start | bytes 6291460
  25.4 8.1 %copy-start.1 = (bf16[9,256,256]{2,1,0:T(8,128)(2,1)S(1)}, bf16[9,256,256]{2,1,0:T(8,128)(2,1)}, u32[]{:S(2)}) copy-start(bf16[9,256,256]{2,1,0:T(8,128)(2,1)} %constant.13.clone.refs_13_.refs_10_) | copy-start | bytes 3538948
  27.5 12.6 %collective-permute-start.14 = (bf16[512,128]{1,0:T(8,128)(2,1)S(1)}, bf16[512,128]{1,0:T(8,128)(2,1)S(1)}, u32[]{:S(2)}, u32[]{:S(2)}) collective-permute-start(bf16[512,128]{1,0:T(8,128)(2,1)S(1)} %get-tuple-element.57), channel_id=1, source_target_pairs={{0,1},{1,0},{2,3},{3,2},{4,5},{5,4},{6,7},{7,6},{8,9},{9,8},{10,11... | collective-permute-start | bytes 393224 | tf_op jit(solution)/shard_map/ppermute | solution.py:282
  28.1 19.4 %collective-permute-start.15 = (bf16[512,128]{1,0:T(8,128)(2,1)S(1)}, bf16[512,128]{1,0:T(8,128)(2,1)S(1)}, u32[]{:S(2)}, u32[]{:S(2)}) collective-permute-start(bf16[512,128]{1,0:T(8,128)(2,1)S(1)} %get-tuple-element.58), channel_id=1, source_target_pairs={{0,4},{1,5},{2,6},{3,7},{4,0},{5,1},{6,2},{7,3},{8,12},{9,13},{10,... | collective-permute-start | bytes 393224 | tf_op jit(solution)/shard_map/ppermute | solution.py:282
  29.1 21.2 %collective-permute-start.16 = (bf16[512,128]{1,0:T(8,128)(2,1)S(1)}, bf16[512,128]{1,0:T(8,128)(2,1)S(1)}, u32[]{:S(2)}, u32[]{:S(2)}) collective-permute-start(bf16[512,128]{1,0:T(8,128)(2,1)S(1)} %get-tuple-element.59), channel_id=1, source_target_pairs={{0,5},{1,4},{2,7},{3,6},{4,1},{5,0},{6,3},{7,2},{8,13},{9,12},{10,... | collective-permute-start | bytes 393224 | tf_op jit(solution)/shard_map/ppermute | solution.py:282
  32.6 18.3 %collective-permute-start.17 = (bf16[512,128]{1,0:T(8,128)(2,1)S(1)}, bf16[512,128]{1,0:T(8,128)(2,1)S(1)}, u32[]{:S(2)}, u32[]{:S(2)}) collective-permute-start(bf16[512,128]{1,0:T(8,128)(2,1)S(1)} %get-tuple-element.60), channel_id=1, source_target_pairs={{0,6},{1,7},{2,4},{3,5},{4,2},{5,3},{6,0},{7,1},{8,14},{9,15},{10,... | collective-permute-start | bytes 393224 | tf_op jit(solution)/shard_map/ppermute | solution.py:282
  37.7 15.1 %collective-permute-start.18 = (bf16[512,128]{1,0:T(8,128)(2,1)S(1)}, bf16[512,128]{1,0:T(8,128)(2,1)S(1)}, u32[]{:S(2)}, u32[]{:S(2)}) collective-permute-start(bf16[512,128]{1,0:T(8,128)(2,1)S(1)} %get-tuple-element.61), channel_id=1, source_target_pairs={{0,7},{1,6},{2,5},{3,4},{4,3},{5,2},{6,1},{7,0},{8,15},{9,14},{10,... | collective-permute-start | bytes 393224 | tf_op jit(solution)/shard_map/ppermute | solution.py:282
  40.0 15.9 %collective-permute-start.19 = (bf16[512,128]{1,0:T(8,128)(2,1)S(1)}, bf16[512,128]{1,0:T(8,128)(2,1)S(1)}, u32[]{:S(2)}, u32[]{:S(2)}) collective-permute-start(bf16[512,128]{1,0:T(8,128)(2,1)S(1)} %get-tuple-element.62), channel_id=1, source_target_pairs={{0,2},{1,3},{2,0},{3,1},{4,6},{5,7},{6,4},{7,5},{8,10},{9,11},{10,... | collective-permute-start | bytes 393224 | tf_op jit(solution)/shard_map/ppermute | solution.py:282
  47.5 10.6 %collective-permute-start.20 = (bf16[512,128]{1,0:T(8,128)(2,1)S(1)}, bf16[512,128]{1,0:T(8,128)(2,1)S(1)}, u32[]{:S(2)}, u32[]{:S(2)}) collective-permute-start(bf16[512,128]{1,0:T(8,128)(2,1)S(1)} %get-tuple-element.63), channel_id=1, source_target_pairs={{0,3},{1,2},{2,1},{3,0},{4,7},{5,6},{6,5},{7,4},{8,11},{9,10},{10,... | collective-permute-start | bytes 393224 | tf_op jit(solution)/shard_map/ppermute | solution.py:282
  50.4 13.5 %collective-permute-start.7 = (bf16[512,128]{1,0:T(8,128)(2,1)S(1)}, bf16[512,128]{1,0:T(8,128)(2,1)S(1)}, u32[]{:S(2)}, u32[]{:S(2)}) collective-permute-start(bf16[512,128]{1,0:T(8,128)(2,1)S(1)} %get-tuple-element.49), channel_id=1, source_target_pairs={{0,1},{1,0},{2,3},{3,2},{4,5},{5,4},{6,7},{7,6},{8,9},{9,8},{10,11... | collective-permute-start | bytes 393224 | tf_op jit(solution)/shard_map/ppermute | solution.py:282
  50.9 14.4 %collective-permute-start.8 = (bf16[512,128]{1,0:T(8,128)(2,1)S(1)}, bf16[512,128]{1,0:T(8,128)(2,1)S(1)}, u32[]{:S(2)}, u32[]{:S(2)}) collective-permute-start(bf16[512,128]{1,0:T(8,128)(2,1)S(1)} %get-tuple-element.50), channel_id=1, source_target_pairs={{0,4},{1,5},{2,6},{3,7},{4,0},{5,1},{6,2},{7,3},{8,12},{9,13},{10,... | collective-permute-start | bytes 393224 | tf_op jit(solution)/shard_map/ppermute | solution.py:282
  52.8 12.6 %collective-permute-start.9 = (bf16[512,128]{1,0:T(8,128)(2,1)S(1)}, bf16[512,128]{1,0:T(8,128)(2,1)S(1)}, u32[]{:S(2)}, u32[]{:S(2)}) collective-permute-start(bf16[512,128]{1,0:T(8,128)(2,1)S(1)} %get-tuple-element.51), channel_id=1, source_target_pairs={{0,2},{1,3},{2,0},{3,1},{4,6},{5,7},{6,4},{7,5},{8,10},{9,11},{10,... | collective-permute-start | bytes 393224 | tf_op jit(solution)/shard_map/ppermute | solution.py:282
  56.0 13.7 %collective-permute-start.10 = (bf16[512,128]{1,0:T(8,128)(2,1)S(1)}, bf16[512,128]{1,0:T(8,128)(2,1)S(1)}, u32[]{:S(2)}, u32[]{:S(2)}) collective-permute-start(bf16[512,128]{1,0:T(8,128)(2,1)S(1)} %get-tuple-element.52), channel_id=1, source_target_pairs={{0,5},{1,4},{2,7},{3,6},{4,1},{5,0},{6,3},{7,2},{8,13},{9,12},{10,... | collective-permute-start | bytes 393224 | tf_op jit(solution)/shard_map/ppermute | solution.py:282
  58.0 14.7 %collective-permute-start.11 = (bf16[512,128]{1,0:T(8,128)(2,1)S(1)}, bf16[512,128]{1,0:T(8,128)(2,1)S(1)}, u32[]{:S(2)}, u32[]{:S(2)}) collective-permute-start(bf16[512,128]{1,0:T(8,128)(2,1)S(1)} %get-tuple-element.53), channel_id=1, source_target_pairs={{0,6},{1,7},{2,4},{3,5},{4,2},{5,3},{6,0},{7,1},{8,14},{9,15},{10,... | collective-permute-start | bytes 393224 | tf_op jit(solution)/shard_map/ppermute | solution.py:282
  63.8 15.6 %collective-permute-start.21 = (bf16[512,256]{1,0:T(8,128)(2,1)S(1)}, bf16[512,256]{1,0:T(8,128)(2,1)S(1)}, u32[]{:S(2)}, u32[]{:S(2)}) collective-permute-start(bf16[512,256]{1,0:T(8,128)(2,1)S(1)} %get-tuple-element.66), channel_id=1, source_target_pairs={{0,16},{8,24},{16,0},{24,8},{1,17},{9,25},{17,1},{25,9},{2,18},{10... | collective-permute-start | bytes 786440 | tf_op jit(solution)/shard_map/ppermute | solution.py:282
  65.4 14.1 %collective-permute-start.22 = (bf16[512,256]{1,0:T(8,128)(2,1)S(1)}, bf16[512,256]{1,0:T(8,128)(2,1)S(1)}, u32[]{:S(2)}, u32[]{:S(2)}) collective-permute-start(bf16[512,256]{1,0:T(8,128)(2,1)S(1)} %get-tuple-element.67), channel_id=1, source_target_pairs={{0,24},{8,16},{16,8},{24,0},{1,25},{9,17},{17,9},{25,1},{2,26},{10... | collective-permute-start | bytes 786440 | tf_op jit(solution)/shard_map/ppermute | solution.py:282
  65.4 14.1 %collective-permute-start.23 = (bf16[512,256]{1,0:T(8,128)(2,1)S(1)}, bf16[512,256]{1,0:T(8,128)(2,1)S(1)}, u32[]{:S(2)}, u32[]{:S(2)}) collective-permute-start(bf16[512,256]{1,0:T(8,128)(2,1)S(1)} %get-tuple-element.68), channel_id=1, source_target_pairs={{0,8},{8,0},{16,24},{24,16},{1,9},{9,1},{17,25},{25,17},{2,10},{10... | collective-permute-start | bytes 786440 | tf_op jit(solution)/shard_map/ppermute | solution.py:282
  69.7 9.0 %collective-permute-start.12 = (bf16[512,128]{1,0:T(8,128)(2,1)S(1)}, bf16[512,128]{1,0:T(8,128)(2,1)S(1)}, u32[]{:S(2)}, u32[]{:S(2)}) collective-permute-start(bf16[512,128]{1,0:T(8,128)(2,1)S(1)} %get-tuple-element.54), channel_id=1, source_target_pairs={{0,7},{1,6},{2,5},{3,4},{4,3},{5,2},{6,1},{7,0},{8,15},{9,14},{10,... | collective-permute-start | bytes 393224 | tf_op jit(solution)/shard_map/ppermute | solution.py:282
  72.7 6.7 %collective-permute-start.13 = (bf16[512,128]{1,0:T(8,128)(2,1)S(1)}, bf16[512,128]{1,0:T(8,128)(2,1)S(1)}, u32[]{:S(2)}, u32[]{:S(2)}) collective-permute-start(bf16[512,128]{1,0:T(8,128)(2,1)S(1)} %get-tuple-element.55), channel_id=1, source_target_pairs={{0,3},{1,2},{2,1},{3,0},{4,7},{5,6},{6,5},{7,4},{8,11},{9,10},{10,... | collective-permute-start | bytes 393224 | tf_op jit(solution)/shard_map/ppermute | solution.py:282

commit v24 on v23

--- a/solution.py
+++ b/solution.py
@@ -288,7 +288,7 @@
     channels, span = saved_input.shape[1:]
     rows, length = long_filter.shape
     width = length // BLOCKS
-    grad_order, input_order, back_order = (spread(count, o) for o in ((4, 1, 5, 2, 6, 7, 3), (1, 4, 5, 6, 7, 2, 3), (1, 4, 2, 5, 6, 7, 3)))
+    grad_order, input_order, back_order = (spread(count, o) for o in ((4, 1, 5, 2, 6, 7, 3), (4, 5, 6, 1, 7, 2, 3), (1, 2, 4, 5, 6, 7, 3)))
     late = 3
     at = count - 1 - late
     every = range(count + 8)

time: 81.4 us -> 83.9 us (1.031)
  waiting for transfers between devices: 15.1 us -> 19.4 us
  starting transfers between devices: 49.2 us -> 47.3 us
    ppermute x24, waiting for transfers between devices: 15.1 us -> 19.4 us  [exchange(): lax.ppermute(piece, axis, [(i, i ^ k) for i in range(size)])]
    ppermute x24, starting transfers between devices: 49.2 us -> 47.3 us  [exchange(): lax.ppermute(piece, axis, [(i, i ^ k) for i in range(size)])]
  transfers between devices with their start and end apart: 24 -> 24, of which waited for: 4 -> 6; matrix products, arithmetic and copies ran while one was open for 0% -> 0% of each run, Pallas kernels for 13% -> 12%
where the time goes in v24:
time: 83.9 us; the launch traced here: 83.7 us
  starting transfers between devices  47.3 us (56%)
  waiting for transfers between devices  19.4 us (23%)
  Pallas kernels  14.6 us (17%)
  local copies, waits for them, and re-layouts  1.6 us (2%)
    ppermute x24, starting transfers between devices, exchange(): lax.ppermute(piece, axis, [(i, i ^ k) for i in range(size)])  47.3 us
    ppermute x24, waiting for transfers between devices, exchange(): lax.ppermute(piece, axis, [(i, i ^ k) for i in range(size)])  19.4 us
    pallas_call x5, Pallas kernels, call(): pl.pallas_call(kernel, out_shape=list(outs), in_specs=specs, out_specs=[s...  14.6 us
  transfers between devices with their start and end apart: 24, of which 6 were waited for; matrix products, arithmetic and copies ran while one was open for 0% of the time, Pallas kernels for 12%

profile of v24, /device:TPU:0, one launch (start us, length us, event | category | flops | bytes accessed | tf_op | source)
XLA Modules:
  0.0 83.7 jit_solution(16183469427187996214)
XLA Ops:
  0.6 0.0 copy-start
  0.6 0.1 pad_add_fusion.where
  0.7 2.3 %shard_map.77 = (bf16[512,128]{1,0:T(8,128)(2,1)S(1)}, bf16[512,128]{1,0:T(8,128)(2,1)S(1)}, bf16[512,128]{1,0:T(8,128)(2,1)S(1)}, bf16[512,128]{1,0:T(8,128)(2,...) custom-call(s32[2]{0:T(128)S(1)} %pad_add_fusion.where, ...), custom_call_target="tpu_custom_call" | custom-call | bytes 3145736 | tf_op jit(solution)/shard_map/pallas_call | solution.py:257
  3.0 4.1 %collective-permute-start = (bf16[512,128]{1,0:T(8,128)(2,1)S(1)}, bf16[512,128]{1,0:T(8,128)(2,1)S(1)}, u32[]{:S(2)}, u32[]{:S(2)}) collective-permute-start(bf16[512,128]{1,0:T(8,128)(2,1)S(1)} %get-tuple-element.37), channel_id=1, source_target_pairs={{0,4},{1,5},{2,6},{3,7},{4,0},{5,1},{6,2},{7,3},{8,12},{9,13},{10,... | collective-permute-start | bytes 393224 | tf_op jit(solution)/shard_map/ppermute | solution.py:282
  7.1 1.5 %collective-permute-start.1 = (bf16[512,128]{1,0:T(8,128)(2,1)S(1)}, bf16[512,128]{1,0:T(8,128)(2,1)S(1)}, u32[]{:S(2)}, u32[]{:S(2)}) collective-permute-start(bf16[512,128]{1,0:T(8,128)(2,1)S(1)} %get-tuple-element.38), channel_id=1, source_target_pairs={{0,1},{1,0},{2,3},{3,2},{4,5},{5,4},{6,7},{7,6},{8,9},{9,8},{10,11... | collective-permute-start | bytes 393224 | tf_op jit(solution)/shard_map/ppermute | solution.py:282
  8.7 0.0 collective-permute-start.2
  8.7 1.8 %collective-permute-start.3 = (bf16[512,128]{1,0:T(8,128)(2,1)S(1)}, bf16[512,128]{1,0:T(8,128)(2,1)S(1)}, u32[]{:S(2)}, u32[]{:S(2)}) collective-permute-start(bf16[512,128]{1,0:T(8,128)(2,1)S(1)} %get-tuple-element.40), channel_id=1, source_target_pairs={{0,2},{1,3},{2,0},{3,1},{4,6},{5,7},{6,4},{7,5},{8,10},{9,11},{10,... | collective-permute-start | bytes 393224 | tf_op jit(solution)/shard_map/ppermute | solution.py:282
  10.5 2.5 %collective-permute-start.4 = (bf16[512,128]{1,0:T(8,128)(2,1)S(1)}, bf16[512,128]{1,0:T(8,128)(2,1)S(1)}, u32[]{:S(2)}, u32[]{:S(2)}) collective-permute-start(bf16[512,128]{1,0:T(8,128)(2,1)S(1)} %get-tuple-element.41), channel_id=1, source_target_pairs={{0,6},{1,7},{2,4},{3,5},{4,2},{5,3},{6,0},{7,1},{8,14},{9,15},{10,... | collective-permute-start | bytes 393224 | tf_op jit(solution)/shard_map/ppermute | solution.py:282
  13.0 4.8 %collective-permute-done.refs_0_ = bf16[512,128]{1,0:T(8,128)(2,1)S(1)} collective-permute-done((bf16[512,128]{1,0:T(8,128)(2,1)S(1)}, bf16[512,128]{1,0:T(8,128)(2,1)S(1)}, u32[]{:S(2)}, u32[]{:S(2)}) %collective-permute-start) | collective-permute-done | bytes 131104 | tf_op jit(solution)/shard_map/ppermute | solution.py:282
  17.8 5.9 %collective-permute-start.5 = (bf16[512,128]{1,0:T(8,128)(2,1)S(1)}, bf16[512,128]{1,0:T(8,128)(2,1)S(1)}, u32[]{:S(2)}, u32[]{:S(2)}) collective-permute-start(bf16[512,128]{1,0:T(8,128)(2,1)S(1)} %get-tuple-element.42), channel_id=1, source_target_pairs={{0,7},{1,6},{2,5},{3,4},{4,3},{5,2},{6,1},{7,0},{8,15},{9,14},{10,... | collective-permute-start | bytes 393224 | tf_op jit(solution)/shard_map/ppermute | solution.py:282
  23.8 0.0 collective-permute-done.1.refs_1_
  23.8 0.0 collective-permute-start.6
  23.8 0.0 copy-done
  23.8 0.0 copy-start.2
  23.8 1.6 %copy-done.2 = f32[512,1024]{1,0:T(8,128)S(1)} copy-done((f32[512,1024]{1,0:T(8,128)S(1)}, f32[512,1024]{1,0:T(8,128)}, u32[]{:S(2)}) %copy-start.2) | copy-done | bytes 2097176
  25.4 0.0 copy-start.1
  25.4 2.1 %shard_map.78 = (bf16[512,128]{1,0:T(8,128)(2,1)S(1)}, bf16[512,128]{1,0:T(8,128)(2,1)S(1)}, bf16[512,128]{1,0:T(8,128)(2,1)S(1)}, bf16[512,128]{1,0:T(8,128)(2,...) custom-call(s32[2]{0:T(128)S(1)} %pad_add_fusion.where, ...), custom_call_target="tpu_custom_call" | custom-call | flops 603979776 | bytes 7733256 | tf_op jit(solution)/shard_map/pallas_call | solution.py:257
  27.5 0.0 collective-permute-done.2.refs_2_
  27.5 0.6 collective-permute-start.14
  28.1 0.0 collective-permute-done.3.refs_3_
  28.1 2.3 %collective-permute-start.15 = (bf16[512,128]{1,0:T(8,128)(2,1)S(1)}, bf16[512,128]{1,0:T(8,128)(2,1)S(1)}, u32[]{:S(2)}, u32[]{:S(2)}) collective-permute-start(bf16[512,128]{1,0:T(8,128)(2,1)S(1)} %get-tuple-element.58), channel_id=1, source_target_pairs={{0,5},{1,4},{2,7},{3,6},{4,1},{5,0},{6,3},{7,2},{8,13},{9,12},{10,... | collective-permute-start | bytes 393224 | tf_op jit(solution)/shard_map/ppermute | solution.py:282
  30.4 0.0 collective-permute-done.4.refs_4_
  30.4 2.5 %collective-permute-start.16 = (bf16[512,128]{1,0:T(8,128)(2,1)S(1)}, bf16[512,128]{1,0:T(8,128)(2,1)S(1)}, u32[]{:S(2)}, u32[]{:S(2)}) collective-permute-start(bf16[512,128]{1,0:T(8,128)(2,1)S(1)} %get-tuple-element.59), channel_id=1, source_target_pairs={{0,6},{1,7},{2,4},{3,5},{4,2},{5,3},{6,0},{7,1},{8,14},{9,15},{10,... | collective-permute-start | bytes 393224 | tf_op jit(solution)/shard_map/ppermute | solution.py:282
  32.9 0.0 collective-permute-done.5.refs_5_
  32.9 0.5 collective-permute-start.17
  33.5 0.0 collective-permute-done.6.refs_6_
  33.5 0.0 copy-done.1
  33.5 4.2 %shard_map.79 = (bf16[512,128]{1,0:T(8,128)(2,1)S(1)}, bf16[512,128]{1,0:T(8,128)(2,1)S(1)}, bf16[512,128]{1,0:T(8,128)(2,1)S(1)}, bf16[512,128]{1,0:T(8,128)(2,...) custom-call(s32[2]{0:T(128)S(1)} %pad_add_fusion.where, ...), custom_call_target="tpu_custom_call", output_to_operand_aliasing={{0}: (9, {}), {1}: (10, {}), {2}: (11, {})} | custom-call | flops 1207959552 | bytes 9961480 | tf_op jit(solution)/shard_map/pallas_call | solution.py:257
  37.7 2.3 %collective-permute-start.18 = (bf16[512,128]{1,0:T(8,128)(2,1)S(1)}, bf16[512,128]{1,0:T(8,128)(2,1)S(1)}, u32[]{:S(2)}, u32[]{:S(2)}) collective-permute-start(bf16[512,128]{1,0:T(8,128)(2,1)S(1)} %get-tuple-element.61), channel_id=1, source_target_pairs={{0,7},{1,6},{2,5},{3,4},{4,3},{5,2},{6,1},{7,0},{8,15},{9,14},{10,... | collective-permute-start | bytes 393224 | tf_op jit(solution)/shard_map/ppermute | solution.py:282
  40.0 3.7 %collective-permute-done.14.refs_0_ = bf16[512,128]{1,0:T(8,128)(2,1)S(1)} collective-permute-done((bf16[512,128]{1,0:T(8,128)(2,1)S(1)}, bf16[512,128]{1,0:T(8,128)(2,1)S(1)}, u32[]{:S(2)}, u32[]{:S(2)}) %collective-permute-start.14) | collective-permute-done | bytes 131104 | tf_op jit(solution)/shard_map/ppermute | solution.py:282
  43.8 6.4 %collective-permute-start.19 = (bf16[512,128]{1,0:T(8,128)(2,1)S(1)}, bf16[512,128]{1,0:T(8,128)(2,1)S(1)}, u32[]{:S(2)}, u32[]{:S(2)}) collective-permute-start(bf16[512,128]{1,0:T(8,128)(2,1)S(1)} %get-tuple-element.62), channel_id=1, source_target_pairs={{0,2},{1,3},{2,0},{3,1},{4,6},{5,7},{6,4},{7,5},{8,10},{9,11},{10,... | collective-permute-start | bytes 393224 | tf_op jit(solution)/shard_map/ppermute | solution.py:282
  50.2 0.0 collective-permute-done.15.refs_1_
  50.2 0.0 collective-permute-start.20
  50.2 0.0 collective-permute-done.16.refs_2_
  50.2 1.5 %collective-permute-start.7 = (bf16[512,128]{1,0:T(8,128)(2,1)S(1)}, bf16[512,128]{1,0:T(8,128)(2,1)S(1)}, u32[]{:S(2)}, u32[]{:S(2)}) collective-permute-start(bf16[512,128]{1,0:T(8,128)(2,1)S(1)} %get-tuple-element.49), channel_id=1, source_target_pairs={{0,1},{1,0},{2,3},{3,2},{4,5},{5,4},{6,7},{7,6},{8,9},{9,8},{10,11... | collective-permute-start | bytes 393224 | tf_op jit(solution)/shard_map/ppermute | solution.py:282
  51.8 0.0 collective-permute-done.17.refs_3_
  51.8 2.0 %collective-permute-start.8 = (bf16[512,128]{1,0:T(8,128)(2,1)S(1)}, bf16[512,128]{1,0:T(8,128)(2,1)S(1)}, u32[]{:S(2)}, u32[]{:S(2)}) collective-permute-start(bf16[512,128]{1,0:T(8,128)(2,1)S(1)} %get-tuple-element.50), channel_id=1, source_target_pairs={{0,2},{1,3},{2,0},{3,1},{4,6},{5,7},{6,4},{7,5},{8,10},{9,11},{10,... | collective-permute-start | bytes 393224 | tf_op jit(solution)/shard_map/ppermute | solution.py:282
  53.7 0.0 collective-permute-done.18.refs_4_
  53.7 4.8 %collective-permute-start.9 = (bf16[512,128]{1,0:T(8,128)(2,1)S(1)}, bf16[512,128]{1,0:T(8,128)(2,1)S(1)}, u32[]{:S(2)}, u32[]{:S(2)}) collective-permute-start(bf16[512,128]{1,0:T(8,128)(2,1)S(1)} %get-tuple-element.51), channel_id=1, source_target_pairs={{0,4},{1,5},{2,6},{3,7},{4,0},{5,1},{6,2},{7,3},{8,12},{9,13},{10,... | collective-permute-start | bytes 393224 | tf_op jit(solution)/shard_map/ppermute | solution.py:282
  58.5 0.0 collective-permute-done.19.refs_5_
  58.5 0.0 collective-permute-start.10
  58.5 0.0 collective-permute-done.20.refs_6_
  58.5 3.4 %collective-permute-start.11 = (bf16[512,128]{1,0:T(8,128)(2,1)S(1)}, bf16[512,128]{1,0:T(8,128)(2,1)S(1)}, u32[]{:S(2)}, u32[]{:S(2)}) collective-permute-start(bf16[512,128]{1,0:T(8,128)(2,1)S(1)} %get-tuple-element.53), channel_id=1, source_target_pairs={{0,6},{1,7},{2,4},{3,5},{4,2},{5,3},{6,0},{7,1},{8,14},{9,15},{10,... | collective-permute-start | bytes 393224 | tf_op jit(solution)/shard_map/ppermute | solution.py:282
  62.0 4.1 %shard_map.80 = (bf16[512,256]{1,0:T(8,128)(2,1)S(1)}, bf16[512,256]{1,0:T(8,128)(2,1)S(1)}, bf16[512,256]{1,0:T(8,128)(2,1)S(1)}, bf16[512,256]{1,0:T(8,128)(2,1)S(1)}) custom-call(s32[2]{0:T(128)S(1)} %pad_add_fusion.where, bf16[512,128]{1,0:T(8,128)(2,1)S(1)} %collective-permute-done.14.refs_0_, bf16[512,128]{1,0:T(8,128)(2,1)S(1)} %collective-permute-done.15.refs_1_, ...), custom_call_target="tpu_custom_call" | custom-call | flops 1207959552 | bytes 6815752 | tf_op jit(solution)/shard_map/pallas_call | solution.py:257
  66.1 0.0 collective-permute-done.7.refs_0_
  66.1 1.6 %collective-permute-start.21 = (bf16[512,256]{1,0:T(8,128)(2,1)S(1)}, bf16[512,256]{1,0:T(8,128)(2,1)S(1)}, u32[]{:S(2)}, u32[]{:S(2)}) collective-permute-start(bf16[512,256]{1,0:T(8,128)(2,1)S(1)} %get-tuple-element.66), channel_id=1, source_target_pairs={{0,16},{8,24},{16,0},{24,8},{1,17},{9,25},{17,1},{25,9},{2,18},{10... | collective-permute-start | bytes 786440 | tf_op jit(solution)/shard_map/ppermute | solution.py:282
  67.7 0.0 collective-permute-done.8.refs_1_
  67.7 0.0 collective-permute-start.22
  67.7 3.2 %collective-permute-done.9.refs_2_ = bf16[512,128]{1,0:T(8,128)(2,1)S(1)} collective-permute-done((bf16[512,128]{1,0:T(8,128)(2,1)S(1)}, bf16[512,128]{1,0:T(8,128)(2,1)S(1)}, u32[]{:S(2)}, u32[]{:S(2)}) %collective-permute-start.9) | collective-permute-done | bytes 131104 | tf_op jit(solution)/shard_map/ppermute | solution.py:282
  70.9 0.0 collective-permute-start.23
  70.9 1.9 %collective-permute-done.10.refs_3_ = bf16[512,128]{1,0:T(8,128)(2,1)S(1)} collective-permute-done((bf16[512,128]{1,0:T(8,128)(2,1)S(1)}, bf16[512,128]{1,0:T(8,128)(2,1)S(1)}, u32[]{:S(2)}, u32[]{:S(2)}) %collective-permute-start.10) | collective-permute-done | bytes 131104 | tf_op jit(solution)/shard_map/ppermute | solution.py:282
  72.8 1.8 %collective-permute-start.12 = (bf16[512,128]{1,0:T(8,128)(2,1)S(1)}, bf16[512,128]{1,0:T(8,128)(2,1)S(1)}, u32[]{:S(2)}, u32[]{:S(2)}) collective-permute-start(bf16[512,128]{1,0:T(8,128)(2,1)S(1)} %get-tuple-element.54), channel_id=1, source_target_pairs={{0,7},{1,6},{2,5},{3,4},{4,3},{5,2},{6,1},{7,0},{8,15},{9,14},{10,... | collective-permute-start | bytes 393224 | tf_op jit(solution)/shard_map/ppermute | solution.py:282
  74.6 0.0 collective-permute-done.11.refs_4_
  74.6 1.6 %collective-permute-start.13 = (bf16[512,128]{1,0:T(8,128)(2,1)S(1)}, bf16[512,128]{1,0:T(8,128)(2,1)S(1)}, u32[]{:S(2)}, u32[]{:S(2)}) collective-permute-start(bf16[512,128]{1,0:T(8,128)(2,1)S(1)} %get-tuple-element.55), channel_id=1, source_target_pairs={{0,3},{1,2},{2,1},{3,0},{4,7},{5,6},{6,5},{7,4},{8,11},{9,10},{10,... | collective-permute-start | bytes 393224 | tf_op jit(solution)/shard_map/ppermute | solution.py:282
  76.2 5.0 %collective-permute-done.12.refs_5_ = bf16[512,128]{1,0:T(8,128)(2,1)S(1)} collective-permute-done((bf16[512,128]{1,0:T(8,128)(2,1)S(1)}, bf16[512,128]{1,0:T(8,128)(2,1)S(1)}, u32[]{:S(2)}, u32[]{:S(2)}) %collective-permute-start.12) | collective-permute-done | bytes 131104 | tf_op jit(solution)/shard_map/ppermute | solution.py:282
  81.1 0.8 collective-permute-done.13.refs_6_
  81.9 0.0 collective-permute-done.21.refs_8_
  81.9 0.0 collective-permute-done.22.refs_9_
  81.9 0.0 collective-permute-done.23.refs_10_
  81.9 1.8 %shard_map.81 = (bf16[8,512,128]{2,1,0:T(8,128)(2,1)}, f32[512,256]{1,0:T(8,128)}) custom-call(s32[2]{0:T(128)S(1)} %pad_add_fusion.where, bf16[512,128]{1,0:T(8,128)(2,1)S(1)} %collective-permute-done.7.refs_0_, bf16[512,128]{1,0:T(8,128)(2,1)S(1)} %collective-permute-done.8.refs_1_, bf16[512,128]{1,0:T(8,128)(2,1)S(1)} %collective-permute-done.9.refs_2_, ...), custom_call_target="tpu_custom_call" | custom-call | bytes 3670024 | tf_op jit(solution)/shard_map/pallas_call | solution.py:257
Async XLA Ops:
  0.6 23.1 %copy-start = (bf16[9,256,256]{2,1,0:T(8,128)(2,1)S(1)}, bf16[9,256,256]{2,1,0:T(8,128)(2,1)}, u32[]{:S(2)}) copy-start(bf16[9,256,256]{2,1,0:T(8,128)(2,1)} %constant.12.clone.forward.refs_12_.refs_9_) | copy-start | bytes 3538948
  3.0 14.8 %collective-permute-start = (bf16[512,128]{1,0:T(8,128)(2,1)S(1)}, bf16[512,128]{1,0:T(8,128)(2,1)S(1)}, u32[]{:S(2)}, u32[]{:S(2)}) collective-permute-start(bf16[512,128]{1,0:T(8,128)(2,1)S(1)} %get-tuple-element.37), channel_id=1, source_target_pairs={{0,4},{1,5},{2,6},{3,7},{4,0},{5,1},{6,2},{7,3},{8,12},{9,13},{10,... | collective-permute-start | bytes 393224 | tf_op jit(solution)/shard_map/ppermute | solution.py:282
  7.1 16.6 %collective-permute-start.1 = (bf16[512,128]{1,0:T(8,128)(2,1)S(1)}, bf16[512,128]{1,0:T(8,128)(2,1)S(1)}, u32[]{:S(2)}, u32[]{:S(2)}) collective-permute-start(bf16[512,128]{1,0:T(8,128)(2,1)S(1)} %get-tuple-element.38), channel_id=1, source_target_pairs={{0,1},{1,0},{2,3},{3,2},{4,5},{5,4},{6,7},{7,6},{8,9},{9,8},{10,11... | collective-permute-start | bytes 393224 | tf_op jit(solution)/shard_map/ppermute | solution.py:282
  8.7 18.8 %collective-permute-start.2 = (bf16[512,128]{1,0:T(8,128)(2,1)S(1)}, bf16[512,128]{1,0:T(8,128)(2,1)S(1)}, u32[]{:S(2)}, u32[]{:S(2)}) collective-permute-start(bf16[512,128]{1,0:T(8,128)(2,1)S(1)} %get-tuple-element.39), channel_id=1, source_target_pairs={{0,5},{1,4},{2,7},{3,6},{4,1},{5,0},{6,3},{7,2},{8,13},{9,12},{10,... | collective-permute-start | bytes 393224 | tf_op jit(solution)/shard_map/ppermute | solution.py:282
  8.7 19.4 %collective-permute-start.3 = (bf16[512,128]{1,0:T(8,128)(2,1)S(1)}, bf16[512,128]{1,0:T(8,128)(2,1)S(1)}, u32[]{:S(2)}, u32[]{:S(2)}) collective-permute-start(bf16[512,128]{1,0:T(8,128)(2,1)S(1)} %get-tuple-element.40), channel_id=1, source_target_pairs={{0,2},{1,3},{2,0},{3,1},{4,6},{5,7},{6,4},{7,5},{8,10},{9,11},{10,... | collective-permute-start | bytes 393224 | tf_op jit(solution)/shard_map/ppermute | solution.py:282
  10.5 19.9 %collective-permute-start.4 = (bf16[512,128]{1,0:T(8,128)(2,1)S(1)}, bf16[512,128]{1,0:T(8,128)(2,1)S(1)}, u32[]{:S(2)}, u32[]{:S(2)}) collective-permute-start(bf16[512,128]{1,0:T(8,128)(2,1)S(1)} %get-tuple-element.41), channel_id=1, source_target_pairs={{0,6},{1,7},{2,4},{3,5},{4,2},{5,3},{6,0},{7,1},{8,14},{9,15},{10,... | collective-permute-start | bytes 393224 | tf_op jit(solution)/shard_map/ppermute | solution.py:282
  17.8 15.1 %collective-permute-start.5 = (bf16[512,128]{1,0:T(8,128)(2,1)S(1)}, bf16[512,128]{1,0:T(8,128)(2,1)S(1)}, u32[]{:S(2)}, u32[]{:S(2)}) collective-permute-start(bf16[512,128]{1,0:T(8,128)(2,1)S(1)} %get-tuple-element.42), channel_id=1, source_target_pairs={{0,7},{1,6},{2,5},{3,4},{4,3},{5,2},{6,1},{7,0},{8,15},{9,14},{10,... | collective-permute-start | bytes 393224 | tf_op jit(solution)/shard_map/ppermute | solution.py:282
  23.8 9.7 %collective-permute-start.6 = (bf16[512,128]{1,0:T(8,128)(2,1)S(1)}, bf16[512,128]{1,0:T(8,128)(2,1)S(1)}, u32[]{:S(2)}, u32[]{:S(2)}) collective-permute-start(bf16[512,128]{1,0:T(8,128)(2,1)S(1)} %get-tuple-element.43), channel_id=1, source_target_pairs={{0,3},{1,2},{2,1},{3,0},{4,7},{5,6},{6,5},{7,4},{8,11},{9,10},{10,... | collective-permute-start | bytes 393224 | tf_op jit(solution)/shard_map/ppermute | solution.py:282
  23.8 1.6 %copy-start.2 = (f32[512,1024]{1,0:T(8,128)S(1)}, f32[512,1024]{1,0:T(8,128)}, u32[]{:S(2)}) copy-start(f32[512,1024]{1,0:T(8,128)} %taps.1) | copy-start | bytes 6291460
  25.4 8.1 %copy-start.1 = (bf16[9,256,256]{2,1,0:T(8,128)(2,1)S(1)}, bf16[9,256,256]{2,1,0:T(8,128)(2,1)}, u32[]{:S(2)}) copy-start(bf16[9,256,256]{2,1,0:T(8,128)(2,1)} %constant.13.clone.refs_13_.refs_10_) | copy-start | bytes 3538948
  27.5 16.3 %collective-permute-start.14 = (bf16[512,128]{1,0:T(8,128)(2,1)S(1)}, bf16[512,128]{1,0:T(8,128)(2,1)S(1)}, u32[]{:S(2)}, u32[]{:S(2)}) collective-permute-start(bf16[512,128]{1,0:T(8,128)(2,1)S(1)} %get-tuple-element.57), channel_id=1, source_target_pairs={{0,4},{1,5},{2,6},{3,7},{4,0},{5,1},{6,2},{7,3},{8,12},{9,13},{10,... | collective-permute-start | bytes 393224 | tf_op jit(solution)/shard_map/ppermute | solution.py:282
  28.1 22.1 %collective-permute-start.15 = (bf16[512,128]{1,0:T(8,128)(2,1)S(1)}, bf16[512,128]{1,0:T(8,128)(2,1)S(1)}, u32[]{:S(2)}, u32[]{:S(2)}) collective-permute-start(bf16[512,128]{1,0:T(8,128)(2,1)S(1)} %get-tuple-element.58), channel_id=1, source_target_pairs={{0,5},{1,4},{2,7},{3,6},{4,1},{5,0},{6,3},{7,2},{8,13},{9,12},{10,... | collective-permute-start | bytes 393224 | tf_op jit(solution)/shard_map/ppermute | solution.py:282
  30.4 19.8 %collective-permute-start.16 = (bf16[512,128]{1,0:T(8,128)(2,1)S(1)}, bf16[512,128]{1,0:T(8,128)(2,1)S(1)}, u32[]{:S(2)}, u32[]{:S(2)}) collective-permute-start(bf16[512,128]{1,0:T(8,128)(2,1)S(1)} %get-tuple-element.59), channel_id=1, source_target_pairs={{0,6},{1,7},{2,4},{3,5},{4,2},{5,3},{6,0},{7,1},{8,14},{9,15},{10,... | collective-permute-start | bytes 393224 | tf_op jit(solution)/shard_map/ppermute | solution.py:282
  32.9 18.8 %collective-permute-start.17 = (bf16[512,128]{1,0:T(8,128)(2,1)S(1)}, bf16[512,128]{1,0:T(8,128)(2,1)S(1)}, u32[]{:S(2)}, u32[]{:S(2)}) collective-permute-start(bf16[512,128]{1,0:T(8,128)(2,1)S(1)} %get-tuple-element.60), channel_id=1, source_target_pairs={{0,1},{1,0},{2,3},{3,2},{4,5},{5,4},{6,7},{7,6},{8,9},{9,8},{10,11... | collective-permute-start | bytes 393224 | tf_op jit(solution)/shard_map/ppermute | solution.py:282
  37.7 16.0 %collective-permute-start.18 = (bf16[512,128]{1,0:T(8,128)(2,1)S(1)}, bf16[512,128]{1,0:T(8,128)(2,1)S(1)}, u32[]{:S(2)}, u32[]{:S(2)}) collective-permute-start(bf16[512,128]{1,0:T(8,128)(2,1)S(1)} %get-tuple-element.61), channel_id=1, source_target_pairs={{0,7},{1,6},{2,5},{3,4},{4,3},{5,2},{6,1},{7,0},{8,15},{9,14},{10,... | collective-permute-start | bytes 393224 | tf_op jit(solution)/shard_map/ppermute | solution.py:282
  43.8 14.8 %collective-permute-start.19 = (bf16[512,128]{1,0:T(8,128)(2,1)S(1)}, bf16[512,128]{1,0:T(8,128)(2,1)S(1)}, u32[]{:S(2)}, u32[]{:S(2)}) collective-permute-start(bf16[512,128]{1,0:T(8,128)(2,1)S(1)} %get-tuple-element.62), channel_id=1, source_target_pairs={{0,2},{1,3},{2,0},{3,1},{4,6},{5,7},{6,4},{7,5},{8,10},{9,11},{10,... | collective-permute-start | bytes 393224 | tf_op jit(solution)/shard_map/ppermute | solution.py:282
  50.2 8.3 %collective-permute-start.20 = (bf16[512,128]{1,0:T(8,128)(2,1)S(1)}, bf16[512,128]{1,0:T(8,128)(2,1)S(1)}, u32[]{:S(2)}, u32[]{:S(2)}) collective-permute-start(bf16[512,128]{1,0:T(8,128)(2,1)S(1)} %get-tuple-element.63), channel_id=1, source_target_pairs={{0,3},{1,2},{2,1},{3,0},{4,7},{5,6},{6,5},{7,4},{8,11},{9,10},{10,... | collective-permute-start | bytes 393224 | tf_op jit(solution)/shard_map/ppermute | solution.py:282
  50.2 15.8 %collective-permute-start.7 = (bf16[512,128]{1,0:T(8,128)(2,1)S(1)}, bf16[512,128]{1,0:T(8,128)(2,1)S(1)}, u32[]{:S(2)}, u32[]{:S(2)}) collective-permute-start(bf16[512,128]{1,0:T(8,128)(2,1)S(1)} %get-tuple-element.49), channel_id=1, source_target_pairs={{0,1},{1,0},{2,3},{3,2},{4,5},{5,4},{6,7},{7,6},{8,9},{9,8},{10,11... | collective-permute-start | bytes 393224 | tf_op jit(solution)/shard_map/ppermute | solution.py:282
  51.8 15.9 %collective-permute-start.8 = (bf16[512,128]{1,0:T(8,128)(2,1)S(1)}, bf16[512,128]{1,0:T(8,128)(2,1)S(1)}, u32[]{:S(2)}, u32[]{:S(2)}) collective-permute-start(bf16[512,128]{1,0:T(8,128)(2,1)S(1)} %get-tuple-element.50), channel_id=1, source_target_pairs={{0,2},{1,3},{2,0},{3,1},{4,6},{5,7},{6,4},{7,5},{8,10},{9,11},{10,... | collective-permute-start | bytes 393224 | tf_op jit(solution)/shard_map/ppermute | solution.py:282
  53.7 17.1 %collective-permute-start.9 = (bf16[512,128]{1,0:T(8,128)(2,1)S(1)}, bf16[512,128]{1,0:T(8,128)(2,1)S(1)}, u32[]{:S(2)}, u32[]{:S(2)}) collective-permute-start(bf16[512,128]{1,0:T(8,128)(2,1)S(1)} %get-tuple-element.51), channel_id=1, source_target_pairs={{0,4},{1,5},{2,6},{3,7},{4,0},{5,1},{6,2},{7,3},{8,12},{9,13},{10,... | collective-permute-start | bytes 393224 | tf_op jit(solution)/shard_map/ppermute | solution.py:282
  58.5 14.3 %collective-permute-start.10 = (bf16[512,128]{1,0:T(8,128)(2,1)S(1)}, bf16[512,128]{1,0:T(8,128)(2,1)S(1)}, u32[]{:S(2)}, u32[]{:S(2)}) collective-permute-start(bf16[512,128]{1,0:T(8,128)(2,1)S(1)} %get-tuple-element.52), channel_id=1, source_target_pairs={{0,5},{1,4},{2,7},{3,6},{4,1},{5,0},{6,3},{7,2},{8,13},{9,12},{10,... | collective-permute-start | bytes 393224 | tf_op jit(solution)/shard_map/ppermute | solution.py:282
  58.5 16.1 %collective-permute-start.11 = (bf16[512,128]{1,0:T(8,128)(2,1)S(1)}, bf16[512,128]{1,0:T(8,128)(2,1)S(1)}, u32[]{:S(2)}, u32[]{:S(2)}) collective-permute-start(bf16[512,128]{1,0:T(8,128)(2,1)S(1)} %get-tuple-element.53), channel_id=1, source_target_pairs={{0,6},{1,7},{2,4},{3,5},{4,2},{5,3},{6,0},{7,1},{8,14},{9,15},{10,... | collective-permute-start | bytes 393224 | tf_op jit(solution)/shard_map/ppermute | solution.py:282
  66.1 15.8 %collective-permute-start.21 = (bf16[512,256]{1,0:T(8,128)(2,1)S(1)}, bf16[512,256]{1,0:T(8,128)(2,1)S(1)}, u32[]{:S(2)}, u32[]{:S(2)}) collective-permute-start(bf16[512,256]{1,0:T(8,128)(2,1)S(1)} %get-tuple-element.66), channel_id=1, source_target_pairs={{0,16},{8,24},{16,0},{24,8},{1,17},{9,25},{17,1},{25,9},{2,18},{10... | collective-permute-start | bytes 786440 | tf_op jit(solution)/shard_map/ppermute | solution.py:282
  67.7 14.2 %collective-permute-start.22 = (bf16[512,256]{1,0:T(8,128)(2,1)S(1)}, bf16[512,256]{1,0:T(8,128)(2,1)S(1)}, u32[]{:S(2)}, u32[]{:S(2)}) collective-permute-start(bf16[512,256]{1,0:T(8,128)(2,1)S(1)} %get-tuple-element.67), channel_id=1, source_target_pairs={{0,24},{8,16},{16,8},{24,0},{1,25},{9,17},{17,9},{25,1},{2,26},{10... | collective-permute-start | bytes 786440 | tf_op jit(solution)/shard_map/ppermute | solution.py:282
  70.9 11.0 %collective-permute-start.23 = (bf16[512,256]{1,0:T(8,128)(2,1)S(1)}, bf16[512,256]{1,0:T(8,128)(2,1)S(1)}, u32[]{:S(2)}, u32[]{:S(2)}) collective-permute-start(bf16[512,256]{1,0:T(8,128)(2,1)S(1)} %get-tuple-element.68), channel_id=1, source_target_pairs={{0,8},{8,0},{16,24},{24,16},{1,9},{9,1},{17,25},{25,17},{2,10},{10... | collective-permute-start | bytes 786440 | tf_op jit(solution)/shard_map/ppermute | solution.py:282
  72.8 8.3 %collective-permute-start.12 = (bf16[512,128]{1,0:T(8,128)(2,1)S(1)}, bf16[512,128]{1,0:T(8,128)(2,1)S(1)}, u32[]{:S(2)}, u32[]{:S(2)}) collective-permute-start(bf16[512,128]{1,0:T(8,128)(2,1)S(1)} %get-tuple-element.54), channel_id=1, source_target_pairs={{0,7},{1,6},{2,5},{3,4},{4,3},{5,2},{6,1},{7,0},{8,15},{9,14},{10,... | collective-permute-start | bytes 393224 | tf_op jit(solution)/shard_map/ppermute | solution.py:282
  74.6 7.3 %collective-permute-start.13 = (bf16[512,128]{1,0:T(8,128)(2,1)S(1)}, bf16[512,128]{1,0:T(8,128)(2,1)S(1)}, u32[]{:S(2)}, u32[]{:S(2)}) collective-permute-start(bf16[512,128]{1,0:T(8,128)(2,1)S(1)} %get-tuple-element.55), channel_id=1, source_target_pairs={{0,3},{1,2},{2,1},{3,0},{4,7},{5,6},{6,5},{7,4},{8,11},{9,10},{10,... | collective-permute-start | bytes 393224 | tf_op jit(solution)/shard_map/ppermute | solution.py:282

commit v25 on v24

--- a/solution.py
+++ b/solution.py
@@ -288,8 +288,8 @@
     channels, span = saved_input.shape[1:]
     rows, length = long_filter.shape
     width = length // BLOCKS
-    grad_order, input_order, back_order = (spread(count, o) for o in ((4, 1, 5, 2, 6, 7, 3), (4, 5, 6, 1, 7, 2, 3), (1, 2, 4, 5, 6, 7, 3)))
-    late = 3
+    grad_order, input_order, back_order = (spread(count, o) for o in ((4, 1, 5, 2, 6, 7, 3), (4, 5, 6, 7, 1, 2, 3), (1, 4, 2, 5, 6, 7, 3)))
+    late = 4
     at = count - 1 - late
     every = range(count + 8)
     where = jnp.stack([lax.axis_index("ctx"), lax.axis_index("dp")]).astype(jnp.int32)

time: 83.9 us -> 84.6 us (level)
  transfers between devices with their start and end apart: 24 -> 24, of which waited for: 6 -> 5; matrix products, arithmetic and copies ran while one was open for 0% -> 0% of each run, Pallas kernels for 12% -> 12%
where the time goes in v25:
time: 84.6 us; the launch traced here: 84.4 us
  starting transfers between devices  47.6 us (56%)
  waiting for transfers between devices  19.8 us (23%)
  Pallas kernels  14.6 us (17%)
  local copies, waits for them, and re-layouts  1.6 us (2%)
    ppermute x24, starting transfers between devices, exchange(): lax.ppermute(piece, axis, [(i, i ^ k) for i in range(size)])  47.6 us
    ppermute x24, waiting for transfers between devices, exchange(): lax.ppermute(piece, axis, [(i, i ^ k) for i in range(size)])  19.8 us
    pallas_call x5, Pallas kernels, call(): pl.pallas_call(kernel, out_shape=list(outs), in_specs=specs, out_specs=[s...  14.6 us
  transfers between devices with their start and end apart: 24, of which 5 were waited for; matrix products, arithmetic and copies ran while one was open for 0% of the time, Pallas kernels for 12%

profile of v25, /device:TPU:0, one launch (start us, length us, event | category | flops | bytes accessed | tf_op | source)
XLA Modules:
  0.0 84.4 jit_solution(3922722552527414717)
XLA Ops:
  0.6 0.0 copy-start
  0.6 0.1 pad_add_fusion.where
  0.7 2.3 %shard_map.77 = (bf16[512,128]{1,0:T(8,128)(2,1)S(1)}, bf16[512,128]{1,0:T(8,128)(2,1)S(1)}, bf16[512,128]{1,0:T(8,128)(2,1)S(1)}, bf16[512,128]{1,0:T(8,128)(2,...) custom-call(s32[2]{0:T(128)S(1)} %pad_add_fusion.where, ...), custom_call_target="tpu_custom_call" | custom-call | bytes 3145736 | tf_op jit(solution)/shard_map/pallas_call | solution.py:257
  3.0 4.1 %collective-permute-start = (bf16[512,128]{1,0:T(8,128)(2,1)S(1)}, bf16[512,128]{1,0:T(8,128)(2,1)S(1)}, u32[]{:S(2)}, u32[]{:S(2)}) collective-permute-start(bf16[512,128]{1,0:T(8,128)(2,1)S(1)} %get-tuple-element.38), channel_id=1, source_target_pairs={{0,4},{1,5},{2,6},{3,7},{4,0},{5,1},{6,2},{7,3},{8,12},{9,13},{10,... | collective-permute-start | bytes 393224 | tf_op jit(solution)/shard_map/ppermute | solution.py:282
  7.1 1.5 %collective-permute-start.1 = (bf16[512,128]{1,0:T(8,128)(2,1)S(1)}, bf16[512,128]{1,0:T(8,128)(2,1)S(1)}, u32[]{:S(2)}, u32[]{:S(2)}) collective-permute-start(bf16[512,128]{1,0:T(8,128)(2,1)S(1)} %get-tuple-element.39), channel_id=1, source_target_pairs={{0,1},{1,0},{2,3},{3,2},{4,5},{5,4},{6,7},{7,6},{8,9},{9,8},{10,11... | collective-permute-start | bytes 393224 | tf_op jit(solution)/shard_map/ppermute | solution.py:282
  8.7 0.0 collective-permute-start.2
  8.7 1.8 %collective-permute-start.3 = (bf16[512,128]{1,0:T(8,128)(2,1)S(1)}, bf16[512,128]{1,0:T(8,128)(2,1)S(1)}, u32[]{:S(2)}, u32[]{:S(2)}) collective-permute-start(bf16[512,128]{1,0:T(8,128)(2,1)S(1)} %get-tuple-element.41), channel_id=1, source_target_pairs={{0,2},{1,3},{2,0},{3,1},{4,6},{5,7},{6,4},{7,5},{8,10},{9,11},{10,... | collective-permute-start | bytes 393224 | tf_op jit(solution)/shard_map/ppermute | solution.py:282
  10.5 2.5 %collective-permute-start.4 = (bf16[512,128]{1,0:T(8,128)(2,1)S(1)}, bf16[512,128]{1,0:T(8,128)(2,1)S(1)}, u32[]{:S(2)}, u32[]{:S(2)}) collective-permute-start(bf16[512,128]{1,0:T(8,128)(2,1)S(1)} %get-tuple-element.42), channel_id=1, source_target_pairs={{0,6},{1,7},{2,4},{3,5},{4,2},{5,3},{6,0},{7,1},{8,14},{9,15},{10,... | collective-permute-start | bytes 393224 | tf_op jit(solution)/shard_map/ppermute | solution.py:282
  13.0 4.8 %collective-permute-done.refs_0_ = bf16[512,128]{1,0:T(8,128)(2,1)S(1)} collective-permute-done((bf16[512,128]{1,0:T(8,128)(2,1)S(1)}, bf16[512,128]{1,0:T(8,128)(2,1)S(1)}, u32[]{:S(2)}, u32[]{:S(2)}) %collective-permute-start) | collective-permute-done | bytes 131104 | tf_op jit(solution)/shard_map/ppermute | solution.py:282
  17.8 5.9 %collective-permute-start.5 = (bf16[512,128]{1,0:T(8,128)(2,1)S(1)}, bf16[512,128]{1,0:T(8,128)(2,1)S(1)}, u32[]{:S(2)}, u32[]{:S(2)}) collective-permute-start(bf16[512,128]{1,0:T(8,128)(2,1)S(1)} %get-tuple-element.43), channel_id=1, source_target_pairs={{0,7},{1,6},{2,5},{3,4},{4,3},{5,2},{6,1},{7,0},{8,15},{9,14},{10,... | collective-permute-start | bytes 393224 | tf_op jit(solution)/shard_map/ppermute | solution.py:282
  23.8 0.0 collective-permute-done.1.refs_1_
  23.8 0.0 collective-permute-start.6
  23.8 0.0 copy-done
  23.8 0.0 copy-start.2
  23.8 1.6 %copy-done.2 = f32[512,1024]{1,0:T(8,128)S(1)} copy-done((f32[512,1024]{1,0:T(8,128)S(1)}, f32[512,1024]{1,0:T(8,128)}, u32[]{:S(2)}) %copy-start.2) | copy-done | bytes 2097176
  25.4 0.0 copy-start.1
  25.4 2.1 %shard_map.78 = (bf16[512,128]{1,0:T(8,128)(2,1)S(1)}, bf16[512,128]{1,0:T(8,128)(2,1)S(1)}, bf16[512,128]{1,0:T(8,128)(2,1)S(1)}, bf16[512,128]{1,0:T(8,128)(2,...) custom-call(s32[2]{0:T(128)S(1)} %pad_add_fusion.where, ...), custom_call_target="tpu_custom_call" | custom-call | flops 603979776 | bytes 7733256 | tf_op jit(solution)/shard_map/pallas_call | solution.py:257
  27.5 0.0 collective-permute-done.2.refs_2_
  27.5 0.6 collective-permute-start.14
  28.1 0.0 collective-permute-done.3.refs_3_
  28.1 2.3 %collective-permute-start.15 = (bf16[512,128]{1,0:T(8,128)(2,1)S(1)}, bf16[512,128]{1,0:T(8,128)(2,1)S(1)}, u32[]{:S(2)}, u32[]{:S(2)}) collective-permute-start(bf16[512,128]{1,0:T(8,128)(2,1)S(1)} %get-tuple-element.60), channel_id=1, source_target_pairs={{0,5},{1,4},{2,7},{3,6},{4,1},{5,0},{6,3},{7,2},{8,13},{9,12},{10,... | collective-permute-start | bytes 393224 | tf_op jit(solution)/shard_map/ppermute | solution.py:282
  30.4 0.0 collective-permute-done.4.refs_4_
  30.4 2.5 %collective-permute-start.16 = (bf16[512,128]{1,0:T(8,128)(2,1)S(1)}, bf16[512,128]{1,0:T(8,128)(2,1)S(1)}, u32[]{:S(2)}, u32[]{:S(2)}) collective-permute-start(bf16[512,128]{1,0:T(8,128)(2,1)S(1)} %get-tuple-element.61), channel_id=1, source_target_pairs={{0,6},{1,7},{2,4},{3,5},{4,2},{5,3},{6,0},{7,1},{8,14},{9,15},{10,... | collective-permute-start | bytes 393224 | tf_op jit(solution)/shard_map/ppermute | solution.py:282
  32.9 0.0 collective-permute-done.5.refs_5_
  32.9 0.0 collective-permute-done.6.refs_6_
  32.9 0.0 copy-done.1
  32.9 4.3 %shard_map.79 = (bf16[512,128]{1,0:T(8,128)(2,1)S(1)}, bf16[512,128]{1,0:T(8,128)(2,1)S(1)}, bf16[512,128]{1,0:T(8,128)(2,1)S(1)}, bf16[512,128]{1,0:T(8,128)(2,...) custom-call(s32[2]{0:T(128)S(1)} %pad_add_fusion.where, ...), custom_call_target="tpu_custom_call", output_to_operand_aliasing={{0}: (9, {}), {1}: (10, {}), {2}: (11, {}), {3}: (12, {})} | custom-call | flops 1207959552 | bytes 10223624 | tf_op jit(solution)/shard_map/pallas_call | solution.py:257
  37.2 2.3 %collective-permute-start.17 = (bf16[512,128]{1,0:T(8,128)(2,1)S(1)}, bf16[512,128]{1,0:T(8,128)(2,1)S(1)}, u32[]{:S(2)}, u32[]{:S(2)}) collective-permute-start(bf16[512,128]{1,0:T(8,128)(2,1)S(1)} %get-tuple-element.62), channel_id=1, source_target_pairs={{0,7},{1,6},{2,5},{3,4},{4,3},{5,2},{6,1},{7,0},{8,15},{9,14},{10,... | collective-permute-start | bytes 393224 | tf_op jit(solution)/shard_map/ppermute | solution.py:282
  39.6 0.5 collective-permute-start.18
  40.1 5.1 %collective-permute-done.14.refs_0_ = bf16[512,128]{1,0:T(8,128)(2,1)S(1)} collective-permute-done((bf16[512,128]{1,0:T(8,128)(2,1)S(1)}, bf16[512,128]{1,0:T(8,128)(2,1)S(1)}, u32[]{:S(2)}, u32[]{:S(2)}) %collective-permute-start.14) | collective-permute-done | bytes 131104 | tf_op jit(solution)/shard_map/ppermute | solution.py:282
  45.2 5.0 %collective-permute-start.19 = (bf16[512,128]{1,0:T(8,128)(2,1)S(1)}, bf16[512,128]{1,0:T(8,128)(2,1)S(1)}, u32[]{:S(2)}, u32[]{:S(2)}) collective-permute-start(bf16[512,128]{1,0:T(8,128)(2,1)S(1)} %get-tuple-element.64), channel_id=1, source_target_pairs={{0,2},{1,3},{2,0},{3,1},{4,6},{5,7},{6,4},{7,5},{8,10},{9,11},{10,... | collective-permute-start | bytes 393224 | tf_op jit(solution)/shard_map/ppermute | solution.py:282
  50.2 0.0 collective-permute-done.15.refs_1_
  50.2 0.0 collective-permute-start.20
  50.2 0.0 collective-permute-done.16.refs_2_
  50.2 1.5 %collective-permute-start.7 = (bf16[512,128]{1,0:T(8,128)(2,1)S(1)}, bf16[512,128]{1,0:T(8,128)(2,1)S(1)}, u32[]{:S(2)}, u32[]{:S(2)}) collective-permute-start(bf16[512,128]{1,0:T(8,128)(2,1)S(1)} %get-tuple-element.51), channel_id=1, source_target_pairs={{0,1},{1,0},{2,3},{3,2},{4,5},{5,4},{6,7},{7,6},{8,9},{9,8},{10,11... | collective-permute-start | bytes 393224 | tf_op jit(solution)/shard_map/ppermute | solution.py:282
  51.8 0.0 collective-permute-done.17.refs_3_
  51.8 6.8 %collective-permute-start.8 = (bf16[512,128]{1,0:T(8,128)(2,1)S(1)}, bf16[512,128]{1,0:T(8,128)(2,1)S(1)}, u32[]{:S(2)}, u32[]{:S(2)}) collective-permute-start(bf16[512,128]{1,0:T(8,128)(2,1)S(1)} %get-tuple-element.52), channel_id=1, source_target_pairs={{0,4},{1,5},{2,6},{3,7},{4,0},{5,1},{6,2},{7,3},{8,12},{9,13},{10,... | collective-permute-start | bytes 393224 | tf_op jit(solution)/shard_map/ppermute | solution.py:282
  58.6 0.0 collective-permute-done.18.refs_4_
  58.6 1.2 %collective-permute-start.9 = (bf16[512,128]{1,0:T(8,128)(2,1)S(1)}, bf16[512,128]{1,0:T(8,128)(2,1)S(1)}, u32[]{:S(2)}, u32[]{:S(2)}) collective-permute-start(bf16[512,128]{1,0:T(8,128)(2,1)S(1)} %get-tuple-element.53), channel_id=1, source_target_pairs={{0,2},{1,3},{2,0},{3,1},{4,6},{5,7},{6,4},{7,5},{8,10},{9,11},{10,... | collective-permute-start | bytes 393224 | tf_op jit(solution)/shard_map/ppermute | solution.py:282
  59.8 0.0 collective-permute-done.19.refs_5_
  59.8 1.1 %collective-permute-start.10 = (bf16[512,128]{1,0:T(8,128)(2,1)S(1)}, bf16[512,128]{1,0:T(8,128)(2,1)S(1)}, u32[]{:S(2)}, u32[]{:S(2)}) collective-permute-start(bf16[512,128]{1,0:T(8,128)(2,1)S(1)} %get-tuple-element.54), channel_id=1, source_target_pairs={{0,5},{1,4},{2,7},{3,6},{4,1},{5,0},{6,3},{7,2},{8,13},{9,12},{10,... | collective-permute-start | bytes 393224 | tf_op jit(solution)/shard_map/ppermute | solution.py:282
  60.9 0.0 collective-permute-done.20.refs_6_
  60.9 2.1 %collective-permute-start.11 = (bf16[512,128]{1,0:T(8,128)(2,1)S(1)}, bf16[512,128]{1,0:T(8,128)(2,1)S(1)}, u32[]{:S(2)}, u32[]{:S(2)}) collective-permute-start(bf16[512,128]{1,0:T(8,128)(2,1)S(1)} %get-tuple-element.55), channel_id=1, source_target_pairs={{0,6},{1,7},{2,4},{3,5},{4,2},{5,3},{6,0},{7,1},{8,14},{9,15},{10,... | collective-permute-start | bytes 393224 | tf_op jit(solution)/shard_map/ppermute | solution.py:282
  63.0 4.1 %shard_map.80 = (bf16[512,256]{1,0:T(8,128)(2,1)S(1)}, bf16[512,256]{1,0:T(8,128)(2,1)S(1)}, bf16[512,256]{1,0:T(8,128)(2,1)S(1)}, bf16[512,256]{1,0:T(8,128)(2,1)S(1)}) custom-call(s32[2]{0:T(128)S(1)} %pad_add_fusion.where, bf16[512,128]{1,0:T(8,128)(2,1)S(1)} %collective-permute-done.14.refs_0_, bf16[512,128]{1,0:T(8,128)(2,1)S(1)} %collective-permute-done.15.refs_1_, ...), custom_call_target="tpu_custom_call" | custom-call | flops 1207959552 | bytes 6815752 | tf_op jit(solution)/shard_map/pallas_call | solution.py:257
  67.1 0.0 collective-permute-done.7.refs_0_
  67.1 1.5 %collective-permute-start.21 = (bf16[512,256]{1,0:T(8,128)(2,1)S(1)}, bf16[512,256]{1,0:T(8,128)(2,1)S(1)}, u32[]{:S(2)}, u32[]{:S(2)}) collective-permute-start(bf16[512,256]{1,0:T(8,128)(2,1)S(1)} %get-tuple-element.68), channel_id=1, source_target_pairs={{0,16},{8,24},{16,0},{24,8},{1,17},{9,25},{17,1},{25,9},{2,18},{10... | collective-permute-start | bytes 786440 | tf_op jit(solution)/shard_map/ppermute | solution.py:282
  68.6 0.0 collective-permute-done.8.refs_1_
  68.6 0.0 collective-permute-start.22
  68.6 0.0 collective-permute-done.9.refs_2_
  68.7 0.7 collective-permute-start.23
  69.3 3.4 %collective-permute-done.10.refs_3_ = bf16[512,128]{1,0:T(8,128)(2,1)S(1)} collective-permute-done((bf16[512,128]{1,0:T(8,128)(2,1)S(1)}, bf16[512,128]{1,0:T(8,128)(2,1)S(1)}, u32[]{:S(2)}, u32[]{:S(2)}) %collective-permute-start.10) | collective-permute-done | bytes 131104 | tf_op jit(solution)/shard_map/ppermute | solution.py:282
  72.7 3.4 %collective-permute-start.12 = (bf16[512,128]{1,0:T(8,128)(2,1)S(1)}, bf16[512,128]{1,0:T(8,128)(2,1)S(1)}, u32[]{:S(2)}, u32[]{:S(2)}) collective-permute-start(bf16[512,128]{1,0:T(8,128)(2,1)S(1)} %get-tuple-element.56), channel_id=1, source_target_pairs={{0,7},{1,6},{2,5},{3,4},{4,3},{5,2},{6,1},{7,0},{8,15},{9,14},{10,... | collective-permute-start | bytes 393224 | tf_op jit(solution)/shard_map/ppermute | solution.py:282
  76.2 0.0 collective-permute-done.11.refs_4_
  76.2 0.0 collective-permute-start.13
  76.2 5.6 %collective-permute-done.12.refs_5_ = bf16[512,128]{1,0:T(8,128)(2,1)S(1)} collective-permute-done((bf16[512,128]{1,0:T(8,128)(2,1)S(1)}, bf16[512,128]{1,0:T(8,128)(2,1)S(1)}, u32[]{:S(2)}, u32[]{:S(2)}) %collective-permute-start.12) | collective-permute-done | bytes 131104 | tf_op jit(solution)/shard_map/ppermute | solution.py:282
  81.8 0.8 collective-permute-done.13.refs_6_
  82.6 0.0 collective-permute-done.21.refs_8_
  82.6 0.0 collective-permute-done.22.refs_9_
  82.6 0.0 collective-permute-done.23.refs_10_
  82.6 1.8 %shard_map.81 = (bf16[8,512,128]{2,1,0:T(8,128)(2,1)}, f32[512,256]{1,0:T(8,128)}) custom-call(s32[2]{0:T(128)S(1)} %pad_add_fusion.where, bf16[512,128]{1,0:T(8,128)(2,1)S(1)} %collective-permute-done.7.refs_0_, bf16[512,128]{1,0:T(8,128)(2,1)S(1)} %collective-permute-done.8.refs_1_, bf16[512,128]{1,0:T(8,128)(2,1)S(1)} %collective-permute-done.9.refs_2_, ...), custom_call_target="tpu_custom_call" | custom-call | bytes 3670024 | tf_op jit(solution)/shard_map/pallas_call | solution.py:257
Async XLA Ops:
  0.6 23.1 %copy-start = (bf16[9,256,256]{2,1,0:T(8,128)(2,1)S(1)}, bf16[9,256,256]{2,1,0:T(8,128)(2,1)}, u32[]{:S(2)}) copy-start(bf16[9,256,256]{2,1,0:T(8,128)(2,1)} %constant.12.clone.forward.refs_13_.refs_9_) | copy-start | bytes 3538948
  3.0 14.8 %collective-permute-start = (bf16[512,128]{1,0:T(8,128)(2,1)S(1)}, bf16[512,128]{1,0:T(8,128)(2,1)S(1)}, u32[]{:S(2)}, u32[]{:S(2)}) collective-permute-start(bf16[512,128]{1,0:T(8,128)(2,1)S(1)} %get-tuple-element.38), channel_id=1, source_target_pairs={{0,4},{1,5},{2,6},{3,7},{4,0},{5,1},{6,2},{7,3},{8,12},{9,13},{10,... | collective-permute-start | bytes 393224 | tf_op jit(solution)/shard_map/ppermute | solution.py:282
  7.1 16.6 %collective-permute-start.1 = (bf16[512,128]{1,0:T(8,128)(2,1)S(1)}, bf16[512,128]{1,0:T(8,128)(2,1)S(1)}, u32[]{:S(2)}, u32[]{:S(2)}) collective-permute-start(bf16[512,128]{1,0:T(8,128)(2,1)S(1)} %get-tuple-element.39), channel_id=1, source_target_pairs={{0,1},{1,0},{2,3},{3,2},{4,5},{5,4},{6,7},{7,6},{8,9},{9,8},{10,11... | collective-permute-start | bytes 393224 | tf_op jit(solution)/shard_map/ppermute | solution.py:282
  8.7 18.8 %collective-permute-start.2 = (bf16[512,128]{1,0:T(8,128)(2,1)S(1)}, bf16[512,128]{1,0:T(8,128)(2,1)S(1)}, u32[]{:S(2)}, u32[]{:S(2)}) collective-permute-start(bf16[512,128]{1,0:T(8,128)(2,1)S(1)} %get-tuple-element.40), channel_id=1, source_target_pairs={{0,5},{1,4},{2,7},{3,6},{4,1},{5,0},{6,3},{7,2},{8,13},{9,12},{10,... | collective-permute-start | bytes 393224 | tf_op jit(solution)/shard_map/ppermute | solution.py:282
  8.7 19.4 %collective-permute-start.3 = (bf16[512,128]{1,0:T(8,128)(2,1)S(1)}, bf16[512,128]{1,0:T(8,128)(2,1)S(1)}, u32[]{:S(2)}, u32[]{:S(2)}) collective-permute-start(bf16[512,128]{1,0:T(8,128)(2,1)S(1)} %get-tuple-element.41), channel_id=1, source_target_pairs={{0,2},{1,3},{2,0},{3,1},{4,6},{5,7},{6,4},{7,5},{8,10},{9,11},{10,... | collective-permute-start | bytes 393224 | tf_op jit(solution)/shard_map/ppermute | solution.py:282
  10.5 19.9 %collective-permute-start.4 = (bf16[512,128]{1,0:T(8,128)(2,1)S(1)}, bf16[512,128]{1,0:T(8,128)(2,1)S(1)}, u32[]{:S(2)}, u32[]{:S(2)}) collective-permute-start(bf16[512,128]{1,0:T(8,128)(2,1)S(1)} %get-tuple-element.42), channel_id=1, source_target_pairs={{0,6},{1,7},{2,4},{3,5},{4,2},{5,3},{6,0},{7,1},{8,14},{9,15},{10,... | collective-permute-start | bytes 393224 | tf_op jit(solution)/shard_map/ppermute | solution.py:282
  17.8 15.1 %collective-permute-start.5 = (bf16[512,128]{1,0:T(8,128)(2,1)S(1)}, bf16[512,128]{1,0:T(8,128)(2,1)S(1)}, u32[]{:S(2)}, u32[]{:S(2)}) collective-permute-start(bf16[512,128]{1,0:T(8,128)(2,1)S(1)} %get-tuple-element.43), channel_id=1, source_target_pairs={{0,7},{1,6},{2,5},{3,4},{4,3},{5,2},{6,1},{7,0},{8,15},{9,14},{10,... | collective-permute-start | bytes 393224 | tf_op jit(solution)/shard_map/ppermute | solution.py:282
  23.8 9.2 %collective-permute-start.6 = (bf16[512,128]{1,0:T(8,128)(2,1)S(1)}, bf16[512,128]{1,0:T(8,128)(2,1)S(1)}, u32[]{:S(2)}, u32[]{:S(2)}) collective-permute-start(bf16[512,128]{1,0:T(8,128)(2,1)S(1)} %get-tuple-element.44), channel_id=1, source_target_pairs={{0,3},{1,2},{2,1},{3,0},{4,7},{5,6},{6,5},{7,4},{8,11},{9,10},{10,... | collective-permute-start | bytes 393224 | tf_op jit(solution)/shard_map/ppermute | solution.py:282
  23.8 1.6 %copy-start.2 = (f32[512,1024]{1,0:T(8,128)S(1)}, f32[512,1024]{1,0:T(8,128)}, u32[]{:S(2)}) copy-start(f32[512,1024]{1,0:T(8,128)} %taps.1) | copy-start | bytes 6291460
  25.4 7.6 %copy-start.1 = (bf16[9,256,256]{2,1,0:T(8,128)(2,1)S(1)}, bf16[9,256,256]{2,1,0:T(8,128)(2,1)}, u32[]{:S(2)}) copy-start(bf16[9,256,256]{2,1,0:T(8,128)(2,1)} %constant.13.clone.refs_14_.refs_10_) | copy-start | bytes 3538948
  27.5 17.7 %collective-permute-start.14 = (bf16[512,128]{1,0:T(8,128)(2,1)S(1)}, bf16[512,128]{1,0:T(8,128)(2,1)S(1)}, u32[]{:S(2)}, u32[]{:S(2)}) collective-permute-start(bf16[512,128]{1,0:T(8,128)(2,1)S(1)} %get-tuple-element.59), channel_id=1, source_target_pairs={{0,4},{1,5},{2,6},{3,7},{4,0},{5,1},{6,2},{7,3},{8,12},{9,13},{10,... | collective-permute-start | bytes 393224 | tf_op jit(solution)/shard_map/ppermute | solution.py:282
  28.1 22.1 %collective-permute-start.15 = (bf16[512,128]{1,0:T(8,128)(2,1)S(1)}, bf16[512,128]{1,0:T(8,128)(2,1)S(1)}, u32[]{:S(2)}, u32[]{:S(2)}) collective-permute-start(bf16[512,128]{1,0:T(8,128)(2,1)S(1)} %get-tuple-element.60), channel_id=1, source_target_pairs={{0,5},{1,4},{2,7},{3,6},{4,1},{5,0},{6,3},{7,2},{8,13},{9,12},{10,... | collective-permute-start | bytes 393224 | tf_op jit(solution)/shard_map/ppermute | solution.py:282
  30.4 19.8 %collective-permute-start.16 = (bf16[512,128]{1,0:T(8,128)(2,1)S(1)}, bf16[512,128]{1,0:T(8,128)(2,1)S(1)}, u32[]{:S(2)}, u32[]{:S(2)}) collective-permute-start(bf16[512,128]{1,0:T(8,128)(2,1)S(1)} %get-tuple-element.61), channel_id=1, source_target_pairs={{0,6},{1,7},{2,4},{3,5},{4,2},{5,3},{6,0},{7,1},{8,14},{9,15},{10,... | collective-permute-start | bytes 393224 | tf_op jit(solution)/shard_map/ppermute | solution.py:282
  37.2 14.6 %collective-permute-start.17 = (bf16[512,128]{1,0:T(8,128)(2,1)S(1)}, bf16[512,128]{1,0:T(8,128)(2,1)S(1)}, u32[]{:S(2)}, u32[]{:S(2)}) collective-permute-start(bf16[512,128]{1,0:T(8,128)(2,1)S(1)} %get-tuple-element.62), channel_id=1, source_target_pairs={{0,7},{1,6},{2,5},{3,4},{4,3},{5,2},{6,1},{7,0},{8,15},{9,14},{10,... | collective-permute-start | bytes 393224 | tf_op jit(solution)/shard_map/ppermute | solution.py:282
  39.6 19.0 %collective-permute-start.18 = (bf16[512,128]{1,0:T(8,128)(2,1)S(1)}, bf16[512,128]{1,0:T(8,128)(2,1)S(1)}, u32[]{:S(2)}, u32[]{:S(2)}) collective-permute-start(bf16[512,128]{1,0:T(8,128)(2,1)S(1)} %get-tuple-element.63), channel_id=1, source_target_pairs={{0,1},{1,0},{2,3},{3,2},{4,5},{5,4},{6,7},{7,6},{8,9},{9,8},{10,11... | collective-permute-start | bytes 393224 | tf_op jit(solution)/shard_map/ppermute | solution.py:282
  45.2 14.6 %collective-permute-start.19 = (bf16[512,128]{1,0:T(8,128)(2,1)S(1)}, bf16[512,128]{1,0:T(8,128)(2,1)S(1)}, u32[]{:S(2)}, u32[]{:S(2)}) collective-permute-start(bf16[512,128]{1,0:T(8,128)(2,1)S(1)} %get-tuple-element.64), channel_id=1, source_target_pairs={{0,2},{1,3},{2,0},{3,1},{4,6},{5,7},{6,4},{7,5},{8,10},{9,11},{10,... | collective-permute-start | bytes 393224 | tf_op jit(solution)/shard_map/ppermute | solution.py:282
  50.2 10.7 %collective-permute-start.20 = (bf16[512,128]{1,0:T(8,128)(2,1)S(1)}, bf16[512,128]{1,0:T(8,128)(2,1)S(1)}, u32[]{:S(2)}, u32[]{:S(2)}) collective-permute-start(bf16[512,128]{1,0:T(8,128)(2,1)S(1)} %get-tuple-element.65), channel_id=1, source_target_pairs={{0,3},{1,2},{2,1},{3,0},{4,7},{5,6},{6,5},{7,4},{8,11},{9,10},{10,... | collective-permute-start | bytes 393224 | tf_op jit(solution)/shard_map/ppermute | solution.py:282
  50.2 16.9 %collective-permute-start.7 = (bf16[512,128]{1,0:T(8,128)(2,1)S(1)}, bf16[512,128]{1,0:T(8,128)(2,1)S(1)}, u32[]{:S(2)}, u32[]{:S(2)}) collective-permute-start(bf16[512,128]{1,0:T(8,128)(2,1)S(1)} %get-tuple-element.51), channel_id=1, source_target_pairs={{0,1},{1,0},{2,3},{3,2},{4,5},{5,4},{6,7},{7,6},{8,9},{9,8},{10,11... | collective-permute-start | bytes 393224 | tf_op jit(solution)/shard_map/ppermute | solution.py:282
  51.8 16.9 %collective-permute-start.8 = (bf16[512,128]{1,0:T(8,128)(2,1)S(1)}, bf16[512,128]{1,0:T(8,128)(2,1)S(1)}, u32[]{:S(2)}, u32[]{:S(2)}) collective-permute-start(bf16[512,128]{1,0:T(8,128)(2,1)S(1)} %get-tuple-element.52), channel_id=1, source_target_pairs={{0,4},{1,5},{2,6},{3,7},{4,0},{5,1},{6,2},{7,3},{8,12},{9,13},{10,... | collective-permute-start | bytes 393224 | tf_op jit(solution)/shard_map/ppermute | solution.py:282
  58.6 10.1 %collective-permute-start.9 = (bf16[512,128]{1,0:T(8,128)(2,1)S(1)}, bf16[512,128]{1,0:T(8,128)(2,1)S(1)}, u32[]{:S(2)}, u32[]{:S(2)}) collective-permute-start(bf16[512,128]{1,0:T(8,128)(2,1)S(1)} %get-tuple-element.53), channel_id=1, source_target_pairs={{0,2},{1,3},{2,0},{3,1},{4,6},{5,7},{6,4},{7,5},{8,10},{9,11},{10,... | collective-permute-start | bytes 393224 | tf_op jit(solution)/shard_map/ppermute | solution.py:282
  59.8 12.9 %collective-permute-start.10 = (bf16[512,128]{1,0:T(8,128)(2,1)S(1)}, bf16[512,128]{1,0:T(8,128)(2,1)S(1)}, u32[]{:S(2)}, u32[]{:S(2)}) collective-permute-start(bf16[512,128]{1,0:T(8,128)(2,1)S(1)} %get-tuple-element.54), channel_id=1, source_target_pairs={{0,5},{1,4},{2,7},{3,6},{4,1},{5,0},{6,3},{7,2},{8,13},{9,12},{10,... | collective-permute-start | bytes 393224 | tf_op jit(solution)/shard_map/ppermute | solution.py:282
  60.9 15.3 %collective-permute-start.11 = (bf16[512,128]{1,0:T(8,128)(2,1)S(1)}, bf16[512,128]{1,0:T(8,128)(2,1)S(1)}, u32[]{:S(2)}, u32[]{:S(2)}) collective-permute-start(bf16[512,128]{1,0:T(8,128)(2,1)S(1)} %get-tuple-element.55), channel_id=1, source_target_pairs={{0,6},{1,7},{2,4},{3,5},{4,2},{5,3},{6,0},{7,1},{8,14},{9,15},{10,... | collective-permute-start | bytes 393224 | tf_op jit(solution)/shard_map/ppermute | solution.py:282
  67.1 15.5 %collective-permute-start.21 = (bf16[512,256]{1,0:T(8,128)(2,1)S(1)}, bf16[512,256]{1,0:T(8,128)(2,1)S(1)}, u32[]{:S(2)}, u32[]{:S(2)}) collective-permute-start(bf16[512,256]{1,0:T(8,128)(2,1)S(1)} %get-tuple-element.68), channel_id=1, source_target_pairs={{0,16},{8,24},{16,0},{24,8},{1,17},{9,25},{17,1},{25,9},{2,18},{10... | collective-permute-start | bytes 786440 | tf_op jit(solution)/shard_map/ppermute | solution.py:282
  68.6 14.0 %collective-permute-start.22 = (bf16[512,256]{1,0:T(8,128)(2,1)S(1)}, bf16[512,256]{1,0:T(8,128)(2,1)S(1)}, u32[]{:S(2)}, u32[]{:S(2)}) collective-permute-start(bf16[512,256]{1,0:T(8,128)(2,1)S(1)} %get-tuple-element.69), channel_id=1, source_target_pairs={{0,24},{8,16},{16,8},{24,0},{1,25},{9,17},{17,9},{25,1},{2,26},{10... | collective-permute-start | bytes 786440 | tf_op jit(solution)/shard_map/ppermute | solution.py:282
  68.7 14.0 %collective-permute-start.23 = (bf16[512,256]{1,0:T(8,128)(2,1)S(1)}, bf16[512,256]{1,0:T(8,128)(2,1)S(1)}, u32[]{:S(2)}, u32[]{:S(2)}) collective-permute-start(bf16[512,256]{1,0:T(8,128)(2,1)S(1)} %get-tuple-element.70), channel_id=1, source_target_pairs={{0,8},{8,0},{16,24},{24,16},{1,9},{9,1},{17,25},{25,17},{2,10},{10... | collective-permute-start | bytes 786440 | tf_op jit(solution)/shard_map/ppermute | solution.py:282
  72.7 9.1 %collective-permute-start.12 = (bf16[512,128]{1,0:T(8,128)(2,1)S(1)}, bf16[512,128]{1,0:T(8,128)(2,1)S(1)}, u32[]{:S(2)}, u32[]{:S(2)}) collective-permute-start(bf16[512,128]{1,0:T(8,128)(2,1)S(1)} %get-tuple-element.56), channel_id=1, source_target_pairs={{0,7},{1,6},{2,5},{3,4},{4,3},{5,2},{6,1},{7,0},{8,15},{9,14},{10,... | collective-permute-start | bytes 393224 | tf_op jit(solution)/shard_map/ppermute | solution.py:282
  76.2 6.4 %collective-permute-start.13 = (bf16[512,128]{1,0:T(8,128)(2,1)S(1)}, bf16[512,128]{1,0:T(8,128)(2,1)S(1)}, u32[]{:S(2)}, u32[]{:S(2)}) collective-permute-start(bf16[512,128]{1,0:T(8,128)(2,1)S(1)} %get-tuple-element.57), channel_id=1, source_target_pairs={{0,3},{1,2},{2,1},{3,0},{4,7},{5,6},{6,5},{7,4},{8,11},{9,10},{10,... | collective-permute-start | bytes 393224 | tf_op jit(solution)/shard_map/ppermute | solution.py:282

commit v26 on v20

--- a/solution.py
+++ b/solution.py
@@ -315,7 +315,7 @@
     grad_blocks = exchange(grad_pieces, grad_order, "ctx", count)
     *input_pieces, taps_spec = call(
         functools.partial(taps_kernel, input_order),
-        [where, stay[2], long_filter, forward],
+        [where, stay[2], pltpu.with_memory_space_constraint(long_filter, pltpu.HBM), forward],
         [piece] * count + [spec],
         [mid, sems((count,))],
         flops=work,

time: 81.2 us -> 81.2 us (level)
  waiting for transfers between devices: 18.1 us -> 20.1 us
  starting transfers between devices: 46 us -> 44.3 us
  local copies, waits for them, and re-layouts: 1.6 us -> 0.01 us
  Pallas kernels: 14.6 us -> 15.8 us
    ppermute x24, waiting for transfers between devices: 18.1 us -> 20.1 us  [exchange(): lax.ppermute(piece, axis, [(i, i ^ k) for i in range(size)])]
    ppermute x24, starting transfers between devices: 46 us -> 44.3 us  [exchange(): lax.ppermute(piece, axis, [(i, i ^ k) for i in range(size)])]
    unnamed x6 -> x4, local copies, waits for them, and re-layouts: 1.6 us -> 0.01 us
    pallas_call x5, Pallas kernels: 14.6 us -> 15.8 us  [call(): pl.pallas_call(kernel, out_shape=list(outs), in_specs=specs, out_specs=[s...]
  transfers between devices with their start and end apart: 24 -> 24, of which waited for: 6 -> 6; matrix products, arithmetic and copies ran while one was open for 0% -> 0% of each run, Pallas kernels for 13% -> 14%
where the time goes in v26:
time: 81.2 us; the launch traced here: 81.1 us
  starting transfers between devices  44.3 us (55%)
  waiting for transfers between devices  20.1 us (25%)
  Pallas kernels  15.8 us (19%)
    ppermute x24, starting transfers between devices, exchange(): lax.ppermute(piece, axis, [(i, i ^ k) for i in range(size)])  44.3 us
    ppermute x24, waiting for transfers between devices, exchange(): lax.ppermute(piece, axis, [(i, i ^ k) for i in range(size)])  20.1 us
    pallas_call x5, Pallas kernels, call(): pl.pallas_call(kernel, out_shape=list(outs), in_specs=specs, out_specs=[s...  15.8 us
  transfers between devices with their start and end apart: 24, of which 6 were waited for; matrix products, arithmetic and copies ran while one was open for 0% of the time, Pallas kernels for 14%

profile of v26, /device:TPU:0, one launch (start us, length us, event | category | flops | bytes accessed | tf_op | source)
XLA Modules:
  0.0 81.1 jit_solution(229199809339243450)
XLA Ops:
  0.6 0.0 copy-start
  0.6 0.1 pad_add_fusion.where
  0.7 2.3 %shard_map.77 = (bf16[512,128]{1,0:T(8,128)(2,1)S(1)}, bf16[512,128]{1,0:T(8,128)(2,1)S(1)}, bf16[512,128]{1,0:T(8,128)(2,1)S(1)}, bf16[512,128]{1,0:T(8,128)(2,...) custom-call(s32[2]{0:T(128)S(1)} %pad_add_fusion.where, ...), custom_call_target="tpu_custom_call" | custom-call | bytes 3145736 | tf_op jit(solution)/shard_map/pallas_call | solution.py:257
  3.0 4.1 %collective-permute-start = (bf16[512,128]{1,0:T(8,128)(2,1)S(1)}, bf16[512,128]{1,0:T(8,128)(2,1)S(1)}, u32[]{:S(2)}, u32[]{:S(2)}) collective-permute-start(bf16[512,128]{1,0:T(8,128)(2,1)S(1)} %get-tuple-element.37), channel_id=1, source_target_pairs={{0,4},{1,5},{2,6},{3,7},{4,0},{5,1},{6,2},{7,3},{8,12},{9,13},{10,... | collective-permute-start | bytes 393224 | tf_op jit(solution)/shard_map/ppermute | solution.py:282
  7.1 1.5 %collective-permute-start.1 = (bf16[512,128]{1,0:T(8,128)(2,1)S(1)}, bf16[512,128]{1,0:T(8,128)(2,1)S(1)}, u32[]{:S(2)}, u32[]{:S(2)}) collective-permute-start(bf16[512,128]{1,0:T(8,128)(2,1)S(1)} %get-tuple-element.38), channel_id=1, source_target_pairs={{0,1},{1,0},{2,3},{3,2},{4,5},{5,4},{6,7},{7,6},{8,9},{9,8},{10,11... | collective-permute-start | bytes 393224 | tf_op jit(solution)/shard_map/ppermute | solution.py:282
  8.7 0.0 collective-permute-start.2
  8.7 1.8 %collective-permute-start.3 = (bf16[512,128]{1,0:T(8,128)(2,1)S(1)}, bf16[512,128]{1,0:T(8,128)(2,1)S(1)}, u32[]{:S(2)}, u32[]{:S(2)}) collective-permute-start(bf16[512,128]{1,0:T(8,128)(2,1)S(1)} %get-tuple-element.40), channel_id=1, source_target_pairs={{0,2},{1,3},{2,0},{3,1},{4,6},{5,7},{6,4},{7,5},{8,10},{9,11},{10,... | collective-permute-start | bytes 393224 | tf_op jit(solution)/shard_map/ppermute | solution.py:282
  10.5 2.5 %collective-permute-start.4 = (bf16[512,128]{1,0:T(8,128)(2,1)S(1)}, bf16[512,128]{1,0:T(8,128)(2,1)S(1)}, u32[]{:S(2)}, u32[]{:S(2)}) collective-permute-start(bf16[512,128]{1,0:T(8,128)(2,1)S(1)} %get-tuple-element.41), channel_id=1, source_target_pairs={{0,6},{1,7},{2,4},{3,5},{4,2},{5,3},{6,0},{7,1},{8,14},{9,15},{10,... | collective-permute-start | bytes 393224 | tf_op jit(solution)/shard_map/ppermute | solution.py:282
  13.0 4.8 %collective-permute-done.refs_0_ = bf16[512,128]{1,0:T(8,128)(2,1)S(1)} collective-permute-done((bf16[512,128]{1,0:T(8,128)(2,1)S(1)}, bf16[512,128]{1,0:T(8,128)(2,1)S(1)}, u32[]{:S(2)}, u32[]{:S(2)}) %collective-permute-start) | collective-permute-done | bytes 131104 | tf_op jit(solution)/shard_map/ppermute | solution.py:282
  17.8 5.9 %collective-permute-start.5 = (bf16[512,128]{1,0:T(8,128)(2,1)S(1)}, bf16[512,128]{1,0:T(8,128)(2,1)S(1)}, u32[]{:S(2)}, u32[]{:S(2)}) collective-permute-start(bf16[512,128]{1,0:T(8,128)(2,1)S(1)} %get-tuple-element.42), channel_id=1, source_target_pairs={{0,7},{1,6},{2,5},{3,4},{4,3},{5,2},{6,1},{7,0},{8,15},{9,14},{10,... | collective-permute-start | bytes 393224 | tf_op jit(solution)/shard_map/ppermute | solution.py:282
  23.8 0.0 collective-permute-done.1.refs_1_
  23.8 0.0 collective-permute-start.6
  23.8 0.0 copy-done
  23.8 0.0 copy-start.1
  23.8 3.3 %shard_map.78 = (bf16[512,128]{1,0:T(8,128)(2,1)S(1)}, bf16[512,128]{1,0:T(8,128)(2,1)S(1)}, bf16[512,128]{1,0:T(8,128)(2,1)S(1)}, bf16[512,128]{1,0:T(8,128)(2,...) custom-call(s32[2]{0:T(128)S(1)} %pad_add_fusion.where, ...), custom_call_target="tpu_custom_call" | custom-call | flops 603979776 | bytes 7733256 | tf_op jit(solution)/shard_map/pallas_call | solution.py:257
  27.1 0.0 collective-permute-done.2.refs_2_
  27.1 0.6 collective-permute-start.14
  27.7 0.0 collective-permute-done.3.refs_3_
  27.7 2.3 %collective-permute-start.15 = (bf16[512,128]{1,0:T(8,128)(2,1)S(1)}, bf16[512,128]{1,0:T(8,128)(2,1)S(1)}, u32[]{:S(2)}, u32[]{:S(2)}) collective-permute-start(bf16[512,128]{1,0:T(8,128)(2,1)S(1)} %get-tuple-element.58), channel_id=1, source_target_pairs={{0,5},{1,4},{2,7},{3,6},{4,1},{5,0},{6,3},{7,2},{8,13},{9,12},{10,... | collective-permute-start | bytes 393224 | tf_op jit(solution)/shard_map/ppermute | solution.py:282
  30.0 0.0 collective-permute-done.4.refs_4_
  30.0 2.5 %collective-permute-start.16 = (bf16[512,128]{1,0:T(8,128)(2,1)S(1)}, bf16[512,128]{1,0:T(8,128)(2,1)S(1)}, u32[]{:S(2)}, u32[]{:S(2)}) collective-permute-start(bf16[512,128]{1,0:T(8,128)(2,1)S(1)} %get-tuple-element.59), channel_id=1, source_target_pairs={{0,6},{1,7},{2,4},{3,5},{4,2},{5,3},{6,0},{7,1},{8,14},{9,15},{10,... | collective-permute-start | bytes 393224 | tf_op jit(solution)/shard_map/ppermute | solution.py:282
  32.5 0.0 collective-permute-done.5.refs_5_
  32.5 0.5 collective-permute-start.17
  33.0 0.0 collective-permute-done.6.refs_6_
  33.0 0.0 copy-done.1
  33.1 4.2 %shard_map.79 = (bf16[512,128]{1,0:T(8,128)(2,1)S(1)}, bf16[512,128]{1,0:T(8,128)(2,1)S(1)}, bf16[512,128]{1,0:T(8,128)(2,1)S(1)}, bf16[512,128]{1,0:T(8,128)(2,...) custom-call(s32[2]{0:T(128)S(1)} %pad_add_fusion.where, ...), custom_call_target="tpu_custom_call", output_to_operand_aliasing={{0}: (9, {}), {1}: (10, {}), {2}: (11, {})} | custom-call | flops 1207959552 | bytes 9961480 | tf_op jit(solution)/shard_map/pallas_call | solution.py:257
  37.3 2.3 %collective-permute-start.18 = (bf16[512,128]{1,0:T(8,128)(2,1)S(1)}, bf16[512,128]{1,0:T(8,128)(2,1)S(1)}, u32[]{:S(2)}, u32[]{:S(2)}) collective-permute-start(bf16[512,128]{1,0:T(8,128)(2,1)S(1)} %get-tuple-element.61), channel_id=1, source_target_pairs={{0,7},{1,6},{2,5},{3,4},{4,3},{5,2},{6,1},{7,0},{8,15},{9,14},{10,... | collective-permute-start | bytes 393224 | tf_op jit(solution)/shard_map/ppermute | solution.py:282
  39.6 5.7 %collective-permute-done.14.refs_0_ = bf16[512,128]{1,0:T(8,128)(2,1)S(1)} collective-permute-done((bf16[512,128]{1,0:T(8,128)(2,1)S(1)}, bf16[512,128]{1,0:T(8,128)(2,1)S(1)}, u32[]{:S(2)}, u32[]{:S(2)}) %collective-permute-start.14) | collective-permute-done | bytes 131104 | tf_op jit(solution)/shard_map/ppermute | solution.py:282
  45.3 4.9 %collective-permute-start.19 = (bf16[512,128]{1,0:T(8,128)(2,1)S(1)}, bf16[512,128]{1,0:T(8,128)(2,1)S(1)}, u32[]{:S(2)}, u32[]{:S(2)}) collective-permute-start(bf16[512,128]{1,0:T(8,128)(2,1)S(1)} %get-tuple-element.62), channel_id=1, source_target_pairs={{0,2},{1,3},{2,0},{3,1},{4,6},{5,7},{6,4},{7,5},{8,10},{9,11},{10,... | collective-permute-start | bytes 393224 | tf_op jit(solution)/shard_map/ppermute | solution.py:282
  50.2 0.0 collective-permute-done.15.refs_1_
  50.2 0.0 collective-permute-start.20
  50.2 0.0 collective-permute-done.16.refs_2_
  50.2 1.5 %collective-permute-start.7 = (bf16[512,128]{1,0:T(8,128)(2,1)S(1)}, bf16[512,128]{1,0:T(8,128)(2,1)S(1)}, u32[]{:S(2)}, u32[]{:S(2)}) collective-permute-start(bf16[512,128]{1,0:T(8,128)(2,1)S(1)} %get-tuple-element.49), channel_id=1, source_target_pairs={{0,1},{1,0},{2,3},{3,2},{4,5},{5,4},{6,7},{7,6},{8,9},{9,8},{10,11... | collective-permute-start | bytes 393224 | tf_op jit(solution)/shard_map/ppermute | solution.py:282
  51.8 0.0 collective-permute-done.17.refs_3_
  51.8 2.5 %collective-permute-start.8 = (bf16[512,128]{1,0:T(8,128)(2,1)S(1)}, bf16[512,128]{1,0:T(8,128)(2,1)S(1)}, u32[]{:S(2)}, u32[]{:S(2)}) collective-permute-start(bf16[512,128]{1,0:T(8,128)(2,1)S(1)} %get-tuple-element.50), channel_id=1, source_target_pairs={{0,4},{1,5},{2,6},{3,7},{4,0},{5,1},{6,2},{7,3},{8,12},{9,13},{10,... | collective-permute-start | bytes 393224 | tf_op jit(solution)/shard_map/ppermute | solution.py:282
  54.3 0.0 collective-permute-done.18.refs_4_
  54.3 0.7 collective-permute-start.9
  55.0 0.0 collective-permute-done.19.refs_5_
  55.0 3.2 %collective-permute-start.10 = (bf16[512,128]{1,0:T(8,128)(2,1)S(1)}, bf16[512,128]{1,0:T(8,128)(2,1)S(1)}, u32[]{:S(2)}, u32[]{:S(2)}) collective-permute-start(bf16[512,128]{1,0:T(8,128)(2,1)S(1)} %get-tuple-element.52), channel_id=1, source_target_pairs={{0,5},{1,4},{2,7},{3,6},{4,1},{5,0},{6,3},{7,2},{8,13},{9,12},{10,... | collective-permute-start | bytes 393224 | tf_op jit(solution)/shard_map/ppermute | solution.py:282
  58.1 1.4 %collective-permute-done.20.refs_6_ = bf16[512,128]{1,0:T(8,128)(2,1)S(1)} collective-permute-done((bf16[512,128]{1,0:T(8,128)(2,1)S(1)}, bf16[512,128]{1,0:T(8,128)(2,1)S(1)}, u32[]{:S(2)}, u32[]{:S(2)}) %collective-permute-start.20) | collective-permute-done | bytes 131104 | tf_op jit(solution)/shard_map/ppermute | solution.py:282
  59.5 0.4 collective-permute-start.11
  60.0 4.1 %shard_map.80 = (bf16[512,256]{1,0:T(8,128)(2,1)S(1)}, bf16[512,256]{1,0:T(8,128)(2,1)S(1)}, bf16[512,256]{1,0:T(8,128)(2,1)S(1)}, bf16[512,256]{1,0:T(8,128)(2,1)S(1)}) custom-call(s32[2]{0:T(128)S(1)} %pad_add_fusion.where, bf16[512,128]{1,0:T(8,128)(2,1)S(1)} %collective-permute-done.14.refs_0_, bf16[512,128]{1,0:T(8,128)(2,1)S(1)} %collective-permute-done.15.refs_1_, ...), custom_call_target="tpu_custom_call" | custom-call | flops 1207959552 | bytes 6815752 | tf_op jit(solution)/shard_map/pallas_call | solution.py:257
  64.1 0.0 collective-permute-done.7.refs_0_
  64.1 1.5 %collective-permute-start.21 = (bf16[512,256]{1,0:T(8,128)(2,1)S(1)}, bf16[512,256]{1,0:T(8,128)(2,1)S(1)}, u32[]{:S(2)}, u32[]{:S(2)}) collective-permute-start(bf16[512,256]{1,0:T(8,128)(2,1)S(1)} %get-tuple-element.66), channel_id=1, source_target_pairs={{0,16},{8,24},{16,0},{24,8},{1,17},{9,25},{17,1},{25,9},{2,18},{10... | collective-permute-start | bytes 786440 | tf_op jit(solution)/shard_map/ppermute | solution.py:282
  65.6 0.0 collective-permute-done.8.refs_1_
  65.6 0.0 collective-permute-start.22
  65.6 0.0 collective-permute-done.9.refs_2_
  65.6 0.7 collective-permute-start.23
  66.3 3.1 %collective-permute-done.10.refs_3_ = bf16[512,128]{1,0:T(8,128)(2,1)S(1)} collective-permute-done((bf16[512,128]{1,0:T(8,128)(2,1)S(1)}, bf16[512,128]{1,0:T(8,128)(2,1)S(1)}, u32[]{:S(2)}, u32[]{:S(2)}) %collective-permute-start.10) | collective-permute-done | bytes 131104 | tf_op jit(solution)/shard_map/ppermute | solution.py:282
  69.4 4.0 %collective-permute-start.12 = (bf16[512,128]{1,0:T(8,128)(2,1)S(1)}, bf16[512,128]{1,0:T(8,128)(2,1)S(1)}, u32[]{:S(2)}, u32[]{:S(2)}) collective-permute-start(bf16[512,128]{1,0:T(8,128)(2,1)S(1)} %get-tuple-element.54), channel_id=1, source_target_pairs={{0,7},{1,6},{2,5},{3,4},{4,3},{5,2},{6,1},{7,0},{8,15},{9,14},{10,... | collective-permute-start | bytes 393224 | tf_op jit(solution)/shard_map/ppermute | solution.py:282
  73.4 0.0 collective-permute-done.11.refs_4_
  73.4 0.8 collective-permute-start.13
  74.1 3.3 %collective-permute-done.12.refs_5_ = bf16[512,128]{1,0:T(8,128)(2,1)S(1)} collective-permute-done((bf16[512,128]{1,0:T(8,128)(2,1)S(1)}, bf16[512,128]{1,0:T(8,128)(2,1)S(1)}, u32[]{:S(2)}, u32[]{:S(2)}) %collective-permute-start.12) | collective-permute-done | bytes 131104 | tf_op jit(solution)/shard_map/ppermute | solution.py:282
  77.4 1.8 %collective-permute-done.13.refs_6_ = bf16[512,128]{1,0:T(8,128)(2,1)S(1)} collective-permute-done((bf16[512,128]{1,0:T(8,128)(2,1)S(1)}, bf16[512,128]{1,0:T(8,128)(2,1)S(1)}, u32[]{:S(2)}, u32[]{:S(2)}) %collective-permute-start.13) | collective-permute-done | bytes 131104 | tf_op jit(solution)/shard_map/ppermute | solution.py:282
  79.2 0.0 collective-permute-done.21.refs_8_
  79.2 0.0 collective-permute-done.22.refs_9_
  79.2 0.0 collective-permute-done.23.refs_10_
  79.2 1.8 %shard_map.81 = (bf16[8,512,128]{2,1,0:T(8,128)(2,1)}, f32[512,256]{1,0:T(8,128)}) custom-call(s32[2]{0:T(128)S(1)} %pad_add_fusion.where, bf16[512,128]{1,0:T(8,128)(2,1)S(1)} %collective-permute-done.7.refs_0_, bf16[512,128]{1,0:T(8,128)(2,1)S(1)} %collective-permute-done.8.refs_1_, bf16[512,128]{1,0:T(8,128)(2,1)S(1)} %collective-permute-done.9.refs_2_, ...), custom_call_target="tpu_custom_call" | custom-call | bytes 3670024 | tf_op jit(solution)/shard_map/pallas_call | solution.py:257
Async XLA Ops:
  0.6 23.1 %copy-start = (bf16[9,256,256]{2,1,0:T(8,128)(2,1)S(1)}, bf16[9,256,256]{2,1,0:T(8,128)(2,1)}, u32[]{:S(2)}) copy-start(bf16[9,256,256]{2,1,0:T(8,128)(2,1)} %constant.12.clone.forward.refs_12_.refs_9_) | copy-start | bytes 3538948
  3.0 14.8 %collective-permute-start = (bf16[512,128]{1,0:T(8,128)(2,1)S(1)}, bf16[512,128]{1,0:T(8,128)(2,1)S(1)}, u32[]{:S(2)}, u32[]{:S(2)}) collective-permute-start(bf16[512,128]{1,0:T(8,128)(2,1)S(1)} %get-tuple-element.37), channel_id=1, source_target_pairs={{0,4},{1,5},{2,6},{3,7},{4,0},{5,1},{6,2},{7,3},{8,12},{9,13},{10,... | collective-permute-start | bytes 393224 | tf_op jit(solution)/shard_map/ppermute | solution.py:282
  7.1 16.6 %collective-permute-start.1 = (bf16[512,128]{1,0:T(8,128)(2,1)S(1)}, bf16[512,128]{1,0:T(8,128)(2,1)S(1)}, u32[]{:S(2)}, u32[]{:S(2)}) collective-permute-start(bf16[512,128]{1,0:T(8,128)(2,1)S(1)} %get-tuple-element.38), channel_id=1, source_target_pairs={{0,1},{1,0},{2,3},{3,2},{4,5},{5,4},{6,7},{7,6},{8,9},{9,8},{10,11... | collective-permute-start | bytes 393224 | tf_op jit(solution)/shard_map/ppermute | solution.py:282
  8.7 18.4 %collective-permute-start.2 = (bf16[512,128]{1,0:T(8,128)(2,1)S(1)}, bf16[512,128]{1,0:T(8,128)(2,1)S(1)}, u32[]{:S(2)}, u32[]{:S(2)}) collective-permute-start(bf16[512,128]{1,0:T(8,128)(2,1)S(1)} %get-tuple-element.39), channel_id=1, source_target_pairs={{0,5},{1,4},{2,7},{3,6},{4,1},{5,0},{6,3},{7,2},{8,13},{9,12},{10,... | collective-permute-start | bytes 393224 | tf_op jit(solution)/shard_map/ppermute | solution.py:282
  8.7 19.0 %collective-permute-start.3 = (bf16[512,128]{1,0:T(8,128)(2,1)S(1)}, bf16[512,128]{1,0:T(8,128)(2,1)S(1)}, u32[]{:S(2)}, u32[]{:S(2)}) collective-permute-start(bf16[512,128]{1,0:T(8,128)(2,1)S(1)} %get-tuple-element.40), channel_id=1, source_target_pairs={{0,2},{1,3},{2,0},{3,1},{4,6},{5,7},{6,4},{7,5},{8,10},{9,11},{10,... | collective-permute-start | bytes 393224 | tf_op jit(solution)/shard_map/ppermute | solution.py:282
  10.5 19.5 %collective-permute-start.4 = (bf16[512,128]{1,0:T(8,128)(2,1)S(1)}, bf16[512,128]{1,0:T(8,128)(2,1)S(1)}, u32[]{:S(2)}, u32[]{:S(2)}) collective-permute-start(bf16[512,128]{1,0:T(8,128)(2,1)S(1)} %get-tuple-element.41), channel_id=1, source_target_pairs={{0,6},{1,7},{2,4},{3,5},{4,2},{5,3},{6,0},{7,1},{8,14},{9,15},{10,... | collective-permute-start | bytes 393224 | tf_op jit(solution)/shard_map/ppermute | solution.py:282
  17.8 14.7 %collective-permute-start.5 = (bf16[512,128]{1,0:T(8,128)(2,1)S(1)}, bf16[512,128]{1,0:T(8,128)(2,1)S(1)}, u32[]{:S(2)}, u32[]{:S(2)}) collective-permute-start(bf16[512,128]{1,0:T(8,128)(2,1)S(1)} %get-tuple-element.42), channel_id=1, source_target_pairs={{0,7},{1,6},{2,5},{3,4},{4,3},{5,2},{6,1},{7,0},{8,15},{9,14},{10,... | collective-permute-start | bytes 393224 | tf_op jit(solution)/shard_map/ppermute | solution.py:282
  23.8 9.3 %collective-permute-start.6 = (bf16[512,128]{1,0:T(8,128)(2,1)S(1)}, bf16[512,128]{1,0:T(8,128)(2,1)S(1)}, u32[]{:S(2)}, u32[]{:S(2)}) collective-permute-start(bf16[512,128]{1,0:T(8,128)(2,1)S(1)} %get-tuple-element.43), channel_id=1, source_target_pairs={{0,3},{1,2},{2,1},{3,0},{4,7},{5,6},{6,5},{7,4},{8,11},{9,10},{10,... | collective-permute-start | bytes 393224 | tf_op jit(solution)/shard_map/ppermute | solution.py:282
  23.8 9.3 %copy-start.1 = (bf16[9,256,256]{2,1,0:T(8,128)(2,1)S(1)}, bf16[9,256,256]{2,1,0:T(8,128)(2,1)}, u32[]{:S(2)}) copy-start(bf16[9,256,256]{2,1,0:T(8,128)(2,1)} %constant.13.clone.refs_13_.refs_10_) | copy-start | bytes 3538948
  27.1 18.3 %collective-permute-start.14 = (bf16[512,128]{1,0:T(8,128)(2,1)S(1)}, bf16[512,128]{1,0:T(8,128)(2,1)S(1)}, u32[]{:S(2)}, u32[]{:S(2)}) collective-permute-start(bf16[512,128]{1,0:T(8,128)(2,1)S(1)} %get-tuple-element.57), channel_id=1, source_target_pairs={{0,4},{1,5},{2,6},{3,7},{4,0},{5,1},{6,2},{7,3},{8,12},{9,13},{10,... | collective-permute-start | bytes 393224 | tf_op jit(solution)/shard_map/ppermute | solution.py:282
  27.7 22.5 %collective-permute-start.15 = (bf16[512,128]{1,0:T(8,128)(2,1)S(1)}, bf16[512,128]{1,0:T(8,128)(2,1)S(1)}, u32[]{:S(2)}, u32[]{:S(2)}) collective-permute-start(bf16[512,128]{1,0:T(8,128)(2,1)S(1)} %get-tuple-element.58), channel_id=1, source_target_pairs={{0,5},{1,4},{2,7},{3,6},{4,1},{5,0},{6,3},{7,2},{8,13},{9,12},{10,... | collective-permute-start | bytes 393224 | tf_op jit(solution)/shard_map/ppermute | solution.py:282
  30.0 20.2 %collective-permute-start.16 = (bf16[512,128]{1,0:T(8,128)(2,1)S(1)}, bf16[512,128]{1,0:T(8,128)(2,1)S(1)}, u32[]{:S(2)}, u32[]{:S(2)}) collective-permute-start(bf16[512,128]{1,0:T(8,128)(2,1)S(1)} %get-tuple-element.59), channel_id=1, source_target_pairs={{0,6},{1,7},{2,4},{3,5},{4,2},{5,3},{6,0},{7,1},{8,14},{9,15},{10,... | collective-permute-start | bytes 393224 | tf_op jit(solution)/shard_map/ppermute | solution.py:282
  32.5 19.3 %collective-permute-start.17 = (bf16[512,128]{1,0:T(8,128)(2,1)S(1)}, bf16[512,128]{1,0:T(8,128)(2,1)S(1)}, u32[]{:S(2)}, u32[]{:S(2)}) collective-permute-start(bf16[512,128]{1,0:T(8,128)(2,1)S(1)} %get-tuple-element.60), channel_id=1, source_target_pairs={{0,1},{1,0},{2,3},{3,2},{4,5},{5,4},{6,7},{7,6},{8,9},{9,8},{10,11... | collective-permute-start | bytes 393224 | tf_op jit(solution)/shard_map/ppermute | solution.py:282
  37.3 17.0 %collective-permute-start.18 = (bf16[512,128]{1,0:T(8,128)(2,1)S(1)}, bf16[512,128]{1,0:T(8,128)(2,1)S(1)}, u32[]{:S(2)}, u32[]{:S(2)}) collective-permute-start(bf16[512,128]{1,0:T(8,128)(2,1)S(1)} %get-tuple-element.61), channel_id=1, source_target_pairs={{0,7},{1,6},{2,5},{3,4},{4,3},{5,2},{6,1},{7,0},{8,15},{9,14},{10,... | collective-permute-start | bytes 393224 | tf_op jit(solution)/shard_map/ppermute | solution.py:282
  45.3 9.7 %collective-permute-start.19 = (bf16[512,128]{1,0:T(8,128)(2,1)S(1)}, bf16[512,128]{1,0:T(8,128)(2,1)S(1)}, u32[]{:S(2)}, u32[]{:S(2)}) collective-permute-start(bf16[512,128]{1,0:T(8,128)(2,1)S(1)} %get-tuple-element.62), channel_id=1, source_target_pairs={{0,2},{1,3},{2,0},{3,1},{4,6},{5,7},{6,4},{7,5},{8,10},{9,11},{10,... | collective-permute-start | bytes 393224 | tf_op jit(solution)/shard_map/ppermute | solution.py:282
  50.2 9.3 %collective-permute-start.20 = (bf16[512,128]{1,0:T(8,128)(2,1)S(1)}, bf16[512,128]{1,0:T(8,128)(2,1)S(1)}, u32[]{:S(2)}, u32[]{:S(2)}) collective-permute-start(bf16[512,128]{1,0:T(8,128)(2,1)S(1)} %get-tuple-element.63), channel_id=1, source_target_pairs={{0,3},{1,2},{2,1},{3,0},{4,7},{5,6},{6,5},{7,4},{8,11},{9,10},{10,... | collective-permute-start | bytes 393224 | tf_op jit(solution)/shard_map/ppermute | solution.py:282
  50.2 13.8 %collective-permute-start.7 = (bf16[512,128]{1,0:T(8,128)(2,1)S(1)}, bf16[512,128]{1,0:T(8,128)(2,1)S(1)}, u32[]{:S(2)}, u32[]{:S(2)}) collective-permute-start(bf16[512,128]{1,0:T(8,128)(2,1)S(1)} %get-tuple-element.49), channel_id=1, source_target_pairs={{0,1},{1,0},{2,3},{3,2},{4,5},{5,4},{6,7},{7,6},{8,9},{9,8},{10,11... | collective-permute-start | bytes 393224 | tf_op jit(solution)/shard_map/ppermute | solution.py:282
  51.8 13.8 %collective-permute-start.8 = (bf16[512,128]{1,0:T(8,128)(2,1)S(1)}, bf16[512,128]{1,0:T(8,128)(2,1)S(1)}, u32[]{:S(2)}, u32[]{:S(2)}) collective-permute-start(bf16[512,128]{1,0:T(8,128)(2,1)S(1)} %get-tuple-element.50), channel_id=1, source_target_pairs={{0,4},{1,5},{2,6},{3,7},{4,0},{5,1},{6,2},{7,3},{8,12},{9,13},{10,... | collective-permute-start | bytes 393224 | tf_op jit(solution)/shard_map/ppermute | solution.py:282
  54.3 11.3 %collective-permute-start.9 = (bf16[512,128]{1,0:T(8,128)(2,1)S(1)}, bf16[512,128]{1,0:T(8,128)(2,1)S(1)}, u32[]{:S(2)}, u32[]{:S(2)}) collective-permute-start(bf16[512,128]{1,0:T(8,128)(2,1)S(1)} %get-tuple-element.51), channel_id=1, source_target_pairs={{0,2},{1,3},{2,0},{3,1},{4,6},{5,7},{6,4},{7,5},{8,10},{9,11},{10,... | collective-permute-start | bytes 393224 | tf_op jit(solution)/shard_map/ppermute | solution.py:282
  55.0 14.4 %collective-permute-start.10 = (bf16[512,128]{1,0:T(8,128)(2,1)S(1)}, bf16[512,128]{1,0:T(8,128)(2,1)S(1)}, u32[]{:S(2)}, u32[]{:S(2)}) collective-permute-start(bf16[512,128]{1,0:T(8,128)(2,1)S(1)} %get-tuple-element.52), channel_id=1, source_target_pairs={{0,5},{1,4},{2,7},{3,6},{4,1},{5,0},{6,3},{7,2},{8,13},{9,12},{10,... | collective-permute-start | bytes 393224 | tf_op jit(solution)/shard_map/ppermute | solution.py:282
  59.5 13.8 %collective-permute-start.11 = (bf16[512,128]{1,0:T(8,128)(2,1)S(1)}, bf16[512,128]{1,0:T(8,128)(2,1)S(1)}, u32[]{:S(2)}, u32[]{:S(2)}) collective-permute-start(bf16[512,128]{1,0:T(8,128)(2,1)S(1)} %get-tuple-element.53), channel_id=1, source_target_pairs={{0,6},{1,7},{2,4},{3,5},{4,2},{5,3},{6,0},{7,1},{8,14},{9,15},{10,... | collective-permute-start | bytes 393224 | tf_op jit(solution)/shard_map/ppermute | solution.py:282
  64.1 15.2 %collective-permute-start.21 = (bf16[512,256]{1,0:T(8,128)(2,1)S(1)}, bf16[512,256]{1,0:T(8,128)(2,1)S(1)}, u32[]{:S(2)}, u32[]{:S(2)}) collective-permute-start(bf16[512,256]{1,0:T(8,128)(2,1)S(1)} %get-tuple-element.66), channel_id=1, source_target_pairs={{0,16},{8,24},{16,0},{24,8},{1,17},{9,25},{17,1},{25,9},{2,18},{10... | collective-permute-start | bytes 786440 | tf_op jit(solution)/shard_map/ppermute | solution.py:282
  65.6 13.6 %collective-permute-start.22 = (bf16[512,256]{1,0:T(8,128)(2,1)S(1)}, bf16[512,256]{1,0:T(8,128)(2,1)S(1)}, u32[]{:S(2)}, u32[]{:S(2)}) collective-permute-start(bf16[512,256]{1,0:T(8,128)(2,1)S(1)} %get-tuple-element.67), channel_id=1, source_target_pairs={{0,24},{8,16},{16,8},{24,0},{1,25},{9,17},{17,9},{25,1},{2,26},{10... | collective-permute-start | bytes 786440 | tf_op jit(solution)/shard_map/ppermute | solution.py:282
  65.6 13.6 %collective-permute-start.23 = (bf16[512,256]{1,0:T(8,128)(2,1)S(1)}, bf16[512,256]{1,0:T(8,128)(2,1)S(1)}, u32[]{:S(2)}, u32[]{:S(2)}) collective-permute-start(bf16[512,256]{1,0:T(8,128)(2,1)S(1)} %get-tuple-element.68), channel_id=1, source_target_pairs={{0,8},{8,0},{16,24},{24,16},{1,9},{9,1},{17,25},{25,17},{2,10},{10... | collective-permute-start | bytes 786440 | tf_op jit(solution)/shard_map/ppermute | solution.py:282
  69.4 8.0 %collective-permute-start.12 = (bf16[512,128]{1,0:T(8,128)(2,1)S(1)}, bf16[512,128]{1,0:T(8,128)(2,1)S(1)}, u32[]{:S(2)}, u32[]{:S(2)}) collective-permute-start(bf16[512,128]{1,0:T(8,128)(2,1)S(1)} %get-tuple-element.54), channel_id=1, source_target_pairs={{0,7},{1,6},{2,5},{3,4},{4,3},{5,2},{6,1},{7,0},{8,15},{9,14},{10,... | collective-permute-start | bytes 393224 | tf_op jit(solution)/shard_map/ppermute | solution.py:282
  73.4 5.9 %collective-permute-start.13 = (bf16[512,128]{1,0:T(8,128)(2,1)S(1)}, bf16[512,128]{1,0:T(8,128)(2,1)S(1)}, u32[]{:S(2)}, u32[]{:S(2)}) collective-permute-start(bf16[512,128]{1,0:T(8,128)(2,1)S(1)} %get-tuple-element.55), channel_id=1, source_target_pairs={{0,3},{1,2},{2,1},{3,0},{4,7},{5,6},{6,5},{7,4},{8,11},{9,10},{10,... | collective-permute-start | bytes 393224 | tf_op jit(solution)/shard_map/ppermute | solution.py:282

commit v27 on v26

--- a/solution.py
+++ b/solution.py
@@ -288,7 +288,7 @@
     channels, span = saved_input.shape[1:]
     rows, length = long_filter.shape
     width = length // BLOCKS
-    grad_order, input_order, back_order = (spread(count, o) for o in ((4, 1, 5, 2, 6, 7, 3), (4, 5, 6, 1, 7, 2, 3), (1, 4, 2, 5, 6, 7, 3)))
+    grad_order, input_order, back_order = (spread(count, o) for o in ((4, 1, 5, 6, 2, 7, 3), (4, 5, 6, 1, 7, 2, 3), (1, 4, 2, 5, 6, 7, 3)))
     late = 3
     at = count - 1 - late
     every = range(count + 8)

time: 81.2 us -> 81.3 us (level)
  no operation moved by 1% of the time
where the time goes in v27:
time: 81.3 us; the launch traced here: 81.2 us
  starting transfers between devices  43.9 us (54%)
  waiting for transfers between devices  20.7 us (25%)
  Pallas kernels  15.8 us (19%)
    ppermute x24, starting transfers between devices, exchange(): lax.ppermute(piece, axis, [(i, i ^ k) for i in range(size)])  43.9 us
    ppermute x24, waiting for transfers between devices, exchange(): lax.ppermute(piece, axis, [(i, i ^ k) for i in range(size)])  20.7 us
    pallas_call x5, Pallas kernels, call(): pl.pallas_call(kernel, out_shape=list(outs), in_specs=specs, out_specs=[s...  15.8 us
  transfers between devices with their start and end apart: 24, of which 6 were waited for; matrix products, arithmetic and copies ran while one was open for 0% of the time, Pallas kernels for 14%

profile of v27, /device:TPU:0, one launch (start us, length us, event | category | flops | bytes accessed | tf_op | source)
XLA Modules:
  0.0 81.2 jit_solution(18157468359059270872)
XLA Ops:
  0.6 0.0 copy-start
  0.6 0.1 pad_add_fusion.where
  0.7 2.3 %shard_map.77 = (bf16[512,128]{1,0:T(8,128)(2,1)S(1)}, bf16[512,128]{1,0:T(8,128)(2,1)S(1)}, bf16[512,128]{1,0:T(8,128)(2,1)S(1)}, bf16[512,128]{1,0:T(8,128)(2,...) custom-call(s32[2]{0:T(128)S(1)} %pad_add_fusion.where, ...), custom_call_target="tpu_custom_call" | custom-call | bytes 3145736 | tf_op jit(solution)/shard_map/pallas_call | solution.py:257
  3.0 4.1 %collective-permute-start = (bf16[512,128]{1,0:T(8,128)(2,1)S(1)}, bf16[512,128]{1,0:T(8,128)(2,1)S(1)}, u32[]{:S(2)}, u32[]{:S(2)}) collective-permute-start(bf16[512,128]{1,0:T(8,128)(2,1)S(1)} %get-tuple-element.37), channel_id=1, source_target_pairs={{0,4},{1,5},{2,6},{3,7},{4,0},{5,1},{6,2},{7,3},{8,12},{9,13},{10,... | collective-permute-start | bytes 393224 | tf_op jit(solution)/shard_map/ppermute | solution.py:282
  7.1 1.5 %collective-permute-start.1 = (bf16[512,128]{1,0:T(8,128)(2,1)S(1)}, bf16[512,128]{1,0:T(8,128)(2,1)S(1)}, u32[]{:S(2)}, u32[]{:S(2)}) collective-permute-start(bf16[512,128]{1,0:T(8,128)(2,1)S(1)} %get-tuple-element.38), channel_id=1, source_target_pairs={{0,1},{1,0},{2,3},{3,2},{4,5},{5,4},{6,7},{7,6},{8,9},{9,8},{10,11... | collective-permute-start | bytes 393224 | tf_op jit(solution)/shard_map/ppermute | solution.py:282
  8.7 0.0 collective-permute-start.2
  8.7 3.9 %collective-permute-start.3 = (bf16[512,128]{1,0:T(8,128)(2,1)S(1)}, bf16[512,128]{1,0:T(8,128)(2,1)S(1)}, u32[]{:S(2)}, u32[]{:S(2)}) collective-permute-start(bf16[512,128]{1,0:T(8,128)(2,1)S(1)} %get-tuple-element.40), channel_id=1, source_target_pairs={{0,6},{1,7},{2,4},{3,5},{4,2},{5,3},{6,0},{7,1},{8,14},{9,15},{10,... | collective-permute-start | bytes 393224 | tf_op jit(solution)/shard_map/ppermute | solution.py:282
  12.5 0.0 collective-permute-start.4
  12.6 7.4 %collective-permute-done.refs_0_ = bf16[512,128]{1,0:T(8,128)(2,1)S(1)} collective-permute-done((bf16[512,128]{1,0:T(8,128)(2,1)S(1)}, bf16[512,128]{1,0:T(8,128)(2,1)S(1)}, u32[]{:S(2)}, u32[]{:S(2)}) %collective-permute-start) | collective-permute-done | bytes 131104 | tf_op jit(solution)/shard_map/ppermute | solution.py:282
  20.0 3.8 %collective-permute-start.5 = (bf16[512,128]{1,0:T(8,128)(2,1)S(1)}, bf16[512,128]{1,0:T(8,128)(2,1)S(1)}, u32[]{:S(2)}, u32[]{:S(2)}) collective-permute-start(bf16[512,128]{1,0:T(8,128)(2,1)S(1)} %get-tuple-element.42), channel_id=1, source_target_pairs={{0,7},{1,6},{2,5},{3,4},{4,3},{5,2},{6,1},{7,0},{8,15},{9,14},{10,... | collective-permute-start | bytes 393224 | tf_op jit(solution)/shard_map/ppermute | solution.py:282
  23.8 0.0 collective-permute-done.1.refs_1_
  23.8 0.0 collective-permute-start.6
  23.8 0.0 copy-done
  23.8 0.0 copy-start.1
  23.8 3.3 %shard_map.78 = (bf16[512,128]{1,0:T(8,128)(2,1)S(1)}, bf16[512,128]{1,0:T(8,128)(2,1)S(1)}, bf16[512,128]{1,0:T(8,128)(2,1)S(1)}, bf16[512,128]{1,0:T(8,128)(2,...) custom-call(s32[2]{0:T(128)S(1)} %pad_add_fusion.where, ...), custom_call_target="tpu_custom_call" | custom-call | flops 603979776 | bytes 7733256 | tf_op jit(solution)/shard_map/pallas_call | solution.py:257
  27.1 0.0 collective-permute-done.2.refs_2_
  27.1 1.5 %collective-permute-start.14 = (bf16[512,128]{1,0:T(8,128)(2,1)S(1)}, bf16[512,128]{1,0:T(8,128)(2,1)S(1)}, u32[]{:S(2)}, u32[]{:S(2)}) collective-permute-start(bf16[512,128]{1,0:T(8,128)(2,1)S(1)} %get-tuple-element.57), channel_id=1, source_target_pairs={{0,4},{1,5},{2,6},{3,7},{4,0},{5,1},{6,2},{7,3},{8,12},{9,13},{10,... | collective-permute-start | bytes 393224 | tf_op jit(solution)/shard_map/ppermute | solution.py:282
  28.6 0.0 collective-permute-done.3.refs_3_
  28.6 2.6 %collective-permute-start.15 = (bf16[512,128]{1,0:T(8,128)(2,1)S(1)}, bf16[512,128]{1,0:T(8,128)(2,1)S(1)}, u32[]{:S(2)}, u32[]{:S(2)}) collective-permute-start(bf16[512,128]{1,0:T(8,128)(2,1)S(1)} %get-tuple-element.58), channel_id=1, source_target_pairs={{0,5},{1,4},{2,7},{3,6},{4,1},{5,0},{6,3},{7,2},{8,13},{9,12},{10,... | collective-permute-start | bytes 393224 | tf_op jit(solution)/shard_map/ppermute | solution.py:282
  31.2 0.0 collective-permute-done.4.refs_4_
  31.2 1.3 %collective-permute-start.16 = (bf16[512,128]{1,0:T(8,128)(2,1)S(1)}, bf16[512,128]{1,0:T(8,128)(2,1)S(1)}, u32[]{:S(2)}, u32[]{:S(2)}) collective-permute-start(bf16[512,128]{1,0:T(8,128)(2,1)S(1)} %get-tuple-element.59), channel_id=1, source_target_pairs={{0,6},{1,7},{2,4},{3,5},{4,2},{5,3},{6,0},{7,1},{8,14},{9,15},{10,... | collective-permute-start | bytes 393224 | tf_op jit(solution)/shard_map/ppermute | solution.py:282
  32.6 0.0 collective-permute-done.5.refs_5_
  32.6 0.5 collective-permute-start.17
  33.0 0.0 collective-permute-done.6.refs_6_
  33.0 0.0 copy-done.1
  33.1 4.2 %shard_map.79 = (bf16[512,128]{1,0:T(8,128)(2,1)S(1)}, bf16[512,128]{1,0:T(8,128)(2,1)S(1)}, bf16[512,128]{1,0:T(8,128)(2,1)S(1)}, bf16[512,128]{1,0:T(8,128)(2,...) custom-call(s32[2]{0:T(128)S(1)} %pad_add_fusion.where, ...), custom_call_target="tpu_custom_call", output_to_operand_aliasing={{0}: (9, {}), {1}: (10, {}), {2}: (11, {})} | custom-call | flops 1207959552 | bytes 9961480 | tf_op jit(solution)/shard_map/pallas_call | solution.py:257
  37.3 3.5 %collective-permute-start.18 = (bf16[512,128]{1,0:T(8,128)(2,1)S(1)}, bf16[512,128]{1,0:T(8,128)(2,1)S(1)}, u32[]{:S(2)}, u32[]{:S(2)}) collective-permute-start(bf16[512,128]{1,0:T(8,128)(2,1)S(1)} %get-tuple-element.61), channel_id=1, source_target_pairs={{0,7},{1,6},{2,5},{3,4},{4,3},{5,2},{6,1},{7,0},{8,15},{9,14},{10,... | collective-permute-start | bytes 393224 | tf_op jit(solution)/shard_map/ppermute | solution.py:282
  40.8 4.7 %collective-permute-done.14.refs_0_ = bf16[512,128]{1,0:T(8,128)(2,1)S(1)} collective-permute-done((bf16[512,128]{1,0:T(8,128)(2,1)S(1)}, bf16[512,128]{1,0:T(8,128)(2,1)S(1)}, u32[]{:S(2)}, u32[]{:S(2)}) %collective-permute-start.14) | collective-permute-done | bytes 131104 | tf_op jit(solution)/shard_map/ppermute | solution.py:282
  45.5 3.3 %collective-permute-start.19 = (bf16[512,128]{1,0:T(8,128)(2,1)S(1)}, bf16[512,128]{1,0:T(8,128)(2,1)S(1)}, u32[]{:S(2)}, u32[]{:S(2)}) collective-permute-start(bf16[512,128]{1,0:T(8,128)(2,1)S(1)} %get-tuple-element.62), channel_id=1, source_target_pairs={{0,2},{1,3},{2,0},{3,1},{4,6},{5,7},{6,4},{7,5},{8,10},{9,11},{10,... | collective-permute-start | bytes 393224 | tf_op jit(solution)/shard_map/ppermute | solution.py:282
  48.8 0.5 collective-permute-done.15.refs_1_
  49.3 0.0 collective-permute-start.20
  49.3 0.0 collective-permute-done.16.refs_2_
  49.3 1.1 %collective-permute-start.7 = (bf16[512,128]{1,0:T(8,128)(2,1)S(1)}, bf16[512,128]{1,0:T(8,128)(2,1)S(1)}, u32[]{:S(2)}, u32[]{:S(2)}) collective-permute-start(bf16[512,128]{1,0:T(8,128)(2,1)S(1)} %get-tuple-element.49), channel_id=1, source_target_pairs={{0,1},{1,0},{2,3},{3,2},{4,5},{5,4},{6,7},{7,6},{8,9},{9,8},{10,11... | collective-permute-start | bytes 393224 | tf_op jit(solution)/shard_map/ppermute | solution.py:282
  50.4 0.0 collective-permute-done.17.refs_3_
  50.4 3.9 %collective-permute-start.8 = (bf16[512,128]{1,0:T(8,128)(2,1)S(1)}, bf16[512,128]{1,0:T(8,128)(2,1)S(1)}, u32[]{:S(2)}, u32[]{:S(2)}) collective-permute-start(bf16[512,128]{1,0:T(8,128)(2,1)S(1)} %get-tuple-element.50), channel_id=1, source_target_pairs={{0,4},{1,5},{2,6},{3,7},{4,0},{5,1},{6,2},{7,3},{8,12},{9,13},{10,... | collective-permute-start | bytes 393224 | tf_op jit(solution)/shard_map/ppermute | solution.py:282
  54.3 0.0 collective-permute-done.18.refs_4_
  54.3 1.2 %collective-permute-start.9 = (bf16[512,128]{1,0:T(8,128)(2,1)S(1)}, bf16[512,128]{1,0:T(8,128)(2,1)S(1)}, u32[]{:S(2)}, u32[]{:S(2)}) collective-permute-start(bf16[512,128]{1,0:T(8,128)(2,1)S(1)} %get-tuple-element.51), channel_id=1, source_target_pairs={{0,2},{1,3},{2,0},{3,1},{4,6},{5,7},{6,4},{7,5},{8,10},{9,11},{10,... | collective-permute-start | bytes 393224 | tf_op jit(solution)/shard_map/ppermute | solution.py:282
  55.5 0.0 collective-permute-done.19.refs_5_
  55.5 3.0 %collective-permute-start.10 = (bf16[512,128]{1,0:T(8,128)(2,1)S(1)}, bf16[512,128]{1,0:T(8,128)(2,1)S(1)}, u32[]{:S(2)}, u32[]{:S(2)}) collective-permute-start(bf16[512,128]{1,0:T(8,128)(2,1)S(1)} %get-tuple-element.52), channel_id=1, source_target_pairs={{0,5},{1,4},{2,7},{3,6},{4,1},{5,0},{6,3},{7,2},{8,13},{9,12},{10,... | collective-permute-start | bytes 393224 | tf_op jit(solution)/shard_map/ppermute | solution.py:282
  58.4 0.0 collective-permute-done.20.refs_6_
  58.4 3.0 %collective-permute-start.11 = (bf16[512,128]{1,0:T(8,128)(2,1)S(1)}, bf16[512,128]{1,0:T(8,128)(2,1)S(1)}, u32[]{:S(2)}, u32[]{:S(2)}) collective-permute-start(bf16[512,128]{1,0:T(8,128)(2,1)S(1)} %get-tuple-element.53), channel_id=1, source_target_pairs={{0,6},{1,7},{2,4},{3,5},{4,2},{5,3},{6,0},{7,1},{8,14},{9,15},{10,... | collective-permute-start | bytes 393224 | tf_op jit(solution)/shard_map/ppermute | solution.py:282
  61.4 4.1 %shard_map.80 = (bf16[512,256]{1,0:T(8,128)(2,1)S(1)}, bf16[512,256]{1,0:T(8,128)(2,1)S(1)}, bf16[512,256]{1,0:T(8,128)(2,1)S(1)}, bf16[512,256]{1,0:T(8,128)(2,1)S(1)}) custom-call(s32[2]{0:T(128)S(1)} %pad_add_fusion.where, bf16[512,128]{1,0:T(8,128)(2,1)S(1)} %collective-permute-done.14.refs_0_, bf16[512,128]{1,0:T(8,128)(2,1)S(1)} %collective-permute-done.15.refs_1_, ...), custom_call_target="tpu_custom_call" | custom-call | flops 1207959552 | bytes 6815752 | tf_op jit(solution)/shard_map/pallas_call | solution.py:257
  65.5 0.0 collective-permute-done.7.refs_0_
  65.6 1.6 %collective-permute-start.21 = (bf16[512,256]{1,0:T(8,128)(2,1)S(1)}, bf16[512,256]{1,0:T(8,128)(2,1)S(1)}, u32[]{:S(2)}, u32[]{:S(2)}) collective-permute-start(bf16[512,256]{1,0:T(8,128)(2,1)S(1)} %get-tuple-element.66), channel_id=1, source_target_pairs={{0,16},{8,24},{16,0},{24,8},{1,17},{9,25},{17,1},{25,9},{2,18},{10... | collective-permute-start | bytes 786440 | tf_op jit(solution)/shard_map/ppermute | solution.py:282
  67.1 0.0 collective-permute-done.8.refs_1_
  67.1 0.0 collective-permute-start.22
  67.2 0.0 collective-permute-done.9.refs_2_
  67.2 0.6 collective-permute-start.23
  67.8 1.7 %collective-permute-done.10.refs_3_ = bf16[512,128]{1,0:T(8,128)(2,1)S(1)} collective-permute-done((bf16[512,128]{1,0:T(8,128)(2,1)S(1)}, bf16[512,128]{1,0:T(8,128)(2,1)S(1)}, u32[]{:S(2)}, u32[]{:S(2)}) %collective-permute-start.10) | collective-permute-done | bytes 131104 | tf_op jit(solution)/shard_map/ppermute | solution.py:282
  69.4 3.4 %collective-permute-start.12 = (bf16[512,128]{1,0:T(8,128)(2,1)S(1)}, bf16[512,128]{1,0:T(8,128)(2,1)S(1)}, u32[]{:S(2)}, u32[]{:S(2)}) collective-permute-start(bf16[512,128]{1,0:T(8,128)(2,1)S(1)} %get-tuple-element.54), channel_id=1, source_target_pairs={{0,7},{1,6},{2,5},{3,4},{4,3},{5,2},{6,1},{7,0},{8,15},{9,14},{10,... | collective-permute-start | bytes 393224 | tf_op jit(solution)/shard_map/ppermute | solution.py:282
  72.9 0.0 collective-permute-done.11.refs_4_
  72.9 0.0 collective-permute-start.13
  72.9 5.5 %collective-permute-done.12.refs_5_ = bf16[512,128]{1,0:T(8,128)(2,1)S(1)} collective-permute-done((bf16[512,128]{1,0:T(8,128)(2,1)S(1)}, bf16[512,128]{1,0:T(8,128)(2,1)S(1)}, u32[]{:S(2)}, u32[]{:S(2)}) %collective-permute-start.12) | collective-permute-done | bytes 131104 | tf_op jit(solution)/shard_map/ppermute | solution.py:282
  78.4 1.0 %collective-permute-done.13.refs_6_ = bf16[512,128]{1,0:T(8,128)(2,1)S(1)} collective-permute-done((bf16[512,128]{1,0:T(8,128)(2,1)S(1)}, bf16[512,128]{1,0:T(8,128)(2,1)S(1)}, u32[]{:S(2)}, u32[]{:S(2)}) %collective-permute-start.13) | collective-permute-done | bytes 131104 | tf_op jit(solution)/shard_map/ppermute | solution.py:282
  79.3 0.0 collective-permute-done.21.refs_8_
  79.3 0.0 collective-permute-done.22.refs_9_
  79.3 0.0 collective-permute-done.23.refs_10_
  79.3 1.8 %shard_map.81 = (bf16[8,512,128]{2,1,0:T(8,128)(2,1)}, f32[512,256]{1,0:T(8,128)}) custom-call(s32[2]{0:T(128)S(1)} %pad_add_fusion.where, bf16[512,128]{1,0:T(8,128)(2,1)S(1)} %collective-permute-done.7.refs_0_, bf16[512,128]{1,0:T(8,128)(2,1)S(1)} %collective-permute-done.8.refs_1_, bf16[512,128]{1,0:T(8,128)(2,1)S(1)} %collective-permute-done.9.refs_2_, ...), custom_call_target="tpu_custom_call" | custom-call | bytes 3670024 | tf_op jit(solution)/shard_map/pallas_call | solution.py:257
Async XLA Ops:
  0.6 23.1 %copy-start = (bf16[9,256,256]{2,1,0:T(8,128)(2,1)S(1)}, bf16[9,256,256]{2,1,0:T(8,128)(2,1)}, u32[]{:S(2)}) copy-start(bf16[9,256,256]{2,1,0:T(8,128)(2,1)} %constant.12.clone.forward.refs_12_.refs_9_) | copy-start | bytes 3538948
  3.0 16.9 %collective-permute-start = (bf16[512,128]{1,0:T(8,128)(2,1)S(1)}, bf16[512,128]{1,0:T(8,128)(2,1)S(1)}, u32[]{:S(2)}, u32[]{:S(2)}) collective-permute-start(bf16[512,128]{1,0:T(8,128)(2,1)S(1)} %get-tuple-element.37), channel_id=1, source_target_pairs={{0,4},{1,5},{2,6},{3,7},{4,0},{5,1},{6,2},{7,3},{8,12},{9,13},{10,... | collective-permute-start | bytes 393224 | tf_op jit(solution)/shard_map/ppermute | solution.py:282
  7.1 16.6 %collective-permute-start.1 = (bf16[512,128]{1,0:T(8,128)(2,1)S(1)}, bf16[512,128]{1,0:T(8,128)(2,1)S(1)}, u32[]{:S(2)}, u32[]{:S(2)}) collective-permute-start(bf16[512,128]{1,0:T(8,128)(2,1)S(1)} %get-tuple-element.38), channel_id=1, source_target_pairs={{0,1},{1,0},{2,3},{3,2},{4,5},{5,4},{6,7},{7,6},{8,9},{9,8},{10,11... | collective-permute-start | bytes 393224 | tf_op jit(solution)/shard_map/ppermute | solution.py:282
  8.7 18.4 %collective-permute-start.2 = (bf16[512,128]{1,0:T(8,128)(2,1)S(1)}, bf16[512,128]{1,0:T(8,128)(2,1)S(1)}, u32[]{:S(2)}, u32[]{:S(2)}) collective-permute-start(bf16[512,128]{1,0:T(8,128)(2,1)S(1)} %get-tuple-element.39), channel_id=1, source_target_pairs={{0,5},{1,4},{2,7},{3,6},{4,1},{5,0},{6,3},{7,2},{8,13},{9,12},{10,... | collective-permute-start | bytes 393224 | tf_op jit(solution)/shard_map/ppermute | solution.py:282
  8.7 19.9 %collective-permute-start.3 = (bf16[512,128]{1,0:T(8,128)(2,1)S(1)}, bf16[512,128]{1,0:T(8,128)(2,1)S(1)}, u32[]{:S(2)}, u32[]{:S(2)}) collective-permute-start(bf16[512,128]{1,0:T(8,128)(2,1)S(1)} %get-tuple-element.40), channel_id=1, source_target_pairs={{0,6},{1,7},{2,4},{3,5},{4,2},{5,3},{6,0},{7,1},{8,14},{9,15},{10,... | collective-permute-start | bytes 393224 | tf_op jit(solution)/shard_map/ppermute | solution.py:282
  12.5 18.7 %collective-permute-start.4 = (bf16[512,128]{1,0:T(8,128)(2,1)S(1)}, bf16[512,128]{1,0:T(8,128)(2,1)S(1)}, u32[]{:S(2)}, u32[]{:S(2)}) collective-permute-start(bf16[512,128]{1,0:T(8,128)(2,1)S(1)} %get-tuple-element.41), channel_id=1, source_target_pairs={{0,2},{1,3},{2,0},{3,1},{4,6},{5,7},{6,4},{7,5},{8,10},{9,11},{10,... | collective-permute-start | bytes 393224 | tf_op jit(solution)/shard_map/ppermute | solution.py:282
  20.0 12.6 %collective-permute-start.5 = (bf16[512,128]{1,0:T(8,128)(2,1)S(1)}, bf16[512,128]{1,0:T(8,128)(2,1)S(1)}, u32[]{:S(2)}, u32[]{:S(2)}) collective-permute-start(bf16[512,128]{1,0:T(8,128)(2,1)S(1)} %get-tuple-element.42), channel_id=1, source_target_pairs={{0,7},{1,6},{2,5},{3,4},{4,3},{5,2},{6,1},{7,0},{8,15},{9,14},{10,... | collective-permute-start | bytes 393224 | tf_op jit(solution)/shard_map/ppermute | solution.py:282
  23.8 9.3 %collective-permute-start.6 = (bf16[512,128]{1,0:T(8,128)(2,1)S(1)}, bf16[512,128]{1,0:T(8,128)(2,1)S(1)}, u32[]{:S(2)}, u32[]{:S(2)}) collective-permute-start(bf16[512,128]{1,0:T(8,128)(2,1)S(1)} %get-tuple-element.43), channel_id=1, source_target_pairs={{0,3},{1,2},{2,1},{3,0},{4,7},{5,6},{6,5},{7,4},{8,11},{9,10},{10,... | collective-permute-start | bytes 393224 | tf_op jit(solution)/shard_map/ppermute | solution.py:282
  23.8 9.3 %copy-start.1 = (bf16[9,256,256]{2,1,0:T(8,128)(2,1)S(1)}, bf16[9,256,256]{2,1,0:T(8,128)(2,1)}, u32[]{:S(2)}) copy-start(bf16[9,256,256]{2,1,0:T(8,128)(2,1)} %constant.13.clone.refs_13_.refs_10_) | copy-start | bytes 3538948
  27.1 18.4 %collective-permute-start.14 = (bf16[512,128]{1,0:T(8,128)(2,1)S(1)}, bf16[512,128]{1,0:T(8,128)(2,1)S(1)}, u32[]{:S(2)}, u32[]{:S(2)}) collective-permute-start(bf16[512,128]{1,0:T(8,128)(2,1)S(1)} %get-tuple-element.57), channel_id=1, source_target_pairs={{0,4},{1,5},{2,6},{3,7},{4,0},{5,1},{6,2},{7,3},{8,12},{9,13},{10,... | collective-permute-start | bytes 393224 | tf_op jit(solution)/shard_map/ppermute | solution.py:282
  28.6 20.7 %collective-permute-start.15 = (bf16[512,128]{1,0:T(8,128)(2,1)S(1)}, bf16[512,128]{1,0:T(8,128)(2,1)S(1)}, u32[]{:S(2)}, u32[]{:S(2)}) collective-permute-start(bf16[512,128]{1,0:T(8,128)(2,1)S(1)} %get-tuple-element.58), channel_id=1, source_target_pairs={{0,5},{1,4},{2,7},{3,6},{4,1},{5,0},{6,3},{7,2},{8,13},{9,12},{10,... | collective-permute-start | bytes 393224 | tf_op jit(solution)/shard_map/ppermute | solution.py:282
  31.2 18.1 %collective-permute-start.16 = (bf16[512,128]{1,0:T(8,128)(2,1)S(1)}, bf16[512,128]{1,0:T(8,128)(2,1)S(1)}, u32[]{:S(2)}, u32[]{:S(2)}) collective-permute-start(bf16[512,128]{1,0:T(8,128)(2,1)S(1)} %get-tuple-element.59), channel_id=1, source_target_pairs={{0,6},{1,7},{2,4},{3,5},{4,2},{5,3},{6,0},{7,1},{8,14},{9,15},{10,... | collective-permute-start | bytes 393224 | tf_op jit(solution)/shard_map/ppermute | solution.py:282
  32.6 17.8 %collective-permute-start.17 = (bf16[512,128]{1,0:T(8,128)(2,1)S(1)}, bf16[512,128]{1,0:T(8,128)(2,1)S(1)}, u32[]{:S(2)}, u32[]{:S(2)}) collective-permute-start(bf16[512,128]{1,0:T(8,128)(2,1)S(1)} %get-tuple-element.60), channel_id=1, source_target_pairs={{0,1},{1,0},{2,3},{3,2},{4,5},{5,4},{6,7},{7,6},{8,9},{9,8},{10,11... | collective-permute-start | bytes 393224 | tf_op jit(solution)/shard_map/ppermute | solution.py:282
  37.3 17.0 %collective-permute-start.18 = (bf16[512,128]{1,0:T(8,128)(2,1)S(1)}, bf16[512,128]{1,0:T(8,128)(2,1)S(1)}, u32[]{:S(2)}, u32[]{:S(2)}) collective-permute-start(bf16[512,128]{1,0:T(8,128)(2,1)S(1)} %get-tuple-element.61), channel_id=1, source_target_pairs={{0,7},{1,6},{2,5},{3,4},{4,3},{5,2},{6,1},{7,0},{8,15},{9,14},{10,... | collective-permute-start | bytes 393224 | tf_op jit(solution)/shard_map/ppermute | solution.py:282
  45.5 10.0 %collective-permute-start.19 = (bf16[512,128]{1,0:T(8,128)(2,1)S(1)}, bf16[512,128]{1,0:T(8,128)(2,1)S(1)}, u32[]{:S(2)}, u32[]{:S(2)}) collective-permute-start(bf16[512,128]{1,0:T(8,128)(2,1)S(1)} %get-tuple-element.62), channel_id=1, source_target_pairs={{0,2},{1,3},{2,0},{3,1},{4,6},{5,7},{6,4},{7,5},{8,10},{9,11},{10,... | collective-permute-start | bytes 393224 | tf_op jit(solution)/shard_map/ppermute | solution.py:282
  49.3 9.2 %collective-permute-start.20 = (bf16[512,128]{1,0:T(8,128)(2,1)S(1)}, bf16[512,128]{1,0:T(8,128)(2,1)S(1)}, u32[]{:S(2)}, u32[]{:S(2)}) collective-permute-start(bf16[512,128]{1,0:T(8,128)(2,1)S(1)} %get-tuple-element.63), channel_id=1, source_target_pairs={{0,3},{1,2},{2,1},{3,0},{4,7},{5,6},{6,5},{7,4},{8,11},{9,10},{10,... | collective-permute-start | bytes 393224 | tf_op jit(solution)/shard_map/ppermute | solution.py:282
  49.3 16.3 %collective-permute-start.7 = (bf16[512,128]{1,0:T(8,128)(2,1)S(1)}, bf16[512,128]{1,0:T(8,128)(2,1)S(1)}, u32[]{:S(2)}, u32[]{:S(2)}) collective-permute-start(bf16[512,128]{1,0:T(8,128)(2,1)S(1)} %get-tuple-element.49), channel_id=1, source_target_pairs={{0,1},{1,0},{2,3},{3,2},{4,5},{5,4},{6,7},{7,6},{8,9},{9,8},{10,11... | collective-permute-start | bytes 393224 | tf_op jit(solution)/shard_map/ppermute | solution.py:282
  50.4 16.8 %collective-permute-start.8 = (bf16[512,128]{1,0:T(8,128)(2,1)S(1)}, bf16[512,128]{1,0:T(8,128)(2,1)S(1)}, u32[]{:S(2)}, u32[]{:S(2)}) collective-permute-start(bf16[512,128]{1,0:T(8,128)(2,1)S(1)} %get-tuple-element.50), channel_id=1, source_target_pairs={{0,4},{1,5},{2,6},{3,7},{4,0},{5,1},{6,2},{7,3},{8,12},{9,13},{10,... | collective-permute-start | bytes 393224 | tf_op jit(solution)/shard_map/ppermute | solution.py:282
  54.3 12.9 %collective-permute-start.9 = (bf16[512,128]{1,0:T(8,128)(2,1)S(1)}, bf16[512,128]{1,0:T(8,128)(2,1)S(1)}, u32[]{:S(2)}, u32[]{:S(2)}) collective-permute-start(bf16[512,128]{1,0:T(8,128)(2,1)S(1)} %get-tuple-element.51), channel_id=1, source_target_pairs={{0,2},{1,3},{2,0},{3,1},{4,6},{5,7},{6,4},{7,5},{8,10},{9,11},{10,... | collective-permute-start | bytes 393224 | tf_op jit(solution)/shard_map/ppermute | solution.py:282
  55.5 14.0 %collective-permute-start.10 = (bf16[512,128]{1,0:T(8,128)(2,1)S(1)}, bf16[512,128]{1,0:T(8,128)(2,1)S(1)}, u32[]{:S(2)}, u32[]{:S(2)}) collective-permute-start(bf16[512,128]{1,0:T(8,128)(2,1)S(1)} %get-tuple-element.52), channel_id=1, source_target_pairs={{0,5},{1,4},{2,7},{3,6},{4,1},{5,0},{6,3},{7,2},{8,13},{9,12},{10,... | collective-permute-start | bytes 393224 | tf_op jit(solution)/shard_map/ppermute | solution.py:282
  58.4 14.4 %collective-permute-start.11 = (bf16[512,128]{1,0:T(8,128)(2,1)S(1)}, bf16[512,128]{1,0:T(8,128)(2,1)S(1)}, u32[]{:S(2)}, u32[]{:S(2)}) collective-permute-start(bf16[512,128]{1,0:T(8,128)(2,1)S(1)} %get-tuple-element.53), channel_id=1, source_target_pairs={{0,6},{1,7},{2,4},{3,5},{4,2},{5,3},{6,0},{7,1},{8,14},{9,15},{10,... | collective-permute-start | bytes 393224 | tf_op jit(solution)/shard_map/ppermute | solution.py:282
  65.6 13.8 %collective-permute-start.21 = (bf16[512,256]{1,0:T(8,128)(2,1)S(1)}, bf16[512,256]{1,0:T(8,128)(2,1)S(1)}, u32[]{:S(2)}, u32[]{:S(2)}) collective-permute-start(bf16[512,256]{1,0:T(8,128)(2,1)S(1)} %get-tuple-element.66), channel_id=1, source_target_pairs={{0,16},{8,24},{16,0},{24,8},{1,17},{9,25},{17,1},{25,9},{2,18},{10... | collective-permute-start | bytes 786440 | tf_op jit(solution)/shard_map/ppermute | solution.py:282
  67.1 12.2 %collective-permute-start.22 = (bf16[512,256]{1,0:T(8,128)(2,1)S(1)}, bf16[512,256]{1,0:T(8,128)(2,1)S(1)}, u32[]{:S(2)}, u32[]{:S(2)}) collective-permute-start(bf16[512,256]{1,0:T(8,128)(2,1)S(1)} %get-tuple-element.67), channel_id=1, source_target_pairs={{0,24},{8,16},{16,8},{24,0},{1,25},{9,17},{17,9},{25,1},{2,26},{10... | collective-permute-start | bytes 786440 | tf_op jit(solution)/shard_map/ppermute | solution.py:282
  67.2 12.2 %collective-permute-start.23 = (bf16[512,256]{1,0:T(8,128)(2,1)S(1)}, bf16[512,256]{1,0:T(8,128)(2,1)S(1)}, u32[]{:S(2)}, u32[]{:S(2)}) collective-permute-start(bf16[512,256]{1,0:T(8,128)(2,1)S(1)} %get-tuple-element.68), channel_id=1, source_target_pairs={{0,8},{8,0},{16,24},{24,16},{1,9},{9,1},{17,25},{25,17},{2,10},{10... | collective-permute-start | bytes 786440 | tf_op jit(solution)/shard_map/ppermute | solution.py:282
  69.4 8.9 %collective-permute-start.12 = (bf16[512,128]{1,0:T(8,128)(2,1)S(1)}, bf16[512,128]{1,0:T(8,128)(2,1)S(1)}, u32[]{:S(2)}, u32[]{:S(2)}) collective-permute-start(bf16[512,128]{1,0:T(8,128)(2,1)S(1)} %get-tuple-element.54), channel_id=1, source_target_pairs={{0,7},{1,6},{2,5},{3,4},{4,3},{5,2},{6,1},{7,0},{8,15},{9,14},{10,... | collective-permute-start | bytes 393224 | tf_op jit(solution)/shard_map/ppermute | solution.py:282
  72.9 6.4 %collective-permute-start.13 = (bf16[512,128]{1,0:T(8,128)(2,1)S(1)}, bf16[512,128]{1,0:T(8,128)(2,1)S(1)}, u32[]{:S(2)}, u32[]{:S(2)}) collective-permute-start(bf16[512,128]{1,0:T(8,128)(2,1)S(1)} %get-tuple-element.55), channel_id=1, source_target_pairs={{0,3},{1,2},{2,1},{3,0},{4,7},{5,6},{6,5},{7,4},{8,11},{9,10},{10,... | collective-permute-start | bytes 393224 | tf_op jit(solution)/shard_map/ppermute | solution.py:282
